TPU v7x, 32 devices: a whole 2x2x4 slice. The times are simulated.
32 devices in a mesh: head: 4 (over y, x), tok: 8 (over z, core).
Axes of the slice: x: 2, y: 2, z: 4, core: 2. Of those that a mesh axis runs over, the one named last changes fastest.
Arguments:
- query_input: bfloat16 [2048, 2048], P('tok', 'head'), may hold values from -6 to 6
- key_input: bfloat16 [2048, 2048], P('tok', 'head'), may hold values from -6 to 6
- value_input: bfloat16 [2048, 2048], P('tok', 'head'), may hold values from -6 to 6
- out_grad: bfloat16 [2048, 2048], P('tok', 'head'), may hold values from -0.890625 to 0.890625
- token_rates: float32 [2048, 4], P('tok', 'head'), may hold values from 0.00088388345 to 0.008838835
- out_gain: float32 [2048], P('head'), may hold values from 0.1 to 1.9
- gate_prior: bfloat16 [4, 512, 256], P('head'), may hold values from -0.8242256 to 0.8242256
- up_prior: bfloat16 [4, 512, 256], P('head'), may hold values from -0.8242256 to 0.8242256
- down_prior: bfloat16 [4, 256, 512], P('head'), may hold values from -3.496893 to 3.496893
Outputs:
- query_grad: bfloat16 [2048, 2048], P('tok', 'head')
- key_grad: bfloat16 [2048, 2048], P('tok', 'head')
- value_grad: bfloat16 [2048, 2048], P('tok', 'head')
- gate_prior_grad: float32 [4, 512, 256], P('head', None, 'tok')
- up_prior_grad: float32 [4, 512, 256], P('head', None, 'tok')
- down_prior_grad: float32 [4, 256, 512], P('head', None, 'tok')
All inputs are finite; a program needn't handle non-finite values.
Results may differ from a plain program's by a relative error of at most 0.014.
Values may be sent and summed in bfloat16 or wider, within the bound.
No kernel may reach another device: no remote copies, remote signals or barrier semaphores. Data moves between devices by JAX's collectives and lax.ppermute only.
A program may use at most 64 MiB of HBM per device.

v0:
```python
import jax
import jax.numpy as jnp
from jax import lax
from jax.sharding import PartitionSpec as P

EPSILON = 1e-06


def matmul(first_op, second_op):
    return jnp.dot(first_op, second_op, preferred_element_type=jnp.float32)


def contract_rows(first_op, second_op):
    return lax.dot_general(
        first_op, second_op, (((0,), (0,)), ((), ())), preferred_element_type=jnp.float32
    )


def contract_cols(first_op, second_op):
    return lax.dot_general(
        first_op, second_op, (((1,), (1,)), ((), ())), preferred_element_type=jnp.float32
    )


def silu_parts(hidden):
    sigmoid_value = jax.nn.sigmoid(hidden)
    silu_value = hidden * sigmoid_value
    silu_slope = sigmoid_value * (1.0 + hidden * (1.0 - sigmoid_value))
    curvature = sigmoid_value * (1.0 - sigmoid_value) * (2.0 + hidden * (1.0 - 2.0 * sigmoid_value))
    return (silu_value, silu_slope, curvature)


def update_forward(key_head, value_head, rate_head, priors):
    gate_weight, up_weight, down_weight = priors
    gate_pre = matmul(key_head, gate_weight)
    up_pre = matmul(key_head, up_weight)
    silu_value, silu_slope, curvature = silu_parts(gate_pre)
    mixed_act = (silu_value * up_pre).astype(jnp.bfloat16)
    value_push = (-rate_head[:, None] * value_head.astype(jnp.float32)).astype(jnp.bfloat16)
    down_update = contract_rows(mixed_act, value_push)
    down_back = contract_cols(value_push, down_weight)
    gate_back = (down_back * up_pre * silu_slope).astype(jnp.bfloat16)
    up_back = (down_back * silu_value).astype(jnp.bfloat16)
    gate_update = contract_rows(key_head, gate_back)
    up_update = contract_rows(key_head, up_back)
    update_saved = (
        up_pre,
        silu_value,
        silu_slope,
        curvature,
        mixed_act,
        value_push,
        down_back,
        gate_back,
        up_back,
    )
    return ((gate_update, up_update, down_update), update_saved)


def renormalize(prior, update):
    prior_f = prior.astype(jnp.float32)
    moved_weight = prior_f - update
    prior_norm = jnp.sqrt(jnp.sum(prior_f * prior_f, axis=0) + EPSILON)
    moved_norm = jnp.sqrt(jnp.sum(moved_weight * moved_weight, axis=0) + EPSILON)
    return (moved_weight, prior_norm, moved_norm)


def apply_forward(query_head, fast_weights):
    gate_pre = matmul(query_head, fast_weights[0])
    up_pre = matmul(query_head, fast_weights[1])
    silu_value, silu_slope, curvature = silu_parts(gate_pre)
    mixed_act = (silu_value * up_pre).astype(jnp.bfloat16)
    output = matmul(mixed_act, fast_weights[2])
    return (output, (up_pre, silu_value, silu_slope, mixed_act))


def apply_backward(query_head, fast_weights, apply_saved, out_back):
    up_pre, silu_value, silu_slope, mixed_act = apply_saved
    down_grad = contract_rows(mixed_act, out_back)
    mixed_back = contract_cols(out_back, fast_weights[2])
    gate_back = (mixed_back * up_pre * silu_slope).astype(jnp.bfloat16)
    up_back = (mixed_back * silu_value).astype(jnp.bfloat16)
    gate_grad = contract_rows(query_head, gate_back)
    up_grad = contract_rows(query_head, up_back)
    query_back = (
        contract_cols(gate_back, fast_weights[0]) + contract_cols(up_back, fast_weights[1])
    ).astype(jnp.bfloat16)
    return ((gate_grad, up_grad, down_grad), query_back)


def norm_adjoint(prior, moved_weight, prior_norm, moved_norm, fast_grad, column_dot):
    moved_grad = (
        prior_norm
        / moved_norm
        * (fast_grad - moved_weight * (column_dot / (moved_norm * moved_norm)))
    )
    direct = prior.astype(jnp.float32) * (column_dot / (moved_norm * prior_norm))
    return (moved_grad, direct)


def second_adjoint(key_head, rate_head, priors, update_saved, cotangent):
    gate_weight, up_weight, down_weight = priors
    (
        up_pre,
        silu_value,
        silu_slope,
        curvature,
        mixed_act,
        value_push,
        down_back,
        gate_back,
        up_back,
    ) = update_saved
    gate_cot, up_cot, down_cot = cotangent
    gate_bar = matmul(key_head, gate_cot)
    up_bar = matmul(key_head, up_cot)
    mixed_bar = contract_cols(value_push, down_cot)
    push_bar = matmul(mixed_act, down_cot)
    down_back_bar = (gate_bar * up_pre * silu_slope + up_bar * silu_value).astype(jnp.bfloat16)
    up_pre_bar = (gate_bar * down_back * silu_slope + mixed_bar * silu_value).astype(jnp.bfloat16)
    gate_pre_bar = (
        (up_bar * down_back + mixed_bar * up_pre) * silu_slope
        + gate_bar * down_back * up_pre * curvature
    ).astype(jnp.bfloat16)
    down_prior_bar = contract_rows(down_back_bar, value_push)
    gate_prior_bar = contract_rows(key_head, gate_pre_bar)
    up_prior_bar = contract_rows(key_head, up_pre_bar)
    value_grad = (rate_head[:, None] * (push_bar + matmul(down_back_bar, down_weight))).astype(
        jnp.bfloat16
    )
    key_total = (
        contract_cols(gate_back, gate_cot)
        + contract_cols(up_back, up_cot)
        + contract_cols(gate_pre_bar, gate_weight)
        + contract_cols(up_pre_bar, up_weight)
    )
    key_grad = (-key_total).astype(jnp.bfloat16)
    return ((gate_prior_bar, up_prior_bar, down_prior_bar), key_grad, value_grad)


def per_device(
    query_input,
    key_input,
    value_input,
    out_grad,
    token_rates,
    out_gain,
    gate_prior,
    up_prior,
    down_prior,
):
    rate_head = token_rates[:, 0]
    priors = (gate_prior[0], up_prior[0], down_prior[0])
    tok_count = lax.axis_size("tok")
    tok_index = lax.axis_index("tok")
    local_updates, update_saved = update_forward(key_input, value_input, rate_head, priors)
    update_sums = lax.psum((local_updates[0], local_updates[1], local_updates[2]), "tok")
    renormed = [
        renormalize(priors[matrix_index], update_sums[matrix_index]) for matrix_index in range(3)
    ]
    fast_weights = tuple(
        (
            (moved_weight * (prior_norm / moved_norm)).astype(jnp.bfloat16)
            for moved_weight, prior_norm, moved_norm in renormed
        )
    )
    output, apply_saved = apply_forward(query_input, fast_weights)
    gain_weighted = out_grad.astype(jnp.float32) * out_gain
    square_sum, dot_sum = lax.psum(
        (jnp.sum(output * output, axis=1), jnp.sum(gain_weighted * output, axis=1)), "head"
    )
    full_width = lax.axis_size("head") * output.shape[1]
    inverse = lax.rsqrt(square_sum / full_width + EPSILON)
    out_back = (
        inverse[:, None] * gain_weighted
        - output * (inverse * inverse * inverse * dot_sum / full_width)[:, None]
    ).astype(jnp.bfloat16)
    fast_parts, query_grad = apply_backward(query_input, fast_weights, apply_saved, out_back)
    owned_parts = []
    fast_grads = lax.psum((fast_parts[0], fast_parts[1], fast_parts[2]), "tok")
    pieces = []
    for matrix_index in range(3):
        moved_weight, prior_norm, moved_norm = renormed[matrix_index]
        column_dot = jnp.sum(fast_grads[matrix_index] * moved_weight, axis=0)
        moved_grad, direct = norm_adjoint(
            priors[matrix_index],
            moved_weight,
            prior_norm,
            moved_norm,
            fast_grads[matrix_index],
            column_dot,
        )
        pieces.append(moved_grad.astype(jnp.bfloat16))
        shard_span = moved_weight.shape[1] // tok_count
        owned_parts.append(
            lax.dynamic_slice_in_dim(moved_grad + direct, tok_index * shard_span, shard_span, 1)
        )
    cotangent = (pieces[0], pieces[1], pieces[2])
    prior_bars, key_grad, value_grad = second_adjoint(
        key_input, rate_head, priors, update_saved, cotangent
    )
    prior_terms = [-prior_bars[matrix_index] for matrix_index in range(3)]
    summed_parts = (
        lax.psum_scatter(prior_terms[0], "tok", scatter_dimension=1, tiled=True),
        lax.psum_scatter(prior_terms[1], "tok", scatter_dimension=1, tiled=True),
        lax.psum_scatter(prior_terms[2], "tok", scatter_dimension=1, tiled=True),
    )
    results = tuple(
        (summed_parts[matrix_index] + owned_parts[matrix_index] for matrix_index in range(3))
    )
    return (query_grad, key_grad, value_grad, results[0][None], results[1][None], results[2][None])


def solution(mesh):
    in_specs = (
        P("tok", "head"),
        P("tok", "head"),
        P("tok", "head"),
        P("tok", "head"),
        P("tok", "head"),
        P("head"),
        P("head", None, None),
        P("head", None, None),
        P("head", None, None),
    )
    out_specs = (
        P("tok", "head"),
        P("tok", "head"),
        P("tok", "head"),
        P("head", None, "tok"),
        P("head", None, "tok"),
        P("head", None, "tok"),
    )
    return jax.shard_map(
        per_device, mesh=mesh, in_specs=in_specs, out_specs=out_specs, check_vma=False
    )
```

profile of v0, /device:TPU:0, one launch (start us, length us, event | category | flops | bytes accessed | tf_op | source)
XLA Modules:
  0.0 272.6 jit_solution(14333376142792450456)
XLA Ops:
  7.2 0.7 neg.27
  8.1 1.2 fusion.15
  10.4 0.9 multiply_convert_fusion.6
  11.4 1.0 convolution_bitcast_fusion.3
  12.4 1.1 convolution_bitcast_fusion.2
  13.5 1.1 fusion.49
  14.7 0.9 copy-done.11
  15.9 63.6 %all-reduce.8.cloned.1.call-done = (f32[512,256]{0,1:T(8,128)}, f32[512,256]{0,1:T(8,128)}, f32[256,512]{1,0:T(8,128)}) async-done(((f32[512,256]{0,1:T(8,128)}, f32[512,256]{0,1:T(8,128)}, f32[256,512]{1,0:T(8,128)}), (f32[512,256]{0,1:T(8,128)}, f32[512,256]{0,1:T(8,128)}, f32[256,512]{1,0:T(8,128)})) %all-reduce.8.cloned.1.call-update) | async-done | bytes 1572880 | tf_op jit(solution)/shard_map/psum | solution.py:157
  79.5 1.3 multiply_reduce_fusion.9
  84.4 0.8 copy-done.8
  85.5 1.0 multiply_convert_fusion.7
  86.5 1.0 multiply_reduce_fusion.4
  87.6 9.8 %all-reduce.2 = (f32[256]{0:T(256)S(1)}, f32[256]{0:T(256)S(1)}) all-reduce(f32[256]{0:T(256)S(1)} %get-tuple-element.19, f32[256]{0:T(256)S(1)} %get-tuple-element.18), channel_id=1, replica_groups=mesh['head'=4,'tok'=8] {'head'}, use_global_device_ids=true, to_apply=%region_12.0 | all-reduce | flops 512 | bytes 4096 | tf_op jit(solution)/shard_map/psum | solution.py:169
  97.4 1.3 subtract_convert_fusion
  98.8 1.1 fusion.51
  100.1 1.0 convolution_bitcast_fusion.1
  101.2 1.1 convolution_bitcast_fusion
  102.3 59.9 %all-reduce.6.cloned.1.call-done = (f32[512,256]{0,1:T(8,128)}, f32[512,256]{0,1:T(8,128)}, f32[256,512]{1,0:T(8,128)}) async-done(((f32[512,256]{0,1:T(8,128)}, f32[512,256]{0,1:T(8,128)}, f32[256,512]{1,0:T(8,128)}), (f32[512,256]{0,1:T(8,128)}, f32[512,256]{0,1:T(8,128)}, f32[256,512]{1,0:T(8,128)})) %all-reduce.6.cloned.1.call-update) | async-done | bytes 1572880 | tf_op jit(solution)/shard_map/psum | solution.py:180
  162.2 1.2 multiply_reduce_fusion.1
  164.8 0.6 multiply_divide_fusion.3
  165.4 0.6 copy-done.44
  166.5 1.0 copy-done.13
  167.6 0.6 multiply_divide_fusion
  168.7 0.6 copy-done.38
  169.9 1.1 fusion
  171.1 0.9 bitcast_convert_fusion.2
  172.0 0.8 bitcast_convert_fusion
  172.9 0.9 copy-done.10
  174.1 1.1 fusion.2
  175.2 0.9 copy-done.17
  176.1 0.9 fusion.6
  177.1 1.1 fusion.1
  178.4 0.8 copy-done.7
  179.4 0.7 copy-done.12
  180.5 0.9 copy-done.28
  181.6 0.7 copy-done.58
  182.3 0.7 copy-done.57
  183.1 0.8 dynamic-slice.2
  183.8 1.0 fusion.7
  184.8 0.7 copy-done.56
  185.5 0.9 fusion.5
  186.4 15.5 %reduce-scatter.10.cloned.1.call-done = f32[64,256]{1,0:T(8,128)} async-done(((f32[512,256]{1,0:T(8,128)}), f32[64,256]{1,0:T(8,128)}) %reduce-scatter.10.cloned.1.call-update) | async-done | bytes 65552
  201.9 0.9 copy.36
  203.0 0.7 copy.30
  203.7 29.6 %reduce-scatter.6.cloned.1.call-done = f32[512,32]{0,1:T(8,128)} async-done(((f32[512,256]{0,1:T(8,128)}), f32[512,32]{0,1:T(8,128)}) %reduce-scatter.6.cloned.1.call-update) | async-done | bytes 65552 | tf_op jit(solution)/shard_map/reduce_scatter | solution.py:204
  233.3 1.6 fusion.44
  234.8 29.7 %reduce-scatter.8.cloned.1.call-done = f32[512,32]{0,1:T(8,128)} async-done(((f32[512,256]{0,1:T(8,128)}), f32[512,32]{0,1:T(8,128)}) %reduce-scatter.8.cloned.1.call-update) | async-done | bytes 65552 | tf_op jit(solution)/shard_map/reduce_scatter | solution.py:205
  264.5 1.6 fusion.42
  (149 shorter events, 10.5 us)
Async XLA Ops:
  7.2 1.0 copy-start
  7.2 72.3 %all-reduce.8.cloned.1.call-start = ((), (), s32[]{:S(2)}) async-start(), calls=%async_computation.7 | async-start | bytes 3145728 | tf_op jit(solution)/shard_map/psum | solution.py:157
  8.1 1.3 copy-start.1
  8.1 1.3 copy-start.5
  9.4 1.0 copy-start.18
  11.4 1.0 copy-start.29
  11.4 2.1 copy-start.27
  14.6 0.9 copy-start.11
  14.6 147.6 %all-reduce.6.cloned.1.call-start = ((), (), s32[]{:S(2)}) async-start(), calls=%async_computation.6 | async-start | bytes 3145728 | tf_op jit(solution)/shard_map/psum | solution.py:180
  79.5 1.9 copy-start.3
  81.4 1.0 copy-start.4
  81.9 2.5 copy-start.9
  83.2 1.0 copy-start.2
  83.8 1.7 copy-start.16
  84.3 0.9 copy-start.8
  85.5 1.0 copy-start.39
  85.5 1.0 copy-start.20
  85.5 1.0 copy-start.55
  86.5 1.1 copy-start.33
  97.4 1.3 copy-start.34
  98.7 1.1 copy-start.40
  98.7 1.1 copy-start.60
  100.1 1.1 copy-start.23
  100.1 1.1 copy-start.21
  102.3 99.6 %reduce-scatter.10.cloned.1.call-start = ((), (), s32[]{:S(2)}) async-start(), calls=%async_computation.5 | async-start | bytes 589824
  162.2 1.3 copy-start.52
  162.2 1.3 copy-start.54
  162.2 1.9 copy-start.14
  164.1 1.3 copy-start.15
  164.1 1.3 copy-start.46
  166.2 2.4 copy-start.6
  166.2 1.2 copy-start.13
  168.3 1.0 copy-start.38
  168.4 1.0 copy-start.42
  168.4 1.1 copy-start.59
  169.9 1.2 copy-start.35
  169.9 4.2 %copy-start.31 = (bf16[256,256]{1,0:T(8,128)(2,1)}, bf16[256,256]{1,0:T(8,128)(2,1)S(1)}, u32[]{:S(2)}) copy-start(bf16[256,256]{1,0:T(8,128)(2,1)S(1)} %get-tuple-element.35) | copy-start | bytes 393220
  169.9 7.2 %copy-start.25 = (bf16[256,256]{1,0:T(8,128)(2,1)}, bf16[256,256]{1,0:T(8,128)(2,1)S(1)}, u32[]{:S(2)}) copy-start(bf16[256,256]{1,0:T(8,128)(2,1)S(1)} %get-tuple-element.36) | copy-start | bytes 393220
  171.1 62.2 %reduce-scatter.6.cloned.1.call-start = ((), (), s32[]{:S(2)}) async-start(), calls=%async_computation.3 | async-start | bytes 589824 | tf_op jit(solution)/shard_map/reduce_scatter | solution.py:204
  172.9 1.0 copy-start.24
  175.1 1.0 copy-start.22
  175.2 89.3 %reduce-scatter.8.cloned.1.call-start = ((), (), s32[]{:S(2)}) async-start(), calls=%async_computation.4 | async-start | bytes 589824 | tf_op jit(solution)/shard_map/reduce_scatter | solution.py:205
  178.1 1.0 copy-start.7
  178.1 1.1 copy-start.30
  179.2 1.0 copy-start.32
  181.4 2.5 copy-start.19
  181.4 2.5 copy-start.26
  183.8 1.0 copy-start.36
  (18 other events, 12.8 us)
Sparse Core Ops, SparseCore 0:
  14.8 64.6 all-reduce.7
  102.4 59.7 all-reduce.5
  171.2 30.6 reduce-scatter.9
  204.1 29.1 reduce-scatter.5
  235.4 29.0 reduce-scatter.7
where the time goes:
time: 273 us
  waiting for transfers between devices  198 us (73%)
  matrix products  19.6 us (7%)
  local copies, waits for them, and re-layouts  17.8 us (7%)
  between operations  14.3 us (5%)
  other arithmetic  12.6 us (5%)
  blocking collectives  9.81 us (4%)
    psum x1, waiting for transfers between devices, per_device(): lax.psum((local_updates[0], local_updates[1], local_updates[2]), 'tok')  63.6 us
    psum x1, waiting for transfers between devices, per_device(): fast_grads = lax.psum((fast_parts[0], fast_parts[1], fast_parts[2]), 'tok')  59.9 us
    reduce_scatter x1, waiting for transfers between devices, per_device(): lax.psum_scatter(prior_terms[1], 'tok', scatter_dimension=1, tiled=True)  29.7 us
    reduce_scatter x1, waiting for transfers between devices, per_device(): lax.psum_scatter(prior_terms[0], 'tok', scatter_dimension=1, tiled=True)  29.6 us
    unnamed x126, local copies, waits for them, and re-layouts  16.9 us
    unnamed x6, waiting for transfers between devices  15.6 us
    psum x1, blocking collectives, per_device(): lax.psum((jnp.sum(output * output, axis=1), jnp.sum(gain_weighted * outpu...  9.81 us
    dot_general x9, matrix products, contract_rows(): lax.dot_general(first_op, second_op, (((0,), (0,)), ((), ())), preferred_...  9.66 us
  transfers between devices with their start and end apart: 5, of which 5 were waited for; matrix products, arithmetic and copies ran while one was open for 5% of the time, Pallas kernels for 0%

commit v1 on v0

v1 whole, which is shorter than its diff:
```python
import jax
import jax.numpy as jnp
from jax import lax
from jax.sharding import PartitionSpec as P

EPSILON = 1e-06
CORES = 2


def nn(a, b):
    return lax.dot_general(a, b, (((1,), (0,)), ((), ())), preferred_element_type=jnp.float32)


def nt(a, b):
    return lax.dot_general(a, b, (((1,), (1,)), ((), ())), preferred_element_type=jnp.float32)


def tn(a, b):
    return lax.dot_general(a, b, (((0,), (0,)), ((), ())), preferred_element_type=jnp.float32)


def silu_parts(hidden):
    sigmoid_value = jax.nn.sigmoid(hidden)
    silu_value = hidden * sigmoid_value
    silu_slope = sigmoid_value * (1.0 + hidden * (1.0 - sigmoid_value))
    curvature = sigmoid_value * (1.0 - sigmoid_value) * (2.0 + hidden * (1.0 - 2.0 * sigmoid_value))
    return silu_value, silu_slope, curvature


def chip_perm(count, shift):
    chips = count // CORES
    return [(t, ((t // CORES + shift) % chips) * CORES + t % CORES) for t in range(count)]


def core_perm(count):
    return [(t, t ^ 1) for t in range(count)]


def pack(gate, up, down):
    folds = gate.shape[1] // down.shape[1]
    rows = down.shape[0] // folds
    down = jnp.concatenate([down[i * rows : (i + 1) * rows] for i in range(folds)], axis=1)
    return jnp.concatenate([gate, up, down], axis=0)


def unpack(packed, fh):
    g = packed.shape[0] // 3
    folds = packed.shape[1] // fh
    down = packed[2 * g :]
    down = jnp.concatenate([down[:, i * fh : (i + 1) * fh] for i in range(folds)], axis=0)
    return packed[:g], packed[g : 2 * g], down


def scatter_sum(gate, up, down, tok):
    count = lax.axis_size("tok")
    chips = count // CORES
    chip, core = tok // CORES, tok % CORES
    g, d = gate.shape[0] // count, down.shape[0] // count

    def piece(shift):
        t = lax.rem(chip + shift, chips) * CORES + core
        return pack(
            lax.dynamic_slice_in_dim(gate, t * g, g, 0),
            lax.dynamic_slice_in_dim(up, t * g, g, 0),
            lax.dynamic_slice_in_dim(down, t * d, d, 0),
        )

    total = piece(0)
    for shift in range(1, chips):
        sent = piece(shift).astype(jnp.bfloat16)
        total = total + lax.ppermute(sent, "tok", chip_perm(count, shift)).astype(jnp.float32)
    return total


def gather(packed, tok, fh):
    count = lax.axis_size("tok")
    chips = count // CORES
    chip, core = tok // CORES, tok % CORES
    held = jnp.zeros((count,) + packed.shape, packed.dtype)
    for shift in range(chips):
        mine = packed if shift == 0 else lax.ppermute(packed, "tok", chip_perm(count, shift))
        other = lax.ppermute(mine, "tok", core_perm(count))
        source = lax.rem(chip + chips - shift, chips) * CORES
        held = lax.dynamic_update_index_in_dim(held, mine, source + core, 0)
        held = lax.dynamic_update_index_in_dim(held, other, source + 1 - core, 0)
    gate, up, down = jax.vmap(lambda x: unpack(x, fh))(held)
    return tuple(x.reshape((-1, x.shape[-1])) for x in (gate, up, down))


def norm_of(rows):
    return jnp.sqrt(jnp.sum(rows * rows, axis=1, keepdims=True) + EPSILON)


def per_device(
    query_input,
    key_input,
    value_input,
    out_grad,
    token_rates,
    out_gain,
    gate_prior,
    up_prior,
    down_prior,
):
    count = lax.axis_size("tok")
    tok = lax.axis_index("tok")
    own = key_input.shape[0]
    w1t, w3t, w2 = gate_prior[0].T, up_prior[0].T, down_prior[0]
    fh = w2.shape[0]
    g, d = fh // count, w2.shape[1] // count
    rates = token_rates.T

    pair = lambda x: lax.ppermute(x, "tok", core_perm(count))
    keys = jnp.concatenate([key_input, pair(key_input)], axis=0)
    values = jnp.concatenate([value_input, pair(value_input)], axis=0)
    rate = jnp.concatenate([rates, pair(rates)], axis=1)
    queries = jnp.concatenate([query_input, pair(query_input)], axis=0)
    grads = jnp.concatenate([out_grad, pair(out_grad)], axis=0)

    gate_pre, up_pre = nt(w1t, keys), nt(w3t, keys)
    silu_value, silu_slope, curvature = silu_parts(gate_pre)
    mixed = (silu_value * up_pre).astype(jnp.bfloat16)
    push = (-rate * values.T.astype(jnp.float32)).astype(jnp.bfloat16)
    down_update = nt(push, mixed)
    down_back = nn(w2, push)
    gate_back = (down_back * up_pre * silu_slope).astype(jnp.bfloat16)
    up_back = (down_back * silu_value).astype(jnp.bfloat16)
    update = unpack(scatter_sum(nn(gate_back, keys), nn(up_back, keys), down_update, tok), fh)

    priors = [
        lax.dynamic_slice_in_dim(x, tok * n, n, 0).astype(jnp.float32)
        for x, n in ((w1t, g), (w3t, g), (w2.T, d))
    ]
    moved = [p - u for p, u in zip(priors, update)]
    prior_norm = [norm_of(p) for p in priors]
    moved_norm = [norm_of(m) for m in moved]
    fast = [
        (m * (p / n)).astype(jnp.bfloat16) for m, p, n in zip(moved, prior_norm, moved_norm)
    ]
    f1t, f3t, f2t = gather(pack(*fast), tok, fh)

    q_gate, q_up = nt(f1t, queries), nt(f3t, queries)
    q_silu, q_slope, _ = silu_parts(q_gate)
    q_mixed = (q_silu * q_up).astype(jnp.bfloat16)
    output = nn(f2t, q_mixed)
    weighted = grads.T.astype(jnp.float32) * out_gain[:, None]
    sums = lax.psum(
        jnp.stack([jnp.sum(output * output, axis=0), jnp.sum(weighted * output, axis=0)]), "head"
    )
    full_width = lax.axis_size("head") * output.shape[0]
    inverse = lax.rsqrt(sums[0:1] / full_width + EPSILON)
    out_back = (
        inverse * weighted - output * (inverse * inverse * inverse * sums[1:2] / full_width)
    ).astype(jnp.bfloat16)
    q_back = tn(f2t, out_back)
    q_gate_back = (q_back * q_up * q_slope).astype(jnp.bfloat16)
    q_up_back = (q_back * q_silu).astype(jnp.bfloat16)
    fast_grad = unpack(
        scatter_sum(nn(q_gate_back, queries), nn(q_up_back, queries), nt(out_back, q_mixed), tok),
        fh,
    )
    query_grad = (tn(q_gate_back[:, :own], f1t) + tn(q_up_back[:, :own], f3t)).astype(jnp.bfloat16)

    cotangent, owned = [], []
    for p, m, pn, mn, fg in zip(priors, moved, prior_norm, moved_norm, fast_grad):
        column_dot = jnp.sum(fg * m, axis=1, keepdims=True)
        moved_grad = pn / mn * (fg - m * (column_dot / (mn * mn)))
        cotangent.append(moved_grad.astype(jnp.bfloat16))
        owned.append(moved_grad + p * (column_dot / (mn * pn)))
    c1t, c3t, c2t = gather(pack(*cotangent), tok, fh)

    gate_bar, up_bar, mixed_bar = nt(c1t, keys), nt(c3t, keys), tn(c2t, push)
    down_back_bar = (gate_bar * up_pre * silu_slope + up_bar * silu_value).astype(jnp.bfloat16)
    up_pre_bar = (gate_bar * down_back * silu_slope + mixed_bar * silu_value).astype(jnp.bfloat16)
    gate_pre_bar = (
        (up_bar * down_back + mixed_bar * up_pre) * silu_slope
        + gate_bar * down_back * up_pre * curvature
    ).astype(jnp.bfloat16)
    bars = unpack(
        scatter_sum(nn(gate_pre_bar, keys), nn(up_pre_bar, keys), nt(push, down_back_bar), tok), fh
    )
    value_grad = (
        rates * (nn(c2t, mixed[:, :own]) + tn(w2, down_back_bar[:, :own]))
    ).astype(jnp.bfloat16).T
    key_grad = (
        -(
            tn(gate_back[:, :own], c1t)
            + tn(up_back[:, :own], c3t)
            + tn(gate_pre_bar[:, :own], w1t)
            + tn(up_pre_bar[:, :own], w3t)
        )
    ).astype(jnp.bfloat16)
    results = [(o - b).T[None] for o, b in zip(owned, bars)]
    return (query_grad, key_grad, value_grad, *results)


def solution(mesh):
    tokens = P("tok", "head")
    in_specs = (tokens,) * 5 + (P("head"),) + (P("head", None, None),) * 3
    out_specs = (tokens,) * 3 + (P("head", None, "tok"),) * 3
    return jax.shard_map(
        per_device, mesh=mesh, in_specs=in_specs, out_specs=out_specs, check_vma=False
    )
```

time: 273 us -> 111 us (0.41)
  waiting for transfers between devices: 198 us -> 37 us
  starting transfers between devices: 0.21 us -> 27.4 us
  between operations: 14.3 us -> 1.95 us
  other arithmetic: 12.6 us -> 4.04 us
  local copies, waits for them, and re-layouts: 17.8 us -> 12.4 us
    psum x2 -> x0, waiting for transfers between devices: 124 us -> none  [the longest x1 63.6 us: per_device(): lax.psum((local_updates[0], local_updates[1], local_updates[2]), 'tok')]
    reduce_scatter x2 -> x0, waiting for transfers between devices: 59.2 us -> none  [the longest x1 29.7 us: per_device(): lax.psum_scatter(prior_terms[1], 'tok', scatter_dimension=1, tiled=True)]
    ppermute x0 -> x28, waiting for transfers between devices: none -> 37 us  [the longest x9 23.6 us: scatter_sum(): lax.ppermute(sent, 'tok', chip_perm(count, shift)).astype(jnp.float32)]
    ppermute x0 -> x28, starting transfers between devices: none -> 27.4 us  [the longest x9 14.6 us: scatter_sum(): lax.ppermute(sent, 'tok', chip_perm(count, shift)).astype(jnp.float32)]
    unnamed x6 -> x0, waiting for transfers between devices: 15.6 us -> none
    unnamed x126 -> x76, local copies, waits for them, and re-layouts: 16.9 us -> 11.3 us
  transfers between devices with their start and end apart: 5 -> 28, of which waited for: 5 -> 14; matrix products, arithmetic and copies ran while one was open for 5% -> 8% of each run, Pallas kernels for 0% -> 0%
where the time goes in v1:
time: 111 us; the launch traced here: 110 us
  waiting for transfers between devices  37 us (33%)
  starting transfers between devices  27.4 us (25%)
  matrix products  17.4 us (16%)
  local copies, waits for them, and re-layouts  12.4 us (11%)
  blocking collectives  9.92 us (9%)
  other arithmetic  4.04 us (4%)
  between operations  1.95 us (2%)
    ppermute x9, waiting for transfers between devices, scatter_sum(): lax.ppermute(sent, 'tok', chip_perm(count, shift)).astype(jnp.float32)  23.6 us
    ppermute x9, starting transfers between devices, scatter_sum(): lax.ppermute(sent, 'tok', chip_perm(count, shift)).astype(jnp.float32)  14.6 us
    ppermute x6, waiting for transfers between devices, gather(): lax.ppermute(packed, 'tok', chip_perm(count, shift))  11.7 us
    unnamed x76, local copies, waits for them, and re-layouts  11.3 us
    ppermute x6, starting transfers between devices, gather(): lax.ppermute(packed, 'tok', chip_perm(count, shift))  10 us
    psum x1, blocking collectives, per_device(): lax.psum(jnp.stack([jnp.sum(output * output, axis=0), jnp.sum(weighted *...  9.92 us
    dot_general x9, matrix products, nt(): lax.dot_general(a, b, (((1,), (1,)), ((), ())), preferred_element_type=jn...  6.17 us
    dot_general x9, matrix products, nn(): lax.dot_general(a, b, (((1,), (0,)), ((), ())), preferred_element_type=jn...  5.65 us
  transfers between devices with their start and end apart: 28, of which 14 were waited for; matrix products, arithmetic and copies ran while one was open for 8% of the time, Pallas kernels for 0%

profile of v1, /device:TPU:0, one launch (start us, length us, event | category | flops | bytes accessed | tf_op | source)
XLA Modules:
  0.0 110.2 jit_solution(11055129194927575501)
XLA Ops:
  0.7 0.5 collective-permute-start.2
  1.9 1.1 copy.22
  3.0 0.5 collective-permute-start.14
  3.7 0.8 copy-done.1
  5.1 0.6 copy-done.20
  7.5 2.2 %multiply_convert_fusion.6 = (bf16[256,512]{0,1:T(8,128)(2,1)S(1)}, bf16[256,512]{0,1:T(8,128)(2,1)S(1)}, bf16[256,512]{0,1:T(8,128)(2,1)S(1)}, f32[256,512]{0,1:T(8,128)}) fusion(f32[256,512]{0,1:T(8,128)S(1)} %convolution_bitcast_fusion.1, f32[256,512]{0,1:T(8,128)S(1)} %convolution_bitcast_fusion, bf16[1,256,512]{2,1,0:T(8,128)(2,1)S(1)} %copy-done, ...), kind=kOutput, calls=%fused_computation.39 | convolution fusion | flops 137756672 | bytes 3147776 | tf_op jit(solution)/shard_map/dot_general | solution.py:11
  10.9 1.4 %fusion.63 = f32[512,256]{1,0:T(8,128)S(1)} fusion(bf16[256,512]{0,1:T(8,128)(2,1)S(1)} %get-tuple-element.24, bf16[256,512]{1,0:T(8,128)(2,1)} %collective-permute-done.1, bf16[256,512]{1,0:T(8,128)(2,1)S(1)} %copy-done.31, f32[512]{0:T(512)S(1)} %maximum_negate_fusion), kind=kOutput, calls=%fused_computation.208 | convolution fusion | flops 135790592 | bytes 1312768 | tf_op jit(solution)/shard_map/dot_general | solution.py:15
  12.4 5.1 %collective-permute-start.5 = (bf16[96,512]{1,0:T(8,128)(2,1)S(1)}, bf16[96,512]{1,0:T(8,128)(2,1)S(1)}, u32[]{:S(2)}, u32[]{:S(2)}) collective-permute-start(bf16[96,512]{1,0:T(8,128)(2,1)S(1)} %maximum_maximum_fusion.2), channel_id=1, source_target_pairs={{0,6},{1,7},{2,0},{3,1},{4,2},{5,3},{6,4},{7,5},{8,14},{9,15},{10,... | collective-permute-start | bytes 294920 | tf_op jit(solution)/shard_map/ppermute | solution.py:71
  17.6 1.0 collective-permute-start.3
  18.7 2.0 %collective-permute-done.5 = bf16[96,512]{1,0:T(8,128)(2,1)S(1)} collective-permute-done((bf16[96,512]{1,0:T(8,128)(2,1)S(1)}, bf16[96,512]{1,0:T(8,128)(2,1)S(1)}, u32[]{:S(2)}, u32[]{:S(2)}) %collective-permute-start.5) | collective-permute-done | bytes 98336 | tf_op jit(solution)/shard_map/ppermute | solution.py:71
  20.7 5.8 %collective-permute-done.4 = bf16[96,512]{1,0:T(8,128)(2,1)S(1)} collective-permute-done((bf16[96,512]{1,0:T(8,128)(2,1)S(1)}, bf16[96,512]{1,0:T(8,128)(2,1)S(1)}, u32[]{:S(2)}, u32[]{:S(2)}) %collective-permute-start.4) | collective-permute-done | bytes 98336 | tf_op jit(solution)/shard_map/ppermute | solution.py:71
  28.1 2.1 %collective-permute-start.9 = (bf16[96,512]{1,0:T(8,128)(2,1)S(1)}, bf16[96,512]{1,0:T(8,128)(2,1)S(1)}, u32[]{:S(2)}, u32[]{:S(2)}) collective-permute-start(bf16[96,512]{1,0:T(8,128)(2,1)S(1)} %maximum_maximum_fusion.3), channel_id=1, source_target_pairs={{0,4},{1,5},{2,6},{3,7},{4,0},{5,1},{6,2},{7,3},{8,12},{9,13},{10,... | collective-permute-start | bytes 294920 | tf_op jit(solution)/shard_map/ppermute | solution.py:81
  30.1 2.8 %collective-permute-start.11 = (bf16[96,512]{1,0:T(8,128)(2,1)S(1)}, bf16[96,512]{1,0:T(8,128)(2,1)S(1)}, u32[]{:S(2)}, u32[]{:S(2)}) collective-permute-start(bf16[96,512]{1,0:T(8,128)(2,1)S(1)} %maximum_maximum_fusion.3), channel_id=1, source_target_pairs={{0,6},{1,7},{2,0},{3,1},{4,2},{5,3},{6,4},{7,5},{8,14},{9,15},{10,... | collective-permute-start | bytes 294920 | tf_op jit(solution)/shard_map/ppermute | solution.py:81
  33.0 2.3 %collective-permute-done.7 = bf16[96,512]{1,0:T(8,128)(2,1)S(1)} collective-permute-done((bf16[96,512]{1,0:T(8,128)(2,1)S(1)}, bf16[96,512]{1,0:T(8,128)(2,1)S(1)}, u32[]{:S(2)}, u32[]{:S(2)}) %collective-permute-start.7) | collective-permute-done | bytes 98336 | tf_op jit(solution)/shard_map/ppermute | solution.py:81
  35.3 3.6 %collective-permute-done.9 = bf16[96,512]{1,0:T(8,128)(2,1)S(1)} collective-permute-done((bf16[96,512]{1,0:T(8,128)(2,1)S(1)}, bf16[96,512]{1,0:T(8,128)(2,1)S(1)}, u32[]{:S(2)}, u32[]{:S(2)}) %collective-permute-start.9) | collective-permute-done | bytes 98336 | tf_op jit(solution)/shard_map/ppermute | solution.py:81
  38.8 0.5 collective-permute-start.12
  39.4 0.7 collective-permute-done.10
  41.0 1.1 %multiply_convert_fusion.3 = (bf16[256,512]{0,1:T(8,128)(2,1)S(1)}, f32[256,512]{0,1:T(8,128)}) fusion(f32[256,512]{0,1:T(8,128)S(1)} %fusion.85, bf16[256,512]{1,0:T(8,128)(2,1)S(1)} %bitcast.248, bf16[512,512]{1,0:T(8,128)(2,1)S(1)} %constant_dynamic-update-slice_fusion.2), kind=kOutput, calls=%fused_computation.34 | convolution fusion | flops 135004160 | bytes 2097152 | tf_op jit(solution)/shard_map/dot_general | solution.py:15
  42.2 0.7 copy-done.26
  42.9 1.3 %multiply_reduce_fusion = (f32[512]{0:T(512)S(1)}, f32[512]{0:T(512)S(1)}, f32[512,512]{1,0:T(8,128)S(1)}) fusion(f32[512]{0:T(512)S(1)} %copy-done.26, bf16[256,512]{0,1:T(8,128)(2,1)} %collective-permute-done.14, bf16[256,512]{0,1:T(8,128)(2,1)S(1)} %copy-done.4, bf16[512,256]{1,0:T(8,128)(2,1)S(1)} %bitcast.252, bf16[256,512]{0,1:T(8,128)(2,1)S(1)} %get-tuple-element.108), kind=kOutput, calls=%fused_computation.19 | convolution fusion | flops 136576000 | bytes 2103296 | tf_op jit(solution)/shard_map/dot_general | solution.py:11
  44.2 9.9 %psum.7 = f32[2,512]{1,0:T(2,128)S(1)} all-reduce(f32[2,512]{1,0:T(2,128)S(1)} %pad_maximum_fusion.4), channel_id=1, replica_groups=mesh['head'=4,'tok'=8] {'head'}, use_global_device_ids=true, to_apply=%region_8.9 | all-reduce | flops 1024 | bytes 8192 | tf_op jit(solution)/shard_map/psum | solution.py:147
  54.2 1.3 %fusion.7 = bf16[512,512]{1,0:T(8,128)(2,1)S(1)} fusion(f32[512,512]{1,0:T(8,128)S(1)} %get-tuple-element.110, f32[512]{0:T(512)S(1)} %bitcast.254, f32[512]{0:T(512)S(1)} %bitcast.255, f32[512]{0:T(512)S(1)} %copy-done.26, bf16[256,512]{0,1:T(8,128)(2,1)} %collective-permute-done.14, bf16[256,512]{0,1:T(8,128)(2,1)} %copy-done.3), kind=kLoop, calls=%fused_computation.17 | loop fusion | flops 2359296 | bytes 2103296 | tf_op jit(solution)/shard_map/convert_element_type | solution.py:154
  55.8 0.7 copy-done.16
  58.7 0.9 fusion.3
  59.7 3.6 %collective-permute-start.17 = (bf16[96,512]{1,0:T(8,128)(2,1)S(1)}, bf16[96,512]{1,0:T(8,128)(2,1)S(1)}, u32[]{:S(2)}, u32[]{:S(2)}) collective-permute-start(bf16[96,512]{1,0:T(8,128)(2,1)S(1)} %maximum_maximum_fusion.6), channel_id=1, source_target_pairs={{0,6},{1,7},{2,0},{3,1},{4,2},{5,3},{6,4},{7,5},{8,14},{9,15},{10,... | collective-permute-start | bytes 294920 | tf_op jit(solution)/shard_map/ppermute | solution.py:71
  63.4 0.6 collective-permute-start.15
  64.0 2.0 %collective-permute-done.17 = bf16[96,512]{1,0:T(8,128)(2,1)S(1)} collective-permute-done((bf16[96,512]{1,0:T(8,128)(2,1)S(1)}, bf16[96,512]{1,0:T(8,128)(2,1)S(1)}, u32[]{:S(2)}, u32[]{:S(2)}) %collective-permute-start.17) | collective-permute-done | bytes 98336 | tf_op jit(solution)/shard_map/ppermute | solution.py:71
  65.9 4.9 %collective-permute-done.16 = bf16[96,512]{1,0:T(8,128)(2,1)S(1)} collective-permute-done((bf16[96,512]{1,0:T(8,128)(2,1)S(1)}, bf16[96,512]{1,0:T(8,128)(2,1)S(1)}, u32[]{:S(2)}, u32[]{:S(2)}) %collective-permute-start.16) | collective-permute-done | bytes 98336 | tf_op jit(solution)/shard_map/ppermute | solution.py:71
  71.2 0.5 copy-done.28
  72.1 2.1 %collective-permute-start.21 = (bf16[96,512]{1,0:T(8,128)(2,1)S(1)}, bf16[96,512]{1,0:T(8,128)(2,1)S(1)}, u32[]{:S(2)}, u32[]{:S(2)}) collective-permute-start(bf16[96,512]{1,0:T(8,128)(2,1)S(1)} %maximum_maximum_fusion.7), channel_id=1, source_target_pairs={{0,4},{1,5},{2,6},{3,7},{4,0},{5,1},{6,2},{7,3},{8,12},{9,13},{10,... | collective-permute-start | bytes 294920 | tf_op jit(solution)/shard_map/ppermute | solution.py:81
  74.3 2.6 %collective-permute-start.23 = (bf16[96,512]{1,0:T(8,128)(2,1)S(1)}, bf16[96,512]{1,0:T(8,128)(2,1)S(1)}, u32[]{:S(2)}, u32[]{:S(2)}) collective-permute-start(bf16[96,512]{1,0:T(8,128)(2,1)S(1)} %maximum_maximum_fusion.7), channel_id=1, source_target_pairs={{0,6},{1,7},{2,0},{3,1},{4,2},{5,3},{6,4},{7,5},{8,14},{9,15},{10,... | collective-permute-start | bytes 294920 | tf_op jit(solution)/shard_map/ppermute | solution.py:81
  77.0 2.6 %collective-permute-done.19 = bf16[96,512]{1,0:T(8,128)(2,1)S(1)} collective-permute-done((bf16[96,512]{1,0:T(8,128)(2,1)S(1)}, bf16[96,512]{1,0:T(8,128)(2,1)S(1)}, u32[]{:S(2)}, u32[]{:S(2)}) %collective-permute-start.19) | collective-permute-done | bytes 98336 | tf_op jit(solution)/shard_map/ppermute | solution.py:81
  79.7 3.3 %collective-permute-done.21 = bf16[96,512]{1,0:T(8,128)(2,1)S(1)} collective-permute-done((bf16[96,512]{1,0:T(8,128)(2,1)S(1)}, bf16[96,512]{1,0:T(8,128)(2,1)S(1)}, u32[]{:S(2)}, u32[]{:S(2)}) %collective-permute-start.21) | collective-permute-done | bytes 98336 | tf_op jit(solution)/shard_map/ppermute | solution.py:81
  83.5 0.7 collective-permute-done.22
  84.5 0.9 copy-done.8
  86.0 0.9 copy-done.24
  87.9 1.4 %fusion.62 = f32[256,512]{0,1:T(8,128)S(1)} fusion(bf16[512,256]{1,0:T(8,128)(2,1)S(1)} %bitcast.247, bf16[256,512]{1,0:T(8,128)(2,1)} %collective-permute-done.1, bf16[256,512]{1,0:T(8,128)(2,1)S(1)} %copy-done.32, f32[512]{0:T(512)S(1)} %copy-done.30), kind=kOutput, calls=%fused_computation.207 | convolution fusion | flops 135790592 | bytes 1312768 | tf_op jit(solution)/shard_map/dot_general | solution.py:19
  89.3 0.7 add_convert_fusion
  90.8 0.9 copy-done.10
  92.2 1.0 fusion.4
  93.2 0.9 fusion.2
  94.1 1.4 %fusion.61 = f32[512,256]{1,0:T(8,128)S(1)} fusion(bf16[256,512]{0,1:T(8,128)(2,1)S(1)} %get-tuple-element.18, bf16[256,512]{1,0:T(8,128)(2,1)} %collective-permute-done.1, bf16[256,512]{1,0:T(8,128)(2,1)S(1)} %copy-done.32, f32[512]{0:T(512)S(1)} %copy-done.30), kind=kOutput, calls=%fused_computation.206 | convolution fusion | flops 135790592 | bytes 1312768 | tf_op jit(solution)/shard_map/dot_general | solution.py:15
  95.6 3.4 %collective-permute-start.27 = (bf16[96,512]{1,0:T(8,128)(2,1)S(1)}, bf16[96,512]{1,0:T(8,128)(2,1)S(1)}, u32[]{:S(2)}, u32[]{:S(2)}) collective-permute-start(bf16[96,512]{1,0:T(8,128)(2,1)S(1)} %maximum_maximum_fusion.10), channel_id=1, source_target_pairs={{0,6},{1,7},{2,0},{3,1},{4,2},{5,3},{6,4},{7,5},{8,14},{9,15},{10,... | collective-permute-start | bytes 294920 | tf_op jit(solution)/shard_map/ppermute | solution.py:71
  99.1 0.6 collective-permute-start.25
  99.7 2.4 %collective-permute-done.27 = bf16[96,512]{1,0:T(8,128)(2,1)S(1)} collective-permute-done((bf16[96,512]{1,0:T(8,128)(2,1)S(1)}, bf16[96,512]{1,0:T(8,128)(2,1)S(1)}, u32[]{:S(2)}, u32[]{:S(2)}) %collective-permute-start.27) | collective-permute-done | bytes 98336 | tf_op jit(solution)/shard_map/ppermute | solution.py:71
  102.2 6.4 %collective-permute-done.26 = bf16[96,512]{1,0:T(8,128)(2,1)S(1)} collective-permute-done((bf16[96,512]{1,0:T(8,128)(2,1)S(1)}, bf16[96,512]{1,0:T(8,128)(2,1)S(1)}, u32[]{:S(2)}, u32[]{:S(2)}) %collective-permute-start.26) | collective-permute-done | bytes 98336 | tf_op jit(solution)/shard_map/ppermute | solution.py:71
  108.7 0.8 fusion.39
  109.4 0.7 fusion.41
  (204 shorter events, 13.8 us)
Async XLA Ops:
  0.6 4.1 %copy-start = (bf16[1,256,512]{2,1,0:T(8,128)(2,1)S(1)}, bf16[1,256,512]{2,1,0:T(8,128)(2,1)}, u32[]{:S(2)}) copy-start(bf16[1,256,512]{2,1,0:T(8,128)(2,1)} %param.17) | copy-start | bytes 786436
  0.7 5.4 %collective-permute-start.2 = (bf16[256,512]{1,0:T(8,128)(2,1)}, bf16[256,512]{1,0:T(8,128)(2,1)S(1)}, u32[]{:S(2)}, u32[]{:S(2)}) collective-permute-start(bf16[256,512]{1,0:T(8,128)(2,1)} %param.10), channel_id=1, source_target_pairs={{0,1},{1,0},{2,3},{3,2},{4,5},{5,4},{6,7},{7,6},{8,9},{9,8},{10,11... | collective-permute-start | bytes 786440 | tf_op jit(solution)/shard_map/ppermute | solution.py:113
  1.2 5.5 %collective-permute-start.1 = (bf16[256,512]{1,0:T(8,128)(2,1)}, bf16[256,512]{1,0:T(8,128)(2,1)}, u32[]{:S(2)}, u32[]{:S(2)}) collective-permute-start(bf16[256,512]{1,0:T(8,128)(2,1)} %param.11), channel_id=1, source_target_pairs={{0,1},{1,0},{2,3},{3,2},{4,5},{5,4},{6,7},{7,6},{8,9},{9,8},{10,11... | collective-permute-start | bytes 786440 | tf_op jit(solution)/shard_map/ppermute | solution.py:113
  1.4 2.1 %copy-start.19 = (bf16[256,512]{1,0:T(8,128)(2,1)S(1)}, bf16[256,512]{1,0:T(8,128)(2,1)}, u32[]{:S(2)}) copy-start(bf16[256,512]{1,0:T(8,128)(2,1)} %param.10) | copy-start | bytes 786436
  1.4 4.6 %collective-permute-start = (f32[1,256]{1,0:T(1,128)S(1)}, f32[1,256]{1,0:T(1,128)S(1)}, u32[]{:S(2)}, u32[]{:S(2)}) collective-permute-start(f32[1,256]{1,0:T(1,128)S(1)} %bitcast.256), channel_id=1, source_target_pairs={{0,1},{1,0},{2,3},{3,2},{4,5},{5,4},{6,7},{7,6},{8,9},{9,8},{10,11... | collective-permute-start | bytes 3080 | tf_op jit(solution)/shard_map/ppermute | solution.py:113
  1.8 16.8 %collective-permute-start.13 = (bf16[256,512]{1,0:T(8,128)(2,1)}, bf16[256,512]{1,0:T(8,128)(2,1)S(1)}, u32[]{:S(2)}, u32[]{:S(2)}) collective-permute-start(bf16[256,512]{1,0:T(8,128)(2,1)} %param.9), channel_id=1, source_target_pairs={{0,1},{1,0},{2,3},{3,2},{4,5},{5,4},{6,7},{7,6},{8,9},{9,8},{10,11... | collective-permute-start | bytes 786440 | tf_op jit(solution)/shard_map/ppermute | solution.py:113
  3.0 39.2 %collective-permute-start.14 = (bf16[256,512]{0,1:T(8,128)(2,1)S(1)}, bf16[256,512]{0,1:T(8,128)(2,1)}, u32[]{:S(2)}, u32[]{:S(2)}) collective-permute-start(bf16[256,512]{0,1:T(8,128)(2,1)S(1)} %copy.22), channel_id=1, source_target_pairs={{0,1},{1,0},{2,3},{3,2},{4,5},{5,4},{6,7},{7,6},{8,9},{9,8},{10,11... | collective-permute-start | bytes 786440 | tf_op jit(solution)/shard_map/ppermute | solution.py:113
  3.7 1.0 copy-start.2
  4.8 1.0 copy-start.20
  6.0 4.8 %copy-start.29 = (f32[512]{0:T(512)}, f32[512]{0:T(512)S(1)}, u32[]{:S(2)}) copy-start(f32[512]{0:T(512)S(1)} %maximum_negate_fusion) | copy-start | bytes 6148
  6.4 1.1 %copy-start.31 = (bf16[256,512]{1,0:T(8,128)(2,1)S(1)}, bf16[256,512]{1,0:T(8,128)(2,1)}, u32[]{:S(2)}) copy-start(bf16[256,512]{1,0:T(8,128)(2,1)} %param.11) | copy-start | bytes 786436
  6.7 3.0 %copy-start.13 = (f32[256,512]{0,1:T(8,128)}, f32[256,512]{0,1:T(8,128)S(1)}, u32[]{:S(2)}) copy-start(f32[256,512]{0,1:T(8,128)S(1)} %convolution_bitcast_fusion) | copy-start | bytes 1572868
  9.7 1.1 %copy-start.23 = (bf16[256,512]{0,1:T(8,128)(2,1)}, bf16[256,512]{0,1:T(8,128)(2,1)S(1)}, u32[]{:S(2)}) copy-start(bf16[256,512]{0,1:T(8,128)(2,1)S(1)} %get-tuple-element.24) | copy-start | bytes 786436
  12.4 8.3 %collective-permute-start.5 = (bf16[96,512]{1,0:T(8,128)(2,1)S(1)}, bf16[96,512]{1,0:T(8,128)(2,1)S(1)}, u32[]{:S(2)}, u32[]{:S(2)}) collective-permute-start(bf16[96,512]{1,0:T(8,128)(2,1)S(1)} %maximum_maximum_fusion.2), channel_id=1, source_target_pairs={{0,6},{1,7},{2,0},{3,1},{4,2},{5,3},{6,4},{7,5},{8,14},{9,15},{10,... | collective-permute-start | bytes 294920 | tf_op jit(solution)/shard_map/ppermute | solution.py:71
  17.5 9.0 %collective-permute-start.4 = (bf16[96,512]{1,0:T(8,128)(2,1)S(1)}, bf16[96,512]{1,0:T(8,128)(2,1)S(1)}, u32[]{:S(2)}, u32[]{:S(2)}) collective-permute-start(bf16[96,512]{1,0:T(8,128)(2,1)S(1)} %maximum_maximum_fusion.1), channel_id=1, source_target_pairs={{0,4},{1,5},{2,6},{3,7},{4,0},{5,1},{6,2},{7,3},{8,12},{9,13},{10,... | collective-permute-start | bytes 294920 | tf_op jit(solution)/shard_map/ppermute | solution.py:71
  17.6 8.9 %collective-permute-start.3 = (bf16[96,512]{1,0:T(8,128)(2,1)S(1)}, bf16[96,512]{1,0:T(8,128)(2,1)S(1)}, u32[]{:S(2)}, u32[]{:S(2)}) collective-permute-start(bf16[96,512]{1,0:T(8,128)(2,1)S(1)} %maximum_maximum_fusion), channel_id=1, source_target_pairs={{0,2},{1,3},{2,4},{3,5},{4,6},{5,7},{6,0},{7,1},{8,10},{9,11},{10,... | collective-permute-start | bytes 294920 | tf_op jit(solution)/shard_map/ppermute | solution.py:71
  27.6 11.7 %collective-permute-start.6 = (bf16[96,512]{1,0:T(8,128)(2,1)S(1)}, bf16[96,512]{1,0:T(8,128)(2,1)S(1)}, u32[]{:S(2)}, u32[]{:S(2)}) collective-permute-start(bf16[96,512]{1,0:T(8,128)(2,1)S(1)} %maximum_maximum_fusion.3), channel_id=1, source_target_pairs={{0,1},{1,0},{2,3},{3,2},{4,5},{5,4},{6,7},{7,6},{8,9},{9,8},{10,11... | collective-permute-start | bytes 294920 | tf_op jit(solution)/shard_map/ppermute | solution.py:82
  27.7 7.5 %collective-permute-start.7 = (bf16[96,512]{1,0:T(8,128)(2,1)S(1)}, bf16[96,512]{1,0:T(8,128)(2,1)S(1)}, u32[]{:S(2)}, u32[]{:S(2)}) collective-permute-start(bf16[96,512]{1,0:T(8,128)(2,1)S(1)} %maximum_maximum_fusion.3), channel_id=1, source_target_pairs={{0,2},{1,3},{2,4},{3,5},{4,6},{5,7},{6,0},{7,1},{8,10},{9,11},{10,... | collective-permute-start | bytes 294920 | tf_op jit(solution)/shard_map/ppermute | solution.py:81
  28.1 10.8 %collective-permute-start.9 = (bf16[96,512]{1,0:T(8,128)(2,1)S(1)}, bf16[96,512]{1,0:T(8,128)(2,1)S(1)}, u32[]{:S(2)}, u32[]{:S(2)}) collective-permute-start(bf16[96,512]{1,0:T(8,128)(2,1)S(1)} %maximum_maximum_fusion.3), channel_id=1, source_target_pairs={{0,4},{1,5},{2,6},{3,7},{4,0},{5,1},{6,2},{7,3},{8,12},{9,13},{10,... | collective-permute-start | bytes 294920 | tf_op jit(solution)/shard_map/ppermute | solution.py:81
  30.1 8.7 %collective-permute-start.11 = (bf16[96,512]{1,0:T(8,128)(2,1)S(1)}, bf16[96,512]{1,0:T(8,128)(2,1)S(1)}, u32[]{:S(2)}, u32[]{:S(2)}) collective-permute-start(bf16[96,512]{1,0:T(8,128)(2,1)S(1)} %maximum_maximum_fusion.3), channel_id=1, source_target_pairs={{0,6},{1,7},{2,0},{3,1},{4,2},{5,3},{6,4},{7,5},{8,14},{9,15},{10,... | collective-permute-start | bytes 294920 | tf_op jit(solution)/shard_map/ppermute | solution.py:81
  35.3 4.1 %collective-permute-start.8 = (bf16[96,512]{1,0:T(8,128)(2,1)S(1)}, bf16[96,512]{1,0:T(8,128)(2,1)S(1)}, u32[]{:S(2)}, u32[]{:S(2)}) collective-permute-start(bf16[96,512]{1,0:T(8,128)(2,1)S(1)} %collective-permute-done.7), channel_id=1, source_target_pairs={{0,1},{1,0},{2,3},{3,2},{4,5},{5,4},{6,7},{7,6},{8,9},{9,8},{10,11... | collective-permute-start | bytes 294920 | tf_op jit(solution)/shard_map/ppermute | solution.py:82
  38.8 1.3 %collective-permute-start.10 = (bf16[96,512]{1,0:T(8,128)(2,1)S(1)}, bf16[96,512]{1,0:T(8,128)(2,1)S(1)}, u32[]{:S(2)}, u32[]{:S(2)}) collective-permute-start(bf16[96,512]{1,0:T(8,128)(2,1)S(1)} %collective-permute-done.9), channel_id=1, source_target_pairs={{0,1},{1,0},{2,3},{3,2},{4,5},{5,4},{6,7},{7,6},{8,9},{9,8},{10,11... | collective-permute-start | bytes 294920 | tf_op jit(solution)/shard_map/ppermute | solution.py:82
  38.8 1.5 %collective-permute-start.12 = (bf16[96,512]{1,0:T(8,128)(2,1)S(1)}, bf16[96,512]{1,0:T(8,128)(2,1)S(1)}, u32[]{:S(2)}, u32[]{:S(2)}) collective-permute-start(bf16[96,512]{1,0:T(8,128)(2,1)S(1)} %collective-permute-done.11), channel_id=1, source_target_pairs={{0,1},{1,0},{2,3},{3,2},{4,5},{5,4},{6,7},{7,6},{8,9},{9,8},{10,11... | collective-permute-start | bytes 294920 | tf_op jit(solution)/shard_map/ppermute | solution.py:82
  40.7 1.5 %copy-start.15 = (f32[256,512]{0,1:T(8,128)}, f32[256,512]{0,1:T(8,128)S(1)}, u32[]{:S(2)}) copy-start(f32[256,512]{0,1:T(8,128)S(1)} %fusion.85) | copy-start | bytes 1572868
  40.7 1.4 %copy-start.21 = (bf16[8,64,256]{2,1,0:T(8,128)(2,1)}, bf16[8,64,256]{2,1,0:T(8,128)(2,1)S(1)}, u32[]{:S(2)}) copy-start(bf16[8,64,256]{2,1,0:T(8,128)(2,1)S(1)} %pad_maximum_fusion.1) | copy-start | bytes 786436
  41.0 1.2 %copy-start.4 = (bf16[256,512]{0,1:T(8,128)(2,1)S(1)}, bf16[256,512]{0,1:T(8,128)(2,1)}, u32[]{:S(2)}) copy-start(bf16[256,512]{0,1:T(8,128)(2,1)} %copy-done.3) | copy-start | bytes 786436
  42.2 2.0 %copy-start.17 = (bf16[256,512]{0,1:T(8,128)(2,1)}, bf16[256,512]{0,1:T(8,128)(2,1)S(1)}, u32[]{:S(2)}) copy-start(bf16[256,512]{0,1:T(8,128)(2,1)S(1)} %get-tuple-element.108) | copy-start | bytes 786436
  54.1 1.3 %copy-start.18 = (bf16[256,512]{0,1:T(8,128)(2,1)S(1)}, bf16[256,512]{0,1:T(8,128)(2,1)}, u32[]{:S(2)}) copy-start(bf16[256,512]{0,1:T(8,128)(2,1)} %copy-done.17) | copy-start | bytes 786436
  55.5 1.0 copy-start.16
  55.5 1.1 copy-start.22
  55.5 1.3 %copy-start.33 = (f32[256,512]{0,1:T(8,128)S(1)}, f32[256,512]{0,1:T(8,128)}, u32[]{:S(2)}) copy-start(f32[256,512]{0,1:T(8,128)} %get-tuple-element.109) | copy-start | bytes 1572868
  59.7 6.3 %collective-permute-start.17 = (bf16[96,512]{1,0:T(8,128)(2,1)S(1)}, bf16[96,512]{1,0:T(8,128)(2,1)S(1)}, u32[]{:S(2)}, u32[]{:S(2)}) collective-permute-start(bf16[96,512]{1,0:T(8,128)(2,1)S(1)} %maximum_maximum_fusion.6), channel_id=1, source_target_pairs={{0,6},{1,7},{2,0},{3,1},{4,2},{5,3},{6,4},{7,5},{8,14},{9,15},{10,... | collective-permute-start | bytes 294920 | tf_op jit(solution)/shard_map/ppermute | solution.py:71
  63.3 7.6 %collective-permute-start.16 = (bf16[96,512]{1,0:T(8,128)(2,1)S(1)}, bf16[96,512]{1,0:T(8,128)(2,1)S(1)}, u32[]{:S(2)}, u32[]{:S(2)}) collective-permute-start(bf16[96,512]{1,0:T(8,128)(2,1)S(1)} %maximum_maximum_fusion.5), channel_id=1, source_target_pairs={{0,4},{1,5},{2,6},{3,7},{4,0},{5,1},{6,2},{7,3},{8,12},{9,13},{10,... | collective-permute-start | bytes 294920 | tf_op jit(solution)/shard_map/ppermute | solution.py:71
  63.4 7.5 %collective-permute-start.15 = (bf16[96,512]{1,0:T(8,128)(2,1)S(1)}, bf16[96,512]{1,0:T(8,128)(2,1)S(1)}, u32[]{:S(2)}, u32[]{:S(2)}) collective-permute-start(bf16[96,512]{1,0:T(8,128)(2,1)S(1)} %maximum_maximum_fusion.4), channel_id=1, source_target_pairs={{0,2},{1,3},{2,4},{3,5},{4,6},{5,7},{6,0},{7,1},{8,10},{9,11},{10,... | collective-permute-start | bytes 294920 | tf_op jit(solution)/shard_map/ppermute | solution.py:71
  72.0 7.6 %collective-permute-start.18 = (bf16[96,512]{1,0:T(8,128)(2,1)S(1)}, bf16[96,512]{1,0:T(8,128)(2,1)S(1)}, u32[]{:S(2)}, u32[]{:S(2)}) collective-permute-start(bf16[96,512]{1,0:T(8,128)(2,1)S(1)} %maximum_maximum_fusion.7), channel_id=1, source_target_pairs={{0,1},{1,0},{2,3},{3,2},{4,5},{5,4},{6,7},{7,6},{8,9},{9,8},{10,11... | collective-permute-start | bytes 294920 | tf_op jit(solution)/shard_map/ppermute | solution.py:82
  72.1 7.5 %collective-permute-start.19 = (bf16[96,512]{1,0:T(8,128)(2,1)S(1)}, bf16[96,512]{1,0:T(8,128)(2,1)S(1)}, u32[]{:S(2)}, u32[]{:S(2)}) collective-permute-start(bf16[96,512]{1,0:T(8,128)(2,1)S(1)} %maximum_maximum_fusion.7), channel_id=1, source_target_pairs={{0,2},{1,3},{2,4},{3,5},{4,6},{5,7},{6,0},{7,1},{8,10},{9,11},{10,... | collective-permute-start | bytes 294920 | tf_op jit(solution)/shard_map/ppermute | solution.py:81
  72.1 10.8 %collective-permute-start.21 = (bf16[96,512]{1,0:T(8,128)(2,1)S(1)}, bf16[96,512]{1,0:T(8,128)(2,1)S(1)}, u32[]{:S(2)}, u32[]{:S(2)}) collective-permute-start(bf16[96,512]{1,0:T(8,128)(2,1)S(1)} %maximum_maximum_fusion.7), channel_id=1, source_target_pairs={{0,4},{1,5},{2,6},{3,7},{4,0},{5,1},{6,2},{7,3},{8,12},{9,13},{10,... | collective-permute-start | bytes 294920 | tf_op jit(solution)/shard_map/ppermute | solution.py:81
  74.3 8.7 %collective-permute-start.23 = (bf16[96,512]{1,0:T(8,128)(2,1)S(1)}, bf16[96,512]{1,0:T(8,128)(2,1)S(1)}, u32[]{:S(2)}, u32[]{:S(2)}) collective-permute-start(bf16[96,512]{1,0:T(8,128)(2,1)S(1)} %maximum_maximum_fusion.7), channel_id=1, source_target_pairs={{0,6},{1,7},{2,0},{3,1},{4,2},{5,3},{6,4},{7,5},{8,14},{9,15},{10,... | collective-permute-start | bytes 294920 | tf_op jit(solution)/shard_map/ppermute | solution.py:81
  79.6 3.8 %collective-permute-start.20 = (bf16[96,512]{1,0:T(8,128)(2,1)S(1)}, bf16[96,512]{1,0:T(8,128)(2,1)S(1)}, u32[]{:S(2)}, u32[]{:S(2)}) collective-permute-start(bf16[96,512]{1,0:T(8,128)(2,1)S(1)} %collective-permute-done.19), channel_id=1, source_target_pairs={{0,1},{1,0},{2,3},{3,2},{4,5},{5,4},{6,7},{7,6},{8,9},{9,8},{10,11... | collective-permute-start | bytes 294920 | tf_op jit(solution)/shard_map/ppermute | solution.py:82
  82.9 1.3 %collective-permute-start.22 = (bf16[96,512]{1,0:T(8,128)(2,1)S(1)}, bf16[96,512]{1,0:T(8,128)(2,1)S(1)}, u32[]{:S(2)}, u32[]{:S(2)}) collective-permute-start(bf16[96,512]{1,0:T(8,128)(2,1)S(1)} %collective-permute-done.21), channel_id=1, source_target_pairs={{0,1},{1,0},{2,3},{3,2},{4,5},{5,4},{6,7},{7,6},{8,9},{9,8},{10,11... | collective-permute-start | bytes 294920 | tf_op jit(solution)/shard_map/ppermute | solution.py:82
  82.9 1.5 %collective-permute-start.24 = (bf16[96,512]{1,0:T(8,128)(2,1)S(1)}, bf16[96,512]{1,0:T(8,128)(2,1)S(1)}, u32[]{:S(2)}, u32[]{:S(2)}) collective-permute-start(bf16[96,512]{1,0:T(8,128)(2,1)S(1)} %collective-permute-done.23), channel_id=1, source_target_pairs={{0,1},{1,0},{2,3},{3,2},{4,5},{5,4},{6,7},{7,6},{8,9},{9,8},{10,11... | collective-permute-start | bytes 294920 | tf_op jit(solution)/shard_map/ppermute | solution.py:82
  86.9 1.0 copy-start.32
  87.9 1.4 %copy-start.12 = (f32[256,512]{0,1:T(8,128)S(1)}, f32[256,512]{0,1:T(8,128)}, u32[]{:S(2)}) copy-start(f32[256,512]{0,1:T(8,128)} %copy-done.11) | copy-start | bytes 1572868
  87.9 1.4 %copy-start.14 = (f32[256,512]{0,1:T(8,128)S(1)}, f32[256,512]{0,1:T(8,128)}, u32[]{:S(2)}) copy-start(f32[256,512]{0,1:T(8,128)} %copy-done.13) | copy-start | bytes 1572868
  87.9 1.4 %copy-start.34 = (f32[256,512]{0,1:T(8,128)S(1)}, f32[256,512]{0,1:T(8,128)}, u32[]{:S(2)}) copy-start(f32[256,512]{0,1:T(8,128)} %get-tuple-element.107) | copy-start | bytes 1572868
  95.6 6.6 %collective-permute-start.27 = (bf16[96,512]{1,0:T(8,128)(2,1)S(1)}, bf16[96,512]{1,0:T(8,128)(2,1)S(1)}, u32[]{:S(2)}, u32[]{:S(2)}) collective-permute-start(bf16[96,512]{1,0:T(8,128)(2,1)S(1)} %maximum_maximum_fusion.10), channel_id=1, source_target_pairs={{0,6},{1,7},{2,0},{3,1},{4,2},{5,3},{6,4},{7,5},{8,14},{9,15},{10,... | collective-permute-start | bytes 294920 | tf_op jit(solution)/shard_map/ppermute | solution.py:71
  99.0 9.6 %collective-permute-start.26 = (bf16[96,512]{1,0:T(8,128)(2,1)S(1)}, bf16[96,512]{1,0:T(8,128)(2,1)S(1)}, u32[]{:S(2)}, u32[]{:S(2)}) collective-permute-start(bf16[96,512]{1,0:T(8,128)(2,1)S(1)} %maximum_maximum_fusion.9), channel_id=1, source_target_pairs={{0,4},{1,5},{2,6},{3,7},{4,0},{5,1},{6,2},{7,3},{8,12},{9,13},{10,... | collective-permute-start | bytes 294920 | tf_op jit(solution)/shard_map/ppermute | solution.py:71
  99.1 9.5 %collective-permute-start.25 = (bf16[96,512]{1,0:T(8,128)(2,1)S(1)}, bf16[96,512]{1,0:T(8,128)(2,1)S(1)}, u32[]{:S(2)}, u32[]{:S(2)}) collective-permute-start(bf16[96,512]{1,0:T(8,128)(2,1)S(1)} %maximum_maximum_fusion.8), channel_id=1, source_target_pairs={{0,2},{1,3},{2,4},{3,5},{4,6},{5,7},{6,0},{7,1},{8,10},{9,11},{10,... | collective-permute-start | bytes 294920 | tf_op jit(solution)/shard_map/ppermute | solution.py:71
  (15 other events, 11.7 us)

commit v2 on v1

--- a/solution.py
+++ b/solution.py
@@ -27,9 +27,17 @@
     return silu_value, silu_slope, curvature
 
 
-def chip_perm(count, shift):
+def partner(index, step, count):
+    return index ^ step if count & (count - 1) == 0 else (index + step) % count
+
+
+def source(index, step, count):
+    return index ^ step if count & (count - 1) == 0 else (index + count - step) % count
+
+
+def chip_perm(count, step):
     chips = count // CORES
-    return [(t, ((t // CORES + shift) % chips) * CORES + t % CORES) for t in range(count)]
+    return [(t, partner(t // CORES, step, chips) * CORES + t % CORES) for t in range(count)]
 
 
 def core_perm(count):
@@ -58,7 +66,7 @@
     g, d = gate.shape[0] // count, down.shape[0] // count
 
     def piece(shift):
-        t = lax.rem(chip + shift, chips) * CORES + core
+        t = partner(chip, shift, chips) * CORES + core
         return pack(
             lax.dynamic_slice_in_dim(gate, t * g, g, 0),
             lax.dynamic_slice_in_dim(up, t * g, g, 0),
@@ -66,7 +74,7 @@
         )
 
     total = piece(0)
-    for shift in range(1, chips):
+    for shift in reversed(range(1, chips)):
         sent = piece(shift).astype(jnp.bfloat16)
         total = total + lax.ppermute(sent, "tok", chip_perm(count, shift)).astype(jnp.float32)
     return total
@@ -77,12 +85,12 @@
     chips = count // CORES
     chip, core = tok // CORES, tok % CORES
     held = jnp.zeros((count,) + packed.shape, packed.dtype)
-    for shift in range(chips):
+    for shift in (0, *reversed(range(1, chips))):
         mine = packed if shift == 0 else lax.ppermute(packed, "tok", chip_perm(count, shift))
         other = lax.ppermute(mine, "tok", core_perm(count))
-        source = lax.rem(chip + chips - shift, chips) * CORES
-        held = lax.dynamic_update_index_in_dim(held, mine, source + core, 0)
-        held = lax.dynamic_update_index_in_dim(held, other, source + 1 - core, 0)
+        origin = source(chip, shift, chips) * CORES
+        held = lax.dynamic_update_index_in_dim(held, mine, origin + core, 0)
+        held = lax.dynamic_update_index_in_dim(held, other, origin + 1 - core, 0)
     gate, up, down = jax.vmap(lambda x: unpack(x, fh))(held)
     return tuple(x.reshape((-1, x.shape[-1])) for x in (gate, up, down))
 
@@ -144,10 +152,13 @@
     q_mixed = (q_silu * q_up).astype(jnp.bfloat16)
     output = nn(f2t, q_mixed)
     weighted = grads.T.astype(jnp.float32) * out_gain[:, None]
-    sums = lax.psum(
-        jnp.stack([jnp.sum(output * output, axis=0), jnp.sum(weighted * output, axis=0)]), "head"
-    )
-    full_width = lax.axis_size("head") * output.shape[0]
+    part = jnp.stack([jnp.sum(output * output, axis=0), jnp.sum(weighted * output, axis=0)])
+    heads = lax.axis_size("head")
+    sums = part
+    for step in range(1, heads):
+        perm = [(h, partner(h, step, heads)) for h in range(heads)]
+        sums = sums + lax.ppermute(part, "head", perm)
+    full_width = heads * output.shape[0]
     inverse = lax.rsqrt(sums[0:1] / full_width + EPSILON)
     out_back = (
         inverse * weighted - output * (inverse * inverse * inverse * sums[1:2] / full_width)

time: 111 us -> 95.7 us (0.86)
  blocking collectives: 9.92 us -> 0 us
  local copies, waits for them, and re-layouts: 12.4 us -> 5.37 us
  waiting for transfers between devices: 37 us -> 40.6 us
  matrix products: 17.4 us -> 14.8 us
  starting transfers between devices: 27.4 us -> 29.8 us
    psum x1 -> x0, blocking collectives: 9.92 us -> none  [per_device(): lax.psum(jnp.stack([jnp.sum(output * output, axis=0), jnp.sum(weighted *...]
    unnamed x76 -> x22, local copies, waits for them, and re-layouts: 11.3 us -> 4.25 us
    ppermute x6, waiting for transfers between devices: 11.7 us -> 16.3 us  [gather(): lax.ppermute(packed, 'tok', chip_perm(count, shift))]
    ppermute x9, waiting for transfers between devices: 23.6 us -> 19.5 us  [scatter_sum(): lax.ppermute(sent, 'tok', chip_perm(count, shift)).astype(jnp.float32)]
    ppermute x0 -> x3, starting transfers between devices: none -> 3.57 us  [per_device(): sums = sums + lax.ppermute(part, 'head', perm)]
    ppermute x0 -> x3, waiting for transfers between devices: none -> 3.08 us  [per_device(): sums = sums + lax.ppermute(part, 'head', perm)]
    dot_general x9, matrix products: 5.65 us -> 3.94 us  [nn(): lax.dot_general(a, b, (((1,), (0,)), ((), ())), preferred_element_type=jn...]
  transfers between devices with their start and end apart: 28 -> 31, of which waited for: 14 -> 18; matrix products, arithmetic and copies ran while one was open for 8% -> 8% of each run, Pallas kernels for 0% -> 0%
where the time goes in v2:
time: 95.7 us; the launch traced here: 95.3 us
  waiting for transfers between devices  40.6 us (42%)
  starting transfers between devices  29.8 us (31%)
  matrix products  14.8 us (15%)
  local copies, waits for them, and re-layouts  5.37 us (6%)
  other arithmetic  2.99 us (3%)
  between operations  1.74 us (2%)
    ppermute x9, waiting for transfers between devices, scatter_sum(): lax.ppermute(sent, 'tok', chip_perm(count, shift)).astype(jnp.float32)  19.5 us
    ppermute x6, waiting for transfers between devices, gather(): lax.ppermute(packed, 'tok', chip_perm(count, shift))  16.3 us
    ppermute x9, starting transfers between devices, scatter_sum(): lax.ppermute(sent, 'tok', chip_perm(count, shift)).astype(jnp.float32)  14.5 us
    ppermute x6, starting transfers between devices, gather(): lax.ppermute(packed, 'tok', chip_perm(count, shift))  8.91 us
    dot_general x9, matrix products, tn(): lax.dot_general(a, b, (((0,), (0,)), ((), ())), preferred_element_type=jn...  5.53 us
    dot_general x9, matrix products, nt(): lax.dot_general(a, b, (((1,), (1,)), ((), ())), preferred_element_type=jn...  5.37 us
    unnamed x22, local copies, waits for them, and re-layouts  4.25 us
    dot_general x9, matrix products, nn(): lax.dot_general(a, b, (((1,), (0,)), ((), ())), preferred_element_type=jn...  3.94 us
  transfers between devices with their start and end apart: 31, of which 18 were waited for; matrix products, arithmetic and copies ran while one was open for 8% of the time, Pallas kernels for 0%

profile of v2, /device:TPU:0, one launch (start us, length us, event | category | flops | bytes accessed | tf_op | source)
XLA Modules:
  0.0 95.3 jit_solution(8033483162242796740)
XLA Ops:
  0.7 0.5 collective-permute-start.2
  1.9 1.1 %copy.22 = bf16[256,512]{0,1:T(8,128)(2,1)S(1)} copy(bf16[256,512]{1,0:T(8,128)(2,1)} %param.12) | data formatting | bytes 524288 | tf_op args[3]
  3.0 0.5 collective-permute-start.14
  3.5 0.9 copy-done.1
  5.0 0.5 copy-done.4
  6.5 0.6 copy-done.7
  7.1 1.4 %multiply_convert_fusion.6 = (bf16[256,512]{0,1:T(8,128)(2,1)S(1)}, bf16[256,512]{0,1:T(8,128)(2,1)S(1)}, bf16[256,512]{0,1:T(8,128)(2,1)S(1)}, f32[256,512]{0,1:T(8,128)S(1)}) fusion(f32[256,512]{0,1:T(8,128)S(1)} %convolution_bitcast_fusion.1, f32[256,512]{0,1:T(8,128)S(1)} %convolution_bitcast_fusion, bf16[1,256,512]{2,1,0:T(8,128)(2,1)S(1)} %copy-done, ...), kind=kOutput, calls=%fused_computation.39 | convolution fusion | flops 137756672 | bytes 3147776 | tf_op jit(solution)/shard_map/dot_general | solution.py:11
  9.2 1.4 %fusion.63 = f32[512,256]{1,0:T(8,128)S(1)} fusion(bf16[256,512]{0,1:T(8,128)(2,1)S(1)} %get-tuple-element.24, bf16[256,512]{1,0:T(8,128)(2,1)} %collective-permute-done.1, bf16[256,512]{1,0:T(8,128)(2,1)S(1)} %copy-done.7, f32[512]{0:T(512)S(1)} %maximum_negate_fusion), kind=kOutput, calls=%fused_computation.209 | convolution fusion | flops 135790592 | bytes 1312768 | tf_op jit(solution)/shard_map/dot_general | solution.py:15
  10.7 2.7 %collective-permute-start.5 = (bf16[96,512]{1,0:T(8,128)(2,1)S(1)}, bf16[96,512]{1,0:T(8,128)(2,1)S(1)}, u32[]{:S(2)}, u32[]{:S(2)}) collective-permute-start(bf16[96,512]{1,0:T(8,128)(2,1)S(1)} %maximum_maximum_fusion.2), channel_id=1, source_target_pairs={{0,2},{1,3},{2,0},{3,1},{4,6},{5,7},{6,4},{7,5},{8,10},{9,11},{10,... | collective-permute-start | bytes 294920 | tf_op jit(solution)/shard_map/ppermute | solution.py:79
  13.4 2.7 %collective-permute-start.4 = (bf16[96,512]{1,0:T(8,128)(2,1)S(1)}, bf16[96,512]{1,0:T(8,128)(2,1)S(1)}, u32[]{:S(2)}, u32[]{:S(2)}) collective-permute-start(bf16[96,512]{1,0:T(8,128)(2,1)S(1)} %maximum_maximum_fusion.1), channel_id=1, source_target_pairs={{0,4},{1,5},{2,6},{3,7},{4,0},{5,1},{6,2},{7,3},{8,12},{9,13},{10,... | collective-permute-start | bytes 294920 | tf_op jit(solution)/shard_map/ppermute | solution.py:79
  16.2 0.6 collective-permute-done.5
  16.8 7.4 %collective-permute-done.4 = bf16[96,512]{1,0:T(8,128)(2,1)S(1)} collective-permute-done((bf16[96,512]{1,0:T(8,128)(2,1)S(1)}, bf16[96,512]{1,0:T(8,128)(2,1)S(1)}, u32[]{:S(2)}, u32[]{:S(2)}) %collective-permute-start.4) | collective-permute-done | bytes 98336 | tf_op jit(solution)/shard_map/ppermute | solution.py:79
  24.9 2.6 %collective-permute-start.7 = (bf16[96,512]{1,0:T(8,128)(2,1)S(1)}, bf16[96,512]{1,0:T(8,128)(2,1)S(1)}, u32[]{:S(2)}, u32[]{:S(2)}) collective-permute-start(bf16[96,512]{1,0:T(8,128)(2,1)S(1)} %maximum_maximum_fusion.3), channel_id=1, source_target_pairs={{0,6},{1,7},{2,4},{3,5},{4,2},{5,3},{6,0},{7,1},{8,14},{9,15},{10,... | collective-permute-start | bytes 294920 | tf_op jit(solution)/shard_map/ppermute | solution.py:89
  27.5 0.9 collective-permute-start.9
  28.3 1.0 %collective-permute-start.11 = (bf16[96,512]{1,0:T(8,128)(2,1)S(1)}, bf16[96,512]{1,0:T(8,128)(2,1)S(1)}, u32[]{:S(2)}, u32[]{:S(2)}) collective-permute-start(bf16[96,512]{1,0:T(8,128)(2,1)S(1)} %maximum_maximum_fusion.3), channel_id=1, source_target_pairs={{0,2},{1,3},{2,0},{3,1},{4,6},{5,7},{6,4},{7,5},{8,10},{9,11},{10,... | collective-permute-start | bytes 294920 | tf_op jit(solution)/shard_map/ppermute | solution.py:89
  29.4 2.9 %collective-permute-done.7 = bf16[96,512]{1,0:T(8,128)(2,1)S(1)} collective-permute-done((bf16[96,512]{1,0:T(8,128)(2,1)S(1)}, bf16[96,512]{1,0:T(8,128)(2,1)S(1)}, u32[]{:S(2)}, u32[]{:S(2)}) %collective-permute-start.7) | collective-permute-done | bytes 98336 | tf_op jit(solution)/shard_map/ppermute | solution.py:89
  32.3 5.5 %collective-permute-done.9 = bf16[96,512]{1,0:T(8,128)(2,1)S(1)} collective-permute-done((bf16[96,512]{1,0:T(8,128)(2,1)S(1)}, bf16[96,512]{1,0:T(8,128)(2,1)S(1)}, u32[]{:S(2)}, u32[]{:S(2)}) %collective-permute-start.9) | collective-permute-done | bytes 98336 | tf_op jit(solution)/shard_map/ppermute | solution.py:89
  37.8 0.5 collective-permute-start.12
  38.4 0.7 collective-permute-done.10
  40.0 0.7 copy-done.6
  41.1 2.5 %collective-permute-start.17 = (f32[2,512]{1,0:T(2,128)S(1)}, f32[2,512]{1,0:T(2,128)S(1)}, u32[]{:S(2)}, u32[]{:S(2)}) collective-permute-start(f32[2,512]{1,0:T(2,128)S(1)} %pad_maximum_fusion.4), channel_id=1, source_target_pairs={{0,24},{8,16},{16,8},{24,0},{1,25},{9,17},{17,9},{25,1},{2,26},{10... | collective-permute-start | bytes 12296 | tf_op jit(solution)/shard_map/ppermute | solution.py:160
  43.6 0.5 collective-permute-start.16
  44.1 0.5 collective-permute-start.15
  44.7 1.0 %collective-permute-done.17 = f32[2,512]{1,0:T(2,128)S(1)} collective-permute-done((f32[2,512]{1,0:T(2,128)S(1)}, f32[2,512]{1,0:T(2,128)S(1)}, u32[]{:S(2)}, u32[]{:S(2)}) %collective-permute-start.17) | collective-permute-done | bytes 4128 | tf_op jit(solution)/shard_map/ppermute | solution.py:160
  45.7 1.6 %collective-permute-done.16 = f32[2,512]{1,0:T(2,128)S(1)} collective-permute-done((f32[2,512]{1,0:T(2,128)S(1)}, f32[2,512]{1,0:T(2,128)S(1)}, u32[]{:S(2)}, u32[]{:S(2)}) %collective-permute-start.16) | collective-permute-done | bytes 4128 | tf_op jit(solution)/shard_map/ppermute | solution.py:160
  49.8 0.9 fusion.3
  50.9 3.1 %collective-permute-start.19 = (bf16[96,512]{1,0:T(8,128)(2,1)S(1)}, bf16[96,512]{1,0:T(8,128)(2,1)S(1)}, u32[]{:S(2)}, u32[]{:S(2)}) collective-permute-start(bf16[96,512]{1,0:T(8,128)(2,1)S(1)} %maximum_maximum_fusion.5), channel_id=1, source_target_pairs={{0,4},{1,5},{2,6},{3,7},{4,0},{5,1},{6,2},{7,3},{8,12},{9,13},{10,... | collective-permute-start | bytes 294920 | tf_op jit(solution)/shard_map/ppermute | solution.py:79
  54.0 1.4 %collective-permute-start.18 = (bf16[96,512]{1,0:T(8,128)(2,1)S(1)}, bf16[96,512]{1,0:T(8,128)(2,1)S(1)}, u32[]{:S(2)}, u32[]{:S(2)}) collective-permute-start(bf16[96,512]{1,0:T(8,128)(2,1)S(1)} %maximum_maximum_fusion.4), channel_id=1, source_target_pairs={{0,6},{1,7},{2,4},{3,5},{4,2},{5,3},{6,0},{7,1},{8,14},{9,15},{10,... | collective-permute-start | bytes 294920 | tf_op jit(solution)/shard_map/ppermute | solution.py:79
  55.4 4.1 %collective-permute-done.19 = bf16[96,512]{1,0:T(8,128)(2,1)S(1)} collective-permute-done((bf16[96,512]{1,0:T(8,128)(2,1)S(1)}, bf16[96,512]{1,0:T(8,128)(2,1)S(1)}, u32[]{:S(2)}, u32[]{:S(2)}) %collective-permute-start.19) | collective-permute-done | bytes 98336 | tf_op jit(solution)/shard_map/ppermute | solution.py:79
  59.5 1.1 %collective-permute-done.18 = bf16[96,512]{1,0:T(8,128)(2,1)S(1)} collective-permute-done((bf16[96,512]{1,0:T(8,128)(2,1)S(1)}, bf16[96,512]{1,0:T(8,128)(2,1)S(1)}, u32[]{:S(2)}, u32[]{:S(2)}) %collective-permute-start.18) | collective-permute-done | bytes 98336 | tf_op jit(solution)/shard_map/ppermute | solution.py:79
  61.3 2.4 %collective-permute-start.22 = (bf16[96,512]{1,0:T(8,128)(2,1)S(1)}, bf16[96,512]{1,0:T(8,128)(2,1)S(1)}, u32[]{:S(2)}, u32[]{:S(2)}) collective-permute-start(bf16[96,512]{1,0:T(8,128)(2,1)S(1)} %maximum_maximum_fusion.7), channel_id=1, source_target_pairs={{0,6},{1,7},{2,4},{3,5},{4,2},{5,3},{6,0},{7,1},{8,14},{9,15},{10,... | collective-permute-start | bytes 294920 | tf_op jit(solution)/shard_map/ppermute | solution.py:89
  63.7 0.7 collective-permute-start.24
  64.4 1.3 %collective-permute-start.26 = (bf16[96,512]{1,0:T(8,128)(2,1)S(1)}, bf16[96,512]{1,0:T(8,128)(2,1)S(1)}, u32[]{:S(2)}, u32[]{:S(2)}) collective-permute-start(bf16[96,512]{1,0:T(8,128)(2,1)S(1)} %maximum_maximum_fusion.7), channel_id=1, source_target_pairs={{0,2},{1,3},{2,0},{3,1},{4,6},{5,7},{6,4},{7,5},{8,10},{9,11},{10,... | collective-permute-start | bytes 294920 | tf_op jit(solution)/shard_map/ppermute | solution.py:89
  65.8 3.0 %collective-permute-done.22 = bf16[96,512]{1,0:T(8,128)(2,1)S(1)} collective-permute-done((bf16[96,512]{1,0:T(8,128)(2,1)S(1)}, bf16[96,512]{1,0:T(8,128)(2,1)S(1)}, u32[]{:S(2)}, u32[]{:S(2)}) %collective-permute-start.22) | collective-permute-done | bytes 98336 | tf_op jit(solution)/shard_map/ppermute | solution.py:89
  68.9 5.0 %collective-permute-done.24 = bf16[96,512]{1,0:T(8,128)(2,1)S(1)} collective-permute-done((bf16[96,512]{1,0:T(8,128)(2,1)S(1)}, bf16[96,512]{1,0:T(8,128)(2,1)S(1)}, u32[]{:S(2)}, u32[]{:S(2)}) %collective-permute-start.24) | collective-permute-done | bytes 98336 | tf_op jit(solution)/shard_map/ppermute | solution.py:89
  73.8 0.5 collective-permute-start.27
  74.4 0.7 collective-permute-done.25
  76.2 1.3 %fusion.62 = f32[256,512]{0,1:T(8,128)S(1)} fusion(bf16[512,256]{1,0:T(8,128)(2,1)S(1)} %bitcast.247, bf16[256,512]{1,0:T(8,128)(2,1)} %collective-permute-done.1, bf16[256,512]{1,0:T(8,128)(2,1)S(1)} %copy-done.7, f32[512]{0:T(512)S(1)} %maximum_negate_fusion), kind=kOutput, calls=%fused_computation.208 | convolution fusion | flops 135790592 | bytes 1312768 | tf_op jit(solution)/shard_map/dot_general | solution.py:19
  77.5 0.7 add_convert_fusion
  79.5 1.0 %fusion.4 = bf16[256,512]{1,0:T(8,128)(2,1)} fusion(f32[256,512]{1,0:T(8,128)S(1)} %convolution_add_fusion.2, bf16[1,512,256]{2,1,0:T(8,128)(2,1)S(1)} %copy-done.2, bf16[256,512]{0,1:T(8,128)(2,1)S(1)} %get-tuple-element.20), kind=kOutput, calls=%fused_computation.12 | convolution fusion | flops 67502080 | bytes 1179648 | tf_op jit(solution)/shard_map/dot_general | solution.py:19
  80.4 0.9 fusion.2
  81.4 1.4 %fusion.61 = f32[512,256]{1,0:T(8,128)S(1)} fusion(bf16[256,512]{0,1:T(8,128)(2,1)S(1)} %get-tuple-element.18, bf16[256,512]{1,0:T(8,128)(2,1)} %collective-permute-done.1, bf16[256,512]{1,0:T(8,128)(2,1)S(1)} %copy-done.7, f32[512]{0:T(512)S(1)} %maximum_negate_fusion), kind=kOutput, calls=%fused_computation.207 | convolution fusion | flops 135790592 | bytes 1312768 | tf_op jit(solution)/shard_map/dot_general | solution.py:15
  82.9 3.0 %collective-permute-start.29 = (bf16[96,512]{1,0:T(8,128)(2,1)S(1)}, bf16[96,512]{1,0:T(8,128)(2,1)S(1)}, u32[]{:S(2)}, u32[]{:S(2)}) collective-permute-start(bf16[96,512]{1,0:T(8,128)(2,1)S(1)} %maximum_maximum_fusion.9), channel_id=1, source_target_pairs={{0,4},{1,5},{2,6},{3,7},{4,0},{5,1},{6,2},{7,3},{8,12},{9,13},{10,... | collective-permute-start | bytes 294920 | tf_op jit(solution)/shard_map/ppermute | solution.py:79
  86.0 1.5 %collective-permute-start.28 = (bf16[96,512]{1,0:T(8,128)(2,1)S(1)}, bf16[96,512]{1,0:T(8,128)(2,1)S(1)}, u32[]{:S(2)}, u32[]{:S(2)}) collective-permute-start(bf16[96,512]{1,0:T(8,128)(2,1)S(1)} %maximum_maximum_fusion.8), channel_id=1, source_target_pairs={{0,6},{1,7},{2,4},{3,5},{4,2},{5,3},{6,0},{7,1},{8,14},{9,15},{10,... | collective-permute-start | bytes 294920 | tf_op jit(solution)/shard_map/ppermute | solution.py:79
  87.4 2.2 %collective-permute-done.30 = bf16[96,512]{1,0:T(8,128)(2,1)S(1)} collective-permute-done((bf16[96,512]{1,0:T(8,128)(2,1)S(1)}, bf16[96,512]{1,0:T(8,128)(2,1)S(1)}, u32[]{:S(2)}, u32[]{:S(2)}) %collective-permute-start.30) | collective-permute-done | bytes 98336 | tf_op jit(solution)/shard_map/ppermute | solution.py:79
  89.6 4.2 %collective-permute-done.29 = bf16[96,512]{1,0:T(8,128)(2,1)S(1)} collective-permute-done((bf16[96,512]{1,0:T(8,128)(2,1)S(1)}, bf16[96,512]{1,0:T(8,128)(2,1)S(1)}, u32[]{:S(2)}, u32[]{:S(2)}) %collective-permute-start.29) | collective-permute-done | bytes 98336 | tf_op jit(solution)/shard_map/ppermute | solution.py:79
  93.9 0.8 fusion.39
  94.6 0.7 fusion.41
  (156 shorter events, 10.7 us)
Async XLA Ops:
  0.6 4.1 %copy-start = (bf16[1,256,512]{2,1,0:T(8,128)(2,1)S(1)}, bf16[1,256,512]{2,1,0:T(8,128)(2,1)}, u32[]{:S(2)}) copy-start(bf16[1,256,512]{2,1,0:T(8,128)(2,1)} %param.17) | copy-start | bytes 786436
  0.6 0.7 copy-start.5
  0.7 5.2 %collective-permute-start.2 = (bf16[256,512]{1,0:T(8,128)(2,1)}, bf16[256,512]{1,0:T(8,128)(2,1)S(1)}, u32[]{:S(2)}, u32[]{:S(2)}) collective-permute-start(bf16[256,512]{1,0:T(8,128)(2,1)} %param.10), channel_id=1, source_target_pairs={{0,1},{1,0},{2,3},{3,2},{4,5},{5,4},{6,7},{7,6},{8,9},{9,8},{10,11... | collective-permute-start | bytes 786440 | tf_op jit(solution)/shard_map/ppermute | solution.py:121
  1.2 5.3 %collective-permute-start.1 = (bf16[256,512]{1,0:T(8,128)(2,1)}, bf16[256,512]{1,0:T(8,128)(2,1)}, u32[]{:S(2)}, u32[]{:S(2)}) collective-permute-start(bf16[256,512]{1,0:T(8,128)(2,1)} %param.11), channel_id=1, source_target_pairs={{0,1},{1,0},{2,3},{3,2},{4,5},{5,4},{6,7},{7,6},{8,9},{9,8},{10,11... | collective-permute-start | bytes 786440 | tf_op jit(solution)/shard_map/ppermute | solution.py:121
  1.4 2.1 %copy-start.3 = (bf16[256,512]{1,0:T(8,128)(2,1)S(1)}, bf16[256,512]{1,0:T(8,128)(2,1)}, u32[]{:S(2)}) copy-start(bf16[256,512]{1,0:T(8,128)(2,1)} %param.10) | copy-start | bytes 786436
  1.4 4.4 %collective-permute-start = (f32[1,256]{1,0:T(1,128)S(1)}, f32[1,256]{1,0:T(1,128)S(1)}, u32[]{:S(2)}, u32[]{:S(2)}) collective-permute-start(f32[1,256]{1,0:T(1,128)S(1)} %bitcast.260), channel_id=1, source_target_pairs={{0,1},{1,0},{2,3},{3,2},{4,5},{5,4},{6,7},{7,6},{8,9},{9,8},{10,11... | collective-permute-start | bytes 3080 | tf_op jit(solution)/shard_map/ppermute | solution.py:121
  1.8 14.4 %collective-permute-start.13 = (bf16[256,512]{1,0:T(8,128)(2,1)}, bf16[256,512]{1,0:T(8,128)(2,1)S(1)}, u32[]{:S(2)}, u32[]{:S(2)}) collective-permute-start(bf16[256,512]{1,0:T(8,128)(2,1)} %param.9), channel_id=1, source_target_pairs={{0,1},{1,0},{2,3},{3,2},{4,5},{5,4},{6,7},{7,6},{8,9},{9,8},{10,11... | collective-permute-start | bytes 786440 | tf_op jit(solution)/shard_map/ppermute | solution.py:121
  3.0 37.1 %collective-permute-start.14 = (bf16[256,512]{0,1:T(8,128)(2,1)S(1)}, bf16[256,512]{0,1:T(8,128)(2,1)S(1)}, u32[]{:S(2)}, u32[]{:S(2)}) collective-permute-start(bf16[256,512]{0,1:T(8,128)(2,1)S(1)} %copy.22), channel_id=1, source_target_pairs={{0,1},{1,0},{2,3},{3,2},{4,5},{5,4},{6,7},{7,6},{8,9},{9,8},{10,11... | collective-permute-start | bytes 786440 | tf_op jit(solution)/shard_map/ppermute | solution.py:121
  3.5 1.0 copy-start.1
  3.5 1.0 %copy-start.2 = (bf16[1,512,256]{2,1,0:T(8,128)(2,1)S(1)}, bf16[1,512,256]{2,1,0:T(8,128)(2,1)}, u32[]{:S(2)}) copy-start(bf16[1,512,256]{2,1,0:T(8,128)(2,1)} %param.16) | copy-start | bytes 786436
  4.6 1.0 copy-start.4
  6.2 1.0 copy-start.7
  10.7 6.1 %collective-permute-start.5 = (bf16[96,512]{1,0:T(8,128)(2,1)S(1)}, bf16[96,512]{1,0:T(8,128)(2,1)S(1)}, u32[]{:S(2)}, u32[]{:S(2)}) collective-permute-start(bf16[96,512]{1,0:T(8,128)(2,1)S(1)} %maximum_maximum_fusion.2), channel_id=1, source_target_pairs={{0,2},{1,3},{2,0},{3,1},{4,6},{5,7},{6,4},{7,5},{8,10},{9,11},{10,... | collective-permute-start | bytes 294920 | tf_op jit(solution)/shard_map/ppermute | solution.py:79
  13.4 10.8 %collective-permute-start.4 = (bf16[96,512]{1,0:T(8,128)(2,1)S(1)}, bf16[96,512]{1,0:T(8,128)(2,1)S(1)}, u32[]{:S(2)}, u32[]{:S(2)}) collective-permute-start(bf16[96,512]{1,0:T(8,128)(2,1)S(1)} %maximum_maximum_fusion.1), channel_id=1, source_target_pairs={{0,4},{1,5},{2,6},{3,7},{4,0},{5,1},{6,2},{7,3},{8,12},{9,13},{10,... | collective-permute-start | bytes 294920 | tf_op jit(solution)/shard_map/ppermute | solution.py:79
  16.1 8.1 %collective-permute-start.3 = (bf16[96,512]{1,0:T(8,128)(2,1)S(1)}, bf16[96,512]{1,0:T(8,128)(2,1)S(1)}, u32[]{:S(2)}, u32[]{:S(2)}) collective-permute-start(bf16[96,512]{1,0:T(8,128)(2,1)S(1)} %maximum_maximum_fusion), channel_id=1, source_target_pairs={{0,6},{1,7},{2,4},{3,5},{4,2},{5,3},{6,0},{7,1},{8,14},{9,15},{10,... | collective-permute-start | bytes 294920 | tf_op jit(solution)/shard_map/ppermute | solution.py:79
  24.8 13.5 %collective-permute-start.6 = (bf16[96,512]{1,0:T(8,128)(2,1)S(1)}, bf16[96,512]{1,0:T(8,128)(2,1)S(1)}, u32[]{:S(2)}, u32[]{:S(2)}) collective-permute-start(bf16[96,512]{1,0:T(8,128)(2,1)S(1)} %maximum_maximum_fusion.3), channel_id=1, source_target_pairs={{0,1},{1,0},{2,3},{3,2},{4,5},{5,4},{6,7},{7,6},{8,9},{9,8},{10,11... | collective-permute-start | bytes 294920 | tf_op jit(solution)/shard_map/ppermute | solution.py:90
  24.9 7.4 %collective-permute-start.7 = (bf16[96,512]{1,0:T(8,128)(2,1)S(1)}, bf16[96,512]{1,0:T(8,128)(2,1)S(1)}, u32[]{:S(2)}, u32[]{:S(2)}) collective-permute-start(bf16[96,512]{1,0:T(8,128)(2,1)S(1)} %maximum_maximum_fusion.3), channel_id=1, source_target_pairs={{0,6},{1,7},{2,4},{3,5},{4,2},{5,3},{6,0},{7,1},{8,14},{9,15},{10,... | collective-permute-start | bytes 294920 | tf_op jit(solution)/shard_map/ppermute | solution.py:89
  27.5 10.3 %collective-permute-start.9 = (bf16[96,512]{1,0:T(8,128)(2,1)S(1)}, bf16[96,512]{1,0:T(8,128)(2,1)S(1)}, u32[]{:S(2)}, u32[]{:S(2)}) collective-permute-start(bf16[96,512]{1,0:T(8,128)(2,1)S(1)} %maximum_maximum_fusion.3), channel_id=1, source_target_pairs={{0,4},{1,5},{2,6},{3,7},{4,0},{5,1},{6,2},{7,3},{8,12},{9,13},{10,... | collective-permute-start | bytes 294920 | tf_op jit(solution)/shard_map/ppermute | solution.py:89
  28.3 9.4 %collective-permute-start.11 = (bf16[96,512]{1,0:T(8,128)(2,1)S(1)}, bf16[96,512]{1,0:T(8,128)(2,1)S(1)}, u32[]{:S(2)}, u32[]{:S(2)}) collective-permute-start(bf16[96,512]{1,0:T(8,128)(2,1)S(1)} %maximum_maximum_fusion.3), channel_id=1, source_target_pairs={{0,2},{1,3},{2,0},{3,1},{4,6},{5,7},{6,4},{7,5},{8,10},{9,11},{10,... | collective-permute-start | bytes 294920 | tf_op jit(solution)/shard_map/ppermute | solution.py:89
  32.3 6.1 %collective-permute-start.8 = (bf16[96,512]{1,0:T(8,128)(2,1)S(1)}, bf16[96,512]{1,0:T(8,128)(2,1)S(1)}, u32[]{:S(2)}, u32[]{:S(2)}) collective-permute-start(bf16[96,512]{1,0:T(8,128)(2,1)S(1)} %collective-permute-done.7), channel_id=1, source_target_pairs={{0,1},{1,0},{2,3},{3,2},{4,5},{5,4},{6,7},{7,6},{8,9},{9,8},{10,11... | collective-permute-start | bytes 294920 | tf_op jit(solution)/shard_map/ppermute | solution.py:90
  37.8 1.3 %collective-permute-start.10 = (bf16[96,512]{1,0:T(8,128)(2,1)S(1)}, bf16[96,512]{1,0:T(8,128)(2,1)S(1)}, u32[]{:S(2)}, u32[]{:S(2)}) collective-permute-start(bf16[96,512]{1,0:T(8,128)(2,1)S(1)} %collective-permute-done.9), channel_id=1, source_target_pairs={{0,1},{1,0},{2,3},{3,2},{4,5},{5,4},{6,7},{7,6},{8,9},{9,8},{10,11... | collective-permute-start | bytes 294920 | tf_op jit(solution)/shard_map/ppermute | solution.py:90
  37.8 1.5 %collective-permute-start.12 = (bf16[96,512]{1,0:T(8,128)(2,1)S(1)}, bf16[96,512]{1,0:T(8,128)(2,1)S(1)}, u32[]{:S(2)}, u32[]{:S(2)}) collective-permute-start(bf16[96,512]{1,0:T(8,128)(2,1)S(1)} %collective-permute-done.11), channel_id=1, source_target_pairs={{0,1},{1,0},{2,3},{3,2},{4,5},{5,4},{6,7},{7,6},{8,9},{9,8},{10,11... | collective-permute-start | bytes 294920 | tf_op jit(solution)/shard_map/ppermute | solution.py:90
  40.0 0.7 copy-start.6
  41.1 4.6 %collective-permute-start.17 = (f32[2,512]{1,0:T(2,128)S(1)}, f32[2,512]{1,0:T(2,128)S(1)}, u32[]{:S(2)}, u32[]{:S(2)}) collective-permute-start(f32[2,512]{1,0:T(2,128)S(1)} %pad_maximum_fusion.4), channel_id=1, source_target_pairs={{0,24},{8,16},{16,8},{24,0},{1,25},{9,17},{17,9},{25,1},{2,26},{10... | collective-permute-start | bytes 12296 | tf_op jit(solution)/shard_map/ppermute | solution.py:160
  43.6 3.6 %collective-permute-start.16 = (f32[2,512]{1,0:T(2,128)S(1)}, f32[2,512]{1,0:T(2,128)S(1)}, u32[]{:S(2)}, u32[]{:S(2)}) collective-permute-start(f32[2,512]{1,0:T(2,128)S(1)} %pad_maximum_fusion.4), channel_id=1, source_target_pairs={{0,16},{8,24},{16,0},{24,8},{1,17},{9,25},{17,1},{25,9},{2,18},{10... | collective-permute-start | bytes 12296 | tf_op jit(solution)/shard_map/ppermute | solution.py:160
  44.1 3.6 %collective-permute-start.15 = (f32[2,512]{1,0:T(2,128)S(1)}, f32[2,512]{1,0:T(2,128)S(1)}, u32[]{:S(2)}, u32[]{:S(2)}) collective-permute-start(f32[2,512]{1,0:T(2,128)S(1)} %pad_maximum_fusion.4), channel_id=1, source_target_pairs={{0,8},{8,0},{16,24},{24,16},{1,9},{9,1},{17,25},{25,17},{2,10},{10... | collective-permute-start | bytes 12296 | tf_op jit(solution)/shard_map/ppermute | solution.py:160
  50.8 4.7 %collective-permute-start.20 = (bf16[96,512]{1,0:T(8,128)(2,1)S(1)}, bf16[96,512]{1,0:T(8,128)(2,1)S(1)}, u32[]{:S(2)}, u32[]{:S(2)}) collective-permute-start(bf16[96,512]{1,0:T(8,128)(2,1)S(1)} %maximum_maximum_fusion.6), channel_id=1, source_target_pairs={{0,2},{1,3},{2,0},{3,1},{4,6},{5,7},{6,4},{7,5},{8,10},{9,11},{10,... | collective-permute-start | bytes 294920 | tf_op jit(solution)/shard_map/ppermute | solution.py:79
  50.9 8.7 %collective-permute-start.19 = (bf16[96,512]{1,0:T(8,128)(2,1)S(1)}, bf16[96,512]{1,0:T(8,128)(2,1)S(1)}, u32[]{:S(2)}, u32[]{:S(2)}) collective-permute-start(bf16[96,512]{1,0:T(8,128)(2,1)S(1)} %maximum_maximum_fusion.5), channel_id=1, source_target_pairs={{0,4},{1,5},{2,6},{3,7},{4,0},{5,1},{6,2},{7,3},{8,12},{9,13},{10,... | collective-permute-start | bytes 294920 | tf_op jit(solution)/shard_map/ppermute | solution.py:79
  54.0 6.6 %collective-permute-start.18 = (bf16[96,512]{1,0:T(8,128)(2,1)S(1)}, bf16[96,512]{1,0:T(8,128)(2,1)S(1)}, u32[]{:S(2)}, u32[]{:S(2)}) collective-permute-start(bf16[96,512]{1,0:T(8,128)(2,1)S(1)} %maximum_maximum_fusion.4), channel_id=1, source_target_pairs={{0,6},{1,7},{2,4},{3,5},{4,2},{5,3},{6,0},{7,1},{8,14},{9,15},{10,... | collective-permute-start | bytes 294920 | tf_op jit(solution)/shard_map/ppermute | solution.py:79
  61.2 7.6 %collective-permute-start.21 = (bf16[96,512]{1,0:T(8,128)(2,1)S(1)}, bf16[96,512]{1,0:T(8,128)(2,1)S(1)}, u32[]{:S(2)}, u32[]{:S(2)}) collective-permute-start(bf16[96,512]{1,0:T(8,128)(2,1)S(1)} %maximum_maximum_fusion.7), channel_id=1, source_target_pairs={{0,1},{1,0},{2,3},{3,2},{4,5},{5,4},{6,7},{7,6},{8,9},{9,8},{10,11... | collective-permute-start | bytes 294920 | tf_op jit(solution)/shard_map/ppermute | solution.py:90
  61.3 7.6 %collective-permute-start.22 = (bf16[96,512]{1,0:T(8,128)(2,1)S(1)}, bf16[96,512]{1,0:T(8,128)(2,1)S(1)}, u32[]{:S(2)}, u32[]{:S(2)}) collective-permute-start(bf16[96,512]{1,0:T(8,128)(2,1)S(1)} %maximum_maximum_fusion.7), channel_id=1, source_target_pairs={{0,6},{1,7},{2,4},{3,5},{4,2},{5,3},{6,0},{7,1},{8,14},{9,15},{10,... | collective-permute-start | bytes 294920 | tf_op jit(solution)/shard_map/ppermute | solution.py:89
  63.7 10.1 %collective-permute-start.24 = (bf16[96,512]{1,0:T(8,128)(2,1)S(1)}, bf16[96,512]{1,0:T(8,128)(2,1)S(1)}, u32[]{:S(2)}, u32[]{:S(2)}) collective-permute-start(bf16[96,512]{1,0:T(8,128)(2,1)S(1)} %maximum_maximum_fusion.7), channel_id=1, source_target_pairs={{0,4},{1,5},{2,6},{3,7},{4,0},{5,1},{6,2},{7,3},{8,12},{9,13},{10,... | collective-permute-start | bytes 294920 | tf_op jit(solution)/shard_map/ppermute | solution.py:89
  64.4 9.4 %collective-permute-start.26 = (bf16[96,512]{1,0:T(8,128)(2,1)S(1)}, bf16[96,512]{1,0:T(8,128)(2,1)S(1)}, u32[]{:S(2)}, u32[]{:S(2)}) collective-permute-start(bf16[96,512]{1,0:T(8,128)(2,1)S(1)} %maximum_maximum_fusion.7), channel_id=1, source_target_pairs={{0,2},{1,3},{2,0},{3,1},{4,6},{5,7},{6,4},{7,5},{8,10},{9,11},{10,... | collective-permute-start | bytes 294920 | tf_op jit(solution)/shard_map/ppermute | solution.py:89
  68.8 5.5 %collective-permute-start.23 = (bf16[96,512]{1,0:T(8,128)(2,1)S(1)}, bf16[96,512]{1,0:T(8,128)(2,1)S(1)}, u32[]{:S(2)}, u32[]{:S(2)}) collective-permute-start(bf16[96,512]{1,0:T(8,128)(2,1)S(1)} %collective-permute-done.22), channel_id=1, source_target_pairs={{0,1},{1,0},{2,3},{3,2},{4,5},{5,4},{6,7},{7,6},{8,9},{9,8},{10,11... | collective-permute-start | bytes 294920 | tf_op jit(solution)/shard_map/ppermute | solution.py:90
  73.8 1.3 %collective-permute-start.25 = (bf16[96,512]{1,0:T(8,128)(2,1)S(1)}, bf16[96,512]{1,0:T(8,128)(2,1)S(1)}, u32[]{:S(2)}, u32[]{:S(2)}) collective-permute-start(bf16[96,512]{1,0:T(8,128)(2,1)S(1)} %collective-permute-done.24), channel_id=1, source_target_pairs={{0,1},{1,0},{2,3},{3,2},{4,5},{5,4},{6,7},{7,6},{8,9},{9,8},{10,11... | collective-permute-start | bytes 294920 | tf_op jit(solution)/shard_map/ppermute | solution.py:90
  73.8 1.5 %collective-permute-start.27 = (bf16[96,512]{1,0:T(8,128)(2,1)S(1)}, bf16[96,512]{1,0:T(8,128)(2,1)S(1)}, u32[]{:S(2)}, u32[]{:S(2)}) collective-permute-start(bf16[96,512]{1,0:T(8,128)(2,1)S(1)} %collective-permute-done.26), channel_id=1, source_target_pairs={{0,1},{1,0},{2,3},{3,2},{4,5},{5,4},{6,7},{7,6},{8,9},{9,8},{10,11... | collective-permute-start | bytes 294920 | tf_op jit(solution)/shard_map/ppermute | solution.py:90
  82.8 6.8 %collective-permute-start.30 = (bf16[96,512]{1,0:T(8,128)(2,1)S(1)}, bf16[96,512]{1,0:T(8,128)(2,1)S(1)}, u32[]{:S(2)}, u32[]{:S(2)}) collective-permute-start(bf16[96,512]{1,0:T(8,128)(2,1)S(1)} %maximum_maximum_fusion.10), channel_id=1, source_target_pairs={{0,2},{1,3},{2,0},{3,1},{4,6},{5,7},{6,4},{7,5},{8,10},{9,11},{10,... | collective-permute-start | bytes 294920 | tf_op jit(solution)/shard_map/ppermute | solution.py:79
  82.9 10.9 %collective-permute-start.29 = (bf16[96,512]{1,0:T(8,128)(2,1)S(1)}, bf16[96,512]{1,0:T(8,128)(2,1)S(1)}, u32[]{:S(2)}, u32[]{:S(2)}) collective-permute-start(bf16[96,512]{1,0:T(8,128)(2,1)S(1)} %maximum_maximum_fusion.9), channel_id=1, source_target_pairs={{0,4},{1,5},{2,6},{3,7},{4,0},{5,1},{6,2},{7,3},{8,12},{9,13},{10,... | collective-permute-start | bytes 294920 | tf_op jit(solution)/shard_map/ppermute | solution.py:79
  86.0 7.8 %collective-permute-start.28 = (bf16[96,512]{1,0:T(8,128)(2,1)S(1)}, bf16[96,512]{1,0:T(8,128)(2,1)S(1)}, u32[]{:S(2)}, u32[]{:S(2)}) collective-permute-start(bf16[96,512]{1,0:T(8,128)(2,1)S(1)} %maximum_maximum_fusion.8), channel_id=1, source_target_pairs={{0,6},{1,7},{2,4},{3,5},{4,2},{5,3},{6,0},{7,1},{8,14},{9,15},{10,... | collective-permute-start | bytes 294920 | tf_op jit(solution)/shard_map/ppermute | solution.py:79

commit v3 on v2

v3 whole, which is shorter than its diff:
```python
import functools

import jax
import jax.numpy as jnp
from jax import lax
from jax.experimental import pallas as pl
from jax.experimental.pallas import tpu as pltpu
from jax.sharding import PartitionSpec as P

EPSILON = 1e-06
CORES = 2
ROW_TILE = 16
VMEM_LIMIT = 24 * 1024 * 1024
BF16, F32 = jnp.bfloat16, jnp.float32


def nn(a, b):
    return lax.dot_general(a, b, (((1,), (0,)), ((), ())), preferred_element_type=F32)


def nt(a, b):
    return lax.dot_general(a, b, (((1,), (1,)), ((), ())), preferred_element_type=F32)


def tn(a, b):
    return lax.dot_general(a, b, (((0,), (0,)), ((), ())), preferred_element_type=F32)


def silu_parts(hidden):
    sigmoid_value = jax.nn.sigmoid(hidden)
    silu_value = hidden * sigmoid_value
    silu_slope = sigmoid_value * (1.0 + hidden * (1.0 - sigmoid_value))
    curvature = sigmoid_value * (1.0 - sigmoid_value) * (2.0 + hidden * (1.0 - 2.0 * sigmoid_value))
    return silu_value, silu_slope, curvature


def partner(index, step, count):
    return index ^ step if count & (count - 1) == 0 else (index + step) % count


def source(index, step, count):
    return index ^ step if count & (count - 1) == 0 else (index + count - step) % count


def chip_perm(count, step):
    chips = count // CORES
    return [(t, partner(t // CORES, step, chips) * CORES + t % CORES) for t in range(count)]


def core_perm(count):
    return [(t, t ^ 1) for t in range(count)]


def pack(gate, up, down):
    folds = gate.shape[1] // down.shape[1]
    rows = down.shape[0] // folds
    down = jnp.concatenate([down[i * rows : (i + 1) * rows] for i in range(folds)], axis=1)
    return jnp.concatenate([gate, up, down], axis=0)


def unpack(packed, fh):
    g = packed.shape[0] // 3
    folds = packed.shape[1] // fh
    down = packed[2 * g :]
    down = jnp.concatenate([down[:, i * fh : (i + 1) * fh] for i in range(folds)], axis=0)
    return packed[:g], packed[g : 2 * g], down


def update_forward(w1t, w3t, w2, keys, push):
    gate_pre, up_pre = nt(w1t, keys), nt(w3t, keys)
    silu, slope, curvature = silu_parts(gate_pre)
    mixed = (silu * up_pre).astype(BF16)
    down_back = nn(w2, push)
    back_slope = down_back * slope
    gate_back = (down_back * up_pre * slope).astype(BF16)
    up_back = (down_back * silu).astype(BF16)
    return up_pre, silu, slope, curvature, mixed, down_back, back_slope, gate_back, up_back


def apply_forward(f1t, f3t, f2t, queries, weighted):
    q_gate, q_up = nt(f1t, queries), nt(f3t, queries)
    silu, slope, _ = silu_parts(q_gate)
    mixed = (silu * q_up).astype(BF16)
    output = nn(f2t, mixed)
    square = jnp.sum(output * output, axis=0, keepdims=True)
    dot = jnp.sum(weighted * output, axis=0, keepdims=True)
    return output, mixed, q_up * slope, silu, jnp.concatenate([square, dot], axis=0)


def apply_backward(f2t, sums, full_width, output, weighted, mixed, up_slope, silu, queries):
    inverse = lax.rsqrt(sums[0:1] / full_width + EPSILON)
    scale = inverse * inverse * inverse * sums[1:2] / full_width
    out_back = (inverse * weighted - output * scale).astype(BF16)
    q_back = tn(f2t, out_back)
    gate_back = (q_back * up_slope).astype(BF16)
    up_back = (q_back * silu).astype(BF16)
    return gate_back, up_back, nn(gate_back, queries), nn(up_back, queries), nt(out_back, mixed)


def second_adjoint(c1t, c3t, c2t, keys, push, up_slope, silu, back_slope, back_curve):
    gate_bar, up_bar, mixed_bar = nt(c1t, keys), nt(c3t, keys), tn(c2t, push)
    down_back_bar = (gate_bar * up_slope + up_bar * silu).astype(BF16)
    up_pre_bar = (gate_bar * back_slope + mixed_bar * silu).astype(BF16)
    gate_pre_bar = (up_bar * back_slope + mixed_bar * up_slope + gate_bar * back_curve).astype(BF16)
    return (
        down_back_bar,
        up_pre_bar,
        gate_pre_bar,
        nn(gate_pre_bar, keys),
        nn(up_pre_bar, keys),
        nt(push, down_back_bar),
    )


def push_of(rates, values):
    return (-rates * values.T.astype(F32)).astype(BF16)


def both(own_ref, other_ref, axis=0):
    return jnp.concatenate([own_ref[...], other_ref[...]], axis=axis)


def send_pieces(chips, gate_ref, up_ref, down_ref, outs):
    tok = lax.axis_index("tok")
    chip, core = tok // CORES, tok % CORES
    g = gate_ref.shape[0] // (chips * CORES)
    d = down_ref.shape[0] // (chips * CORES)
    fh = down_ref.shape[1]
    for step, out in enumerate(outs):
        t = partner(chip, step, chips) * CORES + core
        out[:g] = gate_ref[pl.ds(pl.multiple_of(t * g, g), g), :].astype(out.dtype)
        out[g : 2 * g] = up_ref[pl.ds(pl.multiple_of(t * g, g), g), :].astype(out.dtype)
        for i in range(d // g):
            rows = pl.ds(pl.multiple_of(t * d + i * g, g), g)
            out[2 * g :, i * fh : (i + 1) * fh] = down_ref[rows, :].astype(out.dtype)


def place_pieces(chips, pieces, gate_ref, up_ref, down_ref):
    tok = lax.axis_index("tok")
    chip, core = tok // CORES, tok % CORES
    g = gate_ref.shape[0] // (chips * CORES)
    d = down_ref.shape[0] // (chips * CORES)
    fh = down_ref.shape[1]
    for step in range(chips):
        first = source(chip, step, chips) * CORES
        for piece, t in ((pieces[2 * step], first + core), (pieces[2 * step + 1], first + 1 - core)):
            gate_ref[pl.ds(pl.multiple_of(t * g, g), g), :] = piece[:g]
            up_ref[pl.ds(pl.multiple_of(t * g, g), g), :] = piece[g : 2 * g]
            for i in range(d // g):
                rows = pl.ds(pl.multiple_of(t * d + i * g, g), g)
                down_ref[rows, :] = piece[2 * g :, i * fh : (i + 1) * fh]


def update_kernel(chips, ko, kx, vo, vx, ro, rx, w1t, w3t, w2, *rest):
    outs, (gate, up, down) = rest[:chips], rest[chips:]
    keys = both(ko, kx)
    push = push_of(both(ro, rx, 1), both(vo, vx))
    *_, mixed, _, _, gate_back, up_back = update_forward(w1t[...], w3t[...], w2[...], keys, push)
    down[...] = nt(push, mixed)
    gate[...] = nn(gate_back, keys)
    up[...] = nn(up_back, keys)
    send_pieces(chips, gate, up, down, outs)


def saved_kernel(
    ko, kx, vo, vx, ro, rx, w1t, w3t, w2, go, gx, gain,
    push_ref, up_slope_ref, silu_ref, back_slope_ref, back_curve_ref,
    mixed_ref, gate_back_ref, up_back_ref, weighted_ref,
):
    push = push_of(both(ro, rx, 1), both(vo, vx))
    push_ref[...] = push
    up_pre, silu, slope, curvature, mixed, down_back, back_slope, gate_back, up_back = (
        update_forward(w1t[...], w3t[...], w2[...], both(ko, kx), push)
    )
    up_slope_ref[...] = up_pre * slope
    silu_ref[...] = silu
    back_slope_ref[...] = back_slope
    back_curve_ref[...] = down_back * up_pre * curvature
    own = mixed_ref.shape[1]
    mixed_ref[...] = mixed[:, :own]
    gate_back_ref[...] = gate_back[:, :own]
    up_back_ref[...] = up_back[:, :own]
    weighted_ref[...] = both(go, gx).T.astype(F32) * gain[...]


def apply_kernel(chips, *refs):
    pieces, refs = refs[: 2 * chips], refs[2 * chips :]
    qo, qx, weighted, f1t, f3t, f2t, output, mixed, up_slope, silu, sums = refs
    place_pieces(chips, pieces, f1t, f3t, f2t)
    output[...], mixed[...], up_slope[...], silu[...], sums[...] = apply_forward(
        f1t[...], f3t[...], f2t[...], both(qo, qx), weighted[...]
    )


def back_kernel(chips, heads, *refs):
    sums = sum(r[...] for r in refs[1:heads]) + refs[0][...]
    f2t, output, weighted, mixed, up_slope, silu, qo, qx, gate_back, up_back = refs[heads : heads + 10]
    outs, (gate, up, down) = refs[heads + 10 : heads + 10 + chips], refs[heads + 10 + chips :]
    width = heads * output.shape[0]
    gb, ub, gate[...], up[...], down[...] = apply_backward(
        f2t[...], sums, width, output[...], weighted[...], mixed[...], up_slope[...], silu[...],
        both(qo, qx),
    )
    send_pieces(chips, gate, up, down, outs)
    own = gate_back.shape[1]
    gate_back[...], up_back[...] = gb[:, :own], ub[:, :own]


def query_kernel(gate_back, up_back, f1t, f3t, out):
    out[...] = (tn(gate_back[...], f1t[...]) + tn(up_back[...], f3t[...])).astype(BF16)


def second_kernel(chips, *refs):
    pieces, refs = refs[: 2 * chips], refs[2 * chips :]
    ko, kx, push, up_slope, silu, back_slope, back_curve = refs[:7]
    c1t, c3t, c2t, dbb_ref, upb_ref, gpb_ref = refs[7:13]
    outs, (gate, up, down) = refs[13 : 13 + chips], refs[13 + chips :]
    place_pieces(chips, pieces, c1t, c3t, c2t)
    dbb, upb, gpb, gate[...], up[...], down[...] = second_adjoint(
        c1t[...], c3t[...], c2t[...], both(ko, kx), push[...],
        up_slope[...], silu[...], back_slope[...], back_curve[...],
    )
    send_pieces(chips, gate, up, down, outs)
    own = dbb_ref.shape[1]
    dbb_ref[...], upb_ref[...], gpb_ref[...] = dbb[:, :own], upb[:, :own], gpb[:, :own]


def token_grads(rates, mixed, dbb, upb, gpb, gate_back, up_back, c1t, c3t, c2t, w1t, w3t, w2):
    value_grad = (rates * (nn(c2t, mixed) + tn(w2, dbb))).T.astype(BF16)
    key_total = tn(gate_back, c1t) + tn(up_back, c3t) + tn(gpb, w1t) + tn(upb, w3t)
    return value_grad, (-key_total).astype(BF16)


def token_kernel(*refs):
    value_grad, key_grad = refs[-2:]
    value_grad[...], key_grad[...] = token_grads(*(r[...] for r in refs[:-2]))


def call(kernel, outs, args, scratch=(), name=None):
    vmem = pl.BlockSpec(memory_space=pltpu.VMEM)
    return pl.pallas_call(
        kernel,
        out_shape=[jax.ShapeDtypeStruct(s, t) for s, t in outs],
        in_specs=[vmem] * len(args),
        out_specs=[vmem] * len(outs),
        scratch_shapes=[pltpu.VMEM(s, t) for s, t in scratch],
        compiler_params=pltpu.CompilerParams(vmem_limit_bytes=VMEM_LIMIT),
        name=name,
    )(*args)


def exchange_sum(pieces, chips):
    count = chips * CORES
    got = {s: lax.ppermute(pieces[s], "tok", chip_perm(count, s)) for s in reversed(range(1, chips))}
    total = pieces[0]
    for step in range(1, chips):
        total = total + got[step].astype(F32)
    return total


def gather(packed, chips):
    count = chips * CORES
    pieces = [None] * count
    for step in (0, *reversed(range(1, chips))):
        mine = packed if step == 0 else lax.ppermute(packed, "tok", chip_perm(count, step))
        pieces[2 * step] = mine
        pieces[2 * step + 1] = lax.ppermute(mine, "tok", core_perm(count))
    return pieces


def sliced_pieces(gate, up, down, tok, chips):
    chip, core = tok // CORES, tok % CORES
    g, d = gate.shape[0] // (chips * CORES), down.shape[0] // (chips * CORES)
    pieces = []
    for step in range(chips):
        t = partner(chip, step, chips) * CORES + core
        piece = pack(
            lax.dynamic_slice_in_dim(gate, t * g, g, 0),
            lax.dynamic_slice_in_dim(up, t * g, g, 0),
            lax.dynamic_slice_in_dim(down, t * d, d, 0),
        )
        pieces.append(piece if step == 0 else piece.astype(BF16))
    return pieces


def whole_matrices(pieces, tok, chips, fh):
    chip, core = tok // CORES, tok % CORES
    held = jnp.zeros((chips * CORES,) + pieces[0].shape, pieces[0].dtype)
    for step in range(chips):
        first = source(chip, step, chips) * CORES
        held = lax.dynamic_update_index_in_dim(held, pieces[2 * step], first + core, 0)
        held = lax.dynamic_update_index_in_dim(held, pieces[2 * step + 1], first + 1 - core, 0)
    parts = jax.vmap(lambda x: unpack(x, fh))(held)
    return tuple(x.reshape((-1, x.shape[-1])) for x in parts)


def norm_of(rows):
    return jnp.sqrt(jnp.sum(rows * rows, axis=1, keepdims=True) + EPSILON)


def per_device(
    query_input,
    key_input,
    value_input,
    out_grad,
    token_rates,
    out_gain,
    gate_prior,
    up_prior,
    down_prior,
):
    count, heads = lax.axis_size("tok"), lax.axis_size("head")
    tok = lax.axis_index("tok")
    chips = count // CORES
    own, dh = key_input.shape
    n = own * CORES
    w1t, w3t, w2 = gate_prior[0].T, up_prior[0].T, down_prior[0]
    fh = w2.shape[0]
    g, d = fh // count, dh // count
    tiled = g % ROW_TILE == 0 and d % g == 0 and dh // g == fh // g * (d // g)
    rates = token_rates.T
    gain = out_gain[:, None]

    pair = lambda x: lax.ppermute(x, "tok", core_perm(count))
    key_other, value_other, rate_other = pair(key_input), pair(value_input), pair(rates)
    query_other, grad_other = pair(query_input), pair(out_grad)
    messages = [((3 * g, dh), F32)] + [((3 * g, dh), BF16)] * (chips - 1)
    matrices = [((fh, dh), BF16), ((fh, dh), BF16), ((dh, fh), BF16)]
    sums_scratch = [((fh, dh), F32), ((fh, dh), F32), ((dh, fh), F32)]
    hidden = ((fh, n), F32)
    own_hidden = ((fh, own), BF16)
    joined = lambda a, b, axis=0: jnp.concatenate([a, b], axis=axis)

    inputs = (
        key_input, key_other, value_input, value_other, rates, rate_other, w1t, w3t, w2,
    )
    if tiled:
        pieces = call(
            functools.partial(update_kernel, chips), messages, inputs, sums_scratch, "update"
        )
        push, up_slope, silu, back_slope, back_curve, mixed, gate_back, up_back, weighted = call(
            saved_kernel,
            [((dh, n), BF16)] + [hidden] * 4 + [own_hidden] * 3 + [((dh, n), F32)],
            (*inputs, out_grad, grad_other, gain),
            name="saved",
        )
    else:
        keys = joined(key_input, key_other)
        queries = joined(query_input, query_other)
        push = push_of(joined(rates, rate_other, 1), joined(value_input, value_other))
        up_pre, silu, slope, curvature, mixed, down_back, back_slope, gate_back, up_back = (
            update_forward(w1t, w3t, w2, keys, push)
        )
        up_slope, back_curve = up_pre * slope, down_back * up_pre * curvature
        weighted = joined(out_grad, grad_other).T.astype(F32) * gain
        pieces = sliced_pieces(nn(gate_back, keys), nn(up_back, keys), nt(push, mixed), tok, chips)
        mixed, gate_back, up_back = mixed[:, :own], gate_back[:, :own], up_back[:, :own]
    update = unpack(exchange_sum(pieces, chips), fh)

    priors = [
        lax.dynamic_slice_in_dim(x, tok * rows, rows, 0).astype(F32)
        for x, rows in ((w1t, g), (w3t, g), (w2.T, d))
    ]
    moved = [p - u for p, u in zip(priors, update)]
    prior_norm = [norm_of(p) for p in priors]
    moved_norm = [norm_of(m) for m in moved]
    fast = [(m * (p / q)).astype(BF16) for m, p, q in zip(moved, prior_norm, moved_norm)]
    pieces = gather(pack(*fast), chips)

    if tiled:
        f1t, f3t, f2t, output, q_mixed, q_slope, q_silu, part = call(
            functools.partial(apply_kernel, chips),
            matrices + [((dh, n), F32), ((fh, n), BF16), hidden, hidden, ((2, n), F32)],
            (*pieces, query_input, query_other, weighted),
            name="apply",
        )
    else:
        f1t, f3t, f2t = whole_matrices(pieces, tok, chips, fh)
        output, q_mixed, q_slope, q_silu, part = apply_forward(f1t, f3t, f2t, queries, weighted)
    sums = [part] + [
        lax.ppermute(part, "head", [(h, partner(h, step, heads)) for h in range(heads)])
        for step in range(1, heads)
    ]
    if tiled:
        q_gate_back, q_up_back, *pieces = call(
            functools.partial(back_kernel, chips, heads),
            [own_hidden] * 2 + messages,
            (*sums, f2t, output, weighted, q_mixed, q_slope, q_silu, query_input, query_other),
            sums_scratch,
            "apply_back",
        )
        (query_grad,) = call(
            query_kernel, [((own, dh), BF16)], (q_gate_back, q_up_back, f1t, f3t), name="query_grad"
        )
    else:
        q_gate_back, q_up_back, *grads = apply_backward(
            f2t, sum(sums[1:], sums[0]), heads * dh, output, weighted, q_mixed, q_slope, q_silu, queries
        )
        pieces = sliced_pieces(*grads, tok, chips)
        query_grad = (tn(q_gate_back[:, :own], f1t) + tn(q_up_back[:, :own], f3t)).astype(BF16)
    fast_grad = unpack(exchange_sum(pieces, chips), fh)

    cotangent, owned = [], []
    for p, m, pn, mn, fg in zip(priors, moved, prior_norm, moved_norm, fast_grad):
        column_dot = jnp.sum(fg * m, axis=1, keepdims=True)
        moved_grad = pn / mn * (fg - m * (column_dot / (mn * mn)))
        cotangent.append(moved_grad.astype(BF16))
        owned.append(moved_grad + p * (column_dot / (mn * pn)))
    pieces = gather(pack(*cotangent), chips)

    if tiled:
        c1t, c3t, c2t, dbb, upb, gpb, *pieces = call(
            functools.partial(second_kernel, chips),
            matrices + [own_hidden] * 3 + messages,
            (*pieces, key_input, key_other, push, up_slope, silu, back_slope, back_curve),
            sums_scratch,
            "second_adjoint",
        )
    else:
        c1t, c3t, c2t = whole_matrices(pieces, tok, chips, fh)
        dbb, upb, gpb, *bars = second_adjoint(
            c1t, c3t, c2t, keys, push, up_slope, silu, back_slope, back_curve
        )
        pieces = sliced_pieces(*bars, tok, chips)
        dbb, upb, gpb = dbb[:, :own], upb[:, :own], gpb[:, :own]
    token_args = (
        rates, mixed, dbb, upb, gpb, gate_back, up_back, c1t, c3t, c2t, w1t, w3t, w2,
    )
    if tiled:
        value_grad, key_grad = call(
            token_kernel, [((own, dh), BF16)] * 2, token_args, name="token_grads"
        )
    else:
        value_grad, key_grad = token_grads(*token_args)
    bars = unpack(exchange_sum(pieces, chips), fh)
    results = [(o - b).T[None] for o, b in zip(owned, bars)]
    return (query_grad, key_grad, value_grad, *results)


def solution(mesh):
    tokens = P("tok", "head")
    in_specs = (tokens,) * 5 + (P("head"),) + (P("head", None, None),) * 3
    out_specs = (tokens,) * 3 + (P("head", None, "tok"),) * 3
    return jax.shard_map(
        per_device, mesh=mesh, in_specs=in_specs, out_specs=out_specs, check_vma=False
    )
```

time: 95.7 us -> 82.7 us (0.86)
  matrix products: 14.8 us -> 0 us
  Pallas kernels: 0 us -> 8.71 us
  waiting for transfers between devices: 40.6 us -> 33.1 us
  local copies, waits for them, and re-layouts: 5.37 us -> 7.49 us
    dot_general x27 -> x0, matrix products: 14.8 us -> none  [the longest x9 5.53 us: tn(): lax.dot_general(a, b, (((0,), (0,)), ((), ())), preferred_element_type=jn...]
    pallas_call x0 -> x7, Pallas kernels: none -> 8.71 us  [call(): pl.pallas_call(kernel, out_shape=[jax.ShapeDtypeStruct(s, t) for s, t in...]
    ppermute x26, waiting for transfers between devices: 40.6 us -> 33.1 us  [the longest x9 17.1 us: exchange_sum(): lax.ppermute(pieces[s], 'tok', chip_perm(count, s))]
    unnamed x22 -> x61, local copies, waits for them, and re-layouts: 4.25 us -> 6.56 us
  transfers between devices with their start and end apart: 31 -> 31, of which waited for: 18 -> 15; matrix products, arithmetic and copies ran while one was open for 8% -> 3% of each run, Pallas kernels for 0% -> 6%
where the time goes in v3:
time: 82.7 us; the launch traced here: 82.3 us
  waiting for transfers between devices  33.1 us (40%)
  starting transfers between devices  29.2 us (35%)
  Pallas kernels  8.71 us (11%)
  local copies, waits for them, and re-layouts  7.49 us (9%)
  other arithmetic  2.56 us (3%)
  between operations  1.25 us (2%)
    ppermute x9, waiting for transfers between devices, exchange_sum(): lax.ppermute(pieces[s], 'tok', chip_perm(count, s))  17.1 us
    ppermute x9, starting transfers between devices, exchange_sum(): lax.ppermute(pieces[s], 'tok', chip_perm(count, s))  14.1 us
    ppermute x6, waiting for transfers between devices, gather(): lax.ppermute(packed, 'tok', chip_perm(count, step))  12 us
    ppermute x6, starting transfers between devices, gather(): lax.ppermute(packed, 'tok', chip_perm(count, step))  8.91 us
    pallas_call x7, Pallas kernels, call(): pl.pallas_call(kernel, out_shape=[jax.ShapeDtypeStruct(s, t) for s, t in...  8.71 us
    unnamed x61, local copies, waits for them, and re-layouts  6.56 us
    ppermute x3, starting transfers between devices, per_device(): lax.ppermute(part, 'head', [(h, partner(h, step, heads)) for h in range(h...  3.55 us
    ppermute x3, waiting for transfers between devices, per_device(): lax.ppermute(part, 'head', [(h, partner(h, step, heads)) for h in range(h...  3.08 us
  transfers between devices with their start and end apart: 31, of which 15 were waited for; matrix products, arithmetic and copies ran while one was open for 3% of the time, Pallas kernels for 6%

profile of v3, /device:TPU:0, one launch (start us, length us, event | category | flops | bytes accessed | tf_op | source)
XLA Modules:
  0.0 82.3 jit_solution(11429778582758936434)
XLA Ops:
  0.6 0.5 collective-permute-start.1
  2.3 1.1 %copy.20 = bf16[1,512,256]{1,2,0:T(8,128)(2,1)S(1)} copy(bf16[1,512,256]{2,1,0:T(8,128)(2,1)} %param.15) | data formatting | bytes 524288 | tf_op args[6]
  3.7 0.7 copy-done
  4.5 1.2 %update.1 = (f32[96,512]{1,0:T(8,128)S(1)}, bf16[96,512]{1,0:T(8,128)(2,1)S(1)}, bf16[96,512]{1,0:T(8,128)(2,1)S(1)}, bf16[96,512]{1,0:T(8,128)(2,1)S(1)}) custom-call(bf16[256,512]{1,0:T(8,128)(2,1)S(1)} %copy-done.1, bf16[256,512]{1,0:T(8,128)(2,1)S(1)} %collective-permute-done.kx.refs_9_, bf16[256,512]{1,0:T(8,128)(2,1)S(1)} %copy-done.3, ...), custom_call_target="tpu_custom_call" | custom-call | tf_op jit(solution)/shard_map/update/pallas_call | solution.py:241
  5.7 2.6 %collective-permute-start.3 = (bf16[96,512]{1,0:T(8,128)(2,1)S(1)}, bf16[96,512]{1,0:T(8,128)(2,1)S(1)}, u32[]{:S(2)}, u32[]{:S(2)}) collective-permute-start(bf16[96,512]{1,0:T(8,128)(2,1)S(1)} %get-tuple-element.46), channel_id=1, source_target_pairs={{0,2},{1,3},{2,0},{3,1},{4,6},{5,7},{6,4},{7,5},{8,10},{9,11},{10,... | collective-permute-start | bytes 294920 | tf_op jit(solution)/shard_map/ppermute | solution.py:254
  8.3 2.6 %collective-permute-start.4 = (bf16[96,512]{1,0:T(8,128)(2,1)S(1)}, bf16[96,512]{1,0:T(8,128)(2,1)S(1)}, u32[]{:S(2)}, u32[]{:S(2)}) collective-permute-start(bf16[96,512]{1,0:T(8,128)(2,1)S(1)} %get-tuple-element.47), channel_id=1, source_target_pairs={{0,4},{1,5},{2,6},{3,7},{4,0},{5,1},{6,2},{7,3},{8,12},{9,13},{10,... | collective-permute-start | bytes 294920 | tf_op jit(solution)/shard_map/ppermute | solution.py:254
  11.1 0.7 collective-permute-done.3
  11.8 7.3 %collective-permute-done.4 = bf16[96,512]{1,0:T(8,128)(2,1)S(1)} collective-permute-done((bf16[96,512]{1,0:T(8,128)(2,1)S(1)}, bf16[96,512]{1,0:T(8,128)(2,1)S(1)}, u32[]{:S(2)}, u32[]{:S(2)}) %collective-permute-start.4) | collective-permute-done | bytes 98336 | tf_op jit(solution)/shard_map/ppermute | solution.py:254
  20.8 2.6 %collective-permute-start.11 = (bf16[96,512]{1,0:T(8,128)(2,1)S(1)}, bf16[96,512]{1,0:T(8,128)(2,1)S(1)}, u32[]{:S(2)}, u32[]{:S(2)}) collective-permute-start(bf16[96,512]{1,0:T(8,128)(2,1)S(1)} %maximum_maximum_fusion.refs_0_), channel_id=1, source_target_pairs={{0,6},{1,7},{2,4},{3,5},{4,2},{5,3},{6,0},{7,1},{8,14},{9,15},{10,... | collective-permute-start | bytes 294920 | tf_op jit(solution)/shard_map/ppermute | solution.py:265
  23.4 0.9 %collective-permute-start.9 = (bf16[96,512]{1,0:T(8,128)(2,1)S(1)}, bf16[96,512]{1,0:T(8,128)(2,1)S(1)}, u32[]{:S(2)}, u32[]{:S(2)}) collective-permute-start(bf16[96,512]{1,0:T(8,128)(2,1)S(1)} %maximum_maximum_fusion.refs_0_), channel_id=1, source_target_pairs={{0,4},{1,5},{2,6},{3,7},{4,0},{5,1},{6,2},{7,3},{8,12},{9,13},{10,... | collective-permute-start | bytes 294920 | tf_op jit(solution)/shard_map/ppermute | solution.py:265
  24.3 1.0 %collective-permute-start.7 = (bf16[96,512]{1,0:T(8,128)(2,1)S(1)}, bf16[96,512]{1,0:T(8,128)(2,1)S(1)}, u32[]{:S(2)}, u32[]{:S(2)}) collective-permute-start(bf16[96,512]{1,0:T(8,128)(2,1)S(1)} %maximum_maximum_fusion.refs_0_), channel_id=1, source_target_pairs={{0,2},{1,3},{2,0},{3,1},{4,6},{5,7},{6,4},{7,5},{8,10},{9,11},{10,... | collective-permute-start | bytes 294920 | tf_op jit(solution)/shard_map/ppermute | solution.py:265
  25.3 2.9 %collective-permute-done.11.refs_6_ = bf16[96,512]{1,0:T(8,128)(2,1)S(1)} collective-permute-done((bf16[96,512]{1,0:T(8,128)(2,1)S(1)}, bf16[96,512]{1,0:T(8,128)(2,1)S(1)}, u32[]{:S(2)}, u32[]{:S(2)}) %collective-permute-start.11) | collective-permute-done | bytes 98336 | tf_op jit(solution)/shard_map/ppermute | solution.py:265
  28.2 4.4 %collective-permute-done.9.refs_4_ = bf16[96,512]{1,0:T(8,128)(2,1)S(1)} collective-permute-done((bf16[96,512]{1,0:T(8,128)(2,1)S(1)}, bf16[96,512]{1,0:T(8,128)(2,1)S(1)}, u32[]{:S(2)}, u32[]{:S(2)}) %collective-permute-start.9) | collective-permute-done | bytes 98336 | tf_op jit(solution)/shard_map/ppermute | solution.py:265
  32.6 0.5 collective-permute-start.8
  33.1 0.8 copy.25.gain
  33.9 1.0 %saved.1 = (bf16[512,512]{1,0:T(8,128)(2,1)S(1)}, f32[256,512]{1,0:T(8,128)S(1)}, f32[256,512]{1,0:T(8,128)S(1)}, f32[256,512]{1,0:T(8,128)S(1)}, f32[256,512]{1...) custom-call(bf16[256,512]{1,0:T(8,128)(2,1)S(1)} %copy-done.1, ...), custom_call_target="tpu_custom_call" | custom-call | tf_op jit(solution)/shard_map/saved/pallas_call | solution.py:241
  35.0 1.8 %apply.1 = (bf16[256,512]{1,0:T(8,128)(2,1)S(1)}, bf16[256,512]{1,0:T(8,128)(2,1)S(1)}, bf16[512,256]{1,0:T(8,128)(2,1)S(1)}, f32[512,512]{1,0:T(8,128)S(1)}, bf...) custom-call(bf16[96,512]{1,0:T(8,128)(2,1)S(1)} %maximum_maximum_fusion.refs, ...), custom_call_target="tpu_custom_call" | custom-call | tf_op jit(solution)/shard_map/apply/pallas_call | solution.py:241
  36.8 2.5 %collective-permute-start.17 = (f32[2,512]{1,0:T(2,128)S(1)}, f32[2,512]{1,0:T(2,128)S(1)}, u32[]{:S(2)}, u32[]{:S(2)}) collective-permute-start(f32[2,512]{1,0:T(2,128)S(1)} %get-tuple-element.50.refs_0_), channel_id=1, source_target_pairs={{0,24},{8,16},{16,8},{24,0},{1,25},{9,17},{17,9},{25,1},{2,26},{10... | collective-permute-start | bytes 12296 | tf_op jit(solution)/shard_map/ppermute | solution.py:381
  39.3 0.5 collective-permute-start.16
  39.8 0.5 collective-permute-start.15
  40.3 1.0 %collective-permute-done.17.refs_3_ = f32[2,512]{1,0:T(2,128)S(1)} collective-permute-done((f32[2,512]{1,0:T(2,128)S(1)}, f32[2,512]{1,0:T(2,128)S(1)}, u32[]{:S(2)}, u32[]{:S(2)}) %collective-permute-start.17) | collective-permute-done | bytes 4128 | tf_op jit(solution)/shard_map/ppermute | solution.py:381
  41.4 1.6 %collective-permute-done.16.refs_2_ = f32[2,512]{1,0:T(2,128)S(1)} collective-permute-done((f32[2,512]{1,0:T(2,128)S(1)}, f32[2,512]{1,0:T(2,128)S(1)}, u32[]{:S(2)}, u32[]{:S(2)}) %collective-permute-start.16) | collective-permute-done | bytes 4128 | tf_op jit(solution)/shard_map/ppermute | solution.py:381
  42.9 0.5 collective-permute-done.15.refs_1_
  43.4 0.9 %apply_back.1 = (bf16[256,256]{1,0:T(8,128)(2,1)S(1)}, bf16[256,256]{1,0:T(8,128)(2,1)S(1)}, f32[96,512]{1,0:T(8,128)S(1)}, bf16[96,512]{1,0:T(8,128)(2,1)S(1)},...) custom-call(f32[2,512]{1,0:T(2,128)S(1)} %get-tuple-element.50.refs_0_, ...), custom_call_target="tpu_custom_call" | custom-call | tf_op jit(solution)/shard_map/apply_back/pallas_call | solution.py:241
  44.4 2.9 %collective-permute-start.19 = (bf16[96,512]{1,0:T(8,128)(2,1)S(1)}, bf16[96,512]{1,0:T(8,128)(2,1)S(1)}, u32[]{:S(2)}, u32[]{:S(2)}) collective-permute-start(bf16[96,512]{1,0:T(8,128)(2,1)S(1)} %get-tuple-element.63), channel_id=1, source_target_pairs={{0,4},{1,5},{2,6},{3,7},{4,0},{5,1},{6,2},{7,3},{8,12},{9,13},{10,... | collective-permute-start | bytes 294920 | tf_op jit(solution)/shard_map/ppermute | solution.py:254
  47.3 1.5 %collective-permute-start.20 = (bf16[96,512]{1,0:T(8,128)(2,1)S(1)}, bf16[96,512]{1,0:T(8,128)(2,1)S(1)}, u32[]{:S(2)}, u32[]{:S(2)}) collective-permute-start(bf16[96,512]{1,0:T(8,128)(2,1)S(1)} %get-tuple-element.64), channel_id=1, source_target_pairs={{0,6},{1,7},{2,4},{3,5},{4,2},{5,3},{6,0},{7,1},{8,14},{9,15},{10,... | collective-permute-start | bytes 294920 | tf_op jit(solution)/shard_map/ppermute | solution.py:254
  49.0 3.6 %collective-permute-done.19 = bf16[96,512]{1,0:T(8,128)(2,1)S(1)} collective-permute-done((bf16[96,512]{1,0:T(8,128)(2,1)S(1)}, bf16[96,512]{1,0:T(8,128)(2,1)S(1)}, u32[]{:S(2)}, u32[]{:S(2)}) %collective-permute-start.19) | collective-permute-done | bytes 98336 | tf_op jit(solution)/shard_map/ppermute | solution.py:254
  52.7 1.2 %collective-permute-done.20 = bf16[96,512]{1,0:T(8,128)(2,1)S(1)} collective-permute-done((bf16[96,512]{1,0:T(8,128)(2,1)S(1)}, bf16[96,512]{1,0:T(8,128)(2,1)S(1)}, u32[]{:S(2)}, u32[]{:S(2)}) %collective-permute-start.20) | collective-permute-done | bytes 98336 | tf_op jit(solution)/shard_map/ppermute | solution.py:254
  53.9 0.8 copy-done.7
  54.9 0.6 copy-done.26
  55.6 0.6 copy-done.22
  56.4 0.5 copy-done.18
  57.1 0.6 copy-done.16
  57.7 2.2 %collective-permute-start.26 = (bf16[96,512]{1,0:T(8,128)(2,1)S(1)}, bf16[96,512]{1,0:T(8,128)(2,1)S(1)}, u32[]{:S(2)}, u32[]{:S(2)}) collective-permute-start(bf16[96,512]{1,0:T(8,128)(2,1)S(1)} %maximum_maximum_fusion.1.refs_0_), channel_id=1, source_target_pairs={{0,6},{1,7},{2,4},{3,5},{4,2},{5,3},{6,0},{7,1},{8,14},{9,15},{10,... | collective-permute-start | bytes 294920 | tf_op jit(solution)/shard_map/ppermute | solution.py:265
  60.0 0.8 collective-permute-start.24
  60.8 1.4 %collective-permute-start.22 = (bf16[96,512]{1,0:T(8,128)(2,1)S(1)}, bf16[96,512]{1,0:T(8,128)(2,1)S(1)}, u32[]{:S(2)}, u32[]{:S(2)}) collective-permute-start(bf16[96,512]{1,0:T(8,128)(2,1)S(1)} %maximum_maximum_fusion.1.refs_0_), channel_id=1, source_target_pairs={{0,2},{1,3},{2,0},{3,1},{4,6},{5,7},{6,4},{7,5},{8,10},{9,11},{10,... | collective-permute-start | bytes 294920 | tf_op jit(solution)/shard_map/ppermute | solution.py:265
  62.2 2.1 %collective-permute-done.26.refs_6_ = bf16[96,512]{1,0:T(8,128)(2,1)S(1)} collective-permute-done((bf16[96,512]{1,0:T(8,128)(2,1)S(1)}, bf16[96,512]{1,0:T(8,128)(2,1)S(1)}, u32[]{:S(2)}, u32[]{:S(2)}) %collective-permute-start.26) | collective-permute-done | bytes 98336 | tf_op jit(solution)/shard_map/ppermute | solution.py:265
  64.3 2.6 %collective-permute-done.24.refs_4_ = bf16[96,512]{1,0:T(8,128)(2,1)S(1)} collective-permute-done((bf16[96,512]{1,0:T(8,128)(2,1)S(1)}, bf16[96,512]{1,0:T(8,128)(2,1)S(1)}, u32[]{:S(2)}, u32[]{:S(2)}) %collective-permute-start.24) | collective-permute-done | bytes 98336 | tf_op jit(solution)/shard_map/ppermute | solution.py:265
  66.9 0.5 collective-permute-start.23
  67.4 0.8 collective-permute-done.25.refs_5_
  68.4 1.4 %second_adjoint.1 = (bf16[256,512]{1,0:T(8,128)(2,1)S(1)}, bf16[256,512]{1,0:T(8,128)(2,1)S(1)}, bf16[512,256]{1,0:T(8,128)(2,1)S(1)}, bf16[256,256]{1,0:T(8,128...) custom-call(bf16[96,512]{1,0:T(8,128)(2,1)S(1)} %maximum_maximum_fus, ...), custom_call_target="tpu_custom_call" | custom-call | tf_op jit(solution)/shard_map/second_adjoint/pallas_call | solution.py:241
  69.9 2.7 %collective-permute-start.29 = (bf16[96,512]{1,0:T(8,128)(2,1)S(1)}, bf16[96,512]{1,0:T(8,128)(2,1)S(1)}, u32[]{:S(2)}, u32[]{:S(2)}) collective-permute-start(bf16[96,512]{1,0:T(8,128)(2,1)S(1)} %get-tuple-element.82), channel_id=1, source_target_pairs={{0,4},{1,5},{2,6},{3,7},{4,0},{5,1},{6,2},{7,3},{8,12},{9,13},{10,... | collective-permute-start | bytes 294920 | tf_op jit(solution)/shard_map/ppermute | solution.py:254
  72.6 1.7 %collective-permute-start.30 = (bf16[96,512]{1,0:T(8,128)(2,1)S(1)}, bf16[96,512]{1,0:T(8,128)(2,1)S(1)}, u32[]{:S(2)}, u32[]{:S(2)}) collective-permute-start(bf16[96,512]{1,0:T(8,128)(2,1)S(1)} %get-tuple-element.83), channel_id=1, source_target_pairs={{0,6},{1,7},{2,4},{3,5},{4,2},{5,3},{6,0},{7,1},{8,14},{9,15},{10,... | collective-permute-start | bytes 294920 | tf_op jit(solution)/shard_map/ppermute | solution.py:254
  74.3 1.0 %query_grad.1 = bf16[256,512]{1,0:T(8,128)(2,1)} custom-call(bf16[256,256]{1,0:T(8,128)(2,1)S(1)} %get-tuple-element.56.gate_back, bf16[256,256]{1,0:T(8,128)(2,1)S(1)} %get-tuple-element.57.up_back, bf16[256,512]{1,0:T(8,128)(2,1)S(1)} %get-tuple-element.58.f1t, bf16[256,512]{1,0:T(8,128)(2,1)S(1)} %get-tuple-element.59.f3t), custom_call_target="tpu_custom_call" | custom-call | tf_op jit(solution)/shard_map/query_grad/pallas_call | solution.py:241
  75.3 1.4 %token_grads.1 = (bf16[256,512]{1,0:T(8,128)(2,1)}, bf16[256,512]{1,0:T(8,128)(2,1)}) custom-call(f32[1,256]{1,0:T(1,128)S(1)} %bitcast.114, bf16[256,256]{1,0:T(8,128)(2,1)S(1)} %get-tuple-element.60.refs_1_, bf16[256,256]{1,0:T(8,128)(2,1)S(1)} %get-tuple-element.70.refs_2_, bf16[256,256]{1,0:T(8,128)(2,1)S(1)} %get-tuple-element.71.refs_3_, ...), custom_call_target="tpu_custom_call" | custom-call | tf_op jit(solution)/shard_map/token_grads/pallas_call | solution.py:241
  76.7 4.1 %collective-permute-done.29 = bf16[96,512]{1,0:T(8,128)(2,1)S(1)} collective-permute-done((bf16[96,512]{1,0:T(8,128)(2,1)S(1)}, bf16[96,512]{1,0:T(8,128)(2,1)S(1)}, u32[]{:S(2)}, u32[]{:S(2)}) %collective-permute-start.29) | collective-permute-done | bytes 98336 | tf_op jit(solution)/shard_map/ppermute | solution.py:254
  80.8 0.8 fusion
  81.6 0.7 fusion.2
  (110 shorter events, 4.4 us)
Async XLA Ops:
  0.6 3.0 %collective-permute-start.1 = (bf16[256,512]{1,0:T(8,128)(2,1)}, bf16[256,512]{1,0:T(8,128)(2,1)S(1)}, u32[]{:S(2)}, u32[]{:S(2)}) collective-permute-start(bf16[256,512]{1,0:T(8,128)(2,1)} %vo.3), channel_id=1, source_target_pairs={{0,1},{1,0},{2,3},{3,2},{4,5},{5,4},{6,7},{7,6},{8,9},{9,8},{10,11... | collective-permute-start | bytes 786440 | tf_op jit(solution)/shard_map/ppermute | solution.py:324
  1.2 2.5 %collective-permute-start = (bf16[256,512]{1,0:T(8,128)(2,1)}, bf16[256,512]{1,0:T(8,128)(2,1)S(1)}, u32[]{:S(2)}, u32[]{:S(2)}) collective-permute-start(bf16[256,512]{1,0:T(8,128)(2,1)} %refs_8_.3), channel_id=1, source_target_pairs={{0,1},{1,0},{2,3},{3,2},{4,5},{5,4},{6,7},{7,6},{8,9},{9,8},{10,11... | collective-permute-start | bytes 786440 | tf_op jit(solution)/shard_map/ppermute | solution.py:324
  1.3 2.3 %collective-permute-start.2 = (f32[1,256]{1,0:T(1,128)S(1)}, f32[1,256]{1,0:T(1,128)S(1)}, u32[]{:S(2)}, u32[]{:S(2)}) collective-permute-start(f32[1,256]{1,0:T(1,128)S(1)} %bitcast.111), channel_id=1, source_target_pairs={{0,1},{1,0},{2,3},{3,2},{4,5},{5,4},{6,7},{7,6},{8,9},{9,8},{10,11... | collective-permute-start | bytes 3080 | tf_op jit(solution)/shard_map/ppermute | solution.py:324
  1.8 23.5 %collective-permute-start.14 = (bf16[256,512]{1,0:T(8,128)(2,1)}, bf16[256,512]{1,0:T(8,128)(2,1)S(1)}, u32[]{:S(2)}, u32[]{:S(2)}) collective-permute-start(bf16[256,512]{1,0:T(8,128)(2,1)} %go.1), channel_id=1, source_target_pairs={{0,1},{1,0},{2,3},{3,2},{4,5},{5,4},{6,7},{7,6},{8,9},{9,8},{10,11... | collective-permute-start | bytes 786440 | tf_op jit(solution)/shard_map/ppermute | solution.py:324
  1.8 33.1 %collective-permute-start.13 = (bf16[256,512]{1,0:T(8,128)(2,1)}, bf16[256,512]{1,0:T(8,128)(2,1)S(1)}, u32[]{:S(2)}, u32[]{:S(2)}) collective-permute-start(bf16[256,512]{1,0:T(8,128)(2,1)} %refs_10_.1), channel_id=1, source_target_pairs={{0,1},{1,0},{2,3},{3,2},{4,5},{5,4},{6,7},{7,6},{8,9},{9,8},{10,11... | collective-permute-start | bytes 786440 | tf_op jit(solution)/shard_map/ppermute | solution.py:324
  2.3 1.2 %copy-start.14 = (bf16[1,512,256]{2,1,0:T(8,128)(2,1)S(1)}, bf16[1,512,256]{2,1,0:T(8,128)(2,1)}, u32[]{:S(2)}) copy-start(bf16[1,512,256]{2,1,0:T(8,128)(2,1)} %param.16) | copy-start | bytes 786436
  2.3 1.4 %copy-start.3 = (bf16[256,512]{1,0:T(8,128)(2,1)S(1)}, bf16[256,512]{1,0:T(8,128)(2,1)}, u32[]{:S(2)}) copy-start(bf16[256,512]{1,0:T(8,128)(2,1)} %vo.3) | copy-start | bytes 786436
  3.4 1.0 %copy-start = (bf16[1,256,512]{2,1,0:T(8,128)(2,1)S(1)}, bf16[1,256,512]{2,1,0:T(8,128)(2,1)}, u32[]{:S(2)}) copy-start(bf16[1,256,512]{2,1,0:T(8,128)(2,1)} %param.17) | copy-start | bytes 786436
  3.5 1.0 %copy-start.1 = (bf16[256,512]{1,0:T(8,128)(2,1)S(1)}, bf16[256,512]{1,0:T(8,128)(2,1)}, u32[]{:S(2)}) copy-start(bf16[256,512]{1,0:T(8,128)(2,1)} %refs_8_.3) | copy-start | bytes 786436
  5.7 6.1 %collective-permute-start.3 = (bf16[96,512]{1,0:T(8,128)(2,1)S(1)}, bf16[96,512]{1,0:T(8,128)(2,1)S(1)}, u32[]{:S(2)}, u32[]{:S(2)}) collective-permute-start(bf16[96,512]{1,0:T(8,128)(2,1)S(1)} %get-tuple-element.46), channel_id=1, source_target_pairs={{0,2},{1,3},{2,0},{3,1},{4,6},{5,7},{6,4},{7,5},{8,10},{9,11},{10,... | collective-permute-start | bytes 294920 | tf_op jit(solution)/shard_map/ppermute | solution.py:254
  8.3 10.7 %collective-permute-start.4 = (bf16[96,512]{1,0:T(8,128)(2,1)S(1)}, bf16[96,512]{1,0:T(8,128)(2,1)S(1)}, u32[]{:S(2)}, u32[]{:S(2)}) collective-permute-start(bf16[96,512]{1,0:T(8,128)(2,1)S(1)} %get-tuple-element.47), channel_id=1, source_target_pairs={{0,4},{1,5},{2,6},{3,7},{4,0},{5,1},{6,2},{7,3},{8,12},{9,13},{10,... | collective-permute-start | bytes 294920 | tf_op jit(solution)/shard_map/ppermute | solution.py:254
  10.9 8.2 %collective-permute-start.5 = (bf16[96,512]{1,0:T(8,128)(2,1)S(1)}, bf16[96,512]{1,0:T(8,128)(2,1)S(1)}, u32[]{:S(2)}, u32[]{:S(2)}) collective-permute-start(bf16[96,512]{1,0:T(8,128)(2,1)S(1)} %get-tuple-element.48), channel_id=1, source_target_pairs={{0,6},{1,7},{2,4},{3,5},{4,2},{5,3},{6,0},{7,1},{8,14},{9,15},{10,... | collective-permute-start | bytes 294920 | tf_op jit(solution)/shard_map/ppermute | solution.py:254
  11.1 8.9 %copy-start.8 = (bf16[1,256,64]{1,2,0:T(8,128)(2,1)}, bf16[1,256,64]{1,2,0:T(8,128)(2,1)S(1)}, u32[]{:S(2)}) copy-start(bf16[1,256,64]{1,2,0:T(8,128)(2,1)S(1)} %copy.26) | copy-start | bytes 98308
  19.1 0.9 %copy-start.10 = (f32[32,256]{1,0:T(8,128)}, f32[32,256]{1,0:T(8,128)S(1)}, u32[]{:S(2)}) copy-start(f32[32,256]{1,0:T(8,128)S(1)} %get-tuple-element.105) | copy-start | bytes 98308
  19.1 0.9 %copy-start.12 = (f32[32,256]{1,0:T(8,128)}, f32[32,256]{1,0:T(8,128)S(1)}, u32[]{:S(2)}) copy-start(f32[32,256]{1,0:T(8,128)S(1)} %get-tuple-element.106) | copy-start | bytes 98308
  19.3 0.8 copy-start.21
  19.3 0.8 copy-start.25
  19.4 0.8 copy-start.27
  19.4 0.8 %copy-start.6 = (f32[32,512]{1,0:T(8,128)}, f32[32,512]{1,0:T(8,128)S(1)}, u32[]{:S(2)}) copy-start(f32[32,512]{1,0:T(8,128)S(1)} %get-tuple-element.98) | copy-start | bytes 196612
  20.8 13.2 %copy-start.4 = (bf16[256,512]{1,0:T(8,128)(2,1)S(1)}, bf16[256,512]{1,0:T(8,128)(2,1)}, u32[]{:S(2)}) copy-start(bf16[256,512]{1,0:T(8,128)(2,1)} %go.1) | copy-start | bytes 786436
  20.8 7.4 %collective-permute-start.11 = (bf16[96,512]{1,0:T(8,128)(2,1)S(1)}, bf16[96,512]{1,0:T(8,128)(2,1)S(1)}, u32[]{:S(2)}, u32[]{:S(2)}) collective-permute-start(bf16[96,512]{1,0:T(8,128)(2,1)S(1)} %maximum_maximum_fusion.refs_0_), channel_id=1, source_target_pairs={{0,6},{1,7},{2,4},{3,5},{4,2},{5,3},{6,0},{7,1},{8,14},{9,15},{10,... | collective-permute-start | bytes 294920 | tf_op jit(solution)/shard_map/ppermute | solution.py:265
  23.4 9.2 %collective-permute-start.9 = (bf16[96,512]{1,0:T(8,128)(2,1)S(1)}, bf16[96,512]{1,0:T(8,128)(2,1)S(1)}, u32[]{:S(2)}, u32[]{:S(2)}) collective-permute-start(bf16[96,512]{1,0:T(8,128)(2,1)S(1)} %maximum_maximum_fusion.refs_0_), channel_id=1, source_target_pairs={{0,4},{1,5},{2,6},{3,7},{4,0},{5,1},{6,2},{7,3},{8,12},{9,13},{10,... | collective-permute-start | bytes 294920 | tf_op jit(solution)/shard_map/ppermute | solution.py:265
  24.3 8.3 %collective-permute-start.7 = (bf16[96,512]{1,0:T(8,128)(2,1)S(1)}, bf16[96,512]{1,0:T(8,128)(2,1)S(1)}, u32[]{:S(2)}, u32[]{:S(2)}) collective-permute-start(bf16[96,512]{1,0:T(8,128)(2,1)S(1)} %maximum_maximum_fusion.refs_0_), channel_id=1, source_target_pairs={{0,2},{1,3},{2,0},{3,1},{4,6},{5,7},{6,4},{7,5},{8,10},{9,11},{10,... | collective-permute-start | bytes 294920 | tf_op jit(solution)/shard_map/ppermute | solution.py:265
  25.3 9.7 %collective-permute-start.6 = (bf16[96,512]{1,0:T(8,128)(2,1)S(1)}, bf16[96,512]{1,0:T(8,128)(2,1)S(1)}, u32[]{:S(2)}, u32[]{:S(2)}) collective-permute-start(bf16[96,512]{1,0:T(8,128)(2,1)S(1)} %maximum_maximum_fusion.refs_0_), channel_id=1, source_target_pairs={{0,1},{1,0},{2,3},{3,2},{4,5},{5,4},{6,7},{7,6},{8,9},{9,8},{10,11... | collective-permute-start | bytes 294920 | tf_op jit(solution)/shard_map/ppermute | solution.py:267
  28.2 6.8 %collective-permute-start.12 = (bf16[96,512]{1,0:T(8,128)(2,1)S(1)}, bf16[96,512]{1,0:T(8,128)(2,1)S(1)}, u32[]{:S(2)}, u32[]{:S(2)}) collective-permute-start(bf16[96,512]{1,0:T(8,128)(2,1)S(1)} %collective-permute-done.11.refs_6_), channel_id=1, source_target_pairs={{0,1},{1,0},{2,3},{3,2},{4,5},{5,4},{6,7},{7,6},{8,9},{9,8},{10,11... | collective-permute-start | bytes 294920 | tf_op jit(solution)/shard_map/ppermute | solution.py:267
  32.6 2.4 %collective-permute-start.10 = (bf16[96,512]{1,0:T(8,128)(2,1)S(1)}, bf16[96,512]{1,0:T(8,128)(2,1)}, u32[]{:S(2)}, u32[]{:S(2)}) collective-permute-start(bf16[96,512]{1,0:T(8,128)(2,1)S(1)} %collective-permute-done.9.refs_4_), channel_id=1, source_target_pairs={{0,1},{1,0},{2,3},{3,2},{4,5},{5,4},{6,7},{7,6},{8,9},{9,8},{10,11... | collective-permute-start | bytes 294920 | tf_op jit(solution)/shard_map/ppermute | solution.py:267
  32.6 2.4 %collective-permute-start.8 = (bf16[96,512]{1,0:T(8,128)(2,1)S(1)}, bf16[96,512]{1,0:T(8,128)(2,1)}, u32[]{:S(2)}, u32[]{:S(2)}) collective-permute-start(bf16[96,512]{1,0:T(8,128)(2,1)S(1)} %collective-permute-done.7.refs_2_), channel_id=1, source_target_pairs={{0,1},{1,0},{2,3},{3,2},{4,5},{5,4},{6,7},{7,6},{8,9},{9,8},{10,11... | collective-permute-start | bytes 294920 | tf_op jit(solution)/shard_map/ppermute | solution.py:267
  33.9 1.1 %copy-start.2 = (bf16[256,512]{1,0:T(8,128)(2,1)S(1)}, bf16[256,512]{1,0:T(8,128)(2,1)}, u32[]{:S(2)}) copy-start(bf16[256,512]{1,0:T(8,128)(2,1)} %refs_10_.1) | copy-start | bytes 786436
  36.8 4.6 %collective-permute-start.17 = (f32[2,512]{1,0:T(2,128)S(1)}, f32[2,512]{1,0:T(2,128)S(1)}, u32[]{:S(2)}, u32[]{:S(2)}) collective-permute-start(f32[2,512]{1,0:T(2,128)S(1)} %get-tuple-element.50.refs_0_), channel_id=1, source_target_pairs={{0,24},{8,16},{16,8},{24,0},{1,25},{9,17},{17,9},{25,1},{2,26},{10... | collective-permute-start | bytes 12296 | tf_op jit(solution)/shard_map/ppermute | solution.py:381
  39.3 3.6 %collective-permute-start.16 = (f32[2,512]{1,0:T(2,128)S(1)}, f32[2,512]{1,0:T(2,128)S(1)}, u32[]{:S(2)}, u32[]{:S(2)}) collective-permute-start(f32[2,512]{1,0:T(2,128)S(1)} %get-tuple-element.50.refs_0_), channel_id=1, source_target_pairs={{0,16},{8,24},{16,0},{24,8},{1,17},{9,25},{17,1},{25,9},{2,18},{10... | collective-permute-start | bytes 12296 | tf_op jit(solution)/shard_map/ppermute | solution.py:381
  39.8 3.6 %collective-permute-start.15 = (f32[2,512]{1,0:T(2,128)S(1)}, f32[2,512]{1,0:T(2,128)S(1)}, u32[]{:S(2)}, u32[]{:S(2)}) collective-permute-start(f32[2,512]{1,0:T(2,128)S(1)} %get-tuple-element.50.refs_0_), channel_id=1, source_target_pairs={{0,8},{8,0},{16,24},{24,16},{1,9},{9,1},{17,25},{25,17},{2,10},{10... | collective-permute-start | bytes 12296 | tf_op jit(solution)/shard_map/ppermute | solution.py:381
  44.3 4.7 %collective-permute-start.18 = (bf16[96,512]{1,0:T(8,128)(2,1)S(1)}, bf16[96,512]{1,0:T(8,128)(2,1)S(1)}, u32[]{:S(2)}, u32[]{:S(2)}) collective-permute-start(bf16[96,512]{1,0:T(8,128)(2,1)S(1)} %get-tuple-element.62), channel_id=1, source_target_pairs={{0,2},{1,3},{2,0},{3,1},{4,6},{5,7},{6,4},{7,5},{8,10},{9,11},{10,... | collective-permute-start | bytes 294920 | tf_op jit(solution)/shard_map/ppermute | solution.py:254
  44.4 8.2 %collective-permute-start.19 = (bf16[96,512]{1,0:T(8,128)(2,1)S(1)}, bf16[96,512]{1,0:T(8,128)(2,1)S(1)}, u32[]{:S(2)}, u32[]{:S(2)}) collective-permute-start(bf16[96,512]{1,0:T(8,128)(2,1)S(1)} %get-tuple-element.63), channel_id=1, source_target_pairs={{0,4},{1,5},{2,6},{3,7},{4,0},{5,1},{6,2},{7,3},{8,12},{9,13},{10,... | collective-permute-start | bytes 294920 | tf_op jit(solution)/shard_map/ppermute | solution.py:254
  47.3 6.5 %collective-permute-start.20 = (bf16[96,512]{1,0:T(8,128)(2,1)S(1)}, bf16[96,512]{1,0:T(8,128)(2,1)S(1)}, u32[]{:S(2)}, u32[]{:S(2)}) collective-permute-start(bf16[96,512]{1,0:T(8,128)(2,1)S(1)} %get-tuple-element.64), channel_id=1, source_target_pairs={{0,6},{1,7},{2,4},{3,5},{4,2},{5,3},{6,0},{7,1},{8,14},{9,15},{10,... | collective-permute-start | bytes 294920 | tf_op jit(solution)/shard_map/ppermute | solution.py:254
  53.8 0.8 %copy-start.7 = (f32[32,512]{1,0:T(8,128)S(1)}, f32[32,512]{1,0:T(8,128)}, u32[]{:S(2)}) copy-start(f32[32,512]{1,0:T(8,128)} %copy-done.6) | copy-start | bytes 196612
  54.8 1.4 %copy-start.9 = (bf16[1,256,64]{1,2,0:T(8,128)(2,1)S(1)}, bf16[1,256,64]{1,2,0:T(8,128)(2,1)}, u32[]{:S(2)}) copy-start(bf16[1,256,64]{1,2,0:T(8,128)(2,1)} %copy-done.8) | copy-start | bytes 98308
  54.8 1.4 %copy-start.11 = (f32[32,256]{1,0:T(8,128)S(1)}, f32[32,256]{1,0:T(8,128)}, u32[]{:S(2)}) copy-start(f32[32,256]{1,0:T(8,128)} %copy-done.10) | copy-start | bytes 98308
  54.8 1.4 %copy-start.13 = (f32[32,256]{1,0:T(8,128)S(1)}, f32[32,256]{1,0:T(8,128)}, u32[]{:S(2)}) copy-start(f32[32,256]{1,0:T(8,128)} %copy-done.12) | copy-start | bytes 98308
  57.7 6.6 %collective-permute-start.26 = (bf16[96,512]{1,0:T(8,128)(2,1)S(1)}, bf16[96,512]{1,0:T(8,128)(2,1)S(1)}, u32[]{:S(2)}, u32[]{:S(2)}) collective-permute-start(bf16[96,512]{1,0:T(8,128)(2,1)S(1)} %maximum_maximum_fusion.1.refs_0_), channel_id=1, source_target_pairs={{0,6},{1,7},{2,4},{3,5},{4,2},{5,3},{6,0},{7,1},{8,14},{9,15},{10,... | collective-permute-start | bytes 294920 | tf_op jit(solution)/shard_map/ppermute | solution.py:265
  60.0 6.9 %collective-permute-start.24 = (bf16[96,512]{1,0:T(8,128)(2,1)S(1)}, bf16[96,512]{1,0:T(8,128)(2,1)S(1)}, u32[]{:S(2)}, u32[]{:S(2)}) collective-permute-start(bf16[96,512]{1,0:T(8,128)(2,1)S(1)} %maximum_maximum_fusion.1.refs_0_), channel_id=1, source_target_pairs={{0,4},{1,5},{2,6},{3,7},{4,0},{5,1},{6,2},{7,3},{8,12},{9,13},{10,... | collective-permute-start | bytes 294920 | tf_op jit(solution)/shard_map/ppermute | solution.py:265
  60.8 6.1 %collective-permute-start.22 = (bf16[96,512]{1,0:T(8,128)(2,1)S(1)}, bf16[96,512]{1,0:T(8,128)(2,1)S(1)}, u32[]{:S(2)}, u32[]{:S(2)}) collective-permute-start(bf16[96,512]{1,0:T(8,128)(2,1)S(1)} %maximum_maximum_fusion.1.refs_0_), channel_id=1, source_target_pairs={{0,2},{1,3},{2,0},{3,1},{4,6},{5,7},{6,4},{7,5},{8,10},{9,11},{10,... | collective-permute-start | bytes 294920 | tf_op jit(solution)/shard_map/ppermute | solution.py:265
  62.2 5.2 %collective-permute-start.21 = (bf16[96,512]{1,0:T(8,128)(2,1)S(1)}, bf16[96,512]{1,0:T(8,128)(2,1)S(1)}, u32[]{:S(2)}, u32[]{:S(2)}) collective-permute-start(bf16[96,512]{1,0:T(8,128)(2,1)S(1)} %maximum_maximum_fusion.1.refs_0_), channel_id=1, source_target_pairs={{0,1},{1,0},{2,3},{3,2},{4,5},{5,4},{6,7},{7,6},{8,9},{9,8},{10,11... | collective-permute-start | bytes 294920 | tf_op jit(solution)/shard_map/ppermute | solution.py:267
  64.3 3.1 %collective-permute-start.27 = (bf16[96,512]{1,0:T(8,128)(2,1)S(1)}, bf16[96,512]{1,0:T(8,128)(2,1)S(1)}, u32[]{:S(2)}, u32[]{:S(2)}) collective-permute-start(bf16[96,512]{1,0:T(8,128)(2,1)S(1)} %collective-permute-done.26.refs_6_), channel_id=1, source_target_pairs={{0,1},{1,0},{2,3},{3,2},{4,5},{5,4},{6,7},{7,6},{8,9},{9,8},{10,11... | collective-permute-start | bytes 294920 | tf_op jit(solution)/shard_map/ppermute | solution.py:267
  66.9 1.3 %collective-permute-start.25 = (bf16[96,512]{1,0:T(8,128)(2,1)S(1)}, bf16[96,512]{1,0:T(8,128)(2,1)S(1)}, u32[]{:S(2)}, u32[]{:S(2)}) collective-permute-start(bf16[96,512]{1,0:T(8,128)(2,1)S(1)} %collective-permute-done.24.refs_4_), channel_id=1, source_target_pairs={{0,1},{1,0},{2,3},{3,2},{4,5},{5,4},{6,7},{7,6},{8,9},{9,8},{10,11... | collective-permute-start | bytes 294920 | tf_op jit(solution)/shard_map/ppermute | solution.py:267
  66.9 1.5 %collective-permute-start.23 = (bf16[96,512]{1,0:T(8,128)(2,1)S(1)}, bf16[96,512]{1,0:T(8,128)(2,1)S(1)}, u32[]{:S(2)}, u32[]{:S(2)}) collective-permute-start(bf16[96,512]{1,0:T(8,128)(2,1)S(1)} %collective-permute-done.22.refs_2_), channel_id=1, source_target_pairs={{0,1},{1,0},{2,3},{3,2},{4,5},{5,4},{6,7},{7,6},{8,9},{9,8},{10,11... | collective-permute-start | bytes 294920 | tf_op jit(solution)/shard_map/ppermute | solution.py:267
  69.8 6.9 %collective-permute-start.28 = (bf16[96,512]{1,0:T(8,128)(2,1)S(1)}, bf16[96,512]{1,0:T(8,128)(2,1)S(1)}, u32[]{:S(2)}, u32[]{:S(2)}) collective-permute-start(bf16[96,512]{1,0:T(8,128)(2,1)S(1)} %get-tuple-element.81), channel_id=1, source_target_pairs={{0,2},{1,3},{2,0},{3,1},{4,6},{5,7},{6,4},{7,5},{8,10},{9,11},{10,... | collective-permute-start | bytes 294920 | tf_op jit(solution)/shard_map/ppermute | solution.py:254
  69.9 10.9 %collective-permute-start.29 = (bf16[96,512]{1,0:T(8,128)(2,1)S(1)}, bf16[96,512]{1,0:T(8,128)(2,1)S(1)}, u32[]{:S(2)}, u32[]{:S(2)}) collective-permute-start(bf16[96,512]{1,0:T(8,128)(2,1)S(1)} %get-tuple-element.82), channel_id=1, source_target_pairs={{0,4},{1,5},{2,6},{3,7},{4,0},{5,1},{6,2},{7,3},{8,12},{9,13},{10,... | collective-permute-start | bytes 294920 | tf_op jit(solution)/shard_map/ppermute | solution.py:254
  72.6 8.1 %collective-permute-start.30 = (bf16[96,512]{1,0:T(8,128)(2,1)S(1)}, bf16[96,512]{1,0:T(8,128)(2,1)S(1)}, u32[]{:S(2)}, u32[]{:S(2)}) collective-permute-start(bf16[96,512]{1,0:T(8,128)(2,1)S(1)} %get-tuple-element.83), channel_id=1, source_target_pairs={{0,6},{1,7},{2,4},{3,5},{4,2},{5,3},{6,0},{7,1},{8,14},{9,15},{10,... | collective-permute-start | bytes 294920 | tf_op jit(solution)/shard_map/ppermute | solution.py:254
  (12 other events, 7.5 us)

commit v4 on v3

--- a/solution.py
+++ b/solution.py
@@ -110,6 +110,34 @@
         nn(up_pre_bar, keys),
         nt(push, down_back_bar),
     )
+
+
+def norm_of(rows):
+    return jnp.sqrt(jnp.sum(rows * rows, axis=1, keepdims=True) + EPSILON)
+
+
+def owner_forward(prior, update, fh):
+    moved = prior - update
+    fast = [m * (norm_of(p) / norm_of(m)) for p, m in zip(unpack(prior, fh), unpack(moved, fh))]
+    return pack(*fast).astype(BF16), moved
+
+
+def owner_backward(prior, moved, fast_grad, fh):
+    cotangent, owned = [], []
+    for p, m, fg in zip(unpack(prior, fh), unpack(moved, fh), unpack(fast_grad, fh)):
+        prior_norm, moved_norm = norm_of(p), norm_of(m)
+        column_dot = jnp.sum(fg * m, axis=1, keepdims=True)
+        moved_grad = (prior_norm / moved_norm) * (fg - m * (column_dot / (moved_norm * moved_norm)))
+        cotangent.append(moved_grad)
+        owned.append(moved_grad + p * (column_dot / (moved_norm * prior_norm)))
+    return pack(*cotangent).astype(BF16), pack(*owned)
+
+
+def total_of(pieces):
+    total = pieces[0]
+    for piece in pieces[1:]:
+        total = total + piece.astype(F32)
+    return total
 
 
 def push_of(rates, values):
@@ -163,9 +191,9 @@
 
 
 def saved_kernel(
-    ko, kx, vo, vx, ro, rx, w1t, w3t, w2, go, gx, gain,
+    chips, ko, kx, vo, vx, ro, rx, w1t, w3t, w2, go, gx, gain,
     push_ref, up_slope_ref, silu_ref, back_slope_ref, back_curve_ref,
-    mixed_ref, gate_back_ref, up_back_ref, weighted_ref,
+    mixed_ref, gate_back_ref, up_back_ref, weighted_ref, prior_ref, down_ref,
 ):
     push = push_of(both(ro, rx, 1), both(vo, vx))
     push_ref[...] = push
@@ -180,7 +208,33 @@
     mixed_ref[...] = mixed[:, :own]
     gate_back_ref[...] = gate_back[:, :own]
     up_back_ref[...] = up_back[:, :own]
-    weighted_ref[...] = both(go, gx).T.astype(F32) * gain[...]
+    weighted_ref[...] = (both(go, gx).astype(F32) * gain[...]).T
+    tok = lax.axis_index("tok")
+    g, (d, fh) = prior_ref.shape[0] // 3, (down_ref.shape[0] // (chips * CORES), down_ref.shape[1])
+    rows = pl.ds(pl.multiple_of(tok * g, g), g)
+    prior_ref[:g] = w1t[rows, :].astype(F32)
+    prior_ref[g : 2 * g] = w3t[rows, :].astype(F32)
+    down_ref[...] = w2[...].astype(F32).T
+    for i in range(d // g):
+        rows = pl.ds(pl.multiple_of(tok * d + i * g, g), g)
+        prior_ref[2 * g :, i * fh : (i + 1) * fh] = down_ref[rows, :]
+
+
+def owner_forward_kernel(fh, prior, *refs):
+    fast, moved = refs[-2:]
+    fast[...], moved[...] = owner_forward(prior[...], total_of([r[...] for r in refs[:-2]]), fh)
+
+
+def owner_backward_kernel(fh, prior, moved, *refs):
+    cotangent, owned = refs[-2:]
+    fast_grad = total_of([r[...] for r in refs[:-2]])
+    cotangent[...], owned[...] = owner_backward(prior[...], moved[...], fast_grad, fh)
+
+
+def owner_result_kernel(fh, owned, *refs):
+    gate, up, down = refs[-3:]
+    bars = total_of([r[...] for r in refs[:-3]])
+    gate[...], up[...], down[...] = unpack(owned[...] - bars, fh)
 
 
 def apply_kernel(chips, *refs):
@@ -193,12 +247,11 @@
 
 
 def back_kernel(chips, heads, *refs):
-    sums = sum(r[...] for r in refs[1:heads]) + refs[0][...]
-    f2t, output, weighted, mixed, up_slope, silu, qo, qx, gate_back, up_back = refs[heads : heads + 10]
-    outs, (gate, up, down) = refs[heads + 10 : heads + 10 + chips], refs[heads + 10 + chips :]
+    sums, f2t, output, weighted, mixed, up_slope, silu, qo, qx, gate_back, up_back = refs[:11]
+    outs, (gate, up, down) = refs[11 : 11 + chips], refs[11 + chips :]
     width = heads * output.shape[0]
     gb, ub, gate[...], up[...], down[...] = apply_backward(
-        f2t[...], sums, width, output[...], weighted[...], mixed[...], up_slope[...], silu[...],
+        f2t[...], sums[...], width, output[...], weighted[...], mixed[...], up_slope[...], silu[...],
         both(qo, qx),
     )
     send_pieces(chips, gate, up, down, outs)
@@ -236,7 +289,7 @@
     value_grad[...], key_grad[...] = token_grads(*(r[...] for r in refs[:-2]))
 
 
-def call(kernel, outs, args, scratch=(), name=None):
+def call(kernel, outs, args, scratch=(), name=None, flops=0):
     vmem = pl.BlockSpec(memory_space=pltpu.VMEM)
     return pl.pallas_call(
         kernel,
@@ -245,23 +298,35 @@
         out_specs=[vmem] * len(outs),
         scratch_shapes=[pltpu.VMEM(s, t) for s, t in scratch],
         compiler_params=pltpu.CompilerParams(vmem_limit_bytes=VMEM_LIMIT),
+        cost_estimate=pl.CostEstimate(
+            flops=flops,
+            bytes_accessed=sum(a.size * a.dtype.itemsize for a in args),
+            transcendentals=0,
+        ),
         name=name,
     )(*args)
 
 
-def exchange_sum(pieces, chips):
+def exchange(pieces, chips):
     count = chips * CORES
-    got = {s: lax.ppermute(pieces[s], "tok", chip_perm(count, s)) for s in reversed(range(1, chips))}
-    total = pieces[0]
-    for step in range(1, chips):
-        total = total + got[step].astype(F32)
-    return total
+    got = [lax.ppermute(pieces[s], "tok", chip_perm(count, s)) for s in reversed(range(1, chips))]
+    return [pieces[0], *got]
+
+
+def head_sum(part, heads):
+    if heads & (heads - 1) == 0:
+        step = 1
+        while step < heads:
+            part = part + lax.ppermute(part, "head", [(h, h ^ step) for h in range(heads)])
+            step *= 2
+        return part
+    return lax.psum(part, "head")
 
 
 def gather(packed, chips):
     count = chips * CORES
     pieces = [None] * count
-    for step in (0, *reversed(range(1, chips))):
+    for step in range(chips):
         mine = packed if step == 0 else lax.ppermute(packed, "tok", chip_perm(count, step))
         pieces[2 * step] = mine
         pieces[2 * step + 1] = lax.ppermute(mine, "tok", core_perm(count))
@@ -292,10 +357,6 @@
         held = lax.dynamic_update_index_in_dim(held, pieces[2 * step + 1], first + 1 - core, 0)
     parts = jax.vmap(lambda x: unpack(x, fh))(held)
     return tuple(x.reshape((-1, x.shape[-1])) for x in parts)
-
-
-def norm_of(rows):
-    return jnp.sqrt(jnp.sum(rows * rows, axis=1, keepdims=True) + EPSILON)
 
 
 def per_device(
@@ -319,7 +380,9 @@
     g, d = fh // count, dh // count
     tiled = g % ROW_TILE == 0 and d % g == 0 and dh // g == fh // g * (d // g)
     rates = token_rates.T
-    gain = out_gain[:, None]
+    gain = out_gain[None, :]
+    product = 2 * n * dh * fh
+    owner = ((3 * g, dh), BF16), ((3 * g, dh), F32)
 
     pair = lambda x: lax.ppermute(x, "tok", core_perm(count))
     key_other, value_other, rate_other = pair(key_input), pair(value_input), pair(rates)
@@ -336,13 +399,20 @@
     )
     if tiled:
         pieces = call(
-            functools.partial(update_kernel, chips), messages, inputs, sums_scratch, "update"
-        )
-        push, up_slope, silu, back_slope, back_curve, mixed, gate_back, up_back, weighted = call(
-            saved_kernel,
-            [((dh, n), BF16)] + [hidden] * 4 + [own_hidden] * 3 + [((dh, n), F32)],
+            functools.partial(update_kernel, chips),
+            messages,
+            inputs,
+            sums_scratch,
+            "update",
+            6 * product,
+        )
+        push, up_slope, silu, back_slope, back_curve, mixed, gate_back, up_back, weighted, prior = call(
+            functools.partial(saved_kernel, chips),
+            [((dh, n), BF16)] + [hidden] * 4 + [own_hidden] * 3 + [((dh, n), F32), owner[1]],
             (*inputs, out_grad, grad_other, gain),
-            name="saved",
+            [((dh, fh), F32)],
+            "saved",
+            3 * product,
         )
     else:
         keys = joined(key_input, key_other)
@@ -352,20 +422,23 @@
             update_forward(w1t, w3t, w2, keys, push)
         )
         up_slope, back_curve = up_pre * slope, down_back * up_pre * curvature
-        weighted = joined(out_grad, grad_other).T.astype(F32) * gain
+        weighted = (joined(out_grad, grad_other).astype(F32) * gain).T
         pieces = sliced_pieces(nn(gate_back, keys), nn(up_back, keys), nt(push, mixed), tok, chips)
         mixed, gate_back, up_back = mixed[:, :own], gate_back[:, :own], up_back[:, :own]
-    update = unpack(exchange_sum(pieces, chips), fh)
-
-    priors = [
-        lax.dynamic_slice_in_dim(x, tok * rows, rows, 0).astype(F32)
-        for x, rows in ((w1t, g), (w3t, g), (w2.T, d))
-    ]
-    moved = [p - u for p, u in zip(priors, update)]
-    prior_norm = [norm_of(p) for p in priors]
-    moved_norm = [norm_of(m) for m in moved]
-    fast = [(m * (p / q)).astype(BF16) for m, p, q in zip(moved, prior_norm, moved_norm)]
-    pieces = gather(pack(*fast), chips)
+        prior = pack(
+            *(
+                lax.dynamic_slice_in_dim(x, tok * rows, rows, 0).astype(F32)
+                for x, rows in ((w1t, g), (w3t, g), (w2.T, d))
+            )
+        )
+    pieces = exchange(pieces, chips)
+    if tiled:
+        fast, moved = call(
+            functools.partial(owner_forward_kernel, fh), owner, (prior, *pieces), name="owner_forward"
+        )
+    else:
+        fast, moved = owner_forward(prior, total_of(pieces), fh)
+    pieces = gather(fast, chips)
 
     if tiled:
         f1t, f3t, f2t, output, q_mixed, q_slope, q_silu, part = call(
@@ -373,40 +446,45 @@
             matrices + [((dh, n), F32), ((fh, n), BF16), hidden, hidden, ((2, n), F32)],
             (*pieces, query_input, query_other, weighted),
             name="apply",
+            flops=3 * product,
         )
     else:
         f1t, f3t, f2t = whole_matrices(pieces, tok, chips, fh)
         output, q_mixed, q_slope, q_silu, part = apply_forward(f1t, f3t, f2t, queries, weighted)
-    sums = [part] + [
-        lax.ppermute(part, "head", [(h, partner(h, step, heads)) for h in range(heads)])
-        for step in range(1, heads)
-    ]
+    sums = head_sum(part, heads)
     if tiled:
         q_gate_back, q_up_back, *pieces = call(
             functools.partial(back_kernel, chips, heads),
             [own_hidden] * 2 + messages,
-            (*sums, f2t, output, weighted, q_mixed, q_slope, q_silu, query_input, query_other),
+            (sums, f2t, output, weighted, q_mixed, q_slope, q_silu, query_input, query_other),
             sums_scratch,
             "apply_back",
+            4 * product,
         )
         (query_grad,) = call(
-            query_kernel, [((own, dh), BF16)], (q_gate_back, q_up_back, f1t, f3t), name="query_grad"
+            query_kernel,
+            [((own, dh), BF16)],
+            (q_gate_back, q_up_back, f1t, f3t),
+            name="query_grad",
+            flops=product,
         )
     else:
         q_gate_back, q_up_back, *grads = apply_backward(
-            f2t, sum(sums[1:], sums[0]), heads * dh, output, weighted, q_mixed, q_slope, q_silu, queries
+            f2t, sums, heads * dh, output, weighted, q_mixed, q_slope, q_silu, queries
         )
         pieces = sliced_pieces(*grads, tok, chips)
         query_grad = (tn(q_gate_back[:, :own], f1t) + tn(q_up_back[:, :own], f3t)).astype(BF16)
-    fast_grad = unpack(exchange_sum(pieces, chips), fh)
-
-    cotangent, owned = [], []
-    for p, m, pn, mn, fg in zip(priors, moved, prior_norm, moved_norm, fast_grad):
-        column_dot = jnp.sum(fg * m, axis=1, keepdims=True)
-        moved_grad = pn / mn * (fg - m * (column_dot / (mn * mn)))
-        cotangent.append(moved_grad.astype(BF16))
-        owned.append(moved_grad + p * (column_dot / (mn * pn)))
-    pieces = gather(pack(*cotangent), chips)
+    pieces = exchange(pieces, chips)
+    if tiled:
+        cotangent, owned = call(
+            functools.partial(owner_backward_kernel, fh),
+            owner,
+            (prior, moved, *pieces),
+            name="owner_backward",
+        )
+    else:
+        cotangent, owned = owner_backward(prior, moved, total_of(pieces), fh)
+    pieces = gather(cotangent, chips)
 
     if tiled:
         c1t, c3t, c2t, dbb, upb, gpb, *pieces = call(
@@ -415,6 +493,7 @@
             (*pieces, key_input, key_other, push, up_slope, silu, back_slope, back_curve),
             sums_scratch,
             "second_adjoint",
+            6 * product,
         )
     else:
         c1t, c3t, c2t = whole_matrices(pieces, tok, chips, fh)
@@ -428,12 +507,21 @@
     )
     if tiled:
         value_grad, key_grad = call(
-            token_kernel, [((own, dh), BF16)] * 2, token_args, name="token_grads"
+            token_kernel, [((own, dh), BF16)] * 2, token_args, name="token_grads", flops=3 * product
         )
     else:
         value_grad, key_grad = token_grads(*token_args)
-    bars = unpack(exchange_sum(pieces, chips), fh)
-    results = [(o - b).T[None] for o, b in zip(owned, bars)]
+    pieces = exchange(pieces, chips)
+    if tiled:
+        results = call(
+            functools.partial(owner_result_kernel, fh),
+            [((g, dh), F32)] * 2 + [((d, fh), F32)],
+            (owned, *pieces),
+            name="owner_result",
+        )
+    else:
+        results = unpack(owned - total_of(pieces), fh)
+    results = [r.T[None] for r in results]
     return (query_grad, key_grad, value_grad, *results)
 
 

time: 82.7 us -> 75.4 us (0.912)
  local copies, waits for them, and re-layouts: 7.49 us -> 2.13 us
  other arithmetic: 2.56 us -> 0.01 us
  waiting for transfers between devices: 33.1 us -> 34.7 us
    unnamed x61 -> x18, local copies, waits for them, and re-layouts: 6.56 us -> 2.13 us
    broadcast_in_dim x2 -> x0, other arithmetic: 1.49 us -> none  [per_device(): results = [(o - b).T[None] for o, b in zip(owned, bars)]]
    ppermute x8, waiting for transfers between devices: 0.95 us -> 1.88 us  [gather(): pieces[2 * step + 1] = lax.ppermute(mine, 'tok', core_perm(count))]
    ppermute x12 -> x11, waiting for transfers between devices: 20.1 us -> 20.8 us  [the longest x9 16.6 us: exchange(): lax.ppermute(pieces[s], 'tok', chip_perm(count, s))]
    pallas_call x7 -> x10, Pallas kernels: 8.71 us -> 8.78 us  [call(): pl.pallas_call(kernel, out_shape=[jax.ShapeDtypeStruct(s, t) for s, t in...]
    ppermute x12 -> x11, starting transfers between devices: 17.7 us -> 17.7 us  [the longest x9 14.7 us: exchange(): lax.ppermute(pieces[s], 'tok', chip_perm(count, s))]
  transfers between devices with their start and end apart: 31 -> 30, of which waited for: 15 -> 16; matrix products, arithmetic and copies ran while one was open for 3% -> 2% of each run, Pallas kernels for 6% -> 6%
where the time goes in v4:
time: 75.4 us; the launch traced here: 75.2 us
  waiting for transfers between devices  34.7 us (46%)
  starting transfers between devices  28.8 us (38%)
  Pallas kernels  8.78 us (12%)
  local copies, waits for them, and re-layouts  2.13 us (3%)
  between operations  0.81 us (1%)
    ppermute x9, waiting for transfers between devices, exchange(): lax.ppermute(pieces[s], 'tok', chip_perm(count, s))  16.6 us
    ppermute x9, starting transfers between devices, exchange(): lax.ppermute(pieces[s], 'tok', chip_perm(count, s))  14.7 us
    ppermute x6, waiting for transfers between devices, gather(): lax.ppermute(packed, 'tok', chip_perm(count, step))  12 us
    ppermute x6, starting transfers between devices, gather(): lax.ppermute(packed, 'tok', chip_perm(count, step))  8.91 us
    pallas_call x10, Pallas kernels, call(): pl.pallas_call(kernel, out_shape=[jax.ShapeDtypeStruct(s, t) for s, t in...  8.78 us
    ppermute x2, waiting for transfers between devices, head_sum(): lax.ppermute(part, 'head', [(h, h ^ step) for h in range(heads)])  4.22 us
    ppermute x2, starting transfers between devices, head_sum(): lax.ppermute(part, 'head', [(h, h ^ step) for h in range(heads)])  3.08 us
    unnamed x18, local copies, waits for them, and re-layouts  2.13 us
  transfers between devices with their start and end apart: 30, of which 16 were waited for; matrix products, arithmetic and copies ran while one was open for 2% of the time, Pallas kernels for 6%

profile of v4, /device:TPU:0, one launch (start us, length us, event | category | flops | bytes accessed | tf_op | source)
XLA Modules:
  0.0 75.2 jit_solution(6232208998393692757)
XLA Ops:
  0.6 0.5 collective-permute-start.1
  1.2 0.1 collective-permute-start
  1.2 0.4 collective-permute-start.3
  1.7 0.1 collective-permute-start.2
  1.8 1.1 %copy.15 = bf16[1,512,256]{1,2,0:T(8,128)(2,1)S(1)} copy(bf16[1,512,256]{2,1,0:T(8,128)(2,1)} %param.15) | data formatting | bytes 524288 | tf_op args[6]
  2.9 0.1 copy.16
  3.1 0.7 copy-done.1
  3.9 0.1 copy-done.2
  4.0 1.2 %update.1 = (f32[96,512]{1,0:T(8,128)S(1)}, bf16[96,512]{1,0:T(8,128)(2,1)S(1)}, bf16[96,512]{1,0:T(8,128)(2,1)S(1)}, bf16[96,512]{1,0:T(8,128)(2,1)S(1)}) custom-call(bf16[256,512]{1,0:T(8,128)(2,1)S(1)} %copy-done.2, bf16[256,512]{1,0:T(8,128)(2,1)S(1)} %collective-permute-done.kx.refs_9_, bf16[256,512]{1,0:T(8,128)(2,1)S(1)} %copy-done.3, ...), custom_call_target="tpu_custom_call" | custom-call | flops 805306368 | bytes 1837056 | tf_op jit(solution)/shard_map/update/pallas_call | solution.py:294
  5.1 5.1 %collective-permute-start.4 = (bf16[96,512]{1,0:T(8,128)(2,1)S(1)}, bf16[96,512]{1,0:T(8,128)(2,1)S(1)}, u32[]{:S(2)}, u32[]{:S(2)}) collective-permute-start(bf16[96,512]{1,0:T(8,128)(2,1)S(1)} %get-tuple-element.55), channel_id=1, source_target_pairs={{0,6},{1,7},{2,4},{3,5},{4,2},{5,3},{6,0},{7,1},{8,14},{9,15},{10,... | collective-permute-start | bytes 294920 | tf_op jit(solution)/shard_map/ppermute | solution.py:312
  10.2 0.6 collective-permute-start.6
  10.9 1.0 %saved.1 = (bf16[512,512]{1,0:T(8,128)(2,1)S(1)}, f32[256,512]{1,0:T(8,128)S(1)}, f32[256,512]{1,0:T(8,128)S(1)}, f32[256,512]{1,0:T(8,128)S(1)}, f32[256,512]{1...) custom-call(bf16[256,512]{1,0:T(8,128)(2,1)S(1)} %copy-done.2, ...), custom_call_target="tpu_custom_call" | custom-call | flops 402653184 | bytes 2363392 | tf_op jit(solution)/shard_map/saved/pallas_call | solution.py:294
  11.9 2.0 %collective-permute-done.4.refs_1_ = bf16[96,512]{1,0:T(8,128)(2,1)S(1)} collective-permute-done((bf16[96,512]{1,0:T(8,128)(2,1)S(1)}, bf16[96,512]{1,0:T(8,128)(2,1)S(1)}, u32[]{:S(2)}, u32[]{:S(2)}) %collective-permute-start.4) | collective-permute-done | bytes 98336 | tf_op jit(solution)/shard_map/ppermute | solution.py:312
  13.9 4.8 %collective-permute-done.5.refs_2_ = bf16[96,512]{1,0:T(8,128)(2,1)S(1)} collective-permute-done((bf16[96,512]{1,0:T(8,128)(2,1)S(1)}, bf16[96,512]{1,0:T(8,128)(2,1)S(1)}, u32[]{:S(2)}, u32[]{:S(2)}) %collective-permute-start.5) | collective-permute-done | bytes 98336 | tf_op jit(solution)/shard_map/ppermute | solution.py:312
  18.7 0.2 owner_forward.1
  18.9 2.5 %collective-permute-start.12 = (bf16[96,512]{1,0:T(8,128)(2,1)S(1)}, bf16[96,512]{1,0:T(8,128)(2,1)S(1)}, u32[]{:S(2)}, u32[]{:S(2)}) collective-permute-start(bf16[96,512]{1,0:T(8,128)(2,1)S(1)} %get-tuple-element.58.refs_0_), channel_id=1, source_target_pairs={{0,6},{1,7},{2,4},{3,5},{4,2},{5,3},{6,0},{7,1},{8,14},{9,15},{10,... | collective-permute-start | bytes 294920 | tf_op jit(solution)/shard_map/ppermute | solution.py:330
  21.5 1.9 %collective-permute-start.8 = (bf16[96,512]{1,0:T(8,128)(2,1)S(1)}, bf16[96,512]{1,0:T(8,128)(2,1)S(1)}, u32[]{:S(2)}, u32[]{:S(2)}) collective-permute-start(bf16[96,512]{1,0:T(8,128)(2,1)S(1)} %get-tuple-element.58.refs_0_), channel_id=1, source_target_pairs={{0,2},{1,3},{2,0},{3,1},{4,6},{5,7},{6,4},{7,5},{8,10},{9,11},{10,... | collective-permute-start | bytes 294920 | tf_op jit(solution)/shard_map/ppermute | solution.py:330
  23.4 3.1 %collective-permute-done.12.refs_6_ = bf16[96,512]{1,0:T(8,128)(2,1)S(1)} collective-permute-done((bf16[96,512]{1,0:T(8,128)(2,1)S(1)}, bf16[96,512]{1,0:T(8,128)(2,1)S(1)}, u32[]{:S(2)}, u32[]{:S(2)}) %collective-permute-start.12) | collective-permute-done | bytes 98336 | tf_op jit(solution)/shard_map/ppermute | solution.py:330
  26.5 3.4 %collective-permute-done.10.refs_4_ = bf16[96,512]{1,0:T(8,128)(2,1)S(1)} collective-permute-done((bf16[96,512]{1,0:T(8,128)(2,1)S(1)}, bf16[96,512]{1,0:T(8,128)(2,1)S(1)}, u32[]{:S(2)}, u32[]{:S(2)}) %collective-permute-start.10) | collective-permute-done | bytes 98336 | tf_op jit(solution)/shard_map/ppermute | solution.py:330
  29.9 0.5 collective-permute-start.9
  30.4 0.8 %collective-permute-done.11.refs_5_ = bf16[96,512]{1,0:T(8,128)(2,1)S(1)} collective-permute-done((bf16[96,512]{1,0:T(8,128)(2,1)S(1)}, bf16[96,512]{1,0:T(8,128)(2,1)S(1)}, u32[]{:S(2)}, u32[]{:S(2)}) %collective-permute-start.11) | collective-permute-done | bytes 98336 | tf_op jit(solution)/shard_map/ppermute | solution.py:332
  31.2 0.2 collective-permute-done.9.refs_3_
  31.3 0.8 %apply.1 = (bf16[256,512]{1,0:T(8,128)(2,1)S(1)}, bf16[256,512]{1,0:T(8,128)(2,1)S(1)}, bf16[512,256]{1,0:T(8,128)(2,1)S(1)}, f32[512,512]{1,0:T(8,128)S(1)}, bf...) custom-call(bf16[96,512]{1,0:T(8,128)(2,1)S(1)} %get-tuple-element.58.refs_0, ...), custom_call_target="tpu_custom_call" | custom-call | flops 402653184 | bytes 2359296 | tf_op jit(solution)/shard_map/apply/pallas_call | solution.py:294
  32.2 1.6 %collective-permute-start.15 = (f32[2,512]{1,0:T(2,128)S(1)}, f32[2,512]{1,0:T(2,128)S(1)}, u32[]{:S(2)}, u32[]{:S(2)}) collective-permute-start(f32[2,512]{1,0:T(2,128)S(1)} %get-tuple-element.60), channel_id=1, source_target_pairs={{0,8},{8,0},{16,24},{24,16},{1,9},{9,1},{17,25},{25,17},{2,10},{10... | collective-permute-start | bytes 12296 | tf_op jit(solution)/shard_map/ppermute | solution.py:320
  33.7 2.1 %collective-permute-done.15 = f32[2,512]{1,0:T(2,128)S(1)} collective-permute-done((f32[2,512]{1,0:T(2,128)S(1)}, f32[2,512]{1,0:T(2,128)S(1)}, u32[]{:S(2)}, u32[]{:S(2)}) %collective-permute-start.15) | collective-permute-done | bytes 4128 | tf_op jit(solution)/shard_map/ppermute | solution.py:320
  35.9 1.5 %collective-permute-start.16 = (f32[2,512]{1,0:T(2,128)S(1)}, f32[2,512]{1,0:T(2,128)S(1)}, u32[]{:S(2)}, u32[]{:S(2)}) collective-permute-start(f32[2,512]{1,0:T(2,128)S(1)} %add.6), channel_id=1, source_target_pairs={{0,16},{8,24},{16,0},{24,8},{1,17},{9,25},{17,1},{25,9},{2,18},{10... | collective-permute-start | bytes 12296 | tf_op jit(solution)/shard_map/ppermute | solution.py:320
  37.4 2.1 %collective-permute-done.16 = f32[2,512]{1,0:T(2,128)S(1)} collective-permute-done((f32[2,512]{1,0:T(2,128)S(1)}, f32[2,512]{1,0:T(2,128)S(1)}, u32[]{:S(2)}, u32[]{:S(2)}) %collective-permute-start.16) | collective-permute-done | bytes 4128 | tf_op jit(solution)/shard_map/ppermute | solution.py:320
  39.5 0.9 %apply_back.1 = (bf16[256,256]{1,0:T(8,128)(2,1)S(1)}, bf16[256,256]{1,0:T(8,128)(2,1)S(1)}, f32[96,512]{1,0:T(8,128)S(1)}, bf16[96,512]{1,0:T(8,128)(2,1)S(1)},...) custom-call(f32[2,512]{1,0:T(2,128)S(1)} %add.7.refs_0_, bf16[512,256]{1,0:T(8,128)(2,1)S(1)} %get-tuple-element.61.refs_1_, ...), custom_call_target="tpu_custom_call" | custom-call | flops 536870912 | bytes 4198400 | tf_op jit(solution)/shard_map/apply_back/pallas_call | solution.py:294
  40.4 1.6 %collective-permute-start.17 = (bf16[96,512]{1,0:T(8,128)(2,1)S(1)}, bf16[96,512]{1,0:T(8,128)(2,1)S(1)}, u32[]{:S(2)}, u32[]{:S(2)}) collective-permute-start(bf16[96,512]{1,0:T(8,128)(2,1)S(1)} %get-tuple-element.73), channel_id=1, source_target_pairs={{0,6},{1,7},{2,4},{3,5},{4,2},{5,3},{6,0},{7,1},{8,14},{9,15},{10,... | collective-permute-start | bytes 294920 | tf_op jit(solution)/shard_map/ppermute | solution.py:312
  42.0 2.8 %collective-permute-start.19 = (bf16[96,512]{1,0:T(8,128)(2,1)S(1)}, bf16[96,512]{1,0:T(8,128)(2,1)S(1)}, u32[]{:S(2)}, u32[]{:S(2)}) collective-permute-start(bf16[96,512]{1,0:T(8,128)(2,1)S(1)} %get-tuple-element.75), channel_id=1, source_target_pairs={{0,2},{1,3},{2,0},{3,1},{4,6},{5,7},{6,4},{7,5},{8,10},{9,11},{10,... | collective-permute-start | bytes 294920 | tf_op jit(solution)/shard_map/ppermute | solution.py:312
  44.9 2.5 %collective-permute-done.17.refs_1_ = bf16[96,512]{1,0:T(8,128)(2,1)S(1)} collective-permute-done((bf16[96,512]{1,0:T(8,128)(2,1)S(1)}, bf16[96,512]{1,0:T(8,128)(2,1)S(1)}, u32[]{:S(2)}, u32[]{:S(2)}) %collective-permute-start.17) | collective-permute-done | bytes 98336 | tf_op jit(solution)/shard_map/ppermute | solution.py:312
  47.4 2.9 %collective-permute-done.18.refs_2_ = bf16[96,512]{1,0:T(8,128)(2,1)S(1)} collective-permute-done((bf16[96,512]{1,0:T(8,128)(2,1)S(1)}, bf16[96,512]{1,0:T(8,128)(2,1)S(1)}, u32[]{:S(2)}, u32[]{:S(2)}) %collective-permute-start.18) | collective-permute-done | bytes 98336 | tf_op jit(solution)/shard_map/ppermute | solution.py:312
  50.3 0.2 owner_backward.1
  50.5 1.6 %collective-permute-start.25 = (bf16[96,512]{1,0:T(8,128)(2,1)S(1)}, bf16[96,512]{1,0:T(8,128)(2,1)S(1)}, u32[]{:S(2)}, u32[]{:S(2)}) collective-permute-start(bf16[96,512]{1,0:T(8,128)(2,1)S(1)} %get-tuple-element.76.refs_0_), channel_id=1, source_target_pairs={{0,6},{1,7},{2,4},{3,5},{4,2},{5,3},{6,0},{7,1},{8,14},{9,15},{10,... | collective-permute-start | bytes 294920 | tf_op jit(solution)/shard_map/ppermute | solution.py:330
  52.1 2.8 %collective-permute-start.21 = (bf16[96,512]{1,0:T(8,128)(2,1)S(1)}, bf16[96,512]{1,0:T(8,128)(2,1)S(1)}, u32[]{:S(2)}, u32[]{:S(2)}) collective-permute-start(bf16[96,512]{1,0:T(8,128)(2,1)S(1)} %get-tuple-element.76.refs_0_), channel_id=1, source_target_pairs={{0,2},{1,3},{2,0},{3,1},{4,6},{5,7},{6,4},{7,5},{8,10},{9,11},{10,... | collective-permute-start | bytes 294920 | tf_op jit(solution)/shard_map/ppermute | solution.py:330
  54.9 3.2 %collective-permute-done.25.refs_6_ = bf16[96,512]{1,0:T(8,128)(2,1)S(1)} collective-permute-done((bf16[96,512]{1,0:T(8,128)(2,1)S(1)}, bf16[96,512]{1,0:T(8,128)(2,1)S(1)}, u32[]{:S(2)}, u32[]{:S(2)}) %collective-permute-start.25) | collective-permute-done | bytes 98336 | tf_op jit(solution)/shard_map/ppermute | solution.py:330
  58.2 2.3 %collective-permute-done.23.refs_4_ = bf16[96,512]{1,0:T(8,128)(2,1)S(1)} collective-permute-done((bf16[96,512]{1,0:T(8,128)(2,1)S(1)}, bf16[96,512]{1,0:T(8,128)(2,1)S(1)}, u32[]{:S(2)}, u32[]{:S(2)}) %collective-permute-start.23) | collective-permute-done | bytes 98336 | tf_op jit(solution)/shard_map/ppermute | solution.py:330
  60.5 0.5 collective-permute-start.22
  61.0 0.8 %collective-permute-done.24.refs_5_ = bf16[96,512]{1,0:T(8,128)(2,1)S(1)} collective-permute-done((bf16[96,512]{1,0:T(8,128)(2,1)S(1)}, bf16[96,512]{1,0:T(8,128)(2,1)S(1)}, u32[]{:S(2)}, u32[]{:S(2)}) %collective-permute-start.24) | collective-permute-done | bytes 98336 | tf_op jit(solution)/shard_map/ppermute | solution.py:332
  61.7 0.2 collective-permute-done.22.refs_3_
  61.9 1.4 %second_adjoint.1 = (bf16[256,512]{1,0:T(8,128)(2,1)S(1)}, bf16[256,512]{1,0:T(8,128)(2,1)S(1)}, bf16[512,256]{1,0:T(8,128)(2,1)S(1)}, bf16[256,256]{1,0:T(8,128...) custom-call(bf16[96,512]{1,0:T(8,128)(2,1)S(1)} %get-tuple-element.7, ...), custom_call_target="tpu_custom_call" | custom-call | flops 805306368 | bytes 3932160 | tf_op jit(solution)/shard_map/second_adjoint/pallas_call | solution.py:294
  63.3 1.6 %collective-permute-start.27 = (bf16[96,512]{1,0:T(8,128)(2,1)S(1)}, bf16[96,512]{1,0:T(8,128)(2,1)S(1)}, u32[]{:S(2)}, u32[]{:S(2)}) collective-permute-start(bf16[96,512]{1,0:T(8,128)(2,1)S(1)} %get-tuple-element.94), channel_id=1, source_target_pairs={{0,6},{1,7},{2,4},{3,5},{4,2},{5,3},{6,0},{7,1},{8,14},{9,15},{10,... | collective-permute-start | bytes 294920 | tf_op jit(solution)/shard_map/ppermute | solution.py:312
  65.0 2.8 %collective-permute-start.29 = (bf16[96,512]{1,0:T(8,128)(2,1)S(1)}, bf16[96,512]{1,0:T(8,128)(2,1)S(1)}, u32[]{:S(2)}, u32[]{:S(2)}) collective-permute-start(bf16[96,512]{1,0:T(8,128)(2,1)S(1)} %get-tuple-element.96), channel_id=1, source_target_pairs={{0,2},{1,3},{2,0},{3,1},{4,6},{5,7},{6,4},{7,5},{8,10},{9,11},{10,... | collective-permute-start | bytes 294920 | tf_op jit(solution)/shard_map/ppermute | solution.py:312
  67.8 1.0 %query_grad.1 = bf16[256,512]{1,0:T(8,128)(2,1)} custom-call(bf16[256,256]{1,0:T(8,128)(2,1)S(1)} %get-tuple-element.66.gate_back, bf16[256,256]{1,0:T(8,128)(2,1)S(1)} %get-tuple-element.67.up_back, bf16[256,512]{1,0:T(8,128)(2,1)S(1)} %get-tuple-element.68.f1t, bf16[256,512]{1,0:T(8,128)(2,1)S(1)} %get-tuple-element.69.f3t), custom_call_target="tpu_custom_call" | custom-call | flops 134217728 | bytes 786432 | tf_op jit(solution)/shard_map/query_grad/pallas_call | solution.py:294
  68.8 1.4 %token_grads.1 = (bf16[256,512]{1,0:T(8,128)(2,1)}, bf16[256,512]{1,0:T(8,128)(2,1)}) custom-call(f32[1,256]{1,0:T(1,128)S(1)} %bitcast.30, bf16[256,256]{1,0:T(8,128)(2,1)S(1)} %get-tuple-element.70.refs_1_, bf16[256,256]{1,0:T(8,128)(2,1)S(1)} %get-tuple-element.82.refs_2_, bf16[256,256]{1,0:T(8,128)(2,1)S(1)} %get-tuple-element.83.refs_3_, ...), custom_call_target="tpu_custom_call" | custom-call | flops 402653184 | bytes 2360320 | tf_op jit(solution)/shard_map/token_grads/pallas_call | solution.py:294
  70.2 0.7 collective-permute-done.27.refs_1_
  70.9 3.5 %collective-permute-done.28.refs_2_ = bf16[96,512]{1,0:T(8,128)(2,1)S(1)} collective-permute-done((bf16[96,512]{1,0:T(8,128)(2,1)S(1)}, bf16[96,512]{1,0:T(8,128)(2,1)S(1)}, u32[]{:S(2)}, u32[]{:S(2)}) %collective-permute-start.28) | collective-permute-done | bytes 98336 | tf_op jit(solution)/shard_map/ppermute | solution.py:312
  74.5 0.7 owner_result.1
  (42 shorter events, 0.1 us)
Async XLA Ops:
  0.6 1.0 %copy-start.5 = (f32[256,1]{0,1:T(1,128)S(1)}, f32[256,1]{0,1:T(1,128)}, u32[]{:S(2)}) copy-start(f32[256,1]{0,1:T(1,128)} %param.13) | copy-start | bytes 3076
  0.6 2.5 %collective-permute-start.1 = (bf16[256,512]{1,0:T(8,128)(2,1)}, bf16[256,512]{1,0:T(8,128)(2,1)S(1)}, u32[]{:S(2)}, u32[]{:S(2)}) collective-permute-start(bf16[256,512]{1,0:T(8,128)(2,1)} %vo.3), channel_id=1, source_target_pairs={{0,1},{1,0},{2,3},{3,2},{4,5},{5,4},{6,7},{7,6},{8,9},{9,8},{10,11... | collective-permute-start | bytes 786440 | tf_op jit(solution)/shard_map/ppermute | solution.py:387
  1.2 2.0 %collective-permute-start = (bf16[256,512]{1,0:T(8,128)(2,1)}, bf16[256,512]{1,0:T(8,128)(2,1)S(1)}, u32[]{:S(2)}, u32[]{:S(2)}) collective-permute-start(bf16[256,512]{1,0:T(8,128)(2,1)} %refs_8_.3), channel_id=1, source_target_pairs={{0,1},{1,0},{2,3},{3,2},{4,5},{5,4},{6,7},{7,6},{8,9},{9,8},{10,11... | collective-permute-start | bytes 786440 | tf_op jit(solution)/shard_map/ppermute | solution.py:387
  1.2 9.6 %collective-permute-start.3 = (bf16[256,512]{1,0:T(8,128)(2,1)}, bf16[256,512]{1,0:T(8,128)(2,1)S(1)}, u32[]{:S(2)}, u32[]{:S(2)}) collective-permute-start(bf16[256,512]{1,0:T(8,128)(2,1)} %go.1), channel_id=1, source_target_pairs={{0,1},{1,0},{2,3},{3,2},{4,5},{5,4},{6,7},{7,6},{8,9},{9,8},{10,11... | collective-permute-start | bytes 786440 | tf_op jit(solution)/shard_map/ppermute | solution.py:387
  1.7 1.2 %copy-start.7 = (bf16[1,512,256]{2,1,0:T(8,128)(2,1)S(1)}, bf16[1,512,256]{2,1,0:T(8,128)(2,1)}, u32[]{:S(2)}) copy-start(bf16[1,512,256]{2,1,0:T(8,128)(2,1)} %param.16) | copy-start | bytes 786436
  1.7 1.4 %collective-permute-start.2 = (f32[1,256]{1,0:T(1,128)S(1)}, f32[1,256]{1,0:T(1,128)S(1)}, u32[]{:S(2)}, u32[]{:S(2)}) collective-permute-start(f32[1,256]{1,0:T(1,128)S(1)} %bitcast.27), channel_id=1, source_target_pairs={{0,1},{1,0},{2,3},{3,2},{4,5},{5,4},{6,7},{7,6},{8,9},{9,8},{10,11... | collective-permute-start | bytes 3080 | tf_op jit(solution)/shard_map/ppermute | solution.py:387
  1.8 1.4 %copy-start.3 = (bf16[256,512]{1,0:T(8,128)(2,1)S(1)}, bf16[256,512]{1,0:T(8,128)(2,1)}, u32[]{:S(2)}) copy-start(bf16[256,512]{1,0:T(8,128)(2,1)} %vo.3) | copy-start | bytes 786436
  2.9 1.0 %copy-start.1 = (bf16[1,256,512]{2,1,0:T(8,128)(2,1)S(1)}, bf16[1,256,512]{2,1,0:T(8,128)(2,1)}, u32[]{:S(2)}) copy-start(bf16[1,256,512]{2,1,0:T(8,128)(2,1)} %param.17) | copy-start | bytes 786436
  2.9 1.0 %copy-start.2 = (bf16[256,512]{1,0:T(8,128)(2,1)S(1)}, bf16[256,512]{1,0:T(8,128)(2,1)}, u32[]{:S(2)}) copy-start(bf16[256,512]{1,0:T(8,128)(2,1)} %refs_8_.3) | copy-start | bytes 786436
  4.0 6.9 %copy-start = (bf16[256,512]{1,0:T(8,128)(2,1)S(1)}, bf16[256,512]{1,0:T(8,128)(2,1)}, u32[]{:S(2)}) copy-start(bf16[256,512]{1,0:T(8,128)(2,1)} %refs_7_.1) | copy-start | bytes 786436
  4.0 6.9 %copy-start.4 = (bf16[256,512]{1,0:T(8,128)(2,1)S(1)}, bf16[256,512]{1,0:T(8,128)(2,1)}, u32[]{:S(2)}) copy-start(bf16[256,512]{1,0:T(8,128)(2,1)} %go.1) | copy-start | bytes 786436
  5.1 8.8 %collective-permute-start.4 = (bf16[96,512]{1,0:T(8,128)(2,1)S(1)}, bf16[96,512]{1,0:T(8,128)(2,1)S(1)}, u32[]{:S(2)}, u32[]{:S(2)}) collective-permute-start(bf16[96,512]{1,0:T(8,128)(2,1)S(1)} %get-tuple-element.55), channel_id=1, source_target_pairs={{0,6},{1,7},{2,4},{3,5},{4,2},{5,3},{6,0},{7,1},{8,14},{9,15},{10,... | collective-permute-start | bytes 294920 | tf_op jit(solution)/shard_map/ppermute | solution.py:312
  10.2 0.7 copy-start.6
  10.2 8.5 %collective-permute-start.5 = (bf16[96,512]{1,0:T(8,128)(2,1)S(1)}, bf16[96,512]{1,0:T(8,128)(2,1)S(1)}, u32[]{:S(2)}, u32[]{:S(2)}) collective-permute-start(bf16[96,512]{1,0:T(8,128)(2,1)S(1)} %get-tuple-element.56), channel_id=1, source_target_pairs={{0,4},{1,5},{2,6},{3,7},{4,0},{5,1},{6,2},{7,3},{8,12},{9,13},{10,... | collective-permute-start | bytes 294920 | tf_op jit(solution)/shard_map/ppermute | solution.py:312
  10.2 8.5 %collective-permute-start.6 = (bf16[96,512]{1,0:T(8,128)(2,1)S(1)}, bf16[96,512]{1,0:T(8,128)(2,1)S(1)}, u32[]{:S(2)}, u32[]{:S(2)}) collective-permute-start(bf16[96,512]{1,0:T(8,128)(2,1)S(1)} %get-tuple-element.57), channel_id=1, source_target_pairs={{0,2},{1,3},{2,0},{3,1},{4,6},{5,7},{6,4},{7,5},{8,10},{9,11},{10,... | collective-permute-start | bytes 294920 | tf_op jit(solution)/shard_map/ppermute | solution.py:312
  10.9 19.5 %collective-permute-start.14 = (bf16[256,512]{1,0:T(8,128)(2,1)S(1)}, bf16[256,512]{1,0:T(8,128)(2,1)S(1)}, u32[]{:S(2)}, u32[]{:S(2)}) collective-permute-start(bf16[256,512]{1,0:T(8,128)(2,1)S(1)} %copy-done), channel_id=1, source_target_pairs={{0,1},{1,0},{2,3},{3,2},{4,5},{5,4},{6,7},{7,6},{8,9},{9,8},{10,11... | collective-permute-start | bytes 786440 | tf_op jit(solution)/shard_map/ppermute | solution.py:387
  18.9 7.6 %collective-permute-start.12 = (bf16[96,512]{1,0:T(8,128)(2,1)S(1)}, bf16[96,512]{1,0:T(8,128)(2,1)S(1)}, u32[]{:S(2)}, u32[]{:S(2)}) collective-permute-start(bf16[96,512]{1,0:T(8,128)(2,1)S(1)} %get-tuple-element.58.refs_0_), channel_id=1, source_target_pairs={{0,6},{1,7},{2,4},{3,5},{4,2},{5,3},{6,0},{7,1},{8,14},{9,15},{10,... | collective-permute-start | bytes 294920 | tf_op jit(solution)/shard_map/ppermute | solution.py:330
  21.5 8.4 %collective-permute-start.10 = (bf16[96,512]{1,0:T(8,128)(2,1)S(1)}, bf16[96,512]{1,0:T(8,128)(2,1)S(1)}, u32[]{:S(2)}, u32[]{:S(2)}) collective-permute-start(bf16[96,512]{1,0:T(8,128)(2,1)S(1)} %get-tuple-element.58.refs_0_), channel_id=1, source_target_pairs={{0,4},{1,5},{2,6},{3,7},{4,0},{5,1},{6,2},{7,3},{8,12},{9,13},{10,... | collective-permute-start | bytes 294920 | tf_op jit(solution)/shard_map/ppermute | solution.py:330
  21.5 8.4 %collective-permute-start.8 = (bf16[96,512]{1,0:T(8,128)(2,1)S(1)}, bf16[96,512]{1,0:T(8,128)(2,1)S(1)}, u32[]{:S(2)}, u32[]{:S(2)}) collective-permute-start(bf16[96,512]{1,0:T(8,128)(2,1)S(1)} %get-tuple-element.58.refs_0_), channel_id=1, source_target_pairs={{0,2},{1,3},{2,0},{3,1},{4,6},{5,7},{6,4},{7,5},{8,10},{9,11},{10,... | collective-permute-start | bytes 294920 | tf_op jit(solution)/shard_map/ppermute | solution.py:330
  23.4 7.0 %collective-permute-start.7 = (bf16[96,512]{1,0:T(8,128)(2,1)S(1)}, bf16[96,512]{1,0:T(8,128)(2,1)S(1)}, u32[]{:S(2)}, u32[]{:S(2)}) collective-permute-start(bf16[96,512]{1,0:T(8,128)(2,1)S(1)} %get-tuple-element.58.refs_0_), channel_id=1, source_target_pairs={{0,1},{1,0},{2,3},{3,2},{4,5},{5,4},{6,7},{7,6},{8,9},{9,8},{10,11... | collective-permute-start | bytes 294920 | tf_op jit(solution)/shard_map/ppermute | solution.py:332
  26.5 3.9 %collective-permute-start.13 = (bf16[96,512]{1,0:T(8,128)(2,1)S(1)}, bf16[96,512]{1,0:T(8,128)(2,1)S(1)}, u32[]{:S(2)}, u32[]{:S(2)}) collective-permute-start(bf16[96,512]{1,0:T(8,128)(2,1)S(1)} %collective-permute-done.12.refs_6_), channel_id=1, source_target_pairs={{0,1},{1,0},{2,3},{3,2},{4,5},{5,4},{6,7},{7,6},{8,9},{9,8},{10,11... | collective-permute-start | bytes 294920 | tf_op jit(solution)/shard_map/ppermute | solution.py:332
  29.9 1.3 %collective-permute-start.11 = (bf16[96,512]{1,0:T(8,128)(2,1)S(1)}, bf16[96,512]{1,0:T(8,128)(2,1)S(1)}, u32[]{:S(2)}, u32[]{:S(2)}) collective-permute-start(bf16[96,512]{1,0:T(8,128)(2,1)S(1)} %collective-permute-done.10.refs_4_), channel_id=1, source_target_pairs={{0,1},{1,0},{2,3},{3,2},{4,5},{5,4},{6,7},{7,6},{8,9},{9,8},{10,11... | collective-permute-start | bytes 294920 | tf_op jit(solution)/shard_map/ppermute | solution.py:332
  29.9 1.5 %collective-permute-start.9 = (bf16[96,512]{1,0:T(8,128)(2,1)S(1)}, bf16[96,512]{1,0:T(8,128)(2,1)S(1)}, u32[]{:S(2)}, u32[]{:S(2)}) collective-permute-start(bf16[96,512]{1,0:T(8,128)(2,1)S(1)} %collective-permute-done.8.refs_2_), channel_id=1, source_target_pairs={{0,1},{1,0},{2,3},{3,2},{4,5},{5,4},{6,7},{7,6},{8,9},{9,8},{10,11... | collective-permute-start | bytes 294920 | tf_op jit(solution)/shard_map/ppermute | solution.py:332
  32.2 3.7 %collective-permute-start.15 = (f32[2,512]{1,0:T(2,128)S(1)}, f32[2,512]{1,0:T(2,128)S(1)}, u32[]{:S(2)}, u32[]{:S(2)}) collective-permute-start(f32[2,512]{1,0:T(2,128)S(1)} %get-tuple-element.60), channel_id=1, source_target_pairs={{0,8},{8,0},{16,24},{24,16},{1,9},{9,1},{17,25},{25,17},{2,10},{10... | collective-permute-start | bytes 12296 | tf_op jit(solution)/shard_map/ppermute | solution.py:320
  35.9 3.6 %collective-permute-start.16 = (f32[2,512]{1,0:T(2,128)S(1)}, f32[2,512]{1,0:T(2,128)S(1)}, u32[]{:S(2)}, u32[]{:S(2)}) collective-permute-start(f32[2,512]{1,0:T(2,128)S(1)} %add.6), channel_id=1, source_target_pairs={{0,16},{8,24},{16,0},{24,8},{1,17},{9,25},{17,1},{25,9},{2,18},{10... | collective-permute-start | bytes 12296 | tf_op jit(solution)/shard_map/ppermute | solution.py:320
  40.4 7.0 %collective-permute-start.17 = (bf16[96,512]{1,0:T(8,128)(2,1)S(1)}, bf16[96,512]{1,0:T(8,128)(2,1)S(1)}, u32[]{:S(2)}, u32[]{:S(2)}) collective-permute-start(bf16[96,512]{1,0:T(8,128)(2,1)S(1)} %get-tuple-element.73), channel_id=1, source_target_pairs={{0,6},{1,7},{2,4},{3,5},{4,2},{5,3},{6,0},{7,1},{8,14},{9,15},{10,... | collective-permute-start | bytes 294920 | tf_op jit(solution)/shard_map/ppermute | solution.py:312
  42.0 8.2 %collective-permute-start.18 = (bf16[96,512]{1,0:T(8,128)(2,1)S(1)}, bf16[96,512]{1,0:T(8,128)(2,1)S(1)}, u32[]{:S(2)}, u32[]{:S(2)}) collective-permute-start(bf16[96,512]{1,0:T(8,128)(2,1)S(1)} %get-tuple-element.74), channel_id=1, source_target_pairs={{0,4},{1,5},{2,6},{3,7},{4,0},{5,1},{6,2},{7,3},{8,12},{9,13},{10,... | collective-permute-start | bytes 294920 | tf_op jit(solution)/shard_map/ppermute | solution.py:312
  42.0 8.2 %collective-permute-start.19 = (bf16[96,512]{1,0:T(8,128)(2,1)S(1)}, bf16[96,512]{1,0:T(8,128)(2,1)S(1)}, u32[]{:S(2)}, u32[]{:S(2)}) collective-permute-start(bf16[96,512]{1,0:T(8,128)(2,1)S(1)} %get-tuple-element.75), channel_id=1, source_target_pairs={{0,2},{1,3},{2,0},{3,1},{4,6},{5,7},{6,4},{7,5},{8,10},{9,11},{10,... | collective-permute-start | bytes 294920 | tf_op jit(solution)/shard_map/ppermute | solution.py:312
  50.5 7.7 %collective-permute-start.25 = (bf16[96,512]{1,0:T(8,128)(2,1)S(1)}, bf16[96,512]{1,0:T(8,128)(2,1)S(1)}, u32[]{:S(2)}, u32[]{:S(2)}) collective-permute-start(bf16[96,512]{1,0:T(8,128)(2,1)S(1)} %get-tuple-element.76.refs_0_), channel_id=1, source_target_pairs={{0,6},{1,7},{2,4},{3,5},{4,2},{5,3},{6,0},{7,1},{8,14},{9,15},{10,... | collective-permute-start | bytes 294920 | tf_op jit(solution)/shard_map/ppermute | solution.py:330
  52.1 8.3 %collective-permute-start.23 = (bf16[96,512]{1,0:T(8,128)(2,1)S(1)}, bf16[96,512]{1,0:T(8,128)(2,1)S(1)}, u32[]{:S(2)}, u32[]{:S(2)}) collective-permute-start(bf16[96,512]{1,0:T(8,128)(2,1)S(1)} %get-tuple-element.76.refs_0_), channel_id=1, source_target_pairs={{0,4},{1,5},{2,6},{3,7},{4,0},{5,1},{6,2},{7,3},{8,12},{9,13},{10,... | collective-permute-start | bytes 294920 | tf_op jit(solution)/shard_map/ppermute | solution.py:330
  52.1 8.3 %collective-permute-start.21 = (bf16[96,512]{1,0:T(8,128)(2,1)S(1)}, bf16[96,512]{1,0:T(8,128)(2,1)S(1)}, u32[]{:S(2)}, u32[]{:S(2)}) collective-permute-start(bf16[96,512]{1,0:T(8,128)(2,1)S(1)} %get-tuple-element.76.refs_0_), channel_id=1, source_target_pairs={{0,2},{1,3},{2,0},{3,1},{4,6},{5,7},{6,4},{7,5},{8,10},{9,11},{10,... | collective-permute-start | bytes 294920 | tf_op jit(solution)/shard_map/ppermute | solution.py:330
  54.9 6.0 %collective-permute-start.20 = (bf16[96,512]{1,0:T(8,128)(2,1)S(1)}, bf16[96,512]{1,0:T(8,128)(2,1)S(1)}, u32[]{:S(2)}, u32[]{:S(2)}) collective-permute-start(bf16[96,512]{1,0:T(8,128)(2,1)S(1)} %get-tuple-element.76.refs_0_), channel_id=1, source_target_pairs={{0,1},{1,0},{2,3},{3,2},{4,5},{5,4},{6,7},{7,6},{8,9},{9,8},{10,11... | collective-permute-start | bytes 294920 | tf_op jit(solution)/shard_map/ppermute | solution.py:332
  58.2 2.8 %collective-permute-start.26 = (bf16[96,512]{1,0:T(8,128)(2,1)S(1)}, bf16[96,512]{1,0:T(8,128)(2,1)S(1)}, u32[]{:S(2)}, u32[]{:S(2)}) collective-permute-start(bf16[96,512]{1,0:T(8,128)(2,1)S(1)} %collective-permute-done.25.refs_6_), channel_id=1, source_target_pairs={{0,1},{1,0},{2,3},{3,2},{4,5},{5,4},{6,7},{7,6},{8,9},{9,8},{10,11... | collective-permute-start | bytes 294920 | tf_op jit(solution)/shard_map/ppermute | solution.py:332
  60.4 1.3 %collective-permute-start.24 = (bf16[96,512]{1,0:T(8,128)(2,1)S(1)}, bf16[96,512]{1,0:T(8,128)(2,1)S(1)}, u32[]{:S(2)}, u32[]{:S(2)}) collective-permute-start(bf16[96,512]{1,0:T(8,128)(2,1)S(1)} %collective-permute-done.23.refs_4_), channel_id=1, source_target_pairs={{0,1},{1,0},{2,3},{3,2},{4,5},{5,4},{6,7},{7,6},{8,9},{9,8},{10,11... | collective-permute-start | bytes 294920 | tf_op jit(solution)/shard_map/ppermute | solution.py:332
  60.5 1.4 %collective-permute-start.22 = (bf16[96,512]{1,0:T(8,128)(2,1)S(1)}, bf16[96,512]{1,0:T(8,128)(2,1)S(1)}, u32[]{:S(2)}, u32[]{:S(2)}) collective-permute-start(bf16[96,512]{1,0:T(8,128)(2,1)S(1)} %collective-permute-done.21.refs_2_), channel_id=1, source_target_pairs={{0,1},{1,0},{2,3},{3,2},{4,5},{5,4},{6,7},{7,6},{8,9},{9,8},{10,11... | collective-permute-start | bytes 294920 | tf_op jit(solution)/shard_map/ppermute | solution.py:332
  63.3 7.6 %collective-permute-start.27 = (bf16[96,512]{1,0:T(8,128)(2,1)S(1)}, bf16[96,512]{1,0:T(8,128)(2,1)S(1)}, u32[]{:S(2)}, u32[]{:S(2)}) collective-permute-start(bf16[96,512]{1,0:T(8,128)(2,1)S(1)} %get-tuple-element.94), channel_id=1, source_target_pairs={{0,6},{1,7},{2,4},{3,5},{4,2},{5,3},{6,0},{7,1},{8,14},{9,15},{10,... | collective-permute-start | bytes 294920 | tf_op jit(solution)/shard_map/ppermute | solution.py:312
  65.0 9.5 %collective-permute-start.28 = (bf16[96,512]{1,0:T(8,128)(2,1)S(1)}, bf16[96,512]{1,0:T(8,128)(2,1)S(1)}, u32[]{:S(2)}, u32[]{:S(2)}) collective-permute-start(bf16[96,512]{1,0:T(8,128)(2,1)S(1)} %get-tuple-element.95), channel_id=1, source_target_pairs={{0,4},{1,5},{2,6},{3,7},{4,0},{5,1},{6,2},{7,3},{8,12},{9,13},{10,... | collective-permute-start | bytes 294920 | tf_op jit(solution)/shard_map/ppermute | solution.py:312
  65.0 9.5 %collective-permute-start.29 = (bf16[96,512]{1,0:T(8,128)(2,1)S(1)}, bf16[96,512]{1,0:T(8,128)(2,1)S(1)}, u32[]{:S(2)}, u32[]{:S(2)}) collective-permute-start(bf16[96,512]{1,0:T(8,128)(2,1)S(1)} %get-tuple-element.96), channel_id=1, source_target_pairs={{0,2},{1,3},{2,0},{3,1},{4,6},{5,7},{6,4},{7,5},{8,10},{9,11},{10,... | collective-permute-start | bytes 294920 | tf_op jit(solution)/shard_map/ppermute | solution.py:312

commit v5 on v4

--- a/solution.py
+++ b/solution.py
@@ -32,19 +32,6 @@
     silu_slope = sigmoid_value * (1.0 + hidden * (1.0 - sigmoid_value))
     curvature = sigmoid_value * (1.0 - sigmoid_value) * (2.0 + hidden * (1.0 - 2.0 * sigmoid_value))
     return silu_value, silu_slope, curvature
-
-
-def partner(index, step, count):
-    return index ^ step if count & (count - 1) == 0 else (index + step) % count
-
-
-def source(index, step, count):
-    return index ^ step if count & (count - 1) == 0 else (index + count - step) % count
-
-
-def chip_perm(count, step):
-    chips = count // CORES
-    return [(t, partner(t // CORES, step, chips) * CORES + t % CORES) for t in range(count)]
 
 
 def core_perm(count):
@@ -133,13 +120,6 @@
     return pack(*cotangent).astype(BF16), pack(*owned)
 
 
-def total_of(pieces):
-    total = pieces[0]
-    for piece in pieces[1:]:
-        total = total + piece.astype(F32)
-    return total
-
-
 def push_of(rates, values):
     return (-rates * values.T.astype(F32)).astype(BF16)
 
@@ -148,57 +128,72 @@
     return jnp.concatenate([own_ref[...], other_ref[...]], axis=axis)
 
 
-def send_pieces(chips, gate_ref, up_ref, down_ref, outs):
+def cut_piece(out, at, t, g, d, gate_ref, up_ref, down_ref):
+    fh = down_ref.shape[1]
+    out[at : at + g] = gate_ref[pl.ds(pl.multiple_of(t * g, g), g), :].astype(out.dtype)
+    out[at + g : at + 2 * g] = up_ref[pl.ds(pl.multiple_of(t * g, g), g), :].astype(out.dtype)
+    for i in range(d // g):
+        rows = pl.ds(pl.multiple_of(t * d + i * g, g), g)
+        out[at + 2 * g : at + 3 * g, i * fh : (i + 1) * fh] = down_ref[rows, :].astype(out.dtype)
+
+
+def send_pieces(chips, gate_ref, up_ref, down_ref, own, sent):
     tok = lax.axis_index("tok")
-    chip, core = tok // CORES, tok % CORES
+    g = gate_ref.shape[0] // (chips * CORES)
+    d = down_ref.shape[0] // (chips * CORES)
+    cut_piece(own, 0, tok, g, d, gate_ref, up_ref, down_ref)
+    for chip in range(chips):
+        t = chip * CORES + tok % CORES
+        cut_piece(sent, 3 * g * chip, t, g, d, gate_ref, up_ref, down_ref)
+
+
+def place_pieces(chips, mine, other, gate_ref, up_ref, down_ref):
+    core = lax.axis_index("tok") % CORES
     g = gate_ref.shape[0] // (chips * CORES)
     d = down_ref.shape[0] // (chips * CORES)
     fh = down_ref.shape[1]
-    for step, out in enumerate(outs):
-        t = partner(chip, step, chips) * CORES + core
-        out[:g] = gate_ref[pl.ds(pl.multiple_of(t * g, g), g), :].astype(out.dtype)
-        out[g : 2 * g] = up_ref[pl.ds(pl.multiple_of(t * g, g), g), :].astype(out.dtype)
-        for i in range(d // g):
-            rows = pl.ds(pl.multiple_of(t * d + i * g, g), g)
-            out[2 * g :, i * fh : (i + 1) * fh] = down_ref[rows, :].astype(out.dtype)
-
-
-def place_pieces(chips, pieces, gate_ref, up_ref, down_ref):
-    tok = lax.axis_index("tok")
-    chip, core = tok // CORES, tok % CORES
-    g = gate_ref.shape[0] // (chips * CORES)
-    d = down_ref.shape[0] // (chips * CORES)
-    fh = down_ref.shape[1]
-    for step in range(chips):
-        first = source(chip, step, chips) * CORES
-        for piece, t in ((pieces[2 * step], first + core), (pieces[2 * step + 1], first + 1 - core)):
-            gate_ref[pl.ds(pl.multiple_of(t * g, g), g), :] = piece[:g]
-            up_ref[pl.ds(pl.multiple_of(t * g, g), g), :] = piece[g : 2 * g]
+    for chip in range(chips):
+        at = 3 * g * chip
+        for piece, c in ((mine, core), (other, 1 - core)):
+            t = chip * CORES + c
+            gate_ref[pl.ds(pl.multiple_of(t * g, g), g), :] = piece[at : at + g]
+            up_ref[pl.ds(pl.multiple_of(t * g, g), g), :] = piece[at + g : at + 2 * g]
             for i in range(d // g):
                 rows = pl.ds(pl.multiple_of(t * d + i * g, g), g)
-                down_ref[rows, :] = piece[2 * g :, i * fh : (i + 1) * fh]
-
-
-def update_kernel(chips, ko, kx, vo, vx, ro, rx, w1t, w3t, w2, *rest):
-    outs, (gate, up, down) = rest[:chips], rest[chips:]
+                down_ref[rows, :] = piece[at + 2 * g : at + 3 * g, i * fh : (i + 1) * fh]
+
+
+def total_in_kernel(own, got):
+    chip = lax.axis_index("tok") // CORES
+    rows = own.shape[0]
+    chips = got.shape[0] // rows
+    total = own[...]
+    for step in range(1, chips):
+        at = lax.rem(chip + step, chips) * rows
+        total = total + got[pl.ds(pl.multiple_of(at, rows), rows), :].astype(F32)
+    return total
+
+
+def update_kernel(chips, ko, kx, vo, vx, ro, rx, w1, w3, w2, *rest):
+    outs, (gate, up, down) = rest[:2], rest[2:]
     keys = both(ko, kx)
     push = push_of(both(ro, rx, 1), both(vo, vx))
-    *_, mixed, _, _, gate_back, up_back = update_forward(w1t[...], w3t[...], w2[...], keys, push)
+    *_, mixed, _, _, gate_back, up_back = update_forward(w1[...].T, w3[...].T, w2[...], keys, push)
     down[...] = nt(push, mixed)
     gate[...] = nn(gate_back, keys)
     up[...] = nn(up_back, keys)
-    send_pieces(chips, gate, up, down, outs)
+    send_pieces(chips, gate, up, down, *outs)
 
 
 def saved_kernel(
-    chips, ko, kx, vo, vx, ro, rx, w1t, w3t, w2, go, gx, gain,
+    chips, ko, kx, vo, vx, ro, rx, w1, w3, w2, go, gx, gain,
     push_ref, up_slope_ref, silu_ref, back_slope_ref, back_curve_ref,
-    mixed_ref, gate_back_ref, up_back_ref, weighted_ref, prior_ref, down_ref,
+    mixed_ref, gate_back_ref, up_back_ref, weighted_ref, prior_ref, gate_ref, up_ref, down_ref,
 ):
     push = push_of(both(ro, rx, 1), both(vo, vx))
     push_ref[...] = push
     up_pre, silu, slope, curvature, mixed, down_back, back_slope, gate_back, up_back = (
-        update_forward(w1t[...], w3t[...], w2[...], both(ko, kx), push)
+        update_forward(w1[...].T, w3[...].T, w2[...], both(ko, kx), push)
     )
     up_slope_ref[...] = up_pre * slope
     silu_ref[...] = silu
@@ -212,35 +207,45 @@
     tok = lax.axis_index("tok")
     g, (d, fh) = prior_ref.shape[0] // 3, (down_ref.shape[0] // (chips * CORES), down_ref.shape[1])
     rows = pl.ds(pl.multiple_of(tok * g, g), g)
-    prior_ref[:g] = w1t[rows, :].astype(F32)
-    prior_ref[g : 2 * g] = w3t[rows, :].astype(F32)
+    gate_ref[...] = w1[...].astype(F32).T
+    up_ref[...] = w3[...].astype(F32).T
+    prior_ref[:g] = gate_ref[rows, :]
+    prior_ref[g : 2 * g] = up_ref[rows, :]
     down_ref[...] = w2[...].astype(F32).T
     for i in range(d // g):
         rows = pl.ds(pl.multiple_of(tok * d + i * g, g), g)
         prior_ref[2 * g :, i * fh : (i + 1) * fh] = down_ref[rows, :]
 
 
+def repeat(out, piece):
+    rows = piece.shape[0]
+    for chip in range(out.shape[0] // rows):
+        out[chip * rows : (chip + 1) * rows] = piece
+
+
 def owner_forward_kernel(fh, prior, *refs):
     fast, moved = refs[-2:]
-    fast[...], moved[...] = owner_forward(prior[...], total_of([r[...] for r in refs[:-2]]), fh)
+    piece, moved[...] = owner_forward(prior[...], total_in_kernel(*refs[:-2]), fh)
+    repeat(fast, piece)
 
 
 def owner_backward_kernel(fh, prior, moved, *refs):
     cotangent, owned = refs[-2:]
-    fast_grad = total_of([r[...] for r in refs[:-2]])
-    cotangent[...], owned[...] = owner_backward(prior[...], moved[...], fast_grad, fh)
+    fast_grad = total_in_kernel(*refs[:-2])
+    piece, owned[...] = owner_backward(prior[...], moved[...], fast_grad, fh)
+    repeat(cotangent, piece)
 
 
 def owner_result_kernel(fh, owned, *refs):
     gate, up, down = refs[-3:]
-    bars = total_of([r[...] for r in refs[:-3]])
+    bars = total_in_kernel(*refs[:-3])
     gate[...], up[...], down[...] = unpack(owned[...] - bars, fh)
 
 
 def apply_kernel(chips, *refs):
-    pieces, refs = refs[: 2 * chips], refs[2 * chips :]
+    pieces, refs = refs[:2], refs[2:]
     qo, qx, weighted, f1t, f3t, f2t, output, mixed, up_slope, silu, sums = refs
-    place_pieces(chips, pieces, f1t, f3t, f2t)
+    place_pieces(chips, *pieces, f1t, f3t, f2t)
     output[...], mixed[...], up_slope[...], silu[...], sums[...] = apply_forward(
         f1t[...], f3t[...], f2t[...], both(qo, qx), weighted[...]
     )
@@ -248,13 +253,13 @@
 
 def back_kernel(chips, heads, *refs):
     sums, f2t, output, weighted, mixed, up_slope, silu, qo, qx, gate_back, up_back = refs[:11]
-    outs, (gate, up, down) = refs[11 : 11 + chips], refs[11 + chips :]
+    outs, (gate, up, down) = refs[11:13], refs[13:]
     width = heads * output.shape[0]
     gb, ub, gate[...], up[...], down[...] = apply_backward(
         f2t[...], sums[...], width, output[...], weighted[...], mixed[...], up_slope[...], silu[...],
         both(qo, qx),
     )
-    send_pieces(chips, gate, up, down, outs)
+    send_pieces(chips, gate, up, down, *outs)
     own = gate_back.shape[1]
     gate_back[...], up_back[...] = gb[:, :own], ub[:, :own]
 
@@ -264,23 +269,23 @@
 
 
 def second_kernel(chips, *refs):
-    pieces, refs = refs[: 2 * chips], refs[2 * chips :]
+    pieces, refs = refs[:2], refs[2:]
     ko, kx, push, up_slope, silu, back_slope, back_curve = refs[:7]
     c1t, c3t, c2t, dbb_ref, upb_ref, gpb_ref = refs[7:13]
-    outs, (gate, up, down) = refs[13 : 13 + chips], refs[13 + chips :]
-    place_pieces(chips, pieces, c1t, c3t, c2t)
+    outs, (gate, up, down) = refs[13:15], refs[15:]
+    place_pieces(chips, *pieces, c1t, c3t, c2t)
     dbb, upb, gpb, gate[...], up[...], down[...] = second_adjoint(
         c1t[...], c3t[...], c2t[...], both(ko, kx), push[...],
         up_slope[...], silu[...], back_slope[...], back_curve[...],
     )
-    send_pieces(chips, gate, up, down, outs)
+    send_pieces(chips, gate, up, down, *outs)
     own = dbb_ref.shape[1]
     dbb_ref[...], upb_ref[...], gpb_ref[...] = dbb[:, :own], upb[:, :own], gpb[:, :own]
 
 
-def token_grads(rates, mixed, dbb, upb, gpb, gate_back, up_back, c1t, c3t, c2t, w1t, w3t, w2):
+def token_grads(rates, mixed, dbb, upb, gpb, gate_back, up_back, c1t, c3t, c2t, w1, w3, w2):
     value_grad = (rates * (nn(c2t, mixed) + tn(w2, dbb))).T.astype(BF16)
-    key_total = tn(gate_back, c1t) + tn(up_back, c3t) + tn(gpb, w1t) + tn(upb, w3t)
+    key_total = tn(gate_back, c1t) + tn(up_back, c3t) + tn(gpb, w1.T) + tn(upb, w3.T)
     return value_grad, (-key_total).astype(BF16)
 
 
@@ -307,54 +312,43 @@
     )(*args)
 
 
-def exchange(pieces, chips):
-    count = chips * CORES
-    got = [lax.ppermute(pieces[s], "tok", chip_perm(count, s)) for s in reversed(range(1, chips))]
-    return [pieces[0], *got]
+def over_chips(blocks, count):
+    groups = [list(range(core, count, CORES)) for core in range(CORES)]
+    return lax.all_to_all(blocks, "tok", 0, 0, axis_index_groups=groups, tiled=True)
+
+
+def gather(copies, count):
+    mine = over_chips(copies, count)
+    return mine, lax.ppermute(mine, "tok", core_perm(count))
 
 
 def head_sum(part, heads):
-    if heads & (heads - 1) == 0:
-        step = 1
-        while step < heads:
-            part = part + lax.ppermute(part, "head", [(h, h ^ step) for h in range(heads)])
-            step *= 2
-        return part
-    return lax.psum(part, "head")
-
-
-def gather(packed, chips):
-    count = chips * CORES
-    pieces = [None] * count
-    for step in range(chips):
-        mine = packed if step == 0 else lax.ppermute(packed, "tok", chip_perm(count, step))
-        pieces[2 * step] = mine
-        pieces[2 * step + 1] = lax.ppermute(mine, "tok", core_perm(count))
-    return pieces
-
-
-def sliced_pieces(gate, up, down, tok, chips):
-    chip, core = tok // CORES, tok % CORES
-    g, d = gate.shape[0] // (chips * CORES), down.shape[0] // (chips * CORES)
-    pieces = []
-    for step in range(chips):
-        t = partner(chip, step, chips) * CORES + core
-        piece = pack(
-            lax.dynamic_slice_in_dim(gate, t * g, g, 0),
-            lax.dynamic_slice_in_dim(up, t * g, g, 0),
-            lax.dynamic_slice_in_dim(down, t * d, d, 0),
-        )
-        pieces.append(piece if step == 0 else piece.astype(BF16))
-    return pieces
-
-
-def whole_matrices(pieces, tok, chips, fh):
-    chip, core = tok // CORES, tok % CORES
-    held = jnp.zeros((chips * CORES,) + pieces[0].shape, pieces[0].dtype)
-    for step in range(chips):
-        first = source(chip, step, chips) * CORES
-        held = lax.dynamic_update_index_in_dim(held, pieces[2 * step], first + core, 0)
-        held = lax.dynamic_update_index_in_dim(held, pieces[2 * step + 1], first + 1 - core, 0)
+    total = part
+    for step in range(1, heads):
+        total = total + lax.ppermute(part, "head", [(h, (h + step) % heads) for h in range(heads)])
+    return total
+
+
+def sliced_pieces(gate, up, down, tok, count):
+    g, d = gate.shape[0] // count, down.shape[0] // count
+    rows = lambda x, size, t: lax.dynamic_slice_in_dim(x, t * size, size, 0)
+    piece = lambda t: pack(rows(gate, g, t), rows(up, g, t), rows(down, d, t))
+    sent = [piece(t + tok % CORES) for t in range(0, count, CORES)]
+    return piece(tok), jnp.concatenate(sent, axis=0).astype(BF16)
+
+
+def total_of(own, got, tok):
+    blocks = got.reshape((-1,) + own.shape)
+    chip = lax.broadcasted_iota(jnp.int32, (blocks.shape[0], 1, 1), 0)
+    others = jnp.where(chip == tok // CORES, 0.0, blocks.astype(F32))
+    return own + jnp.sum(others, axis=0)
+
+
+def whole_matrices(mine, other, tok, count, fh):
+    shape = (count // CORES, -1, mine.shape[1])
+    pair = jnp.stack([mine.reshape(shape), other.reshape(shape)], axis=1)
+    pair = jnp.where(tok % CORES == 0, pair, pair[:, ::-1])
+    held = pair.reshape((count, -1, mine.shape[1]))
     parts = jax.vmap(lambda x: unpack(x, fh))(held)
     return tuple(x.reshape((-1, x.shape[-1])) for x in parts)
 
@@ -375,19 +369,18 @@
     chips = count // CORES
     own, dh = key_input.shape
     n = own * CORES
-    w1t, w3t, w2 = gate_prior[0].T, up_prior[0].T, down_prior[0]
+    w1, w3, w2 = gate_prior[0], up_prior[0], down_prior[0]
     fh = w2.shape[0]
     g, d = fh // count, dh // count
     tiled = g % ROW_TILE == 0 and d % g == 0 and dh // g == fh // g * (d // g)
     rates = token_rates.T
     gain = out_gain[None, :]
     product = 2 * n * dh * fh
-    owner = ((3 * g, dh), BF16), ((3 * g, dh), F32)
+    owner = ((3 * g * chips, dh), BF16), ((3 * g, dh), F32)
 
     pair = lambda x: lax.ppermute(x, "tok", core_perm(count))
     key_other, value_other, rate_other = pair(key_input), pair(value_input), pair(rates)
-    query_other, grad_other = pair(query_input), pair(out_grad)
-    messages = [((3 * g, dh), F32)] + [((3 * g, dh), BF16)] * (chips - 1)
+    messages = [((3 * g, dh), F32), ((3 * g * chips, dh), BF16)]
     matrices = [((fh, dh), BF16), ((fh, dh), BF16), ((dh, fh), BF16)]
     sums_scratch = [((fh, dh), F32), ((fh, dh), F32), ((dh, fh), F32)]
     hidden = ((fh, n), F32)
@@ -395,7 +388,7 @@
     joined = lambda a, b, axis=0: jnp.concatenate([a, b], axis=axis)
 
     inputs = (
-        key_input, key_other, value_input, value_other, rates, rate_other, w1t, w3t, w2,
+        key_input, key_other, value_input, value_other, rates, rate_other, w1, w3, w2,
     )
     if tiled:
         pieces = call(
@@ -406,39 +399,45 @@
             "update",
             6 * product,
         )
+        query_later, grad_later, *pieces = lax.optimization_barrier(
+            (query_input, out_grad, *pieces)
+        )
+        query_other, grad_other = pair(query_later), pair(grad_later)
         push, up_slope, silu, back_slope, back_curve, mixed, gate_back, up_back, weighted, prior = call(
             functools.partial(saved_kernel, chips),
             [((dh, n), BF16)] + [hidden] * 4 + [own_hidden] * 3 + [((dh, n), F32), owner[1]],
             (*inputs, out_grad, grad_other, gain),
-            [((dh, fh), F32)],
+            sums_scratch,
             "saved",
             3 * product,
         )
     else:
+        query_other, grad_other = pair(query_input), pair(out_grad)
         keys = joined(key_input, key_other)
         queries = joined(query_input, query_other)
         push = push_of(joined(rates, rate_other, 1), joined(value_input, value_other))
         up_pre, silu, slope, curvature, mixed, down_back, back_slope, gate_back, up_back = (
-            update_forward(w1t, w3t, w2, keys, push)
+            update_forward(w1.T, w3.T, w2, keys, push)
         )
         up_slope, back_curve = up_pre * slope, down_back * up_pre * curvature
         weighted = (joined(out_grad, grad_other).astype(F32) * gain).T
-        pieces = sliced_pieces(nn(gate_back, keys), nn(up_back, keys), nt(push, mixed), tok, chips)
+        pieces = sliced_pieces(nn(gate_back, keys), nn(up_back, keys), nt(push, mixed), tok, count)
         mixed, gate_back, up_back = mixed[:, :own], gate_back[:, :own], up_back[:, :own]
         prior = pack(
             *(
                 lax.dynamic_slice_in_dim(x, tok * rows, rows, 0).astype(F32)
-                for x, rows in ((w1t, g), (w3t, g), (w2.T, d))
+                for x, rows in ((w1.T, g), (w3.T, g), (w2.T, d))
             )
         )
-    pieces = exchange(pieces, chips)
+    pieces = pieces[0], over_chips(pieces[1], count)
     if tiled:
         fast, moved = call(
             functools.partial(owner_forward_kernel, fh), owner, (prior, *pieces), name="owner_forward"
         )
     else:
-        fast, moved = owner_forward(prior, total_of(pieces), fh)
-    pieces = gather(fast, chips)
+        fast, moved = owner_forward(prior, total_of(*pieces, tok), fh)
+        fast = jnp.tile(fast, (chips, 1))
+    pieces = gather(fast, count)
 
     if tiled:
         f1t, f3t, f2t, output, q_mixed, q_slope, q_silu, part = call(
@@ -449,7 +448,7 @@
             flops=3 * product,
         )
     else:
-        f1t, f3t, f2t = whole_matrices(pieces, tok, chips, fh)
+        f1t, f3t, f2t = whole_matrices(*pieces, tok, count, fh)
         output, q_mixed, q_slope, q_silu, part = apply_forward(f1t, f3t, f2t, queries, weighted)
     sums = head_sum(part, heads)
     if tiled:
@@ -472,9 +471,9 @@
         q_gate_back, q_up_back, *grads = apply_backward(
             f2t, sums, heads * dh, output, weighted, q_mixed, q_slope, q_silu, queries
         )
-        pieces = sliced_pieces(*grads, tok, chips)
+        pieces = sliced_pieces(*grads, tok, count)
         query_grad = (tn(q_gate_back[:, :own], f1t) + tn(q_up_back[:, :own], f3t)).astype(BF16)
-    pieces = exchange(pieces, chips)
+    pieces = pieces[0], over_chips(pieces[1], count)
     if tiled:
         cotangent, owned = call(
             functools.partial(owner_backward_kernel, fh),
@@ -483,8 +482,9 @@
             name="owner_backward",
         )
     else:
-        cotangent, owned = owner_backward(prior, moved, total_of(pieces), fh)
-    pieces = gather(cotangent, chips)
+        cotangent, owned = owner_backward(prior, moved, total_of(*pieces, tok), fh)
+        cotangent = jnp.tile(cotangent, (chips, 1))
+    pieces = gather(cotangent, count)
 
     if tiled:
         c1t, c3t, c2t, dbb, upb, gpb, *pieces = call(
@@ -496,14 +496,14 @@
             6 * product,
         )
     else:
-        c1t, c3t, c2t = whole_matrices(pieces, tok, chips, fh)
+        c1t, c3t, c2t = whole_matrices(*pieces, tok, count, fh)
         dbb, upb, gpb, *bars = second_adjoint(
             c1t, c3t, c2t, keys, push, up_slope, silu, back_slope, back_curve
         )
-        pieces = sliced_pieces(*bars, tok, chips)
+        pieces = sliced_pieces(*bars, tok, count)
         dbb, upb, gpb = dbb[:, :own], upb[:, :own], gpb[:, :own]
     token_args = (
-        rates, mixed, dbb, upb, gpb, gate_back, up_back, c1t, c3t, c2t, w1t, w3t, w2,
+        rates, mixed, dbb, upb, gpb, gate_back, up_back, c1t, c3t, c2t, w1, w3, w2,
     )
     if tiled:
         value_grad, key_grad = call(
@@ -511,7 +511,7 @@
         )
     else:
         value_grad, key_grad = token_grads(*token_args)
-    pieces = exchange(pieces, chips)
+    pieces = pieces[0], over_chips(pieces[1], count)
     if tiled:
         results = call(
             functools.partial(owner_result_kernel, fh),
@@ -520,7 +520,7 @@
             name="owner_result",
         )
     else:
-        results = unpack(owned - total_of(pieces), fh)
+        results = unpack(owned - total_of(*pieces, tok), fh)
     results = [r.T[None] for r in results]
     return (query_grad, key_grad, value_grad, *results)
 

time: 75.4 us -> 108 us (1.43)
  blocking collectives: 0 us -> 42.2 us
  local copies, waits for them, and re-layouts: 2.13 us -> 17.2 us
  waiting for transfers between devices: 34.7 us -> 20.7 us
  starting transfers between devices: 28.8 us -> 15.1 us
  Pallas kernels: 8.78 us -> 10.7 us
    all_to_all x0 -> x3, blocking collectives: none -> 42.2 us  [over_chips(): lax.all_to_all(blocks, 'tok', 0, 0, axis_index_groups=groups, tiled=True)]
    ppermute x25 -> x5, waiting for transfers between devices: 34.6 us -> 5.63 us  [the longest x3 3.91 us: head_sum(): lax.ppermute(part, 'head', [(h, (h + step) % heads) for h in range(heads)])]
    ppermute x25 -> x5, starting transfers between devices: 27.7 us -> 3.6 us  [the longest x3 3.6 us: head_sum(): lax.ppermute(part, 'head', [(h, (h + step) % heads) for h in range(heads)])]
    unnamed x18 -> x98, local copies, waits for them, and re-layouts: 2.13 us -> 17.2 us
    all_to_all x0 -> x2, waiting for transfers between devices: none -> 10.8 us  [over_chips(): lax.all_to_all(blocks, 'tok', 0, 0, axis_index_groups=groups, tiled=True)]
    all_to_all x0 -> x2, starting transfers between devices: none -> 9.98 us  [over_chips(): lax.all_to_all(blocks, 'tok', 0, 0, axis_index_groups=groups, tiled=True)]
    ppermute x5, waiting for transfers between devices: 0.01 us -> 4.25 us  [per_device(): pair = lambda x: lax.ppermute(x, 'tok', core_perm(count))]
    pallas_call x10, Pallas kernels: 8.78 us -> 10.7 us  [call(): pl.pallas_call(kernel, out_shape=[jax.ShapeDtypeStruct(s, t) for s, t in...]
  transfers between devices with their start and end apart: 30 -> 12, of which waited for: 16 -> 10; matrix products, arithmetic and copies ran while one was open for 2% -> 0% of each run, Pallas kernels for 6% -> 3%
where the time goes in v5:
time: 108 us; the launch traced here: 107 us
  blocking collectives  42.2 us (39%)
  waiting for transfers between devices  20.7 us (19%)
  local copies, waits for them, and re-layouts  17.2 us (16%)
  starting transfers between devices  15.1 us (14%)
  Pallas kernels  10.7 us (10%)
    all_to_all x3, blocking collectives, over_chips(): lax.all_to_all(blocks, 'tok', 0, 0, axis_index_groups=groups, tiled=True)  42.2 us
    unnamed x98, local copies, waits for them, and re-layouts  17.2 us
    all_to_all x2, waiting for transfers between devices, over_chips(): lax.all_to_all(blocks, 'tok', 0, 0, axis_index_groups=groups, tiled=True)  10.8 us
    pallas_call x10, Pallas kernels, call(): pl.pallas_call(kernel, out_shape=[jax.ShapeDtypeStruct(s, t) for s, t in...  10.7 us
    all_to_all x2, starting transfers between devices, over_chips(): lax.all_to_all(blocks, 'tok', 0, 0, axis_index_groups=groups, tiled=True)  9.98 us
    ppermute x5, waiting for transfers between devices, per_device(): pair = lambda x: lax.ppermute(x, 'tok', core_perm(count))  4.25 us
    ppermute x3, waiting for transfers between devices, head_sum(): lax.ppermute(part, 'head', [(h, (h + step) % heads) for h in range(heads)])  3.91 us
    ppermute x3, starting transfers between devices, head_sum(): lax.ppermute(part, 'head', [(h, (h + step) % heads) for h in range(heads)])  3.6 us
  transfers between devices with their start and end apart: 12, of which 10 were waited for; matrix products, arithmetic and copies ran while one was open for 0% of the time, Pallas kernels for 3%

profile of v5, /device:TPU:0, one launch (start us, length us, event | category | flops | bytes accessed | tf_op | source)
XLA Modules:
  0.0 106.8 jit_solution(10507009743384660005)
XLA Ops:
  0.6 0.5 collective-permute-start.1
  1.3 0.5 collective-permute-start.2
  1.8 0.9 collective-permute-done.2.rx
  2.9 0.9 copy-done.1
  3.9 0.9 copy-done.3
  4.8 0.9 copy-done.5
  5.8 0.9 copy-done.7
  6.7 0.9 copy-done.17
  7.7 2.0 %update.1 = (f32[96,512]{1,0:T(8,128)S(1)}, bf16[384,512]{1,0:T(8,128)(2,1)}) custom-call(bf16[256,512]{1,0:T(8,128)(2,1)S(1)} %copy-done.7, bf16[256,512]{1,0:T(8,128)(2,1)S(1)} %collective-permute-done.kx.refs_3_, bf16[256,512]{1,0:T(8,128)(2,1)S(1)} %copy-done.17, bf16[256,512]{1,0:T(8,128)(2,1)S(1)} %collective-permute-done.1.vx, f32[1,256]{1,0:T(1,128)S(1)} %bitcast.44, ...), custom_call_target="tpu_custom_call" | custom-call | flops 805306368 | bytes 1837056 | tf_op jit(solution)/shard_map/update/pallas_call | solution.py:299
  9.7 0.7 copy-done.29
  10.4 6.4 %all-to-all-start = ((bf16[4,96,512]{2,1,0:T(8,128)(2,1)}), bf16[4,96,512]{2,1,0:T(8,128)(2,1)S(1)}, u32[]{:S(2)}, u32[]{:S(2)}) async-start(bf16[4,96,512]{2,1,0:T(8,128)(2,1)} %bitcast.5), calls=%async_computation | async-start | bytes 786432 | tf_op jit(solution)/shard_map/all_to_all | solution.py:317
  16.7 1.5 %collective-permute-done.3.gx = bf16[256,512]{1,0:T(8,128)(2,1)S(1)} collective-permute-done((bf16[256,512]{1,0:T(8,128)(2,1)S(1)}, bf16[256,512]{1,0:T(8,128)(2,1)S(1)}, u32[]{:S(2)}, u32[]{:S(2)}) %collective-permute-start.3) | collective-permute-done | bytes 262176 | tf_op jit(solution)/shard_map/ppermute | solution.py:381
  18.3 0.9 copy-done.18
  19.3 0.9 copy-done.20
  20.2 0.9 copy-done.22
  21.2 1.3 %saved.1 = (bf16[512,512]{1,0:T(8,128)(2,1)S(1)}, f32[256,512]{1,0:T(8,128)S(1)}, f32[256,512]{1,0:T(8,128)S(1)}, f32[256,512]{1,0:T(8,128)S(1)}, f32[256,512]{1...) custom-call(bf16[256,512]{1,0:T(8,128)(2,1)S(1)} %copy-done.8, ...), custom_call_target="tpu_custom_call" | custom-call | flops 402653184 | bytes 2363392 | tf_op jit(solution)/shard_map/saved/pallas_call | solution.py:299
  22.4 0.8 copy-done.9
  23.2 0.8 copy-done.11
  24.0 0.8 copy-done.13
  24.8 0.8 copy-done.15
  25.6 0.6 copy-done.31
  26.3 0.6 copy-done.33
  26.9 0.6 copy-done.35
  27.6 1.2 %all-to-all-done = bf16[4,96,512]{2,1,0:T(8,128)(2,1)S(1)} async-done(((bf16[4,96,512]{2,1,0:T(8,128)(2,1)}), bf16[4,96,512]{2,1,0:T(8,128)(2,1)S(1)}, u32[]{:S(2)}, u32[]{:S(2)}) %all-to-all-start) | async-done | bytes 393248 | tf_op jit(solution)/shard_map/all_to_all | solution.py:317
  28.7 0.9 copy-done.30
  29.9 15.8 %all_to_all.55 = bf16[4,96,512]{2,1,0:T(8,128)(2,1)S(1)} all-to-all(bf16[4,96,512]{2,1,0:T(8,128)(2,1)S(1)} %bitcast.42), channel_id=1, replica_groups={{0,2,4,6},{1,3,5,7},{8,10,12,14},{9,11,13,15},{16,18,20,22},{17,19,21,2..., dimensions={0} | all-to-all | bytes 786432 | tf_op jit(solution)/shard_map/all_to_all | solution.py:317
  45.7 0.5 collective-permute-start.5
  46.2 1.6 %collective-permute-done.5.refs_3_.refs_8_ = bf16[256,512]{1,0:T(8,128)(2,1)S(1)} collective-permute-done((bf16[256,512]{1,0:T(8,128)(2,1)S(1)}, bf16[256,512]{1,0:T(8,128)(2,1)S(1)}, u32[]{:S(2)}, u32[]{:S(2)}) %collective-permute-start.5) | collective-permute-done | bytes 262176 | tf_op jit(solution)/shard_map/ppermute | solution.py:381
  47.8 0.8 apply.1
  48.6 2.5 %collective-permute-start.8 = (f32[2,512]{1,0:T(2,128)S(1)}, f32[2,512]{1,0:T(2,128)S(1)}, u32[]{:S(2)}, u32[]{:S(2)}) collective-permute-start(f32[2,512]{1,0:T(2,128)S(1)} %get-tuple-element.60), channel_id=1, source_target_pairs={{0,24},{8,0},{16,8},{24,16},{1,25},{9,1},{17,9},{25,17},{2,26},{10... | collective-permute-start | bytes 12296 | tf_op jit(solution)/shard_map/ppermute | solution.py:328
  51.1 0.5 collective-permute-start.7
  51.6 0.6 collective-permute-start.6
  52.4 2.3 %collective-permute-done.7 = f32[2,512]{1,0:T(2,128)S(1)} collective-permute-done((f32[2,512]{1,0:T(2,128)S(1)}, f32[2,512]{1,0:T(2,128)S(1)}, u32[]{:S(2)}, u32[]{:S(2)}) %collective-permute-start.7) | collective-permute-done | bytes 4128 | tf_op jit(solution)/shard_map/ppermute | solution.py:328
  54.7 1.4 %collective-permute-done.6 = f32[2,512]{1,0:T(2,128)S(1)} collective-permute-done((f32[2,512]{1,0:T(2,128)S(1)}, f32[2,512]{1,0:T(2,128)S(1)}, u32[]{:S(2)}, u32[]{:S(2)}) %collective-permute-start.6) | collective-permute-done | bytes 4128 | tf_op jit(solution)/shard_map/ppermute | solution.py:328
  56.1 1.0 apply_back.1
  57.2 13.1 %all_to_all.56 = bf16[4,96,512]{2,1,0:T(8,128)(2,1)S(1)} all-to-all(bf16[4,96,512]{2,1,0:T(8,128)(2,1)S(1)} %bitcast.40), channel_id=1, replica_groups={{0,2,4,6},{1,3,5,7},{8,10,12,14},{9,11,13,15},{16,18,20,22},{17,19,21,2..., dimensions={0} | all-to-all | bytes 786432 | tf_op jit(solution)/shard_map/all_to_all | solution.py:317
  70.5 0.7 copy-done.27
  71.2 13.2 %all_to_all.57 = bf16[4,96,512]{2,1,0:T(8,128)(2,1)S(1)} all-to-all(bf16[4,96,512]{2,1,0:T(8,128)(2,1)S(1)} %bitcast.41), channel_id=1, replica_groups={{0,2,4,6},{1,3,5,7},{8,10,12,14},{9,11,13,15},{16,18,20,22},{17,19,21,2..., dimensions={0} | all-to-all | bytes 786432 | tf_op jit(solution)/shard_map/all_to_all | solution.py:317
  84.4 1.7 %collective-permute-done.9.refs_1_ = bf16[384,512]{1,0:T(8,128)(2,1)S(1)} collective-permute-done((bf16[384,512]{1,0:T(8,128)(2,1)S(1)}, bf16[384,512]{1,0:T(8,128)(2,1)S(1)}, u32[]{:S(2)}, u32[]{:S(2)}) %collective-permute-start.9) | collective-permute-done | bytes 393248 | tf_op jit(solution)/shard_map/ppermute | solution.py:322
  86.1 2.2 %second_adjoint.1 = (bf16[256,512]{1,0:T(8,128)(2,1)S(1)}, bf16[256,512]{1,0:T(8,128)(2,1)S(1)}, bf16[512,256]{1,0:T(8,128)(2,1)S(1)}, bf16[256,256]{1,0:T(8,128...) custom-call(bf16[384,512]{1,0:T(8,128)(2,1)S(1)} %bitcast.30, ...), custom_call_target="tpu_custom_call" | custom-call | flops 805306368 | bytes 3932160 | tf_op jit(solution)/shard_map/second_adjoint/pallas_call | solution.py:299
  88.4 0.6 copy-done.37
  89.0 0.6 copy-done.39
  89.6 0.6 copy-done.41
  90.3 3.6 %all-to-all-start.4 = ((bf16[4,96,512]{2,1,0:T(8,128)(2,1)}), bf16[4,96,512]{2,1,0:T(8,128)(2,1)S(1)}, u32[]{:S(2)}, u32[]{:S(2)}) async-start(bf16[4,96,512]{2,1,0:T(8,128)(2,1)} %bitcast.13), calls=%async_computation.4 | async-start | bytes 786432 | tf_op jit(solution)/shard_map/all_to_all | solution.py:317
  94.0 1.0 query_grad.1
  95.2 1.4 %token_grads.1 = (bf16[256,512]{1,0:T(8,128)(2,1)}, bf16[256,512]{1,0:T(8,128)(2,1)}) custom-call(f32[1,256]{1,0:T(1,128)S(1)} %bitcast.46, bf16[256,256]{1,0:T(8,128)(2,1)S(1)} %copy-done.32, bf16[256,256]{1,0:T(8,128)(2,1)S(1)} %copy-done.38, bf16[256,256]{1,0:T(8,128)(2,1)S(1)} %copy-done.40, bf16[256,256]{1,0:T(8,128)(2,1)S(1)} %copy-done.42, ...), custom_call_target="tpu_custom_call" | custom-call | flops 402653184 | bytes 2360320 | tf_op jit(solution)/shard_map/token_grads/pallas_call | solution.py:299
  96.5 9.6 %all-to-all-done.4 = bf16[4,96,512]{2,1,0:T(8,128)(2,1)S(1)} async-done(((bf16[4,96,512]{2,1,0:T(8,128)(2,1)}), bf16[4,96,512]{2,1,0:T(8,128)(2,1)S(1)}, u32[]{:S(2)}, u32[]{:S(2)}) %all-to-all-start.4) | async-done | bytes 393248 | tf_op jit(solution)/shard_map/all_to_all | solution.py:317
  106.1 0.7 owner_result.1
  (88 shorter events, 1.2 us)
Async XLA Ops:
  0.6 2.1 %collective-permute-start.1 = (bf16[256,512]{1,0:T(8,128)(2,1)}, bf16[256,512]{1,0:T(8,128)(2,1)S(1)}, u32[]{:S(2)}, u32[]{:S(2)}) collective-permute-start(bf16[256,512]{1,0:T(8,128)(2,1)} %vo.3), channel_id=1, source_target_pairs={{0,1},{1,0},{2,3},{3,2},{4,5},{5,4},{6,7},{7,6},{8,9},{9,8},{10,11... | collective-permute-start | bytes 786440 | tf_op jit(solution)/shard_map/ppermute | solution.py:381
  1.2 1.7 %collective-permute-start = (bf16[256,512]{1,0:T(8,128)(2,1)}, bf16[256,512]{1,0:T(8,128)(2,1)S(1)}, u32[]{:S(2)}, u32[]{:S(2)}) collective-permute-start(bf16[256,512]{1,0:T(8,128)(2,1)} %refs_2_.3), channel_id=1, source_target_pairs={{0,1},{1,0},{2,3},{3,2},{4,5},{5,4},{6,7},{7,6},{8,9},{9,8},{10,11... | collective-permute-start | bytes 786440 | tf_op jit(solution)/shard_map/ppermute | solution.py:381
  1.3 1.4 %collective-permute-start.2 = (f32[1,256]{1,0:T(1,128)S(1)}, f32[1,256]{1,0:T(1,128)S(1)}, u32[]{:S(2)}, u32[]{:S(2)}) collective-permute-start(f32[1,256]{1,0:T(1,128)S(1)} %bitcast.43), channel_id=1, source_target_pairs={{0,1},{1,0},{2,3},{3,2},{4,5},{5,4},{6,7},{7,6},{8,9},{9,8},{10,11... | collective-permute-start | bytes 3080 | tf_op jit(solution)/shard_map/ppermute | solution.py:381
  2.7 7.0 %copy-start.21 = (bf16[256,512]{1,0:T(8,128)(2,1)}, bf16[256,512]{1,0:T(8,128)(2,1)S(1)}, u32[]{:S(2)}) copy-start(bf16[256,512]{1,0:T(8,128)(2,1)S(1)} %collective-permute-done.1.vx) | copy-start | bytes 786436
  2.9 0.9 copy-start.1
  3.9 0.9 copy-start.3
  4.8 0.9 copy-start.5
  5.8 0.9 copy-start.7
  6.7 0.9 copy-start.17
  7.7 9.1 %copy-start.19 = (bf16[256,512]{1,0:T(8,128)(2,1)S(1)}, bf16[256,512]{1,0:T(8,128)(2,1)}, u32[]{:S(2)}) copy-start(bf16[256,512]{1,0:T(8,128)(2,1)} %go.1) | copy-start | bytes 786436
  7.7 10.6 %copy-start.8 = (bf16[256,512]{1,0:T(8,128)(2,1)S(1)}, bf16[256,512]{1,0:T(8,128)(2,1)}, u32[]{:S(2)}) copy-start(bf16[256,512]{1,0:T(8,128)(2,1)} %refs_2_.3) | copy-start | bytes 786436
  10.3 7.9 %copy-start.48 = (f32[512]{0:T(512)S(1)}, f32[512]{0:T(512)}, u32[]{:S(2)}) copy-start(f32[512]{0:T(512)} %param.14) | copy-start | bytes 6148
  10.3 7.9 %copy-start.2 = (bf16[1,512,256]{2,1,0:T(8,128)(2,1)S(1)}, bf16[1,512,256]{2,1,0:T(8,128)(2,1)}, u32[]{:S(2)}) copy-start(bf16[1,512,256]{2,1,0:T(8,128)(2,1)} %param.15) | copy-start | bytes 786436
  10.3 7.9 %copy-start.4 = (bf16[1,512,256]{2,1,0:T(8,128)(2,1)S(1)}, bf16[1,512,256]{2,1,0:T(8,128)(2,1)}, u32[]{:S(2)}) copy-start(bf16[1,512,256]{2,1,0:T(8,128)(2,1)} %param.16) | copy-start | bytes 786436
  10.3 7.9 %copy-start.6 = (bf16[1,256,512]{2,1,0:T(8,128)(2,1)S(1)}, bf16[1,256,512]{2,1,0:T(8,128)(2,1)}, u32[]{:S(2)}) copy-start(bf16[1,256,512]{2,1,0:T(8,128)(2,1)} %param.17) | copy-start | bytes 786436
  10.4 18.4 %all-to-all-start = ((bf16[4,96,512]{2,1,0:T(8,128)(2,1)}), bf16[4,96,512]{2,1,0:T(8,128)(2,1)S(1)}, u32[]{:S(2)}, u32[]{:S(2)}) async-start(bf16[4,96,512]{2,1,0:T(8,128)(2,1)} %bitcast.5), calls=%async_computation | async-start | bytes 786432 | tf_op jit(solution)/shard_map/all_to_all | solution.py:317
  16.7 1.5 %collective-permute-start.3 = (bf16[256,512]{1,0:T(8,128)(2,1)S(1)}, bf16[256,512]{1,0:T(8,128)(2,1)S(1)}, u32[]{:S(2)}, u32[]{:S(2)}) collective-permute-start(bf16[256,512]{1,0:T(8,128)(2,1)S(1)} %copy-done.19), channel_id=1, source_target_pairs={{0,1},{1,0},{2,3},{3,2},{4,5},{5,4},{6,7},{7,6},{8,9},{9,8},{10,11... | collective-permute-start | bytes 786440 | tf_op jit(solution)/shard_map/ppermute | solution.py:381
  18.3 1.0 copy-start.18
  19.3 0.9 copy-start.20
  20.2 0.9 copy-start.22
  28.7 0.9 copy-start.30
  29.9 15.8 %copy-start = (bf16[256,512]{1,0:T(8,128)(2,1)S(1)}, bf16[256,512]{1,0:T(8,128)(2,1)}, u32[]{:S(2)}) copy-start(bf16[256,512]{1,0:T(8,128)(2,1)} %refs_7_.1) | copy-start | bytes 786436
  45.7 2.1 %collective-permute-start.4 = (bf16[384,512]{1,0:T(8,128)(2,1)S(1)}, bf16[384,512]{1,0:T(8,128)(2,1)S(1)}, u32[]{:S(2)}, u32[]{:S(2)}) collective-permute-start(bf16[384,512]{1,0:T(8,128)(2,1)S(1)} %bitcast.26), channel_id=1, source_target_pairs={{0,1},{1,0},{2,3},{3,2},{4,5},{5,4},{6,7},{7,6},{8,9},{9,8},{10,11... | collective-permute-start | bytes 1179656 | tf_op jit(solution)/shard_map/ppermute | solution.py:322
  45.7 2.1 %collective-permute-start.5 = (bf16[256,512]{1,0:T(8,128)(2,1)S(1)}, bf16[256,512]{1,0:T(8,128)(2,1)S(1)}, u32[]{:S(2)}, u32[]{:S(2)}) collective-permute-start(bf16[256,512]{1,0:T(8,128)(2,1)S(1)} %copy-done), channel_id=1, source_target_pairs={{0,1},{1,0},{2,3},{3,2},{4,5},{5,4},{6,7},{7,6},{8,9},{9,8},{10,11... | collective-permute-start | bytes 786440 | tf_op jit(solution)/shard_map/ppermute | solution.py:381
  48.6 8.5 %copy-start.23 = (bf16[256,512]{1,0:T(8,128)(2,1)}, bf16[256,512]{1,0:T(8,128)(2,1)S(1)}, u32[]{:S(2)}) copy-start(bf16[256,512]{1,0:T(8,128)(2,1)S(1)} %get-tuple-element.68.f1t) | copy-start | bytes 786436
  48.6 8.5 %copy-start.25 = (bf16[256,512]{1,0:T(8,128)(2,1)}, bf16[256,512]{1,0:T(8,128)(2,1)S(1)}, u32[]{:S(2)}) copy-start(bf16[256,512]{1,0:T(8,128)(2,1)S(1)} %get-tuple-element.69.f3t) | copy-start | bytes 786436
  48.6 3.8 %collective-permute-start.8 = (f32[2,512]{1,0:T(2,128)S(1)}, f32[2,512]{1,0:T(2,128)S(1)}, u32[]{:S(2)}, u32[]{:S(2)}) collective-permute-start(f32[2,512]{1,0:T(2,128)S(1)} %get-tuple-element.60), channel_id=1, source_target_pairs={{0,24},{8,0},{16,8},{24,16},{1,25},{9,1},{17,9},{25,17},{2,26},{10... | collective-permute-start | bytes 12296 | tf_op jit(solution)/shard_map/ppermute | solution.py:328
  51.1 3.6 %collective-permute-start.7 = (f32[2,512]{1,0:T(2,128)S(1)}, f32[2,512]{1,0:T(2,128)S(1)}, u32[]{:S(2)}, u32[]{:S(2)}) collective-permute-start(f32[2,512]{1,0:T(2,128)S(1)} %get-tuple-element.60), channel_id=1, source_target_pairs={{0,16},{8,24},{16,0},{24,8},{1,17},{9,25},{17,1},{25,9},{2,18},{10... | collective-permute-start | bytes 12296 | tf_op jit(solution)/shard_map/ppermute | solution.py:328
  51.6 4.5 %collective-permute-start.6 = (f32[2,512]{1,0:T(2,128)S(1)}, f32[2,512]{1,0:T(2,128)S(1)}, u32[]{:S(2)}, u32[]{:S(2)}) collective-permute-start(f32[2,512]{1,0:T(2,128)S(1)} %get-tuple-element.60), channel_id=1, source_target_pairs={{0,8},{8,16},{16,24},{24,0},{1,9},{9,17},{17,25},{25,1},{2,10},{10... | collective-permute-start | bytes 12296 | tf_op jit(solution)/shard_map/ppermute | solution.py:328
  57.2 13.2 %copy-start.43 = (bf16[256,256]{1,0:T(8,128)(2,1)}, bf16[256,256]{1,0:T(8,128)(2,1)S(1)}, u32[]{:S(2)}) copy-start(bf16[256,256]{1,0:T(8,128)(2,1)S(1)} %get-tuple-element.66.gate_back) | copy-start | bytes 393220
  57.2 13.1 %copy-start.45 = (bf16[256,256]{1,0:T(8,128)(2,1)}, bf16[256,256]{1,0:T(8,128)(2,1)S(1)}, u32[]{:S(2)}) copy-start(bf16[256,256]{1,0:T(8,128)(2,1)S(1)} %get-tuple-element.67.up_back) | copy-start | bytes 393220
  57.2 28.9 %copy-start.16 = (f32[256,512]{1,0:T(8,128)S(1)}, f32[256,512]{1,0:T(8,128)}, u32[]{:S(2)}) copy-start(f32[256,512]{1,0:T(8,128)} %copy-done.15) | copy-start | bytes 1572868
  70.3 15.8 %copy-start.12 = (f32[256,512]{1,0:T(8,128)S(1)}, f32[256,512]{1,0:T(8,128)}, u32[]{:S(2)}) copy-start(f32[256,512]{1,0:T(8,128)} %copy-done.11) | copy-start | bytes 1572868
  70.3 15.8 %copy-start.14 = (f32[256,512]{1,0:T(8,128)S(1)}, f32[256,512]{1,0:T(8,128)}, u32[]{:S(2)}) copy-start(f32[256,512]{1,0:T(8,128)} %copy-done.13) | copy-start | bytes 1572868
  71.2 14.9 %copy-start.10 = (f32[256,512]{1,0:T(8,128)S(1)}, f32[256,512]{1,0:T(8,128)}, u32[]{:S(2)}) copy-start(f32[256,512]{1,0:T(8,128)} %copy-done.9) | copy-start | bytes 1572868
  84.4 1.7 %collective-permute-start.9 = (bf16[384,512]{1,0:T(8,128)(2,1)S(1)}, bf16[384,512]{1,0:T(8,128)(2,1)S(1)}, u32[]{:S(2)}, u32[]{:S(2)}) collective-permute-start(bf16[384,512]{1,0:T(8,128)(2,1)S(1)} %bitcast.29), channel_id=1, source_target_pairs={{0,1},{1,0},{2,3},{3,2},{4,5},{5,4},{6,7},{7,6},{8,9},{9,8},{10,11... | collective-permute-start | bytes 1179656 | tf_op jit(solution)/shard_map/ppermute | solution.py:322
  90.3 3.6 %copy-start.24 = (bf16[256,512]{1,0:T(8,128)(2,1)S(1)}, bf16[256,512]{1,0:T(8,128)(2,1)}, u32[]{:S(2)}) copy-start(bf16[256,512]{1,0:T(8,128)(2,1)} %copy-done.23) | copy-start | bytes 786436
  90.3 3.6 %copy-start.26 = (bf16[256,512]{1,0:T(8,128)(2,1)S(1)}, bf16[256,512]{1,0:T(8,128)(2,1)}, u32[]{:S(2)}) copy-start(bf16[256,512]{1,0:T(8,128)(2,1)} %copy-done.25) | copy-start | bytes 786436
  90.3 3.6 %copy-start.44 = (bf16[256,256]{1,0:T(8,128)(2,1)S(1)}, bf16[256,256]{1,0:T(8,128)(2,1)}, u32[]{:S(2)}) copy-start(bf16[256,256]{1,0:T(8,128)(2,1)} %copy-done.43) | copy-start | bytes 393220
  90.3 3.6 %copy-start.46 = (bf16[256,256]{1,0:T(8,128)(2,1)S(1)}, bf16[256,256]{1,0:T(8,128)(2,1)}, u32[]{:S(2)}) copy-start(bf16[256,256]{1,0:T(8,128)(2,1)} %copy-done.45) | copy-start | bytes 393220
  90.3 15.8 %all-to-all-start.4 = ((bf16[4,96,512]{2,1,0:T(8,128)(2,1)}), bf16[4,96,512]{2,1,0:T(8,128)(2,1)S(1)}, u32[]{:S(2)}, u32[]{:S(2)}) async-start(bf16[4,96,512]{2,1,0:T(8,128)(2,1)} %bitcast.13), calls=%async_computation.4 | async-start | bytes 786432 | tf_op jit(solution)/shard_map/all_to_all | solution.py:317
  93.9 1.1 %copy-start.32 = (bf16[256,256]{1,0:T(8,128)(2,1)S(1)}, bf16[256,256]{1,0:T(8,128)(2,1)}, u32[]{:S(2)}) copy-start(bf16[256,256]{1,0:T(8,128)(2,1)} %copy-done.31) | copy-start | bytes 393220
  94.0 1.1 %copy-start.34 = (bf16[256,256]{1,0:T(8,128)(2,1)S(1)}, bf16[256,256]{1,0:T(8,128)(2,1)}, u32[]{:S(2)}) copy-start(bf16[256,256]{1,0:T(8,128)(2,1)} %copy-done.33) | copy-start | bytes 393220
  94.0 1.1 %copy-start.36 = (bf16[256,256]{1,0:T(8,128)(2,1)S(1)}, bf16[256,256]{1,0:T(8,128)(2,1)}, u32[]{:S(2)}) copy-start(bf16[256,256]{1,0:T(8,128)(2,1)} %copy-done.35) | copy-start | bytes 393220
  94.0 1.1 %copy-start.38 = (bf16[256,256]{1,0:T(8,128)(2,1)S(1)}, bf16[256,256]{1,0:T(8,128)(2,1)}, u32[]{:S(2)}) copy-start(bf16[256,256]{1,0:T(8,128)(2,1)} %copy-done.37) | copy-start | bytes 393220
  94.0 1.1 %copy-start.40 = (bf16[256,256]{1,0:T(8,128)(2,1)S(1)}, bf16[256,256]{1,0:T(8,128)(2,1)}, u32[]{:S(2)}) copy-start(bf16[256,256]{1,0:T(8,128)(2,1)} %copy-done.39) | copy-start | bytes 393220
  94.0 1.2 %copy-start.42 = (bf16[256,256]{1,0:T(8,128)(2,1)S(1)}, bf16[256,256]{1,0:T(8,128)(2,1)}, u32[]{:S(2)}) copy-start(bf16[256,256]{1,0:T(8,128)(2,1)} %copy-done.41) | copy-start | bytes 393220
  95.2 11.0 %copy-start.28 = (f32[96,512]{1,0:T(8,128)S(1)}, f32[96,512]{1,0:T(8,128)}, u32[]{:S(2)}) copy-start(f32[96,512]{1,0:T(8,128)} %copy-done.27) | copy-start | bytes 589828
  (13 other events, 9.1 us)

commit v6 on v3

v6 whole, which is shorter than its diff:
```python
import functools

import jax
import jax.numpy as jnp
from jax import lax
from jax.experimental import pallas as pl
from jax.experimental.pallas import tpu as pltpu
from jax.sharding import PartitionSpec as P

EPSILON = 1e-06
CORES = 2
ROW_TILE = 16
VMEM_LIMIT = 24 * 1024 * 1024
BF16, F32 = jnp.bfloat16, jnp.float32


def nn(a, b):
    return lax.dot_general(a, b, (((1,), (0,)), ((), ())), preferred_element_type=F32)


def nt(a, b):
    return lax.dot_general(a, b, (((1,), (1,)), ((), ())), preferred_element_type=F32)


def tn(a, b):
    return lax.dot_general(a, b, (((0,), (0,)), ((), ())), preferred_element_type=F32)


def silu_parts(hidden):
    sigmoid_value = jax.nn.sigmoid(hidden)
    silu_value = hidden * sigmoid_value
    silu_slope = sigmoid_value * (1.0 + hidden * (1.0 - sigmoid_value))
    curvature = sigmoid_value * (1.0 - sigmoid_value) * (2.0 + hidden * (1.0 - 2.0 * sigmoid_value))
    return silu_value, silu_slope, curvature


def partner(index, step, count):
    return index ^ step if count & (count - 1) == 0 else (index + step) % count


def source(index, step, count):
    return index ^ step if count & (count - 1) == 0 else (index + count - step) % count


def chip_perm(count, step):
    chips = count // CORES
    return [(t, partner(t // CORES, step, chips) * CORES + t % CORES) for t in range(count)]


def core_perm(count):
    return [(t, t ^ 1) for t in range(count)]


def pack(gate, up, down):
    folds = gate.shape[1] // down.shape[1]
    rows = down.shape[0] // folds
    down = jnp.concatenate([down[i * rows : (i + 1) * rows] for i in range(folds)], axis=1)
    return jnp.concatenate([gate, up, down], axis=0)


def unpack(packed, fh):
    g = packed.shape[0] // 3
    folds = packed.shape[1] // fh
    down = packed[2 * g :]
    down = jnp.concatenate([down[:, i * fh : (i + 1) * fh] for i in range(folds)], axis=0)
    return packed[:g], packed[g : 2 * g], down


def update_forward(w1t, w3t, w2, keys, push):
    gate_pre, up_pre = nt(w1t, keys), nt(w3t, keys)
    silu, slope, curvature = silu_parts(gate_pre)
    mixed = (silu * up_pre).astype(BF16)
    down_back = nn(w2, push)
    back_slope = down_back * slope
    gate_back = (down_back * up_pre * slope).astype(BF16)
    up_back = (down_back * silu).astype(BF16)
    return up_pre, silu, slope, curvature, mixed, down_back, back_slope, gate_back, up_back


def apply_forward(f1t, f3t, f2t, queries, weighted):
    q_gate, q_up = nt(f1t, queries), nt(f3t, queries)
    silu, slope, _ = silu_parts(q_gate)
    mixed = (silu * q_up).astype(BF16)
    output = nn(f2t, mixed)
    square = jnp.sum(output * output, axis=0, keepdims=True)
    dot = jnp.sum(weighted * output, axis=0, keepdims=True)
    return output, mixed, q_up * slope, silu, jnp.concatenate([square, dot], axis=0)


def apply_backward(f2t, sums, full_width, output, weighted, mixed, up_slope, silu, queries):
    inverse = lax.rsqrt(sums[0:1] / full_width + EPSILON)
    scale = inverse * inverse * inverse * sums[1:2] / full_width
    out_back = (inverse * weighted - output * scale).astype(BF16)
    q_back = tn(f2t, out_back)
    gate_back = (q_back * up_slope).astype(BF16)
    up_back = (q_back * silu).astype(BF16)
    return gate_back, up_back, nn(gate_back, queries), nn(up_back, queries), nt(out_back, mixed)


def second_adjoint(c1t, c3t, c2t, keys, push, up_slope, silu, back_slope, back_curve):
    gate_bar, up_bar, mixed_bar = nt(c1t, keys), nt(c3t, keys), tn(c2t, push)
    down_back_bar = (gate_bar * up_slope + up_bar * silu).astype(BF16)
    up_pre_bar = (gate_bar * back_slope + mixed_bar * silu).astype(BF16)
    gate_pre_bar = (up_bar * back_slope + mixed_bar * up_slope + gate_bar * back_curve).astype(BF16)
    return (
        down_back_bar,
        up_pre_bar,
        gate_pre_bar,
        nn(gate_pre_bar, keys),
        nn(up_pre_bar, keys),
        nt(push, down_back_bar),
    )


def folds_of(rows, folds):
    width = rows.shape[1] // folds
    return [rows[:, i * width : (i + 1) * width] for i in range(folds)]


def norm_of(rows):
    return jnp.sqrt(jnp.sum(rows * rows, axis=1, keepdims=True) + EPSILON)


def owner_forward(prior, update, folds):
    moved = prior - update
    fast = [
        m * (norm_of(p) / norm_of(m)) for p, m in zip(folds_of(prior, folds), folds_of(moved, folds))
    ]
    return jnp.concatenate(fast, axis=1).astype(BF16), moved


def owner_backward(prior, moved, fast_grad, folds):
    cotangent, owned = [], []
    for p, m, fg in zip(*(folds_of(x, folds) for x in (prior, moved, fast_grad))):
        prior_norm, moved_norm = norm_of(p), norm_of(m)
        column_dot = jnp.sum(fg * m, axis=1, keepdims=True)
        moved_grad = (prior_norm / moved_norm) * (fg - m * (column_dot / (moved_norm * moved_norm)))
        cotangent.append(moved_grad)
        owned.append(moved_grad + p * (column_dot / (moved_norm * prior_norm)))
    return jnp.concatenate(cotangent, axis=1).astype(BF16), jnp.concatenate(owned, axis=1)


def push_of(rates, values):
    return (-rates * values.T.astype(F32)).astype(BF16)


def both(own_ref, other_ref, axis=0):
    return jnp.concatenate([own_ref[...], other_ref[...]], axis=axis)


def cut_share(out, ref, chips, folds):
    core = lax.axis_index("tok") % CORES
    rows, width = ref.shape[0] // (chips * CORES), ref.shape[1]
    height = rows // folds
    for chip in range(chips):
        for i in range(folds):
            at = pl.multiple_of((chip * CORES + core) * rows + i * height, height)
            out[chip * height : (chip + 1) * height, i * width : (i + 1) * width] = ref[
                pl.ds(at, height), :
            ].astype(out.dtype)


def place_shares(ref, mine, other, chips, folds):
    core = lax.axis_index("tok") % CORES
    rows, width = ref.shape[0] // (chips * CORES), ref.shape[1]
    height = rows // folds
    for share, c in ((mine, core), (other, 1 - core)):
        for chip in range(chips):
            for i in range(folds):
                at = pl.multiple_of((chip * CORES + c) * rows + i * height, height)
                ref[pl.ds(at, height), :] = share[
                    chip * height : (chip + 1) * height, i * width : (i + 1) * width
                ]


def send_pieces(chips, folds, owned, gate_ref, up_ref, down_ref, outs):
    tok = lax.axis_index("tok")
    chip, core = tok // CORES, tok % CORES
    half = chips // 2
    g, width = gate_ref.shape[0] // (chips * CORES), down_ref.shape[1]
    for step, out in enumerate(outs):
        to = partner(chip, step, chips)
        holds = ((chip == half - 1) & (to < half)) | ((chip == half) & (to >= half))
        first = (to * CORES + core) * g
        for k, ref in enumerate((gate_ref, up_ref, down_ref)):
            if k < 2:
                rows = ref[pl.ds(pl.multiple_of(first, g), g), :]
            else:
                parts = [
                    ref[pl.ds(pl.multiple_of(first * folds + i * g, g), g), :] for i in range(folds)
                ]
                rows = jnp.concatenate(parts, axis=1)
            rest = owned[k][pl.ds(pl.multiple_of(to * g, g), g), :]
            out[k * g : (k + 1) * g] = jnp.where(holds, rest - rows, -rows).astype(out.dtype)


def cut_matrices(chips, folds, gate_ref, up_ref, down_ref, outs):
    for k, ref in enumerate((gate_ref, up_ref, down_ref)):
        folded = folds if k == 2 else 1
        cut_share(outs[k], ref, chips, folded)
        outs[3 + k][...] = outs[k][...].astype(BF16)


def update_kernel(chips, folds, ko, kx, vo, vx, ro, rx, w1t, w3t, w2, *rest):
    outs, (gate, up, down) = rest[:6], rest[6:]
    keys = both(ko, kx)
    push = push_of(both(ro, rx, 1), both(vo, vx))
    *_, mixed, _, _, gate_back, up_back = update_forward(w1t[...], w3t[...], w2[...], keys, push)
    down[...] = nt(push, mixed)
    gate[...] = nn(gate_back, keys)
    up[...] = nn(up_back, keys)
    cut_matrices(chips, folds, gate, up, down, outs)


def saved_kernel(
    chips, folds, ko, kx, vo, vx, ro, rx, w1t, w3t, w2, go, gx, gain,
    push_ref, up_slope_ref, silu_ref, back_slope_ref, back_curve_ref,
    mixed_ref, gate_back_ref, up_back_ref, weighted_ref, p1_ref, p3_ref, p2_ref,
    gate_ref, up_ref, down_ref,
):
    push = push_of(both(ro, rx, 1), both(vo, vx))
    push_ref[...] = push
    up_pre, silu, slope, curvature, mixed, down_back, back_slope, gate_back, up_back = (
        update_forward(w1t[...], w3t[...], w2[...], both(ko, kx), push)
    )
    up_slope_ref[...] = up_pre * slope
    silu_ref[...] = silu
    back_slope_ref[...] = back_slope
    back_curve_ref[...] = down_back * up_pre * curvature
    own = mixed_ref.shape[1]
    mixed_ref[...] = mixed[:, :own]
    gate_back_ref[...] = gate_back[:, :own]
    up_back_ref[...] = up_back[:, :own]
    weighted_ref[...] = (both(go, gx).astype(F32) * gain[...]).T
    gate_ref[...] = w1t[...].astype(F32)
    up_ref[...] = w3t[...].astype(F32)
    down_ref[...] = w2[...].astype(F32).T
    cut_share(p1_ref, gate_ref, chips, 1)
    cut_share(p3_ref, up_ref, chips, 1)
    cut_share(p2_ref, down_ref, chips, folds)


def carry_kernel(own, got, out):
    out[...] = (own[...] + got[...].astype(F32)).astype(BF16)


def owner_forward_kernel(folds, prior, mine, other, fast, moved):
    total = mine[...].astype(F32) + other[...].astype(F32)
    fast[...], moved[...] = owner_forward(prior[...], total, folds)


def owner_backward_kernel(folds, prior, moved, mine, other, cotangent, owned):
    total = mine[...].astype(F32) + other[...].astype(F32)
    cotangent[...], owned[...] = owner_backward(prior[...], moved[...], total, folds)


def owner_result_kernel(folds, own, *refs):
    gate, up, down = refs[-3:]
    total = own[...]
    for piece in refs[:-3]:
        total = total + piece[...].astype(F32)
    g = gate.shape[0]
    gate[...], up[...] = total[:g], total[g : 2 * g]
    for i, rows in enumerate(folds_of(total[2 * g :], folds)):
        down[i * g : (i + 1) * g] = rows


def apply_kernel(chips, folds, *refs):
    pieces, refs = refs[:6], refs[6:]
    qo, qx, weighted, f1t, f3t, f2t, output, mixed, up_slope, silu, sums = refs
    for k, ref in enumerate((f1t, f3t, f2t)):
        place_shares(ref, pieces[k], pieces[3 + k], chips, folds if k == 2 else 1)
    output[...], mixed[...], up_slope[...], silu[...], sums[...] = apply_forward(
        f1t[...], f3t[...], f2t[...], both(qo, qx), weighted[...]
    )


def back_kernel(chips, folds, heads, *refs):
    parts, refs = refs[:heads], refs[heads:]
    sums = parts[0][...]
    for part in parts[1:]:
        sums = sums + part[...]
    f2t, output, weighted, mixed, up_slope, silu, qo, qx, gate_back, up_back = refs[:10]
    outs, (gate, up, down) = refs[10:16], refs[16:]
    width = heads * output.shape[0]
    gb, ub, gate[...], up[...], down[...] = apply_backward(
        f2t[...], sums, width, output[...], weighted[...], mixed[...], up_slope[...], silu[...],
        both(qo, qx),
    )
    cut_matrices(chips, folds, gate, up, down, outs)
    own = gate_back.shape[1]
    gate_back[...], up_back[...] = gb[:, :own], ub[:, :own]


def query_kernel(gate_back, up_back, f1t, f3t, out):
    out[...] = (tn(gate_back[...], f1t[...]) + tn(up_back[...], f3t[...])).astype(BF16)


def second_kernel(chips, folds, *refs):
    pieces, owned, refs = refs[:6], refs[6:9], refs[9:]
    ko, kx, push, up_slope, silu, back_slope, back_curve = refs[:7]
    c1t, c3t, c2t, dbb_ref, upb_ref, gpb_ref = refs[7:13]
    outs, (gate, up, down) = refs[13 : 13 + chips], refs[13 + chips :]
    for k, ref in enumerate((c1t, c3t, c2t)):
        place_shares(ref, pieces[k], pieces[3 + k], chips, folds if k == 2 else 1)
    dbb, upb, gpb, gate[...], up[...], down[...] = second_adjoint(
        c1t[...], c3t[...], c2t[...], both(ko, kx), push[...],
        up_slope[...], silu[...], back_slope[...], back_curve[...],
    )
    send_pieces(chips, folds, owned, gate, up, down, outs)
    own = dbb_ref.shape[1]
    dbb_ref[...], upb_ref[...], gpb_ref[...] = dbb[:, :own], upb[:, :own], gpb[:, :own]


def token_grads(rates, mixed, dbb, upb, gpb, gate_back, up_back, c1t, c3t, c2t, w1t, w3t, w2):
    value_grad = (rates * (nn(c2t, mixed) + tn(w2, dbb))).T.astype(BF16)
    key_total = tn(gate_back, c1t) + tn(up_back, c3t) + tn(gpb, w1t) + tn(upb, w3t)
    return value_grad, (-key_total).astype(BF16)


def token_kernel(*refs):
    value_grad, key_grad = refs[-2:]
    value_grad[...], key_grad[...] = token_grads(*(r[...] for r in refs[:-2]))


def call(kernel, outs, args, scratch=(), name=None, flops=0):
    vmem = pl.BlockSpec(memory_space=pltpu.VMEM)
    return pl.pallas_call(
        kernel,
        out_shape=[jax.ShapeDtypeStruct(s, t) for s, t in outs],
        in_specs=[vmem] * len(args),
        out_specs=[vmem] * len(outs),
        scratch_shapes=[pltpu.VMEM(s, t) for s, t in scratch],
        compiler_params=pltpu.CompilerParams(vmem_limit_bytes=VMEM_LIMIT),
        cost_estimate=pl.CostEstimate(
            flops=flops,
            bytes_accessed=sum(a.size * a.dtype.itemsize for a in args),
            transcendentals=0,
        ),
        name=name,
    )(*args)


def exchange(pieces, chips):
    count = chips * CORES
    got = [lax.ppermute(pieces[s], "tok", chip_perm(count, s)) for s in reversed(range(1, chips))]
    return [pieces[0], *got]


def between_chips(x, pairs):
    perm = [(a * CORES + c, b * CORES + c) for a, b in pairs for c in range(CORES)]
    return lax.ppermute(x, "tok", perm)


def outer_pairs(chips, hop):
    return [(hop, hop + 1), (chips - 1 - hop, chips - 2 - hop)]


def half_sums(own, own_rounded, chips):
    carried, shape = own_rounded, [(own.shape, BF16)]
    for hop in range(chips // 2 - 1):
        got = between_chips(carried, outer_pairs(chips, hop))
        (carried,) = call(carry_kernel, shape, (own, got), name="carry")
    half = chips // 2
    return carried, between_chips(carried, [(half - 1, half), (half, half - 1)])


def from_inner(x, chip, chips):
    for hop in reversed(range(chips // 2 - 1)):
        pairs = outer_pairs(chips, hop)
        got = between_chips(x, [(b, a) for a, b in pairs])
        x = jnp.where((chip == pairs[0][0]) | (chip == pairs[1][0]), got, x)
    return x, lax.ppermute(x, "tok", core_perm(chips * CORES))


def head_parts(part, heads):
    got = [
        lax.ppermute(part, "head", [(h, partner(h, step, heads)) for h in range(heads)])
        for step in range(1, heads)
    ]
    return [part, *got]


def over_chips(blocks, count):
    groups = [list(range(core, count, CORES)) for core in range(CORES)]
    return lax.all_to_all(blocks, "tok", 0, 0, axis_index_groups=groups, tiled=True)


def gather_blocks(copies, count):
    mine = over_chips(copies, count)
    return mine, lax.ppermute(mine, "tok", core_perm(count))


def sliced_pieces(gate, up, down, tok, count):
    g, d = gate.shape[0] // count, down.shape[0] // count
    rows = lambda x, size, t: lax.dynamic_slice_in_dim(x, t * size, size, 0)
    piece = lambda t: pack(rows(gate, g, t), rows(up, g, t), rows(down, d, t))
    sent = [piece(t + tok % CORES) for t in range(0, count, CORES)]
    return piece(tok), jnp.concatenate(sent, axis=0).astype(BF16)


def total_of(own, got, tok):
    blocks = got.reshape((-1,) + own.shape)
    chip = lax.broadcasted_iota(jnp.int32, (blocks.shape[0], 1, 1), 0)
    others = jnp.where(chip == tok // CORES, 0.0, blocks.astype(F32))
    return own + jnp.sum(others, axis=0)


def whole_matrices(mine, other, tok, count, fh):
    shape = (count // CORES, -1, mine.shape[1])
    pair = jnp.stack([mine.reshape(shape), other.reshape(shape)], axis=1)
    pair = jnp.where(tok % CORES == 0, pair, pair[:, ::-1])
    held = pair.reshape((count, -1, mine.shape[1]))
    parts = jax.vmap(lambda x: unpack(x, fh))(held)
    return tuple(x.reshape((-1, x.shape[-1])) for x in parts)


def packed_owner_forward(prior, update, fh):
    fast, moved = zip(*(owner_forward(p, u, 1) for p, u in zip(unpack(prior, fh), unpack(update, fh))))
    return pack(*fast), pack(*moved)


def packed_owner_backward(prior, moved, fast_grad, fh):
    parts = (unpack(x, fh) for x in (prior, moved, fast_grad))
    cotangent, owned = zip(*(owner_backward(p, m, f, 1) for p, m, f in zip(*parts)))
    return pack(*cotangent), pack(*owned)


def per_device(
    query_input,
    key_input,
    value_input,
    out_grad,
    token_rates,
    out_gain,
    gate_prior,
    up_prior,
    down_prior,
):
    count, heads = lax.axis_size("tok"), lax.axis_size("head")
    tok = lax.axis_index("tok")
    chips, chip = count // CORES, tok // CORES
    own, dh = key_input.shape
    n = own * CORES
    w1, w3, w2 = gate_prior[0], up_prior[0], down_prior[0]
    fh = w2.shape[0]
    g, d = fh // count, dh // count
    rates = token_rates.T
    gain = out_gain[None, :]
    inputs = query_input, key_input, value_input, out_grad, rates, gain, w1, w3, w2

    if g % ROW_TILE or d % g or dh * g != fh * d or chips % 2:
        query_grad, key_grad, value_grad, *results = by_blocks(inputs, tok, count, heads)
    else:
        query_grad, key_grad, value_grad, *results = by_line(inputs, chip, chips, heads)
    return (query_grad, key_grad, value_grad, *(r.T[None] for r in results))


def by_line(inputs, chip, chips, heads):
    query_input, key_input, value_input, out_grad, rates, gain, w1, w3, w2 = inputs
    count = chips * CORES
    own, dh = key_input.shape
    n, fh = own * CORES, w2.shape[0]
    g, d, folds = fh // count, dh // count, dh // fh
    w1t, w3t = w1.T, w3.T
    product = 2 * n * dh * fh

    share = (g * chips, dh)
    share_sums = [(share, F32)] * 3 + [(share, BF16)] * 3
    matrices = [((fh, dh), BF16), ((fh, dh), BF16), ((dh, fh), BF16)]
    sums_scratch = [((fh, dh), F32), ((fh, dh), F32), ((dh, fh), F32)]
    hidden = ((fh, n), F32)
    own_hidden = ((fh, own), BF16)
    folds_by_matrix = (1, 1, folds)

    pair = lambda x: lax.ppermute(x, "tok", core_perm(count))
    key_other, value_other, rate_other = pair(key_input), pair(value_input), pair(rates)
    keys_values = (
        key_input, key_other, value_input, value_other, rates, rate_other, w1t, w3t, w2,
    )
    sums = call(
        functools.partial(update_kernel, chips, folds),
        share_sums,
        keys_values,
        sums_scratch,
        "update",
        6 * product,
    )
    query_later, grad_later, *sums = lax.optimization_barrier((query_input, out_grad, *sums))
    query_other, grad_other = pair(query_later), pair(grad_later)
    *saved, weighted, p1, p3, p2 = call(
        functools.partial(saved_kernel, chips, folds),
        [((dh, n), BF16)] + [hidden] * 4 + [own_hidden] * 3 + [((dh, n), F32)] + [(share, F32)] * 3,
        (*keys_values, out_grad, grad_other, gain),
        sums_scratch,
        "saved",
        3 * product,
    )
    push, up_slope, silu, back_slope, back_curve, mixed, gate_back, up_back = saved
    priors = p1, p3, p2

    fast, moved = [], []
    for k in range(3):
        mine, other = half_sums(sums[k], sums[3 + k], chips)
        rows, rows_moved = call(
            functools.partial(owner_forward_kernel, folds_by_matrix[k]),
            [(share, BF16), (share, F32)],
            (priors[k], mine, other),
            name="owner_forward",
        )
        moved.append(rows_moved)
        fast.append(from_inner(rows, chip, chips))
    f1t, f3t, f2t, output, q_mixed, q_slope, q_silu, part = call(
        functools.partial(apply_kernel, chips, folds),
        matrices + [((dh, n), F32), ((fh, n), BF16), hidden, hidden, ((2, n), F32)],
        (*(f[0] for f in fast), *(f[1] for f in fast), query_input, query_other, weighted),
        name="apply",
        flops=3 * product,
    )
    q_gate_back, q_up_back, *sums = call(
        functools.partial(back_kernel, chips, folds, heads),
        [own_hidden] * 2 + share_sums,
        (
            *head_parts(part, heads),
            f2t, output, weighted, q_mixed, q_slope, q_silu, query_input, query_other,
        ),
        sums_scratch,
        "apply_back",
        4 * product,
    )
    (query_grad,) = call(
        query_kernel,
        [((own, dh), BF16)],
        (q_gate_back, q_up_back, f1t, f3t),
        name="query_grad",
        flops=product,
    )

    cotangent, owned = [], []
    for k in range(3):
        mine, other = half_sums(sums[k], sums[3 + k], chips)
        rows, rows_owned = call(
            functools.partial(owner_backward_kernel, folds_by_matrix[k]),
            [(share, BF16), (share, F32)],
            (priors[k], moved[k], mine, other),
            name="owner_backward",
        )
        owned.append(rows_owned)
        cotangent.append(from_inner(rows, chip, chips))
    c1t, c3t, c2t, dbb, upb, gpb, *pieces = call(
        functools.partial(second_kernel, chips, folds),
        matrices + [own_hidden] * 3 + [((3 * g, dh), F32)] + [((3 * g, dh), BF16)] * (chips - 1),
        (
            *(c[0] for c in cotangent), *(c[1] for c in cotangent), *owned,
            key_input, key_other, push, up_slope, silu, back_slope, back_curve,
        ),
        sums_scratch,
        "second_adjoint",
        6 * product,
    )
    value_grad, key_grad = call(
        token_kernel,
        [((own, dh), BF16)] * 2,
        (rates, mixed, dbb, upb, gpb, gate_back, up_back, c1t, c3t, c2t, w1t, w3t, w2),
        name="token_grads",
        flops=3 * product,
    )
    results = call(
        functools.partial(owner_result_kernel, folds),
        [((g, dh), F32)] * 2 + [((d, fh), F32)],
        exchange(pieces, chips),
        name="owner_result",
    )
    return query_grad, key_grad, value_grad, *results


def by_blocks(inputs, tok, count, heads):
    query_input, key_input, value_input, out_grad, rates, gain, w1, w3, w2 = inputs
    own, dh = key_input.shape
    fh, chips = w2.shape[0], count // CORES
    g, d = fh // count, dh // count
    w1t, w3t = w1.T, w3.T
    pair = lambda x, axis=0: jnp.concatenate(
        [x, lax.ppermute(x, "tok", core_perm(count))], axis=axis
    )
    keys, values, queries, rate = pair(key_input), pair(value_input), pair(query_input), pair(rates, 1)
    weighted = (pair(out_grad).astype(F32) * gain).T
    push = push_of(rate, values)
    up_pre, silu, slope, curvature, mixed, down_back, back_slope, gate_back, up_back = (
        update_forward(w1t, w3t, w2, keys, push)
    )
    up_slope, back_curve = up_pre * slope, down_back * up_pre * curvature
    piece, sent = sliced_pieces(
        nn(gate_back, keys), nn(up_back, keys), nt(push, mixed), tok, count
    )
    prior = pack(
        *(
            lax.dynamic_slice_in_dim(x, tok * rows, rows, 0).astype(F32)
            for x, rows in ((w1t, g), (w3t, g), (w2.T, d))
        )
    )
    update = total_of(piece, over_chips(sent, count), tok)
    fast, moved = packed_owner_forward(prior, update, fh)
    blocks = gather_blocks(jnp.tile(fast, (chips, 1)), count)
    f1t, f3t, f2t = whole_matrices(*blocks, tok, count, fh)
    output, q_mixed, q_slope, q_silu, part = apply_forward(f1t, f3t, f2t, queries, weighted)
    sums = lax.psum(part, "head")
    q_gate_back, q_up_back, *grads = apply_backward(
        f2t, sums, heads * dh, output, weighted, q_mixed, q_slope, q_silu, queries
    )
    piece, sent = sliced_pieces(*grads, tok, count)
    query_grad = (tn(q_gate_back[:, :own], f1t) + tn(q_up_back[:, :own], f3t)).astype(BF16)
    fast_grad = total_of(piece, over_chips(sent, count), tok)
    cotangent, owned = packed_owner_backward(prior, moved, fast_grad, fh)
    blocks = gather_blocks(jnp.tile(cotangent, (chips, 1)), count)
    c1t, c3t, c2t = whole_matrices(*blocks, tok, count, fh)
    dbb, upb, gpb, *bars = second_adjoint(
        c1t, c3t, c2t, keys, push, up_slope, silu, back_slope, back_curve
    )
    piece, sent = sliced_pieces(*bars, tok, count)
    value_grad, key_grad = token_grads(
        rates, mixed[:, :own], dbb[:, :own], upb[:, :own], gpb[:, :own],
        gate_back[:, :own], up_back[:, :own], c1t, c3t, c2t, w1t, w3t, w2,
    )
    results = unpack(owned - total_of(piece, over_chips(sent, count), tok), fh)
    return query_grad, key_grad, value_grad, *results


def solution(mesh):
    tokens = P("tok", "head")
    in_specs = (tokens,) * 5 + (P("head"),) + (P("head", None, None),) * 3
    out_specs = (tokens,) * 3 + (P("head", None, "tok"),) * 3
    return jax.shard_map(
        per_device, mesh=mesh, in_specs=in_specs, out_specs=out_specs, check_vma=False
    )
```

time: 82.7 us -> 95.3 us (1.15)
  starting transfers between devices: 29.2 us -> 34.7 us
  waiting for transfers between devices: 33.1 us -> 37.6 us
  Pallas kernels: 8.71 us -> 13.1 us
  other arithmetic: 2.56 us -> 1 us
    ppermute x31 -> x35, starting transfers between devices: 29.2 us -> 34.7 us  [the longest x18 25 us: between_chips(): return lax.ppermute(x, 'tok', perm)]
    ppermute x31 -> x35, waiting for transfers between devices: 33.1 us -> 37.6 us  [the longest x18 27.9 us: between_chips(): return lax.ppermute(x, 'tok', perm)]
    pallas_call x7 -> x20, Pallas kernels: 8.71 us -> 13.1 us  [call(): pl.pallas_call(kernel, out_shape=[jax.ShapeDtypeStruct(s, t) for s, t in...]
    broadcast_in_dim x2 -> x0, other arithmetic: 1.49 us -> none  [per_device(): results = [(o - b).T[None] for o, b in zip(owned, bars)]]
    select_n x0 -> x6, other arithmetic: none -> 1 us  [from_inner(): x = jnp.where((chip == pairs[0][0]) | (chip == pairs[1][0]), got, x)]
    unnamed x61 -> x58, local copies, waits for them, and re-layouts: 6.56 us -> 6.96 us
  transfers between devices with their start and end apart: 31 -> 35, of which waited for: 15 -> 19; matrix products, arithmetic and copies ran while one was open for 3% -> 2% of each run, Pallas kernels for 6% -> 9%
where the time goes in v6:
time: 95.3 us; the launch traced here: 94.7 us
  waiting for transfers between devices  37.6 us (39%)
  starting transfers between devices  34.7 us (36%)
  Pallas kernels  13.1 us (14%)
  local copies, waits for them, and re-layouts  6.96 us (7%)
  between operations  1.26 us (1%)
  other arithmetic  1 us (1%)
    ppermute x18, waiting for transfers between devices, between_chips(): return lax.ppermute(x, 'tok', perm)  27.9 us
    ppermute x18, starting transfers between devices, between_chips(): return lax.ppermute(x, 'tok', perm)  25 us
    pallas_call x20, Pallas kernels, call(): pl.pallas_call(kernel, out_shape=[jax.ShapeDtypeStruct(s, t) for s, t in...  13.1 us
    unnamed x58, local copies, waits for them, and re-layouts  6.96 us
    ppermute x3, starting transfers between devices, exchange(): lax.ppermute(pieces[s], 'tok', chip_perm(count, s))  4.45 us
    ppermute x3, waiting for transfers between devices, exchange(): lax.ppermute(pieces[s], 'tok', chip_perm(count, s))  4.07 us
    ppermute x3, starting transfers between devices, head_parts(): lax.ppermute(part, 'head', [(h, partner(h, step, heads)) for h in range(h...  3.55 us
    ppermute x3, waiting for transfers between devices, head_parts(): lax.ppermute(part, 'head', [(h, partner(h, step, heads)) for h in range(h...  3.07 us
  transfers between devices with their start and end apart: 35, of which 19 were waited for; matrix products, arithmetic and copies ran while one was open for 2% of the time, Pallas kernels for 9%

profile of v6, /device:TPU:0, one launch (start us, length us, event | category | flops | bytes accessed | tf_op | source)
XLA Modules:
  0.0 94.7 jit_solution(7692127288935198953)
XLA Ops:
  1.8 1.1 %copy.15 = bf16[1,512,256]{1,2,0:T(8,128)(2,1)S(1)} copy(bf16[1,512,256]{2,1,0:T(8,128)(2,1)} %param.15) | data formatting | bytes 524288 | tf_op args[6]
  4.0 1.2 %update.1 = (f32[128,512]{1,0:T(8,128)S(1)}, f32[128,512]{1,0:T(8,128)S(1)}, f32[128,512]{1,0:T(8,128)S(1)}, bf16[128,512]{1,0:T(8,128)(2,1)S(1)}, bf16[128,512]...) custom-call(bf16[256,512]{1,0:T(8,128)(2,1)S(1)} %copy-done.1, bf16[256,512]{1,0:T(8,128)(2,1)S(1)} %collective-permute-done.kx.refs_10_, ...), custom_call_target="tpu_custom_call" | custom-call | flops 805306368 | bytes 1837056 | tf_op jit(solution)/shard_map/update/pallas_call | solution.py:328
  5.4 4.9 %collective-permute-start.10 = (bf16[128,512]{1,0:T(8,128)(2,1)S(1)}, bf16[128,512]{1,0:T(8,128)(2,1)S(1)}, u32[]{:S(2)}, u32[]{:S(2)}) collective-permute-start(bf16[128,512]{1,0:T(8,128)(2,1)S(1)} %get-tuple-element.92), channel_id=1, source_target_pairs={{0,2},{1,3},{6,4},{7,5},{8,10},{9,11},{14,12},{15,13},{16,18},{17,... | collective-permute-start | bytes 393224 | tf_op jit(solution)/shard_map/ppermute | solution.py:352
  10.3 1.3 %collective-permute-start.4 = (bf16[128,512]{1,0:T(8,128)(2,1)S(1)}, bf16[128,512]{1,0:T(8,128)(2,1)S(1)}, u32[]{:S(2)}, u32[]{:S(2)}) collective-permute-start(bf16[128,512]{1,0:T(8,128)(2,1)S(1)} %get-tuple-element.84), channel_id=1, source_target_pairs={{0,2},{1,3},{6,4},{7,5},{8,10},{9,11},{14,12},{15,13},{16,18},{17,... | collective-permute-start | bytes 393224 | tf_op jit(solution)/shard_map/ppermute | solution.py:352
  11.6 1.3 %collective-permute-start.7 = (bf16[128,512]{1,0:T(8,128)(2,1)S(1)}, bf16[128,512]{1,0:T(8,128)(2,1)S(1)}, u32[]{:S(2)}, u32[]{:S(2)}) collective-permute-start(bf16[128,512]{1,0:T(8,128)(2,1)S(1)} %get-tuple-element.88), channel_id=1, source_target_pairs={{0,2},{1,3},{6,4},{7,5},{8,10},{9,11},{14,12},{15,13},{16,18},{17,... | collective-permute-start | bytes 393224 | tf_op jit(solution)/shard_map/ppermute | solution.py:352
  12.9 1.2 %collective-permute-done.10.got = bf16[128,512]{1,0:T(8,128)(2,1)S(1)} collective-permute-done((bf16[128,512]{1,0:T(8,128)(2,1)S(1)}, bf16[128,512]{1,0:T(8,128)(2,1)S(1)}, u32[]{:S(2)}, u32[]{:S(2)}) %collective-permute-start.10) | collective-permute-done | bytes 131104 | tf_op jit(solution)/shard_map/ppermute | solution.py:352
  14.9 2.1 %collective-permute-done.4.got = bf16[128,512]{1,0:T(8,128)(2,1)S(1)} collective-permute-done((bf16[128,512]{1,0:T(8,128)(2,1)S(1)}, bf16[128,512]{1,0:T(8,128)(2,1)S(1)}, u32[]{:S(2)}, u32[]{:S(2)}) %collective-permute-start.4) | collective-permute-done | bytes 131104 | tf_op jit(solution)/shard_map/ppermute | solution.py:352
  17.0 1.5 %collective-permute-start.5 = (bf16[128,512]{1,0:T(8,128)(2,1)S(1)}, bf16[128,512]{1,0:T(8,128)(2,1)}, u32[]{:S(2)}, u32[]{:S(2)}) collective-permute-start(bf16[128,512]{1,0:T(8,128)(2,1)S(1)} %carry.6.mine), channel_id=1, source_target_pairs={{2,4},{3,5},{4,2},{5,3},{10,12},{11,13},{12,10},{13,11},{18,20},{1... | collective-permute-start | bytes 393224 | tf_op jit(solution)/shard_map/ppermute | solution.py:352
  19.5 1.3 %collective-permute-start.8 = (bf16[128,512]{1,0:T(8,128)(2,1)}, bf16[128,512]{1,0:T(8,128)(2,1)}, u32[]{:S(2)}, u32[]{:S(2)}) collective-permute-start(bf16[128,512]{1,0:T(8,128)(2,1)} %carry.7.mine), channel_id=1, source_target_pairs={{2,4},{3,5},{4,2},{5,3},{10,12},{11,13},{12,10},{13,11},{18,20},{1... | collective-permute-start | bytes 393224 | tf_op jit(solution)/shard_map/ppermute | solution.py:352
  20.8 1.1 %saved.1 = (bf16[512,512]{1,0:T(8,128)(2,1)S(1)}, f32[256,512]{1,0:T(8,128)S(1)}, f32[256,512]{1,0:T(8,128)S(1)}, f32[256,512]{1,0:T(8,128)S(1)}, f32[256,512]{1...) custom-call(bf16[256,512]{1,0:T(8,128)(2,1)S(1)} %copy-done.1, ...), custom_call_target="tpu_custom_call" | custom-call | flops 402653184 | bytes 2363392 | tf_op jit(solution)/shard_map/saved/pallas_call | solution.py:328
  22.0 0.8 copy-done.3
  22.8 0.8 copy-done.5
  23.6 0.8 copy-done.7
  24.4 0.8 copy-done.9
  25.2 0.8 copy-done.11
  26.0 0.9 owner_forward.5
  27.6 1.3 %collective-permute-start.12 = (bf16[128,512]{1,0:T(8,128)(2,1)}, bf16[128,512]{1,0:T(8,128)(2,1)}, u32[]{:S(2)}, u32[]{:S(2)}) collective-permute-start(bf16[128,512]{1,0:T(8,128)(2,1)} %get-tuple-element.93), channel_id=1, source_target_pairs={{2,0},{3,1},{4,6},{5,7},{10,8},{11,9},{12,14},{13,15},{18,16},{19,... | collective-permute-start | bytes 393224 | tf_op jit(solution)/shard_map/ppermute | solution.py:352
  29.0 1.1 %owner_forward.4 = (bf16[128,512]{1,0:T(8,128)(2,1)S(1)}, f32[128,512]{1,0:T(8,128)S(1)}) custom-call(f32[128,512]{1,0:T(8,128)S(1)} %get-tuple-element.86.prior, bf16[128,512]{1,0:T(8,128)(2,1)} %carry.7.mine, bf16[128,512]{1,0:T(8,128)(2,1)} %collective-permute-done.8.other), custom_call_target="tpu_custom_call" | custom-call | bytes 524288 | tf_op jit(solution)/shard_map/owner_forward/pallas_call | solution.py:328
  30.1 1.3 %collective-permute-start.9 = (bf16[128,512]{1,0:T(8,128)(2,1)S(1)}, bf16[128,512]{1,0:T(8,128)(2,1)S(1)}, u32[]{:S(2)}, u32[]{:S(2)}) collective-permute-start(bf16[128,512]{1,0:T(8,128)(2,1)S(1)} %get-tuple-element.89), channel_id=1, source_target_pairs={{2,0},{3,1},{4,6},{5,7},{10,8},{11,9},{12,14},{13,15},{18,16},{19,... | collective-permute-start | bytes 393224 | tf_op jit(solution)/shard_map/ppermute | solution.py:352
  31.4 1.1 %owner_forward.3 = (bf16[128,512]{1,0:T(8,128)(2,1)S(1)}, f32[128,512]{1,0:T(8,128)S(1)}) custom-call(f32[128,512]{1,0:T(8,128)S(1)} %get-tuple-element.82.prior, bf16[128,512]{1,0:T(8,128)(2,1)S(1)} %carry.6.mine, bf16[128,512]{1,0:T(8,128)(2,1)} %collective-permute-done.5.other), custom_call_target="tpu_custom_call" | custom-call | bytes 524288 | tf_op jit(solution)/shard_map/owner_forward/pallas_call | solution.py:328
  32.5 1.3 %collective-permute-start.6 = (bf16[128,512]{1,0:T(8,128)(2,1)S(1)}, bf16[128,512]{1,0:T(8,128)(2,1)S(1)}, u32[]{:S(2)}, u32[]{:S(2)}) collective-permute-start(bf16[128,512]{1,0:T(8,128)(2,1)S(1)} %get-tuple-element.85), channel_id=1, source_target_pairs={{2,0},{3,1},{4,6},{5,7},{10,8},{11,9},{12,14},{13,15},{18,16},{19,... | collective-permute-start | bytes 393224 | tf_op jit(solution)/shard_map/ppermute | solution.py:352
  33.8 4.4 %collective-permute-done.12 = bf16[128,512]{1,0:T(8,128)(2,1)} collective-permute-done((bf16[128,512]{1,0:T(8,128)(2,1)}, bf16[128,512]{1,0:T(8,128)(2,1)}, u32[]{:S(2)}, u32[]{:S(2)}) %collective-permute-start.12) | collective-permute-done | bytes 131104 | tf_op jit(solution)/shard_map/ppermute | solution.py:352
  38.2 0.9 broadcast_select_fusion.3.refs_2_
  39.2 3.2 %collective-permute-done.9 = bf16[128,512]{1,0:T(8,128)(2,1)S(1)} collective-permute-done((bf16[128,512]{1,0:T(8,128)(2,1)S(1)}, bf16[128,512]{1,0:T(8,128)(2,1)S(1)}, u32[]{:S(2)}, u32[]{:S(2)}) %collective-permute-start.9) | collective-permute-done | bytes 131104 | tf_op jit(solution)/shard_map/ppermute | solution.py:352
  42.5 2.5 %collective-permute-done.6 = bf16[128,512]{1,0:T(8,128)(2,1)S(1)} collective-permute-done((bf16[128,512]{1,0:T(8,128)(2,1)S(1)}, bf16[128,512]{1,0:T(8,128)(2,1)S(1)}, u32[]{:S(2)}, u32[]{:S(2)}) %collective-permute-start.6) | collective-permute-done | bytes 131104 | tf_op jit(solution)/shard_map/ppermute | solution.py:352
  45.1 1.3 %collective-permute-done.13.refs_3_ = bf16[128,512]{1,0:T(8,128)(2,1)S(1)} collective-permute-done((bf16[128,512]{1,0:T(8,128)(2,1)S(1)}, bf16[128,512]{1,0:T(8,128)(2,1)S(1)}, u32[]{:S(2)}, u32[]{:S(2)}) %collective-permute-start.13) | collective-permute-done | bytes 131104 | tf_op jit(solution)/shard_map/ppermute | solution.py:373
  47.2 2.5 %collective-permute-start.19 = (f32[2,512]{1,0:T(2,128)S(1)}, f32[2,512]{1,0:T(2,128)S(1)}, u32[]{:S(2)}, u32[]{:S(2)}) collective-permute-start(f32[2,512]{1,0:T(2,128)S(1)} %get-tuple-element.96.refs_0_), channel_id=1, source_target_pairs={{0,24},{8,16},{16,8},{24,0},{1,25},{9,17},{17,9},{25,1},{2,26},{10... | collective-permute-start | bytes 12296 | tf_op jit(solution)/shard_map/ppermute | solution.py:378
  50.8 1.0 %collective-permute-done.19.refs_3_ = f32[2,512]{1,0:T(2,128)S(1)} collective-permute-done((f32[2,512]{1,0:T(2,128)S(1)}, f32[2,512]{1,0:T(2,128)S(1)}, u32[]{:S(2)}, u32[]{:S(2)}) %collective-permute-start.19) | collective-permute-done | bytes 4128 | tf_op jit(solution)/shard_map/ppermute | solution.py:378
  51.8 1.5 %collective-permute-done.18.refs_2_ = f32[2,512]{1,0:T(2,128)S(1)} collective-permute-done((f32[2,512]{1,0:T(2,128)S(1)}, f32[2,512]{1,0:T(2,128)S(1)}, u32[]{:S(2)}, u32[]{:S(2)}) %collective-permute-start.18) | collective-permute-done | bytes 4128 | tf_op jit(solution)/shard_map/ppermute | solution.py:378
  53.9 1.0 %apply_back.1 = (bf16[256,256]{1,0:T(8,128)(2,1)S(1)}, bf16[256,256]{1,0:T(8,128)(2,1)S(1)}, f32[128,512]{1,0:T(8,128)S(1)}, f32[128,512]{1,0:T(8,128)S(1)}, f32...) custom-call(f32[2,512]{1,0:T(2,128)S(1)} %get-tuple-element.96.refs_, ...), custom_call_target="tpu_custom_call" | custom-call | flops 536870912 | bytes 4210688 | tf_op jit(solution)/shard_map/apply_back/pallas_call | solution.py:328
  54.8 1.5 %collective-permute-start.20 = (bf16[128,512]{1,0:T(8,128)(2,1)S(1)}, bf16[128,512]{1,0:T(8,128)(2,1)S(1)}, u32[]{:S(2)}, u32[]{:S(2)}) collective-permute-start(bf16[128,512]{1,0:T(8,128)(2,1)S(1)} %get-tuple-element.109), channel_id=1, source_target_pairs={{0,2},{1,3},{6,4},{7,5},{8,10},{9,11},{14,12},{15,13},{16,18},{17,... | collective-permute-start | bytes 393224 | tf_op jit(solution)/shard_map/ppermute | solution.py:352
  56.3 1.3 %collective-permute-start.23 = (bf16[128,512]{1,0:T(8,128)(2,1)S(1)}, bf16[128,512]{1,0:T(8,128)(2,1)S(1)}, u32[]{:S(2)}, u32[]{:S(2)}) collective-permute-start(bf16[128,512]{1,0:T(8,128)(2,1)S(1)} %get-tuple-element.113), channel_id=1, source_target_pairs={{0,2},{1,3},{6,4},{7,5},{8,10},{9,11},{14,12},{15,13},{16,18},{17,... | collective-permute-start | bytes 393224 | tf_op jit(solution)/shard_map/ppermute | solution.py:352
  57.6 1.3 %collective-permute-start.26 = (bf16[128,512]{1,0:T(8,128)(2,1)S(1)}, bf16[128,512]{1,0:T(8,128)(2,1)S(1)}, u32[]{:S(2)}, u32[]{:S(2)}) collective-permute-start(bf16[128,512]{1,0:T(8,128)(2,1)S(1)} %get-tuple-element.117), channel_id=1, source_target_pairs={{0,2},{1,3},{6,4},{7,5},{8,10},{9,11},{14,12},{15,13},{16,18},{17,... | collective-permute-start | bytes 393224 | tf_op jit(solution)/shard_map/ppermute | solution.py:352
  58.9 1.3 %collective-permute-done.20.got = bf16[128,512]{1,0:T(8,128)(2,1)S(1)} collective-permute-done((bf16[128,512]{1,0:T(8,128)(2,1)S(1)}, bf16[128,512]{1,0:T(8,128)(2,1)S(1)}, u32[]{:S(2)}, u32[]{:S(2)}) %collective-permute-start.20) | collective-permute-done | bytes 131104 | tf_op jit(solution)/shard_map/ppermute | solution.py:352
  60.9 1.0 %collective-permute-done.23.got = bf16[128,512]{1,0:T(8,128)(2,1)S(1)} collective-permute-done((bf16[128,512]{1,0:T(8,128)(2,1)S(1)}, bf16[128,512]{1,0:T(8,128)(2,1)S(1)}, u32[]{:S(2)}, u32[]{:S(2)}) %collective-permute-start.23) | collective-permute-done | bytes 131104 | tf_op jit(solution)/shard_map/ppermute | solution.py:352
  64.3 1.3 %collective-permute-start.22 = (bf16[128,512]{1,0:T(8,128)(2,1)S(1)}, bf16[128,512]{1,0:T(8,128)(2,1)S(1)}, u32[]{:S(2)}, u32[]{:S(2)}) collective-permute-start(bf16[128,512]{1,0:T(8,128)(2,1)S(1)} %get-tuple-element.110), channel_id=1, source_target_pairs={{2,0},{3,1},{4,6},{5,7},{10,8},{11,9},{12,14},{13,15},{18,16},{19,... | collective-permute-start | bytes 393224 | tf_op jit(solution)/shard_map/ppermute | solution.py:352
  65.9 1.4 %collective-permute-start.25 = (bf16[128,512]{1,0:T(8,128)(2,1)S(1)}, bf16[128,512]{1,0:T(8,128)(2,1)S(1)}, u32[]{:S(2)}, u32[]{:S(2)}) collective-permute-start(bf16[128,512]{1,0:T(8,128)(2,1)S(1)} %get-tuple-element.114), channel_id=1, source_target_pairs={{2,0},{3,1},{4,6},{5,7},{10,8},{11,9},{12,14},{13,15},{18,16},{19,... | collective-permute-start | bytes 393224 | tf_op jit(solution)/shard_map/ppermute | solution.py:352
  67.6 1.4 %collective-permute-start.28 = (bf16[128,512]{1,0:T(8,128)(2,1)S(1)}, bf16[128,512]{1,0:T(8,128)(2,1)S(1)}, u32[]{:S(2)}, u32[]{:S(2)}) collective-permute-start(bf16[128,512]{1,0:T(8,128)(2,1)S(1)} %get-tuple-element.118), channel_id=1, source_target_pairs={{2,0},{3,1},{4,6},{5,7},{10,8},{11,9},{12,14},{13,15},{18,16},{19,... | collective-permute-start | bytes 393224 | tf_op jit(solution)/shard_map/ppermute | solution.py:352
  69.1 7.1 %collective-permute-done.22 = bf16[128,512]{1,0:T(8,128)(2,1)S(1)} collective-permute-done((bf16[128,512]{1,0:T(8,128)(2,1)S(1)}, bf16[128,512]{1,0:T(8,128)(2,1)S(1)}, u32[]{:S(2)}, u32[]{:S(2)}) %collective-permute-start.22) | collective-permute-done | bytes 131104 | tf_op jit(solution)/shard_map/ppermute | solution.py:352
  76.3 1.3 %collective-permute-done.25 = bf16[128,512]{1,0:T(8,128)(2,1)S(1)} collective-permute-done((bf16[128,512]{1,0:T(8,128)(2,1)S(1)}, bf16[128,512]{1,0:T(8,128)(2,1)S(1)}, u32[]{:S(2)}, u32[]{:S(2)}) %collective-permute-start.25) | collective-permute-done | bytes 131104 | tf_op jit(solution)/shard_map/ppermute | solution.py:352
  77.7 2.5 %collective-permute-done.28 = bf16[128,512]{1,0:T(8,128)(2,1)S(1)} collective-permute-done((bf16[128,512]{1,0:T(8,128)(2,1)S(1)}, bf16[128,512]{1,0:T(8,128)(2,1)S(1)}, u32[]{:S(2)}, u32[]{:S(2)}) %collective-permute-start.28) | collective-permute-done | bytes 131104 | tf_op jit(solution)/shard_map/ppermute | solution.py:352
  80.3 1.3 %collective-permute-done.31.refs_5_ = bf16[128,512]{1,0:T(8,128)(2,1)S(1)} collective-permute-done((bf16[128,512]{1,0:T(8,128)(2,1)S(1)}, bf16[128,512]{1,0:T(8,128)(2,1)S(1)}, u32[]{:S(2)}, u32[]{:S(2)}) %collective-permute-start.31) | collective-permute-done | bytes 131104 | tf_op jit(solution)/shard_map/ppermute | solution.py:373
  81.7 1.3 %second_adjoint.1 = (bf16[256,512]{1,0:T(8,128)(2,1)S(1)}, bf16[256,512]{1,0:T(8,128)(2,1)S(1)}, bf16[512,256]{1,0:T(8,128)(2,1)S(1)}, bf16[256,256]{1,0:T(8,128...) custom-call(bf16[128,512]{1,0:T(8,128)(2,1)S(1)} %broadcast_select_f, ...), custom_call_target="tpu_custom_call" | custom-call | flops 805306368 | bytes 4718592 | tf_op jit(solution)/shard_map/second_adjoint/pallas_call | solution.py:328
  83.0 1.8 %collective-permute-start.32 = (bf16[96,512]{1,0:T(8,128)(2,1)S(1)}, bf16[96,512]{1,0:T(8,128)(2,1)S(1)}, u32[]{:S(2)}, u32[]{:S(2)}) collective-permute-start(bf16[96,512]{1,0:T(8,128)(2,1)S(1)} %get-tuple-element.138), channel_id=1, source_target_pairs={{0,6},{1,7},{2,4},{3,5},{4,2},{5,3},{6,0},{7,1},{8,14},{9,15},{10,... | collective-permute-start | bytes 294920 | tf_op jit(solution)/shard_map/ppermute | solution.py:346
  84.9 2.6 %collective-permute-start.34 = (bf16[96,512]{1,0:T(8,128)(2,1)S(1)}, bf16[96,512]{1,0:T(8,128)(2,1)S(1)}, u32[]{:S(2)}, u32[]{:S(2)}) collective-permute-start(bf16[96,512]{1,0:T(8,128)(2,1)S(1)} %get-tuple-element.140), channel_id=1, source_target_pairs={{0,2},{1,3},{2,0},{3,1},{4,6},{5,7},{6,4},{7,5},{8,10},{9,11},{10,... | collective-permute-start | bytes 294920 | tf_op jit(solution)/shard_map/ppermute | solution.py:346
  87.5 1.0 %query_grad.1 = bf16[256,512]{1,0:T(8,128)(2,1)} custom-call(bf16[256,256]{1,0:T(8,128)(2,1)S(1)} %get-tuple-element.102.gate_back, bf16[256,256]{1,0:T(8,128)(2,1)S(1)} %get-tuple-element.103.up_back, bf16[256,512]{1,0:T(8,128)(2,1)S(1)} %get-tuple-element.104.f1t, bf16[256,512]{1,0:T(8,128)(2,1)S(1)} %get-tuple-element.105.f3t), custom_call_target="tpu_custom_call" | custom-call | flops 134217728 | bytes 786432 | tf_op jit(solution)/shard_map/query_grad/pallas_call | solution.py:328
  88.5 1.4 %token_grads.1 = (bf16[256,512]{1,0:T(8,128)(2,1)}, bf16[256,512]{1,0:T(8,128)(2,1)}) custom-call(f32[1,256]{1,0:T(1,128)S(1)} %bitcast.30, bf16[256,256]{1,0:T(8,128)(2,1)S(1)} %copy-done.20, bf16[256,256]{1,0:T(8,128)(2,1)S(1)} %get-tuple-element.127.refs_2_, bf16[256,256]{1,0:T(8,128)(2,1)S(1)} %get-tuple-element.128.refs_3_, ...), custom_call_target="tpu_custom_call" | custom-call | flops 402653184 | bytes 2360320 | tf_op jit(solution)/shard_map/token_grads/pallas_call | solution.py:328
  90.6 3.3 %collective-permute-done.33.refs_1_ = bf16[96,512]{1,0:T(8,128)(2,1)S(1)} collective-permute-done((bf16[96,512]{1,0:T(8,128)(2,1)S(1)}, bf16[96,512]{1,0:T(8,128)(2,1)S(1)}, u32[]{:S(2)}, u32[]{:S(2)}) %collective-permute-start.33) | collective-permute-done | bytes 98336 | tf_op jit(solution)/shard_map/ppermute | solution.py:346
  (106 shorter events, 12.7 us)
Async XLA Ops:
  0.6 2.5 %collective-permute-start.1 = (bf16[256,512]{1,0:T(8,128)(2,1)}, bf16[256,512]{1,0:T(8,128)(2,1)S(1)}, u32[]{:S(2)}, u32[]{:S(2)}) collective-permute-start(bf16[256,512]{1,0:T(8,128)(2,1)} %vo.3), channel_id=1, source_target_pairs={{0,1},{1,0},{2,3},{3,2},{4,5},{5,4},{6,7},{7,6},{8,9},{9,8},{10,11... | collective-permute-start | bytes 786440 | tf_op jit(solution)/shard_map/ppermute | solution.py:476
  1.2 2.0 %collective-permute-start = (bf16[256,512]{1,0:T(8,128)(2,1)}, bf16[256,512]{1,0:T(8,128)(2,1)S(1)}, u32[]{:S(2)}, u32[]{:S(2)}) collective-permute-start(bf16[256,512]{1,0:T(8,128)(2,1)} %refs_9_.1), channel_id=1, source_target_pairs={{0,1},{1,0},{2,3},{3,2},{4,5},{5,4},{6,7},{7,6},{8,9},{9,8},{10,11... | collective-permute-start | bytes 786440 | tf_op jit(solution)/shard_map/ppermute | solution.py:476
  1.3 1.6 %copy-start.27 = (bf16[1,512,256]{2,1,0:T(8,128)(2,1)S(1)}, bf16[1,512,256]{2,1,0:T(8,128)(2,1)}, u32[]{:S(2)}) copy-start(bf16[1,512,256]{2,1,0:T(8,128)(2,1)} %param.16) | copy-start | bytes 786436
  1.3 1.8 %collective-permute-start.2 = (f32[1,256]{1,0:T(1,128)S(1)}, f32[1,256]{1,0:T(1,128)S(1)}, u32[]{:S(2)}, u32[]{:S(2)}) collective-permute-start(f32[1,256]{1,0:T(1,128)S(1)} %bitcast.27), channel_id=1, source_target_pairs={{0,1},{1,0},{2,3},{3,2},{4,5},{5,4},{6,7},{7,6},{8,9},{9,8},{10,11... | collective-permute-start | bytes 3080 | tf_op jit(solution)/shard_map/ppermute | solution.py:476
  1.8 1.4 %copy-start.13 = (bf16[256,512]{1,0:T(8,128)(2,1)S(1)}, bf16[256,512]{1,0:T(8,128)(2,1)}, u32[]{:S(2)}) copy-start(bf16[256,512]{1,0:T(8,128)(2,1)} %vo.3) | copy-start | bytes 786436
  3.1 2.1 %copy-start.17 = (bf16[256,512]{1,0:T(8,128)(2,1)}, bf16[256,512]{1,0:T(8,128)(2,1)S(1)}, u32[]{:S(2)}) copy-start(bf16[256,512]{1,0:T(8,128)(2,1)S(1)} %collective-permute-done.1.vx) | copy-start | bytes 786436
  4.0 1.3 %copy-start.14 = (bf16[256,512]{1,0:T(8,128)(2,1)S(1)}, bf16[256,512]{1,0:T(8,128)(2,1)}, u32[]{:S(2)}) copy-start(bf16[256,512]{1,0:T(8,128)(2,1)} %go.1) | copy-start | bytes 786436
  5.2 15.6 %collective-permute-start.3 = (bf16[256,512]{1,0:T(8,128)(2,1)S(1)}, bf16[256,512]{1,0:T(8,128)(2,1)S(1)}, u32[]{:S(2)}, u32[]{:S(2)}) collective-permute-start(bf16[256,512]{1,0:T(8,128)(2,1)S(1)} %copy-done.14), channel_id=1, source_target_pairs={{0,1},{1,0},{2,3},{3,2},{4,5},{5,4},{6,7},{7,6},{8,9},{9,8},{10,11... | collective-permute-start | bytes 786440 | tf_op jit(solution)/shard_map/ppermute | solution.py:476
  5.4 8.8 %collective-permute-start.10 = (bf16[128,512]{1,0:T(8,128)(2,1)S(1)}, bf16[128,512]{1,0:T(8,128)(2,1)S(1)}, u32[]{:S(2)}, u32[]{:S(2)}) collective-permute-start(bf16[128,512]{1,0:T(8,128)(2,1)S(1)} %get-tuple-element.92), channel_id=1, source_target_pairs={{0,2},{1,3},{6,4},{7,5},{8,10},{9,11},{14,12},{15,13},{16,18},{17,... | collective-permute-start | bytes 393224 | tf_op jit(solution)/shard_map/ppermute | solution.py:352
  10.3 6.7 %collective-permute-start.4 = (bf16[128,512]{1,0:T(8,128)(2,1)S(1)}, bf16[128,512]{1,0:T(8,128)(2,1)S(1)}, u32[]{:S(2)}, u32[]{:S(2)}) collective-permute-start(bf16[128,512]{1,0:T(8,128)(2,1)S(1)} %get-tuple-element.84), channel_id=1, source_target_pairs={{0,2},{1,3},{6,4},{7,5},{8,10},{9,11},{14,12},{15,13},{16,18},{17,... | collective-permute-start | bytes 393224 | tf_op jit(solution)/shard_map/ppermute | solution.py:352
  11.6 7.2 %collective-permute-start.7 = (bf16[128,512]{1,0:T(8,128)(2,1)S(1)}, bf16[128,512]{1,0:T(8,128)(2,1)S(1)}, u32[]{:S(2)}, u32[]{:S(2)}) collective-permute-start(bf16[128,512]{1,0:T(8,128)(2,1)S(1)} %get-tuple-element.88), channel_id=1, source_target_pairs={{0,2},{1,3},{6,4},{7,5},{8,10},{9,11},{14,12},{15,13},{16,18},{17,... | collective-permute-start | bytes 393224 | tf_op jit(solution)/shard_map/ppermute | solution.py:352
  14.2 11.8 %collective-permute-start.11 = (bf16[128,512]{1,0:T(8,128)(2,1)S(1)}, bf16[128,512]{1,0:T(8,128)(2,1)S(1)}, u32[]{:S(2)}, u32[]{:S(2)}) collective-permute-start(bf16[128,512]{1,0:T(8,128)(2,1)S(1)} %carry.8.mine), channel_id=1, source_target_pairs={{2,4},{3,5},{4,2},{5,3},{10,12},{11,13},{12,10},{13,11},{18,20},{1... | collective-permute-start | bytes 393224 | tf_op jit(solution)/shard_map/ppermute | solution.py:352
  17.0 3.8 %copy-start.18 = (bf16[256,512]{1,0:T(8,128)(2,1)S(1)}, bf16[256,512]{1,0:T(8,128)(2,1)}, u32[]{:S(2)}) copy-start(bf16[256,512]{1,0:T(8,128)(2,1)} %copy-done.17) | copy-start | bytes 786436
  17.0 14.4 %collective-permute-start.5 = (bf16[128,512]{1,0:T(8,128)(2,1)S(1)}, bf16[128,512]{1,0:T(8,128)(2,1)}, u32[]{:S(2)}, u32[]{:S(2)}) collective-permute-start(bf16[128,512]{1,0:T(8,128)(2,1)S(1)} %carry.6.mine), channel_id=1, source_target_pairs={{2,4},{3,5},{4,2},{5,3},{10,12},{11,13},{12,10},{13,11},{18,20},{1... | collective-permute-start | bytes 393224 | tf_op jit(solution)/shard_map/ppermute | solution.py:352
  18.8 2.0 %copy-start.26 = (f32[512]{0:T(512)S(1)}, f32[512]{0:T(512)}, u32[]{:S(2)}) copy-start(f32[512]{0:T(512)} %param.14) | copy-start | bytes 6148
  19.5 9.5 %collective-permute-start.8 = (bf16[128,512]{1,0:T(8,128)(2,1)}, bf16[128,512]{1,0:T(8,128)(2,1)}, u32[]{:S(2)}, u32[]{:S(2)}) collective-permute-start(bf16[128,512]{1,0:T(8,128)(2,1)} %carry.7.mine), channel_id=1, source_target_pairs={{2,4},{3,5},{4,2},{5,3},{10,12},{11,13},{12,10},{13,11},{18,20},{1... | collective-permute-start | bytes 393224 | tf_op jit(solution)/shard_map/ppermute | solution.py:352
  26.0 2.9 %copy-start = (bf16[256,512]{1,0:T(8,128)(2,1)S(1)}, bf16[256,512]{1,0:T(8,128)(2,1)}, u32[]{:S(2)}) copy-start(bf16[256,512]{1,0:T(8,128)(2,1)} %refs_10_.1) | copy-start | bytes 786436
  27.6 10.6 %collective-permute-start.12 = (bf16[128,512]{1,0:T(8,128)(2,1)}, bf16[128,512]{1,0:T(8,128)(2,1)}, u32[]{:S(2)}, u32[]{:S(2)}) collective-permute-start(bf16[128,512]{1,0:T(8,128)(2,1)} %get-tuple-element.93), channel_id=1, source_target_pairs={{2,0},{3,1},{4,6},{5,7},{10,8},{11,9},{12,14},{13,15},{18,16},{19,... | collective-permute-start | bytes 393224 | tf_op jit(solution)/shard_map/ppermute | solution.py:352
  28.9 16.2 %collective-permute-start.16 = (bf16[256,512]{1,0:T(8,128)(2,1)S(1)}, bf16[256,512]{1,0:T(8,128)(2,1)S(1)}, u32[]{:S(2)}, u32[]{:S(2)}) collective-permute-start(bf16[256,512]{1,0:T(8,128)(2,1)S(1)} %copy-done), channel_id=1, source_target_pairs={{0,1},{1,0},{2,3},{3,2},{4,5},{5,4},{6,7},{7,6},{8,9},{9,8},{10,11... | collective-permute-start | bytes 786440 | tf_op jit(solution)/shard_map/ppermute | solution.py:476
  30.1 12.3 %collective-permute-start.9 = (bf16[128,512]{1,0:T(8,128)(2,1)S(1)}, bf16[128,512]{1,0:T(8,128)(2,1)S(1)}, u32[]{:S(2)}, u32[]{:S(2)}) collective-permute-start(bf16[128,512]{1,0:T(8,128)(2,1)S(1)} %get-tuple-element.89), channel_id=1, source_target_pairs={{2,0},{3,1},{4,6},{5,7},{10,8},{11,9},{12,14},{13,15},{18,16},{19,... | collective-permute-start | bytes 393224 | tf_op jit(solution)/shard_map/ppermute | solution.py:352
  32.5 12.5 %collective-permute-start.6 = (bf16[128,512]{1,0:T(8,128)(2,1)S(1)}, bf16[128,512]{1,0:T(8,128)(2,1)S(1)}, u32[]{:S(2)}, u32[]{:S(2)}) collective-permute-start(bf16[128,512]{1,0:T(8,128)(2,1)S(1)} %get-tuple-element.85), channel_id=1, source_target_pairs={{2,0},{3,1},{4,6},{5,7},{10,8},{11,9},{12,14},{13,15},{18,16},{19,... | collective-permute-start | bytes 393224 | tf_op jit(solution)/shard_map/ppermute | solution.py:352
  39.1 6.0 %collective-permute-start.15 = (bf16[128,512]{1,0:T(8,128)(2,1)S(1)}, bf16[128,512]{1,0:T(8,128)(2,1)S(1)}, u32[]{:S(2)}, u32[]{:S(2)}) collective-permute-start(bf16[128,512]{1,0:T(8,128)(2,1)S(1)} %broadcast_select_fusion.3.refs_2_), channel_id=1, source_target_pairs={{0,1},{1,0},{2,3},{3,2},{4,5},{5,4},{6,7},{7,6},{8,9},{9,8},{10,11... | collective-permute-start | bytes 393224 | tf_op jit(solution)/shard_map/ppermute | solution.py:373
  42.4 2.7 %collective-permute-start.14 = (bf16[128,512]{1,0:T(8,128)(2,1)S(1)}, bf16[128,512]{1,0:T(8,128)(2,1)S(1)}, u32[]{:S(2)}, u32[]{:S(2)}) collective-permute-start(bf16[128,512]{1,0:T(8,128)(2,1)S(1)} %broadcast_select_fusion.4.refs_1_), channel_id=1, source_target_pairs={{0,1},{1,0},{2,3},{3,2},{4,5},{5,4},{6,7},{7,6},{8,9},{9,8},{10,11... | collective-permute-start | bytes 393224 | tf_op jit(solution)/shard_map/ppermute | solution.py:373
  45.0 1.4 %collective-permute-start.13 = (bf16[128,512]{1,0:T(8,128)(2,1)S(1)}, bf16[128,512]{1,0:T(8,128)(2,1)S(1)}, u32[]{:S(2)}, u32[]{:S(2)}) collective-permute-start(bf16[128,512]{1,0:T(8,128)(2,1)S(1)} %broadcast_select_fusion.5.refs_0_), channel_id=1, source_target_pairs={{0,1},{1,0},{2,3},{3,2},{4,5},{5,4},{6,7},{7,6},{8,9},{9,8},{10,11... | collective-permute-start | bytes 393224 | tf_op jit(solution)/shard_map/ppermute | solution.py:373
  47.2 4.6 %collective-permute-start.19 = (f32[2,512]{1,0:T(2,128)S(1)}, f32[2,512]{1,0:T(2,128)S(1)}, u32[]{:S(2)}, u32[]{:S(2)}) collective-permute-start(f32[2,512]{1,0:T(2,128)S(1)} %get-tuple-element.96.refs_0_), channel_id=1, source_target_pairs={{0,24},{8,16},{16,8},{24,0},{1,25},{9,17},{17,9},{25,1},{2,26},{10... | collective-permute-start | bytes 12296 | tf_op jit(solution)/shard_map/ppermute | solution.py:378
  49.7 3.6 %collective-permute-start.18 = (f32[2,512]{1,0:T(2,128)S(1)}, f32[2,512]{1,0:T(2,128)S(1)}, u32[]{:S(2)}, u32[]{:S(2)}) collective-permute-start(f32[2,512]{1,0:T(2,128)S(1)} %get-tuple-element.96.refs_0_), channel_id=1, source_target_pairs={{0,16},{8,24},{16,0},{24,8},{1,17},{9,25},{17,1},{25,9},{2,18},{10... | collective-permute-start | bytes 12296 | tf_op jit(solution)/shard_map/ppermute | solution.py:378
  50.3 3.6 %collective-permute-start.17 = (f32[2,512]{1,0:T(2,128)S(1)}, f32[2,512]{1,0:T(2,128)S(1)}, u32[]{:S(2)}, u32[]{:S(2)}) collective-permute-start(f32[2,512]{1,0:T(2,128)S(1)} %get-tuple-element.96.refs_0_), channel_id=1, source_target_pairs={{0,8},{8,0},{16,24},{24,16},{1,9},{9,1},{17,25},{25,17},{2,10},{10... | collective-permute-start | bytes 12296 | tf_op jit(solution)/shard_map/ppermute | solution.py:378
  54.8 5.4 %collective-permute-start.20 = (bf16[128,512]{1,0:T(8,128)(2,1)S(1)}, bf16[128,512]{1,0:T(8,128)(2,1)S(1)}, u32[]{:S(2)}, u32[]{:S(2)}) collective-permute-start(bf16[128,512]{1,0:T(8,128)(2,1)S(1)} %get-tuple-element.109), channel_id=1, source_target_pairs={{0,2},{1,3},{6,4},{7,5},{8,10},{9,11},{14,12},{15,13},{16,18},{17,... | collective-permute-start | bytes 393224 | tf_op jit(solution)/shard_map/ppermute | solution.py:352
  56.3 5.7 %collective-permute-start.23 = (bf16[128,512]{1,0:T(8,128)(2,1)S(1)}, bf16[128,512]{1,0:T(8,128)(2,1)S(1)}, u32[]{:S(2)}, u32[]{:S(2)}) collective-permute-start(bf16[128,512]{1,0:T(8,128)(2,1)S(1)} %get-tuple-element.113), channel_id=1, source_target_pairs={{0,2},{1,3},{6,4},{7,5},{8,10},{9,11},{14,12},{15,13},{16,18},{17,... | collective-permute-start | bytes 393224 | tf_op jit(solution)/shard_map/ppermute | solution.py:352
  57.6 5.8 %collective-permute-start.26 = (bf16[128,512]{1,0:T(8,128)(2,1)S(1)}, bf16[128,512]{1,0:T(8,128)(2,1)S(1)}, u32[]{:S(2)}, u32[]{:S(2)}) collective-permute-start(bf16[128,512]{1,0:T(8,128)(2,1)S(1)} %get-tuple-element.117), channel_id=1, source_target_pairs={{0,2},{1,3},{6,4},{7,5},{8,10},{9,11},{14,12},{15,13},{16,18},{17,... | collective-permute-start | bytes 393224 | tf_op jit(solution)/shard_map/ppermute | solution.py:352
  60.3 3.8 %collective-permute-start.21 = (bf16[128,512]{1,0:T(8,128)(2,1)S(1)}, bf16[128,512]{1,0:T(8,128)(2,1)S(1)}, u32[]{:S(2)}, u32[]{:S(2)}) collective-permute-start(bf16[128,512]{1,0:T(8,128)(2,1)S(1)} %carry.9.mine), channel_id=1, source_target_pairs={{2,4},{3,5},{4,2},{5,3},{10,12},{11,13},{12,10},{13,11},{18,20},{1... | collective-permute-start | bytes 393224 | tf_op jit(solution)/shard_map/ppermute | solution.py:352
  62.0 3.6 %collective-permute-start.24 = (bf16[128,512]{1,0:T(8,128)(2,1)S(1)}, bf16[128,512]{1,0:T(8,128)(2,1)S(1)}, u32[]{:S(2)}, u32[]{:S(2)}) collective-permute-start(bf16[128,512]{1,0:T(8,128)(2,1)S(1)} %carry.10.mine), channel_id=1, source_target_pairs={{2,4},{3,5},{4,2},{5,3},{10,12},{11,13},{12,10},{13,11},{18,20},{1... | collective-permute-start | bytes 393224 | tf_op jit(solution)/shard_map/ppermute | solution.py:352
  63.4 3.9 %collective-permute-start.27 = (bf16[128,512]{1,0:T(8,128)(2,1)S(1)}, bf16[128,512]{1,0:T(8,128)(2,1)S(1)}, u32[]{:S(2)}, u32[]{:S(2)}) collective-permute-start(bf16[128,512]{1,0:T(8,128)(2,1)S(1)} %carry.11.mine), channel_id=1, source_target_pairs={{2,4},{3,5},{4,2},{5,3},{10,12},{11,13},{12,10},{13,11},{18,20},{1... | collective-permute-start | bytes 393224 | tf_op jit(solution)/shard_map/ppermute | solution.py:352
  64.1 3.2 %copy-start.16 = (f32[128,512]{1,0:T(8,128)S(1)}, f32[128,512]{1,0:T(8,128)}, u32[]{:S(2)}) copy-start(f32[128,512]{1,0:T(8,128)} %copy-done.15) | copy-start | bytes 786436
  64.3 11.9 %collective-permute-start.22 = (bf16[128,512]{1,0:T(8,128)(2,1)S(1)}, bf16[128,512]{1,0:T(8,128)(2,1)S(1)}, u32[]{:S(2)}, u32[]{:S(2)}) collective-permute-start(bf16[128,512]{1,0:T(8,128)(2,1)S(1)} %get-tuple-element.110), channel_id=1, source_target_pairs={{2,0},{3,1},{4,6},{5,7},{10,8},{11,9},{12,14},{13,15},{18,16},{19,... | collective-permute-start | bytes 393224 | tf_op jit(solution)/shard_map/ppermute | solution.py:352
  65.6 16.0 %copy-start.10 = (f32[256,512]{1,0:T(8,128)S(1)}, f32[256,512]{1,0:T(8,128)}, u32[]{:S(2)}) copy-start(f32[256,512]{1,0:T(8,128)} %copy-done.9) | copy-start | bytes 1572868
  65.6 16.0 %copy-start.12 = (f32[256,512]{1,0:T(8,128)S(1)}, f32[256,512]{1,0:T(8,128)}, u32[]{:S(2)}) copy-start(f32[256,512]{1,0:T(8,128)} %copy-done.11) | copy-start | bytes 1572868
  65.9 11.8 %collective-permute-start.25 = (bf16[128,512]{1,0:T(8,128)(2,1)S(1)}, bf16[128,512]{1,0:T(8,128)(2,1)S(1)}, u32[]{:S(2)}, u32[]{:S(2)}) collective-permute-start(bf16[128,512]{1,0:T(8,128)(2,1)S(1)} %get-tuple-element.114), channel_id=1, source_target_pairs={{2,0},{3,1},{4,6},{5,7},{10,8},{11,9},{12,14},{13,15},{18,16},{19,... | collective-permute-start | bytes 393224 | tf_op jit(solution)/shard_map/ppermute | solution.py:352
  67.3 14.3 %copy-start.8 = (f32[256,512]{1,0:T(8,128)S(1)}, f32[256,512]{1,0:T(8,128)}, u32[]{:S(2)}) copy-start(f32[256,512]{1,0:T(8,128)} %copy-done.7) | copy-start | bytes 1572868
  67.6 14.0 %copy-start.4 = (bf16[512,512]{1,0:T(8,128)(2,1)S(1)}, bf16[512,512]{1,0:T(8,128)(2,1)}, u32[]{:S(2)}) copy-start(bf16[512,512]{1,0:T(8,128)(2,1)} %copy-done.3) | copy-start | bytes 1572868
  67.6 14.0 %copy-start.6 = (f32[256,512]{1,0:T(8,128)S(1)}, f32[256,512]{1,0:T(8,128)}, u32[]{:S(2)}) copy-start(f32[256,512]{1,0:T(8,128)} %copy-done.5) | copy-start | bytes 1572868
  67.6 12.6 %collective-permute-start.28 = (bf16[128,512]{1,0:T(8,128)(2,1)S(1)}, bf16[128,512]{1,0:T(8,128)(2,1)S(1)}, u32[]{:S(2)}, u32[]{:S(2)}) collective-permute-start(bf16[128,512]{1,0:T(8,128)(2,1)S(1)} %get-tuple-element.118), channel_id=1, source_target_pairs={{2,0},{3,1},{4,6},{5,7},{10,8},{11,9},{12,14},{13,15},{18,16},{19,... | collective-permute-start | bytes 393224 | tf_op jit(solution)/shard_map/ppermute | solution.py:352
  76.2 4.1 %collective-permute-start.29 = (bf16[128,512]{1,0:T(8,128)(2,1)S(1)}, bf16[128,512]{1,0:T(8,128)(2,1)S(1)}, u32[]{:S(2)}, u32[]{:S(2)}) collective-permute-start(bf16[128,512]{1,0:T(8,128)(2,1)S(1)} %broadcast_select_fusion.2.refs_0_), channel_id=1, source_target_pairs={{0,1},{1,0},{2,3},{3,2},{4,5},{5,4},{6,7},{7,6},{8,9},{9,8},{10,11... | collective-permute-start | bytes 393224 | tf_op jit(solution)/shard_map/ppermute | solution.py:373
  77.6 2.7 %collective-permute-start.30 = (bf16[128,512]{1,0:T(8,128)(2,1)S(1)}, bf16[128,512]{1,0:T(8,128)(2,1)S(1)}, u32[]{:S(2)}, u32[]{:S(2)}) collective-permute-start(bf16[128,512]{1,0:T(8,128)(2,1)S(1)} %broadcast_select_fusion.1.refs_1_), channel_id=1, source_target_pairs={{0,1},{1,0},{2,3},{3,2},{4,5},{5,4},{6,7},{7,6},{8,9},{9,8},{10,11... | collective-permute-start | bytes 393224 | tf_op jit(solution)/shard_map/ppermute | solution.py:373
  80.2 1.4 %collective-permute-start.31 = (bf16[128,512]{1,0:T(8,128)(2,1)S(1)}, bf16[128,512]{1,0:T(8,128)(2,1)S(1)}, u32[]{:S(2)}, u32[]{:S(2)}) collective-permute-start(bf16[128,512]{1,0:T(8,128)(2,1)S(1)} %broadcast_select_fusion.refs_2_), channel_id=1, source_target_pairs={{0,1},{1,0},{2,3},{3,2},{4,5},{5,4},{6,7},{7,6},{8,9},{9,8},{10,11... | collective-permute-start | bytes 393224 | tf_op jit(solution)/shard_map/ppermute | solution.py:373
  83.0 7.6 %collective-permute-start.32 = (bf16[96,512]{1,0:T(8,128)(2,1)S(1)}, bf16[96,512]{1,0:T(8,128)(2,1)S(1)}, u32[]{:S(2)}, u32[]{:S(2)}) collective-permute-start(bf16[96,512]{1,0:T(8,128)(2,1)S(1)} %get-tuple-element.138), channel_id=1, source_target_pairs={{0,6},{1,7},{2,4},{3,5},{4,2},{5,3},{6,0},{7,1},{8,14},{9,15},{10,... | collective-permute-start | bytes 294920 | tf_op jit(solution)/shard_map/ppermute | solution.py:346
  84.9 9.1 %collective-permute-start.33 = (bf16[96,512]{1,0:T(8,128)(2,1)S(1)}, bf16[96,512]{1,0:T(8,128)(2,1)S(1)}, u32[]{:S(2)}, u32[]{:S(2)}) collective-permute-start(bf16[96,512]{1,0:T(8,128)(2,1)S(1)} %get-tuple-element.139), channel_id=1, source_target_pairs={{0,4},{1,5},{2,6},{3,7},{4,0},{5,1},{6,2},{7,3},{8,12},{9,13},{10,... | collective-permute-start | bytes 294920 | tf_op jit(solution)/shard_map/ppermute | solution.py:346
  84.9 9.1 %collective-permute-start.34 = (bf16[96,512]{1,0:T(8,128)(2,1)S(1)}, bf16[96,512]{1,0:T(8,128)(2,1)S(1)}, u32[]{:S(2)}, u32[]{:S(2)}) collective-permute-start(bf16[96,512]{1,0:T(8,128)(2,1)S(1)} %get-tuple-element.140), channel_id=1, source_target_pairs={{0,2},{1,3},{2,0},{3,1},{4,6},{5,7},{6,4},{7,5},{8,10},{9,11},{10,... | collective-permute-start | bytes 294920 | tf_op jit(solution)/shard_map/ppermute | solution.py:346
  (15 other events, 13.1 us)

commit v7 on v6

--- a/solution.py
+++ b/solution.py
@@ -10,7 +10,7 @@
 EPSILON = 1e-06
 CORES = 2
 ROW_TILE = 16
-VMEM_LIMIT = 24 * 1024 * 1024
+VMEM_LIMIT = 16 * 1024 * 1024
 BF16, F32 = jnp.bfloat16, jnp.float32
 
 
@@ -140,6 +140,12 @@
     return jnp.concatenate(cotangent, axis=1).astype(BF16), jnp.concatenate(owned, axis=1)
 
 
+def update_sums(w1t, w3t, w2, keys, rates, values):
+    push = push_of(rates, values)
+    *_, mixed, _, _, gate_back, up_back = update_forward(w1t, w3t, w2, keys, push)
+    return nn(gate_back, keys), nn(up_back, keys), nt(push, mixed)
+
+
 def push_of(rates, values):
     return (-rates * values.T.astype(F32)).astype(BF16)
 
@@ -148,68 +154,74 @@
     return jnp.concatenate([own_ref[...], other_ref[...]], axis=axis)
 
 
-def cut_share(out, ref, chips, folds):
+def rows_of(ref, chip, core, chips, folds, i):
+    rows = ref.shape[0] // (chips * CORES)
+    height = rows // folds
+    return pl.ds(pl.multiple_of((chip * CORES + core) * rows + i * height, height), height)
+
+
+def cut_half(out, ref, parity, chips, folds):
     core = lax.axis_index("tok") % CORES
-    rows, width = ref.shape[0] // (chips * CORES), ref.shape[1]
-    height = rows // folds
-    for chip in range(chips):
+    height, width = ref.shape[0] // (chips * CORES * folds), ref.shape[1]
+    for k in range(chips // 2):
         for i in range(folds):
-            at = pl.multiple_of((chip * CORES + core) * rows + i * height, height)
-            out[chip * height : (chip + 1) * height, i * width : (i + 1) * width] = ref[
-                pl.ds(at, height), :
+            out[k * height : (k + 1) * height, i * width : (i + 1) * width] = ref[
+                rows_of(ref, 2 * k + parity, core, chips, folds, i), :
             ].astype(out.dtype)
 
 
-def place_shares(ref, mine, other, chips, folds):
-    core = lax.axis_index("tok") % CORES
-    rows, width = ref.shape[0] // (chips * CORES), ref.shape[1]
-    height = rows // folds
-    for share, c in ((mine, core), (other, 1 - core)):
-        for chip in range(chips):
-            for i in range(folds):
-                at = pl.multiple_of((chip * CORES + c) * rows + i * height, height)
-                ref[pl.ds(at, height), :] = share[
-                    chip * height : (chip + 1) * height, i * width : (i + 1) * width
-                ]
-
-
-def send_pieces(chips, folds, owned, gate_ref, up_ref, down_ref, outs):
+def place_half(ref, half, parity, core, chips, folds):
+    height, width = ref.shape[0] // (chips * CORES * folds), ref.shape[1]
+    for k in range(chips // 2):
+        for i in range(folds):
+            ref[rows_of(ref, 2 * k + parity, core, chips, folds, i), :] = half[
+                k * height : (k + 1) * height, i * width : (i + 1) * width
+            ]
+
+
+def place_halves(chips, folds, halves, matrices):
+    tok = lax.axis_index("tok")
+    parity, core = tok // CORES % 2, tok % CORES
+    for k, ref in enumerate(matrices):
+        whose = ((parity, core), (1 - parity, core), (parity, 1 - core), (1 - parity, 1 - core))
+        for half, (p, c) in zip(halves[4 * k : 4 * k + 4], whose):
+            place_half(ref, half, p, c, chips, folds if k == 2 else 1)
+
+
+def send_pieces(chips, folds, matrices, outs):
     tok = lax.axis_index("tok")
     chip, core = tok // CORES, tok % CORES
-    half = chips // 2
-    g, width = gate_ref.shape[0] // (chips * CORES), down_ref.shape[1]
     for step, out in enumerate(outs):
         to = partner(chip, step, chips)
-        holds = ((chip == half - 1) & (to < half)) | ((chip == half) & (to >= half))
-        first = (to * CORES + core) * g
-        for k, ref in enumerate((gate_ref, up_ref, down_ref)):
-            if k < 2:
-                rows = ref[pl.ds(pl.multiple_of(first, g), g), :]
-            else:
-                parts = [
-                    ref[pl.ds(pl.multiple_of(first * folds + i * g, g), g), :] for i in range(folds)
-                ]
-                rows = jnp.concatenate(parts, axis=1)
-            rest = owned[k][pl.ds(pl.multiple_of(to * g, g), g), :]
-            out[k * g : (k + 1) * g] = jnp.where(holds, rest - rows, -rows).astype(out.dtype)
-
-
-def cut_matrices(chips, folds, gate_ref, up_ref, down_ref, outs):
-    for k, ref in enumerate((gate_ref, up_ref, down_ref)):
-        folded = folds if k == 2 else 1
-        cut_share(outs[k], ref, chips, folded)
-        outs[3 + k][...] = outs[k][...].astype(BF16)
-
-
-def update_kernel(chips, folds, ko, kx, vo, vx, ro, rx, w1t, w3t, w2, *rest):
-    outs, (gate, up, down) = rest[:6], rest[6:]
-    keys = both(ko, kx)
-    push = push_of(both(ro, rx, 1), both(vo, vx))
-    *_, mixed, _, _, gate_back, up_back = update_forward(w1t[...], w3t[...], w2[...], keys, push)
-    down[...] = nt(push, mixed)
-    gate[...] = nn(gate_back, keys)
-    up[...] = nn(up_back, keys)
-    cut_matrices(chips, folds, gate, up, down, outs)
+        at = 0
+        for k, ref in enumerate(matrices):
+            folded = folds if k == 2 else 1
+            parts = [ref[rows_of(ref, to, core, chips, folded, i), :] for i in range(folded)]
+            rows = jnp.concatenate(parts, axis=1).astype(out.dtype)
+            out[at : at + rows.shape[0]] = rows
+            at += rows.shape[0]
+
+
+def cut_matrices(chips, folds, matrices, outs):
+    parity = lax.axis_index("tok") // CORES % 2
+    for k, ref in enumerate(matrices):
+        cut_half(outs[k], ref, parity, chips, folds if k == 2 else 1)
+        cut_half(outs[3 + k], ref, 1 - parity, chips, folds if k == 2 else 1)
+
+
+def prep_kernel(keys, values, rates, w1, w3, w2, w1t, w3t, gate, up, down):
+    w1t[...], w3t[...] = w1[...].T, w3[...].T
+    gate[...], up[...], down[...] = update_sums(
+        w1t[...], w3t[...], w2[...], keys[...], rates[...], values[...]
+    )
+
+
+def update_kernel(chips, folds, keys, values, rates, w1t, w3t, w2, own_gate, own_up, own_down, *rest):
+    outs, matrices = rest[:6], rest[6:]
+    sums = update_sums(w1t[...], w3t[...], w2[...], keys[...], rates[...], values[...])
+    for ref, own, total in zip(matrices, (own_gate, own_up, own_down), sums):
+        ref[...] = own[...] + total
+    cut_matrices(chips, folds, matrices, outs)
 
 
 def saved_kernel(
@@ -235,41 +247,52 @@
     gate_ref[...] = w1t[...].astype(F32)
     up_ref[...] = w3t[...].astype(F32)
     down_ref[...] = w2[...].astype(F32).T
-    cut_share(p1_ref, gate_ref, chips, 1)
-    cut_share(p3_ref, up_ref, chips, 1)
-    cut_share(p2_ref, down_ref, chips, folds)
+    parity = lax.axis_index("tok") // CORES % 2
+    cut_half(p1_ref, gate_ref, parity, chips, 1)
+    cut_half(p3_ref, up_ref, parity, chips, 1)
+    cut_half(p2_ref, down_ref, parity, chips, folds)
 
 
 def carry_kernel(own, got, out):
     out[...] = (own[...] + got[...].astype(F32)).astype(BF16)
 
 
-def owner_forward_kernel(folds, prior, mine, other, fast, moved):
-    total = mine[...].astype(F32) + other[...].astype(F32)
+def total_of_halves(halves):
+    total = halves[0][...].astype(F32)
+    for half in halves[1:]:
+        total = total + half[...].astype(F32)
+    return total
+
+
+def owner_forward_kernel(folds, prior, *refs):
+    fast, moved = refs[-2:]
+    total = total_of_halves(refs[:-2])
     fast[...], moved[...] = owner_forward(prior[...], total, folds)
 
 
-def owner_backward_kernel(folds, prior, moved, mine, other, cotangent, owned):
-    total = mine[...].astype(F32) + other[...].astype(F32)
+def owner_backward_kernel(folds, prior, moved, *refs):
+    cotangent, owned = refs[-2:]
+    total = total_of_halves(refs[:-2])
     cotangent[...], owned[...] = owner_backward(prior[...], moved[...], total, folds)
 
 
-def owner_result_kernel(folds, own, *refs):
-    gate, up, down = refs[-3:]
-    total = own[...]
-    for piece in refs[:-3]:
-        total = total + piece[...].astype(F32)
-    g = gate.shape[0]
-    gate[...], up[...] = total[:g], total[g : 2 * g]
-    for i, rows in enumerate(folds_of(total[2 * g :], folds)):
-        down[i * g : (i + 1) * g] = rows
+def owner_result_kernel(chips, folds, *refs):
+    owned, pieces, outs = refs[:3], refs[3:-3], refs[-3:]
+    bars = pieces[0][...]
+    for piece in pieces[1:]:
+        bars = bars + piece[...].astype(F32)
+    g = outs[0].shape[0]
+    block = lax.axis_index("tok") // (2 * CORES)
+    for k, out in enumerate(outs):
+        result = owned[k][pl.ds(pl.multiple_of(block * g, g), g), :] - bars[k * g : (k + 1) * g]
+        for i, rows in enumerate(folds_of(result, folds if k == 2 else 1)):
+            out[i * g : (i + 1) * g] = rows
 
 
 def apply_kernel(chips, folds, *refs):
-    pieces, refs = refs[:6], refs[6:]
+    halves, refs = refs[:12], refs[12:]
     qo, qx, weighted, f1t, f3t, f2t, output, mixed, up_slope, silu, sums = refs
-    for k, ref in enumerate((f1t, f3t, f2t)):
-        place_shares(ref, pieces[k], pieces[3 + k], chips, folds if k == 2 else 1)
+    place_halves(chips, folds, halves, (f1t, f3t, f2t))
     output[...], mixed[...], up_slope[...], silu[...], sums[...] = apply_forward(
         f1t[...], f3t[...], f2t[...], both(qo, qx), weighted[...]
     )
@@ -287,7 +310,7 @@
         f2t[...], sums, width, output[...], weighted[...], mixed[...], up_slope[...], silu[...],
         both(qo, qx),
     )
-    cut_matrices(chips, folds, gate, up, down, outs)
+    cut_matrices(chips, folds, (gate, up, down), outs)
     own = gate_back.shape[1]
     gate_back[...], up_back[...] = gb[:, :own], ub[:, :own]
 
@@ -297,17 +320,16 @@
 
 
 def second_kernel(chips, folds, *refs):
-    pieces, owned, refs = refs[:6], refs[6:9], refs[9:]
+    halves, refs = refs[:12], refs[12:]
     ko, kx, push, up_slope, silu, back_slope, back_curve = refs[:7]
     c1t, c3t, c2t, dbb_ref, upb_ref, gpb_ref = refs[7:13]
     outs, (gate, up, down) = refs[13 : 13 + chips], refs[13 + chips :]
-    for k, ref in enumerate((c1t, c3t, c2t)):
-        place_shares(ref, pieces[k], pieces[3 + k], chips, folds if k == 2 else 1)
+    place_halves(chips, folds, halves, (c1t, c3t, c2t))
     dbb, upb, gpb, gate[...], up[...], down[...] = second_adjoint(
         c1t[...], c3t[...], c2t[...], both(ko, kx), push[...],
         up_slope[...], silu[...], back_slope[...], back_curve[...],
     )
-    send_pieces(chips, folds, owned, gate, up, down, outs)
+    send_pieces(chips, folds, (gate, up, down), outs)
     own = dbb_ref.shape[1]
     dbb_ref[...], upb_ref[...], gpb_ref[...] = dbb[:, :own], upb[:, :own], gpb[:, :own]
 
@@ -347,30 +369,19 @@
     return [pieces[0], *got]
 
 
-def between_chips(x, pairs):
-    perm = [(a * CORES + c, b * CORES + c) for a, b in pairs for c in range(CORES)]
-    return lax.ppermute(x, "tok", perm)
-
-
-def outer_pairs(chips, hop):
-    return [(hop, hop + 1), (chips - 1 - hop, chips - 2 - hop)]
-
-
-def half_sums(own, own_rounded, chips):
-    carried, shape = own_rounded, [(own.shape, BF16)]
-    for hop in range(chips // 2 - 1):
-        got = between_chips(carried, outer_pairs(chips, hop))
-        (carried,) = call(carry_kernel, shape, (own, got), name="carry")
-    half = chips // 2
-    return carried, between_chips(carried, [(half - 1, half), (half, half - 1)])
-
-
-def from_inner(x, chip, chips):
-    for hop in reversed(range(chips // 2 - 1)):
-        pairs = outer_pairs(chips, hop)
-        got = between_chips(x, [(b, a) for a, b in pairs])
-        x = jnp.where((chip == pairs[0][0]) | (chip == pairs[1][0]), got, x)
-    return x, lax.ppermute(x, "tok", core_perm(chips * CORES))
+def to_chip(x, step, chips):
+    return lax.ppermute(x, "tok", chip_perm(chips * CORES, step))
+
+
+def half_sums(kept, given, chips):
+    (mine,) = call(carry_kernel, [(given.shape, BF16)], (kept, to_chip(given, 1, chips)), name="carry")
+    return [mine, *(to_chip(mine, step, chips) for step in range(2, chips, 2))]
+
+
+def from_owners(half, chips):
+    other = to_chip(half, 1, chips)
+    perm = core_perm(chips * CORES)
+    return [half, other, lax.ppermute(half, "tok", perm), lax.ppermute(other, "tok", perm)]
 
 
 def head_parts(part, heads):
@@ -439,7 +450,7 @@
 ):
     count, heads = lax.axis_size("tok"), lax.axis_size("head")
     tok = lax.axis_index("tok")
-    chips, chip = count // CORES, tok // CORES
+    chips = count // CORES
     own, dh = key_input.shape
     n = own * CORES
     w1, w3, w2 = gate_prior[0], up_prior[0], down_prior[0]
@@ -449,24 +460,23 @@
     gain = out_gain[None, :]
     inputs = query_input, key_input, value_input, out_grad, rates, gain, w1, w3, w2
 
-    if g % ROW_TILE or d % g or dh * g != fh * d or chips % 2:
+    if g % ROW_TILE or d % g or dh * g != fh * d or chips & (chips - 1) or chips < 2:
         query_grad, key_grad, value_grad, *results = by_blocks(inputs, tok, count, heads)
     else:
-        query_grad, key_grad, value_grad, *results = by_line(inputs, chip, chips, heads)
+        query_grad, key_grad, value_grad, *results = by_line(inputs, chips, heads)
     return (query_grad, key_grad, value_grad, *(r.T[None] for r in results))
 
 
-def by_line(inputs, chip, chips, heads):
+def by_line(inputs, chips, heads):
     query_input, key_input, value_input, out_grad, rates, gain, w1, w3, w2 = inputs
     count = chips * CORES
     own, dh = key_input.shape
     n, fh = own * CORES, w2.shape[0]
     g, d, folds = fh // count, dh // count, dh // fh
-    w1t, w3t = w1.T, w3.T
     product = 2 * n * dh * fh
 
-    share = (g * chips, dh)
-    share_sums = [(share, F32)] * 3 + [(share, BF16)] * 3
+    half = (g * chips // 2, dh)
+    half_shares = [(half, F32)] * 3 + [(half, BF16)] * 3
     matrices = [((fh, dh), BF16), ((fh, dh), BF16), ((dh, fh), BF16)]
     sums_scratch = [((fh, dh), F32), ((fh, dh), F32), ((dh, fh), F32)]
     hidden = ((fh, n), F32)
@@ -475,22 +485,29 @@
 
     pair = lambda x: lax.ppermute(x, "tok", core_perm(count))
     key_other, value_other, rate_other = pair(key_input), pair(value_input), pair(rates)
+    w1t, w3t, *own_sums = call(
+        prep_kernel,
+        [((fh, dh), BF16)] * 2 + sums_scratch,
+        (key_input, value_input, rates, w1, w3, w2),
+        name="own_tokens",
+        flops=3 * product,
+    )
+    sums = call(
+        functools.partial(update_kernel, chips, folds),
+        half_shares,
+        (key_other, value_other, rate_other, w1t, w3t, w2, *own_sums),
+        sums_scratch,
+        "update",
+        3 * product,
+    )
     keys_values = (
         key_input, key_other, value_input, value_other, rates, rate_other, w1t, w3t, w2,
-    )
-    sums = call(
-        functools.partial(update_kernel, chips, folds),
-        share_sums,
-        keys_values,
-        sums_scratch,
-        "update",
-        6 * product,
     )
     query_later, grad_later, *sums = lax.optimization_barrier((query_input, out_grad, *sums))
     query_other, grad_other = pair(query_later), pair(grad_later)
     *saved, weighted, p1, p3, p2 = call(
         functools.partial(saved_kernel, chips, folds),
-        [((dh, n), BF16)] + [hidden] * 4 + [own_hidden] * 3 + [((dh, n), F32)] + [(share, F32)] * 3,
+        [((dh, n), BF16)] + [hidden] * 4 + [own_hidden] * 3 + [((dh, n), F32)] + [(half, F32)] * 3,
         (*keys_values, out_grad, grad_other, gain),
         sums_scratch,
         "saved",
@@ -501,25 +518,25 @@
 
     fast, moved = [], []
     for k in range(3):
-        mine, other = half_sums(sums[k], sums[3 + k], chips)
+        totals = half_sums(sums[k], sums[3 + k], chips)
         rows, rows_moved = call(
             functools.partial(owner_forward_kernel, folds_by_matrix[k]),
-            [(share, BF16), (share, F32)],
-            (priors[k], mine, other),
+            [(half, BF16), (half, F32)],
+            (priors[k], *totals),
             name="owner_forward",
         )
         moved.append(rows_moved)
-        fast.append(from_inner(rows, chip, chips))
+        fast += from_owners(rows, chips)
     f1t, f3t, f2t, output, q_mixed, q_slope, q_silu, part = call(
         functools.partial(apply_kernel, chips, folds),
         matrices + [((dh, n), F32), ((fh, n), BF16), hidden, hidden, ((2, n), F32)],
-        (*(f[0] for f in fast), *(f[1] for f in fast), query_input, query_other, weighted),
+        (*fast, query_input, query_other, weighted),
         name="apply",
         flops=3 * product,
     )
     q_gate_back, q_up_back, *sums = call(
         functools.partial(back_kernel, chips, folds, heads),
-        [own_hidden] * 2 + share_sums,
+        [own_hidden] * 2 + half_shares,
         (
             *head_parts(part, heads),
             f2t, output, weighted, q_mixed, q_slope, q_silu, query_input, query_other,
@@ -538,20 +555,20 @@
 
     cotangent, owned = [], []
     for k in range(3):
-        mine, other = half_sums(sums[k], sums[3 + k], chips)
+        totals = half_sums(sums[k], sums[3 + k], chips)
         rows, rows_owned = call(
             functools.partial(owner_backward_kernel, folds_by_matrix[k]),
-            [(share, BF16), (share, F32)],
-            (priors[k], moved[k], mine, other),
+            [(half, BF16), (half, F32)],
+            (priors[k], moved[k], *totals),
             name="owner_backward",
         )
         owned.append(rows_owned)
-        cotangent.append(from_inner(rows, chip, chips))
+        cotangent += from_owners(rows, chips)
     c1t, c3t, c2t, dbb, upb, gpb, *pieces = call(
         functools.partial(second_kernel, chips, folds),
         matrices + [own_hidden] * 3 + [((3 * g, dh), F32)] + [((3 * g, dh), BF16)] * (chips - 1),
         (
-            *(c[0] for c in cotangent), *(c[1] for c in cotangent), *owned,
+            *cotangent,
             key_input, key_other, push, up_slope, silu, back_slope, back_curve,
         ),
         sums_scratch,
@@ -566,9 +583,9 @@
         flops=3 * product,
     )
     results = call(
-        functools.partial(owner_result_kernel, folds),
+        functools.partial(owner_result_kernel, chips, folds),
         [((g, dh), F32)] * 2 + [((d, fh), F32)],
-        exchange(pieces, chips),
+        (*owned, *exchange(pieces, chips)),
         name="owner_result",
     )
     return query_grad, key_grad, value_grad, *results

time: 95.3 us -> 76.4 us (0.80)
  waiting for transfers between devices: 37.6 us -> 22.8 us
  Pallas kernels: 13.1 us -> 9.76 us
  starting transfers between devices: 34.7 us -> 37.4 us
  local copies, waits for them, and re-layouts: 6.96 us -> 5.25 us
  other arithmetic: 1 us -> 0 us
    ppermute x24 -> x30, waiting for transfers between devices: 30.5 us -> 14.4 us  [the longest x18 11.9 us: to_chip(): return lax.ppermute(x, 'tok', chip_perm(chips * CORES, step))]
    pallas_call x20 -> x21, Pallas kernels: 13.1 us -> 9.76 us  [call(): pl.pallas_call(kernel, out_shape=[jax.ShapeDtypeStruct(s, t) for s, t in...]
    ppermute x24 -> x30, starting transfers between devices: 25.4 us -> 27.8 us  [the longest x18 26.6 us: to_chip(): return lax.ppermute(x, 'tok', chip_perm(chips * CORES, step))]
    unnamed x58 -> x22, local copies, waits for them, and re-layouts: 6.96 us -> 5.25 us
    ppermute x3, waiting for transfers between devices: 4.07 us -> 5.17 us  [exchange(): lax.ppermute(pieces[s], 'tok', chip_perm(count, s))]
    select_n x6 -> x0, other arithmetic: 1 us -> none  [from_inner(): x = jnp.where((chip == pairs[0][0]) | (chip == pairs[1][0]), got, x)]
  transfers between devices with their start and end apart: 35 -> 41, of which waited for: 19 -> 21; matrix products, arithmetic and copies ran while one was open for 2% -> 0% of each run, Pallas kernels for 9% -> 7%
where the time goes in v7:
time: 76.4 us; the launch traced here: 76 us
  starting transfers between devices  37.4 us (49%)
  waiting for transfers between devices  22.8 us (30%)
  Pallas kernels  9.76 us (13%)
  local copies, waits for them, and re-layouts  5.25 us (7%)
  between operations  0.86 us (1%)
    ppermute x18, starting transfers between devices, to_chip(): return lax.ppermute(x, 'tok', chip_perm(chips * CORES, step))  26.6 us
    ppermute x18, waiting for transfers between devices, to_chip(): return lax.ppermute(x, 'tok', chip_perm(chips * CORES, step))  11.9 us
    pallas_call x21, Pallas kernels, call(): pl.pallas_call(kernel, out_shape=[jax.ShapeDtypeStruct(s, t) for s, t in...  9.76 us
    unnamed x22, local copies, waits for them, and re-layouts  5.25 us
    ppermute x3, waiting for transfers between devices, exchange(): lax.ppermute(pieces[s], 'tok', chip_perm(count, s))  5.17 us
    ppermute x3, starting transfers between devices, exchange(): lax.ppermute(pieces[s], 'tok', chip_perm(count, s))  4.45 us
    ppermute x3, starting transfers between devices, head_parts(): lax.ppermute(part, 'head', [(h, partner(h, step, heads)) for h in range(h...  3.55 us
    ppermute x3, waiting for transfers between devices, head_parts(): lax.ppermute(part, 'head', [(h, partner(h, step, heads)) for h in range(h...  3.25 us
  transfers between devices with their start and end apart: 41, of which 21 were waited for; matrix products, arithmetic and copies ran while one was open for 0% of the time, Pallas kernels for 7%

profile of v7, /device:TPU:0, one launch (start us, length us, event | category | flops | bytes accessed | tf_op | source)
XLA Modules:
  0.0 76.0 jit_solution(9568231551357303493)
XLA Ops:
  1.8 0.9 %copy-done = bf16[1,256,512]{2,1,0:T(8,128)(2,1)S(1)} copy-done((bf16[1,256,512]{2,1,0:T(8,128)(2,1)S(1)}, bf16[1,256,512]{2,1,0:T(8,128)(2,1)}, u32[]{:S(2)}) %copy-start) | copy-done | bytes 262168
  2.7 0.9 %copy-done.3 = bf16[256,512]{1,0:T(8,128)(2,1)S(1)} copy-done((bf16[256,512]{1,0:T(8,128)(2,1)S(1)}, bf16[256,512]{1,0:T(8,128)(2,1)}, u32[]{:S(2)}) %copy-start.3) | copy-done | bytes 262168
  3.7 0.9 %copy-done.5 = bf16[256,512]{1,0:T(8,128)(2,1)S(1)} copy-done((bf16[256,512]{1,0:T(8,128)(2,1)S(1)}, bf16[256,512]{1,0:T(8,128)(2,1)}, u32[]{:S(2)}) %copy-start.5) | copy-done | bytes 262168
  4.6 0.9 %copy-done.9 = bf16[1,512,256]{2,1,0:T(8,128)(2,1)S(1)} copy-done((bf16[1,512,256]{2,1,0:T(8,128)(2,1)S(1)}, bf16[1,512,256]{2,1,0:T(8,128)(2,1)}, u32[]{:S(2)}) %copy-start.9) | copy-done | bytes 262168
  5.6 0.9 %copy-done.10 = bf16[1,512,256]{2,1,0:T(8,128)(2,1)S(1)} copy-done((bf16[1,512,256]{2,1,0:T(8,128)(2,1)S(1)}, bf16[1,512,256]{2,1,0:T(8,128)(2,1)}, u32[]{:S(2)}) %copy-start.10) | copy-done | bytes 262168
  6.5 0.7 own_tokens.1
  7.5 0.7 update.1
  8.9 2.6 %collective-permute-start.14 = (bf16[64,512]{1,0:T(8,128)(2,1)S(1)}, bf16[64,512]{1,0:T(8,128)(2,1)S(1)}, u32[]{:S(2)}, u32[]{:S(2)}) collective-permute-start(bf16[64,512]{1,0:T(8,128)(2,1)S(1)} %get-tuple-element.102), channel_id=1, source_target_pairs={{0,2},{1,3},{2,0},{3,1},{4,6},{5,7},{6,4},{7,5},{8,10},{9,11},{10,... | collective-permute-start | bytes 196616 | tf_op jit(solution)/shard_map/ppermute | solution.py:373
  11.6 2.0 %collective-permute-start.4 = (bf16[64,512]{1,0:T(8,128)(2,1)S(1)}, bf16[64,512]{1,0:T(8,128)(2,1)S(1)}, u32[]{:S(2)}, u32[]{:S(2)}) collective-permute-start(bf16[64,512]{1,0:T(8,128)(2,1)S(1)} %get-tuple-element.94), channel_id=1, source_target_pairs={{0,2},{1,3},{2,0},{3,1},{4,6},{5,7},{6,4},{7,5},{8,10},{9,11},{10,... | collective-permute-start | bytes 196616 | tf_op jit(solution)/shard_map/ppermute | solution.py:373
  13.6 0.7 collective-permute-done.14.got
  14.3 3.0 %collective-permute-start.15 = (bf16[64,512]{1,0:T(8,128)(2,1)S(1)}, bf16[64,512]{1,0:T(8,128)(2,1)S(1)}, u32[]{:S(2)}, u32[]{:S(2)}) collective-permute-start(bf16[64,512]{1,0:T(8,128)(2,1)S(1)} %carry.8.refs_0_), channel_id=1, source_target_pairs={{0,4},{1,5},{2,6},{3,7},{4,0},{5,1},{6,2},{7,3},{8,12},{9,13},{10,... | collective-permute-start | bytes 196616 | tf_op jit(solution)/shard_map/ppermute | solution.py:373
  17.3 1.9 %collective-permute-start.10 = (bf16[64,512]{1,0:T(8,128)(2,1)S(1)}, bf16[64,512]{1,0:T(8,128)(2,1)S(1)}, u32[]{:S(2)}, u32[]{:S(2)}) collective-permute-start(bf16[64,512]{1,0:T(8,128)(2,1)S(1)} %carry.7.refs_0_), channel_id=1, source_target_pairs={{0,4},{1,5},{2,6},{3,7},{4,0},{5,1},{6,2},{7,3},{8,12},{9,13},{10,... | collective-permute-start | bytes 196616 | tf_op jit(solution)/shard_map/ppermute | solution.py:373
  19.2 1.2 %collective-permute-start.5 = (bf16[64,512]{1,0:T(8,128)(2,1)S(1)}, bf16[64,512]{1,0:T(8,128)(2,1)S(1)}, u32[]{:S(2)}, u32[]{:S(2)}) collective-permute-start(bf16[64,512]{1,0:T(8,128)(2,1)S(1)} %carry.6.refs_0_), channel_id=1, source_target_pairs={{0,4},{1,5},{2,6},{3,7},{4,0},{5,1},{6,2},{7,3},{8,12},{9,13},{10,... | collective-permute-start | bytes 196616 | tf_op jit(solution)/shard_map/ppermute | solution.py:373
  20.4 1.1 %saved.1 = (bf16[512,512]{1,0:T(8,128)(2,1)S(1)}, f32[256,512]{1,0:T(8,128)S(1)}, f32[256,512]{1,0:T(8,128)S(1)}, f32[256,512]{1,0:T(8,128)S(1)}, f32[256,512]{1...) custom-call(bf16[256,512]{1,0:T(8,128)(2,1)S(1)} %copy-done.4, ...), custom_call_target="tpu_custom_call" | custom-call | flops 402653184 | bytes 2363392 | tf_op jit(solution)/shard_map/saved/pallas_call | solution.py:350
  21.8 2.9 %collective-permute-start.16 = (bf16[64,512]{1,0:T(8,128)(2,1)S(1)}, bf16[64,512]{1,0:T(8,128)(2,1)S(1)}, u32[]{:S(2)}, u32[]{:S(2)}) collective-permute-start(bf16[64,512]{1,0:T(8,128)(2,1)S(1)} %get-tuple-element.103.refs_8_), channel_id=1, source_target_pairs={{0,2},{1,3},{2,0},{3,1},{4,6},{5,7},{6,4},{7,5},{8,10},{9,11},{10,... | collective-permute-start | bytes 196616 | tf_op jit(solution)/shard_map/ppermute | solution.py:373
  24.7 0.7 collective-permute-done.10.refs_1_
  25.5 0.6 collective-permute-start.11
  26.7 1.1 %collective-permute-start.6 = (bf16[64,512]{1,0:T(8,128)(2,1)S(1)}, bf16[64,512]{1,0:T(8,128)(2,1)S(1)}, u32[]{:S(2)}, u32[]{:S(2)}) collective-permute-start(bf16[64,512]{1,0:T(8,128)(2,1)S(1)} %get-tuple-element.95.refs_0_), channel_id=1, source_target_pairs={{0,2},{1,3},{2,0},{3,1},{4,6},{5,7},{6,4},{7,5},{8,10},{9,11},{10,... | collective-permute-start | bytes 196616 | tf_op jit(solution)/shard_map/ppermute | solution.py:373
  28.4 2.1 %collective-permute-done.11.refs_5_ = bf16[64,512]{1,0:T(8,128)(2,1)S(1)} collective-permute-done((bf16[64,512]{1,0:T(8,128)(2,1)S(1)}, bf16[64,512]{1,0:T(8,128)(2,1)S(1)}, u32[]{:S(2)}, u32[]{:S(2)}) %collective-permute-start.11) | collective-permute-done | bytes 65568 | tf_op jit(solution)/shard_map/ppermute | solution.py:373
  30.5 0.7 collective-permute-done.6.refs_1_
  31.8 0.7 collective-permute-done.8.refs_3_
  32.5 0.8 %apply.1 = (bf16[256,512]{1,0:T(8,128)(2,1)S(1)}, bf16[256,512]{1,0:T(8,128)(2,1)S(1)}, bf16[512,256]{1,0:T(8,128)(2,1)S(1)}, f32[512,512]{1,0:T(8,128)S(1)}, bf...) custom-call(bf16[64,512]{1,0:T(8,128)(2,1)S(1)} %get-tuple-element.95.refs_0, ...), custom_call_target="tpu_custom_call" | custom-call | flops 402653184 | bytes 2359296 | tf_op jit(solution)/shard_map/apply/pallas_call | solution.py:350
  33.3 2.7 %collective-permute-start.22 = (f32[2,512]{1,0:T(2,128)S(1)}, f32[2,512]{1,0:T(2,128)S(1)}, u32[]{:S(2)}, u32[]{:S(2)}) collective-permute-start(f32[2,512]{1,0:T(2,128)S(1)} %get-tuple-element.106.refs_0_), channel_id=1, source_target_pairs={{0,24},{8,16},{16,8},{24,0},{1,25},{9,17},{17,9},{25,1},{2,26},{10... | collective-permute-start | bytes 12296 | tf_op jit(solution)/shard_map/ppermute | solution.py:389
  36.9 1.0 %collective-permute-done.22.refs_3_ = f32[2,512]{1,0:T(2,128)S(1)} collective-permute-done((f32[2,512]{1,0:T(2,128)S(1)}, f32[2,512]{1,0:T(2,128)S(1)}, u32[]{:S(2)}, u32[]{:S(2)}) %collective-permute-start.22) | collective-permute-done | bytes 4128 | tf_op jit(solution)/shard_map/ppermute | solution.py:389
  37.9 1.7 %collective-permute-done.21.refs_2_ = f32[2,512]{1,0:T(2,128)S(1)} collective-permute-done((f32[2,512]{1,0:T(2,128)S(1)}, f32[2,512]{1,0:T(2,128)S(1)}, u32[]{:S(2)}, u32[]{:S(2)}) %collective-permute-start.21) | collective-permute-done | bytes 4128 | tf_op jit(solution)/shard_map/ppermute | solution.py:389
  40.1 0.9 %apply_back.1 = (bf16[256,256]{1,0:T(8,128)(2,1)S(1)}, bf16[256,256]{1,0:T(8,128)(2,1)S(1)}, f32[64,512]{1,0:T(8,128)S(1)}, f32[64,512]{1,0:T(8,128)S(1)}, f32[6...) custom-call(f32[2,512]{1,0:T(2,128)S(1)} %get-tuple-element.106.refs_, ...), custom_call_target="tpu_custom_call" | custom-call | flops 536870912 | bytes 4210688 | tf_op jit(solution)/shard_map/apply_back/pallas_call | solution.py:350
  41.0 0.9 %collective-permute-start.23 = (bf16[64,512]{1,0:T(8,128)(2,1)S(1)}, bf16[64,512]{1,0:T(8,128)(2,1)S(1)}, u32[]{:S(2)}, u32[]{:S(2)}) collective-permute-start(bf16[64,512]{1,0:T(8,128)(2,1)S(1)} %get-tuple-element.119), channel_id=1, source_target_pairs={{0,2},{1,3},{2,0},{3,1},{4,6},{5,7},{6,4},{7,5},{8,10},{9,11},{10,... | collective-permute-start | bytes 196616 | tf_op jit(solution)/shard_map/ppermute | solution.py:373
  41.9 1.2 %collective-permute-start.28 = (bf16[64,512]{1,0:T(8,128)(2,1)S(1)}, bf16[64,512]{1,0:T(8,128)(2,1)S(1)}, u32[]{:S(2)}, u32[]{:S(2)}) collective-permute-start(bf16[64,512]{1,0:T(8,128)(2,1)S(1)} %get-tuple-element.123), channel_id=1, source_target_pairs={{0,2},{1,3},{2,0},{3,1},{4,6},{5,7},{6,4},{7,5},{8,10},{9,11},{10,... | collective-permute-start | bytes 196616 | tf_op jit(solution)/shard_map/ppermute | solution.py:373
  43.1 0.8 %collective-permute-start.33 = (bf16[64,512]{1,0:T(8,128)(2,1)S(1)}, bf16[64,512]{1,0:T(8,128)(2,1)S(1)}, u32[]{:S(2)}, u32[]{:S(2)}) collective-permute-start(bf16[64,512]{1,0:T(8,128)(2,1)S(1)} %get-tuple-element.127), channel_id=1, source_target_pairs={{0,2},{1,3},{2,0},{3,1},{4,6},{5,7},{6,4},{7,5},{8,10},{9,11},{10,... | collective-permute-start | bytes 196616 | tf_op jit(solution)/shard_map/ppermute | solution.py:373
  43.9 1.4 %collective-permute-done.23.got = bf16[64,512]{1,0:T(8,128)(2,1)S(1)} collective-permute-done((bf16[64,512]{1,0:T(8,128)(2,1)S(1)}, bf16[64,512]{1,0:T(8,128)(2,1)S(1)}, u32[]{:S(2)}, u32[]{:S(2)}) %collective-permute-start.23) | collective-permute-done | bytes 65568 | tf_op jit(solution)/shard_map/ppermute | solution.py:373
  45.4 3.1 %collective-permute-start.24 = (bf16[64,512]{1,0:T(8,128)(2,1)S(1)}, bf16[64,512]{1,0:T(8,128)(2,1)S(1)}, u32[]{:S(2)}, u32[]{:S(2)}) collective-permute-start(bf16[64,512]{1,0:T(8,128)(2,1)S(1)} %carry.9.refs_0_), channel_id=1, source_target_pairs={{0,4},{1,5},{2,6},{3,7},{4,0},{5,1},{6,2},{7,3},{8,12},{9,13},{10,... | collective-permute-start | bytes 196616 | tf_op jit(solution)/shard_map/ppermute | solution.py:373
  48.5 1.0 %collective-permute-start.29 = (bf16[64,512]{1,0:T(8,128)(2,1)S(1)}, bf16[64,512]{1,0:T(8,128)(2,1)S(1)}, u32[]{:S(2)}, u32[]{:S(2)}) collective-permute-start(bf16[64,512]{1,0:T(8,128)(2,1)S(1)} %carry.10.refs_0_), channel_id=1, source_target_pairs={{0,4},{1,5},{2,6},{3,7},{4,0},{5,1},{6,2},{7,3},{8,12},{9,13},{10,... | collective-permute-start | bytes 196616 | tf_op jit(solution)/shard_map/ppermute | solution.py:373
  49.5 2.0 %collective-permute-start.34 = (bf16[64,512]{1,0:T(8,128)(2,1)S(1)}, bf16[64,512]{1,0:T(8,128)(2,1)S(1)}, u32[]{:S(2)}, u32[]{:S(2)}) collective-permute-start(bf16[64,512]{1,0:T(8,128)(2,1)S(1)} %carry.11.refs_0_), channel_id=1, source_target_pairs={{0,4},{1,5},{2,6},{3,7},{4,0},{5,1},{6,2},{7,3},{8,12},{9,13},{10,... | collective-permute-start | bytes 196616 | tf_op jit(solution)/shard_map/ppermute | solution.py:373
  51.5 1.5 %collective-permute-done.24.refs_1_ = bf16[64,512]{1,0:T(8,128)(2,1)S(1)} collective-permute-done((bf16[64,512]{1,0:T(8,128)(2,1)S(1)}, bf16[64,512]{1,0:T(8,128)(2,1)S(1)}, u32[]{:S(2)}, u32[]{:S(2)}) %collective-permute-start.24) | collective-permute-done | bytes 65568 | tf_op jit(solution)/shard_map/ppermute | solution.py:373
  53.5 1.6 %collective-permute-done.29.refs_1_ = bf16[64,512]{1,0:T(8,128)(2,1)S(1)} collective-permute-done((bf16[64,512]{1,0:T(8,128)(2,1)S(1)}, bf16[64,512]{1,0:T(8,128)(2,1)S(1)}, u32[]{:S(2)}, u32[]{:S(2)}) %collective-permute-start.29) | collective-permute-done | bytes 65568 | tf_op jit(solution)/shard_map/ppermute | solution.py:373
  56.0 1.6 %collective-permute-start.35 = (bf16[64,512]{1,0:T(8,128)(2,1)S(1)}, bf16[64,512]{1,0:T(8,128)(2,1)S(1)}, u32[]{:S(2)}, u32[]{:S(2)}) collective-permute-start(bf16[64,512]{1,0:T(8,128)(2,1)S(1)} %get-tuple-element.128.refs_8_), channel_id=1, source_target_pairs={{0,2},{1,3},{2,0},{3,1},{4,6},{5,7},{6,4},{7,5},{8,10},{9,11},{10,... | collective-permute-start | bytes 196616 | tf_op jit(solution)/shard_map/ppermute | solution.py:373
  58.2 1.6 %collective-permute-done.30.refs_5_ = bf16[64,512]{1,0:T(8,128)(2,1)S(1)} collective-permute-done((bf16[64,512]{1,0:T(8,128)(2,1)S(1)}, bf16[64,512]{1,0:T(8,128)(2,1)S(1)}, u32[]{:S(2)}, u32[]{:S(2)}) %collective-permute-start.30) | collective-permute-done | bytes 65568 | tf_op jit(solution)/shard_map/ppermute | solution.py:373
  59.9 0.7 collective-permute-done.35.refs_9_
  60.6 0.5 collective-permute-done.32.refs_7_
  61.1 0.7 collective-permute-done.37.refs_11_
  61.8 1.5 %second_adjoint.1 = (bf16[256,512]{1,0:T(8,128)(2,1)S(1)}, bf16[256,512]{1,0:T(8,128)(2,1)S(1)}, bf16[512,256]{1,0:T(8,128)(2,1)S(1)}, bf16[256,256]{1,0:T(8,128...) custom-call(bf16[64,512]{1,0:T(8,128)(2,1)S(1)} %get-tuple-element.1, ...), custom_call_target="tpu_custom_call" | custom-call | flops 805306368 | bytes 3932160 | tf_op jit(solution)/shard_map/second_adjoint/pallas_call | solution.py:350
  63.3 3.0 %collective-permute-start.38 = (bf16[96,512]{1,0:T(8,128)(2,1)S(1)}, bf16[96,512]{1,0:T(8,128)(2,1)S(1)}, u32[]{:S(2)}, u32[]{:S(2)}) collective-permute-start(bf16[96,512]{1,0:T(8,128)(2,1)S(1)} %get-tuple-element.148), channel_id=1, source_target_pairs={{0,6},{1,7},{2,4},{3,5},{4,2},{5,3},{6,0},{7,1},{8,14},{9,15},{10,... | collective-permute-start | bytes 294920 | tf_op jit(solution)/shard_map/ppermute | solution.py:368
  66.3 1.4 %collective-permute-start.40 = (bf16[96,512]{1,0:T(8,128)(2,1)S(1)}, bf16[96,512]{1,0:T(8,128)(2,1)S(1)}, u32[]{:S(2)}, u32[]{:S(2)}) collective-permute-start(bf16[96,512]{1,0:T(8,128)(2,1)S(1)} %get-tuple-element.150), channel_id=1, source_target_pairs={{0,2},{1,3},{2,0},{3,1},{4,6},{5,7},{6,4},{7,5},{8,10},{9,11},{10,... | collective-permute-start | bytes 294920 | tf_op jit(solution)/shard_map/ppermute | solution.py:368
  67.8 1.0 %query_grad.1 = bf16[256,512]{1,0:T(8,128)(2,1)} custom-call(bf16[256,256]{1,0:T(8,128)(2,1)S(1)} %get-tuple-element.112.gate_back, bf16[256,256]{1,0:T(8,128)(2,1)S(1)} %get-tuple-element.113.up_back, bf16[256,512]{1,0:T(8,128)(2,1)S(1)} %get-tuple-element.114.f1t, bf16[256,512]{1,0:T(8,128)(2,1)S(1)} %get-tuple-element.115.f3t), custom_call_target="tpu_custom_call" | custom-call | flops 134217728 | bytes 786432 | tf_op jit(solution)/shard_map/query_grad/pallas_call | solution.py:350
  68.8 1.4 %token_grads.1 = (bf16[256,512]{1,0:T(8,128)(2,1)}, bf16[256,512]{1,0:T(8,128)(2,1)}) custom-call(f32[1,256]{1,0:T(1,128)S(1)} %bitcast.21, bf16[256,256]{1,0:T(8,128)(2,1)S(1)} %get-tuple-element.116.refs_1_, bf16[256,256]{1,0:T(8,128)(2,1)S(1)} %get-tuple-element.134.refs_2_, bf16[256,256]{1,0:T(8,128)(2,1)S(1)} %get-tuple-element.135.refs_3_, ...), custom_call_target="tpu_custom_call" | custom-call | flops 402653184 | bytes 2360320 | tf_op jit(solution)/shard_map/token_grads/pallas_call | solution.py:350
  70.1 0.8 collective-permute-done.38.refs_4_
  70.9 4.4 %collective-permute-done.39.refs_5_ = bf16[96,512]{1,0:T(8,128)(2,1)S(1)} collective-permute-done((bf16[96,512]{1,0:T(8,128)(2,1)S(1)}, bf16[96,512]{1,0:T(8,128)(2,1)S(1)}, u32[]{:S(2)}, u32[]{:S(2)}) %collective-permute-start.39) | collective-permute-done | bytes 98336 | tf_op jit(solution)/shard_map/ppermute | solution.py:368
  75.3 0.7 owner_result.1
  (77 shorter events, 7.6 us)
Async XLA Ops:
  0.6 6.6 %collective-permute-start.1 = (bf16[256,512]{1,0:T(8,128)(2,1)}, bf16[256,512]{1,0:T(8,128)(2,1)S(1)}, u32[]{:S(2)}, u32[]{:S(2)}) collective-permute-start(bf16[256,512]{1,0:T(8,128)(2,1)} %vo.1), channel_id=1, source_target_pairs={{0,1},{1,0},{2,3},{3,2},{4,5},{5,4},{6,7},{7,6},{8,9},{9,8},{10,11... | collective-permute-start | bytes 786440 | tf_op jit(solution)/shard_map/ppermute | solution.py:486
  1.2 6.1 %collective-permute-start = (bf16[256,512]{1,0:T(8,128)(2,1)}, bf16[256,512]{1,0:T(8,128)(2,1)S(1)}, u32[]{:S(2)}, u32[]{:S(2)}) collective-permute-start(bf16[256,512]{1,0:T(8,128)(2,1)} %refs_12_.3), channel_id=1, source_target_pairs={{0,1},{1,0},{2,3},{3,2},{4,5},{5,4},{6,7},{7,6},{8,9},{9,8},{10,11... | collective-permute-start | bytes 786440 | tf_op jit(solution)/shard_map/ppermute | solution.py:486
  1.3 6.0 %collective-permute-start.2 = (f32[1,256]{1,0:T(1,128)S(1)}, f32[1,256]{1,0:T(1,128)S(1)}, u32[]{:S(2)}, u32[]{:S(2)}) collective-permute-start(f32[1,256]{1,0:T(1,128)S(1)} %bitcast.18), channel_id=1, source_target_pairs={{0,1},{1,0},{2,3},{3,2},{4,5},{5,4},{6,7},{7,6},{8,9},{9,8},{10,11... | collective-permute-start | bytes 3080 | tf_op jit(solution)/shard_map/ppermute | solution.py:486
  1.8 0.9 %copy-start = (bf16[1,256,512]{2,1,0:T(8,128)(2,1)S(1)}, bf16[1,256,512]{2,1,0:T(8,128)(2,1)}, u32[]{:S(2)}) copy-start(bf16[1,256,512]{2,1,0:T(8,128)(2,1)} %param.17) | copy-start | bytes 786436
  2.7 0.9 %copy-start.3 = (bf16[256,512]{1,0:T(8,128)(2,1)S(1)}, bf16[256,512]{1,0:T(8,128)(2,1)}, u32[]{:S(2)}) copy-start(bf16[256,512]{1,0:T(8,128)(2,1)} %refs_12_.3) | copy-start | bytes 786436
  3.7 0.9 %copy-start.5 = (bf16[256,512]{1,0:T(8,128)(2,1)S(1)}, bf16[256,512]{1,0:T(8,128)(2,1)}, u32[]{:S(2)}) copy-start(bf16[256,512]{1,0:T(8,128)(2,1)} %vo.1) | copy-start | bytes 786436
  4.6 0.9 %copy-start.9 = (bf16[1,512,256]{2,1,0:T(8,128)(2,1)S(1)}, bf16[1,512,256]{2,1,0:T(8,128)(2,1)}, u32[]{:S(2)}) copy-start(bf16[1,512,256]{2,1,0:T(8,128)(2,1)} %param.15) | copy-start | bytes 786436
  7.5 1.0 %copy-start.2 = (bf16[256,512]{1,0:T(8,128)(2,1)S(1)}, bf16[256,512]{1,0:T(8,128)(2,1)}, u32[]{:S(2)}) copy-start(bf16[256,512]{1,0:T(8,128)(2,1)} %refs_10_.1) | copy-start | bytes 786436
  8.4 12.0 %collective-permute-start.3 = (bf16[256,512]{1,0:T(8,128)(2,1)S(1)}, bf16[256,512]{1,0:T(8,128)(2,1)S(1)}, u32[]{:S(2)}, u32[]{:S(2)}) collective-permute-start(bf16[256,512]{1,0:T(8,128)(2,1)S(1)} %copy-done.6), channel_id=1, source_target_pairs={{0,1},{1,0},{2,3},{3,2},{4,5},{5,4},{6,7},{7,6},{8,9},{9,8},{10,11... | collective-permute-start | bytes 786440 | tf_op jit(solution)/shard_map/ppermute | solution.py:486
  8.5 19.3 %collective-permute-start.19 = (bf16[256,512]{1,0:T(8,128)(2,1)S(1)}, bf16[256,512]{1,0:T(8,128)(2,1)S(1)}, u32[]{:S(2)}, u32[]{:S(2)}) collective-permute-start(bf16[256,512]{1,0:T(8,128)(2,1)S(1)} %copy-done.2), channel_id=1, source_target_pairs={{0,1},{1,0},{2,3},{3,2},{4,5},{5,4},{6,7},{7,6},{8,9},{9,8},{10,11... | collective-permute-start | bytes 786440 | tf_op jit(solution)/shard_map/ppermute | solution.py:486
  8.9 5.3 %collective-permute-start.14 = (bf16[64,512]{1,0:T(8,128)(2,1)S(1)}, bf16[64,512]{1,0:T(8,128)(2,1)S(1)}, u32[]{:S(2)}, u32[]{:S(2)}) collective-permute-start(bf16[64,512]{1,0:T(8,128)(2,1)S(1)} %get-tuple-element.102), channel_id=1, source_target_pairs={{0,2},{1,3},{2,0},{3,1},{4,6},{5,7},{6,4},{7,5},{8,10},{9,11},{10,... | collective-permute-start | bytes 196616 | tf_op jit(solution)/shard_map/ppermute | solution.py:373
  11.6 5.7 %collective-permute-start.9 = (bf16[64,512]{1,0:T(8,128)(2,1)S(1)}, bf16[64,512]{1,0:T(8,128)(2,1)S(1)}, u32[]{:S(2)}, u32[]{:S(2)}) collective-permute-start(bf16[64,512]{1,0:T(8,128)(2,1)S(1)} %get-tuple-element.98), channel_id=1, source_target_pairs={{0,2},{1,3},{2,0},{3,1},{4,6},{5,7},{6,4},{7,5},{8,10},{9,11},{10,... | collective-permute-start | bytes 196616 | tf_op jit(solution)/shard_map/ppermute | solution.py:373
  11.6 7.6 %collective-permute-start.4 = (bf16[64,512]{1,0:T(8,128)(2,1)S(1)}, bf16[64,512]{1,0:T(8,128)(2,1)S(1)}, u32[]{:S(2)}, u32[]{:S(2)}) collective-permute-start(bf16[64,512]{1,0:T(8,128)(2,1)S(1)} %get-tuple-element.94), channel_id=1, source_target_pairs={{0,2},{1,3},{2,0},{3,1},{4,6},{5,7},{6,4},{7,5},{8,10},{9,11},{10,... | collective-permute-start | bytes 196616 | tf_op jit(solution)/shard_map/ppermute | solution.py:373
  14.3 6.2 %copy-start.4 = (bf16[256,512]{1,0:T(8,128)(2,1)S(1)}, bf16[256,512]{1,0:T(8,128)(2,1)}, u32[]{:S(2)}) copy-start(bf16[256,512]{1,0:T(8,128)(2,1)} %refs_12_.3) | copy-start | bytes 786436
  14.3 7.2 %collective-permute-start.15 = (bf16[64,512]{1,0:T(8,128)(2,1)S(1)}, bf16[64,512]{1,0:T(8,128)(2,1)S(1)}, u32[]{:S(2)}, u32[]{:S(2)}) collective-permute-start(bf16[64,512]{1,0:T(8,128)(2,1)S(1)} %carry.8.refs_0_), channel_id=1, source_target_pairs={{0,4},{1,5},{2,6},{3,7},{4,0},{5,1},{6,2},{7,3},{8,12},{9,13},{10,... | collective-permute-start | bytes 196616 | tf_op jit(solution)/shard_map/ppermute | solution.py:373
  17.3 8.1 %collective-permute-start.10 = (bf16[64,512]{1,0:T(8,128)(2,1)S(1)}, bf16[64,512]{1,0:T(8,128)(2,1)S(1)}, u32[]{:S(2)}, u32[]{:S(2)}) collective-permute-start(bf16[64,512]{1,0:T(8,128)(2,1)S(1)} %carry.7.refs_0_), channel_id=1, source_target_pairs={{0,4},{1,5},{2,6},{3,7},{4,0},{5,1},{6,2},{7,3},{8,12},{9,13},{10,... | collective-permute-start | bytes 196616 | tf_op jit(solution)/shard_map/ppermute | solution.py:373
  19.2 1.2 %copy-start.8 = (f32[512]{0:T(512)S(1)}, f32[512]{0:T(512)}, u32[]{:S(2)}) copy-start(f32[512]{0:T(512)} %param.14) | copy-start | bytes 6148
  19.2 7.4 %collective-permute-start.5 = (bf16[64,512]{1,0:T(8,128)(2,1)S(1)}, bf16[64,512]{1,0:T(8,128)(2,1)S(1)}, u32[]{:S(2)}, u32[]{:S(2)}) collective-permute-start(bf16[64,512]{1,0:T(8,128)(2,1)S(1)} %carry.6.refs_0_), channel_id=1, source_target_pairs={{0,4},{1,5},{2,6},{3,7},{4,0},{5,1},{6,2},{7,3},{8,12},{9,13},{10,... | collective-permute-start | bytes 196616 | tf_op jit(solution)/shard_map/ppermute | solution.py:373
  21.7 6.1 %collective-permute-start.17 = (bf16[64,512]{1,0:T(8,128)(2,1)S(1)}, bf16[64,512]{1,0:T(8,128)(2,1)S(1)}, u32[]{:S(2)}, u32[]{:S(2)}) collective-permute-start(bf16[64,512]{1,0:T(8,128)(2,1)S(1)} %get-tuple-element.103.refs_8_), channel_id=1, source_target_pairs={{0,1},{1,0},{2,3},{3,2},{4,5},{5,4},{6,7},{7,6},{8,9},{9,8},{10,11... | collective-permute-start | bytes 196616 | tf_op jit(solution)/shard_map/ppermute | solution.py:384
  21.8 6.6 %collective-permute-start.16 = (bf16[64,512]{1,0:T(8,128)(2,1)S(1)}, bf16[64,512]{1,0:T(8,128)(2,1)S(1)}, u32[]{:S(2)}, u32[]{:S(2)}) collective-permute-start(bf16[64,512]{1,0:T(8,128)(2,1)S(1)} %get-tuple-element.103.refs_8_), channel_id=1, source_target_pairs={{0,2},{1,3},{2,0},{3,1},{4,6},{5,7},{6,4},{7,5},{8,10},{9,11},{10,... | collective-permute-start | bytes 196616 | tf_op jit(solution)/shard_map/ppermute | solution.py:373
  25.5 5.0 %collective-permute-start.11 = (bf16[64,512]{1,0:T(8,128)(2,1)S(1)}, bf16[64,512]{1,0:T(8,128)(2,1)S(1)}, u32[]{:S(2)}, u32[]{:S(2)}) collective-permute-start(bf16[64,512]{1,0:T(8,128)(2,1)S(1)} %get-tuple-element.99.refs_4_), channel_id=1, source_target_pairs={{0,2},{1,3},{2,0},{3,1},{4,6},{5,7},{6,4},{7,5},{8,10},{9,11},{10,... | collective-permute-start | bytes 196616 | tf_op jit(solution)/shard_map/ppermute | solution.py:373
  26.7 4.5 %collective-permute-start.6 = (bf16[64,512]{1,0:T(8,128)(2,1)S(1)}, bf16[64,512]{1,0:T(8,128)(2,1)S(1)}, u32[]{:S(2)}, u32[]{:S(2)}) collective-permute-start(bf16[64,512]{1,0:T(8,128)(2,1)S(1)} %get-tuple-element.95.refs_0_), channel_id=1, source_target_pairs={{0,2},{1,3},{2,0},{3,1},{4,6},{5,7},{6,4},{7,5},{8,10},{9,11},{10,... | collective-permute-start | bytes 196616 | tf_op jit(solution)/shard_map/ppermute | solution.py:373
  27.8 3.4 %collective-permute-start.12 = (bf16[64,512]{1,0:T(8,128)(2,1)S(1)}, bf16[64,512]{1,0:T(8,128)(2,1)S(1)}, u32[]{:S(2)}, u32[]{:S(2)}) collective-permute-start(bf16[64,512]{1,0:T(8,128)(2,1)S(1)} %get-tuple-element.99.refs_4_), channel_id=1, source_target_pairs={{0,1},{1,0},{2,3},{3,2},{4,5},{5,4},{6,7},{7,6},{8,9},{9,8},{10,11... | collective-permute-start | bytes 196616 | tf_op jit(solution)/shard_map/ppermute | solution.py:384
  27.8 3.4 %collective-permute-start.7 = (bf16[64,512]{1,0:T(8,128)(2,1)S(1)}, bf16[64,512]{1,0:T(8,128)(2,1)S(1)}, u32[]{:S(2)}, u32[]{:S(2)}) collective-permute-start(bf16[64,512]{1,0:T(8,128)(2,1)S(1)} %get-tuple-element.95.refs_0_), channel_id=1, source_target_pairs={{0,1},{1,0},{2,3},{3,2},{4,5},{5,4},{6,7},{7,6},{8,9},{9,8},{10,11... | collective-permute-start | bytes 196616 | tf_op jit(solution)/shard_map/ppermute | solution.py:384
  28.3 2.9 %collective-permute-start.18 = (bf16[64,512]{1,0:T(8,128)(2,1)S(1)}, bf16[64,512]{1,0:T(8,128)(2,1)S(1)}, u32[]{:S(2)}, u32[]{:S(2)}) collective-permute-start(bf16[64,512]{1,0:T(8,128)(2,1)S(1)} %collective-permute-done.16.refs_9_), channel_id=1, source_target_pairs={{0,1},{1,0},{2,3},{3,2},{4,5},{5,4},{6,7},{7,6},{8,9},{9,8},{10,11... | collective-permute-start | bytes 196616 | tf_op jit(solution)/shard_map/ppermute | solution.py:384
  30.5 1.3 %collective-permute-start.13 = (bf16[64,512]{1,0:T(8,128)(2,1)S(1)}, bf16[64,512]{1,0:T(8,128)(2,1)S(1)}, u32[]{:S(2)}, u32[]{:S(2)}) collective-permute-start(bf16[64,512]{1,0:T(8,128)(2,1)S(1)} %collective-permute-done.11.refs_5_), channel_id=1, source_target_pairs={{0,1},{1,0},{2,3},{3,2},{4,5},{5,4},{6,7},{7,6},{8,9},{9,8},{10,11... | collective-permute-start | bytes 196616 | tf_op jit(solution)/shard_map/ppermute | solution.py:384
  31.3 1.3 %collective-permute-start.8 = (bf16[64,512]{1,0:T(8,128)(2,1)S(1)}, bf16[64,512]{1,0:T(8,128)(2,1)S(1)}, u32[]{:S(2)}, u32[]{:S(2)}) collective-permute-start(bf16[64,512]{1,0:T(8,128)(2,1)S(1)} %collective-permute-done.6.refs_1_), channel_id=1, source_target_pairs={{0,1},{1,0},{2,3},{3,2},{4,5},{5,4},{6,7},{7,6},{8,9},{9,8},{10,11... | collective-permute-start | bytes 196616 | tf_op jit(solution)/shard_map/ppermute | solution.py:384
  33.3 4.6 %collective-permute-start.22 = (f32[2,512]{1,0:T(2,128)S(1)}, f32[2,512]{1,0:T(2,128)S(1)}, u32[]{:S(2)}, u32[]{:S(2)}) collective-permute-start(f32[2,512]{1,0:T(2,128)S(1)} %get-tuple-element.106.refs_0_), channel_id=1, source_target_pairs={{0,24},{8,16},{16,8},{24,0},{1,25},{9,17},{17,9},{25,1},{2,26},{10... | collective-permute-start | bytes 12296 | tf_op jit(solution)/shard_map/ppermute | solution.py:389
  36.0 3.6 %collective-permute-start.21 = (f32[2,512]{1,0:T(2,128)S(1)}, f32[2,512]{1,0:T(2,128)S(1)}, u32[]{:S(2)}, u32[]{:S(2)}) collective-permute-start(f32[2,512]{1,0:T(2,128)S(1)} %get-tuple-element.106.refs_0_), channel_id=1, source_target_pairs={{0,16},{8,24},{16,0},{24,8},{1,17},{9,25},{17,1},{25,9},{2,18},{10... | collective-permute-start | bytes 12296 | tf_op jit(solution)/shard_map/ppermute | solution.py:389
  36.5 3.6 %collective-permute-start.20 = (f32[2,512]{1,0:T(2,128)S(1)}, f32[2,512]{1,0:T(2,128)S(1)}, u32[]{:S(2)}, u32[]{:S(2)}) collective-permute-start(f32[2,512]{1,0:T(2,128)S(1)} %get-tuple-element.106.refs_0_), channel_id=1, source_target_pairs={{0,8},{8,0},{16,24},{24,16},{1,9},{9,1},{17,25},{25,17},{2,10},{10... | collective-permute-start | bytes 12296 | tf_op jit(solution)/shard_map/ppermute | solution.py:389
  41.0 4.3 %collective-permute-start.23 = (bf16[64,512]{1,0:T(8,128)(2,1)S(1)}, bf16[64,512]{1,0:T(8,128)(2,1)S(1)}, u32[]{:S(2)}, u32[]{:S(2)}) collective-permute-start(bf16[64,512]{1,0:T(8,128)(2,1)S(1)} %get-tuple-element.119), channel_id=1, source_target_pairs={{0,2},{1,3},{2,0},{3,1},{4,6},{5,7},{6,4},{7,5},{8,10},{9,11},{10,... | collective-permute-start | bytes 196616 | tf_op jit(solution)/shard_map/ppermute | solution.py:373
  41.9 6.5 %collective-permute-start.28 = (bf16[64,512]{1,0:T(8,128)(2,1)S(1)}, bf16[64,512]{1,0:T(8,128)(2,1)S(1)}, u32[]{:S(2)}, u32[]{:S(2)}) collective-permute-start(bf16[64,512]{1,0:T(8,128)(2,1)S(1)} %get-tuple-element.123), channel_id=1, source_target_pairs={{0,2},{1,3},{2,0},{3,1},{4,6},{5,7},{6,4},{7,5},{8,10},{9,11},{10,... | collective-permute-start | bytes 196616 | tf_op jit(solution)/shard_map/ppermute | solution.py:373
  43.1 6.4 %collective-permute-start.33 = (bf16[64,512]{1,0:T(8,128)(2,1)S(1)}, bf16[64,512]{1,0:T(8,128)(2,1)S(1)}, u32[]{:S(2)}, u32[]{:S(2)}) collective-permute-start(bf16[64,512]{1,0:T(8,128)(2,1)S(1)} %get-tuple-element.127), channel_id=1, source_target_pairs={{0,2},{1,3},{2,0},{3,1},{4,6},{5,7},{6,4},{7,5},{8,10},{9,11},{10,... | collective-permute-start | bytes 196616 | tf_op jit(solution)/shard_map/ppermute | solution.py:373
  45.4 7.7 %collective-permute-start.24 = (bf16[64,512]{1,0:T(8,128)(2,1)S(1)}, bf16[64,512]{1,0:T(8,128)(2,1)S(1)}, u32[]{:S(2)}, u32[]{:S(2)}) collective-permute-start(bf16[64,512]{1,0:T(8,128)(2,1)S(1)} %carry.9.refs_0_), channel_id=1, source_target_pairs={{0,4},{1,5},{2,6},{3,7},{4,0},{5,1},{6,2},{7,3},{8,12},{9,13},{10,... | collective-permute-start | bytes 196616 | tf_op jit(solution)/shard_map/ppermute | solution.py:373
  48.5 6.7 %collective-permute-start.29 = (bf16[64,512]{1,0:T(8,128)(2,1)S(1)}, bf16[64,512]{1,0:T(8,128)(2,1)S(1)}, u32[]{:S(2)}, u32[]{:S(2)}) collective-permute-start(bf16[64,512]{1,0:T(8,128)(2,1)S(1)} %carry.10.refs_0_), channel_id=1, source_target_pairs={{0,4},{1,5},{2,6},{3,7},{4,0},{5,1},{6,2},{7,3},{8,12},{9,13},{10,... | collective-permute-start | bytes 196616 | tf_op jit(solution)/shard_map/ppermute | solution.py:373
  49.5 6.3 %collective-permute-start.34 = (bf16[64,512]{1,0:T(8,128)(2,1)S(1)}, bf16[64,512]{1,0:T(8,128)(2,1)S(1)}, u32[]{:S(2)}, u32[]{:S(2)}) collective-permute-start(bf16[64,512]{1,0:T(8,128)(2,1)S(1)} %carry.11.refs_0_), channel_id=1, source_target_pairs={{0,4},{1,5},{2,6},{3,7},{4,0},{5,1},{6,2},{7,3},{8,12},{9,13},{10,... | collective-permute-start | bytes 196616 | tf_op jit(solution)/shard_map/ppermute | solution.py:373
  53.2 4.5 %collective-permute-start.26 = (bf16[64,512]{1,0:T(8,128)(2,1)S(1)}, bf16[64,512]{1,0:T(8,128)(2,1)S(1)}, u32[]{:S(2)}, u32[]{:S(2)}) collective-permute-start(bf16[64,512]{1,0:T(8,128)(2,1)S(1)} %get-tuple-element.120.refs_0_), channel_id=1, source_target_pairs={{0,1},{1,0},{2,3},{3,2},{4,5},{5,4},{6,7},{7,6},{8,9},{9,8},{10,11... | collective-permute-start | bytes 196616 | tf_op jit(solution)/shard_map/ppermute | solution.py:384
  53.3 5.0 %collective-permute-start.25 = (bf16[64,512]{1,0:T(8,128)(2,1)S(1)}, bf16[64,512]{1,0:T(8,128)(2,1)S(1)}, u32[]{:S(2)}, u32[]{:S(2)}) collective-permute-start(bf16[64,512]{1,0:T(8,128)(2,1)S(1)} %get-tuple-element.120.refs_0_), channel_id=1, source_target_pairs={{0,2},{1,3},{2,0},{3,1},{4,6},{5,7},{6,4},{7,5},{8,10},{9,11},{10,... | collective-permute-start | bytes 196616 | tf_op jit(solution)/shard_map/ppermute | solution.py:373
  55.3 4.6 %collective-permute-start.30 = (bf16[64,512]{1,0:T(8,128)(2,1)S(1)}, bf16[64,512]{1,0:T(8,128)(2,1)S(1)}, u32[]{:S(2)}, u32[]{:S(2)}) collective-permute-start(bf16[64,512]{1,0:T(8,128)(2,1)S(1)} %get-tuple-element.124.refs_4_), channel_id=1, source_target_pairs={{0,2},{1,3},{2,0},{3,1},{4,6},{5,7},{6,4},{7,5},{8,10},{9,11},{10,... | collective-permute-start | bytes 196616 | tf_op jit(solution)/shard_map/ppermute | solution.py:373
  56.0 4.6 %collective-permute-start.35 = (bf16[64,512]{1,0:T(8,128)(2,1)S(1)}, bf16[64,512]{1,0:T(8,128)(2,1)S(1)}, u32[]{:S(2)}, u32[]{:S(2)}) collective-permute-start(bf16[64,512]{1,0:T(8,128)(2,1)S(1)} %get-tuple-element.128.refs_8_), channel_id=1, source_target_pairs={{0,2},{1,3},{2,0},{3,1},{4,6},{5,7},{6,4},{7,5},{8,10},{9,11},{10,... | collective-permute-start | bytes 196616 | tf_op jit(solution)/shard_map/ppermute | solution.py:373
  57.7 2.9 %collective-permute-start.31 = (bf16[64,512]{1,0:T(8,128)(2,1)S(1)}, bf16[64,512]{1,0:T(8,128)(2,1)S(1)}, u32[]{:S(2)}, u32[]{:S(2)}) collective-permute-start(bf16[64,512]{1,0:T(8,128)(2,1)S(1)} %get-tuple-element.124.refs_4_), channel_id=1, source_target_pairs={{0,1},{1,0},{2,3},{3,2},{4,5},{5,4},{6,7},{7,6},{8,9},{9,8},{10,11... | collective-permute-start | bytes 196616 | tf_op jit(solution)/shard_map/ppermute | solution.py:384
  57.7 2.9 %collective-permute-start.36 = (bf16[64,512]{1,0:T(8,128)(2,1)S(1)}, bf16[64,512]{1,0:T(8,128)(2,1)S(1)}, u32[]{:S(2)}, u32[]{:S(2)}) collective-permute-start(bf16[64,512]{1,0:T(8,128)(2,1)S(1)} %get-tuple-element.128.refs_8_), channel_id=1, source_target_pairs={{0,1},{1,0},{2,3},{3,2},{4,5},{5,4},{6,7},{7,6},{8,9},{9,8},{10,11... | collective-permute-start | bytes 196616 | tf_op jit(solution)/shard_map/ppermute | solution.py:384
  58.2 2.4 %collective-permute-start.27 = (bf16[64,512]{1,0:T(8,128)(2,1)S(1)}, bf16[64,512]{1,0:T(8,128)(2,1)S(1)}, u32[]{:S(2)}, u32[]{:S(2)}) collective-permute-start(bf16[64,512]{1,0:T(8,128)(2,1)S(1)} %collective-permute-done.25.refs_1_), channel_id=1, source_target_pairs={{0,1},{1,0},{2,3},{3,2},{4,5},{5,4},{6,7},{7,6},{8,9},{9,8},{10,11... | collective-permute-start | bytes 196616 | tf_op jit(solution)/shard_map/ppermute | solution.py:384
  59.9 1.3 %collective-permute-start.32 = (bf16[64,512]{1,0:T(8,128)(2,1)S(1)}, bf16[64,512]{1,0:T(8,128)(2,1)S(1)}, u32[]{:S(2)}, u32[]{:S(2)}) collective-permute-start(bf16[64,512]{1,0:T(8,128)(2,1)S(1)} %collective-permute-done.30.refs_5_), channel_id=1, source_target_pairs={{0,1},{1,0},{2,3},{3,2},{4,5},{5,4},{6,7},{7,6},{8,9},{9,8},{10,11... | collective-permute-start | bytes 196616 | tf_op jit(solution)/shard_map/ppermute | solution.py:384
  60.6 1.3 %collective-permute-start.37 = (bf16[64,512]{1,0:T(8,128)(2,1)S(1)}, bf16[64,512]{1,0:T(8,128)(2,1)S(1)}, u32[]{:S(2)}, u32[]{:S(2)}) collective-permute-start(bf16[64,512]{1,0:T(8,128)(2,1)S(1)} %collective-permute-done.35.refs_9_), channel_id=1, source_target_pairs={{0,1},{1,0},{2,3},{3,2},{4,5},{5,4},{6,7},{7,6},{8,9},{9,8},{10,11... | collective-permute-start | bytes 196616 | tf_op jit(solution)/shard_map/ppermute | solution.py:384
  63.3 7.6 %collective-permute-start.38 = (bf16[96,512]{1,0:T(8,128)(2,1)S(1)}, bf16[96,512]{1,0:T(8,128)(2,1)S(1)}, u32[]{:S(2)}, u32[]{:S(2)}) collective-permute-start(bf16[96,512]{1,0:T(8,128)(2,1)S(1)} %get-tuple-element.148), channel_id=1, source_target_pairs={{0,6},{1,7},{2,4},{3,5},{4,2},{5,3},{6,0},{7,1},{8,14},{9,15},{10,... | collective-permute-start | bytes 294920 | tf_op jit(solution)/shard_map/ppermute | solution.py:368
  66.3 9.0 %collective-permute-start.39 = (bf16[96,512]{1,0:T(8,128)(2,1)S(1)}, bf16[96,512]{1,0:T(8,128)(2,1)S(1)}, u32[]{:S(2)}, u32[]{:S(2)}) collective-permute-start(bf16[96,512]{1,0:T(8,128)(2,1)S(1)} %get-tuple-element.149), channel_id=1, source_target_pairs={{0,4},{1,5},{2,6},{3,7},{4,0},{5,1},{6,2},{7,3},{8,12},{9,13},{10,... | collective-permute-start | bytes 294920 | tf_op jit(solution)/shard_map/ppermute | solution.py:368
  66.3 9.0 %collective-permute-start.40 = (bf16[96,512]{1,0:T(8,128)(2,1)S(1)}, bf16[96,512]{1,0:T(8,128)(2,1)S(1)}, u32[]{:S(2)}, u32[]{:S(2)}) collective-permute-start(bf16[96,512]{1,0:T(8,128)(2,1)S(1)} %get-tuple-element.150), channel_id=1, source_target_pairs={{0,2},{1,3},{2,0},{3,1},{4,6},{5,7},{6,4},{7,5},{8,10},{9,11},{10,... | collective-permute-start | bytes 294920 | tf_op jit(solution)/shard_map/ppermute | solution.py:368
  (4 other events, 3.5 us)

commit v8 on v7

--- a/solution.py
+++ b/solution.py
@@ -10,7 +10,7 @@
 EPSILON = 1e-06
 CORES = 2
 ROW_TILE = 16
-VMEM_LIMIT = 16 * 1024 * 1024
+VMEM_LIMIT = 24 * 1024 * 1024
 BF16, F32 = jnp.bfloat16, jnp.float32
 
 
@@ -209,18 +209,13 @@
         cut_half(outs[3 + k], ref, 1 - parity, chips, folds if k == 2 else 1)
 
 
-def prep_kernel(keys, values, rates, w1, w3, w2, w1t, w3t, gate, up, down):
-    w1t[...], w3t[...] = w1[...].T, w3[...].T
-    gate[...], up[...], down[...] = update_sums(
-        w1t[...], w3t[...], w2[...], keys[...], rates[...], values[...]
-    )
-
-
-def update_kernel(chips, folds, keys, values, rates, w1t, w3t, w2, own_gate, own_up, own_down, *rest):
+def update_kernel(chips, folds, ko, kx, vo, vx, ro, rx, w1t, w3t, w2, *rest):
     outs, matrices = rest[:6], rest[6:]
-    sums = update_sums(w1t[...], w3t[...], w2[...], keys[...], rates[...], values[...])
-    for ref, own, total in zip(matrices, (own_gate, own_up, own_down), sums):
-        ref[...] = own[...] + total
+    sums = update_sums(
+        w1t[...], w3t[...], w2[...], both(ko, kx), both(ro, rx, 1), both(vo, vx)
+    )
+    for ref, total in zip(matrices, sums):
+        ref[...] = total
     cut_matrices(chips, folds, matrices, outs)
 
 
@@ -378,16 +373,18 @@
     return [mine, *(to_chip(mine, step, chips) for step in range(2, chips, 2))]
 
 
-def from_owners(half, chips):
-    other = to_chip(half, 1, chips)
-    perm = core_perm(chips * CORES)
-    return [half, other, lax.ppermute(half, "tok", perm), lax.ppermute(other, "tok", perm)]
+def from_owners(halves, chips):
+    others = [to_chip(half, 1, chips) for half in halves]
+    *later, others[0] = lax.optimization_barrier((*halves, others[0]))
+    cross = lambda x: lax.ppermute(x, "tok", core_perm(chips * CORES))
+    parts = zip(halves, others, map(cross, later), map(cross, others))
+    return [x for part in parts for x in part]
 
 
 def head_parts(part, heads):
     got = [
         lax.ppermute(part, "head", [(h, partner(h, step, heads)) for h in range(heads)])
-        for step in range(1, heads)
+        for step in reversed(range(1, heads))
     ]
     return [part, *got]
 
@@ -485,26 +482,19 @@
 
     pair = lambda x: lax.ppermute(x, "tok", core_perm(count))
     key_other, value_other, rate_other = pair(key_input), pair(value_input), pair(rates)
-    w1t, w3t, *own_sums = call(
-        prep_kernel,
-        [((fh, dh), BF16)] * 2 + sums_scratch,
-        (key_input, value_input, rates, w1, w3, w2),
-        name="own_tokens",
-        flops=3 * product,
+    w1t, w3t = w1.T, w3.T
+    query_other, grad_other = pair(query_input), pair(out_grad)
+    keys_values = (
+        key_input, key_other, value_input, value_other, rates, rate_other, w1t, w3t, w2,
     )
     sums = call(
         functools.partial(update_kernel, chips, folds),
         half_shares,
-        (key_other, value_other, rate_other, w1t, w3t, w2, *own_sums),
+        keys_values,
         sums_scratch,
         "update",
-        3 * product,
-    )
-    keys_values = (
-        key_input, key_other, value_input, value_other, rates, rate_other, w1t, w3t, w2,
-    )
-    query_later, grad_later, *sums = lax.optimization_barrier((query_input, out_grad, *sums))
-    query_other, grad_other = pair(query_later), pair(grad_later)
+        6 * product,
+    )
     *saved, weighted, p1, p3, p2 = call(
         functools.partial(saved_kernel, chips, folds),
         [((dh, n), BF16)] + [hidden] * 4 + [own_hidden] * 3 + [((dh, n), F32)] + [(half, F32)] * 3,
@@ -526,11 +516,11 @@
             name="owner_forward",
         )
         moved.append(rows_moved)
-        fast += from_owners(rows, chips)
+        fast.append(rows)
     f1t, f3t, f2t, output, q_mixed, q_slope, q_silu, part = call(
         functools.partial(apply_kernel, chips, folds),
         matrices + [((dh, n), F32), ((fh, n), BF16), hidden, hidden, ((2, n), F32)],
-        (*fast, query_input, query_other, weighted),
+        (*from_owners(fast, chips), query_input, query_other, weighted),
         name="apply",
         flops=3 * product,
     )
@@ -563,12 +553,12 @@
             name="owner_backward",
         )
         owned.append(rows_owned)
-        cotangent += from_owners(rows, chips)
+        cotangent.append(rows)
     c1t, c3t, c2t, dbb, upb, gpb, *pieces = call(
         functools.partial(second_kernel, chips, folds),
         matrices + [own_hidden] * 3 + [((3 * g, dh), F32)] + [((3 * g, dh), BF16)] * (chips - 1),
         (
-            *cotangent,
+            *from_owners(cotangent, chips),
             key_input, key_other, push, up_slope, silu, back_slope, back_curve,
         ),
         sums_scratch,

time: 76.4 us -> 73.7 us (0.965)
  local copies, waits for them, and re-layouts: 5.25 us -> 2.12 us
  starting transfers between devices: 37.4 us -> 38.2 us
    unnamed x22 -> x18, local copies, waits for them, and re-layouts: 5.25 us -> 2.12 us
    ppermute x3, waiting for transfers between devices: 3.25 us -> 4.23 us  [head_parts(): lax.ppermute(part, 'head', [(h, partner(h, step, heads)) for h in range(h...]
    ppermute x12, starting transfers between devices: 1.26 us -> 2.12 us  [from_owners(): cross = lambda x: lax.ppermute(x, 'tok', core_perm(chips * CORES))]
    pallas_call x21 -> x20, Pallas kernels: 9.76 us -> 9.52 us  [call(): pl.pallas_call(kernel, out_shape=[jax.ShapeDtypeStruct(s, t) for s, t in...]
  transfers between devices with their start and end apart: 41 -> 41, of which waited for: 21 -> 23; matrix products, arithmetic and copies ran while one was open for 0% -> 2% of each run, Pallas kernels for 7% -> 8%
where the time goes in v8:
time: 73.7 us; the launch traced here: 73.6 us
  starting transfers between devices  38.2 us (52%)
  waiting for transfers between devices  22.9 us (31%)
  Pallas kernels  9.52 us (13%)
  local copies, waits for them, and re-layouts  2.12 us (3%)
  between operations  0.87 us (1%)
    ppermute x18, starting transfers between devices, to_chip(): return lax.ppermute(x, 'tok', chip_perm(chips * CORES, step))  26.9 us
    ppermute x18, waiting for transfers between devices, to_chip(): return lax.ppermute(x, 'tok', chip_perm(chips * CORES, step))  11.7 us
    pallas_call x20, Pallas kernels, call(): pl.pallas_call(kernel, out_shape=[jax.ShapeDtypeStruct(s, t) for s, t in...  9.52 us
    ppermute x3, waiting for transfers between devices, exchange(): lax.ppermute(pieces[s], 'tok', chip_perm(count, s))  4.86 us
    ppermute x3, starting transfers between devices, exchange(): lax.ppermute(pieces[s], 'tok', chip_perm(count, s))  4.47 us
    ppermute x3, waiting for transfers between devices, head_parts(): lax.ppermute(part, 'head', [(h, partner(h, step, heads)) for h in range(h...  4.23 us
    ppermute x3, starting transfers between devices, head_parts(): lax.ppermute(part, 'head', [(h, partner(h, step, heads)) for h in range(h...  3.55 us
    unnamed x18, local copies, waits for them, and re-layouts  2.12 us
  transfers between devices with their start and end apart: 41, of which 23 were waited for; matrix products, arithmetic and copies ran while one was open for 2% of the time, Pallas kernels for 8%

profile of v8, /device:TPU:0, one launch (start us, length us, event | category | flops | bytes accessed | tf_op | source)
XLA Modules:
  0.0 73.6 jit_solution(66826718841185928)
XLA Ops:
  0.6 0.5 collective-permute-start.1
  1.8 1.1 %copy.15 = bf16[1,512,256]{1,2,0:T(8,128)(2,1)S(1)} copy(bf16[1,512,256]{2,1,0:T(8,128)(2,1)} %param.15) | data formatting | bytes 524288 | tf_op args[6]
  3.1 0.7 %copy-done.1 = bf16[1,256,512]{2,1,0:T(8,128)(2,1)S(1)} copy-done((bf16[1,256,512]{2,1,0:T(8,128)(2,1)S(1)}, bf16[1,256,512]{2,1,0:T(8,128)(2,1)}, u32[]{:S(2)}) %copy-start.1) | copy-done | bytes 262168
  4.0 1.2 %update.1 = (f32[64,512]{1,0:T(8,128)S(1)}, f32[64,512]{1,0:T(8,128)S(1)}, f32[64,512]{1,0:T(8,128)S(1)}, bf16[64,512]{1,0:T(8,128)(2,1)S(1)}, bf16[64,512]{1,0:T(8,128)(2,1)S(1)}, /*index=5*/bf16[64,512]{1,0:T(8,128)(2,1)S(1)}) custom-call(bf16[256,512]{1,0:T(8,128)(2,1)S(1)} %copy-done.2, bf16[256,512]{1,0:T(8,128)(2,1)S(1)} %collective-permute-done.kx.refs_13_, ...), custom_call_target="tpu_custom_call" | custom-call | flops 805306368 | bytes 1837056 | tf_op jit(solution)/shard_map/update/pallas_call | solution.py:345
  5.2 3.1 %collective-permute-start.8 = (bf16[64,512]{1,0:T(8,128)(2,1)S(1)}, bf16[64,512]{1,0:T(8,128)(2,1)S(1)}, u32[]{:S(2)}, u32[]{:S(2)}) collective-permute-start(bf16[64,512]{1,0:T(8,128)(2,1)S(1)} %get-tuple-element.85), channel_id=1, source_target_pairs={{0,2},{1,3},{2,0},{3,1},{4,6},{5,7},{6,4},{7,5},{8,10},{9,11},{10,... | collective-permute-start | bytes 196616 | tf_op jit(solution)/shard_map/ppermute | solution.py:368
  8.4 1.9 %collective-permute-start.6 = (bf16[64,512]{1,0:T(8,128)(2,1)S(1)}, bf16[64,512]{1,0:T(8,128)(2,1)S(1)}, u32[]{:S(2)}, u32[]{:S(2)}) collective-permute-start(bf16[64,512]{1,0:T(8,128)(2,1)S(1)} %get-tuple-element.81), channel_id=1, source_target_pairs={{0,2},{1,3},{2,0},{3,1},{4,6},{5,7},{6,4},{7,5},{8,10},{9,11},{10,... | collective-permute-start | bytes 196616 | tf_op jit(solution)/shard_map/ppermute | solution.py:368
  10.6 3.0 %collective-permute-start.9 = (bf16[64,512]{1,0:T(8,128)(2,1)S(1)}, bf16[64,512]{1,0:T(8,128)(2,1)S(1)}, u32[]{:S(2)}, u32[]{:S(2)}) collective-permute-start(bf16[64,512]{1,0:T(8,128)(2,1)S(1)} %carry.8.refs_0_), channel_id=1, source_target_pairs={{0,4},{1,5},{2,6},{3,7},{4,0},{5,1},{6,2},{7,3},{8,12},{9,13},{10,... | collective-permute-start | bytes 196616 | tf_op jit(solution)/shard_map/ppermute | solution.py:368
  13.6 2.2 %collective-permute-start.5 = (bf16[64,512]{1,0:T(8,128)(2,1)S(1)}, bf16[64,512]{1,0:T(8,128)(2,1)S(1)}, u32[]{:S(2)}, u32[]{:S(2)}) collective-permute-start(bf16[64,512]{1,0:T(8,128)(2,1)S(1)} %carry.6.refs_0_), channel_id=1, source_target_pairs={{0,4},{1,5},{2,6},{3,7},{4,0},{5,1},{6,2},{7,3},{8,12},{9,13},{10,... | collective-permute-start | bytes 196616 | tf_op jit(solution)/shard_map/ppermute | solution.py:368
  15.8 1.4 %collective-permute-start.7 = (bf16[64,512]{1,0:T(8,128)(2,1)S(1)}, bf16[64,512]{1,0:T(8,128)(2,1)S(1)}, u32[]{:S(2)}, u32[]{:S(2)}) collective-permute-start(bf16[64,512]{1,0:T(8,128)(2,1)S(1)} %carry.7.refs_0_), channel_id=1, source_target_pairs={{0,4},{1,5},{2,6},{3,7},{4,0},{5,1},{6,2},{7,3},{8,12},{9,13},{10,... | collective-permute-start | bytes 196616 | tf_op jit(solution)/shard_map/ppermute | solution.py:368
  17.2 1.1 %saved.1 = (bf16[512,512]{1,0:T(8,128)(2,1)S(1)}, f32[256,512]{1,0:T(8,128)S(1)}, f32[256,512]{1,0:T(8,128)S(1)}, f32[256,512]{1,0:T(8,128)S(1)}, f32[256,512]{1...) custom-call(bf16[256,512]{1,0:T(8,128)(2,1)S(1)} %copy-done.2, ...), custom_call_target="tpu_custom_call" | custom-call | flops 402653184 | bytes 2363392 | tf_op jit(solution)/shard_map/saved/pallas_call | solution.py:345
  18.5 2.6 %collective-permute-start.16 = (bf16[64,512]{1,0:T(8,128)(2,1)S(1)}, bf16[64,512]{1,0:T(8,128)(2,1)S(1)}, u32[]{:S(2)}, u32[]{:S(2)}) collective-permute-start(bf16[64,512]{1,0:T(8,128)(2,1)S(1)} %get-tuple-element.90.refs_8_), channel_id=1, source_target_pairs={{0,2},{1,3},{2,0},{3,1},{4,6},{5,7},{6,4},{7,5},{8,10},{9,11},{10,... | collective-permute-start | bytes 196616 | tf_op jit(solution)/shard_map/ppermute | solution.py:368
  21.4 1.2 %collective-permute-start.10 = (bf16[64,512]{1,0:T(8,128)(2,1)S(1)}, bf16[64,512]{1,0:T(8,128)(2,1)S(1)}, u32[]{:S(2)}, u32[]{:S(2)}) collective-permute-start(bf16[64,512]{1,0:T(8,128)(2,1)S(1)} %get-tuple-element.88.refs_0_), channel_id=1, source_target_pairs={{0,2},{1,3},{2,0},{3,1},{4,6},{5,7},{6,4},{7,5},{8,10},{9,11},{10,... | collective-permute-start | bytes 196616 | tf_op jit(solution)/shard_map/ppermute | solution.py:368
  23.2 0.5 collective-permute-start.13
  23.7 0.7 collective-permute-done.16.refs_9_
  24.4 1.5 %collective-permute-done.10.refs_1_ = bf16[64,512]{1,0:T(8,128)(2,1)S(1)} collective-permute-done((bf16[64,512]{1,0:T(8,128)(2,1)S(1)}, bf16[64,512]{1,0:T(8,128)(2,1)S(1)}, u32[]{:S(2)}, u32[]{:S(2)}) %collective-permute-start.10) | collective-permute-done | bytes 65568 | tf_op jit(solution)/shard_map/ppermute | solution.py:368
  25.9 0.5 collective-permute-start.14
  26.4 1.1 %collective-permute-done.13.refs_5_ = bf16[64,512]{1,0:T(8,128)(2,1)S(1)} collective-permute-done((bf16[64,512]{1,0:T(8,128)(2,1)S(1)}, bf16[64,512]{1,0:T(8,128)(2,1)S(1)}, u32[]{:S(2)}, u32[]{:S(2)}) %collective-permute-start.13) | collective-permute-done | bytes 65568 | tf_op jit(solution)/shard_map/ppermute | solution.py:368
  27.5 0.5 collective-permute-start.17
  28.1 0.7 collective-permute-done.15.refs_7_
  29.3 0.8 %apply.1 = (bf16[256,512]{1,0:T(8,128)(2,1)S(1)}, bf16[256,512]{1,0:T(8,128)(2,1)S(1)}, bf16[512,256]{1,0:T(8,128)(2,1)S(1)}, f32[512,512]{1,0:T(8,128)S(1)}, bf...) custom-call(bf16[64,512]{1,0:T(8,128)(2,1)S(1)} %get-tuple-element.88.refs_0, ...), custom_call_target="tpu_custom_call" | custom-call | flops 402653184 | bytes 2359296 | tf_op jit(solution)/shard_map/apply/pallas_call | solution.py:345
  30.1 1.8 %collective-permute-start.22 = (f32[2,512]{1,0:T(2,128)S(1)}, f32[2,512]{1,0:T(2,128)S(1)}, u32[]{:S(2)}, u32[]{:S(2)}) collective-permute-start(f32[2,512]{1,0:T(2,128)S(1)} %get-tuple-element.92.refs_0_), channel_id=1, source_target_pairs={{0,8},{8,0},{16,24},{24,16},{1,9},{9,1},{17,25},{25,17},{2,10},{10... | collective-permute-start | bytes 12296 | tf_op jit(solution)/shard_map/ppermute | solution.py:386
  31.9 1.5 %collective-permute-start.21 = (f32[2,512]{1,0:T(2,128)S(1)}, f32[2,512]{1,0:T(2,128)S(1)}, u32[]{:S(2)}, u32[]{:S(2)}) collective-permute-start(f32[2,512]{1,0:T(2,128)S(1)} %get-tuple-element.92.refs_0_), channel_id=1, source_target_pairs={{0,16},{8,24},{16,0},{24,8},{1,17},{9,25},{17,1},{25,9},{2,18},{10... | collective-permute-start | bytes 12296 | tf_op jit(solution)/shard_map/ppermute | solution.py:386
  33.8 1.7 %collective-permute-done.21.refs_2_ = f32[2,512]{1,0:T(2,128)S(1)} collective-permute-done((f32[2,512]{1,0:T(2,128)S(1)}, f32[2,512]{1,0:T(2,128)S(1)}, u32[]{:S(2)}, u32[]{:S(2)}) %collective-permute-start.21) | collective-permute-done | bytes 4128 | tf_op jit(solution)/shard_map/ppermute | solution.py:386
  35.5 2.4 %collective-permute-done.20.refs_1_ = f32[2,512]{1,0:T(2,128)S(1)} collective-permute-done((f32[2,512]{1,0:T(2,128)S(1)}, f32[2,512]{1,0:T(2,128)S(1)}, u32[]{:S(2)}, u32[]{:S(2)}) %collective-permute-start.20) | collective-permute-done | bytes 4128 | tf_op jit(solution)/shard_map/ppermute | solution.py:386
  37.9 0.9 %apply_back.1 = (bf16[256,256]{1,0:T(8,128)(2,1)S(1)}, bf16[256,256]{1,0:T(8,128)(2,1)S(1)}, f32[64,512]{1,0:T(8,128)S(1)}, f32[64,512]{1,0:T(8,128)S(1)}, f32[6...) custom-call(f32[2,512]{1,0:T(2,128)S(1)} %get-tuple-element.92.refs_0, ...), custom_call_target="tpu_custom_call" | custom-call | flops 536870912 | bytes 4210688 | tf_op jit(solution)/shard_map/apply_back/pallas_call | solution.py:345
  38.8 0.6 collective-permute-start.25
  39.4 1.5 %collective-permute-start.23 = (bf16[64,512]{1,0:T(8,128)(2,1)S(1)}, bf16[64,512]{1,0:T(8,128)(2,1)S(1)}, u32[]{:S(2)}, u32[]{:S(2)}) collective-permute-start(bf16[64,512]{1,0:T(8,128)(2,1)S(1)} %get-tuple-element.105), channel_id=1, source_target_pairs={{0,2},{1,3},{2,0},{3,1},{4,6},{5,7},{6,4},{7,5},{8,10},{9,11},{10,... | collective-permute-start | bytes 196616 | tf_op jit(solution)/shard_map/ppermute | solution.py:368
  40.9 0.6 collective-permute-start.27
  41.5 1.7 %collective-permute-done.25.got = bf16[64,512]{1,0:T(8,128)(2,1)S(1)} collective-permute-done((bf16[64,512]{1,0:T(8,128)(2,1)S(1)}, bf16[64,512]{1,0:T(8,128)(2,1)S(1)}, u32[]{:S(2)}, u32[]{:S(2)}) %collective-permute-start.25) | collective-permute-done | bytes 65568 | tf_op jit(solution)/shard_map/ppermute | solution.py:368
  43.2 3.4 %collective-permute-start.26 = (bf16[64,512]{1,0:T(8,128)(2,1)S(1)}, bf16[64,512]{1,0:T(8,128)(2,1)S(1)}, u32[]{:S(2)}, u32[]{:S(2)}) collective-permute-start(bf16[64,512]{1,0:T(8,128)(2,1)S(1)} %carry.10.refs_0_), channel_id=1, source_target_pairs={{0,4},{1,5},{2,6},{3,7},{4,0},{5,1},{6,2},{7,3},{8,12},{9,13},{10,... | collective-permute-start | bytes 196616 | tf_op jit(solution)/shard_map/ppermute | solution.py:368
  46.6 0.7 collective-permute-start.24
  47.3 2.4 %collective-permute-start.28 = (bf16[64,512]{1,0:T(8,128)(2,1)S(1)}, bf16[64,512]{1,0:T(8,128)(2,1)S(1)}, u32[]{:S(2)}, u32[]{:S(2)}) collective-permute-start(bf16[64,512]{1,0:T(8,128)(2,1)S(1)} %carry.11.refs_0_), channel_id=1, source_target_pairs={{0,4},{1,5},{2,6},{3,7},{4,0},{5,1},{6,2},{7,3},{8,12},{9,13},{10,... | collective-permute-start | bytes 196616 | tf_op jit(solution)/shard_map/ppermute | solution.py:368
  49.7 1.2 %collective-permute-done.26.refs_1_ = bf16[64,512]{1,0:T(8,128)(2,1)S(1)} collective-permute-done((bf16[64,512]{1,0:T(8,128)(2,1)S(1)}, bf16[64,512]{1,0:T(8,128)(2,1)S(1)}, u32[]{:S(2)}, u32[]{:S(2)}) %collective-permute-start.26) | collective-permute-done | bytes 65568 | tf_op jit(solution)/shard_map/ppermute | solution.py:368
  51.1 1.3 %collective-permute-done.24.refs_1_ = bf16[64,512]{1,0:T(8,128)(2,1)S(1)} collective-permute-done((bf16[64,512]{1,0:T(8,128)(2,1)S(1)}, bf16[64,512]{1,0:T(8,128)(2,1)S(1)}, u32[]{:S(2)}, u32[]{:S(2)}) %collective-permute-start.24) | collective-permute-done | bytes 65568 | tf_op jit(solution)/shard_map/ppermute | solution.py:368
  52.5 0.8 %collective-permute-start.29 = (bf16[64,512]{1,0:T(8,128)(2,1)S(1)}, bf16[64,512]{1,0:T(8,128)(2,1)S(1)}, u32[]{:S(2)}, u32[]{:S(2)}) collective-permute-start(bf16[64,512]{1,0:T(8,128)(2,1)S(1)} %get-tuple-element.116.refs_0_), channel_id=1, source_target_pairs={{0,2},{1,3},{2,0},{3,1},{4,6},{5,7},{6,4},{7,5},{8,10},{9,11},{10,... | collective-permute-start | bytes 196616 | tf_op jit(solution)/shard_map/ppermute | solution.py:368
  53.9 0.9 %collective-permute-start.35 = (bf16[64,512]{1,0:T(8,128)(2,1)S(1)}, bf16[64,512]{1,0:T(8,128)(2,1)S(1)}, u32[]{:S(2)}, u32[]{:S(2)}) collective-permute-start(bf16[64,512]{1,0:T(8,128)(2,1)S(1)} %get-tuple-element.118.refs_8_), channel_id=1, source_target_pairs={{0,2},{1,3},{2,0},{3,1},{4,6},{5,7},{6,4},{7,5},{8,10},{9,11},{10,... | collective-permute-start | bytes 196616 | tf_op jit(solution)/shard_map/ppermute | solution.py:368
  55.3 1.5 %collective-permute-done.29.refs_1_ = bf16[64,512]{1,0:T(8,128)(2,1)S(1)} collective-permute-done((bf16[64,512]{1,0:T(8,128)(2,1)S(1)}, bf16[64,512]{1,0:T(8,128)(2,1)S(1)}, u32[]{:S(2)}, u32[]{:S(2)}) %collective-permute-start.29) | collective-permute-done | bytes 65568 | tf_op jit(solution)/shard_map/ppermute | solution.py:368
  57.4 0.9 %collective-permute-done.35.refs_9_ = bf16[64,512]{1,0:T(8,128)(2,1)S(1)} collective-permute-done((bf16[64,512]{1,0:T(8,128)(2,1)S(1)}, bf16[64,512]{1,0:T(8,128)(2,1)S(1)}, u32[]{:S(2)}, u32[]{:S(2)}) %collective-permute-start.35) | collective-permute-done | bytes 65568 | tf_op jit(solution)/shard_map/ppermute | solution.py:368
  58.3 0.5 collective-permute-start.37
  58.8 0.7 collective-permute-done.31.refs_3_
  59.7 1.4 %second_adjoint.1 = (bf16[256,512]{1,0:T(8,128)(2,1)S(1)}, bf16[256,512]{1,0:T(8,128)(2,1)S(1)}, bf16[512,256]{1,0:T(8,128)(2,1)S(1)}, bf16[256,256]{1,0:T(8,128...) custom-call(bf16[64,512]{1,0:T(8,128)(2,1)S(1)} %get-tuple-element.1, ...), custom_call_target="tpu_custom_call" | custom-call | flops 805306368 | bytes 3932160 | tf_op jit(solution)/shard_map/second_adjoint/pallas_call | solution.py:345
  61.1 2.3 %collective-permute-start.38 = (bf16[96,512]{1,0:T(8,128)(2,1)S(1)}, bf16[96,512]{1,0:T(8,128)(2,1)S(1)}, u32[]{:S(2)}, u32[]{:S(2)}) collective-permute-start(bf16[96,512]{1,0:T(8,128)(2,1)S(1)} %get-tuple-element.138), channel_id=1, source_target_pairs={{0,6},{1,7},{2,4},{3,5},{4,2},{5,3},{6,0},{7,1},{8,14},{9,15},{10,... | collective-permute-start | bytes 294920 | tf_op jit(solution)/shard_map/ppermute | solution.py:363
  63.5 2.1 %collective-permute-start.40 = (bf16[96,512]{1,0:T(8,128)(2,1)S(1)}, bf16[96,512]{1,0:T(8,128)(2,1)S(1)}, u32[]{:S(2)}, u32[]{:S(2)}) collective-permute-start(bf16[96,512]{1,0:T(8,128)(2,1)S(1)} %get-tuple-element.140), channel_id=1, source_target_pairs={{0,2},{1,3},{2,0},{3,1},{4,6},{5,7},{6,4},{7,5},{8,10},{9,11},{10,... | collective-permute-start | bytes 294920 | tf_op jit(solution)/shard_map/ppermute | solution.py:363
  65.6 1.0 %query_grad.1 = bf16[256,512]{1,0:T(8,128)(2,1)} custom-call(bf16[256,256]{1,0:T(8,128)(2,1)S(1)} %get-tuple-element.98.gate_back, bf16[256,256]{1,0:T(8,128)(2,1)S(1)} %get-tuple-element.99.up_back, bf16[256,512]{1,0:T(8,128)(2,1)S(1)} %get-tuple-element.100.f1t, bf16[256,512]{1,0:T(8,128)(2,1)S(1)} %get-tuple-element.101.f3t), custom_call_target="tpu_custom_call" | custom-call | flops 134217728 | bytes 786432 | tf_op jit(solution)/shard_map/query_grad/pallas_call | solution.py:345
  66.6 1.4 %token_grads.1 = (bf16[256,512]{1,0:T(8,128)(2,1)}, bf16[256,512]{1,0:T(8,128)(2,1)}) custom-call(f32[1,256]{1,0:T(1,128)S(1)} %bitcast.30, bf16[256,256]{1,0:T(8,128)(2,1)S(1)} %get-tuple-element.102.refs_1_, bf16[256,256]{1,0:T(8,128)(2,1)S(1)} %get-tuple-element.124.refs_2_, bf16[256,256]{1,0:T(8,128)(2,1)S(1)} %get-tuple-element.125.refs_3_, ...), custom_call_target="tpu_custom_call" | custom-call | flops 402653184 | bytes 2360320 | tf_op jit(solution)/shard_map/token_grads/pallas_call | solution.py:345
  68.0 0.7 collective-permute-done.38.refs_4_
  68.7 4.1 %collective-permute-done.39.refs_5_ = bf16[96,512]{1,0:T(8,128)(2,1)S(1)} collective-permute-done((bf16[96,512]{1,0:T(8,128)(2,1)S(1)}, bf16[96,512]{1,0:T(8,128)(2,1)S(1)}, u32[]{:S(2)}, u32[]{:S(2)}) %collective-permute-start.39) | collective-permute-done | bytes 98336 | tf_op jit(solution)/shard_map/ppermute | solution.py:363
  72.9 0.7 owner_result.1
  (72 shorter events, 5.8 us)
Async XLA Ops:
  0.6 1.0 %copy-start.5 = (f32[256,1]{0,1:T(1,128)S(1)}, f32[256,1]{0,1:T(1,128)}, u32[]{:S(2)}) copy-start(f32[256,1]{0,1:T(1,128)} %param.13) | copy-start | bytes 3076
  0.6 2.5 %collective-permute-start.1 = (bf16[256,512]{1,0:T(8,128)(2,1)}, bf16[256,512]{1,0:T(8,128)(2,1)S(1)}, u32[]{:S(2)}, u32[]{:S(2)}) collective-permute-start(bf16[256,512]{1,0:T(8,128)(2,1)} %vo.3), channel_id=1, source_target_pairs={{0,1},{1,0},{2,3},{3,2},{4,5},{5,4},{6,7},{7,6},{8,9},{9,8},{10,11... | collective-permute-start | bytes 786440 | tf_op jit(solution)/shard_map/ppermute | solution.py:483
  1.2 2.0 %collective-permute-start = (bf16[256,512]{1,0:T(8,128)(2,1)}, bf16[256,512]{1,0:T(8,128)(2,1)S(1)}, u32[]{:S(2)}, u32[]{:S(2)}) collective-permute-start(bf16[256,512]{1,0:T(8,128)(2,1)} %refs_12_.3), channel_id=1, source_target_pairs={{0,1},{1,0},{2,3},{3,2},{4,5},{5,4},{6,7},{7,6},{8,9},{9,8},{10,11... | collective-permute-start | bytes 786440 | tf_op jit(solution)/shard_map/ppermute | solution.py:483
  1.2 16.0 %collective-permute-start.3 = (bf16[256,512]{1,0:T(8,128)(2,1)}, bf16[256,512]{1,0:T(8,128)(2,1)S(1)}, u32[]{:S(2)}, u32[]{:S(2)}) collective-permute-start(bf16[256,512]{1,0:T(8,128)(2,1)} %go.1), channel_id=1, source_target_pairs={{0,1},{1,0},{2,3},{3,2},{4,5},{5,4},{6,7},{7,6},{8,9},{9,8},{10,11... | collective-permute-start | bytes 786440 | tf_op jit(solution)/shard_map/ppermute | solution.py:483
  1.7 1.2 %copy-start.7 = (bf16[1,512,256]{2,1,0:T(8,128)(2,1)S(1)}, bf16[1,512,256]{2,1,0:T(8,128)(2,1)}, u32[]{:S(2)}) copy-start(bf16[1,512,256]{2,1,0:T(8,128)(2,1)} %param.16) | copy-start | bytes 786436
  1.7 1.4 %collective-permute-start.2 = (f32[1,256]{1,0:T(1,128)S(1)}, f32[1,256]{1,0:T(1,128)S(1)}, u32[]{:S(2)}, u32[]{:S(2)}) collective-permute-start(f32[1,256]{1,0:T(1,128)S(1)} %bitcast.27), channel_id=1, source_target_pairs={{0,1},{1,0},{2,3},{3,2},{4,5},{5,4},{6,7},{7,6},{8,9},{9,8},{10,11... | collective-permute-start | bytes 3080 | tf_op jit(solution)/shard_map/ppermute | solution.py:483
  1.8 1.4 %copy-start.3 = (bf16[256,512]{1,0:T(8,128)(2,1)S(1)}, bf16[256,512]{1,0:T(8,128)(2,1)}, u32[]{:S(2)}) copy-start(bf16[256,512]{1,0:T(8,128)(2,1)} %vo.3) | copy-start | bytes 786436
  2.9 1.0 %copy-start.2 = (bf16[256,512]{1,0:T(8,128)(2,1)S(1)}, bf16[256,512]{1,0:T(8,128)(2,1)}, u32[]{:S(2)}) copy-start(bf16[256,512]{1,0:T(8,128)(2,1)} %refs_12_.3) | copy-start | bytes 786436
  4.0 4.3 %copy-start = (bf16[256,512]{1,0:T(8,128)(2,1)S(1)}, bf16[256,512]{1,0:T(8,128)(2,1)}, u32[]{:S(2)}) copy-start(bf16[256,512]{1,0:T(8,128)(2,1)} %refs_10_.1) | copy-start | bytes 786436
  5.2 5.4 %collective-permute-start.8 = (bf16[64,512]{1,0:T(8,128)(2,1)S(1)}, bf16[64,512]{1,0:T(8,128)(2,1)S(1)}, u32[]{:S(2)}, u32[]{:S(2)}) collective-permute-start(bf16[64,512]{1,0:T(8,128)(2,1)S(1)} %get-tuple-element.85), channel_id=1, source_target_pairs={{0,2},{1,3},{2,0},{3,1},{4,6},{5,7},{6,4},{7,5},{8,10},{9,11},{10,... | collective-permute-start | bytes 196616 | tf_op jit(solution)/shard_map/ppermute | solution.py:368
  8.2 19.3 %collective-permute-start.19 = (bf16[256,512]{1,0:T(8,128)(2,1)S(1)}, bf16[256,512]{1,0:T(8,128)(2,1)S(1)}, u32[]{:S(2)}, u32[]{:S(2)}) collective-permute-start(bf16[256,512]{1,0:T(8,128)(2,1)S(1)} %copy-done), channel_id=1, source_target_pairs={{0,1},{1,0},{2,3},{3,2},{4,5},{5,4},{6,7},{7,6},{8,9},{9,8},{10,11... | collective-permute-start | bytes 786440 | tf_op jit(solution)/shard_map/ppermute | solution.py:483
  8.2 5.3 %collective-permute-start.4 = (bf16[64,512]{1,0:T(8,128)(2,1)S(1)}, bf16[64,512]{1,0:T(8,128)(2,1)S(1)}, u32[]{:S(2)}, u32[]{:S(2)}) collective-permute-start(bf16[64,512]{1,0:T(8,128)(2,1)S(1)} %get-tuple-element.77), channel_id=1, source_target_pairs={{0,2},{1,3},{2,0},{3,1},{4,6},{5,7},{6,4},{7,5},{8,10},{9,11},{10,... | collective-permute-start | bytes 196616 | tf_op jit(solution)/shard_map/ppermute | solution.py:368
  8.4 7.4 %collective-permute-start.6 = (bf16[64,512]{1,0:T(8,128)(2,1)S(1)}, bf16[64,512]{1,0:T(8,128)(2,1)S(1)}, u32[]{:S(2)}, u32[]{:S(2)}) collective-permute-start(bf16[64,512]{1,0:T(8,128)(2,1)S(1)} %get-tuple-element.81), channel_id=1, source_target_pairs={{0,2},{1,3},{2,0},{3,1},{4,6},{5,7},{6,4},{7,5},{8,10},{9,11},{10,... | collective-permute-start | bytes 196616 | tf_op jit(solution)/shard_map/ppermute | solution.py:368
  10.6 7.7 %collective-permute-start.9 = (bf16[64,512]{1,0:T(8,128)(2,1)S(1)}, bf16[64,512]{1,0:T(8,128)(2,1)S(1)}, u32[]{:S(2)}, u32[]{:S(2)}) collective-permute-start(bf16[64,512]{1,0:T(8,128)(2,1)S(1)} %carry.8.refs_0_), channel_id=1, source_target_pairs={{0,4},{1,5},{2,6},{3,7},{4,0},{5,1},{6,2},{7,3},{8,12},{9,13},{10,... | collective-permute-start | bytes 196616 | tf_op jit(solution)/shard_map/ppermute | solution.py:368
  13.6 3.6 %copy-start.4 = (bf16[256,512]{1,0:T(8,128)(2,1)S(1)}, bf16[256,512]{1,0:T(8,128)(2,1)}, u32[]{:S(2)}) copy-start(bf16[256,512]{1,0:T(8,128)(2,1)} %go.1) | copy-start | bytes 786436
  13.6 7.7 %collective-permute-start.5 = (bf16[64,512]{1,0:T(8,128)(2,1)S(1)}, bf16[64,512]{1,0:T(8,128)(2,1)S(1)}, u32[]{:S(2)}, u32[]{:S(2)}) collective-permute-start(bf16[64,512]{1,0:T(8,128)(2,1)S(1)} %carry.6.refs_0_), channel_id=1, source_target_pairs={{0,4},{1,5},{2,6},{3,7},{4,0},{5,1},{6,2},{7,3},{8,12},{9,13},{10,... | collective-permute-start | bytes 196616 | tf_op jit(solution)/shard_map/ppermute | solution.py:368
  15.8 1.4 %copy-start.6 = (f32[512]{0:T(512)S(1)}, f32[512]{0:T(512)}, u32[]{:S(2)}) copy-start(f32[512]{0:T(512)} %param.14) | copy-start | bytes 6148
  15.8 7.2 %collective-permute-start.7 = (bf16[64,512]{1,0:T(8,128)(2,1)S(1)}, bf16[64,512]{1,0:T(8,128)(2,1)S(1)}, u32[]{:S(2)}, u32[]{:S(2)}) collective-permute-start(bf16[64,512]{1,0:T(8,128)(2,1)S(1)} %carry.7.refs_0_), channel_id=1, source_target_pairs={{0,4},{1,5},{2,6},{3,7},{4,0},{5,1},{6,2},{7,3},{8,12},{9,13},{10,... | collective-permute-start | bytes 196616 | tf_op jit(solution)/shard_map/ppermute | solution.py:368
  18.5 5.9 %collective-permute-start.16 = (bf16[64,512]{1,0:T(8,128)(2,1)S(1)}, bf16[64,512]{1,0:T(8,128)(2,1)S(1)}, u32[]{:S(2)}, u32[]{:S(2)}) collective-permute-start(bf16[64,512]{1,0:T(8,128)(2,1)S(1)} %get-tuple-element.90.refs_8_), channel_id=1, source_target_pairs={{0,2},{1,3},{2,0},{3,1},{4,6},{5,7},{6,4},{7,5},{8,10},{9,11},{10,... | collective-permute-start | bytes 196616 | tf_op jit(solution)/shard_map/ppermute | solution.py:368
  21.4 4.5 %collective-permute-start.10 = (bf16[64,512]{1,0:T(8,128)(2,1)S(1)}, bf16[64,512]{1,0:T(8,128)(2,1)S(1)}, u32[]{:S(2)}, u32[]{:S(2)}) collective-permute-start(bf16[64,512]{1,0:T(8,128)(2,1)S(1)} %get-tuple-element.88.refs_0_), channel_id=1, source_target_pairs={{0,2},{1,3},{2,0},{3,1},{4,6},{5,7},{6,4},{7,5},{8,10},{9,11},{10,... | collective-permute-start | bytes 196616 | tf_op jit(solution)/shard_map/ppermute | solution.py:368
  23.2 4.3 %collective-permute-start.13 = (bf16[64,512]{1,0:T(8,128)(2,1)S(1)}, bf16[64,512]{1,0:T(8,128)(2,1)S(1)}, u32[]{:S(2)}, u32[]{:S(2)}) collective-permute-start(bf16[64,512]{1,0:T(8,128)(2,1)S(1)} %get-tuple-element.89.refs_4_), channel_id=1, source_target_pairs={{0,2},{1,3},{2,0},{3,1},{4,6},{5,7},{6,4},{7,5},{8,10},{9,11},{10,... | collective-permute-start | bytes 196616 | tf_op jit(solution)/shard_map/ppermute | solution.py:368
  24.4 3.6 %collective-permute-start.18 = (bf16[64,512]{1,0:T(8,128)(2,1)S(1)}, bf16[64,512]{1,0:T(8,128)(2,1)S(1)}, u32[]{:S(2)}, u32[]{:S(2)}) collective-permute-start(bf16[64,512]{1,0:T(8,128)(2,1)S(1)} %collective-permute-done.16.refs_9_), channel_id=1, source_target_pairs={{0,1},{1,0},{2,3},{3,2},{4,5},{5,4},{6,7},{7,6},{8,9},{9,8},{10,11... | collective-permute-start | bytes 196616 | tf_op jit(solution)/shard_map/ppermute | solution.py:379
  25.9 2.8 %collective-permute-start.11 = (bf16[64,512]{1,0:T(8,128)(2,1)S(1)}, bf16[64,512]{1,0:T(8,128)(2,1)S(1)}, u32[]{:S(2)}, u32[]{:S(2)}) collective-permute-start(bf16[64,512]{1,0:T(8,128)(2,1)S(1)} %get-tuple-element.88.refs_0_), channel_id=1, source_target_pairs={{0,1},{1,0},{2,3},{3,2},{4,5},{5,4},{6,7},{7,6},{8,9},{9,8},{10,11... | collective-permute-start | bytes 196616 | tf_op jit(solution)/shard_map/ppermute | solution.py:379
  25.9 2.8 %collective-permute-start.14 = (bf16[64,512]{1,0:T(8,128)(2,1)S(1)}, bf16[64,512]{1,0:T(8,128)(2,1)S(1)}, u32[]{:S(2)}, u32[]{:S(2)}) collective-permute-start(bf16[64,512]{1,0:T(8,128)(2,1)S(1)} %get-tuple-element.89.refs_4_), channel_id=1, source_target_pairs={{0,1},{1,0},{2,3},{3,2},{4,5},{5,4},{6,7},{7,6},{8,9},{9,8},{10,11... | collective-permute-start | bytes 196616 | tf_op jit(solution)/shard_map/ppermute | solution.py:379
  27.5 1.3 %collective-permute-start.15 = (bf16[64,512]{1,0:T(8,128)(2,1)S(1)}, bf16[64,512]{1,0:T(8,128)(2,1)S(1)}, u32[]{:S(2)}, u32[]{:S(2)}) collective-permute-start(bf16[64,512]{1,0:T(8,128)(2,1)S(1)} %collective-permute-done.13.refs_5_), channel_id=1, source_target_pairs={{0,1},{1,0},{2,3},{3,2},{4,5},{5,4},{6,7},{7,6},{8,9},{9,8},{10,11... | collective-permute-start | bytes 196616 | tf_op jit(solution)/shard_map/ppermute | solution.py:379
  27.5 1.4 %collective-permute-start.17 = (bf16[64,512]{1,0:T(8,128)(2,1)S(1)}, bf16[64,512]{1,0:T(8,128)(2,1)S(1)}, u32[]{:S(2)}, u32[]{:S(2)}) collective-permute-start(bf16[64,512]{1,0:T(8,128)(2,1)S(1)} %get-tuple-element.90.refs_8_), channel_id=1, source_target_pairs={{0,1},{1,0},{2,3},{3,2},{4,5},{5,4},{6,7},{7,6},{8,9},{9,8},{10,11... | collective-permute-start | bytes 196616 | tf_op jit(solution)/shard_map/ppermute | solution.py:379
  28.0 1.3 %collective-permute-start.12 = (bf16[64,512]{1,0:T(8,128)(2,1)S(1)}, bf16[64,512]{1,0:T(8,128)(2,1)S(1)}, u32[]{:S(2)}, u32[]{:S(2)}) collective-permute-start(bf16[64,512]{1,0:T(8,128)(2,1)S(1)} %collective-permute-done.10.refs_1_), channel_id=1, source_target_pairs={{0,1},{1,0},{2,3},{3,2},{4,5},{5,4},{6,7},{7,6},{8,9},{9,8},{10,11... | collective-permute-start | bytes 196616 | tf_op jit(solution)/shard_map/ppermute | solution.py:379
  30.1 3.7 %collective-permute-start.22 = (f32[2,512]{1,0:T(2,128)S(1)}, f32[2,512]{1,0:T(2,128)S(1)}, u32[]{:S(2)}, u32[]{:S(2)}) collective-permute-start(f32[2,512]{1,0:T(2,128)S(1)} %get-tuple-element.92.refs_0_), channel_id=1, source_target_pairs={{0,8},{8,0},{16,24},{24,16},{1,9},{9,1},{17,25},{25,17},{2,10},{10... | collective-permute-start | bytes 12296 | tf_op jit(solution)/shard_map/ppermute | solution.py:386
  31.9 3.6 %collective-permute-start.21 = (f32[2,512]{1,0:T(2,128)S(1)}, f32[2,512]{1,0:T(2,128)S(1)}, u32[]{:S(2)}, u32[]{:S(2)}) collective-permute-start(f32[2,512]{1,0:T(2,128)S(1)} %get-tuple-element.92.refs_0_), channel_id=1, source_target_pairs={{0,16},{8,24},{16,0},{24,8},{1,17},{9,25},{17,1},{25,9},{2,18},{10... | collective-permute-start | bytes 12296 | tf_op jit(solution)/shard_map/ppermute | solution.py:386
  33.4 4.5 %collective-permute-start.20 = (f32[2,512]{1,0:T(2,128)S(1)}, f32[2,512]{1,0:T(2,128)S(1)}, u32[]{:S(2)}, u32[]{:S(2)}) collective-permute-start(f32[2,512]{1,0:T(2,128)S(1)} %get-tuple-element.92.refs_0_), channel_id=1, source_target_pairs={{0,24},{8,16},{16,8},{24,0},{1,25},{9,17},{17,9},{25,1},{2,26},{10... | collective-permute-start | bytes 12296 | tf_op jit(solution)/shard_map/ppermute | solution.py:386
  38.8 4.3 %collective-permute-start.25 = (bf16[64,512]{1,0:T(8,128)(2,1)S(1)}, bf16[64,512]{1,0:T(8,128)(2,1)S(1)}, u32[]{:S(2)}, u32[]{:S(2)}) collective-permute-start(bf16[64,512]{1,0:T(8,128)(2,1)S(1)} %get-tuple-element.109), channel_id=1, source_target_pairs={{0,2},{1,3},{2,0},{3,1},{4,6},{5,7},{6,4},{7,5},{8,10},{9,11},{10,... | collective-permute-start | bytes 196616 | tf_op jit(solution)/shard_map/ppermute | solution.py:368
  39.4 7.2 %collective-permute-start.23 = (bf16[64,512]{1,0:T(8,128)(2,1)S(1)}, bf16[64,512]{1,0:T(8,128)(2,1)S(1)}, u32[]{:S(2)}, u32[]{:S(2)}) collective-permute-start(bf16[64,512]{1,0:T(8,128)(2,1)S(1)} %get-tuple-element.105), channel_id=1, source_target_pairs={{0,2},{1,3},{2,0},{3,1},{4,6},{5,7},{6,4},{7,5},{8,10},{9,11},{10,... | collective-permute-start | bytes 196616 | tf_op jit(solution)/shard_map/ppermute | solution.py:368
  40.9 6.4 %collective-permute-start.27 = (bf16[64,512]{1,0:T(8,128)(2,1)S(1)}, bf16[64,512]{1,0:T(8,128)(2,1)S(1)}, u32[]{:S(2)}, u32[]{:S(2)}) collective-permute-start(bf16[64,512]{1,0:T(8,128)(2,1)S(1)} %get-tuple-element.113), channel_id=1, source_target_pairs={{0,2},{1,3},{2,0},{3,1},{4,6},{5,7},{6,4},{7,5},{8,10},{9,11},{10,... | collective-permute-start | bytes 196616 | tf_op jit(solution)/shard_map/ppermute | solution.py:368
  43.2 7.7 %collective-permute-start.26 = (bf16[64,512]{1,0:T(8,128)(2,1)S(1)}, bf16[64,512]{1,0:T(8,128)(2,1)S(1)}, u32[]{:S(2)}, u32[]{:S(2)}) collective-permute-start(bf16[64,512]{1,0:T(8,128)(2,1)S(1)} %carry.10.refs_0_), channel_id=1, source_target_pairs={{0,4},{1,5},{2,6},{3,7},{4,0},{5,1},{6,2},{7,3},{8,12},{9,13},{10,... | collective-permute-start | bytes 196616 | tf_op jit(solution)/shard_map/ppermute | solution.py:368
  46.6 5.7 %collective-permute-start.24 = (bf16[64,512]{1,0:T(8,128)(2,1)S(1)}, bf16[64,512]{1,0:T(8,128)(2,1)S(1)}, u32[]{:S(2)}, u32[]{:S(2)}) collective-permute-start(bf16[64,512]{1,0:T(8,128)(2,1)S(1)} %carry.9.refs_0_), channel_id=1, source_target_pairs={{0,4},{1,5},{2,6},{3,7},{4,0},{5,1},{6,2},{7,3},{8,12},{9,13},{10,... | collective-permute-start | bytes 196616 | tf_op jit(solution)/shard_map/ppermute | solution.py:368
  47.3 6.4 %collective-permute-start.28 = (bf16[64,512]{1,0:T(8,128)(2,1)S(1)}, bf16[64,512]{1,0:T(8,128)(2,1)S(1)}, u32[]{:S(2)}, u32[]{:S(2)}) collective-permute-start(bf16[64,512]{1,0:T(8,128)(2,1)S(1)} %carry.11.refs_0_), channel_id=1, source_target_pairs={{0,4},{1,5},{2,6},{3,7},{4,0},{5,1},{6,2},{7,3},{8,12},{9,13},{10,... | collective-permute-start | bytes 196616 | tf_op jit(solution)/shard_map/ppermute | solution.py:368
  51.0 4.3 %collective-permute-start.32 = (bf16[64,512]{1,0:T(8,128)(2,1)S(1)}, bf16[64,512]{1,0:T(8,128)(2,1)S(1)}, u32[]{:S(2)}, u32[]{:S(2)}) collective-permute-start(bf16[64,512]{1,0:T(8,128)(2,1)S(1)} %get-tuple-element.117.refs_4_), channel_id=1, source_target_pairs={{0,2},{1,3},{2,0},{3,1},{4,6},{5,7},{6,4},{7,5},{8,10},{9,11},{10,... | collective-permute-start | bytes 196616 | tf_op jit(solution)/shard_map/ppermute | solution.py:368
  52.5 4.3 %collective-permute-start.29 = (bf16[64,512]{1,0:T(8,128)(2,1)S(1)}, bf16[64,512]{1,0:T(8,128)(2,1)S(1)}, u32[]{:S(2)}, u32[]{:S(2)}) collective-permute-start(bf16[64,512]{1,0:T(8,128)(2,1)S(1)} %get-tuple-element.116.refs_0_), channel_id=1, source_target_pairs={{0,2},{1,3},{2,0},{3,1},{4,6},{5,7},{6,4},{7,5},{8,10},{9,11},{10,... | collective-permute-start | bytes 196616 | tf_op jit(solution)/shard_map/ppermute | solution.py:368
  53.9 4.3 %collective-permute-start.35 = (bf16[64,512]{1,0:T(8,128)(2,1)S(1)}, bf16[64,512]{1,0:T(8,128)(2,1)S(1)}, u32[]{:S(2)}, u32[]{:S(2)}) collective-permute-start(bf16[64,512]{1,0:T(8,128)(2,1)S(1)} %get-tuple-element.118.refs_8_), channel_id=1, source_target_pairs={{0,2},{1,3},{2,0},{3,1},{4,6},{5,7},{6,4},{7,5},{8,10},{9,11},{10,... | collective-permute-start | bytes 196616 | tf_op jit(solution)/shard_map/ppermute | solution.py:368
  55.3 3.0 %collective-permute-start.34 = (bf16[64,512]{1,0:T(8,128)(2,1)S(1)}, bf16[64,512]{1,0:T(8,128)(2,1)S(1)}, u32[]{:S(2)}, u32[]{:S(2)}) collective-permute-start(bf16[64,512]{1,0:T(8,128)(2,1)S(1)} %collective-permute-done.32.refs_5_), channel_id=1, source_target_pairs={{0,1},{1,0},{2,3},{3,2},{4,5},{5,4},{6,7},{7,6},{8,9},{9,8},{10,11... | collective-permute-start | bytes 196616 | tf_op jit(solution)/shard_map/ppermute | solution.py:379
  56.8 2.0 %collective-permute-start.30 = (bf16[64,512]{1,0:T(8,128)(2,1)S(1)}, bf16[64,512]{1,0:T(8,128)(2,1)S(1)}, u32[]{:S(2)}, u32[]{:S(2)}) collective-permute-start(bf16[64,512]{1,0:T(8,128)(2,1)S(1)} %get-tuple-element.116.refs_0_), channel_id=1, source_target_pairs={{0,1},{1,0},{2,3},{3,2},{4,5},{5,4},{6,7},{7,6},{8,9},{9,8},{10,11... | collective-permute-start | bytes 196616 | tf_op jit(solution)/shard_map/ppermute | solution.py:379
  56.8 2.0 %collective-permute-start.33 = (bf16[64,512]{1,0:T(8,128)(2,1)S(1)}, bf16[64,512]{1,0:T(8,128)(2,1)S(1)}, u32[]{:S(2)}, u32[]{:S(2)}) collective-permute-start(bf16[64,512]{1,0:T(8,128)(2,1)S(1)} %get-tuple-element.117.refs_4_), channel_id=1, source_target_pairs={{0,1},{1,0},{2,3},{3,2},{4,5},{5,4},{6,7},{7,6},{8,9},{9,8},{10,11... | collective-permute-start | bytes 196616 | tf_op jit(solution)/shard_map/ppermute | solution.py:379
  57.3 1.5 %collective-permute-start.36 = (bf16[64,512]{1,0:T(8,128)(2,1)S(1)}, bf16[64,512]{1,0:T(8,128)(2,1)S(1)}, u32[]{:S(2)}, u32[]{:S(2)}) collective-permute-start(bf16[64,512]{1,0:T(8,128)(2,1)S(1)} %get-tuple-element.118.refs_8_), channel_id=1, source_target_pairs={{0,1},{1,0},{2,3},{3,2},{4,5},{5,4},{6,7},{7,6},{8,9},{9,8},{10,11... | collective-permute-start | bytes 196616 | tf_op jit(solution)/shard_map/ppermute | solution.py:379
  58.3 1.3 %collective-permute-start.31 = (bf16[64,512]{1,0:T(8,128)(2,1)S(1)}, bf16[64,512]{1,0:T(8,128)(2,1)S(1)}, u32[]{:S(2)}, u32[]{:S(2)}) collective-permute-start(bf16[64,512]{1,0:T(8,128)(2,1)S(1)} %collective-permute-done.29.refs_1_), channel_id=1, source_target_pairs={{0,1},{1,0},{2,3},{3,2},{4,5},{5,4},{6,7},{7,6},{8,9},{9,8},{10,11... | collective-permute-start | bytes 196616 | tf_op jit(solution)/shard_map/ppermute | solution.py:379
  58.3 1.4 %collective-permute-start.37 = (bf16[64,512]{1,0:T(8,128)(2,1)S(1)}, bf16[64,512]{1,0:T(8,128)(2,1)S(1)}, u32[]{:S(2)}, u32[]{:S(2)}) collective-permute-start(bf16[64,512]{1,0:T(8,128)(2,1)S(1)} %collective-permute-done.35.refs_9_), channel_id=1, source_target_pairs={{0,1},{1,0},{2,3},{3,2},{4,5},{5,4},{6,7},{7,6},{8,9},{9,8},{10,11... | collective-permute-start | bytes 196616 | tf_op jit(solution)/shard_map/ppermute | solution.py:379
  61.1 7.6 %collective-permute-start.38 = (bf16[96,512]{1,0:T(8,128)(2,1)S(1)}, bf16[96,512]{1,0:T(8,128)(2,1)S(1)}, u32[]{:S(2)}, u32[]{:S(2)}) collective-permute-start(bf16[96,512]{1,0:T(8,128)(2,1)S(1)} %get-tuple-element.138), channel_id=1, source_target_pairs={{0,6},{1,7},{2,4},{3,5},{4,2},{5,3},{6,0},{7,1},{8,14},{9,15},{10,... | collective-permute-start | bytes 294920 | tf_op jit(solution)/shard_map/ppermute | solution.py:363
  63.4 9.4 %collective-permute-start.39 = (bf16[96,512]{1,0:T(8,128)(2,1)S(1)}, bf16[96,512]{1,0:T(8,128)(2,1)S(1)}, u32[]{:S(2)}, u32[]{:S(2)}) collective-permute-start(bf16[96,512]{1,0:T(8,128)(2,1)S(1)} %get-tuple-element.139), channel_id=1, source_target_pairs={{0,4},{1,5},{2,6},{3,7},{4,0},{5,1},{6,2},{7,3},{8,12},{9,13},{10,... | collective-permute-start | bytes 294920 | tf_op jit(solution)/shard_map/ppermute | solution.py:363
  63.5 9.3 %collective-permute-start.40 = (bf16[96,512]{1,0:T(8,128)(2,1)S(1)}, bf16[96,512]{1,0:T(8,128)(2,1)S(1)}, u32[]{:S(2)}, u32[]{:S(2)}) collective-permute-start(bf16[96,512]{1,0:T(8,128)(2,1)S(1)} %get-tuple-element.140), channel_id=1, source_target_pairs={{0,2},{1,3},{2,0},{3,1},{4,6},{5,7},{6,4},{7,5},{8,10},{9,11},{10,... | collective-permute-start | bytes 294920 | tf_op jit(solution)/shard_map/ppermute | solution.py:363
  (1 other events, 1.0 us)

commit v9 on v8

--- a/solution.py
+++ b/solution.py
@@ -294,10 +294,10 @@
 
 
 def back_kernel(chips, folds, heads, *refs):
-    parts, refs = refs[:heads], refs[heads:]
-    sums = parts[0][...]
-    for part in parts[1:]:
-        sums = sums + part[...]
+    total, other, refs = refs[0][...], refs[1][...], refs[2:]
+    own = total.shape[1] // CORES
+    other = jnp.concatenate([other[:, own:], other[:, :own]], axis=1)
+    sums = jnp.where(lax.axis_index("tok") % CORES == 0, other, total)
     f2t, output, weighted, mixed, up_slope, silu, qo, qx, gate_back, up_back = refs[:10]
     outs, (gate, up, down) = refs[10:16], refs[16:]
     width = heads * output.shape[0]
@@ -381,12 +381,17 @@
     return [x for part in parts for x in part]
 
 
-def head_parts(part, heads):
-    got = [
-        lax.ppermute(part, "head", [(h, partner(h, step, heads)) for h in range(heads)])
-        for step in reversed(range(1, heads))
-    ]
-    return [part, *got]
+def head_sums(part, count, heads):
+    total, step = part, 1
+    while step < heads:
+        perm = [
+            (h * count + t, (h ^ step if t % CORES else h) * count + t)
+            for h in range(heads)
+            for t in range(count)
+        ]
+        total = total + lax.ppermute(total, ("head", "tok"), perm)
+        step *= 2
+    return [total, lax.ppermute(total, "tok", core_perm(count))]
 
 
 def over_chips(blocks, count):
@@ -457,7 +462,7 @@
     gain = out_gain[None, :]
     inputs = query_input, key_input, value_input, out_grad, rates, gain, w1, w3, w2
 
-    if g % ROW_TILE or d % g or dh * g != fh * d or chips & (chips - 1) or chips < 2:
+    if g % ROW_TILE or d % g or dh * g != fh * d or chips & (chips - 1) or chips < 2 or heads & (heads - 1):
         query_grad, key_grad, value_grad, *results = by_blocks(inputs, tok, count, heads)
     else:
         query_grad, key_grad, value_grad, *results = by_line(inputs, chips, heads)
@@ -528,7 +533,7 @@
         functools.partial(back_kernel, chips, folds, heads),
         [own_hidden] * 2 + half_shares,
         (
-            *head_parts(part, heads),
+            *head_sums(part, count, heads),
             f2t, output, weighted, q_mixed, q_slope, q_silu, query_input, query_other,
         ),
         sums_scratch,

time: 73.7 us -> 78.1 us (1.060)
  starting transfers between devices: 38.2 us -> 43.8 us
  waiting for transfers between devices: 22.9 us -> 21.5 us
    ppermute x3, starting transfers between devices: 3.55 us -> 8.79 us  [the longest x1 7.47 us: head_sums(): return [total, lax.ppermute(total, 'tok', core_perm(count))]]
    ppermute x3, waiting for transfers between devices: 4.23 us -> 0.83 us  [the longest x1 0.82 us: head_sums(): return [total, lax.ppermute(total, 'tok', core_perm(count))]]
    ppermute x18, waiting for transfers between devices: 11.7 us -> 13.5 us  [to_chip(): return lax.ppermute(x, 'tok', chip_perm(chips * CORES, step))]
  transfers between devices with their start and end apart: 41 -> 41, of which waited for: 23 -> 22; matrix products, arithmetic and copies ran while one was open for 2% -> 2% of each run, Pallas kernels for 8% -> 7%
where the time goes in v9:
time: 78.1 us; the launch traced here: 77.9 us
  starting transfers between devices  43.8 us (56%)
  waiting for transfers between devices  21.5 us (28%)
  Pallas kernels  9.57 us (12%)
  local copies, waits for them, and re-layouts  2.12 us (3%)
  between operations  0.9 us (1%)
    ppermute x18, starting transfers between devices, to_chip(): return lax.ppermute(x, 'tok', chip_perm(chips * CORES, step))  27.3 us
    ppermute x18, waiting for transfers between devices, to_chip(): return lax.ppermute(x, 'tok', chip_perm(chips * CORES, step))  13.5 us
    pallas_call x20, Pallas kernels, call(): pl.pallas_call(kernel, out_shape=[jax.ShapeDtypeStruct(s, t) for s, t in...  9.57 us
    ppermute x1, starting transfers between devices, head_sums(): return [total, lax.ppermute(total, 'tok', core_perm(count))]  7.47 us
    ppermute x3, waiting for transfers between devices, exchange(): lax.ppermute(pieces[s], 'tok', chip_perm(count, s))  4.87 us
    ppermute x3, starting transfers between devices, exchange(): lax.ppermute(pieces[s], 'tok', chip_perm(count, s))  4.45 us
    ppermute x12, waiting for transfers between devices, from_owners(): cross = lambda x: lax.ppermute(x, 'tok', core_perm(chips * CORES))  2.25 us
    unnamed x18, local copies, waits for them, and re-layouts  2.12 us
  transfers between devices with their start and end apart: 41, of which 22 were waited for; matrix products, arithmetic and copies ran while one was open for 2% of the time, Pallas kernels for 7%

profile of v9, /device:TPU:0, one launch (start us, length us, event | category | flops | bytes accessed | tf_op | source)
XLA Modules:
  0.0 77.9 jit_solution(9868587869847375663)
XLA Ops:
  0.6 0.5 collective-permute-start.1
  1.8 1.1 %copy.15 = bf16[1,512,256]{1,2,0:T(8,128)(2,1)S(1)} copy(bf16[1,512,256]{2,1,0:T(8,128)(2,1)} %param.15) | data formatting | bytes 524288 | tf_op args[6]
  3.1 0.7 copy-done.1
  4.0 1.2 %update.1 = (f32[64,512]{1,0:T(8,128)S(1)}, f32[64,512]{1,0:T(8,128)S(1)}, f32[64,512]{1,0:T(8,128)S(1)}, bf16[64,512]{1,0:T(8,128)(2,1)S(1)}, bf16[64,512]{1,0:T(8,128)(2,1)S(1)}, /*index=5*/bf16[64,512]{1,0:T(8,128)(2,1)S(1)}) custom-call(bf16[256,512]{1,0:T(8,128)(2,1)S(1)} %copy-done.2, bf16[256,512]{1,0:T(8,128)(2,1)S(1)} %collective-permute-done.kx.refs_13_, ...), custom_call_target="tpu_custom_call" | custom-call | flops 805306368 | bytes 1837056 | tf_op jit(solution)/shard_map/update/pallas_call | solution.py:345
  5.2 3.1 %collective-permute-start.8 = (bf16[64,512]{1,0:T(8,128)(2,1)S(1)}, bf16[64,512]{1,0:T(8,128)(2,1)S(1)}, u32[]{:S(2)}, u32[]{:S(2)}) collective-permute-start(bf16[64,512]{1,0:T(8,128)(2,1)S(1)} %get-tuple-element.85), channel_id=1, source_target_pairs={{0,2},{1,3},{2,0},{3,1},{4,6},{5,7},{6,4},{7,5},{8,10},{9,11},{10,... | collective-permute-start | bytes 196616 | tf_op jit(solution)/shard_map/ppermute | solution.py:368
  8.4 1.9 %collective-permute-start.6 = (bf16[64,512]{1,0:T(8,128)(2,1)S(1)}, bf16[64,512]{1,0:T(8,128)(2,1)S(1)}, u32[]{:S(2)}, u32[]{:S(2)}) collective-permute-start(bf16[64,512]{1,0:T(8,128)(2,1)S(1)} %get-tuple-element.81), channel_id=1, source_target_pairs={{0,2},{1,3},{2,0},{3,1},{4,6},{5,7},{6,4},{7,5},{8,10},{9,11},{10,... | collective-permute-start | bytes 196616 | tf_op jit(solution)/shard_map/ppermute | solution.py:368
  10.6 3.0 %collective-permute-start.9 = (bf16[64,512]{1,0:T(8,128)(2,1)S(1)}, bf16[64,512]{1,0:T(8,128)(2,1)S(1)}, u32[]{:S(2)}, u32[]{:S(2)}) collective-permute-start(bf16[64,512]{1,0:T(8,128)(2,1)S(1)} %carry.8.refs_0_), channel_id=1, source_target_pairs={{0,4},{1,5},{2,6},{3,7},{4,0},{5,1},{6,2},{7,3},{8,12},{9,13},{10,... | collective-permute-start | bytes 196616 | tf_op jit(solution)/shard_map/ppermute | solution.py:368
  13.6 2.2 %collective-permute-start.5 = (bf16[64,512]{1,0:T(8,128)(2,1)S(1)}, bf16[64,512]{1,0:T(8,128)(2,1)S(1)}, u32[]{:S(2)}, u32[]{:S(2)}) collective-permute-start(bf16[64,512]{1,0:T(8,128)(2,1)S(1)} %carry.6.refs_0_), channel_id=1, source_target_pairs={{0,4},{1,5},{2,6},{3,7},{4,0},{5,1},{6,2},{7,3},{8,12},{9,13},{10,... | collective-permute-start | bytes 196616 | tf_op jit(solution)/shard_map/ppermute | solution.py:368
  15.8 1.4 %collective-permute-start.7 = (bf16[64,512]{1,0:T(8,128)(2,1)S(1)}, bf16[64,512]{1,0:T(8,128)(2,1)S(1)}, u32[]{:S(2)}, u32[]{:S(2)}) collective-permute-start(bf16[64,512]{1,0:T(8,128)(2,1)S(1)} %carry.7.refs_0_), channel_id=1, source_target_pairs={{0,4},{1,5},{2,6},{3,7},{4,0},{5,1},{6,2},{7,3},{8,12},{9,13},{10,... | collective-permute-start | bytes 196616 | tf_op jit(solution)/shard_map/ppermute | solution.py:368
  17.2 1.1 %saved.1 = (bf16[512,512]{1,0:T(8,128)(2,1)S(1)}, f32[256,512]{1,0:T(8,128)S(1)}, f32[256,512]{1,0:T(8,128)S(1)}, f32[256,512]{1,0:T(8,128)S(1)}, f32[256,512]{1...) custom-call(bf16[256,512]{1,0:T(8,128)(2,1)S(1)} %copy-done.2, ...), custom_call_target="tpu_custom_call" | custom-call | flops 402653184 | bytes 2363392 | tf_op jit(solution)/shard_map/saved/pallas_call | solution.py:345
  18.5 2.6 %collective-permute-start.16 = (bf16[64,512]{1,0:T(8,128)(2,1)S(1)}, bf16[64,512]{1,0:T(8,128)(2,1)S(1)}, u32[]{:S(2)}, u32[]{:S(2)}) collective-permute-start(bf16[64,512]{1,0:T(8,128)(2,1)S(1)} %get-tuple-element.90.refs_8_), channel_id=1, source_target_pairs={{0,2},{1,3},{2,0},{3,1},{4,6},{5,7},{6,4},{7,5},{8,10},{9,11},{10,... | collective-permute-start | bytes 196616 | tf_op jit(solution)/shard_map/ppermute | solution.py:368
  21.4 1.2 %collective-permute-start.10 = (bf16[64,512]{1,0:T(8,128)(2,1)S(1)}, bf16[64,512]{1,0:T(8,128)(2,1)S(1)}, u32[]{:S(2)}, u32[]{:S(2)}) collective-permute-start(bf16[64,512]{1,0:T(8,128)(2,1)S(1)} %get-tuple-element.88.refs_0_), channel_id=1, source_target_pairs={{0,2},{1,3},{2,0},{3,1},{4,6},{5,7},{6,4},{7,5},{8,10},{9,11},{10,... | collective-permute-start | bytes 196616 | tf_op jit(solution)/shard_map/ppermute | solution.py:368
  22.6 0.5 collective-permute-done.7.refs_1_
  23.2 0.5 collective-permute-start.13
  23.7 0.7 collective-permute-done.16.refs_9_
  24.4 1.5 %collective-permute-done.10.refs_1_ = bf16[64,512]{1,0:T(8,128)(2,1)S(1)} collective-permute-done((bf16[64,512]{1,0:T(8,128)(2,1)S(1)}, bf16[64,512]{1,0:T(8,128)(2,1)S(1)}, u32[]{:S(2)}, u32[]{:S(2)}) %collective-permute-start.10) | collective-permute-done | bytes 65568 | tf_op jit(solution)/shard_map/ppermute | solution.py:368
  25.9 0.5 collective-permute-start.14
  26.4 1.1 %collective-permute-done.13.refs_5_ = bf16[64,512]{1,0:T(8,128)(2,1)S(1)} collective-permute-done((bf16[64,512]{1,0:T(8,128)(2,1)S(1)}, bf16[64,512]{1,0:T(8,128)(2,1)S(1)}, u32[]{:S(2)}, u32[]{:S(2)}) %collective-permute-start.13) | collective-permute-done | bytes 65568 | tf_op jit(solution)/shard_map/ppermute | solution.py:368
  27.5 0.5 collective-permute-start.17
  28.1 0.7 collective-permute-done.15.refs_7_
  29.3 0.8 %apply.1 = (bf16[256,512]{1,0:T(8,128)(2,1)S(1)}, bf16[256,512]{1,0:T(8,128)(2,1)S(1)}, bf16[512,256]{1,0:T(8,128)(2,1)S(1)}, f32[512,512]{1,0:T(8,128)S(1)}, bf...) custom-call(bf16[64,512]{1,0:T(8,128)(2,1)S(1)} %get-tuple-element.88.refs_0, ...), custom_call_target="tpu_custom_call" | custom-call | flops 402653184 | bytes 2359296 | tf_op jit(solution)/shard_map/apply/pallas_call | solution.py:345
  30.1 0.7 collective-permute-start.20
  30.8 0.7 collective-permute-start.21
  31.5 7.5 %collective-permute-start.22 = (f32[2,512]{1,0:T(2,128)S(1)}, f32[2,512]{1,0:T(2,128)S(1)}, u32[]{:S(2)}, u32[]{:S(2)}) collective-permute-start(f32[2,512]{1,0:T(2,128)S(1)} %add.7.refs_0_), channel_id=1, source_target_pairs={{0,1},{1,0},{2,3},{3,2},{4,5},{5,4},{6,7},{7,6},{8,9},{9,8},{10,11... | collective-permute-start | bytes 12296 | tf_op jit(solution)/shard_map/ppermute | solution.py:394
  39.0 0.8 %collective-permute-done.22.refs_1_ = f32[2,512]{1,0:T(2,128)S(1)} collective-permute-done((f32[2,512]{1,0:T(2,128)S(1)}, f32[2,512]{1,0:T(2,128)S(1)}, u32[]{:S(2)}, u32[]{:S(2)}) %collective-permute-start.22) | collective-permute-done | bytes 4128 | tf_op jit(solution)/shard_map/ppermute | solution.py:394
  39.8 0.9 %apply_back.1 = (bf16[256,256]{1,0:T(8,128)(2,1)S(1)}, bf16[256,256]{1,0:T(8,128)(2,1)S(1)}, f32[64,512]{1,0:T(8,128)S(1)}, f32[64,512]{1,0:T(8,128)S(1)}, f32[6...) custom-call(f32[2,512]{1,0:T(2,128)S(1)} %add.7.refs_0_, ...), custom_call_target="tpu_custom_call" | custom-call | flops 536870912 | bytes 4202496 | tf_op jit(solution)/shard_map/apply_back/pallas_call | solution.py:345
  40.7 0.6 collective-permute-start.25
  41.3 1.5 %collective-permute-start.23 = (bf16[64,512]{1,0:T(8,128)(2,1)S(1)}, bf16[64,512]{1,0:T(8,128)(2,1)S(1)}, u32[]{:S(2)}, u32[]{:S(2)}) collective-permute-start(bf16[64,512]{1,0:T(8,128)(2,1)S(1)} %get-tuple-element.105), channel_id=1, source_target_pairs={{0,2},{1,3},{2,0},{3,1},{4,6},{5,7},{6,4},{7,5},{8,10},{9,11},{10,... | collective-permute-start | bytes 196616 | tf_op jit(solution)/shard_map/ppermute | solution.py:368
  42.8 0.5 collective-permute-start.27
  43.4 2.4 %collective-permute-done.25.got = bf16[64,512]{1,0:T(8,128)(2,1)S(1)} collective-permute-done((bf16[64,512]{1,0:T(8,128)(2,1)S(1)}, bf16[64,512]{1,0:T(8,128)(2,1)S(1)}, u32[]{:S(2)}, u32[]{:S(2)}) %collective-permute-start.25) | collective-permute-done | bytes 65568 | tf_op jit(solution)/shard_map/ppermute | solution.py:368
  45.7 3.0 %collective-permute-start.26 = (bf16[64,512]{1,0:T(8,128)(2,1)S(1)}, bf16[64,512]{1,0:T(8,128)(2,1)S(1)}, u32[]{:S(2)}, u32[]{:S(2)}) collective-permute-start(bf16[64,512]{1,0:T(8,128)(2,1)S(1)} %carry.10.refs_0_), channel_id=1, source_target_pairs={{0,4},{1,5},{2,6},{3,7},{4,0},{5,1},{6,2},{7,3},{8,12},{9,13},{10,... | collective-permute-start | bytes 196616 | tf_op jit(solution)/shard_map/ppermute | solution.py:368
  48.8 1.4 %collective-permute-start.24 = (bf16[64,512]{1,0:T(8,128)(2,1)S(1)}, bf16[64,512]{1,0:T(8,128)(2,1)S(1)}, u32[]{:S(2)}, u32[]{:S(2)}) collective-permute-start(bf16[64,512]{1,0:T(8,128)(2,1)S(1)} %carry.9.refs_0_), channel_id=1, source_target_pairs={{0,4},{1,5},{2,6},{3,7},{4,0},{5,1},{6,2},{7,3},{8,12},{9,13},{10,... | collective-permute-start | bytes 196616 | tf_op jit(solution)/shard_map/ppermute | solution.py:368
  50.2 1.7 %collective-permute-start.28 = (bf16[64,512]{1,0:T(8,128)(2,1)S(1)}, bf16[64,512]{1,0:T(8,128)(2,1)S(1)}, u32[]{:S(2)}, u32[]{:S(2)}) collective-permute-start(bf16[64,512]{1,0:T(8,128)(2,1)S(1)} %carry.11.refs_0_), channel_id=1, source_target_pairs={{0,4},{1,5},{2,6},{3,7},{4,0},{5,1},{6,2},{7,3},{8,12},{9,13},{10,... | collective-permute-start | bytes 196616 | tf_op jit(solution)/shard_map/ppermute | solution.py:368
  51.8 2.4 %collective-permute-done.26.refs_1_ = bf16[64,512]{1,0:T(8,128)(2,1)S(1)} collective-permute-done((bf16[64,512]{1,0:T(8,128)(2,1)S(1)}, bf16[64,512]{1,0:T(8,128)(2,1)S(1)}, u32[]{:S(2)}, u32[]{:S(2)}) %collective-permute-start.26) | collective-permute-done | bytes 65568 | tf_op jit(solution)/shard_map/ppermute | solution.py:368
  54.4 1.4 %collective-permute-start.32 = (bf16[64,512]{1,0:T(8,128)(2,1)S(1)}, bf16[64,512]{1,0:T(8,128)(2,1)S(1)}, u32[]{:S(2)}, u32[]{:S(2)}) collective-permute-start(bf16[64,512]{1,0:T(8,128)(2,1)S(1)} %get-tuple-element.117.refs_4_), channel_id=1, source_target_pairs={{0,2},{1,3},{2,0},{3,1},{4,6},{5,7},{6,4},{7,5},{8,10},{9,11},{10,... | collective-permute-start | bytes 196616 | tf_op jit(solution)/shard_map/ppermute | solution.py:368
  55.8 0.8 %collective-permute-done.24.refs_1_ = bf16[64,512]{1,0:T(8,128)(2,1)S(1)} collective-permute-done((bf16[64,512]{1,0:T(8,128)(2,1)S(1)}, bf16[64,512]{1,0:T(8,128)(2,1)S(1)}, u32[]{:S(2)}, u32[]{:S(2)}) %collective-permute-start.24) | collective-permute-done | bytes 65568 | tf_op jit(solution)/shard_map/ppermute | solution.py:368
  56.9 0.8 %collective-permute-done.28.refs_1_ = bf16[64,512]{1,0:T(8,128)(2,1)S(1)} collective-permute-done((bf16[64,512]{1,0:T(8,128)(2,1)S(1)}, bf16[64,512]{1,0:T(8,128)(2,1)S(1)}, u32[]{:S(2)}, u32[]{:S(2)}) %collective-permute-start.28) | collective-permute-done | bytes 65568 | tf_op jit(solution)/shard_map/ppermute | solution.py:368
  57.9 1.2 %collective-permute-start.35 = (bf16[64,512]{1,0:T(8,128)(2,1)S(1)}, bf16[64,512]{1,0:T(8,128)(2,1)S(1)}, u32[]{:S(2)}, u32[]{:S(2)}) collective-permute-start(bf16[64,512]{1,0:T(8,128)(2,1)S(1)} %get-tuple-element.118.refs_8_), channel_id=1, source_target_pairs={{0,2},{1,3},{2,0},{3,1},{4,6},{5,7},{6,4},{7,5},{8,10},{9,11},{10,... | collective-permute-start | bytes 196616 | tf_op jit(solution)/shard_map/ppermute | solution.py:368
  59.2 2.6 %collective-permute-done.29.refs_1_ = bf16[64,512]{1,0:T(8,128)(2,1)S(1)} collective-permute-done((bf16[64,512]{1,0:T(8,128)(2,1)S(1)}, bf16[64,512]{1,0:T(8,128)(2,1)S(1)}, u32[]{:S(2)}, u32[]{:S(2)}) %collective-permute-start.29) | collective-permute-done | bytes 65568 | tf_op jit(solution)/shard_map/ppermute | solution.py:368
  61.7 0.5 collective-permute-start.33
  64.0 1.4 %second_adjoint.1 = (bf16[256,512]{1,0:T(8,128)(2,1)S(1)}, bf16[256,512]{1,0:T(8,128)(2,1)S(1)}, bf16[512,256]{1,0:T(8,128)(2,1)S(1)}, bf16[256,256]{1,0:T(8,128...) custom-call(bf16[64,512]{1,0:T(8,128)(2,1)S(1)} %get-tuple-element.1, ...), custom_call_target="tpu_custom_call" | custom-call | flops 805306368 | bytes 3932160 | tf_op jit(solution)/shard_map/second_adjoint/pallas_call | solution.py:345
  65.5 3.0 %collective-permute-start.38 = (bf16[96,512]{1,0:T(8,128)(2,1)S(1)}, bf16[96,512]{1,0:T(8,128)(2,1)S(1)}, u32[]{:S(2)}, u32[]{:S(2)}) collective-permute-start(bf16[96,512]{1,0:T(8,128)(2,1)S(1)} %get-tuple-element.138), channel_id=1, source_target_pairs={{0,6},{1,7},{2,4},{3,5},{4,2},{5,3},{6,0},{7,1},{8,14},{9,15},{10,... | collective-permute-start | bytes 294920 | tf_op jit(solution)/shard_map/ppermute | solution.py:363
  68.5 1.4 %collective-permute-start.40 = (bf16[96,512]{1,0:T(8,128)(2,1)S(1)}, bf16[96,512]{1,0:T(8,128)(2,1)S(1)}, u32[]{:S(2)}, u32[]{:S(2)}) collective-permute-start(bf16[96,512]{1,0:T(8,128)(2,1)S(1)} %get-tuple-element.140), channel_id=1, source_target_pairs={{0,2},{1,3},{2,0},{3,1},{4,6},{5,7},{6,4},{7,5},{8,10},{9,11},{10,... | collective-permute-start | bytes 294920 | tf_op jit(solution)/shard_map/ppermute | solution.py:363
  69.9 1.0 %query_grad.1 = bf16[256,512]{1,0:T(8,128)(2,1)} custom-call(bf16[256,256]{1,0:T(8,128)(2,1)S(1)} %get-tuple-element.98.gate_back, bf16[256,256]{1,0:T(8,128)(2,1)S(1)} %get-tuple-element.99.up_back, bf16[256,512]{1,0:T(8,128)(2,1)S(1)} %get-tuple-element.100.f1t, bf16[256,512]{1,0:T(8,128)(2,1)S(1)} %get-tuple-element.101.f3t), custom_call_target="tpu_custom_call" | custom-call | flops 134217728 | bytes 786432 | tf_op jit(solution)/shard_map/query_grad/pallas_call | solution.py:345
  71.0 1.4 %token_grads.1 = (bf16[256,512]{1,0:T(8,128)(2,1)}, bf16[256,512]{1,0:T(8,128)(2,1)}) custom-call(f32[1,256]{1,0:T(1,128)S(1)} %bitcast.30, bf16[256,256]{1,0:T(8,128)(2,1)S(1)} %get-tuple-element.102.refs_1_, bf16[256,256]{1,0:T(8,128)(2,1)S(1)} %get-tuple-element.124.refs_2_, bf16[256,256]{1,0:T(8,128)(2,1)S(1)} %get-tuple-element.125.refs_3_, ...), custom_call_target="tpu_custom_call" | custom-call | flops 402653184 | bytes 2360320 | tf_op jit(solution)/shard_map/token_grads/pallas_call | solution.py:345
  72.3 0.8 collective-permute-done.38.refs_4_
  73.1 4.1 %collective-permute-done.39.refs_5_ = bf16[96,512]{1,0:T(8,128)(2,1)S(1)} collective-permute-done((bf16[96,512]{1,0:T(8,128)(2,1)S(1)}, bf16[96,512]{1,0:T(8,128)(2,1)S(1)}, u32[]{:S(2)}, u32[]{:S(2)}) %collective-permute-start.39) | collective-permute-done | bytes 98336 | tf_op jit(solution)/shard_map/ppermute | solution.py:363
  77.2 0.7 owner_result.1
  (74 shorter events, 5.0 us)
Async XLA Ops:
  0.6 1.0 %copy-start.5 = (f32[256,1]{0,1:T(1,128)S(1)}, f32[256,1]{0,1:T(1,128)}, u32[]{:S(2)}) copy-start(f32[256,1]{0,1:T(1,128)} %param.13) | copy-start | bytes 3076
  0.6 2.5 %collective-permute-start.1 = (bf16[256,512]{1,0:T(8,128)(2,1)}, bf16[256,512]{1,0:T(8,128)(2,1)S(1)}, u32[]{:S(2)}, u32[]{:S(2)}) collective-permute-start(bf16[256,512]{1,0:T(8,128)(2,1)} %vo.3), channel_id=1, source_target_pairs={{0,1},{1,0},{2,3},{3,2},{4,5},{5,4},{6,7},{7,6},{8,9},{9,8},{10,11... | collective-permute-start | bytes 786440 | tf_op jit(solution)/shard_map/ppermute | solution.py:488
  1.2 2.0 %collective-permute-start = (bf16[256,512]{1,0:T(8,128)(2,1)}, bf16[256,512]{1,0:T(8,128)(2,1)S(1)}, u32[]{:S(2)}, u32[]{:S(2)}) collective-permute-start(bf16[256,512]{1,0:T(8,128)(2,1)} %refs_12_.3), channel_id=1, source_target_pairs={{0,1},{1,0},{2,3},{3,2},{4,5},{5,4},{6,7},{7,6},{8,9},{9,8},{10,11... | collective-permute-start | bytes 786440 | tf_op jit(solution)/shard_map/ppermute | solution.py:488
  1.2 16.0 %collective-permute-start.3 = (bf16[256,512]{1,0:T(8,128)(2,1)}, bf16[256,512]{1,0:T(8,128)(2,1)S(1)}, u32[]{:S(2)}, u32[]{:S(2)}) collective-permute-start(bf16[256,512]{1,0:T(8,128)(2,1)} %go.1), channel_id=1, source_target_pairs={{0,1},{1,0},{2,3},{3,2},{4,5},{5,4},{6,7},{7,6},{8,9},{9,8},{10,11... | collective-permute-start | bytes 786440 | tf_op jit(solution)/shard_map/ppermute | solution.py:488
  1.7 1.2 %copy-start.7 = (bf16[1,512,256]{2,1,0:T(8,128)(2,1)S(1)}, bf16[1,512,256]{2,1,0:T(8,128)(2,1)}, u32[]{:S(2)}) copy-start(bf16[1,512,256]{2,1,0:T(8,128)(2,1)} %param.16) | copy-start | bytes 786436
  1.7 1.4 %collective-permute-start.2 = (f32[1,256]{1,0:T(1,128)S(1)}, f32[1,256]{1,0:T(1,128)S(1)}, u32[]{:S(2)}, u32[]{:S(2)}) collective-permute-start(f32[1,256]{1,0:T(1,128)S(1)} %bitcast.27), channel_id=1, source_target_pairs={{0,1},{1,0},{2,3},{3,2},{4,5},{5,4},{6,7},{7,6},{8,9},{9,8},{10,11... | collective-permute-start | bytes 3080 | tf_op jit(solution)/shard_map/ppermute | solution.py:488
  1.8 1.4 %copy-start.3 = (bf16[256,512]{1,0:T(8,128)(2,1)S(1)}, bf16[256,512]{1,0:T(8,128)(2,1)}, u32[]{:S(2)}) copy-start(bf16[256,512]{1,0:T(8,128)(2,1)} %vo.3) | copy-start | bytes 786436
  2.9 1.0 %copy-start.2 = (bf16[256,512]{1,0:T(8,128)(2,1)S(1)}, bf16[256,512]{1,0:T(8,128)(2,1)}, u32[]{:S(2)}) copy-start(bf16[256,512]{1,0:T(8,128)(2,1)} %refs_12_.3) | copy-start | bytes 786436
  4.0 4.3 %copy-start = (bf16[256,512]{1,0:T(8,128)(2,1)S(1)}, bf16[256,512]{1,0:T(8,128)(2,1)}, u32[]{:S(2)}) copy-start(bf16[256,512]{1,0:T(8,128)(2,1)} %refs_8_.1) | copy-start | bytes 786436
  5.2 5.4 %collective-permute-start.8 = (bf16[64,512]{1,0:T(8,128)(2,1)S(1)}, bf16[64,512]{1,0:T(8,128)(2,1)S(1)}, u32[]{:S(2)}, u32[]{:S(2)}) collective-permute-start(bf16[64,512]{1,0:T(8,128)(2,1)S(1)} %get-tuple-element.85), channel_id=1, source_target_pairs={{0,2},{1,3},{2,0},{3,1},{4,6},{5,7},{6,4},{7,5},{8,10},{9,11},{10,... | collective-permute-start | bytes 196616 | tf_op jit(solution)/shard_map/ppermute | solution.py:368
  8.2 19.3 %collective-permute-start.19 = (bf16[256,512]{1,0:T(8,128)(2,1)S(1)}, bf16[256,512]{1,0:T(8,128)(2,1)S(1)}, u32[]{:S(2)}, u32[]{:S(2)}) collective-permute-start(bf16[256,512]{1,0:T(8,128)(2,1)S(1)} %copy-done), channel_id=1, source_target_pairs={{0,1},{1,0},{2,3},{3,2},{4,5},{5,4},{6,7},{7,6},{8,9},{9,8},{10,11... | collective-permute-start | bytes 786440 | tf_op jit(solution)/shard_map/ppermute | solution.py:488
  8.2 5.3 %collective-permute-start.4 = (bf16[64,512]{1,0:T(8,128)(2,1)S(1)}, bf16[64,512]{1,0:T(8,128)(2,1)S(1)}, u32[]{:S(2)}, u32[]{:S(2)}) collective-permute-start(bf16[64,512]{1,0:T(8,128)(2,1)S(1)} %get-tuple-element.77), channel_id=1, source_target_pairs={{0,2},{1,3},{2,0},{3,1},{4,6},{5,7},{6,4},{7,5},{8,10},{9,11},{10,... | collective-permute-start | bytes 196616 | tf_op jit(solution)/shard_map/ppermute | solution.py:368
  8.4 7.4 %collective-permute-start.6 = (bf16[64,512]{1,0:T(8,128)(2,1)S(1)}, bf16[64,512]{1,0:T(8,128)(2,1)S(1)}, u32[]{:S(2)}, u32[]{:S(2)}) collective-permute-start(bf16[64,512]{1,0:T(8,128)(2,1)S(1)} %get-tuple-element.81), channel_id=1, source_target_pairs={{0,2},{1,3},{2,0},{3,1},{4,6},{5,7},{6,4},{7,5},{8,10},{9,11},{10,... | collective-permute-start | bytes 196616 | tf_op jit(solution)/shard_map/ppermute | solution.py:368
  10.6 7.7 %collective-permute-start.9 = (bf16[64,512]{1,0:T(8,128)(2,1)S(1)}, bf16[64,512]{1,0:T(8,128)(2,1)S(1)}, u32[]{:S(2)}, u32[]{:S(2)}) collective-permute-start(bf16[64,512]{1,0:T(8,128)(2,1)S(1)} %carry.8.refs_0_), channel_id=1, source_target_pairs={{0,4},{1,5},{2,6},{3,7},{4,0},{5,1},{6,2},{7,3},{8,12},{9,13},{10,... | collective-permute-start | bytes 196616 | tf_op jit(solution)/shard_map/ppermute | solution.py:368
  13.6 3.6 %copy-start.4 = (bf16[256,512]{1,0:T(8,128)(2,1)S(1)}, bf16[256,512]{1,0:T(8,128)(2,1)}, u32[]{:S(2)}) copy-start(bf16[256,512]{1,0:T(8,128)(2,1)} %go.1) | copy-start | bytes 786436
  13.6 7.7 %collective-permute-start.5 = (bf16[64,512]{1,0:T(8,128)(2,1)S(1)}, bf16[64,512]{1,0:T(8,128)(2,1)S(1)}, u32[]{:S(2)}, u32[]{:S(2)}) collective-permute-start(bf16[64,512]{1,0:T(8,128)(2,1)S(1)} %carry.6.refs_0_), channel_id=1, source_target_pairs={{0,4},{1,5},{2,6},{3,7},{4,0},{5,1},{6,2},{7,3},{8,12},{9,13},{10,... | collective-permute-start | bytes 196616 | tf_op jit(solution)/shard_map/ppermute | solution.py:368
  15.8 1.4 %copy-start.6 = (f32[512]{0:T(512)S(1)}, f32[512]{0:T(512)}, u32[]{:S(2)}) copy-start(f32[512]{0:T(512)} %param.14) | copy-start | bytes 6148
  15.8 7.2 %collective-permute-start.7 = (bf16[64,512]{1,0:T(8,128)(2,1)S(1)}, bf16[64,512]{1,0:T(8,128)(2,1)S(1)}, u32[]{:S(2)}, u32[]{:S(2)}) collective-permute-start(bf16[64,512]{1,0:T(8,128)(2,1)S(1)} %carry.7.refs_0_), channel_id=1, source_target_pairs={{0,4},{1,5},{2,6},{3,7},{4,0},{5,1},{6,2},{7,3},{8,12},{9,13},{10,... | collective-permute-start | bytes 196616 | tf_op jit(solution)/shard_map/ppermute | solution.py:368
  18.5 5.9 %collective-permute-start.16 = (bf16[64,512]{1,0:T(8,128)(2,1)S(1)}, bf16[64,512]{1,0:T(8,128)(2,1)S(1)}, u32[]{:S(2)}, u32[]{:S(2)}) collective-permute-start(bf16[64,512]{1,0:T(8,128)(2,1)S(1)} %get-tuple-element.90.refs_8_), channel_id=1, source_target_pairs={{0,2},{1,3},{2,0},{3,1},{4,6},{5,7},{6,4},{7,5},{8,10},{9,11},{10,... | collective-permute-start | bytes 196616 | tf_op jit(solution)/shard_map/ppermute | solution.py:368
  21.4 4.5 %collective-permute-start.10 = (bf16[64,512]{1,0:T(8,128)(2,1)S(1)}, bf16[64,512]{1,0:T(8,128)(2,1)S(1)}, u32[]{:S(2)}, u32[]{:S(2)}) collective-permute-start(bf16[64,512]{1,0:T(8,128)(2,1)S(1)} %get-tuple-element.88.refs_0_), channel_id=1, source_target_pairs={{0,2},{1,3},{2,0},{3,1},{4,6},{5,7},{6,4},{7,5},{8,10},{9,11},{10,... | collective-permute-start | bytes 196616 | tf_op jit(solution)/shard_map/ppermute | solution.py:368
  23.2 4.3 %collective-permute-start.13 = (bf16[64,512]{1,0:T(8,128)(2,1)S(1)}, bf16[64,512]{1,0:T(8,128)(2,1)S(1)}, u32[]{:S(2)}, u32[]{:S(2)}) collective-permute-start(bf16[64,512]{1,0:T(8,128)(2,1)S(1)} %get-tuple-element.89.refs_4_), channel_id=1, source_target_pairs={{0,2},{1,3},{2,0},{3,1},{4,6},{5,7},{6,4},{7,5},{8,10},{9,11},{10,... | collective-permute-start | bytes 196616 | tf_op jit(solution)/shard_map/ppermute | solution.py:368
  24.4 3.6 %collective-permute-start.18 = (bf16[64,512]{1,0:T(8,128)(2,1)S(1)}, bf16[64,512]{1,0:T(8,128)(2,1)S(1)}, u32[]{:S(2)}, u32[]{:S(2)}) collective-permute-start(bf16[64,512]{1,0:T(8,128)(2,1)S(1)} %collective-permute-done.16.refs_9_), channel_id=1, source_target_pairs={{0,1},{1,0},{2,3},{3,2},{4,5},{5,4},{6,7},{7,6},{8,9},{9,8},{10,11... | collective-permute-start | bytes 196616 | tf_op jit(solution)/shard_map/ppermute | solution.py:379
  25.9 2.8 %collective-permute-start.11 = (bf16[64,512]{1,0:T(8,128)(2,1)S(1)}, bf16[64,512]{1,0:T(8,128)(2,1)S(1)}, u32[]{:S(2)}, u32[]{:S(2)}) collective-permute-start(bf16[64,512]{1,0:T(8,128)(2,1)S(1)} %get-tuple-element.88.refs_0_), channel_id=1, source_target_pairs={{0,1},{1,0},{2,3},{3,2},{4,5},{5,4},{6,7},{7,6},{8,9},{9,8},{10,11... | collective-permute-start | bytes 196616 | tf_op jit(solution)/shard_map/ppermute | solution.py:379
  25.9 2.8 %collective-permute-start.14 = (bf16[64,512]{1,0:T(8,128)(2,1)S(1)}, bf16[64,512]{1,0:T(8,128)(2,1)S(1)}, u32[]{:S(2)}, u32[]{:S(2)}) collective-permute-start(bf16[64,512]{1,0:T(8,128)(2,1)S(1)} %get-tuple-element.89.refs_4_), channel_id=1, source_target_pairs={{0,1},{1,0},{2,3},{3,2},{4,5},{5,4},{6,7},{7,6},{8,9},{9,8},{10,11... | collective-permute-start | bytes 196616 | tf_op jit(solution)/shard_map/ppermute | solution.py:379
  27.5 1.3 %collective-permute-start.15 = (bf16[64,512]{1,0:T(8,128)(2,1)S(1)}, bf16[64,512]{1,0:T(8,128)(2,1)S(1)}, u32[]{:S(2)}, u32[]{:S(2)}) collective-permute-start(bf16[64,512]{1,0:T(8,128)(2,1)S(1)} %collective-permute-done.13.refs_5_), channel_id=1, source_target_pairs={{0,1},{1,0},{2,3},{3,2},{4,5},{5,4},{6,7},{7,6},{8,9},{9,8},{10,11... | collective-permute-start | bytes 196616 | tf_op jit(solution)/shard_map/ppermute | solution.py:379
  27.5 1.4 %collective-permute-start.17 = (bf16[64,512]{1,0:T(8,128)(2,1)S(1)}, bf16[64,512]{1,0:T(8,128)(2,1)S(1)}, u32[]{:S(2)}, u32[]{:S(2)}) collective-permute-start(bf16[64,512]{1,0:T(8,128)(2,1)S(1)} %get-tuple-element.90.refs_8_), channel_id=1, source_target_pairs={{0,1},{1,0},{2,3},{3,2},{4,5},{5,4},{6,7},{7,6},{8,9},{9,8},{10,11... | collective-permute-start | bytes 196616 | tf_op jit(solution)/shard_map/ppermute | solution.py:379
  28.0 1.3 %collective-permute-start.12 = (bf16[64,512]{1,0:T(8,128)(2,1)S(1)}, bf16[64,512]{1,0:T(8,128)(2,1)S(1)}, u32[]{:S(2)}, u32[]{:S(2)}) collective-permute-start(bf16[64,512]{1,0:T(8,128)(2,1)S(1)} %collective-permute-done.10.refs_1_), channel_id=1, source_target_pairs={{0,1},{1,0},{2,3},{3,2},{4,5},{5,4},{6,7},{7,6},{8,9},{9,8},{10,11... | collective-permute-start | bytes 196616 | tf_op jit(solution)/shard_map/ppermute | solution.py:379
  30.1 0.7 collective-permute-start.20
  30.8 0.7 collective-permute-start.21
  31.5 8.3 %collective-permute-start.22 = (f32[2,512]{1,0:T(2,128)S(1)}, f32[2,512]{1,0:T(2,128)S(1)}, u32[]{:S(2)}, u32[]{:S(2)}) collective-permute-start(f32[2,512]{1,0:T(2,128)S(1)} %add.7.refs_0_), channel_id=1, source_target_pairs={{0,1},{1,0},{2,3},{3,2},{4,5},{5,4},{6,7},{7,6},{8,9},{9,8},{10,11... | collective-permute-start | bytes 12296 | tf_op jit(solution)/shard_map/ppermute | solution.py:394
  40.7 5.0 %collective-permute-start.25 = (bf16[64,512]{1,0:T(8,128)(2,1)S(1)}, bf16[64,512]{1,0:T(8,128)(2,1)S(1)}, u32[]{:S(2)}, u32[]{:S(2)}) collective-permute-start(bf16[64,512]{1,0:T(8,128)(2,1)S(1)} %get-tuple-element.109), channel_id=1, source_target_pairs={{0,2},{1,3},{2,0},{3,1},{4,6},{5,7},{6,4},{7,5},{8,10},{9,11},{10,... | collective-permute-start | bytes 196616 | tf_op jit(solution)/shard_map/ppermute | solution.py:368
  41.3 7.4 %collective-permute-start.23 = (bf16[64,512]{1,0:T(8,128)(2,1)S(1)}, bf16[64,512]{1,0:T(8,128)(2,1)S(1)}, u32[]{:S(2)}, u32[]{:S(2)}) collective-permute-start(bf16[64,512]{1,0:T(8,128)(2,1)S(1)} %get-tuple-element.105), channel_id=1, source_target_pairs={{0,2},{1,3},{2,0},{3,1},{4,6},{5,7},{6,4},{7,5},{8,10},{9,11},{10,... | collective-permute-start | bytes 196616 | tf_op jit(solution)/shard_map/ppermute | solution.py:368
  42.8 7.3 %collective-permute-start.27 = (bf16[64,512]{1,0:T(8,128)(2,1)S(1)}, bf16[64,512]{1,0:T(8,128)(2,1)S(1)}, u32[]{:S(2)}, u32[]{:S(2)}) collective-permute-start(bf16[64,512]{1,0:T(8,128)(2,1)S(1)} %get-tuple-element.113), channel_id=1, source_target_pairs={{0,2},{1,3},{2,0},{3,1},{4,6},{5,7},{6,4},{7,5},{8,10},{9,11},{10,... | collective-permute-start | bytes 196616 | tf_op jit(solution)/shard_map/ppermute | solution.py:368
  45.7 8.6 %collective-permute-start.26 = (bf16[64,512]{1,0:T(8,128)(2,1)S(1)}, bf16[64,512]{1,0:T(8,128)(2,1)S(1)}, u32[]{:S(2)}, u32[]{:S(2)}) collective-permute-start(bf16[64,512]{1,0:T(8,128)(2,1)S(1)} %carry.10.refs_0_), channel_id=1, source_target_pairs={{0,4},{1,5},{2,6},{3,7},{4,0},{5,1},{6,2},{7,3},{8,12},{9,13},{10,... | collective-permute-start | bytes 196616 | tf_op jit(solution)/shard_map/ppermute | solution.py:368
  48.8 7.9 %collective-permute-start.24 = (bf16[64,512]{1,0:T(8,128)(2,1)S(1)}, bf16[64,512]{1,0:T(8,128)(2,1)S(1)}, u32[]{:S(2)}, u32[]{:S(2)}) collective-permute-start(bf16[64,512]{1,0:T(8,128)(2,1)S(1)} %carry.9.refs_0_), channel_id=1, source_target_pairs={{0,4},{1,5},{2,6},{3,7},{4,0},{5,1},{6,2},{7,3},{8,12},{9,13},{10,... | collective-permute-start | bytes 196616 | tf_op jit(solution)/shard_map/ppermute | solution.py:368
  50.2 7.6 %collective-permute-start.28 = (bf16[64,512]{1,0:T(8,128)(2,1)S(1)}, bf16[64,512]{1,0:T(8,128)(2,1)S(1)}, u32[]{:S(2)}, u32[]{:S(2)}) collective-permute-start(bf16[64,512]{1,0:T(8,128)(2,1)S(1)} %carry.11.refs_0_), channel_id=1, source_target_pairs={{0,4},{1,5},{2,6},{3,7},{4,0},{5,1},{6,2},{7,3},{8,12},{9,13},{10,... | collective-permute-start | bytes 196616 | tf_op jit(solution)/shard_map/ppermute | solution.py:368
  54.4 4.7 %collective-permute-start.32 = (bf16[64,512]{1,0:T(8,128)(2,1)S(1)}, bf16[64,512]{1,0:T(8,128)(2,1)S(1)}, u32[]{:S(2)}, u32[]{:S(2)}) collective-permute-start(bf16[64,512]{1,0:T(8,128)(2,1)S(1)} %get-tuple-element.117.refs_4_), channel_id=1, source_target_pairs={{0,2},{1,3},{2,0},{3,1},{4,6},{5,7},{6,4},{7,5},{8,10},{9,11},{10,... | collective-permute-start | bytes 196616 | tf_op jit(solution)/shard_map/ppermute | solution.py:368
  56.8 4.9 %collective-permute-start.29 = (bf16[64,512]{1,0:T(8,128)(2,1)S(1)}, bf16[64,512]{1,0:T(8,128)(2,1)S(1)}, u32[]{:S(2)}, u32[]{:S(2)}) collective-permute-start(bf16[64,512]{1,0:T(8,128)(2,1)S(1)} %get-tuple-element.116.refs_0_), channel_id=1, source_target_pairs={{0,2},{1,3},{2,0},{3,1},{4,6},{5,7},{6,4},{7,5},{8,10},{9,11},{10,... | collective-permute-start | bytes 196616 | tf_op jit(solution)/shard_map/ppermute | solution.py:368
  57.9 4.5 %collective-permute-start.35 = (bf16[64,512]{1,0:T(8,128)(2,1)S(1)}, bf16[64,512]{1,0:T(8,128)(2,1)S(1)}, u32[]{:S(2)}, u32[]{:S(2)}) collective-permute-start(bf16[64,512]{1,0:T(8,128)(2,1)S(1)} %get-tuple-element.118.refs_8_), channel_id=1, source_target_pairs={{0,2},{1,3},{2,0},{3,1},{4,6},{5,7},{6,4},{7,5},{8,10},{9,11},{10,... | collective-permute-start | bytes 196616 | tf_op jit(solution)/shard_map/ppermute | solution.py:368
  59.2 3.6 %collective-permute-start.34 = (bf16[64,512]{1,0:T(8,128)(2,1)S(1)}, bf16[64,512]{1,0:T(8,128)(2,1)S(1)}, u32[]{:S(2)}, u32[]{:S(2)}) collective-permute-start(bf16[64,512]{1,0:T(8,128)(2,1)S(1)} %collective-permute-done.32.refs_5_), channel_id=1, source_target_pairs={{0,1},{1,0},{2,3},{3,2},{4,5},{5,4},{6,7},{7,6},{8,9},{9,8},{10,11... | collective-permute-start | bytes 196616 | tf_op jit(solution)/shard_map/ppermute | solution.py:379
  61.7 1.3 %collective-permute-start.30 = (bf16[64,512]{1,0:T(8,128)(2,1)S(1)}, bf16[64,512]{1,0:T(8,128)(2,1)S(1)}, u32[]{:S(2)}, u32[]{:S(2)}) collective-permute-start(bf16[64,512]{1,0:T(8,128)(2,1)S(1)} %get-tuple-element.116.refs_0_), channel_id=1, source_target_pairs={{0,1},{1,0},{2,3},{3,2},{4,5},{5,4},{6,7},{7,6},{8,9},{9,8},{10,11... | collective-permute-start | bytes 196616 | tf_op jit(solution)/shard_map/ppermute | solution.py:379
  61.7 1.4 %collective-permute-start.33 = (bf16[64,512]{1,0:T(8,128)(2,1)S(1)}, bf16[64,512]{1,0:T(8,128)(2,1)S(1)}, u32[]{:S(2)}, u32[]{:S(2)}) collective-permute-start(bf16[64,512]{1,0:T(8,128)(2,1)S(1)} %get-tuple-element.117.refs_4_), channel_id=1, source_target_pairs={{0,1},{1,0},{2,3},{3,2},{4,5},{5,4},{6,7},{7,6},{8,9},{9,8},{10,11... | collective-permute-start | bytes 196616 | tf_op jit(solution)/shard_map/ppermute | solution.py:379
  62.3 1.3 %collective-permute-start.36 = (bf16[64,512]{1,0:T(8,128)(2,1)S(1)}, bf16[64,512]{1,0:T(8,128)(2,1)S(1)}, u32[]{:S(2)}, u32[]{:S(2)}) collective-permute-start(bf16[64,512]{1,0:T(8,128)(2,1)S(1)} %get-tuple-element.118.refs_8_), channel_id=1, source_target_pairs={{0,1},{1,0},{2,3},{3,2},{4,5},{5,4},{6,7},{7,6},{8,9},{9,8},{10,11... | collective-permute-start | bytes 196616 | tf_op jit(solution)/shard_map/ppermute | solution.py:379
  62.4 1.3 %collective-permute-start.31 = (bf16[64,512]{1,0:T(8,128)(2,1)S(1)}, bf16[64,512]{1,0:T(8,128)(2,1)S(1)}, u32[]{:S(2)}, u32[]{:S(2)}) collective-permute-start(bf16[64,512]{1,0:T(8,128)(2,1)S(1)} %collective-permute-done.29.refs_1_), channel_id=1, source_target_pairs={{0,1},{1,0},{2,3},{3,2},{4,5},{5,4},{6,7},{7,6},{8,9},{9,8},{10,11... | collective-permute-start | bytes 196616 | tf_op jit(solution)/shard_map/ppermute | solution.py:379
  62.8 1.3 %collective-permute-start.37 = (bf16[64,512]{1,0:T(8,128)(2,1)S(1)}, bf16[64,512]{1,0:T(8,128)(2,1)S(1)}, u32[]{:S(2)}, u32[]{:S(2)}) collective-permute-start(bf16[64,512]{1,0:T(8,128)(2,1)S(1)} %collective-permute-done.35.refs_9_), channel_id=1, source_target_pairs={{0,1},{1,0},{2,3},{3,2},{4,5},{5,4},{6,7},{7,6},{8,9},{9,8},{10,11... | collective-permute-start | bytes 196616 | tf_op jit(solution)/shard_map/ppermute | solution.py:379
  65.5 7.6 %collective-permute-start.38 = (bf16[96,512]{1,0:T(8,128)(2,1)S(1)}, bf16[96,512]{1,0:T(8,128)(2,1)S(1)}, u32[]{:S(2)}, u32[]{:S(2)}) collective-permute-start(bf16[96,512]{1,0:T(8,128)(2,1)S(1)} %get-tuple-element.138), channel_id=1, source_target_pairs={{0,6},{1,7},{2,4},{3,5},{4,2},{5,3},{6,0},{7,1},{8,14},{9,15},{10,... | collective-permute-start | bytes 294920 | tf_op jit(solution)/shard_map/ppermute | solution.py:363
  68.5 8.7 %collective-permute-start.39 = (bf16[96,512]{1,0:T(8,128)(2,1)S(1)}, bf16[96,512]{1,0:T(8,128)(2,1)S(1)}, u32[]{:S(2)}, u32[]{:S(2)}) collective-permute-start(bf16[96,512]{1,0:T(8,128)(2,1)S(1)} %get-tuple-element.139), channel_id=1, source_target_pairs={{0,4},{1,5},{2,6},{3,7},{4,0},{5,1},{6,2},{7,3},{8,12},{9,13},{10,... | collective-permute-start | bytes 294920 | tf_op jit(solution)/shard_map/ppermute | solution.py:363
  68.5 8.7 %collective-permute-start.40 = (bf16[96,512]{1,0:T(8,128)(2,1)S(1)}, bf16[96,512]{1,0:T(8,128)(2,1)S(1)}, u32[]{:S(2)}, u32[]{:S(2)}) collective-permute-start(bf16[96,512]{1,0:T(8,128)(2,1)S(1)} %get-tuple-element.140), channel_id=1, source_target_pairs={{0,2},{1,3},{2,0},{3,1},{4,6},{5,7},{6,4},{7,5},{8,10},{9,11},{10,... | collective-permute-start | bytes 294920 | tf_op jit(solution)/shard_map/ppermute | solution.py:363
  (1 other events, 1.0 us)

commit v10 on v8

--- a/solution.py
+++ b/solution.py
@@ -87,14 +87,14 @@
     return output, mixed, q_up * slope, silu, jnp.concatenate([square, dot], axis=0)
 
 
-def apply_backward(f2t, sums, full_width, output, weighted, mixed, up_slope, silu, queries):
+def apply_backward(f2t, sums, full_width, output, weighted, up_slope, silu):
     inverse = lax.rsqrt(sums[0:1] / full_width + EPSILON)
     scale = inverse * inverse * inverse * sums[1:2] / full_width
     out_back = (inverse * weighted - output * scale).astype(BF16)
     q_back = tn(f2t, out_back)
     gate_back = (q_back * up_slope).astype(BF16)
     up_back = (q_back * silu).astype(BF16)
-    return gate_back, up_back, nn(gate_back, queries), nn(up_back, queries), nt(out_back, mixed)
+    return gate_back, up_back, out_back
 
 
 def second_adjoint(c1t, c3t, c2t, keys, push, up_slope, silu, back_slope, back_curve):
@@ -102,14 +102,7 @@
     down_back_bar = (gate_bar * up_slope + up_bar * silu).astype(BF16)
     up_pre_bar = (gate_bar * back_slope + mixed_bar * silu).astype(BF16)
     gate_pre_bar = (up_bar * back_slope + mixed_bar * up_slope + gate_bar * back_curve).astype(BF16)
-    return (
-        down_back_bar,
-        up_pre_bar,
-        gate_pre_bar,
-        nn(gate_pre_bar, keys),
-        nn(up_pre_bar, keys),
-        nt(push, down_back_bar),
-    )
+    return down_back_bar, up_pre_bar, gate_pre_bar
 
 
 def folds_of(rows, folds):
@@ -140,12 +133,6 @@
     return jnp.concatenate(cotangent, axis=1).astype(BF16), jnp.concatenate(owned, axis=1)
 
 
-def update_sums(w1t, w3t, w2, keys, rates, values):
-    push = push_of(rates, values)
-    *_, mixed, _, _, gate_back, up_back = update_forward(w1t, w3t, w2, keys, push)
-    return nn(gate_back, keys), nn(up_back, keys), nt(push, mixed)
-
-
 def push_of(rates, values):
     return (-rates * values.T.astype(F32)).astype(BF16)
 
@@ -188,35 +175,52 @@
             place_half(ref, half, p, c, chips, folds if k == 2 else 1)
 
 
-def send_pieces(chips, folds, matrices, outs):
-    tok = lax.axis_index("tok")
-    chip, core = tok // CORES, tok % CORES
-    for step, out in enumerate(outs):
-        to = partner(chip, step, chips)
-        at = 0
-        for k, ref in enumerate(matrices):
-            folded = folds if k == 2 else 1
-            parts = [ref[rows_of(ref, to, core, chips, folded, i), :] for i in range(folded)]
-            rows = jnp.concatenate(parts, axis=1).astype(out.dtype)
-            out[at : at + rows.shape[0]] = rows
-            at += rows.shape[0]
-
-
-def cut_matrices(chips, folds, matrices, outs):
+def products_of_core(chips, folds, order, gate_ref, up_ref, down_ref, tokens, hidden):
+    core = lax.axis_index("tok") % CORES
+
+    def picked(ref):
+        rows = ref.shape[0] // (chips * CORES)
+        blocks = [
+            ref[pl.ds(pl.multiple_of((chip * CORES + core) * rows, rows), rows), :] for chip in order
+        ]
+        return jnp.concatenate(blocks, axis=0)
+
+    gate, up = nn(picked(gate_ref), tokens), nn(picked(up_ref), tokens)
+    down = nt(picked(down_ref), hidden)
+    g, d = gate.shape[0] // chips, down.shape[0] // chips
+    pieces = []
+    for k in range(chips):
+        parts = [down[k * d + i * g : k * d + (i + 1) * g] for i in range(folds)]
+        pieces.append(
+            (gate[k * g : (k + 1) * g], up[k * g : (k + 1) * g], jnp.concatenate(parts, axis=1))
+        )
+    return pieces
+
+
+def send_pieces(chips, folds, operands, outs):
+    chip = lax.axis_index("tok") // CORES
+    order = [partner(chip, step, chips) for step in range(chips)]
+    for out, parts in zip(outs, products_of_core(chips, folds, order, *operands)):
+        out[...] = jnp.concatenate(parts, axis=0).astype(out.dtype)
+
+
+def send_halves(chips, folds, operands, outs):
     parity = lax.axis_index("tok") // CORES % 2
-    for k, ref in enumerate(matrices):
-        cut_half(outs[k], ref, parity, chips, folds if k == 2 else 1)
-        cut_half(outs[3 + k], ref, 1 - parity, chips, folds if k == 2 else 1)
+    half = chips // 2
+    order = [2 * k + p for p in (parity, 1 - parity) for k in range(half)]
+    pieces = products_of_core(chips, folds, order, *operands)
+    for k in range(3):
+        kept, given = ([p[k] for p in part] for part in (pieces[:half], pieces[half:]))
+        outs[k][...] = jnp.concatenate(kept, axis=0)
+        outs[3 + k][...] = jnp.concatenate(given, axis=0).astype(BF16)
 
 
 def update_kernel(chips, folds, ko, kx, vo, vx, ro, rx, w1t, w3t, w2, *rest):
-    outs, matrices = rest[:6], rest[6:]
-    sums = update_sums(
-        w1t[...], w3t[...], w2[...], both(ko, kx), both(ro, rx, 1), both(vo, vx)
-    )
-    for ref, total in zip(matrices, sums):
-        ref[...] = total
-    cut_matrices(chips, folds, matrices, outs)
+    outs, (gate, up, push) = rest[:6], rest[6:]
+    keys = both(ko, kx)
+    push[...] = push_of(both(ro, rx, 1), both(vo, vx))
+    *_, mixed, _, _, gate[...], up[...] = update_forward(w1t[...], w3t[...], w2[...], keys, push[...])
+    send_halves(chips, folds, (gate, up, push, keys, mixed), outs)
 
 
 def saved_kernel(
@@ -301,13 +305,12 @@
     f2t, output, weighted, mixed, up_slope, silu, qo, qx, gate_back, up_back = refs[:10]
     outs, (gate, up, down) = refs[10:16], refs[16:]
     width = heads * output.shape[0]
-    gb, ub, gate[...], up[...], down[...] = apply_backward(
-        f2t[...], sums, width, output[...], weighted[...], mixed[...], up_slope[...], silu[...],
-        both(qo, qx),
-    )
-    cut_matrices(chips, folds, (gate, up, down), outs)
+    gate[...], up[...], down[...] = apply_backward(
+        f2t[...], sums, width, output[...], weighted[...], up_slope[...], silu[...]
+    )
+    send_halves(chips, folds, (gate, up, down, both(qo, qx), mixed[...]), outs)
     own = gate_back.shape[1]
-    gate_back[...], up_back[...] = gb[:, :own], ub[:, :own]
+    gate_back[...], up_back[...] = gate[:, :own], up[:, :own]
 
 
 def query_kernel(gate_back, up_back, f1t, f3t, out):
@@ -318,15 +321,16 @@
     halves, refs = refs[:12], refs[12:]
     ko, kx, push, up_slope, silu, back_slope, back_curve = refs[:7]
     c1t, c3t, c2t, dbb_ref, upb_ref, gpb_ref = refs[7:13]
-    outs, (gate, up, down) = refs[13 : 13 + chips], refs[13 + chips :]
+    outs, (gate, up) = refs[13 : 13 + chips], refs[13 + chips :]
     place_halves(chips, folds, halves, (c1t, c3t, c2t))
-    dbb, upb, gpb, gate[...], up[...], down[...] = second_adjoint(
-        c1t[...], c3t[...], c2t[...], both(ko, kx), push[...],
+    keys = both(ko, kx)
+    dbb, up[...], gate[...] = second_adjoint(
+        c1t[...], c3t[...], c2t[...], keys, push[...],
         up_slope[...], silu[...], back_slope[...], back_curve[...],
     )
-    send_pieces(chips, folds, (gate, up, down), outs)
+    send_pieces(chips, folds, (gate, up, push, keys, dbb), outs)
     own = dbb_ref.shape[1]
-    dbb_ref[...], upb_ref[...], gpb_ref[...] = dbb[:, :own], upb[:, :own], gpb[:, :own]
+    dbb_ref[...], upb_ref[...], gpb_ref[...] = dbb[:, :own], up[:, :own], gate[:, :own]
 
 
 def token_grads(rates, mixed, dbb, upb, gpb, gate_back, up_back, c1t, c3t, c2t, w1t, w3t, w2):
@@ -384,7 +388,7 @@
 def head_parts(part, heads):
     got = [
         lax.ppermute(part, "head", [(h, partner(h, step, heads)) for h in range(heads)])
-        for step in reversed(range(1, heads))
+        for step in range(1, heads)
     ]
     return [part, *got]
 
@@ -476,6 +480,7 @@
     half_shares = [(half, F32)] * 3 + [(half, BF16)] * 3
     matrices = [((fh, dh), BF16), ((fh, dh), BF16), ((dh, fh), BF16)]
     sums_scratch = [((fh, dh), F32), ((fh, dh), F32), ((dh, fh), F32)]
+    operands = [((fh, n), BF16), ((fh, n), BF16), ((dh, n), BF16)]
     hidden = ((fh, n), F32)
     own_hidden = ((fh, own), BF16)
     folds_by_matrix = (1, 1, folds)
@@ -491,7 +496,7 @@
         functools.partial(update_kernel, chips, folds),
         half_shares,
         keys_values,
-        sums_scratch,
+        operands,
         "update",
         6 * product,
     )
@@ -531,7 +536,7 @@
             *head_parts(part, heads),
             f2t, output, weighted, q_mixed, q_slope, q_silu, query_input, query_other,
         ),
-        sums_scratch,
+        operands,
         "apply_back",
         4 * product,
     )
@@ -561,7 +566,7 @@
             *from_owners(cotangent, chips),
             key_input, key_other, push, up_slope, silu, back_slope, back_curve,
         ),
-        sums_scratch,
+        operands[:2],
         "second_adjoint",
         6 * product,
     )
@@ -597,9 +602,8 @@
         update_forward(w1t, w3t, w2, keys, push)
     )
     up_slope, back_curve = up_pre * slope, down_back * up_pre * curvature
-    piece, sent = sliced_pieces(
-        nn(gate_back, keys), nn(up_back, keys), nt(push, mixed), tok, count
-    )
+    sums = nn(gate_back, keys), nn(up_back, keys), nt(push, mixed)
+    piece, sent = sliced_pieces(*sums, tok, count)
     prior = pack(
         *(
             lax.dynamic_slice_in_dim(x, tok * rows, rows, 0).astype(F32)
@@ -612,18 +616,20 @@
     f1t, f3t, f2t = whole_matrices(*blocks, tok, count, fh)
     output, q_mixed, q_slope, q_silu, part = apply_forward(f1t, f3t, f2t, queries, weighted)
     sums = lax.psum(part, "head")
-    q_gate_back, q_up_back, *grads = apply_backward(
-        f2t, sums, heads * dh, output, weighted, q_mixed, q_slope, q_silu, queries
-    )
+    q_gate_back, q_up_back, out_back = apply_backward(
+        f2t, sums, heads * dh, output, weighted, q_slope, q_silu
+    )
+    grads = nn(q_gate_back, queries), nn(q_up_back, queries), nt(out_back, q_mixed)
     piece, sent = sliced_pieces(*grads, tok, count)
     query_grad = (tn(q_gate_back[:, :own], f1t) + tn(q_up_back[:, :own], f3t)).astype(BF16)
     fast_grad = total_of(piece, over_chips(sent, count), tok)
     cotangent, owned = packed_owner_backward(prior, moved, fast_grad, fh)
     blocks = gather_blocks(jnp.tile(cotangent, (chips, 1)), count)
     c1t, c3t, c2t = whole_matrices(*blocks, tok, count, fh)
-    dbb, upb, gpb, *bars = second_adjoint(
+    dbb, upb, gpb = second_adjoint(
         c1t, c3t, c2t, keys, push, up_slope, silu, back_slope, back_curve
     )
+    bars = nn(gpb, keys), nn(upb, keys), nt(push, dbb)
     piece, sent = sliced_pieces(*bars, tok, count)
     value_grad, key_grad = token_grads(
         rates, mixed[:, :own], dbb[:, :own], upb[:, :own], gpb[:, :own],

time: 73.7 us -> 72.6 us (0.985)
  waiting for transfers between devices: 22.9 us -> 21.8 us
    ppermute x3, waiting for transfers between devices: 4.23 us -> 3.27 us  [head_parts(): lax.ppermute(part, 'head', [(h, partner(h, step, heads)) for h in range(h...]
where the time goes in v10:
time: 72.6 us; the launch traced here: 72.4 us
  starting transfers between devices  38.3 us (53%)
  waiting for transfers between devices  21.8 us (30%)
  Pallas kernels  9.33 us (13%)
  local copies, waits for them, and re-layouts  2.12 us (3%)
  between operations  0.87 us (1%)
    ppermute x18, starting transfers between devices, to_chip(): return lax.ppermute(x, 'tok', chip_perm(chips * CORES, step))  27 us
    ppermute x18, waiting for transfers between devices, to_chip(): return lax.ppermute(x, 'tok', chip_perm(chips * CORES, step))  11.6 us
    pallas_call x20, Pallas kernels, call(): pl.pallas_call(kernel, out_shape=[jax.ShapeDtypeStruct(s, t) for s, t in...  9.33 us
    ppermute x3, waiting for transfers between devices, exchange(): lax.ppermute(pieces[s], 'tok', chip_perm(count, s))  4.86 us
    ppermute x3, starting transfers between devices, exchange(): lax.ppermute(pieces[s], 'tok', chip_perm(count, s))  4.47 us
    ppermute x3, starting transfers between devices, head_parts(): lax.ppermute(part, 'head', [(h, partner(h, step, heads)) for h in range(h...  3.55 us
    ppermute x3, waiting for transfers between devices, head_parts(): lax.ppermute(part, 'head', [(h, partner(h, step, heads)) for h in range(h...  3.27 us
    unnamed x18, local copies, waits for them, and re-layouts  2.12 us
  transfers between devices with their start and end apart: 41, of which 23 were waited for; matrix products, arithmetic and copies ran while one was open for 2% of the time, Pallas kernels for 8%

profile of v10, /device:TPU:0, one launch (start us, length us, event | category | flops | bytes accessed | tf_op | source)
XLA Modules:
  0.0 72.4 jit_solution(12035979695196715275)
XLA Ops:
  0.6 0.5 collective-permute-start.1
  1.8 1.1 %copy.15 = bf16[1,512,256]{1,2,0:T(8,128)(2,1)S(1)} copy(bf16[1,512,256]{2,1,0:T(8,128)(2,1)} %param.15) | data formatting | bytes 524288 | tf_op args[6]
  3.1 0.7 %copy-done.1 = bf16[1,256,512]{2,1,0:T(8,128)(2,1)S(1)} copy-done((bf16[1,256,512]{2,1,0:T(8,128)(2,1)S(1)}, bf16[1,256,512]{2,1,0:T(8,128)(2,1)}, u32[]{:S(2)}) %copy-start.1) | copy-done | bytes 262168
  4.0 1.2 %update.1 = (f32[64,512]{1,0:T(8,128)S(1)}, f32[64,512]{1,0:T(8,128)S(1)}, f32[64,512]{1,0:T(8,128)S(1)}, bf16[64,512]{1,0:T(8,128)(2,1)S(1)}, bf16[64,512]{1,0:T(8,128)(2,1)S(1)}, /*index=5*/bf16[64,512]{1,0:T(8,128)(2,1)S(1)}) custom-call(bf16[256,512]{1,0:T(8,128)(2,1)S(1)} %copy-done.2, bf16[256,512]{1,0:T(8,128)(2,1)S(1)} %collective-permute-done.kx.refs_13_, ...), custom_call_target="tpu_custom_call" | custom-call | flops 805306368 | bytes 1837056 | tf_op jit(solution)/shard_map/update/pallas_call | solution.py:349
  5.1 3.1 %collective-permute-start.8 = (bf16[64,512]{1,0:T(8,128)(2,1)S(1)}, bf16[64,512]{1,0:T(8,128)(2,1)S(1)}, u32[]{:S(2)}, u32[]{:S(2)}) collective-permute-start(bf16[64,512]{1,0:T(8,128)(2,1)S(1)} %get-tuple-element.85), channel_id=1, source_target_pairs={{0,2},{1,3},{2,0},{3,1},{4,6},{5,7},{6,4},{7,5},{8,10},{9,11},{10,... | collective-permute-start | bytes 196616 | tf_op jit(solution)/shard_map/ppermute | solution.py:372
  8.4 1.9 %collective-permute-start.6 = (bf16[64,512]{1,0:T(8,128)(2,1)S(1)}, bf16[64,512]{1,0:T(8,128)(2,1)S(1)}, u32[]{:S(2)}, u32[]{:S(2)}) collective-permute-start(bf16[64,512]{1,0:T(8,128)(2,1)S(1)} %get-tuple-element.81), channel_id=1, source_target_pairs={{0,2},{1,3},{2,0},{3,1},{4,6},{5,7},{6,4},{7,5},{8,10},{9,11},{10,... | collective-permute-start | bytes 196616 | tf_op jit(solution)/shard_map/ppermute | solution.py:372
  10.6 3.0 %collective-permute-start.9 = (bf16[64,512]{1,0:T(8,128)(2,1)S(1)}, bf16[64,512]{1,0:T(8,128)(2,1)S(1)}, u32[]{:S(2)}, u32[]{:S(2)}) collective-permute-start(bf16[64,512]{1,0:T(8,128)(2,1)S(1)} %carry.8.refs_0_), channel_id=1, source_target_pairs={{0,4},{1,5},{2,6},{3,7},{4,0},{5,1},{6,2},{7,3},{8,12},{9,13},{10,... | collective-permute-start | bytes 196616 | tf_op jit(solution)/shard_map/ppermute | solution.py:372
  13.6 2.2 %collective-permute-start.5 = (bf16[64,512]{1,0:T(8,128)(2,1)S(1)}, bf16[64,512]{1,0:T(8,128)(2,1)S(1)}, u32[]{:S(2)}, u32[]{:S(2)}) collective-permute-start(bf16[64,512]{1,0:T(8,128)(2,1)S(1)} %carry.6.refs_0_), channel_id=1, source_target_pairs={{0,4},{1,5},{2,6},{3,7},{4,0},{5,1},{6,2},{7,3},{8,12},{9,13},{10,... | collective-permute-start | bytes 196616 | tf_op jit(solution)/shard_map/ppermute | solution.py:372
  15.8 1.4 %collective-permute-start.7 = (bf16[64,512]{1,0:T(8,128)(2,1)S(1)}, bf16[64,512]{1,0:T(8,128)(2,1)S(1)}, u32[]{:S(2)}, u32[]{:S(2)}) collective-permute-start(bf16[64,512]{1,0:T(8,128)(2,1)S(1)} %carry.7.refs_0_), channel_id=1, source_target_pairs={{0,4},{1,5},{2,6},{3,7},{4,0},{5,1},{6,2},{7,3},{8,12},{9,13},{10,... | collective-permute-start | bytes 196616 | tf_op jit(solution)/shard_map/ppermute | solution.py:372
  17.2 1.1 %saved.1 = (bf16[512,512]{1,0:T(8,128)(2,1)S(1)}, f32[256,512]{1,0:T(8,128)S(1)}, f32[256,512]{1,0:T(8,128)S(1)}, f32[256,512]{1,0:T(8,128)S(1)}, f32[256,512]{1...) custom-call(bf16[256,512]{1,0:T(8,128)(2,1)S(1)} %copy-done.2, ...), custom_call_target="tpu_custom_call" | custom-call | flops 402653184 | bytes 2363392 | tf_op jit(solution)/shard_map/saved/pallas_call | solution.py:349
  18.4 2.7 %collective-permute-start.16 = (bf16[64,512]{1,0:T(8,128)(2,1)S(1)}, bf16[64,512]{1,0:T(8,128)(2,1)S(1)}, u32[]{:S(2)}, u32[]{:S(2)}) collective-permute-start(bf16[64,512]{1,0:T(8,128)(2,1)S(1)} %get-tuple-element.90.refs_8_), channel_id=1, source_target_pairs={{0,2},{1,3},{2,0},{3,1},{4,6},{5,7},{6,4},{7,5},{8,10},{9,11},{10,... | collective-permute-start | bytes 196616 | tf_op jit(solution)/shard_map/ppermute | solution.py:372
  21.4 1.2 %collective-permute-start.10 = (bf16[64,512]{1,0:T(8,128)(2,1)S(1)}, bf16[64,512]{1,0:T(8,128)(2,1)S(1)}, u32[]{:S(2)}, u32[]{:S(2)}) collective-permute-start(bf16[64,512]{1,0:T(8,128)(2,1)S(1)} %get-tuple-element.88.refs_0_), channel_id=1, source_target_pairs={{0,2},{1,3},{2,0},{3,1},{4,6},{5,7},{6,4},{7,5},{8,10},{9,11},{10,... | collective-permute-start | bytes 196616 | tf_op jit(solution)/shard_map/ppermute | solution.py:372
  23.1 0.5 collective-permute-start.13
  23.9 2.0 %collective-permute-done.10.refs_1_ = bf16[64,512]{1,0:T(8,128)(2,1)S(1)} collective-permute-done((bf16[64,512]{1,0:T(8,128)(2,1)S(1)}, bf16[64,512]{1,0:T(8,128)(2,1)S(1)}, u32[]{:S(2)}, u32[]{:S(2)}) %collective-permute-start.10) | collective-permute-done | bytes 65568 | tf_op jit(solution)/shard_map/ppermute | solution.py:372
  25.9 0.5 collective-permute-start.14
  26.4 1.1 %collective-permute-done.13.refs_5_ = bf16[64,512]{1,0:T(8,128)(2,1)S(1)} collective-permute-done((bf16[64,512]{1,0:T(8,128)(2,1)S(1)}, bf16[64,512]{1,0:T(8,128)(2,1)S(1)}, u32[]{:S(2)}, u32[]{:S(2)}) %collective-permute-start.13) | collective-permute-done | bytes 65568 | tf_op jit(solution)/shard_map/ppermute | solution.py:372
  27.5 0.5 collective-permute-start.17
  28.1 0.7 collective-permute-done.15.refs_7_
  29.2 0.8 %apply.1 = (bf16[256,512]{1,0:T(8,128)(2,1)S(1)}, bf16[256,512]{1,0:T(8,128)(2,1)S(1)}, bf16[512,256]{1,0:T(8,128)(2,1)S(1)}, f32[512,512]{1,0:T(8,128)S(1)}, bf...) custom-call(bf16[64,512]{1,0:T(8,128)(2,1)S(1)} %get-tuple-element.88.refs_0, ...), custom_call_target="tpu_custom_call" | custom-call | flops 402653184 | bytes 2359296 | tf_op jit(solution)/shard_map/apply/pallas_call | solution.py:349
  30.1 2.7 %collective-permute-start.22 = (f32[2,512]{1,0:T(2,128)S(1)}, f32[2,512]{1,0:T(2,128)S(1)}, u32[]{:S(2)}, u32[]{:S(2)}) collective-permute-start(f32[2,512]{1,0:T(2,128)S(1)} %get-tuple-element.92.refs_0_), channel_id=1, source_target_pairs={{0,24},{8,16},{16,8},{24,0},{1,25},{9,17},{17,9},{25,1},{2,26},{10... | collective-permute-start | bytes 12296 | tf_op jit(solution)/shard_map/ppermute | solution.py:390
  32.8 0.5 collective-permute-start.21
  33.6 1.0 %collective-permute-done.22.refs_3_ = f32[2,512]{1,0:T(2,128)S(1)} collective-permute-done((f32[2,512]{1,0:T(2,128)S(1)}, f32[2,512]{1,0:T(2,128)S(1)}, u32[]{:S(2)}, u32[]{:S(2)}) %collective-permute-start.22) | collective-permute-done | bytes 4128 | tf_op jit(solution)/shard_map/ppermute | solution.py:390
  34.6 1.8 %collective-permute-done.21.refs_2_ = f32[2,512]{1,0:T(2,128)S(1)} collective-permute-done((f32[2,512]{1,0:T(2,128)S(1)}, f32[2,512]{1,0:T(2,128)S(1)}, u32[]{:S(2)}, u32[]{:S(2)}) %collective-permute-start.21) | collective-permute-done | bytes 4128 | tf_op jit(solution)/shard_map/ppermute | solution.py:390
  36.9 0.9 %apply_back.1 = (bf16[256,256]{1,0:T(8,128)(2,1)S(1)}, bf16[256,256]{1,0:T(8,128)(2,1)S(1)}, f32[64,512]{1,0:T(8,128)S(1)}, f32[64,512]{1,0:T(8,128)S(1)}, f32[6...) custom-call(f32[2,512]{1,0:T(2,128)S(1)} %get-tuple-element.92.refs_0, ...), custom_call_target="tpu_custom_call" | custom-call | flops 536870912 | bytes 4210688 | tf_op jit(solution)/shard_map/apply_back/pallas_call | solution.py:349
  37.8 0.6 collective-permute-start.25
  38.4 1.5 %collective-permute-start.23 = (bf16[64,512]{1,0:T(8,128)(2,1)S(1)}, bf16[64,512]{1,0:T(8,128)(2,1)S(1)}, u32[]{:S(2)}, u32[]{:S(2)}) collective-permute-start(bf16[64,512]{1,0:T(8,128)(2,1)S(1)} %get-tuple-element.105), channel_id=1, source_target_pairs={{0,2},{1,3},{2,0},{3,1},{4,6},{5,7},{6,4},{7,5},{8,10},{9,11},{10,... | collective-permute-start | bytes 196616 | tf_op jit(solution)/shard_map/ppermute | solution.py:372
  39.9 0.6 collective-permute-start.27
  40.4 1.7 %collective-permute-done.25.got = bf16[64,512]{1,0:T(8,128)(2,1)S(1)} collective-permute-done((bf16[64,512]{1,0:T(8,128)(2,1)S(1)}, bf16[64,512]{1,0:T(8,128)(2,1)S(1)}, u32[]{:S(2)}, u32[]{:S(2)}) %collective-permute-start.25) | collective-permute-done | bytes 65568 | tf_op jit(solution)/shard_map/ppermute | solution.py:372
  42.1 3.4 %collective-permute-start.26 = (bf16[64,512]{1,0:T(8,128)(2,1)S(1)}, bf16[64,512]{1,0:T(8,128)(2,1)S(1)}, u32[]{:S(2)}, u32[]{:S(2)}) collective-permute-start(bf16[64,512]{1,0:T(8,128)(2,1)S(1)} %carry.10.refs_0_), channel_id=1, source_target_pairs={{0,4},{1,5},{2,6},{3,7},{4,0},{5,1},{6,2},{7,3},{8,12},{9,13},{10,... | collective-permute-start | bytes 196616 | tf_op jit(solution)/shard_map/ppermute | solution.py:372
  45.6 0.7 collective-permute-start.24
  46.3 2.4 %collective-permute-start.28 = (bf16[64,512]{1,0:T(8,128)(2,1)S(1)}, bf16[64,512]{1,0:T(8,128)(2,1)S(1)}, u32[]{:S(2)}, u32[]{:S(2)}) collective-permute-start(bf16[64,512]{1,0:T(8,128)(2,1)S(1)} %carry.11.refs_0_), channel_id=1, source_target_pairs={{0,4},{1,5},{2,6},{3,7},{4,0},{5,1},{6,2},{7,3},{8,12},{9,13},{10,... | collective-permute-start | bytes 196616 | tf_op jit(solution)/shard_map/ppermute | solution.py:372
  48.7 1.1 %collective-permute-done.26.refs_1_ = bf16[64,512]{1,0:T(8,128)(2,1)S(1)} collective-permute-done((bf16[64,512]{1,0:T(8,128)(2,1)S(1)}, bf16[64,512]{1,0:T(8,128)(2,1)S(1)}, u32[]{:S(2)}, u32[]{:S(2)}) %collective-permute-start.26) | collective-permute-done | bytes 65568 | tf_op jit(solution)/shard_map/ppermute | solution.py:372
  50.1 1.3 %collective-permute-done.24.refs_1_ = bf16[64,512]{1,0:T(8,128)(2,1)S(1)} collective-permute-done((bf16[64,512]{1,0:T(8,128)(2,1)S(1)}, bf16[64,512]{1,0:T(8,128)(2,1)S(1)}, u32[]{:S(2)}, u32[]{:S(2)}) %collective-permute-start.24) | collective-permute-done | bytes 65568 | tf_op jit(solution)/shard_map/ppermute | solution.py:372
  51.5 0.8 %collective-permute-start.29 = (bf16[64,512]{1,0:T(8,128)(2,1)S(1)}, bf16[64,512]{1,0:T(8,128)(2,1)S(1)}, u32[]{:S(2)}, u32[]{:S(2)}) collective-permute-start(bf16[64,512]{1,0:T(8,128)(2,1)S(1)} %get-tuple-element.116.refs_0_), channel_id=1, source_target_pairs={{0,2},{1,3},{2,0},{3,1},{4,6},{5,7},{6,4},{7,5},{8,10},{9,11},{10,... | collective-permute-start | bytes 196616 | tf_op jit(solution)/shard_map/ppermute | solution.py:372
  52.9 0.9 %collective-permute-start.35 = (bf16[64,512]{1,0:T(8,128)(2,1)S(1)}, bf16[64,512]{1,0:T(8,128)(2,1)S(1)}, u32[]{:S(2)}, u32[]{:S(2)}) collective-permute-start(bf16[64,512]{1,0:T(8,128)(2,1)S(1)} %get-tuple-element.118.refs_8_), channel_id=1, source_target_pairs={{0,2},{1,3},{2,0},{3,1},{4,6},{5,7},{6,4},{7,5},{8,10},{9,11},{10,... | collective-permute-start | bytes 196616 | tf_op jit(solution)/shard_map/ppermute | solution.py:372
  54.3 1.5 %collective-permute-done.29.refs_1_ = bf16[64,512]{1,0:T(8,128)(2,1)S(1)} collective-permute-done((bf16[64,512]{1,0:T(8,128)(2,1)S(1)}, bf16[64,512]{1,0:T(8,128)(2,1)S(1)}, u32[]{:S(2)}, u32[]{:S(2)}) %collective-permute-start.29) | collective-permute-done | bytes 65568 | tf_op jit(solution)/shard_map/ppermute | solution.py:372
  55.8 0.5 collective-permute-start.33
  56.3 0.9 %collective-permute-done.35.refs_9_ = bf16[64,512]{1,0:T(8,128)(2,1)S(1)} collective-permute-done((bf16[64,512]{1,0:T(8,128)(2,1)S(1)}, bf16[64,512]{1,0:T(8,128)(2,1)S(1)}, u32[]{:S(2)}, u32[]{:S(2)}) %collective-permute-start.35) | collective-permute-done | bytes 65568 | tf_op jit(solution)/shard_map/ppermute | solution.py:372
  57.3 0.5 collective-permute-start.37
  57.8 0.7 %collective-permute-done.31.refs_3_ = bf16[64,512]{1,0:T(8,128)(2,1)S(1)} collective-permute-done((bf16[64,512]{1,0:T(8,128)(2,1)S(1)}, bf16[64,512]{1,0:T(8,128)(2,1)S(1)}, u32[]{:S(2)}, u32[]{:S(2)}) %collective-permute-start.31) | collective-permute-done | bytes 65568 | tf_op jit(solution)/shard_map/ppermute | solution.py:383
  58.7 1.3 %second_adjoint.1 = (bf16[256,512]{1,0:T(8,128)(2,1)S(1)}, bf16[256,512]{1,0:T(8,128)(2,1)S(1)}, bf16[512,256]{1,0:T(8,128)(2,1)S(1)}, bf16[256,256]{1,0:T(8,128...) custom-call(bf16[64,512]{1,0:T(8,128)(2,1)S(1)} %get-tuple-element.1, ...), custom_call_target="tpu_custom_call" | custom-call | flops 805306368 | bytes 3932160 | tf_op jit(solution)/shard_map/second_adjoint/pallas_call | solution.py:349
  60.0 2.3 %collective-permute-start.38 = (bf16[96,512]{1,0:T(8,128)(2,1)S(1)}, bf16[96,512]{1,0:T(8,128)(2,1)S(1)}, u32[]{:S(2)}, u32[]{:S(2)}) collective-permute-start(bf16[96,512]{1,0:T(8,128)(2,1)S(1)} %get-tuple-element.138), channel_id=1, source_target_pairs={{0,6},{1,7},{2,4},{3,5},{4,2},{5,3},{6,0},{7,1},{8,14},{9,15},{10,... | collective-permute-start | bytes 294920 | tf_op jit(solution)/shard_map/ppermute | solution.py:367
  62.4 2.1 %collective-permute-start.40 = (bf16[96,512]{1,0:T(8,128)(2,1)S(1)}, bf16[96,512]{1,0:T(8,128)(2,1)S(1)}, u32[]{:S(2)}, u32[]{:S(2)}) collective-permute-start(bf16[96,512]{1,0:T(8,128)(2,1)S(1)} %get-tuple-element.140), channel_id=1, source_target_pairs={{0,2},{1,3},{2,0},{3,1},{4,6},{5,7},{6,4},{7,5},{8,10},{9,11},{10,... | collective-permute-start | bytes 294920 | tf_op jit(solution)/shard_map/ppermute | solution.py:367
  64.5 1.0 %query_grad.1 = bf16[256,512]{1,0:T(8,128)(2,1)} custom-call(bf16[256,256]{1,0:T(8,128)(2,1)S(1)} %get-tuple-element.98.gate_back, bf16[256,256]{1,0:T(8,128)(2,1)S(1)} %get-tuple-element.99.up_back, bf16[256,512]{1,0:T(8,128)(2,1)S(1)} %get-tuple-element.100.f1t, bf16[256,512]{1,0:T(8,128)(2,1)S(1)} %get-tuple-element.101.f3t), custom_call_target="tpu_custom_call" | custom-call | flops 134217728 | bytes 786432 | tf_op jit(solution)/shard_map/query_grad/pallas_call | solution.py:349
  65.5 1.4 %token_grads.1 = (bf16[256,512]{1,0:T(8,128)(2,1)}, bf16[256,512]{1,0:T(8,128)(2,1)}) custom-call(f32[1,256]{1,0:T(1,128)S(1)} %bitcast.30, bf16[256,256]{1,0:T(8,128)(2,1)S(1)} %get-tuple-element.102.refs_1_, bf16[256,256]{1,0:T(8,128)(2,1)S(1)} %get-tuple-element.124.refs_2_, bf16[256,256]{1,0:T(8,128)(2,1)S(1)} %get-tuple-element.125.refs_3_, ...), custom_call_target="tpu_custom_call" | custom-call | flops 402653184 | bytes 2360320 | tf_op jit(solution)/shard_map/token_grads/pallas_call | solution.py:349
  66.9 0.7 %collective-permute-done.38.refs_4_ = bf16[96,512]{1,0:T(8,128)(2,1)S(1)} collective-permute-done((bf16[96,512]{1,0:T(8,128)(2,1)S(1)}, bf16[96,512]{1,0:T(8,128)(2,1)S(1)}, u32[]{:S(2)}, u32[]{:S(2)}) %collective-permute-start.38) | collective-permute-done | bytes 98336 | tf_op jit(solution)/shard_map/ppermute | solution.py:367
  67.6 4.1 %collective-permute-done.39.refs_5_ = bf16[96,512]{1,0:T(8,128)(2,1)S(1)} collective-permute-done((bf16[96,512]{1,0:T(8,128)(2,1)S(1)}, bf16[96,512]{1,0:T(8,128)(2,1)S(1)}, u32[]{:S(2)}, u32[]{:S(2)}) %collective-permute-start.39) | collective-permute-done | bytes 98336 | tf_op jit(solution)/shard_map/ppermute | solution.py:367
  71.7 0.7 owner_result.1
  (72 shorter events, 5.8 us)
Async XLA Ops:
  0.6 1.0 %copy-start.5 = (f32[256,1]{0,1:T(1,128)S(1)}, f32[256,1]{0,1:T(1,128)}, u32[]{:S(2)}) copy-start(f32[256,1]{0,1:T(1,128)} %param.13) | copy-start | bytes 3076
  0.6 2.5 %collective-permute-start.1 = (bf16[256,512]{1,0:T(8,128)(2,1)}, bf16[256,512]{1,0:T(8,128)(2,1)S(1)}, u32[]{:S(2)}, u32[]{:S(2)}) collective-permute-start(bf16[256,512]{1,0:T(8,128)(2,1)} %vo.3), channel_id=1, source_target_pairs={{0,1},{1,0},{2,3},{3,2},{4,5},{5,4},{6,7},{7,6},{8,9},{9,8},{10,11... | collective-permute-start | bytes 786440 | tf_op jit(solution)/shard_map/ppermute | solution.py:488
  1.2 2.0 %collective-permute-start = (bf16[256,512]{1,0:T(8,128)(2,1)}, bf16[256,512]{1,0:T(8,128)(2,1)S(1)}, u32[]{:S(2)}, u32[]{:S(2)}) collective-permute-start(bf16[256,512]{1,0:T(8,128)(2,1)} %refs_12_.3), channel_id=1, source_target_pairs={{0,1},{1,0},{2,3},{3,2},{4,5},{5,4},{6,7},{7,6},{8,9},{9,8},{10,11... | collective-permute-start | bytes 786440 | tf_op jit(solution)/shard_map/ppermute | solution.py:488
  1.2 15.9 %collective-permute-start.3 = (bf16[256,512]{1,0:T(8,128)(2,1)}, bf16[256,512]{1,0:T(8,128)(2,1)S(1)}, u32[]{:S(2)}, u32[]{:S(2)}) collective-permute-start(bf16[256,512]{1,0:T(8,128)(2,1)} %go.1), channel_id=1, source_target_pairs={{0,1},{1,0},{2,3},{3,2},{4,5},{5,4},{6,7},{7,6},{8,9},{9,8},{10,11... | collective-permute-start | bytes 786440 | tf_op jit(solution)/shard_map/ppermute | solution.py:488
  1.7 1.2 %copy-start.7 = (bf16[1,512,256]{2,1,0:T(8,128)(2,1)S(1)}, bf16[1,512,256]{2,1,0:T(8,128)(2,1)}, u32[]{:S(2)}) copy-start(bf16[1,512,256]{2,1,0:T(8,128)(2,1)} %param.16) | copy-start | bytes 786436
  1.7 1.4 %collective-permute-start.2 = (f32[1,256]{1,0:T(1,128)S(1)}, f32[1,256]{1,0:T(1,128)S(1)}, u32[]{:S(2)}, u32[]{:S(2)}) collective-permute-start(f32[1,256]{1,0:T(1,128)S(1)} %bitcast.27), channel_id=1, source_target_pairs={{0,1},{1,0},{2,3},{3,2},{4,5},{5,4},{6,7},{7,6},{8,9},{9,8},{10,11... | collective-permute-start | bytes 3080 | tf_op jit(solution)/shard_map/ppermute | solution.py:488
  1.8 1.4 %copy-start.3 = (bf16[256,512]{1,0:T(8,128)(2,1)S(1)}, bf16[256,512]{1,0:T(8,128)(2,1)}, u32[]{:S(2)}) copy-start(bf16[256,512]{1,0:T(8,128)(2,1)} %vo.3) | copy-start | bytes 786436
  2.9 1.0 %copy-start.2 = (bf16[256,512]{1,0:T(8,128)(2,1)S(1)}, bf16[256,512]{1,0:T(8,128)(2,1)}, u32[]{:S(2)}) copy-start(bf16[256,512]{1,0:T(8,128)(2,1)} %refs_12_.3) | copy-start | bytes 786436
  4.0 4.2 %copy-start = (bf16[256,512]{1,0:T(8,128)(2,1)S(1)}, bf16[256,512]{1,0:T(8,128)(2,1)}, u32[]{:S(2)}) copy-start(bf16[256,512]{1,0:T(8,128)(2,1)} %refs_10_.1) | copy-start | bytes 786436
  5.1 5.4 %collective-permute-start.8 = (bf16[64,512]{1,0:T(8,128)(2,1)S(1)}, bf16[64,512]{1,0:T(8,128)(2,1)S(1)}, u32[]{:S(2)}, u32[]{:S(2)}) collective-permute-start(bf16[64,512]{1,0:T(8,128)(2,1)S(1)} %get-tuple-element.85), channel_id=1, source_target_pairs={{0,2},{1,3},{2,0},{3,1},{4,6},{5,7},{6,4},{7,5},{8,10},{9,11},{10,... | collective-permute-start | bytes 196616 | tf_op jit(solution)/shard_map/ppermute | solution.py:372
  8.2 19.3 %collective-permute-start.19 = (bf16[256,512]{1,0:T(8,128)(2,1)S(1)}, bf16[256,512]{1,0:T(8,128)(2,1)S(1)}, u32[]{:S(2)}, u32[]{:S(2)}) collective-permute-start(bf16[256,512]{1,0:T(8,128)(2,1)S(1)} %copy-done), channel_id=1, source_target_pairs={{0,1},{1,0},{2,3},{3,2},{4,5},{5,4},{6,7},{7,6},{8,9},{9,8},{10,11... | collective-permute-start | bytes 786440 | tf_op jit(solution)/shard_map/ppermute | solution.py:488
  8.2 5.4 %collective-permute-start.4 = (bf16[64,512]{1,0:T(8,128)(2,1)S(1)}, bf16[64,512]{1,0:T(8,128)(2,1)S(1)}, u32[]{:S(2)}, u32[]{:S(2)}) collective-permute-start(bf16[64,512]{1,0:T(8,128)(2,1)S(1)} %get-tuple-element.77), channel_id=1, source_target_pairs={{0,2},{1,3},{2,0},{3,1},{4,6},{5,7},{6,4},{7,5},{8,10},{9,11},{10,... | collective-permute-start | bytes 196616 | tf_op jit(solution)/shard_map/ppermute | solution.py:372
  8.4 7.4 %collective-permute-start.6 = (bf16[64,512]{1,0:T(8,128)(2,1)S(1)}, bf16[64,512]{1,0:T(8,128)(2,1)S(1)}, u32[]{:S(2)}, u32[]{:S(2)}) collective-permute-start(bf16[64,512]{1,0:T(8,128)(2,1)S(1)} %get-tuple-element.81), channel_id=1, source_target_pairs={{0,2},{1,3},{2,0},{3,1},{4,6},{5,7},{6,4},{7,5},{8,10},{9,11},{10,... | collective-permute-start | bytes 196616 | tf_op jit(solution)/shard_map/ppermute | solution.py:372
  10.6 7.7 %collective-permute-start.9 = (bf16[64,512]{1,0:T(8,128)(2,1)S(1)}, bf16[64,512]{1,0:T(8,128)(2,1)S(1)}, u32[]{:S(2)}, u32[]{:S(2)}) collective-permute-start(bf16[64,512]{1,0:T(8,128)(2,1)S(1)} %carry.8.refs_0_), channel_id=1, source_target_pairs={{0,4},{1,5},{2,6},{3,7},{4,0},{5,1},{6,2},{7,3},{8,12},{9,13},{10,... | collective-permute-start | bytes 196616 | tf_op jit(solution)/shard_map/ppermute | solution.py:372
  13.6 3.6 %copy-start.4 = (bf16[256,512]{1,0:T(8,128)(2,1)S(1)}, bf16[256,512]{1,0:T(8,128)(2,1)}, u32[]{:S(2)}) copy-start(bf16[256,512]{1,0:T(8,128)(2,1)} %go.1) | copy-start | bytes 786436
  13.6 7.7 %collective-permute-start.5 = (bf16[64,512]{1,0:T(8,128)(2,1)S(1)}, bf16[64,512]{1,0:T(8,128)(2,1)S(1)}, u32[]{:S(2)}, u32[]{:S(2)}) collective-permute-start(bf16[64,512]{1,0:T(8,128)(2,1)S(1)} %carry.6.refs_0_), channel_id=1, source_target_pairs={{0,4},{1,5},{2,6},{3,7},{4,0},{5,1},{6,2},{7,3},{8,12},{9,13},{10,... | collective-permute-start | bytes 196616 | tf_op jit(solution)/shard_map/ppermute | solution.py:372
  15.8 1.4 %copy-start.6 = (f32[512]{0:T(512)S(1)}, f32[512]{0:T(512)}, u32[]{:S(2)}) copy-start(f32[512]{0:T(512)} %param.14) | copy-start | bytes 6148
  15.8 7.2 %collective-permute-start.7 = (bf16[64,512]{1,0:T(8,128)(2,1)S(1)}, bf16[64,512]{1,0:T(8,128)(2,1)S(1)}, u32[]{:S(2)}, u32[]{:S(2)}) collective-permute-start(bf16[64,512]{1,0:T(8,128)(2,1)S(1)} %carry.7.refs_0_), channel_id=1, source_target_pairs={{0,4},{1,5},{2,6},{3,7},{4,0},{5,1},{6,2},{7,3},{8,12},{9,13},{10,... | collective-permute-start | bytes 196616 | tf_op jit(solution)/shard_map/ppermute | solution.py:372
  18.4 5.5 %collective-permute-start.16 = (bf16[64,512]{1,0:T(8,128)(2,1)S(1)}, bf16[64,512]{1,0:T(8,128)(2,1)S(1)}, u32[]{:S(2)}, u32[]{:S(2)}) collective-permute-start(bf16[64,512]{1,0:T(8,128)(2,1)S(1)} %get-tuple-element.90.refs_8_), channel_id=1, source_target_pairs={{0,2},{1,3},{2,0},{3,1},{4,6},{5,7},{6,4},{7,5},{8,10},{9,11},{10,... | collective-permute-start | bytes 196616 | tf_op jit(solution)/shard_map/ppermute | solution.py:372
  21.4 4.5 %collective-permute-start.10 = (bf16[64,512]{1,0:T(8,128)(2,1)S(1)}, bf16[64,512]{1,0:T(8,128)(2,1)S(1)}, u32[]{:S(2)}, u32[]{:S(2)}) collective-permute-start(bf16[64,512]{1,0:T(8,128)(2,1)S(1)} %get-tuple-element.88.refs_0_), channel_id=1, source_target_pairs={{0,2},{1,3},{2,0},{3,1},{4,6},{5,7},{6,4},{7,5},{8,10},{9,11},{10,... | collective-permute-start | bytes 196616 | tf_op jit(solution)/shard_map/ppermute | solution.py:372
  23.1 4.3 %collective-permute-start.13 = (bf16[64,512]{1,0:T(8,128)(2,1)S(1)}, bf16[64,512]{1,0:T(8,128)(2,1)S(1)}, u32[]{:S(2)}, u32[]{:S(2)}) collective-permute-start(bf16[64,512]{1,0:T(8,128)(2,1)S(1)} %get-tuple-element.89.refs_4_), channel_id=1, source_target_pairs={{0,2},{1,3},{2,0},{3,1},{4,6},{5,7},{6,4},{7,5},{8,10},{9,11},{10,... | collective-permute-start | bytes 196616 | tf_op jit(solution)/shard_map/ppermute | solution.py:372
  23.9 4.1 %collective-permute-start.18 = (bf16[64,512]{1,0:T(8,128)(2,1)S(1)}, bf16[64,512]{1,0:T(8,128)(2,1)S(1)}, u32[]{:S(2)}, u32[]{:S(2)}) collective-permute-start(bf16[64,512]{1,0:T(8,128)(2,1)S(1)} %collective-permute-done.16.refs_9_), channel_id=1, source_target_pairs={{0,1},{1,0},{2,3},{3,2},{4,5},{5,4},{6,7},{7,6},{8,9},{9,8},{10,11... | collective-permute-start | bytes 196616 | tf_op jit(solution)/shard_map/ppermute | solution.py:383
  25.9 2.8 %collective-permute-start.11 = (bf16[64,512]{1,0:T(8,128)(2,1)S(1)}, bf16[64,512]{1,0:T(8,128)(2,1)S(1)}, u32[]{:S(2)}, u32[]{:S(2)}) collective-permute-start(bf16[64,512]{1,0:T(8,128)(2,1)S(1)} %get-tuple-element.88.refs_0_), channel_id=1, source_target_pairs={{0,1},{1,0},{2,3},{3,2},{4,5},{5,4},{6,7},{7,6},{8,9},{9,8},{10,11... | collective-permute-start | bytes 196616 | tf_op jit(solution)/shard_map/ppermute | solution.py:383
  25.9 2.8 %collective-permute-start.14 = (bf16[64,512]{1,0:T(8,128)(2,1)S(1)}, bf16[64,512]{1,0:T(8,128)(2,1)S(1)}, u32[]{:S(2)}, u32[]{:S(2)}) collective-permute-start(bf16[64,512]{1,0:T(8,128)(2,1)S(1)} %get-tuple-element.89.refs_4_), channel_id=1, source_target_pairs={{0,1},{1,0},{2,3},{3,2},{4,5},{5,4},{6,7},{7,6},{8,9},{9,8},{10,11... | collective-permute-start | bytes 196616 | tf_op jit(solution)/shard_map/ppermute | solution.py:383
  27.5 1.3 %collective-permute-start.15 = (bf16[64,512]{1,0:T(8,128)(2,1)S(1)}, bf16[64,512]{1,0:T(8,128)(2,1)S(1)}, u32[]{:S(2)}, u32[]{:S(2)}) collective-permute-start(bf16[64,512]{1,0:T(8,128)(2,1)S(1)} %collective-permute-done.13.refs_5_), channel_id=1, source_target_pairs={{0,1},{1,0},{2,3},{3,2},{4,5},{5,4},{6,7},{7,6},{8,9},{9,8},{10,11... | collective-permute-start | bytes 196616 | tf_op jit(solution)/shard_map/ppermute | solution.py:383
  27.5 1.4 %collective-permute-start.17 = (bf16[64,512]{1,0:T(8,128)(2,1)S(1)}, bf16[64,512]{1,0:T(8,128)(2,1)S(1)}, u32[]{:S(2)}, u32[]{:S(2)}) collective-permute-start(bf16[64,512]{1,0:T(8,128)(2,1)S(1)} %get-tuple-element.90.refs_8_), channel_id=1, source_target_pairs={{0,1},{1,0},{2,3},{3,2},{4,5},{5,4},{6,7},{7,6},{8,9},{9,8},{10,11... | collective-permute-start | bytes 196616 | tf_op jit(solution)/shard_map/ppermute | solution.py:383
  28.0 1.3 %collective-permute-start.12 = (bf16[64,512]{1,0:T(8,128)(2,1)S(1)}, bf16[64,512]{1,0:T(8,128)(2,1)S(1)}, u32[]{:S(2)}, u32[]{:S(2)}) collective-permute-start(bf16[64,512]{1,0:T(8,128)(2,1)S(1)} %collective-permute-done.10.refs_1_), channel_id=1, source_target_pairs={{0,1},{1,0},{2,3},{3,2},{4,5},{5,4},{6,7},{7,6},{8,9},{9,8},{10,11... | collective-permute-start | bytes 196616 | tf_op jit(solution)/shard_map/ppermute | solution.py:383
  30.1 4.6 %collective-permute-start.22 = (f32[2,512]{1,0:T(2,128)S(1)}, f32[2,512]{1,0:T(2,128)S(1)}, u32[]{:S(2)}, u32[]{:S(2)}) collective-permute-start(f32[2,512]{1,0:T(2,128)S(1)} %get-tuple-element.92.refs_0_), channel_id=1, source_target_pairs={{0,24},{8,16},{16,8},{24,0},{1,25},{9,17},{17,9},{25,1},{2,26},{10... | collective-permute-start | bytes 12296 | tf_op jit(solution)/shard_map/ppermute | solution.py:390
  32.8 3.6 %collective-permute-start.21 = (f32[2,512]{1,0:T(2,128)S(1)}, f32[2,512]{1,0:T(2,128)S(1)}, u32[]{:S(2)}, u32[]{:S(2)}) collective-permute-start(f32[2,512]{1,0:T(2,128)S(1)} %get-tuple-element.92.refs_0_), channel_id=1, source_target_pairs={{0,16},{8,24},{16,0},{24,8},{1,17},{9,25},{17,1},{25,9},{2,18},{10... | collective-permute-start | bytes 12296 | tf_op jit(solution)/shard_map/ppermute | solution.py:390
  33.3 3.6 %collective-permute-start.20 = (f32[2,512]{1,0:T(2,128)S(1)}, f32[2,512]{1,0:T(2,128)S(1)}, u32[]{:S(2)}, u32[]{:S(2)}) collective-permute-start(f32[2,512]{1,0:T(2,128)S(1)} %get-tuple-element.92.refs_0_), channel_id=1, source_target_pairs={{0,8},{8,0},{16,24},{24,16},{1,9},{9,1},{17,25},{25,17},{2,10},{10... | collective-permute-start | bytes 12296 | tf_op jit(solution)/shard_map/ppermute | solution.py:390
  37.8 4.3 %collective-permute-start.25 = (bf16[64,512]{1,0:T(8,128)(2,1)S(1)}, bf16[64,512]{1,0:T(8,128)(2,1)S(1)}, u32[]{:S(2)}, u32[]{:S(2)}) collective-permute-start(bf16[64,512]{1,0:T(8,128)(2,1)S(1)} %get-tuple-element.109), channel_id=1, source_target_pairs={{0,2},{1,3},{2,0},{3,1},{4,6},{5,7},{6,4},{7,5},{8,10},{9,11},{10,... | collective-permute-start | bytes 196616 | tf_op jit(solution)/shard_map/ppermute | solution.py:372
  38.4 7.2 %collective-permute-start.23 = (bf16[64,512]{1,0:T(8,128)(2,1)S(1)}, bf16[64,512]{1,0:T(8,128)(2,1)S(1)}, u32[]{:S(2)}, u32[]{:S(2)}) collective-permute-start(bf16[64,512]{1,0:T(8,128)(2,1)S(1)} %get-tuple-element.105), channel_id=1, source_target_pairs={{0,2},{1,3},{2,0},{3,1},{4,6},{5,7},{6,4},{7,5},{8,10},{9,11},{10,... | collective-permute-start | bytes 196616 | tf_op jit(solution)/shard_map/ppermute | solution.py:372
  39.9 6.4 %collective-permute-start.27 = (bf16[64,512]{1,0:T(8,128)(2,1)S(1)}, bf16[64,512]{1,0:T(8,128)(2,1)S(1)}, u32[]{:S(2)}, u32[]{:S(2)}) collective-permute-start(bf16[64,512]{1,0:T(8,128)(2,1)S(1)} %get-tuple-element.113), channel_id=1, source_target_pairs={{0,2},{1,3},{2,0},{3,1},{4,6},{5,7},{6,4},{7,5},{8,10},{9,11},{10,... | collective-permute-start | bytes 196616 | tf_op jit(solution)/shard_map/ppermute | solution.py:372
  42.1 7.7 %collective-permute-start.26 = (bf16[64,512]{1,0:T(8,128)(2,1)S(1)}, bf16[64,512]{1,0:T(8,128)(2,1)S(1)}, u32[]{:S(2)}, u32[]{:S(2)}) collective-permute-start(bf16[64,512]{1,0:T(8,128)(2,1)S(1)} %carry.10.refs_0_), channel_id=1, source_target_pairs={{0,4},{1,5},{2,6},{3,7},{4,0},{5,1},{6,2},{7,3},{8,12},{9,13},{10,... | collective-permute-start | bytes 196616 | tf_op jit(solution)/shard_map/ppermute | solution.py:372
  45.6 5.7 %collective-permute-start.24 = (bf16[64,512]{1,0:T(8,128)(2,1)S(1)}, bf16[64,512]{1,0:T(8,128)(2,1)S(1)}, u32[]{:S(2)}, u32[]{:S(2)}) collective-permute-start(bf16[64,512]{1,0:T(8,128)(2,1)S(1)} %carry.9.refs_0_), channel_id=1, source_target_pairs={{0,4},{1,5},{2,6},{3,7},{4,0},{5,1},{6,2},{7,3},{8,12},{9,13},{10,... | collective-permute-start | bytes 196616 | tf_op jit(solution)/shard_map/ppermute | solution.py:372
  46.3 6.4 %collective-permute-start.28 = (bf16[64,512]{1,0:T(8,128)(2,1)S(1)}, bf16[64,512]{1,0:T(8,128)(2,1)S(1)}, u32[]{:S(2)}, u32[]{:S(2)}) collective-permute-start(bf16[64,512]{1,0:T(8,128)(2,1)S(1)} %carry.11.refs_0_), channel_id=1, source_target_pairs={{0,4},{1,5},{2,6},{3,7},{4,0},{5,1},{6,2},{7,3},{8,12},{9,13},{10,... | collective-permute-start | bytes 196616 | tf_op jit(solution)/shard_map/ppermute | solution.py:372
  50.0 4.3 %collective-permute-start.32 = (bf16[64,512]{1,0:T(8,128)(2,1)S(1)}, bf16[64,512]{1,0:T(8,128)(2,1)S(1)}, u32[]{:S(2)}, u32[]{:S(2)}) collective-permute-start(bf16[64,512]{1,0:T(8,128)(2,1)S(1)} %get-tuple-element.117.refs_4_), channel_id=1, source_target_pairs={{0,2},{1,3},{2,0},{3,1},{4,6},{5,7},{6,4},{7,5},{8,10},{9,11},{10,... | collective-permute-start | bytes 196616 | tf_op jit(solution)/shard_map/ppermute | solution.py:372
  51.5 4.3 %collective-permute-start.29 = (bf16[64,512]{1,0:T(8,128)(2,1)S(1)}, bf16[64,512]{1,0:T(8,128)(2,1)S(1)}, u32[]{:S(2)}, u32[]{:S(2)}) collective-permute-start(bf16[64,512]{1,0:T(8,128)(2,1)S(1)} %get-tuple-element.116.refs_0_), channel_id=1, source_target_pairs={{0,2},{1,3},{2,0},{3,1},{4,6},{5,7},{6,4},{7,5},{8,10},{9,11},{10,... | collective-permute-start | bytes 196616 | tf_op jit(solution)/shard_map/ppermute | solution.py:372
  52.9 4.3 %collective-permute-start.35 = (bf16[64,512]{1,0:T(8,128)(2,1)S(1)}, bf16[64,512]{1,0:T(8,128)(2,1)S(1)}, u32[]{:S(2)}, u32[]{:S(2)}) collective-permute-start(bf16[64,512]{1,0:T(8,128)(2,1)S(1)} %get-tuple-element.118.refs_8_), channel_id=1, source_target_pairs={{0,2},{1,3},{2,0},{3,1},{4,6},{5,7},{6,4},{7,5},{8,10},{9,11},{10,... | collective-permute-start | bytes 196616 | tf_op jit(solution)/shard_map/ppermute | solution.py:372
  54.3 3.0 %collective-permute-start.34 = (bf16[64,512]{1,0:T(8,128)(2,1)S(1)}, bf16[64,512]{1,0:T(8,128)(2,1)S(1)}, u32[]{:S(2)}, u32[]{:S(2)}) collective-permute-start(bf16[64,512]{1,0:T(8,128)(2,1)S(1)} %collective-permute-done.32.refs_5_), channel_id=1, source_target_pairs={{0,1},{1,0},{2,3},{3,2},{4,5},{5,4},{6,7},{7,6},{8,9},{9,8},{10,11... | collective-permute-start | bytes 196616 | tf_op jit(solution)/shard_map/ppermute | solution.py:383
  55.8 2.0 %collective-permute-start.30 = (bf16[64,512]{1,0:T(8,128)(2,1)S(1)}, bf16[64,512]{1,0:T(8,128)(2,1)S(1)}, u32[]{:S(2)}, u32[]{:S(2)}) collective-permute-start(bf16[64,512]{1,0:T(8,128)(2,1)S(1)} %get-tuple-element.116.refs_0_), channel_id=1, source_target_pairs={{0,1},{1,0},{2,3},{3,2},{4,5},{5,4},{6,7},{7,6},{8,9},{9,8},{10,11... | collective-permute-start | bytes 196616 | tf_op jit(solution)/shard_map/ppermute | solution.py:383
  55.8 2.0 %collective-permute-start.33 = (bf16[64,512]{1,0:T(8,128)(2,1)S(1)}, bf16[64,512]{1,0:T(8,128)(2,1)S(1)}, u32[]{:S(2)}, u32[]{:S(2)}) collective-permute-start(bf16[64,512]{1,0:T(8,128)(2,1)S(1)} %get-tuple-element.117.refs_4_), channel_id=1, source_target_pairs={{0,1},{1,0},{2,3},{3,2},{4,5},{5,4},{6,7},{7,6},{8,9},{9,8},{10,11... | collective-permute-start | bytes 196616 | tf_op jit(solution)/shard_map/ppermute | solution.py:383
  56.3 1.5 %collective-permute-start.36 = (bf16[64,512]{1,0:T(8,128)(2,1)S(1)}, bf16[64,512]{1,0:T(8,128)(2,1)S(1)}, u32[]{:S(2)}, u32[]{:S(2)}) collective-permute-start(bf16[64,512]{1,0:T(8,128)(2,1)S(1)} %get-tuple-element.118.refs_8_), channel_id=1, source_target_pairs={{0,1},{1,0},{2,3},{3,2},{4,5},{5,4},{6,7},{7,6},{8,9},{9,8},{10,11... | collective-permute-start | bytes 196616 | tf_op jit(solution)/shard_map/ppermute | solution.py:383
  57.3 1.3 %collective-permute-start.31 = (bf16[64,512]{1,0:T(8,128)(2,1)S(1)}, bf16[64,512]{1,0:T(8,128)(2,1)S(1)}, u32[]{:S(2)}, u32[]{:S(2)}) collective-permute-start(bf16[64,512]{1,0:T(8,128)(2,1)S(1)} %collective-permute-done.29.refs_1_), channel_id=1, source_target_pairs={{0,1},{1,0},{2,3},{3,2},{4,5},{5,4},{6,7},{7,6},{8,9},{9,8},{10,11... | collective-permute-start | bytes 196616 | tf_op jit(solution)/shard_map/ppermute | solution.py:383
  57.3 1.4 %collective-permute-start.37 = (bf16[64,512]{1,0:T(8,128)(2,1)S(1)}, bf16[64,512]{1,0:T(8,128)(2,1)S(1)}, u32[]{:S(2)}, u32[]{:S(2)}) collective-permute-start(bf16[64,512]{1,0:T(8,128)(2,1)S(1)} %collective-permute-done.35.refs_9_), channel_id=1, source_target_pairs={{0,1},{1,0},{2,3},{3,2},{4,5},{5,4},{6,7},{7,6},{8,9},{9,8},{10,11... | collective-permute-start | bytes 196616 | tf_op jit(solution)/shard_map/ppermute | solution.py:383
  60.0 7.6 %collective-permute-start.38 = (bf16[96,512]{1,0:T(8,128)(2,1)S(1)}, bf16[96,512]{1,0:T(8,128)(2,1)S(1)}, u32[]{:S(2)}, u32[]{:S(2)}) collective-permute-start(bf16[96,512]{1,0:T(8,128)(2,1)S(1)} %get-tuple-element.138), channel_id=1, source_target_pairs={{0,6},{1,7},{2,4},{3,5},{4,2},{5,3},{6,0},{7,1},{8,14},{9,15},{10,... | collective-permute-start | bytes 294920 | tf_op jit(solution)/shard_map/ppermute | solution.py:367
  62.3 9.4 %collective-permute-start.39 = (bf16[96,512]{1,0:T(8,128)(2,1)S(1)}, bf16[96,512]{1,0:T(8,128)(2,1)S(1)}, u32[]{:S(2)}, u32[]{:S(2)}) collective-permute-start(bf16[96,512]{1,0:T(8,128)(2,1)S(1)} %get-tuple-element.139), channel_id=1, source_target_pairs={{0,4},{1,5},{2,6},{3,7},{4,0},{5,1},{6,2},{7,3},{8,12},{9,13},{10,... | collective-permute-start | bytes 294920 | tf_op jit(solution)/shard_map/ppermute | solution.py:367
  62.4 9.3 %collective-permute-start.40 = (bf16[96,512]{1,0:T(8,128)(2,1)S(1)}, bf16[96,512]{1,0:T(8,128)(2,1)S(1)}, u32[]{:S(2)}, u32[]{:S(2)}) collective-permute-start(bf16[96,512]{1,0:T(8,128)(2,1)S(1)} %get-tuple-element.140), channel_id=1, source_target_pairs={{0,2},{1,3},{2,0},{3,1},{4,6},{5,7},{6,4},{7,5},{8,10},{9,11},{10,... | collective-permute-start | bytes 294920 | tf_op jit(solution)/shard_map/ppermute | solution.py:367
  (1 other events, 1.0 us)

commit v11 on v10

--- a/solution.py
+++ b/solution.py
@@ -66,15 +66,21 @@
     return packed[:g], packed[g : 2 * g], down
 
 
-def update_forward(w1t, w3t, w2, keys, push):
+def gate_and_up(w1t, w3t, keys):
     gate_pre, up_pre = nt(w1t, keys), nt(w3t, keys)
     silu, slope, curvature = silu_parts(gate_pre)
-    mixed = (silu * up_pre).astype(BF16)
+    return up_pre, silu, slope, curvature, (silu * up_pre).astype(BF16)
+
+
+def back_through_down(w2, push, up_slope, silu):
     down_back = nn(w2, push)
-    back_slope = down_back * slope
-    gate_back = (down_back * up_pre * slope).astype(BF16)
-    up_back = (down_back * silu).astype(BF16)
-    return up_pre, silu, slope, curvature, mixed, down_back, back_slope, gate_back, up_back
+    return down_back, (down_back * up_slope).astype(BF16), (down_back * silu).astype(BF16)
+
+
+def update_forward(w1t, w3t, w2, keys, push):
+    up_pre, silu, slope, curvature, mixed = gate_and_up(w1t, w3t, keys)
+    down_back, gate_back, up_back = back_through_down(w2, push, up_pre * slope, silu)
+    return up_pre, silu, slope, curvature, mixed, down_back, down_back * slope, gate_back, up_back
 
 
 def apply_forward(f1t, f3t, f2t, queries, weighted):
@@ -87,14 +93,15 @@
     return output, mixed, q_up * slope, silu, jnp.concatenate([square, dot], axis=0)
 
 
-def apply_backward(f2t, sums, full_width, output, weighted, up_slope, silu):
+def output_back(sums, full_width, output, weighted):
     inverse = lax.rsqrt(sums[0:1] / full_width + EPSILON)
     scale = inverse * inverse * inverse * sums[1:2] / full_width
-    out_back = (inverse * weighted - output * scale).astype(BF16)
+    return (inverse * weighted - output * scale).astype(BF16)
+
+
+def apply_backward(f2t, out_back, up_slope, silu):
     q_back = tn(f2t, out_back)
-    gate_back = (q_back * up_slope).astype(BF16)
-    up_back = (q_back * silu).astype(BF16)
-    return gate_back, up_back, out_back
+    return (q_back * up_slope).astype(BF16), (q_back * silu).astype(BF16)
 
 
 def second_adjoint(c1t, c3t, c2t, keys, push, up_slope, silu, back_slope, back_curve):
@@ -175,52 +182,68 @@
             place_half(ref, half, p, c, chips, folds if k == 2 else 1)
 
 
-def products_of_core(chips, folds, order, gate_ref, up_ref, down_ref, tokens, hidden):
+def rows_of_core(ref, order, chips):
     core = lax.axis_index("tok") % CORES
-
-    def picked(ref):
-        rows = ref.shape[0] // (chips * CORES)
-        blocks = [
-            ref[pl.ds(pl.multiple_of((chip * CORES + core) * rows, rows), rows), :] for chip in order
-        ]
-        return jnp.concatenate(blocks, axis=0)
-
-    gate, up = nn(picked(gate_ref), tokens), nn(picked(up_ref), tokens)
-    down = nt(picked(down_ref), hidden)
-    g, d = gate.shape[0] // chips, down.shape[0] // chips
-    pieces = []
-    for k in range(chips):
-        parts = [down[k * d + i * g : k * d + (i + 1) * g] for i in range(folds)]
-        pieces.append(
-            (gate[k * g : (k + 1) * g], up[k * g : (k + 1) * g], jnp.concatenate(parts, axis=1))
-        )
-    return pieces
+    rows = ref.shape[0] // (chips * CORES)
+    blocks = [
+        ref[pl.ds(pl.multiple_of((chip * CORES + core) * rows, rows), rows), :] for chip in order
+    ]
+    return jnp.concatenate(blocks, axis=0)
+
+
+def fold(rows, chips, folds):
+    height = rows.shape[0] // (chips * folds)
+    parts = [rows[i * height : (i + 1) * height] for i in range(chips * folds)]
+    wide = [jnp.concatenate(parts[k : k + folds], axis=1) for k in range(0, len(parts), folds)]
+    return jnp.concatenate(wide, axis=0)
 
 
 def send_pieces(chips, folds, operands, outs):
+    gate_ref, up_ref, down_ref, tokens, hidden = operands
     chip = lax.axis_index("tok") // CORES
     order = [partner(chip, step, chips) for step in range(chips)]
-    for out, parts in zip(outs, products_of_core(chips, folds, order, *operands)):
+    sums = [nn(rows_of_core(ref, order, chips), tokens) for ref in (gate_ref, up_ref)]
+    sums.append(fold(nt(rows_of_core(down_ref, order, chips), hidden), chips, folds))
+    g = sums[0].shape[0] // chips
+    for k, out in enumerate(outs):
+        parts = [x[k * g : (k + 1) * g] for x in sums]
         out[...] = jnp.concatenate(parts, axis=0).astype(out.dtype)
 
 
-def send_halves(chips, folds, operands, outs):
+def halves_order(chips):
     parity = lax.axis_index("tok") // CORES % 2
-    half = chips // 2
-    order = [2 * k + p for p in (parity, 1 - parity) for k in range(half)]
-    pieces = products_of_core(chips, folds, order, *operands)
-    for k in range(3):
-        kept, given = ([p[k] for p in part] for part in (pieces[:half], pieces[half:]))
-        outs[k][...] = jnp.concatenate(kept, axis=0)
-        outs[3 + k][...] = jnp.concatenate(given, axis=0).astype(BF16)
-
-
-def update_kernel(chips, folds, ko, kx, vo, vx, ro, rx, w1t, w3t, w2, *rest):
-    outs, (gate, up, push) = rest[:6], rest[6:]
-    keys = both(ko, kx)
+    return [2 * k + p for p in (parity, 1 - parity) for k in range(chips // 2)]
+
+
+def send_halves(sums, kept, given):
+    half = kept.shape[0]
+    kept[...], given[...] = sums[:half], sums[half:].astype(BF16)
+
+
+def send_down(chips, folds, rows_ref, hidden, kept, given):
+    sums = nt(rows_of_core(rows_ref, halves_order(chips), chips), hidden)
+    send_halves(fold(sums, chips, folds), kept, given)
+
+
+def send_gate_and_up(chips, gate_ref, up_ref, tokens, gate_kept, up_kept, gate_given, up_given):
+    order = halves_order(chips)
+    send_halves(nn(rows_of_core(gate_ref, order, chips), tokens), gate_kept, gate_given)
+    send_halves(nn(rows_of_core(up_ref, order, chips), tokens), up_kept, up_given)
+
+
+def update_down_kernel(
+    chips, folds, ko, kx, vo, vx, ro, rx, w1t, w3t, kept, given, push, up_slope_ref, silu_ref
+):
     push[...] = push_of(both(ro, rx, 1), both(vo, vx))
-    *_, mixed, _, _, gate[...], up[...] = update_forward(w1t[...], w3t[...], w2[...], keys, push[...])
-    send_halves(chips, folds, (gate, up, push, keys, mixed), outs)
+    up_pre, silu, slope, _, mixed = gate_and_up(w1t[...], w3t[...], both(ko, kx))
+    send_down(chips, folds, push, mixed, kept, given)
+    up_slope_ref[...], silu_ref[...] = up_pre * slope, silu
+
+
+def update_gate_kernel(chips, ko, kx, w2, push, up_slope, silu, *rest):
+    outs, (gate, up) = rest[:4], rest[4:]
+    _, gate[...], up[...] = back_through_down(w2[...], push[...], up_slope[...], silu[...])
+    send_gate_and_up(chips, gate, up, both(ko, kx), *outs)
 
 
 def saved_kernel(
@@ -303,12 +326,12 @@
     for part in parts[1:]:
         sums = sums + part[...]
     f2t, output, weighted, mixed, up_slope, silu, qo, qx, gate_back, up_back = refs[:10]
-    outs, (gate, up, down) = refs[10:16], refs[16:]
-    width = heads * output.shape[0]
-    gate[...], up[...], down[...] = apply_backward(
-        f2t[...], sums, width, output[...], weighted[...], up_slope[...], silu[...]
-    )
-    send_halves(chips, folds, (gate, up, down, both(qo, qx), mixed[...]), outs)
+    down_kept, down_given, *outs = refs[10:16]
+    gate, up, out_back = refs[16:]
+    out_back[...] = output_back(sums, heads * output.shape[0], output[...], weighted[...])
+    send_down(chips, folds, out_back, mixed[...], down_kept, down_given)
+    gate[...], up[...] = apply_backward(f2t[...], out_back[...], up_slope[...], silu[...])
+    send_gate_and_up(chips, gate, up, both(qo, qx), *outs)
     own = gate_back.shape[1]
     gate_back[...], up_back[...] = gate[:, :own], up[:, :own]
 
@@ -477,7 +500,8 @@
     product = 2 * n * dh * fh
 
     half = (g * chips // 2, dh)
-    half_shares = [(half, F32)] * 3 + [(half, BF16)] * 3
+    down_halves = [(half, F32), (half, BF16)]
+    gate_halves = [(half, F32)] * 2 + [(half, BF16)] * 2
     matrices = [((fh, dh), BF16), ((fh, dh), BF16), ((dh, fh), BF16)]
     sums_scratch = [((fh, dh), F32), ((fh, dh), F32), ((dh, fh), F32)]
     operands = [((fh, n), BF16), ((fh, n), BF16), ((dh, n), BF16)]
@@ -492,14 +516,22 @@
     keys_values = (
         key_input, key_other, value_input, value_other, rates, rate_other, w1t, w3t, w2,
     )
-    sums = call(
-        functools.partial(update_kernel, chips, folds),
-        half_shares,
-        keys_values,
-        operands,
-        "update",
-        6 * product,
-    )
+    down_kept, down_given, push, up_slope, silu = call(
+        functools.partial(update_down_kernel, chips, folds),
+        down_halves + [((dh, n), BF16), hidden, hidden],
+        keys_values[:-1],
+        name="update_down",
+        flops=3 * product,
+    )
+    gate_kept, up_kept, gate_given, up_given = call(
+        functools.partial(update_gate_kernel, chips),
+        gate_halves,
+        (key_input, key_other, w2, push, up_slope, silu),
+        operands[:2],
+        "update_gate",
+        3 * product,
+    )
+    sums = gate_kept, up_kept, down_kept, gate_given, up_given, down_given
     *saved, weighted, p1, p3, p2 = call(
         functools.partial(saved_kernel, chips, folds),
         [((dh, n), BF16)] + [hidden] * 4 + [own_hidden] * 3 + [((dh, n), F32)] + [(half, F32)] * 3,
@@ -529,9 +561,9 @@
         name="apply",
         flops=3 * product,
     )
-    q_gate_back, q_up_back, *sums = call(
+    q_gate_back, q_up_back, down_kept, down_given, gate_kept, up_kept, gate_given, up_given = call(
         functools.partial(back_kernel, chips, folds, heads),
-        [own_hidden] * 2 + half_shares,
+        [own_hidden] * 2 + down_halves + gate_halves,
         (
             *head_parts(part, heads),
             f2t, output, weighted, q_mixed, q_slope, q_silu, query_input, query_other,
@@ -540,6 +572,7 @@
         "apply_back",
         4 * product,
     )
+    sums = gate_kept, up_kept, down_kept, gate_given, up_given, down_given
     (query_grad,) = call(
         query_kernel,
         [((own, dh), BF16)],
@@ -616,9 +649,8 @@
     f1t, f3t, f2t = whole_matrices(*blocks, tok, count, fh)
     output, q_mixed, q_slope, q_silu, part = apply_forward(f1t, f3t, f2t, queries, weighted)
     sums = lax.psum(part, "head")
-    q_gate_back, q_up_back, out_back = apply_backward(
-        f2t, sums, heads * dh, output, weighted, q_slope, q_silu
-    )
+    out_back = output_back(sums, heads * dh, output, weighted)
+    q_gate_back, q_up_back = apply_backward(f2t, out_back, q_slope, q_silu)
     grads = nn(q_gate_back, queries), nn(q_up_back, queries), nt(out_back, q_mixed)
     piece, sent = sliced_pieces(*grads, tok, count)
     query_grad = (tn(q_gate_back[:, :own], f1t) + tn(q_up_back[:, :own], f3t)).astype(BF16)

time: 72.6 us -> 72.5 us (level)
    ppermute x18, waiting for transfers between devices: 11.6 us -> 10.7 us  [to_chip(): return lax.ppermute(x, 'tok', chip_perm(chips * CORES, step))]
    pallas_call x20 -> x21, Pallas kernels: 9.33 us -> 9.45 us  [call(): pl.pallas_call(kernel, out_shape=[jax.ShapeDtypeStruct(s, t) for s, t in...]
  transfers between devices with their start and end apart: 41 -> 41, of which waited for: 23 -> 20; matrix products, arithmetic and copies ran while one was open for 2% -> 2% of each run, Pallas kernels for 8% -> 8%
where the time goes in v11:
time: 72.5 us; the launch traced here: 72.4 us
  starting transfers between devices  38.6 us (53%)
  waiting for transfers between devices  21.4 us (30%)
  Pallas kernels  9.45 us (13%)
  local copies, waits for them, and re-layouts  2.09 us (3%)
  between operations  0.87 us (1%)
    ppermute x18, starting transfers between devices, to_chip(): return lax.ppermute(x, 'tok', chip_perm(chips * CORES, step))  26.9 us
    ppermute x18, waiting for transfers between devices, to_chip(): return lax.ppermute(x, 'tok', chip_perm(chips * CORES, step))  10.7 us
    pallas_call x21, Pallas kernels, call(): pl.pallas_call(kernel, out_shape=[jax.ShapeDtypeStruct(s, t) for s, t in...  9.45 us
    ppermute x3, waiting for transfers between devices, exchange(): lax.ppermute(pieces[s], 'tok', chip_perm(count, s))  5.24 us
    ppermute x3, starting transfers between devices, exchange(): lax.ppermute(pieces[s], 'tok', chip_perm(count, s))  4.45 us
    ppermute x3, starting transfers between devices, head_parts(): lax.ppermute(part, 'head', [(h, partner(h, step, heads)) for h in range(h...  3.55 us
    ppermute x3, waiting for transfers between devices, head_parts(): lax.ppermute(part, 'head', [(h, partner(h, step, heads)) for h in range(h...  3.35 us
    ppermute x12, starting transfers between devices, from_owners(): cross = lambda x: lax.ppermute(x, 'tok', core_perm(chips * CORES))  2.12 us
  transfers between devices with their start and end apart: 41, of which 20 were waited for; matrix products, arithmetic and copies ran while one was open for 2% of the time, Pallas kernels for 8%

profile of v11, /device:TPU:0, one launch (start us, length us, event | category | flops | bytes accessed | tf_op | source)
XLA Modules:
  0.0 72.4 jit_solution(6917702410633661067)
XLA Ops:
  0.6 0.5 collective-permute-start.1
  2.2 1.1 %copy.15 = bf16[1,512,256]{1,2,0:T(8,128)(2,1)S(1)} copy(bf16[1,512,256]{2,1,0:T(8,128)(2,1)} %param.15) | data formatting | bytes 524288 | tf_op args[6]
  3.5 0.7 %copy-done = bf16[256,512]{1,0:T(8,128)(2,1)S(1)} copy-done((bf16[256,512]{1,0:T(8,128)(2,1)S(1)}, bf16[256,512]{1,0:T(8,128)(2,1)}, u32[]{:S(2)}) %copy-start) | copy-done | bytes 262168
  4.3 0.8 %update_down.1 = (f32[64,512]{1,0:T(8,128)S(1)}, bf16[64,512]{1,0:T(8,128)(2,1)S(1)}, bf16[512,512]{1,0:T(8,128)(2,1)S(1)}, f32[256,512]{1,0:T(8,128)S(1)}, f32[256,512]{1,0:T(8,128)S(1)}) custom-call(bf16[256,512]{1,0:T(8,128)(2,1)S(1)} %copy-done, bf16[256,512]{1,0:T(8,128)(2,1)S(1)} %collective-permute-done.kx.refs_13_, bf16[256,512]{1,0:T(8,128)(2,1)S(1)} %copy-done.3, ...), custom_call_target="tpu_custom_call" | custom-call | flops 402653184 | bytes 1574912 | tf_op jit(solution)/shard_map/update_down/pallas_call | solution.py:372
  5.1 2.7 %collective-permute-start.8 = (bf16[64,512]{1,0:T(8,128)(2,1)S(1)}, bf16[64,512]{1,0:T(8,128)(2,1)S(1)}, u32[]{:S(2)}, u32[]{:S(2)}) collective-permute-start(bf16[64,512]{1,0:T(8,128)(2,1)S(1)} %get-tuple-element.91), channel_id=1, source_target_pairs={{0,2},{1,3},{2,0},{3,1},{4,6},{5,7},{6,4},{7,5},{8,10},{9,11},{10,... | collective-permute-start | bytes 196616 | tf_op jit(solution)/shard_map/ppermute | solution.py:395
  7.8 0.6 update_gate.1
  8.6 1.9 %collective-permute-start.6 = (bf16[64,512]{1,0:T(8,128)(2,1)S(1)}, bf16[64,512]{1,0:T(8,128)(2,1)S(1)}, u32[]{:S(2)}, u32[]{:S(2)}) collective-permute-start(bf16[64,512]{1,0:T(8,128)(2,1)S(1)} %get-tuple-element.87), channel_id=1, source_target_pairs={{0,2},{1,3},{2,0},{3,1},{4,6},{5,7},{6,4},{7,5},{8,10},{9,11},{10,... | collective-permute-start | bytes 196616 | tf_op jit(solution)/shard_map/ppermute | solution.py:395
  10.6 2.8 %collective-permute-start.9 = (bf16[64,512]{1,0:T(8,128)(2,1)S(1)}, bf16[64,512]{1,0:T(8,128)(2,1)S(1)}, u32[]{:S(2)}, u32[]{:S(2)}) collective-permute-start(bf16[64,512]{1,0:T(8,128)(2,1)S(1)} %carry.8.refs_0_), channel_id=1, source_target_pairs={{0,4},{1,5},{2,6},{3,7},{4,0},{5,1},{6,2},{7,3},{8,12},{9,13},{10,... | collective-permute-start | bytes 196616 | tf_op jit(solution)/shard_map/ppermute | solution.py:395
  13.4 2.7 %collective-permute-start.5 = (bf16[64,512]{1,0:T(8,128)(2,1)S(1)}, bf16[64,512]{1,0:T(8,128)(2,1)S(1)}, u32[]{:S(2)}, u32[]{:S(2)}) collective-permute-start(bf16[64,512]{1,0:T(8,128)(2,1)S(1)} %carry.6.refs_0_), channel_id=1, source_target_pairs={{0,4},{1,5},{2,6},{3,7},{4,0},{5,1},{6,2},{7,3},{8,12},{9,13},{10,... | collective-permute-start | bytes 196616 | tf_op jit(solution)/shard_map/ppermute | solution.py:395
  16.1 1.3 %collective-permute-start.7 = (bf16[64,512]{1,0:T(8,128)(2,1)S(1)}, bf16[64,512]{1,0:T(8,128)(2,1)S(1)}, u32[]{:S(2)}, u32[]{:S(2)}) collective-permute-start(bf16[64,512]{1,0:T(8,128)(2,1)S(1)} %carry.7.refs_0_), channel_id=1, source_target_pairs={{0,4},{1,5},{2,6},{3,7},{4,0},{5,1},{6,2},{7,3},{8,12},{9,13},{10,... | collective-permute-start | bytes 196616 | tf_op jit(solution)/shard_map/ppermute | solution.py:395
  17.4 1.1 %saved.1 = (bf16[512,512]{1,0:T(8,128)(2,1)S(1)}, f32[256,512]{1,0:T(8,128)S(1)}, f32[256,512]{1,0:T(8,128)S(1)}, f32[256,512]{1,0:T(8,128)S(1)}, f32[256,512]{1...) custom-call(bf16[256,512]{1,0:T(8,128)(2,1)S(1)} %copy-done, ...), custom_call_target="tpu_custom_call" | custom-call | flops 402653184 | bytes 2363392 | tf_op jit(solution)/shard_map/saved/pallas_call | solution.py:372
  18.7 1.8 %collective-permute-start.16 = (bf16[64,512]{1,0:T(8,128)(2,1)S(1)}, bf16[64,512]{1,0:T(8,128)(2,1)S(1)}, u32[]{:S(2)}, u32[]{:S(2)}) collective-permute-start(bf16[64,512]{1,0:T(8,128)(2,1)S(1)} %get-tuple-element.96.refs_8_), channel_id=1, source_target_pairs={{0,2},{1,3},{2,0},{3,1},{4,6},{5,7},{6,4},{7,5},{8,10},{9,11},{10,... | collective-permute-start | bytes 196616 | tf_op jit(solution)/shard_map/ppermute | solution.py:395
  20.4 1.4 %collective-permute-done.5.refs_1_ = bf16[64,512]{1,0:T(8,128)(2,1)S(1)} collective-permute-done((bf16[64,512]{1,0:T(8,128)(2,1)S(1)}, bf16[64,512]{1,0:T(8,128)(2,1)S(1)}, u32[]{:S(2)}, u32[]{:S(2)}) %collective-permute-start.5) | collective-permute-done | bytes 65568 | tf_op jit(solution)/shard_map/ppermute | solution.py:395
  22.0 0.5 collective-permute-start.10
  23.0 1.3 %collective-permute-start.13 = (bf16[64,512]{1,0:T(8,128)(2,1)S(1)}, bf16[64,512]{1,0:T(8,128)(2,1)S(1)}, u32[]{:S(2)}, u32[]{:S(2)}) collective-permute-start(bf16[64,512]{1,0:T(8,128)(2,1)S(1)} %get-tuple-element.95.refs_4_), channel_id=1, source_target_pairs={{0,2},{1,3},{2,0},{3,1},{4,6},{5,7},{6,4},{7,5},{8,10},{9,11},{10,... | collective-permute-start | bytes 196616 | tf_op jit(solution)/shard_map/ppermute | solution.py:395
  24.3 2.4 %collective-permute-done.10.refs_1_ = bf16[64,512]{1,0:T(8,128)(2,1)S(1)} collective-permute-done((bf16[64,512]{1,0:T(8,128)(2,1)S(1)}, bf16[64,512]{1,0:T(8,128)(2,1)S(1)}, u32[]{:S(2)}, u32[]{:S(2)}) %collective-permute-start.10) | collective-permute-done | bytes 65568 | tf_op jit(solution)/shard_map/ppermute | solution.py:395
  26.7 0.5 collective-permute-start.14
  27.4 0.5 collective-permute-start.17
  28.0 0.7 collective-permute-done.15.refs_7_
  29.2 0.8 %apply.1 = (bf16[256,512]{1,0:T(8,128)(2,1)S(1)}, bf16[256,512]{1,0:T(8,128)(2,1)S(1)}, bf16[512,256]{1,0:T(8,128)(2,1)S(1)}, f32[512,512]{1,0:T(8,128)S(1)}, bf...) custom-call(bf16[64,512]{1,0:T(8,128)(2,1)S(1)} %get-tuple-element.94.refs_0, ...), custom_call_target="tpu_custom_call" | custom-call | flops 402653184 | bytes 2359296 | tf_op jit(solution)/shard_map/apply/pallas_call | solution.py:372
  30.0 2.8 %collective-permute-start.22 = (f32[2,512]{1,0:T(2,128)S(1)}, f32[2,512]{1,0:T(2,128)S(1)}, u32[]{:S(2)}, u32[]{:S(2)}) collective-permute-start(f32[2,512]{1,0:T(2,128)S(1)} %get-tuple-element.98.refs_0_), channel_id=1, source_target_pairs={{0,24},{8,16},{16,8},{24,0},{1,25},{9,17},{17,9},{25,1},{2,26},{10... | collective-permute-start | bytes 12296 | tf_op jit(solution)/shard_map/ppermute | solution.py:413
  33.5 1.0 %collective-permute-done.22.refs_3_ = f32[2,512]{1,0:T(2,128)S(1)} collective-permute-done((f32[2,512]{1,0:T(2,128)S(1)}, f32[2,512]{1,0:T(2,128)S(1)}, u32[]{:S(2)}, u32[]{:S(2)}) %collective-permute-start.22) | collective-permute-done | bytes 4128 | tf_op jit(solution)/shard_map/ppermute | solution.py:413
  34.5 1.8 %collective-permute-done.21.refs_2_ = f32[2,512]{1,0:T(2,128)S(1)} collective-permute-done((f32[2,512]{1,0:T(2,128)S(1)}, f32[2,512]{1,0:T(2,128)S(1)}, u32[]{:S(2)}, u32[]{:S(2)}) %collective-permute-start.21) | collective-permute-done | bytes 4128 | tf_op jit(solution)/shard_map/ppermute | solution.py:413
  36.9 0.8 %apply_back.1 = (bf16[256,256]{1,0:T(8,128)(2,1)S(1)}, bf16[256,256]{1,0:T(8,128)(2,1)S(1)}, f32[64,512]{1,0:T(8,128)S(1)}, bf16[64,512]{1,0:T(8,128)(2,1)S(1)},...) custom-call(f32[2,512]{1,0:T(2,128)S(1)} %get-tuple-element.98.refs_0, ...), custom_call_target="tpu_custom_call" | custom-call | flops 536870912 | bytes 4210688 | tf_op jit(solution)/shard_map/apply_back/pallas_call | solution.py:372
  37.7 0.9 %collective-permute-start.25 = (bf16[64,512]{1,0:T(8,128)(2,1)S(1)}, bf16[64,512]{1,0:T(8,128)(2,1)S(1)}, u32[]{:S(2)}, u32[]{:S(2)}) collective-permute-start(bf16[64,512]{1,0:T(8,128)(2,1)S(1)} %get-tuple-element.115), channel_id=1, source_target_pairs={{0,2},{1,3},{2,0},{3,1},{4,6},{5,7},{6,4},{7,5},{8,10},{9,11},{10,... | collective-permute-start | bytes 196616 | tf_op jit(solution)/shard_map/ppermute | solution.py:395
  38.6 1.2 %collective-permute-start.23 = (bf16[64,512]{1,0:T(8,128)(2,1)S(1)}, bf16[64,512]{1,0:T(8,128)(2,1)S(1)}, u32[]{:S(2)}, u32[]{:S(2)}) collective-permute-start(bf16[64,512]{1,0:T(8,128)(2,1)S(1)} %get-tuple-element.111), channel_id=1, source_target_pairs={{0,2},{1,3},{2,0},{3,1},{4,6},{5,7},{6,4},{7,5},{8,10},{9,11},{10,... | collective-permute-start | bytes 196616 | tf_op jit(solution)/shard_map/ppermute | solution.py:395
  39.8 0.8 %collective-permute-start.27 = (bf16[64,512]{1,0:T(8,128)(2,1)S(1)}, bf16[64,512]{1,0:T(8,128)(2,1)S(1)}, u32[]{:S(2)}, u32[]{:S(2)}) collective-permute-start(bf16[64,512]{1,0:T(8,128)(2,1)S(1)} %get-tuple-element.119), channel_id=1, source_target_pairs={{0,2},{1,3},{2,0},{3,1},{4,6},{5,7},{6,4},{7,5},{8,10},{9,11},{10,... | collective-permute-start | bytes 196616 | tf_op jit(solution)/shard_map/ppermute | solution.py:395
  40.6 1.4 %collective-permute-done.25.got = bf16[64,512]{1,0:T(8,128)(2,1)S(1)} collective-permute-done((bf16[64,512]{1,0:T(8,128)(2,1)S(1)}, bf16[64,512]{1,0:T(8,128)(2,1)S(1)}, u32[]{:S(2)}, u32[]{:S(2)}) %collective-permute-start.25) | collective-permute-done | bytes 65568 | tf_op jit(solution)/shard_map/ppermute | solution.py:395
  42.1 3.2 %collective-permute-start.26 = (bf16[64,512]{1,0:T(8,128)(2,1)S(1)}, bf16[64,512]{1,0:T(8,128)(2,1)S(1)}, u32[]{:S(2)}, u32[]{:S(2)}) collective-permute-start(bf16[64,512]{1,0:T(8,128)(2,1)S(1)} %carry.10.refs_0_), channel_id=1, source_target_pairs={{0,4},{1,5},{2,6},{3,7},{4,0},{5,1},{6,2},{7,3},{8,12},{9,13},{10,... | collective-permute-start | bytes 196616 | tf_op jit(solution)/shard_map/ppermute | solution.py:395
  45.3 0.7 collective-permute-start.24
  46.0 2.4 %collective-permute-start.28 = (bf16[64,512]{1,0:T(8,128)(2,1)S(1)}, bf16[64,512]{1,0:T(8,128)(2,1)S(1)}, u32[]{:S(2)}, u32[]{:S(2)}) collective-permute-start(bf16[64,512]{1,0:T(8,128)(2,1)S(1)} %carry.11.refs_0_), channel_id=1, source_target_pairs={{0,4},{1,5},{2,6},{3,7},{4,0},{5,1},{6,2},{7,3},{8,12},{9,13},{10,... | collective-permute-start | bytes 196616 | tf_op jit(solution)/shard_map/ppermute | solution.py:395
  48.3 1.5 %collective-permute-done.26.refs_1_ = bf16[64,512]{1,0:T(8,128)(2,1)S(1)} collective-permute-done((bf16[64,512]{1,0:T(8,128)(2,1)S(1)}, bf16[64,512]{1,0:T(8,128)(2,1)S(1)}, u32[]{:S(2)}, u32[]{:S(2)}) %collective-permute-start.26) | collective-permute-done | bytes 65568 | tf_op jit(solution)/shard_map/ppermute | solution.py:395
  50.1 0.9 %collective-permute-done.24.refs_1_ = bf16[64,512]{1,0:T(8,128)(2,1)S(1)} collective-permute-done((bf16[64,512]{1,0:T(8,128)(2,1)S(1)}, bf16[64,512]{1,0:T(8,128)(2,1)S(1)}, u32[]{:S(2)}, u32[]{:S(2)}) %collective-permute-start.24) | collective-permute-done | bytes 65568 | tf_op jit(solution)/shard_map/ppermute | solution.py:395
  51.1 1.2 %collective-permute-start.29 = (bf16[64,512]{1,0:T(8,128)(2,1)S(1)}, bf16[64,512]{1,0:T(8,128)(2,1)S(1)}, u32[]{:S(2)}, u32[]{:S(2)}) collective-permute-start(bf16[64,512]{1,0:T(8,128)(2,1)S(1)} %get-tuple-element.122.refs_0_), channel_id=1, source_target_pairs={{0,2},{1,3},{2,0},{3,1},{4,6},{5,7},{6,4},{7,5},{8,10},{9,11},{10,... | collective-permute-start | bytes 196616 | tf_op jit(solution)/shard_map/ppermute | solution.py:395
  52.5 1.3 %collective-permute-start.35 = (bf16[64,512]{1,0:T(8,128)(2,1)S(1)}, bf16[64,512]{1,0:T(8,128)(2,1)S(1)}, u32[]{:S(2)}, u32[]{:S(2)}) collective-permute-start(bf16[64,512]{1,0:T(8,128)(2,1)S(1)} %get-tuple-element.124.refs_8_), channel_id=1, source_target_pairs={{0,2},{1,3},{2,0},{3,1},{4,6},{5,7},{6,4},{7,5},{8,10},{9,11},{10,... | collective-permute-start | bytes 196616 | tf_op jit(solution)/shard_map/ppermute | solution.py:395
  53.8 0.6 collective-permute-done.32.refs_5_
  54.3 1.1 %collective-permute-done.29.refs_1_ = bf16[64,512]{1,0:T(8,128)(2,1)S(1)} collective-permute-done((bf16[64,512]{1,0:T(8,128)(2,1)S(1)}, bf16[64,512]{1,0:T(8,128)(2,1)S(1)}, u32[]{:S(2)}, u32[]{:S(2)}) %collective-permute-start.29) | collective-permute-done | bytes 65568 | tf_op jit(solution)/shard_map/ppermute | solution.py:395
  55.9 0.9 %collective-permute-done.35.refs_9_ = bf16[64,512]{1,0:T(8,128)(2,1)S(1)} collective-permute-done((bf16[64,512]{1,0:T(8,128)(2,1)S(1)}, bf16[64,512]{1,0:T(8,128)(2,1)S(1)}, u32[]{:S(2)}, u32[]{:S(2)}) %collective-permute-start.35) | collective-permute-done | bytes 65568 | tf_op jit(solution)/shard_map/ppermute | solution.py:395
  56.8 0.5 collective-permute-start.37
  57.3 0.7 %collective-permute-done.31.refs_3_ = bf16[64,512]{1,0:T(8,128)(2,1)S(1)} collective-permute-done((bf16[64,512]{1,0:T(8,128)(2,1)S(1)}, bf16[64,512]{1,0:T(8,128)(2,1)S(1)}, u32[]{:S(2)}, u32[]{:S(2)}) %collective-permute-start.31) | collective-permute-done | bytes 65568 | tf_op jit(solution)/shard_map/ppermute | solution.py:406
  58.2 1.3 %second_adjoint.1 = (bf16[256,512]{1,0:T(8,128)(2,1)S(1)}, bf16[256,512]{1,0:T(8,128)(2,1)S(1)}, bf16[512,256]{1,0:T(8,128)(2,1)S(1)}, bf16[256,256]{1,0:T(8,128...) custom-call(bf16[64,512]{1,0:T(8,128)(2,1)S(1)} %get-tuple-element.1, ...), custom_call_target="tpu_custom_call" | custom-call | flops 805306368 | bytes 3932160 | tf_op jit(solution)/shard_map/second_adjoint/pallas_call | solution.py:372
  59.6 2.4 %collective-permute-start.38 = (bf16[96,512]{1,0:T(8,128)(2,1)S(1)}, bf16[96,512]{1,0:T(8,128)(2,1)S(1)}, u32[]{:S(2)}, u32[]{:S(2)}) collective-permute-start(bf16[96,512]{1,0:T(8,128)(2,1)S(1)} %get-tuple-element.144), channel_id=1, source_target_pairs={{0,6},{1,7},{2,4},{3,5},{4,2},{5,3},{6,0},{7,1},{8,14},{9,15},{10,... | collective-permute-start | bytes 294920 | tf_op jit(solution)/shard_map/ppermute | solution.py:390
  62.3 1.7 %collective-permute-start.40 = (bf16[96,512]{1,0:T(8,128)(2,1)S(1)}, bf16[96,512]{1,0:T(8,128)(2,1)S(1)}, u32[]{:S(2)}, u32[]{:S(2)}) collective-permute-start(bf16[96,512]{1,0:T(8,128)(2,1)S(1)} %get-tuple-element.146), channel_id=1, source_target_pairs={{0,2},{1,3},{2,0},{3,1},{4,6},{5,7},{6,4},{7,5},{8,10},{9,11},{10,... | collective-permute-start | bytes 294920 | tf_op jit(solution)/shard_map/ppermute | solution.py:390
  64.0 1.0 %query_grad.1 = bf16[256,512]{1,0:T(8,128)(2,1)} custom-call(bf16[256,256]{1,0:T(8,128)(2,1)S(1)} %get-tuple-element.104.gate_back, bf16[256,256]{1,0:T(8,128)(2,1)S(1)} %get-tuple-element.105.up_back, bf16[256,512]{1,0:T(8,128)(2,1)S(1)} %get-tuple-element.106.f1t, bf16[256,512]{1,0:T(8,128)(2,1)S(1)} %get-tuple-element.107.f3t), custom_call_target="tpu_custom_call" | custom-call | flops 134217728 | bytes 786432 | tf_op jit(solution)/shard_map/query_grad/pallas_call | solution.py:372
  65.0 1.4 %token_grads.1 = (bf16[256,512]{1,0:T(8,128)(2,1)}, bf16[256,512]{1,0:T(8,128)(2,1)}) custom-call(f32[1,256]{1,0:T(1,128)S(1)} %bitcast.30, bf16[256,256]{1,0:T(8,128)(2,1)S(1)} %get-tuple-element.108.refs_1_, bf16[256,256]{1,0:T(8,128)(2,1)S(1)} %get-tuple-element.130.refs_2_, bf16[256,256]{1,0:T(8,128)(2,1)S(1)} %get-tuple-element.131.refs_3_, ...), custom_call_target="tpu_custom_call" | custom-call | flops 402653184 | bytes 2360320 | tf_op jit(solution)/shard_map/token_grads/pallas_call | solution.py:372
  66.4 0.7 %collective-permute-done.38.refs_4_ = bf16[96,512]{1,0:T(8,128)(2,1)S(1)} collective-permute-done((bf16[96,512]{1,0:T(8,128)(2,1)S(1)}, bf16[96,512]{1,0:T(8,128)(2,1)S(1)}, u32[]{:S(2)}, u32[]{:S(2)}) %collective-permute-start.38) | collective-permute-done | bytes 98336 | tf_op jit(solution)/shard_map/ppermute | solution.py:390
  67.1 4.5 %collective-permute-done.39.refs_5_ = bf16[96,512]{1,0:T(8,128)(2,1)S(1)} collective-permute-done((bf16[96,512]{1,0:T(8,128)(2,1)S(1)}, bf16[96,512]{1,0:T(8,128)(2,1)S(1)}, u32[]{:S(2)}, u32[]{:S(2)}) %collective-permute-start.39) | collective-permute-done | bytes 98336 | tf_op jit(solution)/shard_map/ppermute | solution.py:390
  71.7 0.7 owner_result.1
  (73 shorter events, 5.9 us)
Async XLA Ops:
  0.6 1.0 %copy-start.5 = (f32[256,1]{0,1:T(1,128)S(1)}, f32[256,1]{0,1:T(1,128)}, u32[]{:S(2)}) copy-start(f32[256,1]{0,1:T(1,128)} %param.13) | copy-start | bytes 3076
  0.6 2.8 %collective-permute-start.1 = (bf16[256,512]{1,0:T(8,128)(2,1)}, bf16[256,512]{1,0:T(8,128)(2,1)S(1)}, u32[]{:S(2)}, u32[]{:S(2)}) collective-permute-start(bf16[256,512]{1,0:T(8,128)(2,1)} %vo.3), channel_id=1, source_target_pairs={{0,1},{1,0},{2,3},{3,2},{4,5},{5,4},{6,7},{7,6},{8,9},{9,8},{10,11... | collective-permute-start | bytes 786440 | tf_op jit(solution)/shard_map/ppermute | solution.py:512
  1.2 2.3 %collective-permute-start = (bf16[256,512]{1,0:T(8,128)(2,1)}, bf16[256,512]{1,0:T(8,128)(2,1)S(1)}, u32[]{:S(2)}, u32[]{:S(2)}) collective-permute-start(bf16[256,512]{1,0:T(8,128)(2,1)} %refs_12_.3), channel_id=1, source_target_pairs={{0,1},{1,0},{2,3},{3,2},{4,5},{5,4},{6,7},{7,6},{8,9},{9,8},{10,11... | collective-permute-start | bytes 786440 | tf_op jit(solution)/shard_map/ppermute | solution.py:512
  1.2 16.2 %collective-permute-start.3 = (bf16[256,512]{1,0:T(8,128)(2,1)}, bf16[256,512]{1,0:T(8,128)(2,1)S(1)}, u32[]{:S(2)}, u32[]{:S(2)}) collective-permute-start(bf16[256,512]{1,0:T(8,128)(2,1)} %go.1), channel_id=1, source_target_pairs={{0,1},{1,0},{2,3},{3,2},{4,5},{5,4},{6,7},{7,6},{8,9},{9,8},{10,11... | collective-permute-start | bytes 786440 | tf_op jit(solution)/shard_map/ppermute | solution.py:512
  1.7 1.6 %copy-start.7 = (bf16[1,512,256]{2,1,0:T(8,128)(2,1)S(1)}, bf16[1,512,256]{2,1,0:T(8,128)(2,1)}, u32[]{:S(2)}) copy-start(bf16[1,512,256]{2,1,0:T(8,128)(2,1)} %param.16) | copy-start | bytes 786436
  1.7 1.8 %collective-permute-start.2 = (f32[1,256]{1,0:T(1,128)S(1)}, f32[1,256]{1,0:T(1,128)S(1)}, u32[]{:S(2)}, u32[]{:S(2)}) collective-permute-start(f32[1,256]{1,0:T(1,128)S(1)} %bitcast.27), channel_id=1, source_target_pairs={{0,1},{1,0},{2,3},{3,2},{4,5},{5,4},{6,7},{7,6},{8,9},{9,8},{10,11... | collective-permute-start | bytes 3080 | tf_op jit(solution)/shard_map/ppermute | solution.py:512
  1.8 25.6 %collective-permute-start.19 = (bf16[256,512]{1,0:T(8,128)(2,1)}, bf16[256,512]{1,0:T(8,128)(2,1)S(1)}, u32[]{:S(2)}, u32[]{:S(2)}) collective-permute-start(bf16[256,512]{1,0:T(8,128)(2,1)} %refs_10_.1), channel_id=1, source_target_pairs={{0,1},{1,0},{2,3},{3,2},{4,5},{5,4},{6,7},{7,6},{8,9},{9,8},{10,11... | collective-permute-start | bytes 786440 | tf_op jit(solution)/shard_map/ppermute | solution.py:512
  3.3 1.0 %copy-start.3 = (bf16[256,512]{1,0:T(8,128)(2,1)S(1)}, bf16[256,512]{1,0:T(8,128)(2,1)}, u32[]{:S(2)}) copy-start(bf16[256,512]{1,0:T(8,128)(2,1)} %vo.3) | copy-start | bytes 786436
  4.3 3.5 %copy-start.1 = (bf16[1,256,512]{2,1,0:T(8,128)(2,1)S(1)}, bf16[1,256,512]{2,1,0:T(8,128)(2,1)}, u32[]{:S(2)}) copy-start(bf16[1,256,512]{2,1,0:T(8,128)(2,1)} %param.17) | copy-start | bytes 786436
  5.1 5.4 %collective-permute-start.8 = (bf16[64,512]{1,0:T(8,128)(2,1)S(1)}, bf16[64,512]{1,0:T(8,128)(2,1)S(1)}, u32[]{:S(2)}, u32[]{:S(2)}) collective-permute-start(bf16[64,512]{1,0:T(8,128)(2,1)S(1)} %get-tuple-element.91), channel_id=1, source_target_pairs={{0,2},{1,3},{2,0},{3,1},{4,6},{5,7},{6,4},{7,5},{8,10},{9,11},{10,... | collective-permute-start | bytes 196616 | tf_op jit(solution)/shard_map/ppermute | solution.py:395
  8.4 4.9 %collective-permute-start.4 = (bf16[64,512]{1,0:T(8,128)(2,1)S(1)}, bf16[64,512]{1,0:T(8,128)(2,1)S(1)}, u32[]{:S(2)}, u32[]{:S(2)}) collective-permute-start(bf16[64,512]{1,0:T(8,128)(2,1)S(1)} %get-tuple-element.83), channel_id=1, source_target_pairs={{0,2},{1,3},{2,0},{3,1},{4,6},{5,7},{6,4},{7,5},{8,10},{9,11},{10,... | collective-permute-start | bytes 196616 | tf_op jit(solution)/shard_map/ppermute | solution.py:395
  8.6 7.5 %collective-permute-start.6 = (bf16[64,512]{1,0:T(8,128)(2,1)S(1)}, bf16[64,512]{1,0:T(8,128)(2,1)S(1)}, u32[]{:S(2)}, u32[]{:S(2)}) collective-permute-start(bf16[64,512]{1,0:T(8,128)(2,1)S(1)} %get-tuple-element.87), channel_id=1, source_target_pairs={{0,2},{1,3},{2,0},{3,1},{4,6},{5,7},{6,4},{7,5},{8,10},{9,11},{10,... | collective-permute-start | bytes 196616 | tf_op jit(solution)/shard_map/ppermute | solution.py:395
  10.6 8.0 %collective-permute-start.9 = (bf16[64,512]{1,0:T(8,128)(2,1)S(1)}, bf16[64,512]{1,0:T(8,128)(2,1)S(1)}, u32[]{:S(2)}, u32[]{:S(2)}) collective-permute-start(bf16[64,512]{1,0:T(8,128)(2,1)S(1)} %carry.8.refs_0_), channel_id=1, source_target_pairs={{0,4},{1,5},{2,6},{3,7},{4,0},{5,1},{6,2},{7,3},{8,12},{9,13},{10,... | collective-permute-start | bytes 196616 | tf_op jit(solution)/shard_map/ppermute | solution.py:395
  13.4 4.1 %copy-start.4 = (bf16[256,512]{1,0:T(8,128)(2,1)S(1)}, bf16[256,512]{1,0:T(8,128)(2,1)}, u32[]{:S(2)}) copy-start(bf16[256,512]{1,0:T(8,128)(2,1)} %go.1) | copy-start | bytes 786436
  13.4 8.5 %collective-permute-start.5 = (bf16[64,512]{1,0:T(8,128)(2,1)S(1)}, bf16[64,512]{1,0:T(8,128)(2,1)S(1)}, u32[]{:S(2)}, u32[]{:S(2)}) collective-permute-start(bf16[64,512]{1,0:T(8,128)(2,1)S(1)} %carry.6.refs_0_), channel_id=1, source_target_pairs={{0,4},{1,5},{2,6},{3,7},{4,0},{5,1},{6,2},{7,3},{8,12},{9,13},{10,... | collective-permute-start | bytes 196616 | tf_op jit(solution)/shard_map/ppermute | solution.py:395
  16.1 1.3 %copy-start.6 = (f32[512]{0:T(512)S(1)}, f32[512]{0:T(512)}, u32[]{:S(2)}) copy-start(f32[512]{0:T(512)} %param.14) | copy-start | bytes 6148
  16.1 6.7 %collective-permute-start.7 = (bf16[64,512]{1,0:T(8,128)(2,1)S(1)}, bf16[64,512]{1,0:T(8,128)(2,1)S(1)}, u32[]{:S(2)}, u32[]{:S(2)}) collective-permute-start(bf16[64,512]{1,0:T(8,128)(2,1)S(1)} %carry.7.refs_0_), channel_id=1, source_target_pairs={{0,4},{1,5},{2,6},{3,7},{4,0},{5,1},{6,2},{7,3},{8,12},{9,13},{10,... | collective-permute-start | bytes 196616 | tf_op jit(solution)/shard_map/ppermute | solution.py:395
  18.7 5.6 %collective-permute-start.16 = (bf16[64,512]{1,0:T(8,128)(2,1)S(1)}, bf16[64,512]{1,0:T(8,128)(2,1)S(1)}, u32[]{:S(2)}, u32[]{:S(2)}) collective-permute-start(bf16[64,512]{1,0:T(8,128)(2,1)S(1)} %get-tuple-element.96.refs_8_), channel_id=1, source_target_pairs={{0,2},{1,3},{2,0},{3,1},{4,6},{5,7},{6,4},{7,5},{8,10},{9,11},{10,... | collective-permute-start | bytes 196616 | tf_op jit(solution)/shard_map/ppermute | solution.py:395
  21.9 7.3 %copy-start.2 = (bf16[256,512]{1,0:T(8,128)(2,1)S(1)}, bf16[256,512]{1,0:T(8,128)(2,1)}, u32[]{:S(2)}) copy-start(bf16[256,512]{1,0:T(8,128)(2,1)} %refs_10_.1) | copy-start | bytes 786436
  22.0 4.7 %collective-permute-start.10 = (bf16[64,512]{1,0:T(8,128)(2,1)S(1)}, bf16[64,512]{1,0:T(8,128)(2,1)S(1)}, u32[]{:S(2)}, u32[]{:S(2)}) collective-permute-start(bf16[64,512]{1,0:T(8,128)(2,1)S(1)} %get-tuple-element.94.refs_0_), channel_id=1, source_target_pairs={{0,2},{1,3},{2,0},{3,1},{4,6},{5,7},{6,4},{7,5},{8,10},{9,11},{10,... | collective-permute-start | bytes 196616 | tf_op jit(solution)/shard_map/ppermute | solution.py:395
  23.0 4.4 %collective-permute-start.13 = (bf16[64,512]{1,0:T(8,128)(2,1)S(1)}, bf16[64,512]{1,0:T(8,128)(2,1)S(1)}, u32[]{:S(2)}, u32[]{:S(2)}) collective-permute-start(bf16[64,512]{1,0:T(8,128)(2,1)S(1)} %get-tuple-element.95.refs_4_), channel_id=1, source_target_pairs={{0,2},{1,3},{2,0},{3,1},{4,6},{5,7},{6,4},{7,5},{8,10},{9,11},{10,... | collective-permute-start | bytes 196616 | tf_op jit(solution)/shard_map/ppermute | solution.py:395
  24.3 3.6 %collective-permute-start.18 = (bf16[64,512]{1,0:T(8,128)(2,1)S(1)}, bf16[64,512]{1,0:T(8,128)(2,1)S(1)}, u32[]{:S(2)}, u32[]{:S(2)}) collective-permute-start(bf16[64,512]{1,0:T(8,128)(2,1)S(1)} %collective-permute-done.16.refs_9_), channel_id=1, source_target_pairs={{0,1},{1,0},{2,3},{3,2},{4,5},{5,4},{6,7},{7,6},{8,9},{9,8},{10,11... | collective-permute-start | bytes 196616 | tf_op jit(solution)/shard_map/ppermute | solution.py:406
  26.7 2.0 %collective-permute-start.11 = (bf16[64,512]{1,0:T(8,128)(2,1)S(1)}, bf16[64,512]{1,0:T(8,128)(2,1)S(1)}, u32[]{:S(2)}, u32[]{:S(2)}) collective-permute-start(bf16[64,512]{1,0:T(8,128)(2,1)S(1)} %get-tuple-element.94.refs_0_), channel_id=1, source_target_pairs={{0,1},{1,0},{2,3},{3,2},{4,5},{5,4},{6,7},{7,6},{8,9},{9,8},{10,11... | collective-permute-start | bytes 196616 | tf_op jit(solution)/shard_map/ppermute | solution.py:406
  26.7 2.0 %collective-permute-start.14 = (bf16[64,512]{1,0:T(8,128)(2,1)S(1)}, bf16[64,512]{1,0:T(8,128)(2,1)S(1)}, u32[]{:S(2)}, u32[]{:S(2)}) collective-permute-start(bf16[64,512]{1,0:T(8,128)(2,1)S(1)} %get-tuple-element.95.refs_4_), channel_id=1, source_target_pairs={{0,1},{1,0},{2,3},{3,2},{4,5},{5,4},{6,7},{7,6},{8,9},{9,8},{10,11... | collective-permute-start | bytes 196616 | tf_op jit(solution)/shard_map/ppermute | solution.py:406
  27.4 1.3 %collective-permute-start.15 = (bf16[64,512]{1,0:T(8,128)(2,1)S(1)}, bf16[64,512]{1,0:T(8,128)(2,1)S(1)}, u32[]{:S(2)}, u32[]{:S(2)}) collective-permute-start(bf16[64,512]{1,0:T(8,128)(2,1)S(1)} %collective-permute-done.13.refs_5_), channel_id=1, source_target_pairs={{0,1},{1,0},{2,3},{3,2},{4,5},{5,4},{6,7},{7,6},{8,9},{9,8},{10,11... | collective-permute-start | bytes 196616 | tf_op jit(solution)/shard_map/ppermute | solution.py:406
  27.4 1.4 %collective-permute-start.17 = (bf16[64,512]{1,0:T(8,128)(2,1)S(1)}, bf16[64,512]{1,0:T(8,128)(2,1)S(1)}, u32[]{:S(2)}, u32[]{:S(2)}) collective-permute-start(bf16[64,512]{1,0:T(8,128)(2,1)S(1)} %get-tuple-element.96.refs_8_), channel_id=1, source_target_pairs={{0,1},{1,0},{2,3},{3,2},{4,5},{5,4},{6,7},{7,6},{8,9},{9,8},{10,11... | collective-permute-start | bytes 196616 | tf_op jit(solution)/shard_map/ppermute | solution.py:406
  27.9 1.3 %collective-permute-start.12 = (bf16[64,512]{1,0:T(8,128)(2,1)S(1)}, bf16[64,512]{1,0:T(8,128)(2,1)S(1)}, u32[]{:S(2)}, u32[]{:S(2)}) collective-permute-start(bf16[64,512]{1,0:T(8,128)(2,1)S(1)} %collective-permute-done.10.refs_1_), channel_id=1, source_target_pairs={{0,1},{1,0},{2,3},{3,2},{4,5},{5,4},{6,7},{7,6},{8,9},{9,8},{10,11... | collective-permute-start | bytes 196616 | tf_op jit(solution)/shard_map/ppermute | solution.py:406
  30.0 4.6 %collective-permute-start.22 = (f32[2,512]{1,0:T(2,128)S(1)}, f32[2,512]{1,0:T(2,128)S(1)}, u32[]{:S(2)}, u32[]{:S(2)}) collective-permute-start(f32[2,512]{1,0:T(2,128)S(1)} %get-tuple-element.98.refs_0_), channel_id=1, source_target_pairs={{0,24},{8,16},{16,8},{24,0},{1,25},{9,17},{17,9},{25,1},{2,26},{10... | collective-permute-start | bytes 12296 | tf_op jit(solution)/shard_map/ppermute | solution.py:413
  32.8 3.6 %collective-permute-start.21 = (f32[2,512]{1,0:T(2,128)S(1)}, f32[2,512]{1,0:T(2,128)S(1)}, u32[]{:S(2)}, u32[]{:S(2)}) collective-permute-start(f32[2,512]{1,0:T(2,128)S(1)} %get-tuple-element.98.refs_0_), channel_id=1, source_target_pairs={{0,16},{8,24},{16,0},{24,8},{1,17},{9,25},{17,1},{25,9},{2,18},{10... | collective-permute-start | bytes 12296 | tf_op jit(solution)/shard_map/ppermute | solution.py:413
  33.3 3.6 %collective-permute-start.20 = (f32[2,512]{1,0:T(2,128)S(1)}, f32[2,512]{1,0:T(2,128)S(1)}, u32[]{:S(2)}, u32[]{:S(2)}) collective-permute-start(f32[2,512]{1,0:T(2,128)S(1)} %get-tuple-element.98.refs_0_), channel_id=1, source_target_pairs={{0,8},{8,0},{16,24},{24,16},{1,9},{9,1},{17,25},{25,17},{2,10},{10... | collective-permute-start | bytes 12296 | tf_op jit(solution)/shard_map/ppermute | solution.py:413
  37.7 4.3 %collective-permute-start.25 = (bf16[64,512]{1,0:T(8,128)(2,1)S(1)}, bf16[64,512]{1,0:T(8,128)(2,1)S(1)}, u32[]{:S(2)}, u32[]{:S(2)}) collective-permute-start(bf16[64,512]{1,0:T(8,128)(2,1)S(1)} %get-tuple-element.115), channel_id=1, source_target_pairs={{0,2},{1,3},{2,0},{3,1},{4,6},{5,7},{6,4},{7,5},{8,10},{9,11},{10,... | collective-permute-start | bytes 196616 | tf_op jit(solution)/shard_map/ppermute | solution.py:395
  38.6 6.6 %collective-permute-start.23 = (bf16[64,512]{1,0:T(8,128)(2,1)S(1)}, bf16[64,512]{1,0:T(8,128)(2,1)S(1)}, u32[]{:S(2)}, u32[]{:S(2)}) collective-permute-start(bf16[64,512]{1,0:T(8,128)(2,1)S(1)} %get-tuple-element.111), channel_id=1, source_target_pairs={{0,2},{1,3},{2,0},{3,1},{4,6},{5,7},{6,4},{7,5},{8,10},{9,11},{10,... | collective-permute-start | bytes 196616 | tf_op jit(solution)/shard_map/ppermute | solution.py:395
  39.8 6.1 %collective-permute-start.27 = (bf16[64,512]{1,0:T(8,128)(2,1)S(1)}, bf16[64,512]{1,0:T(8,128)(2,1)S(1)}, u32[]{:S(2)}, u32[]{:S(2)}) collective-permute-start(bf16[64,512]{1,0:T(8,128)(2,1)S(1)} %get-tuple-element.119), channel_id=1, source_target_pairs={{0,2},{1,3},{2,0},{3,1},{4,6},{5,7},{6,4},{7,5},{8,10},{9,11},{10,... | collective-permute-start | bytes 196616 | tf_op jit(solution)/shard_map/ppermute | solution.py:395
  42.1 7.8 %collective-permute-start.26 = (bf16[64,512]{1,0:T(8,128)(2,1)S(1)}, bf16[64,512]{1,0:T(8,128)(2,1)S(1)}, u32[]{:S(2)}, u32[]{:S(2)}) collective-permute-start(bf16[64,512]{1,0:T(8,128)(2,1)S(1)} %carry.10.refs_0_), channel_id=1, source_target_pairs={{0,4},{1,5},{2,6},{3,7},{4,0},{5,1},{6,2},{7,3},{8,12},{9,13},{10,... | collective-permute-start | bytes 196616 | tf_op jit(solution)/shard_map/ppermute | solution.py:395
  45.3 5.7 %collective-permute-start.24 = (bf16[64,512]{1,0:T(8,128)(2,1)S(1)}, bf16[64,512]{1,0:T(8,128)(2,1)S(1)}, u32[]{:S(2)}, u32[]{:S(2)}) collective-permute-start(bf16[64,512]{1,0:T(8,128)(2,1)S(1)} %carry.9.refs_0_), channel_id=1, source_target_pairs={{0,4},{1,5},{2,6},{3,7},{4,0},{5,1},{6,2},{7,3},{8,12},{9,13},{10,... | collective-permute-start | bytes 196616 | tf_op jit(solution)/shard_map/ppermute | solution.py:395
  46.0 6.3 %collective-permute-start.28 = (bf16[64,512]{1,0:T(8,128)(2,1)S(1)}, bf16[64,512]{1,0:T(8,128)(2,1)S(1)}, u32[]{:S(2)}, u32[]{:S(2)}) collective-permute-start(bf16[64,512]{1,0:T(8,128)(2,1)S(1)} %carry.11.refs_0_), channel_id=1, source_target_pairs={{0,4},{1,5},{2,6},{3,7},{4,0},{5,1},{6,2},{7,3},{8,12},{9,13},{10,... | collective-permute-start | bytes 196616 | tf_op jit(solution)/shard_map/ppermute | solution.py:395
  50.0 4.3 %collective-permute-start.32 = (bf16[64,512]{1,0:T(8,128)(2,1)S(1)}, bf16[64,512]{1,0:T(8,128)(2,1)S(1)}, u32[]{:S(2)}, u32[]{:S(2)}) collective-permute-start(bf16[64,512]{1,0:T(8,128)(2,1)S(1)} %get-tuple-element.123.refs_4_), channel_id=1, source_target_pairs={{0,2},{1,3},{2,0},{3,1},{4,6},{5,7},{6,4},{7,5},{8,10},{9,11},{10,... | collective-permute-start | bytes 196616 | tf_op jit(solution)/shard_map/ppermute | solution.py:395
  51.1 4.3 %collective-permute-start.29 = (bf16[64,512]{1,0:T(8,128)(2,1)S(1)}, bf16[64,512]{1,0:T(8,128)(2,1)S(1)}, u32[]{:S(2)}, u32[]{:S(2)}) collective-permute-start(bf16[64,512]{1,0:T(8,128)(2,1)S(1)} %get-tuple-element.122.refs_0_), channel_id=1, source_target_pairs={{0,2},{1,3},{2,0},{3,1},{4,6},{5,7},{6,4},{7,5},{8,10},{9,11},{10,... | collective-permute-start | bytes 196616 | tf_op jit(solution)/shard_map/ppermute | solution.py:395
  52.5 4.3 %collective-permute-start.35 = (bf16[64,512]{1,0:T(8,128)(2,1)S(1)}, bf16[64,512]{1,0:T(8,128)(2,1)S(1)}, u32[]{:S(2)}, u32[]{:S(2)}) collective-permute-start(bf16[64,512]{1,0:T(8,128)(2,1)S(1)} %get-tuple-element.124.refs_8_), channel_id=1, source_target_pairs={{0,2},{1,3},{2,0},{3,1},{4,6},{5,7},{6,4},{7,5},{8,10},{9,11},{10,... | collective-permute-start | bytes 196616 | tf_op jit(solution)/shard_map/ppermute | solution.py:395
  54.3 2.5 %collective-permute-start.34 = (bf16[64,512]{1,0:T(8,128)(2,1)S(1)}, bf16[64,512]{1,0:T(8,128)(2,1)S(1)}, u32[]{:S(2)}, u32[]{:S(2)}) collective-permute-start(bf16[64,512]{1,0:T(8,128)(2,1)S(1)} %collective-permute-done.32.refs_5_), channel_id=1, source_target_pairs={{0,1},{1,0},{2,3},{3,2},{4,5},{5,4},{6,7},{7,6},{8,9},{9,8},{10,11... | collective-permute-start | bytes 196616 | tf_op jit(solution)/shard_map/ppermute | solution.py:406
  55.4 1.9 %collective-permute-start.30 = (bf16[64,512]{1,0:T(8,128)(2,1)S(1)}, bf16[64,512]{1,0:T(8,128)(2,1)S(1)}, u32[]{:S(2)}, u32[]{:S(2)}) collective-permute-start(bf16[64,512]{1,0:T(8,128)(2,1)S(1)} %get-tuple-element.122.refs_0_), channel_id=1, source_target_pairs={{0,1},{1,0},{2,3},{3,2},{4,5},{5,4},{6,7},{7,6},{8,9},{9,8},{10,11... | collective-permute-start | bytes 196616 | tf_op jit(solution)/shard_map/ppermute | solution.py:406
  55.4 1.9 %collective-permute-start.33 = (bf16[64,512]{1,0:T(8,128)(2,1)S(1)}, bf16[64,512]{1,0:T(8,128)(2,1)S(1)}, u32[]{:S(2)}, u32[]{:S(2)}) collective-permute-start(bf16[64,512]{1,0:T(8,128)(2,1)S(1)} %get-tuple-element.123.refs_4_), channel_id=1, source_target_pairs={{0,1},{1,0},{2,3},{3,2},{4,5},{5,4},{6,7},{7,6},{8,9},{9,8},{10,11... | collective-permute-start | bytes 196616 | tf_op jit(solution)/shard_map/ppermute | solution.py:406
  55.9 1.4 %collective-permute-start.36 = (bf16[64,512]{1,0:T(8,128)(2,1)S(1)}, bf16[64,512]{1,0:T(8,128)(2,1)S(1)}, u32[]{:S(2)}, u32[]{:S(2)}) collective-permute-start(bf16[64,512]{1,0:T(8,128)(2,1)S(1)} %get-tuple-element.124.refs_8_), channel_id=1, source_target_pairs={{0,1},{1,0},{2,3},{3,2},{4,5},{5,4},{6,7},{7,6},{8,9},{9,8},{10,11... | collective-permute-start | bytes 196616 | tf_op jit(solution)/shard_map/ppermute | solution.py:406
  56.8 1.3 %collective-permute-start.31 = (bf16[64,512]{1,0:T(8,128)(2,1)S(1)}, bf16[64,512]{1,0:T(8,128)(2,1)S(1)}, u32[]{:S(2)}, u32[]{:S(2)}) collective-permute-start(bf16[64,512]{1,0:T(8,128)(2,1)S(1)} %collective-permute-done.29.refs_1_), channel_id=1, source_target_pairs={{0,1},{1,0},{2,3},{3,2},{4,5},{5,4},{6,7},{7,6},{8,9},{9,8},{10,11... | collective-permute-start | bytes 196616 | tf_op jit(solution)/shard_map/ppermute | solution.py:406
  56.8 1.4 %collective-permute-start.37 = (bf16[64,512]{1,0:T(8,128)(2,1)S(1)}, bf16[64,512]{1,0:T(8,128)(2,1)S(1)}, u32[]{:S(2)}, u32[]{:S(2)}) collective-permute-start(bf16[64,512]{1,0:T(8,128)(2,1)S(1)} %collective-permute-done.35.refs_9_), channel_id=1, source_target_pairs={{0,1},{1,0},{2,3},{3,2},{4,5},{5,4},{6,7},{7,6},{8,9},{9,8},{10,11... | collective-permute-start | bytes 196616 | tf_op jit(solution)/shard_map/ppermute | solution.py:406
  59.6 7.6 %collective-permute-start.38 = (bf16[96,512]{1,0:T(8,128)(2,1)S(1)}, bf16[96,512]{1,0:T(8,128)(2,1)S(1)}, u32[]{:S(2)}, u32[]{:S(2)}) collective-permute-start(bf16[96,512]{1,0:T(8,128)(2,1)S(1)} %get-tuple-element.144), channel_id=1, source_target_pairs={{0,6},{1,7},{2,4},{3,5},{4,2},{5,3},{6,0},{7,1},{8,14},{9,15},{10,... | collective-permute-start | bytes 294920 | tf_op jit(solution)/shard_map/ppermute | solution.py:390
  62.0 9.6 %collective-permute-start.39 = (bf16[96,512]{1,0:T(8,128)(2,1)S(1)}, bf16[96,512]{1,0:T(8,128)(2,1)S(1)}, u32[]{:S(2)}, u32[]{:S(2)}) collective-permute-start(bf16[96,512]{1,0:T(8,128)(2,1)S(1)} %get-tuple-element.145), channel_id=1, source_target_pairs={{0,4},{1,5},{2,6},{3,7},{4,0},{5,1},{6,2},{7,3},{8,12},{9,13},{10,... | collective-permute-start | bytes 294920 | tf_op jit(solution)/shard_map/ppermute | solution.py:390
  62.3 9.3 %collective-permute-start.40 = (bf16[96,512]{1,0:T(8,128)(2,1)S(1)}, bf16[96,512]{1,0:T(8,128)(2,1)S(1)}, u32[]{:S(2)}, u32[]{:S(2)}) collective-permute-start(bf16[96,512]{1,0:T(8,128)(2,1)S(1)} %get-tuple-element.146), channel_id=1, source_target_pairs={{0,2},{1,3},{2,0},{3,1},{4,6},{5,7},{6,4},{7,5},{8,10},{9,11},{10,... | collective-permute-start | bytes 294920 | tf_op jit(solution)/shard_map/ppermute | solution.py:390
  (1 other events, 1.0 us)

commit v12 on v10

--- a/solution.py
+++ b/solution.py
@@ -97,12 +97,15 @@
     return gate_back, up_back, out_back
 
 
-def second_adjoint(c1t, c3t, c2t, keys, push, up_slope, silu, back_slope, back_curve):
-    gate_bar, up_bar, mixed_bar = nt(c1t, keys), nt(c3t, keys), tn(c2t, push)
+def second_by_gate_and_up(c1t, c3t, keys, up_slope, silu, back_slope, back_curve):
+    gate_bar, up_bar = nt(c1t, keys), nt(c3t, keys)
     down_back_bar = (gate_bar * up_slope + up_bar * silu).astype(BF16)
-    up_pre_bar = (gate_bar * back_slope + mixed_bar * silu).astype(BF16)
-    gate_pre_bar = (up_bar * back_slope + mixed_bar * up_slope + gate_bar * back_curve).astype(BF16)
-    return down_back_bar, up_pre_bar, gate_pre_bar
+    return down_back_bar, gate_bar * back_slope, up_bar * back_slope + gate_bar * back_curve
+
+
+def second_by_down(c2t, push, up_slope, silu, up_part, gate_part):
+    mixed_bar = tn(c2t, push)
+    return (up_part + mixed_bar * silu).astype(BF16), (gate_part + mixed_bar * up_slope).astype(BF16)
 
 
 def folds_of(rows, folds):
@@ -166,53 +169,45 @@
             ]
 
 
-def place_halves(chips, folds, halves, matrices):
+def place_halves(chips, folds, halves, ref):
     tok = lax.axis_index("tok")
     parity, core = tok // CORES % 2, tok % CORES
-    for k, ref in enumerate(matrices):
-        whose = ((parity, core), (1 - parity, core), (parity, 1 - core), (1 - parity, 1 - core))
-        for half, (p, c) in zip(halves[4 * k : 4 * k + 4], whose):
-            place_half(ref, half, p, c, chips, folds if k == 2 else 1)
-
-
-def products_of_core(chips, folds, order, gate_ref, up_ref, down_ref, tokens, hidden):
+    whose = ((parity, core), (1 - parity, core), (parity, 1 - core), (1 - parity, 1 - core))
+    for half, (p, c) in zip(halves, whose):
+        place_half(ref, half, p, c, chips, folds)
+
+
+def rows_of_core(ref, order, chips):
     core = lax.axis_index("tok") % CORES
-
-    def picked(ref):
-        rows = ref.shape[0] // (chips * CORES)
-        blocks = [
-            ref[pl.ds(pl.multiple_of((chip * CORES + core) * rows, rows), rows), :] for chip in order
-        ]
-        return jnp.concatenate(blocks, axis=0)
-
-    gate, up = nn(picked(gate_ref), tokens), nn(picked(up_ref), tokens)
-    down = nt(picked(down_ref), hidden)
-    g, d = gate.shape[0] // chips, down.shape[0] // chips
-    pieces = []
-    for k in range(chips):
-        parts = [down[k * d + i * g : k * d + (i + 1) * g] for i in range(folds)]
-        pieces.append(
-            (gate[k * g : (k + 1) * g], up[k * g : (k + 1) * g], jnp.concatenate(parts, axis=1))
-        )
-    return pieces
-
-
-def send_pieces(chips, folds, operands, outs):
+    rows = ref.shape[0] // (chips * CORES)
+    blocks = [
+        ref[pl.ds(pl.multiple_of((chip * CORES + core) * rows, rows), rows), :] for chip in order
+    ]
+    return jnp.concatenate(blocks, axis=0)
+
+
+def fold(rows, chips, folds):
+    height = rows.shape[0] // (chips * folds)
+    parts = [rows[i * height : (i + 1) * height] for i in range(chips * folds)]
+    wide = [jnp.concatenate(parts[k : k + folds], axis=1) for k in range(0, len(parts), folds)]
+    return jnp.concatenate(wide, axis=0)
+
+
+def pieces_order(chips):
     chip = lax.axis_index("tok") // CORES
-    order = [partner(chip, step, chips) for step in range(chips)]
-    for out, parts in zip(outs, products_of_core(chips, folds, order, *operands)):
-        out[...] = jnp.concatenate(parts, axis=0).astype(out.dtype)
+    return [partner(chip, step, chips) for step in range(chips)]
 
 
 def send_halves(chips, folds, operands, outs):
+    gate_ref, up_ref, down_ref, tokens, hidden = operands
     parity = lax.axis_index("tok") // CORES % 2
-    half = chips // 2
-    order = [2 * k + p for p in (parity, 1 - parity) for k in range(half)]
-    pieces = products_of_core(chips, folds, order, *operands)
-    for k in range(3):
-        kept, given = ([p[k] for p in part] for part in (pieces[:half], pieces[half:]))
-        outs[k][...] = jnp.concatenate(kept, axis=0)
-        outs[3 + k][...] = jnp.concatenate(given, axis=0).astype(BF16)
+    order = [2 * k + p for p in (parity, 1 - parity) for k in range(chips // 2)]
+    sums = [nn(rows_of_core(ref, order, chips), tokens) for ref in (gate_ref, up_ref)]
+    sums.append(fold(nt(rows_of_core(down_ref, order, chips), hidden), chips, folds))
+    half = outs[0].shape[0]
+    for k, total in enumerate(sums):
+        outs[k][...] = total[:half]
+        outs[3 + k][...] = total[half:].astype(BF16)
 
 
 def update_kernel(chips, folds, ko, kx, vo, vx, ro, rx, w1t, w3t, w2, *rest):
@@ -291,7 +286,9 @@
 def apply_kernel(chips, folds, *refs):
     halves, refs = refs[:12], refs[12:]
     qo, qx, weighted, f1t, f3t, f2t, output, mixed, up_slope, silu, sums = refs
-    place_halves(chips, folds, halves, (f1t, f3t, f2t))
+    place_halves(chips, 1, halves[:4], f1t)
+    place_halves(chips, 1, halves[4:8], f3t)
+    place_halves(chips, folds, halves[8:], f2t)
     output[...], mixed[...], up_slope[...], silu[...], sums[...] = apply_forward(
         f1t[...], f3t[...], f2t[...], both(qo, qx), weighted[...]
     )
@@ -317,20 +314,37 @@
     out[...] = (tn(gate_back[...], f1t[...]) + tn(up_back[...], f3t[...])).astype(BF16)
 
 
-def second_kernel(chips, folds, *refs):
-    halves, refs = refs[:12], refs[12:]
+def second_first_kernel(chips, folds, *refs):
+    halves, refs = refs[:8], refs[8:]
     ko, kx, push, up_slope, silu, back_slope, back_curve = refs[:7]
-    c1t, c3t, c2t, dbb_ref, upb_ref, gpb_ref = refs[7:13]
-    outs, (gate, up) = refs[13 : 13 + chips], refs[13 + chips :]
-    place_halves(chips, folds, halves, (c1t, c3t, c2t))
-    keys = both(ko, kx)
-    dbb, up[...], gate[...] = second_adjoint(
-        c1t[...], c3t[...], c2t[...], keys, push[...],
+    c1t, c3t, dbb_ref, down, up_part, gate_part = refs[7:]
+    place_halves(chips, 1, halves[:4], c1t)
+    place_halves(chips, 1, halves[4:], c3t)
+    dbb, up_part[...], gate_part[...] = second_by_gate_and_up(
+        c1t[...], c3t[...], both(ko, kx),
         up_slope[...], silu[...], back_slope[...], back_curve[...],
     )
-    send_pieces(chips, folds, (gate, up, push, keys, dbb), outs)
-    own = dbb_ref.shape[1]
-    dbb_ref[...], upb_ref[...], gpb_ref[...] = dbb[:, :own], up[:, :own], gate[:, :own]
+    down[...] = fold(nt(rows_of_core(push, pieces_order(chips), chips), dbb), chips, folds)
+    dbb_ref[...] = dbb[:, : dbb_ref.shape[1]]
+
+
+def second_last_kernel(chips, folds, *refs):
+    halves, refs = refs[:4], refs[4:]
+    ko, kx, push, up_slope, silu, up_part, gate_part, down = refs[:8]
+    c2t, upb_ref, gpb_ref = refs[8:11]
+    outs, (gate, up) = refs[11 : 11 + chips], refs[11 + chips :]
+    place_halves(chips, folds, halves, c2t)
+    up[...], gate[...] = second_by_down(
+        c2t[...], push[...], up_slope[...], silu[...], up_part[...], gate_part[...]
+    )
+    keys, order = both(ko, kx), pieces_order(chips)
+    sums = [nn(rows_of_core(ref, order, chips), keys) for ref in (gate, up)] + [down[...]]
+    g = sums[0].shape[0] // chips
+    for k, out in enumerate(outs):
+        parts = [x[k * g : (k + 1) * g] for x in sums]
+        out[...] = jnp.concatenate(parts, axis=0).astype(out.dtype)
+    own = upb_ref.shape[1]
+    upb_ref[...], gpb_ref[...] = up[:, :own], gate[:, :own]
 
 
 def token_grads(rates, mixed, dbb, upb, gpb, gate_back, up_back, c1t, c3t, c2t, w1t, w3t, w2):
@@ -559,16 +573,23 @@
         )
         owned.append(rows_owned)
         cotangent.append(rows)
-    c1t, c3t, c2t, dbb, upb, gpb, *pieces = call(
-        functools.partial(second_kernel, chips, folds),
-        matrices + [own_hidden] * 3 + [((3 * g, dh), F32)] + [((3 * g, dh), BF16)] * (chips - 1),
+    arrived = from_owners(cotangent, chips)
+    c1t, c3t, dbb, down_sums, up_part, gate_part = call(
+        functools.partial(second_first_kernel, chips, folds),
+        matrices[:2] + [own_hidden, ((g * chips, dh), F32), hidden, hidden],
+        (*arrived[:8], key_input, key_other, push, up_slope, silu, back_slope, back_curve),
+        name="second_first",
+        flops=3 * product,
+    )
+    c2t, upb, gpb, *pieces = call(
+        functools.partial(second_last_kernel, chips, folds),
+        matrices[2:] + [own_hidden] * 2 + [((3 * g, dh), F32)] + [((3 * g, dh), BF16)] * (chips - 1),
         (
-            *from_owners(cotangent, chips),
-            key_input, key_other, push, up_slope, silu, back_slope, back_curve,
+            *arrived[8:], key_input, key_other, push, up_slope, silu, up_part, gate_part, down_sums,
         ),
         operands[:2],
-        "second_adjoint",
-        6 * product,
+        "second_last",
+        3 * product,
     )
     value_grad, key_grad = call(
         token_kernel,
@@ -626,9 +647,8 @@
     cotangent, owned = packed_owner_backward(prior, moved, fast_grad, fh)
     blocks = gather_blocks(jnp.tile(cotangent, (chips, 1)), count)
     c1t, c3t, c2t = whole_matrices(*blocks, tok, count, fh)
-    dbb, upb, gpb = second_adjoint(
-        c1t, c3t, c2t, keys, push, up_slope, silu, back_slope, back_curve
-    )
+    dbb, *parts = second_by_gate_and_up(c1t, c3t, keys, up_slope, silu, back_slope, back_curve)
+    upb, gpb = second_by_down(c2t, push, up_slope, silu, *parts)
     bars = nn(gpb, keys), nn(upb, keys), nt(push, dbb)
     piece, sent = sliced_pieces(*bars, tok, count)
     value_grad, key_grad = token_grads(

time: 72.6 us -> 72 us (level)
  waiting for transfers between devices: 21.8 us -> 21 us
    ppermute x12, waiting for transfers between devices: 2.09 us -> 1.29 us  [from_owners(): cross = lambda x: lax.ppermute(x, 'tok', core_perm(chips * CORES))]
    pallas_call x20 -> x21, Pallas kernels: 9.33 us -> 9.49 us  [call(): pl.pallas_call(kernel, out_shape=[jax.ShapeDtypeStruct(s, t) for s, t in...]
  transfers between devices with their start and end apart: 41 -> 41, of which waited for: 23 -> 22; matrix products, arithmetic and copies ran while one was open for 2% -> 2% of each run, Pallas kernels for 8% -> 9%
where the time goes in v12:
time: 72 us; the launch traced here: 71.8 us
  starting transfers between devices  38.3 us (53%)
  waiting for transfers between devices  21 us (29%)
  Pallas kernels  9.49 us (13%)
  local copies, waits for them, and re-layouts  2.12 us (3%)
  between operations  0.88 us (1%)
    ppermute x18, starting transfers between devices, to_chip(): return lax.ppermute(x, 'tok', chip_perm(chips * CORES, step))  27 us
    ppermute x18, waiting for transfers between devices, to_chip(): return lax.ppermute(x, 'tok', chip_perm(chips * CORES, step))  11.6 us
    pallas_call x21, Pallas kernels, call(): pl.pallas_call(kernel, out_shape=[jax.ShapeDtypeStruct(s, t) for s, t in...  9.49 us
    ppermute x3, waiting for transfers between devices, exchange(): lax.ppermute(pieces[s], 'tok', chip_perm(count, s))  4.85 us
    ppermute x3, starting transfers between devices, exchange(): lax.ppermute(pieces[s], 'tok', chip_perm(count, s))  4.45 us
    ppermute x3, starting transfers between devices, head_parts(): lax.ppermute(part, 'head', [(h, partner(h, step, heads)) for h in range(h...  3.55 us
    ppermute x3, waiting for transfers between devices, head_parts(): lax.ppermute(part, 'head', [(h, partner(h, step, heads)) for h in range(h...  3.26 us
    unnamed x18, local copies, waits for them, and re-layouts  2.12 us
  transfers between devices with their start and end apart: 41, of which 22 were waited for; matrix products, arithmetic and copies ran while one was open for 2% of the time, Pallas kernels for 9%

profile of v12, /device:TPU:0, one launch (start us, length us, event | category | flops | bytes accessed | tf_op | source)
XLA Modules:
  0.0 71.8 jit_solution(8262754296941063276)
XLA Ops:
  0.6 0.5 collective-permute-start.1
  1.8 1.1 %copy.15 = bf16[1,512,256]{1,2,0:T(8,128)(2,1)S(1)} copy(bf16[1,512,256]{2,1,0:T(8,128)(2,1)} %param.15) | data formatting | bytes 524288 | tf_op args[6]
  3.1 0.7 %copy-done = bf16[256,512]{1,0:T(8,128)(2,1)S(1)} copy-done((bf16[256,512]{1,0:T(8,128)(2,1)S(1)}, bf16[256,512]{1,0:T(8,128)(2,1)}, u32[]{:S(2)}) %copy-start) | copy-done | bytes 262168
  4.0 1.2 %update.1 = (f32[64,512]{1,0:T(8,128)S(1)}, f32[64,512]{1,0:T(8,128)S(1)}, f32[64,512]{1,0:T(8,128)S(1)}, bf16[64,512]{1,0:T(8,128)(2,1)S(1)}, bf16[64,512]{1,0:T(8,128)(2,1)S(1)}, /*index=5*/bf16[64,512]{1,0:T(8,128)(2,1)S(1)}) custom-call(bf16[256,512]{1,0:T(8,128)(2,1)S(1)} %copy-done, bf16[256,512]{1,0:T(8,128)(2,1)S(1)} %collective-permute-done.kx.refs_9_.refs_5_, ...), custom_call_target="tpu_custom_call" | custom-call | flops 805306368 | bytes 1837056 | tf_op jit(solution)/shard_map/update/pallas_call | solution.py:363
  5.1 3.1 %collective-permute-start.8 = (bf16[64,512]{1,0:T(8,128)(2,1)S(1)}, bf16[64,512]{1,0:T(8,128)(2,1)S(1)}, u32[]{:S(2)}, u32[]{:S(2)}) collective-permute-start(bf16[64,512]{1,0:T(8,128)(2,1)S(1)} %get-tuple-element.88), channel_id=1, source_target_pairs={{0,2},{1,3},{2,0},{3,1},{4,6},{5,7},{6,4},{7,5},{8,10},{9,11},{10,... | collective-permute-start | bytes 196616 | tf_op jit(solution)/shard_map/ppermute | solution.py:386
  8.4 1.9 %collective-permute-start.6 = (bf16[64,512]{1,0:T(8,128)(2,1)S(1)}, bf16[64,512]{1,0:T(8,128)(2,1)S(1)}, u32[]{:S(2)}, u32[]{:S(2)}) collective-permute-start(bf16[64,512]{1,0:T(8,128)(2,1)S(1)} %get-tuple-element.84), channel_id=1, source_target_pairs={{0,2},{1,3},{2,0},{3,1},{4,6},{5,7},{6,4},{7,5},{8,10},{9,11},{10,... | collective-permute-start | bytes 196616 | tf_op jit(solution)/shard_map/ppermute | solution.py:386
  10.6 3.0 %collective-permute-start.9 = (bf16[64,512]{1,0:T(8,128)(2,1)S(1)}, bf16[64,512]{1,0:T(8,128)(2,1)S(1)}, u32[]{:S(2)}, u32[]{:S(2)}) collective-permute-start(bf16[64,512]{1,0:T(8,128)(2,1)S(1)} %carry.8.refs_0_), channel_id=1, source_target_pairs={{0,4},{1,5},{2,6},{3,7},{4,0},{5,1},{6,2},{7,3},{8,12},{9,13},{10,... | collective-permute-start | bytes 196616 | tf_op jit(solution)/shard_map/ppermute | solution.py:386
  13.6 2.2 %collective-permute-start.5 = (bf16[64,512]{1,0:T(8,128)(2,1)S(1)}, bf16[64,512]{1,0:T(8,128)(2,1)S(1)}, u32[]{:S(2)}, u32[]{:S(2)}) collective-permute-start(bf16[64,512]{1,0:T(8,128)(2,1)S(1)} %carry.6.refs_0_), channel_id=1, source_target_pairs={{0,4},{1,5},{2,6},{3,7},{4,0},{5,1},{6,2},{7,3},{8,12},{9,13},{10,... | collective-permute-start | bytes 196616 | tf_op jit(solution)/shard_map/ppermute | solution.py:386
  15.8 1.4 %collective-permute-start.7 = (bf16[64,512]{1,0:T(8,128)(2,1)S(1)}, bf16[64,512]{1,0:T(8,128)(2,1)S(1)}, u32[]{:S(2)}, u32[]{:S(2)}) collective-permute-start(bf16[64,512]{1,0:T(8,128)(2,1)S(1)} %carry.7.refs_0_), channel_id=1, source_target_pairs={{0,4},{1,5},{2,6},{3,7},{4,0},{5,1},{6,2},{7,3},{8,12},{9,13},{10,... | collective-permute-start | bytes 196616 | tf_op jit(solution)/shard_map/ppermute | solution.py:386
  17.2 1.1 %saved.1 = (bf16[512,512]{1,0:T(8,128)(2,1)S(1)}, f32[256,512]{1,0:T(8,128)S(1)}, f32[256,512]{1,0:T(8,128)S(1)}, f32[256,512]{1,0:T(8,128)S(1)}, f32[256,512]{1...) custom-call(bf16[256,512]{1,0:T(8,128)(2,1)S(1)} %copy-done, ...), custom_call_target="tpu_custom_call" | custom-call | flops 402653184 | bytes 2363392 | tf_op jit(solution)/shard_map/saved/pallas_call | solution.py:363
  18.4 2.7 %collective-permute-start.16 = (bf16[64,512]{1,0:T(8,128)(2,1)S(1)}, bf16[64,512]{1,0:T(8,128)(2,1)S(1)}, u32[]{:S(2)}, u32[]{:S(2)}) collective-permute-start(bf16[64,512]{1,0:T(8,128)(2,1)S(1)} %get-tuple-element.93.refs_8_), channel_id=1, source_target_pairs={{0,2},{1,3},{2,0},{3,1},{4,6},{5,7},{6,4},{7,5},{8,10},{9,11},{10,... | collective-permute-start | bytes 196616 | tf_op jit(solution)/shard_map/ppermute | solution.py:386
  21.4 1.2 %collective-permute-start.10 = (bf16[64,512]{1,0:T(8,128)(2,1)S(1)}, bf16[64,512]{1,0:T(8,128)(2,1)S(1)}, u32[]{:S(2)}, u32[]{:S(2)}) collective-permute-start(bf16[64,512]{1,0:T(8,128)(2,1)S(1)} %get-tuple-element.91.refs_0_), channel_id=1, source_target_pairs={{0,2},{1,3},{2,0},{3,1},{4,6},{5,7},{6,4},{7,5},{8,10},{9,11},{10,... | collective-permute-start | bytes 196616 | tf_op jit(solution)/shard_map/ppermute | solution.py:386
  23.1 0.5 collective-permute-start.13
  23.9 2.0 %collective-permute-done.10.refs_1_ = bf16[64,512]{1,0:T(8,128)(2,1)S(1)} collective-permute-done((bf16[64,512]{1,0:T(8,128)(2,1)S(1)}, bf16[64,512]{1,0:T(8,128)(2,1)S(1)}, u32[]{:S(2)}, u32[]{:S(2)}) %collective-permute-start.10) | collective-permute-done | bytes 65568 | tf_op jit(solution)/shard_map/ppermute | solution.py:386
  25.9 0.5 collective-permute-start.14
  26.4 1.1 %collective-permute-done.13.refs_5_ = bf16[64,512]{1,0:T(8,128)(2,1)S(1)} collective-permute-done((bf16[64,512]{1,0:T(8,128)(2,1)S(1)}, bf16[64,512]{1,0:T(8,128)(2,1)S(1)}, u32[]{:S(2)}, u32[]{:S(2)}) %collective-permute-start.13) | collective-permute-done | bytes 65568 | tf_op jit(solution)/shard_map/ppermute | solution.py:386
  27.5 0.5 collective-permute-start.17
  28.1 0.7 collective-permute-done.15.refs_7_
  29.2 0.8 %apply.1 = (bf16[256,512]{1,0:T(8,128)(2,1)S(1)}, bf16[256,512]{1,0:T(8,128)(2,1)S(1)}, bf16[512,256]{1,0:T(8,128)(2,1)S(1)}, f32[512,512]{1,0:T(8,128)S(1)}, bf...) custom-call(bf16[64,512]{1,0:T(8,128)(2,1)S(1)} %get-tuple-element.91.refs_0, ...), custom_call_target="tpu_custom_call" | custom-call | flops 402653184 | bytes 2359296 | tf_op jit(solution)/shard_map/apply/pallas_call | solution.py:363
  30.1 2.7 %collective-permute-start.22 = (f32[2,512]{1,0:T(2,128)S(1)}, f32[2,512]{1,0:T(2,128)S(1)}, u32[]{:S(2)}, u32[]{:S(2)}) collective-permute-start(f32[2,512]{1,0:T(2,128)S(1)} %get-tuple-element.95.refs_0_), channel_id=1, source_target_pairs={{0,24},{8,16},{16,8},{24,0},{1,25},{9,17},{17,9},{25,1},{2,26},{10... | collective-permute-start | bytes 12296 | tf_op jit(solution)/shard_map/ppermute | solution.py:404
  32.8 0.5 collective-permute-start.21
  33.6 1.0 %collective-permute-done.22.refs_3_ = f32[2,512]{1,0:T(2,128)S(1)} collective-permute-done((f32[2,512]{1,0:T(2,128)S(1)}, f32[2,512]{1,0:T(2,128)S(1)}, u32[]{:S(2)}, u32[]{:S(2)}) %collective-permute-start.22) | collective-permute-done | bytes 4128 | tf_op jit(solution)/shard_map/ppermute | solution.py:404
  34.6 1.7 %collective-permute-done.21.refs_2_ = f32[2,512]{1,0:T(2,128)S(1)} collective-permute-done((f32[2,512]{1,0:T(2,128)S(1)}, f32[2,512]{1,0:T(2,128)S(1)}, u32[]{:S(2)}, u32[]{:S(2)}) %collective-permute-start.21) | collective-permute-done | bytes 4128 | tf_op jit(solution)/shard_map/ppermute | solution.py:404
  36.9 0.9 %apply_back.1 = (bf16[256,256]{1,0:T(8,128)(2,1)S(1)}, bf16[256,256]{1,0:T(8,128)(2,1)S(1)}, f32[64,512]{1,0:T(8,128)S(1)}, f32[64,512]{1,0:T(8,128)S(1)}, f32[6...) custom-call(f32[2,512]{1,0:T(2,128)S(1)} %get-tuple-element.95.refs_0, ...), custom_call_target="tpu_custom_call" | custom-call | flops 536870912 | bytes 4210688 | tf_op jit(solution)/shard_map/apply_back/pallas_call | solution.py:363
  37.8 0.6 collective-permute-start.25
  38.4 1.5 %collective-permute-start.23 = (bf16[64,512]{1,0:T(8,128)(2,1)S(1)}, bf16[64,512]{1,0:T(8,128)(2,1)S(1)}, u32[]{:S(2)}, u32[]{:S(2)}) collective-permute-start(bf16[64,512]{1,0:T(8,128)(2,1)S(1)} %get-tuple-element.108), channel_id=1, source_target_pairs={{0,2},{1,3},{2,0},{3,1},{4,6},{5,7},{6,4},{7,5},{8,10},{9,11},{10,... | collective-permute-start | bytes 196616 | tf_op jit(solution)/shard_map/ppermute | solution.py:386
  39.9 0.6 collective-permute-start.27
  40.4 1.7 %collective-permute-done.25.got = bf16[64,512]{1,0:T(8,128)(2,1)S(1)} collective-permute-done((bf16[64,512]{1,0:T(8,128)(2,1)S(1)}, bf16[64,512]{1,0:T(8,128)(2,1)S(1)}, u32[]{:S(2)}, u32[]{:S(2)}) %collective-permute-start.25) | collective-permute-done | bytes 65568 | tf_op jit(solution)/shard_map/ppermute | solution.py:386
  42.1 3.4 %collective-permute-start.26 = (bf16[64,512]{1,0:T(8,128)(2,1)S(1)}, bf16[64,512]{1,0:T(8,128)(2,1)S(1)}, u32[]{:S(2)}, u32[]{:S(2)}) collective-permute-start(bf16[64,512]{1,0:T(8,128)(2,1)S(1)} %carry.10.refs_0_), channel_id=1, source_target_pairs={{0,4},{1,5},{2,6},{3,7},{4,0},{5,1},{6,2},{7,3},{8,12},{9,13},{10,... | collective-permute-start | bytes 196616 | tf_op jit(solution)/shard_map/ppermute | solution.py:386
  45.6 0.7 collective-permute-start.24
  46.3 2.4 %collective-permute-start.28 = (bf16[64,512]{1,0:T(8,128)(2,1)S(1)}, bf16[64,512]{1,0:T(8,128)(2,1)S(1)}, u32[]{:S(2)}, u32[]{:S(2)}) collective-permute-start(bf16[64,512]{1,0:T(8,128)(2,1)S(1)} %carry.11.refs_0_), channel_id=1, source_target_pairs={{0,4},{1,5},{2,6},{3,7},{4,0},{5,1},{6,2},{7,3},{8,12},{9,13},{10,... | collective-permute-start | bytes 196616 | tf_op jit(solution)/shard_map/ppermute | solution.py:386
  48.7 1.2 %collective-permute-done.26.refs_1_ = bf16[64,512]{1,0:T(8,128)(2,1)S(1)} collective-permute-done((bf16[64,512]{1,0:T(8,128)(2,1)S(1)}, bf16[64,512]{1,0:T(8,128)(2,1)S(1)}, u32[]{:S(2)}, u32[]{:S(2)}) %collective-permute-start.26) | collective-permute-done | bytes 65568 | tf_op jit(solution)/shard_map/ppermute | solution.py:386
  50.0 1.3 %collective-permute-done.24.refs_1_ = bf16[64,512]{1,0:T(8,128)(2,1)S(1)} collective-permute-done((bf16[64,512]{1,0:T(8,128)(2,1)S(1)}, bf16[64,512]{1,0:T(8,128)(2,1)S(1)}, u32[]{:S(2)}, u32[]{:S(2)}) %collective-permute-start.24) | collective-permute-done | bytes 65568 | tf_op jit(solution)/shard_map/ppermute | solution.py:386
  51.5 0.8 %collective-permute-start.29 = (bf16[64,512]{1,0:T(8,128)(2,1)S(1)}, bf16[64,512]{1,0:T(8,128)(2,1)S(1)}, u32[]{:S(2)}, u32[]{:S(2)}) collective-permute-start(bf16[64,512]{1,0:T(8,128)(2,1)S(1)} %get-tuple-element.119.refs_0_), channel_id=1, source_target_pairs={{0,2},{1,3},{2,0},{3,1},{4,6},{5,7},{6,4},{7,5},{8,10},{9,11},{10,... | collective-permute-start | bytes 196616 | tf_op jit(solution)/shard_map/ppermute | solution.py:386
  52.9 0.9 %collective-permute-start.35 = (bf16[64,512]{1,0:T(8,128)(2,1)S(1)}, bf16[64,512]{1,0:T(8,128)(2,1)S(1)}, u32[]{:S(2)}, u32[]{:S(2)}) collective-permute-start(bf16[64,512]{1,0:T(8,128)(2,1)S(1)} %get-tuple-element.127.refs_0_), channel_id=1, source_target_pairs={{0,2},{1,3},{2,0},{3,1},{4,6},{5,7},{6,4},{7,5},{8,10},{9,11},{10,... | collective-permute-start | bytes 196616 | tf_op jit(solution)/shard_map/ppermute | solution.py:386
  54.3 1.5 %collective-permute-done.29.refs_1_ = bf16[64,512]{1,0:T(8,128)(2,1)S(1)} collective-permute-done((bf16[64,512]{1,0:T(8,128)(2,1)S(1)}, bf16[64,512]{1,0:T(8,128)(2,1)S(1)}, u32[]{:S(2)}, u32[]{:S(2)}) %collective-permute-start.29) | collective-permute-done | bytes 65568 | tf_op jit(solution)/shard_map/ppermute | solution.py:386
  55.8 0.5 collective-permute-start.33
  56.3 0.9 %collective-permute-done.35.refs_1_ = bf16[64,512]{1,0:T(8,128)(2,1)S(1)} collective-permute-done((bf16[64,512]{1,0:T(8,128)(2,1)S(1)}, bf16[64,512]{1,0:T(8,128)(2,1)S(1)}, u32[]{:S(2)}, u32[]{:S(2)}) %collective-permute-start.35) | collective-permute-done | bytes 65568 | tf_op jit(solution)/shard_map/ppermute | solution.py:386
  57.2 0.5 collective-permute-start.37
  57.8 0.8 %second_first.1 = (bf16[256,512]{1,0:T(8,128)(2,1)S(1)}, bf16[256,512]{1,0:T(8,128)(2,1)S(1)}, bf16[256,256]{1,0:T(8,128)(2,1)S(1)}, f32[128,512]{1,0:T(8,128)S(...) custom-call(bf16[64,512]{1,0:T(8,128)(2,1)S(1)} %get-tuple-element.119.refs_0_, ...), custom_call_target="tpu_custom_call" | custom-call | flops 402653184 | bytes 3670016 | tf_op jit(solution)/shard_map/second_first/pallas_call | solution.py:363
  58.7 0.7 %second_last.1 = (bf16[512,256]{1,0:T(8,128)(2,1)S(1)}, bf16[256,256]{1,0:T(8,128)(2,1)S(1)}, bf16[256,256]{1,0:T(8,128)(2,1)S(1)}, f32[96,512]{1,0:T(8,128)S(1)...) custom-call(bf16[64,512]{1,0:T(8,128)(2,1)S(1)} %get-tuple-element.127.refs_0_, ...), custom_call_target="tpu_custom_call" | custom-call | flops 402653184 | bytes 3670016 | tf_op jit(solution)/shard_map/second_last/pallas_call | solution.py:363
  59.4 2.3 %collective-permute-start.38 = (bf16[96,512]{1,0:T(8,128)(2,1)S(1)}, bf16[96,512]{1,0:T(8,128)(2,1)S(1)}, u32[]{:S(2)}, u32[]{:S(2)}) collective-permute-start(bf16[96,512]{1,0:T(8,128)(2,1)S(1)} %get-tuple-element.144), channel_id=1, source_target_pairs={{0,6},{1,7},{2,4},{3,5},{4,2},{5,3},{6,0},{7,1},{8,14},{9,15},{10,... | collective-permute-start | bytes 294920 | tf_op jit(solution)/shard_map/ppermute | solution.py:381
  61.8 2.1 %collective-permute-start.40 = (bf16[96,512]{1,0:T(8,128)(2,1)S(1)}, bf16[96,512]{1,0:T(8,128)(2,1)S(1)}, u32[]{:S(2)}, u32[]{:S(2)}) collective-permute-start(bf16[96,512]{1,0:T(8,128)(2,1)S(1)} %get-tuple-element.146), channel_id=1, source_target_pairs={{0,2},{1,3},{2,0},{3,1},{4,6},{5,7},{6,4},{7,5},{8,10},{9,11},{10,... | collective-permute-start | bytes 294920 | tf_op jit(solution)/shard_map/ppermute | solution.py:381
  63.9 1.0 %query_grad.1 = bf16[256,512]{1,0:T(8,128)(2,1)} custom-call(bf16[256,256]{1,0:T(8,128)(2,1)S(1)} %get-tuple-element.101.gate_back, bf16[256,256]{1,0:T(8,128)(2,1)S(1)} %get-tuple-element.102.up_back, bf16[256,512]{1,0:T(8,128)(2,1)S(1)} %get-tuple-element.103.f1t, bf16[256,512]{1,0:T(8,128)(2,1)S(1)} %get-tuple-element.104.f3t), custom_call_target="tpu_custom_call" | custom-call | flops 134217728 | bytes 786432 | tf_op jit(solution)/shard_map/query_grad/pallas_call | solution.py:363
  64.9 1.4 %token_grads.1 = (bf16[256,512]{1,0:T(8,128)(2,1)}, bf16[256,512]{1,0:T(8,128)(2,1)}) custom-call(f32[1,256]{1,0:T(1,128)S(1)} %bitcast.30, bf16[256,256]{1,0:T(8,128)(2,1)S(1)} %get-tuple-element.105.refs_1_, bf16[256,256]{1,0:T(8,128)(2,1)S(1)} %get-tuple-element.126.refs_2_, bf16[256,256]{1,0:T(8,128)(2,1)S(1)} %get-tuple-element.131.refs_3_, ...), custom_call_target="tpu_custom_call" | custom-call | flops 402653184 | bytes 2360320 | tf_op jit(solution)/shard_map/token_grads/pallas_call | solution.py:363
  66.2 0.7 %collective-permute-done.38.refs_4_ = bf16[96,512]{1,0:T(8,128)(2,1)S(1)} collective-permute-done((bf16[96,512]{1,0:T(8,128)(2,1)S(1)}, bf16[96,512]{1,0:T(8,128)(2,1)S(1)}, u32[]{:S(2)}, u32[]{:S(2)}) %collective-permute-start.38) | collective-permute-done | bytes 98336 | tf_op jit(solution)/shard_map/ppermute | solution.py:381
  67.0 4.1 %collective-permute-done.39.refs_5_ = bf16[96,512]{1,0:T(8,128)(2,1)S(1)} collective-permute-done((bf16[96,512]{1,0:T(8,128)(2,1)S(1)}, bf16[96,512]{1,0:T(8,128)(2,1)S(1)}, u32[]{:S(2)}, u32[]{:S(2)}) %collective-permute-start.39) | collective-permute-done | bytes 98336 | tf_op jit(solution)/shard_map/ppermute | solution.py:381
  71.1 0.7 owner_result.1
  (73 shorter events, 5.7 us)
Async XLA Ops:
  0.6 1.0 %copy-start.5 = (f32[256,1]{0,1:T(1,128)S(1)}, f32[256,1]{0,1:T(1,128)}, u32[]{:S(2)}) copy-start(f32[256,1]{0,1:T(1,128)} %param.13) | copy-start | bytes 3076
  0.6 2.5 %collective-permute-start.1 = (bf16[256,512]{1,0:T(8,128)(2,1)}, bf16[256,512]{1,0:T(8,128)(2,1)S(1)}, u32[]{:S(2)}, u32[]{:S(2)}) collective-permute-start(bf16[256,512]{1,0:T(8,128)(2,1)} %vo.3), channel_id=1, source_target_pairs={{0,1},{1,0},{2,3},{3,2},{4,5},{5,4},{6,7},{7,6},{8,9},{9,8},{10,11... | collective-permute-start | bytes 786440 | tf_op jit(solution)/shard_map/ppermute | solution.py:502
  1.2 2.0 %collective-permute-start = (bf16[256,512]{1,0:T(8,128)(2,1)}, bf16[256,512]{1,0:T(8,128)(2,1)S(1)}, u32[]{:S(2)}, u32[]{:S(2)}) collective-permute-start(bf16[256,512]{1,0:T(8,128)(2,1)} %refs_4_.1), channel_id=1, source_target_pairs={{0,1},{1,0},{2,3},{3,2},{4,5},{5,4},{6,7},{7,6},{8,9},{9,8},{10,11... | collective-permute-start | bytes 786440 | tf_op jit(solution)/shard_map/ppermute | solution.py:502
  1.2 15.9 %collective-permute-start.3 = (bf16[256,512]{1,0:T(8,128)(2,1)}, bf16[256,512]{1,0:T(8,128)(2,1)S(1)}, u32[]{:S(2)}, u32[]{:S(2)}) collective-permute-start(bf16[256,512]{1,0:T(8,128)(2,1)} %go.1), channel_id=1, source_target_pairs={{0,1},{1,0},{2,3},{3,2},{4,5},{5,4},{6,7},{7,6},{8,9},{9,8},{10,11... | collective-permute-start | bytes 786440 | tf_op jit(solution)/shard_map/ppermute | solution.py:502
  1.7 1.2 %copy-start.7 = (bf16[1,512,256]{2,1,0:T(8,128)(2,1)S(1)}, bf16[1,512,256]{2,1,0:T(8,128)(2,1)}, u32[]{:S(2)}) copy-start(bf16[1,512,256]{2,1,0:T(8,128)(2,1)} %param.16) | copy-start | bytes 786436
  1.7 1.4 %collective-permute-start.2 = (f32[1,256]{1,0:T(1,128)S(1)}, f32[1,256]{1,0:T(1,128)S(1)}, u32[]{:S(2)}, u32[]{:S(2)}) collective-permute-start(f32[1,256]{1,0:T(1,128)S(1)} %bitcast.27), channel_id=1, source_target_pairs={{0,1},{1,0},{2,3},{3,2},{4,5},{5,4},{6,7},{7,6},{8,9},{9,8},{10,11... | collective-permute-start | bytes 3080 | tf_op jit(solution)/shard_map/ppermute | solution.py:502
  1.8 1.4 %copy-start.3 = (bf16[256,512]{1,0:T(8,128)(2,1)S(1)}, bf16[256,512]{1,0:T(8,128)(2,1)}, u32[]{:S(2)}) copy-start(bf16[256,512]{1,0:T(8,128)(2,1)} %vo.3) | copy-start | bytes 786436
  2.9 1.0 %copy-start.2 = (bf16[1,256,512]{2,1,0:T(8,128)(2,1)S(1)}, bf16[1,256,512]{2,1,0:T(8,128)(2,1)}, u32[]{:S(2)}) copy-start(bf16[1,256,512]{2,1,0:T(8,128)(2,1)} %param.17) | copy-start | bytes 786436
  4.0 4.2 %copy-start.1 = (bf16[256,512]{1,0:T(8,128)(2,1)S(1)}, bf16[256,512]{1,0:T(8,128)(2,1)}, u32[]{:S(2)}) copy-start(bf16[256,512]{1,0:T(8,128)(2,1)} %refs_10_.1) | copy-start | bytes 786436
  5.1 5.4 %collective-permute-start.8 = (bf16[64,512]{1,0:T(8,128)(2,1)S(1)}, bf16[64,512]{1,0:T(8,128)(2,1)S(1)}, u32[]{:S(2)}, u32[]{:S(2)}) collective-permute-start(bf16[64,512]{1,0:T(8,128)(2,1)S(1)} %get-tuple-element.88), channel_id=1, source_target_pairs={{0,2},{1,3},{2,0},{3,1},{4,6},{5,7},{6,4},{7,5},{8,10},{9,11},{10,... | collective-permute-start | bytes 196616 | tf_op jit(solution)/shard_map/ppermute | solution.py:386
  8.2 19.3 %collective-permute-start.19 = (bf16[256,512]{1,0:T(8,128)(2,1)S(1)}, bf16[256,512]{1,0:T(8,128)(2,1)S(1)}, u32[]{:S(2)}, u32[]{:S(2)}) collective-permute-start(bf16[256,512]{1,0:T(8,128)(2,1)S(1)} %copy-done.1), channel_id=1, source_target_pairs={{0,1},{1,0},{2,3},{3,2},{4,5},{5,4},{6,7},{7,6},{8,9},{9,8},{10,11... | collective-permute-start | bytes 786440 | tf_op jit(solution)/shard_map/ppermute | solution.py:502
  8.2 5.4 %collective-permute-start.4 = (bf16[64,512]{1,0:T(8,128)(2,1)S(1)}, bf16[64,512]{1,0:T(8,128)(2,1)S(1)}, u32[]{:S(2)}, u32[]{:S(2)}) collective-permute-start(bf16[64,512]{1,0:T(8,128)(2,1)S(1)} %get-tuple-element.80), channel_id=1, source_target_pairs={{0,2},{1,3},{2,0},{3,1},{4,6},{5,7},{6,4},{7,5},{8,10},{9,11},{10,... | collective-permute-start | bytes 196616 | tf_op jit(solution)/shard_map/ppermute | solution.py:386
  8.4 7.4 %collective-permute-start.6 = (bf16[64,512]{1,0:T(8,128)(2,1)S(1)}, bf16[64,512]{1,0:T(8,128)(2,1)S(1)}, u32[]{:S(2)}, u32[]{:S(2)}) collective-permute-start(bf16[64,512]{1,0:T(8,128)(2,1)S(1)} %get-tuple-element.84), channel_id=1, source_target_pairs={{0,2},{1,3},{2,0},{3,1},{4,6},{5,7},{6,4},{7,5},{8,10},{9,11},{10,... | collective-permute-start | bytes 196616 | tf_op jit(solution)/shard_map/ppermute | solution.py:386
  10.6 7.7 %collective-permute-start.9 = (bf16[64,512]{1,0:T(8,128)(2,1)S(1)}, bf16[64,512]{1,0:T(8,128)(2,1)S(1)}, u32[]{:S(2)}, u32[]{:S(2)}) collective-permute-start(bf16[64,512]{1,0:T(8,128)(2,1)S(1)} %carry.8.refs_0_), channel_id=1, source_target_pairs={{0,4},{1,5},{2,6},{3,7},{4,0},{5,1},{6,2},{7,3},{8,12},{9,13},{10,... | collective-permute-start | bytes 196616 | tf_op jit(solution)/shard_map/ppermute | solution.py:386
  13.6 3.6 %copy-start.4 = (bf16[256,512]{1,0:T(8,128)(2,1)S(1)}, bf16[256,512]{1,0:T(8,128)(2,1)}, u32[]{:S(2)}) copy-start(bf16[256,512]{1,0:T(8,128)(2,1)} %go.1) | copy-start | bytes 786436
  13.6 7.7 %collective-permute-start.5 = (bf16[64,512]{1,0:T(8,128)(2,1)S(1)}, bf16[64,512]{1,0:T(8,128)(2,1)S(1)}, u32[]{:S(2)}, u32[]{:S(2)}) collective-permute-start(bf16[64,512]{1,0:T(8,128)(2,1)S(1)} %carry.6.refs_0_), channel_id=1, source_target_pairs={{0,4},{1,5},{2,6},{3,7},{4,0},{5,1},{6,2},{7,3},{8,12},{9,13},{10,... | collective-permute-start | bytes 196616 | tf_op jit(solution)/shard_map/ppermute | solution.py:386
  15.8 1.4 %copy-start.6 = (f32[512]{0:T(512)S(1)}, f32[512]{0:T(512)}, u32[]{:S(2)}) copy-start(f32[512]{0:T(512)} %param.14) | copy-start | bytes 6148
  15.8 7.2 %collective-permute-start.7 = (bf16[64,512]{1,0:T(8,128)(2,1)S(1)}, bf16[64,512]{1,0:T(8,128)(2,1)S(1)}, u32[]{:S(2)}, u32[]{:S(2)}) collective-permute-start(bf16[64,512]{1,0:T(8,128)(2,1)S(1)} %carry.7.refs_0_), channel_id=1, source_target_pairs={{0,4},{1,5},{2,6},{3,7},{4,0},{5,1},{6,2},{7,3},{8,12},{9,13},{10,... | collective-permute-start | bytes 196616 | tf_op jit(solution)/shard_map/ppermute | solution.py:386
  18.4 5.5 %collective-permute-start.16 = (bf16[64,512]{1,0:T(8,128)(2,1)S(1)}, bf16[64,512]{1,0:T(8,128)(2,1)S(1)}, u32[]{:S(2)}, u32[]{:S(2)}) collective-permute-start(bf16[64,512]{1,0:T(8,128)(2,1)S(1)} %get-tuple-element.93.refs_8_), channel_id=1, source_target_pairs={{0,2},{1,3},{2,0},{3,1},{4,6},{5,7},{6,4},{7,5},{8,10},{9,11},{10,... | collective-permute-start | bytes 196616 | tf_op jit(solution)/shard_map/ppermute | solution.py:386
  21.4 4.5 %collective-permute-start.10 = (bf16[64,512]{1,0:T(8,128)(2,1)S(1)}, bf16[64,512]{1,0:T(8,128)(2,1)S(1)}, u32[]{:S(2)}, u32[]{:S(2)}) collective-permute-start(bf16[64,512]{1,0:T(8,128)(2,1)S(1)} %get-tuple-element.91.refs_0_), channel_id=1, source_target_pairs={{0,2},{1,3},{2,0},{3,1},{4,6},{5,7},{6,4},{7,5},{8,10},{9,11},{10,... | collective-permute-start | bytes 196616 | tf_op jit(solution)/shard_map/ppermute | solution.py:386
  23.1 4.3 %collective-permute-start.13 = (bf16[64,512]{1,0:T(8,128)(2,1)S(1)}, bf16[64,512]{1,0:T(8,128)(2,1)S(1)}, u32[]{:S(2)}, u32[]{:S(2)}) collective-permute-start(bf16[64,512]{1,0:T(8,128)(2,1)S(1)} %get-tuple-element.92.refs_4_), channel_id=1, source_target_pairs={{0,2},{1,3},{2,0},{3,1},{4,6},{5,7},{6,4},{7,5},{8,10},{9,11},{10,... | collective-permute-start | bytes 196616 | tf_op jit(solution)/shard_map/ppermute | solution.py:386
  23.9 4.1 %collective-permute-start.18 = (bf16[64,512]{1,0:T(8,128)(2,1)S(1)}, bf16[64,512]{1,0:T(8,128)(2,1)S(1)}, u32[]{:S(2)}, u32[]{:S(2)}) collective-permute-start(bf16[64,512]{1,0:T(8,128)(2,1)S(1)} %collective-permute-done.16.refs_9_), channel_id=1, source_target_pairs={{0,1},{1,0},{2,3},{3,2},{4,5},{5,4},{6,7},{7,6},{8,9},{9,8},{10,11... | collective-permute-start | bytes 196616 | tf_op jit(solution)/shard_map/ppermute | solution.py:397
  25.9 2.8 %collective-permute-start.11 = (bf16[64,512]{1,0:T(8,128)(2,1)S(1)}, bf16[64,512]{1,0:T(8,128)(2,1)S(1)}, u32[]{:S(2)}, u32[]{:S(2)}) collective-permute-start(bf16[64,512]{1,0:T(8,128)(2,1)S(1)} %get-tuple-element.91.refs_0_), channel_id=1, source_target_pairs={{0,1},{1,0},{2,3},{3,2},{4,5},{5,4},{6,7},{7,6},{8,9},{9,8},{10,11... | collective-permute-start | bytes 196616 | tf_op jit(solution)/shard_map/ppermute | solution.py:397
  25.9 2.8 %collective-permute-start.14 = (bf16[64,512]{1,0:T(8,128)(2,1)S(1)}, bf16[64,512]{1,0:T(8,128)(2,1)S(1)}, u32[]{:S(2)}, u32[]{:S(2)}) collective-permute-start(bf16[64,512]{1,0:T(8,128)(2,1)S(1)} %get-tuple-element.92.refs_4_), channel_id=1, source_target_pairs={{0,1},{1,0},{2,3},{3,2},{4,5},{5,4},{6,7},{7,6},{8,9},{9,8},{10,11... | collective-permute-start | bytes 196616 | tf_op jit(solution)/shard_map/ppermute | solution.py:397
  27.5 1.3 %collective-permute-start.15 = (bf16[64,512]{1,0:T(8,128)(2,1)S(1)}, bf16[64,512]{1,0:T(8,128)(2,1)S(1)}, u32[]{:S(2)}, u32[]{:S(2)}) collective-permute-start(bf16[64,512]{1,0:T(8,128)(2,1)S(1)} %collective-permute-done.13.refs_5_), channel_id=1, source_target_pairs={{0,1},{1,0},{2,3},{3,2},{4,5},{5,4},{6,7},{7,6},{8,9},{9,8},{10,11... | collective-permute-start | bytes 196616 | tf_op jit(solution)/shard_map/ppermute | solution.py:397
  27.5 1.4 %collective-permute-start.17 = (bf16[64,512]{1,0:T(8,128)(2,1)S(1)}, bf16[64,512]{1,0:T(8,128)(2,1)S(1)}, u32[]{:S(2)}, u32[]{:S(2)}) collective-permute-start(bf16[64,512]{1,0:T(8,128)(2,1)S(1)} %get-tuple-element.93.refs_8_), channel_id=1, source_target_pairs={{0,1},{1,0},{2,3},{3,2},{4,5},{5,4},{6,7},{7,6},{8,9},{9,8},{10,11... | collective-permute-start | bytes 196616 | tf_op jit(solution)/shard_map/ppermute | solution.py:397
  28.0 1.3 %collective-permute-start.12 = (bf16[64,512]{1,0:T(8,128)(2,1)S(1)}, bf16[64,512]{1,0:T(8,128)(2,1)S(1)}, u32[]{:S(2)}, u32[]{:S(2)}) collective-permute-start(bf16[64,512]{1,0:T(8,128)(2,1)S(1)} %collective-permute-done.10.refs_1_), channel_id=1, source_target_pairs={{0,1},{1,0},{2,3},{3,2},{4,5},{5,4},{6,7},{7,6},{8,9},{9,8},{10,11... | collective-permute-start | bytes 196616 | tf_op jit(solution)/shard_map/ppermute | solution.py:397
  30.1 4.6 %collective-permute-start.22 = (f32[2,512]{1,0:T(2,128)S(1)}, f32[2,512]{1,0:T(2,128)S(1)}, u32[]{:S(2)}, u32[]{:S(2)}) collective-permute-start(f32[2,512]{1,0:T(2,128)S(1)} %get-tuple-element.95.refs_0_), channel_id=1, source_target_pairs={{0,24},{8,16},{16,8},{24,0},{1,25},{9,17},{17,9},{25,1},{2,26},{10... | collective-permute-start | bytes 12296 | tf_op jit(solution)/shard_map/ppermute | solution.py:404
  32.8 3.6 %collective-permute-start.21 = (f32[2,512]{1,0:T(2,128)S(1)}, f32[2,512]{1,0:T(2,128)S(1)}, u32[]{:S(2)}, u32[]{:S(2)}) collective-permute-start(f32[2,512]{1,0:T(2,128)S(1)} %get-tuple-element.95.refs_0_), channel_id=1, source_target_pairs={{0,16},{8,24},{16,0},{24,8},{1,17},{9,25},{17,1},{25,9},{2,18},{10... | collective-permute-start | bytes 12296 | tf_op jit(solution)/shard_map/ppermute | solution.py:404
  33.3 3.6 %collective-permute-start.20 = (f32[2,512]{1,0:T(2,128)S(1)}, f32[2,512]{1,0:T(2,128)S(1)}, u32[]{:S(2)}, u32[]{:S(2)}) collective-permute-start(f32[2,512]{1,0:T(2,128)S(1)} %get-tuple-element.95.refs_0_), channel_id=1, source_target_pairs={{0,8},{8,0},{16,24},{24,16},{1,9},{9,1},{17,25},{25,17},{2,10},{10... | collective-permute-start | bytes 12296 | tf_op jit(solution)/shard_map/ppermute | solution.py:404
  37.8 4.3 %collective-permute-start.25 = (bf16[64,512]{1,0:T(8,128)(2,1)S(1)}, bf16[64,512]{1,0:T(8,128)(2,1)S(1)}, u32[]{:S(2)}, u32[]{:S(2)}) collective-permute-start(bf16[64,512]{1,0:T(8,128)(2,1)S(1)} %get-tuple-element.112), channel_id=1, source_target_pairs={{0,2},{1,3},{2,0},{3,1},{4,6},{5,7},{6,4},{7,5},{8,10},{9,11},{10,... | collective-permute-start | bytes 196616 | tf_op jit(solution)/shard_map/ppermute | solution.py:386
  38.4 7.2 %collective-permute-start.23 = (bf16[64,512]{1,0:T(8,128)(2,1)S(1)}, bf16[64,512]{1,0:T(8,128)(2,1)S(1)}, u32[]{:S(2)}, u32[]{:S(2)}) collective-permute-start(bf16[64,512]{1,0:T(8,128)(2,1)S(1)} %get-tuple-element.108), channel_id=1, source_target_pairs={{0,2},{1,3},{2,0},{3,1},{4,6},{5,7},{6,4},{7,5},{8,10},{9,11},{10,... | collective-permute-start | bytes 196616 | tf_op jit(solution)/shard_map/ppermute | solution.py:386
  39.9 6.4 %collective-permute-start.27 = (bf16[64,512]{1,0:T(8,128)(2,1)S(1)}, bf16[64,512]{1,0:T(8,128)(2,1)S(1)}, u32[]{:S(2)}, u32[]{:S(2)}) collective-permute-start(bf16[64,512]{1,0:T(8,128)(2,1)S(1)} %get-tuple-element.116), channel_id=1, source_target_pairs={{0,2},{1,3},{2,0},{3,1},{4,6},{5,7},{6,4},{7,5},{8,10},{9,11},{10,... | collective-permute-start | bytes 196616 | tf_op jit(solution)/shard_map/ppermute | solution.py:386
  42.1 7.7 %collective-permute-start.26 = (bf16[64,512]{1,0:T(8,128)(2,1)S(1)}, bf16[64,512]{1,0:T(8,128)(2,1)S(1)}, u32[]{:S(2)}, u32[]{:S(2)}) collective-permute-start(bf16[64,512]{1,0:T(8,128)(2,1)S(1)} %carry.10.refs_0_), channel_id=1, source_target_pairs={{0,4},{1,5},{2,6},{3,7},{4,0},{5,1},{6,2},{7,3},{8,12},{9,13},{10,... | collective-permute-start | bytes 196616 | tf_op jit(solution)/shard_map/ppermute | solution.py:386
  45.6 5.7 %collective-permute-start.24 = (bf16[64,512]{1,0:T(8,128)(2,1)S(1)}, bf16[64,512]{1,0:T(8,128)(2,1)S(1)}, u32[]{:S(2)}, u32[]{:S(2)}) collective-permute-start(bf16[64,512]{1,0:T(8,128)(2,1)S(1)} %carry.9.refs_0_), channel_id=1, source_target_pairs={{0,4},{1,5},{2,6},{3,7},{4,0},{5,1},{6,2},{7,3},{8,12},{9,13},{10,... | collective-permute-start | bytes 196616 | tf_op jit(solution)/shard_map/ppermute | solution.py:386
  46.3 6.4 %collective-permute-start.28 = (bf16[64,512]{1,0:T(8,128)(2,1)S(1)}, bf16[64,512]{1,0:T(8,128)(2,1)S(1)}, u32[]{:S(2)}, u32[]{:S(2)}) collective-permute-start(bf16[64,512]{1,0:T(8,128)(2,1)S(1)} %carry.11.refs_0_), channel_id=1, source_target_pairs={{0,4},{1,5},{2,6},{3,7},{4,0},{5,1},{6,2},{7,3},{8,12},{9,13},{10,... | collective-permute-start | bytes 196616 | tf_op jit(solution)/shard_map/ppermute | solution.py:386
  50.0 4.3 %collective-permute-start.32 = (bf16[64,512]{1,0:T(8,128)(2,1)S(1)}, bf16[64,512]{1,0:T(8,128)(2,1)S(1)}, u32[]{:S(2)}, u32[]{:S(2)}) collective-permute-start(bf16[64,512]{1,0:T(8,128)(2,1)S(1)} %get-tuple-element.120.refs_4_), channel_id=1, source_target_pairs={{0,2},{1,3},{2,0},{3,1},{4,6},{5,7},{6,4},{7,5},{8,10},{9,11},{10,... | collective-permute-start | bytes 196616 | tf_op jit(solution)/shard_map/ppermute | solution.py:386
  51.5 4.3 %collective-permute-start.29 = (bf16[64,512]{1,0:T(8,128)(2,1)S(1)}, bf16[64,512]{1,0:T(8,128)(2,1)S(1)}, u32[]{:S(2)}, u32[]{:S(2)}) collective-permute-start(bf16[64,512]{1,0:T(8,128)(2,1)S(1)} %get-tuple-element.119.refs_0_), channel_id=1, source_target_pairs={{0,2},{1,3},{2,0},{3,1},{4,6},{5,7},{6,4},{7,5},{8,10},{9,11},{10,... | collective-permute-start | bytes 196616 | tf_op jit(solution)/shard_map/ppermute | solution.py:386
  52.9 4.3 %collective-permute-start.35 = (bf16[64,512]{1,0:T(8,128)(2,1)S(1)}, bf16[64,512]{1,0:T(8,128)(2,1)S(1)}, u32[]{:S(2)}, u32[]{:S(2)}) collective-permute-start(bf16[64,512]{1,0:T(8,128)(2,1)S(1)} %get-tuple-element.127.refs_0_), channel_id=1, source_target_pairs={{0,2},{1,3},{2,0},{3,1},{4,6},{5,7},{6,4},{7,5},{8,10},{9,11},{10,... | collective-permute-start | bytes 196616 | tf_op jit(solution)/shard_map/ppermute | solution.py:386
  54.3 3.0 %collective-permute-start.34 = (bf16[64,512]{1,0:T(8,128)(2,1)S(1)}, bf16[64,512]{1,0:T(8,128)(2,1)S(1)}, u32[]{:S(2)}, u32[]{:S(2)}) collective-permute-start(bf16[64,512]{1,0:T(8,128)(2,1)S(1)} %collective-permute-done.32.refs_5_), channel_id=1, source_target_pairs={{0,1},{1,0},{2,3},{3,2},{4,5},{5,4},{6,7},{7,6},{8,9},{9,8},{10,11... | collective-permute-start | bytes 196616 | tf_op jit(solution)/shard_map/ppermute | solution.py:397
  55.8 2.0 %collective-permute-start.30 = (bf16[64,512]{1,0:T(8,128)(2,1)S(1)}, bf16[64,512]{1,0:T(8,128)(2,1)S(1)}, u32[]{:S(2)}, u32[]{:S(2)}) collective-permute-start(bf16[64,512]{1,0:T(8,128)(2,1)S(1)} %get-tuple-element.119.refs_0_), channel_id=1, source_target_pairs={{0,1},{1,0},{2,3},{3,2},{4,5},{5,4},{6,7},{7,6},{8,9},{9,8},{10,11... | collective-permute-start | bytes 196616 | tf_op jit(solution)/shard_map/ppermute | solution.py:397
  55.8 2.0 %collective-permute-start.33 = (bf16[64,512]{1,0:T(8,128)(2,1)S(1)}, bf16[64,512]{1,0:T(8,128)(2,1)S(1)}, u32[]{:S(2)}, u32[]{:S(2)}) collective-permute-start(bf16[64,512]{1,0:T(8,128)(2,1)S(1)} %get-tuple-element.120.refs_4_), channel_id=1, source_target_pairs={{0,1},{1,0},{2,3},{3,2},{4,5},{5,4},{6,7},{7,6},{8,9},{9,8},{10,11... | collective-permute-start | bytes 196616 | tf_op jit(solution)/shard_map/ppermute | solution.py:397
  56.3 1.5 %collective-permute-start.31 = (bf16[64,512]{1,0:T(8,128)(2,1)S(1)}, bf16[64,512]{1,0:T(8,128)(2,1)S(1)}, u32[]{:S(2)}, u32[]{:S(2)}) collective-permute-start(bf16[64,512]{1,0:T(8,128)(2,1)S(1)} %collective-permute-done.29.refs_1_), channel_id=1, source_target_pairs={{0,1},{1,0},{2,3},{3,2},{4,5},{5,4},{6,7},{7,6},{8,9},{9,8},{10,11... | collective-permute-start | bytes 196616 | tf_op jit(solution)/shard_map/ppermute | solution.py:397
  57.2 1.3 %collective-permute-start.36 = (bf16[64,512]{1,0:T(8,128)(2,1)S(1)}, bf16[64,512]{1,0:T(8,128)(2,1)S(1)}, u32[]{:S(2)}, u32[]{:S(2)}) collective-permute-start(bf16[64,512]{1,0:T(8,128)(2,1)S(1)} %get-tuple-element.127.refs_0_), channel_id=1, source_target_pairs={{0,1},{1,0},{2,3},{3,2},{4,5},{5,4},{6,7},{7,6},{8,9},{9,8},{10,11... | collective-permute-start | bytes 196616 | tf_op jit(solution)/shard_map/ppermute | solution.py:397
  57.2 1.4 %collective-permute-start.37 = (bf16[64,512]{1,0:T(8,128)(2,1)S(1)}, bf16[64,512]{1,0:T(8,128)(2,1)S(1)}, u32[]{:S(2)}, u32[]{:S(2)}) collective-permute-start(bf16[64,512]{1,0:T(8,128)(2,1)S(1)} %collective-permute-done.35.refs_1_), channel_id=1, source_target_pairs={{0,1},{1,0},{2,3},{3,2},{4,5},{5,4},{6,7},{7,6},{8,9},{9,8},{10,11... | collective-permute-start | bytes 196616 | tf_op jit(solution)/shard_map/ppermute | solution.py:397
  59.4 7.6 %collective-permute-start.38 = (bf16[96,512]{1,0:T(8,128)(2,1)S(1)}, bf16[96,512]{1,0:T(8,128)(2,1)S(1)}, u32[]{:S(2)}, u32[]{:S(2)}) collective-permute-start(bf16[96,512]{1,0:T(8,128)(2,1)S(1)} %get-tuple-element.144), channel_id=1, source_target_pairs={{0,6},{1,7},{2,4},{3,5},{4,2},{5,3},{6,0},{7,1},{8,14},{9,15},{10,... | collective-permute-start | bytes 294920 | tf_op jit(solution)/shard_map/ppermute | solution.py:381
  61.7 9.4 %collective-permute-start.39 = (bf16[96,512]{1,0:T(8,128)(2,1)S(1)}, bf16[96,512]{1,0:T(8,128)(2,1)S(1)}, u32[]{:S(2)}, u32[]{:S(2)}) collective-permute-start(bf16[96,512]{1,0:T(8,128)(2,1)S(1)} %get-tuple-element.145), channel_id=1, source_target_pairs={{0,4},{1,5},{2,6},{3,7},{4,0},{5,1},{6,2},{7,3},{8,12},{9,13},{10,... | collective-permute-start | bytes 294920 | tf_op jit(solution)/shard_map/ppermute | solution.py:381
  61.8 9.3 %collective-permute-start.40 = (bf16[96,512]{1,0:T(8,128)(2,1)S(1)}, bf16[96,512]{1,0:T(8,128)(2,1)S(1)}, u32[]{:S(2)}, u32[]{:S(2)}) collective-permute-start(bf16[96,512]{1,0:T(8,128)(2,1)S(1)} %get-tuple-element.146), channel_id=1, source_target_pairs={{0,2},{1,3},{2,0},{3,1},{4,6},{5,7},{6,4},{7,5},{8,10},{9,11},{10,... | collective-permute-start | bytes 294920 | tf_op jit(solution)/shard_map/ppermute | solution.py:381
  (1 other events, 1.0 us)

commit v13 on v12

--- a/solution.py
+++ b/solution.py
@@ -77,14 +77,17 @@
     return up_pre, silu, slope, curvature, mixed, down_back, back_slope, gate_back, up_back
 
 
-def apply_forward(f1t, f3t, f2t, queries, weighted):
+def apply_gate_and_up(f1t, f3t, queries):
     q_gate, q_up = nt(f1t, queries), nt(f3t, queries)
     silu, slope, _ = silu_parts(q_gate)
-    mixed = (silu * q_up).astype(BF16)
+    return (silu * q_up).astype(BF16), q_up * slope, silu
+
+
+def apply_down(f2t, mixed, weighted):
     output = nn(f2t, mixed)
     square = jnp.sum(output * output, axis=0, keepdims=True)
     dot = jnp.sum(weighted * output, axis=0, keepdims=True)
-    return output, mixed, q_up * slope, silu, jnp.concatenate([square, dot], axis=0)
+    return output, jnp.concatenate([square, dot], axis=0)
 
 
 def apply_backward(f2t, sums, full_width, output, weighted, up_slope, silu):
@@ -283,15 +286,17 @@
             out[i * g : (i + 1) * g] = rows
 
 
-def apply_kernel(chips, folds, *refs):
-    halves, refs = refs[:12], refs[12:]
-    qo, qx, weighted, f1t, f3t, f2t, output, mixed, up_slope, silu, sums = refs
+def apply_first_kernel(chips, *refs):
+    halves, (qo, qx, f1t, f3t, mixed, up_slope, silu) = refs[:8], refs[8:]
     place_halves(chips, 1, halves[:4], f1t)
-    place_halves(chips, 1, halves[4:8], f3t)
-    place_halves(chips, folds, halves[8:], f2t)
-    output[...], mixed[...], up_slope[...], silu[...], sums[...] = apply_forward(
-        f1t[...], f3t[...], f2t[...], both(qo, qx), weighted[...]
-    )
+    place_halves(chips, 1, halves[4:], f3t)
+    mixed[...], up_slope[...], silu[...] = apply_gate_and_up(f1t[...], f3t[...], both(qo, qx))
+
+
+def apply_last_kernel(chips, folds, *refs):
+    halves, (mixed, weighted, f2t, output, sums) = refs[:4], refs[4:]
+    place_halves(chips, folds, halves, f2t)
+    output[...], sums[...] = apply_down(f2t[...], mixed[...], weighted[...])
 
 
 def back_kernel(chips, folds, heads, *refs):
@@ -536,12 +541,20 @@
         )
         moved.append(rows_moved)
         fast.append(rows)
-    f1t, f3t, f2t, output, q_mixed, q_slope, q_silu, part = call(
-        functools.partial(apply_kernel, chips, folds),
-        matrices + [((dh, n), F32), ((fh, n), BF16), hidden, hidden, ((2, n), F32)],
-        (*from_owners(fast, chips), query_input, query_other, weighted),
-        name="apply",
-        flops=3 * product,
+    arrived = from_owners(fast, chips)
+    f1t, f3t, q_mixed, q_slope, q_silu = call(
+        functools.partial(apply_first_kernel, chips),
+        matrices[:2] + [((fh, n), BF16), hidden, hidden],
+        (*arrived[:8], query_input, query_other),
+        name="apply_first",
+        flops=2 * product,
+    )
+    f2t, output, part = call(
+        functools.partial(apply_last_kernel, chips, folds),
+        matrices[2:] + [((dh, n), F32), ((2, n), F32)],
+        (*arrived[8:], q_mixed, weighted),
+        name="apply_last",
+        flops=product,
     )
     q_gate_back, q_up_back, *sums = call(
         functools.partial(back_kernel, chips, folds, heads),
@@ -635,7 +648,8 @@
     fast, moved = packed_owner_forward(prior, update, fh)
     blocks = gather_blocks(jnp.tile(fast, (chips, 1)), count)
     f1t, f3t, f2t = whole_matrices(*blocks, tok, count, fh)
-    output, q_mixed, q_slope, q_silu, part = apply_forward(f1t, f3t, f2t, queries, weighted)
+    q_mixed, q_slope, q_silu = apply_gate_and_up(f1t, f3t, queries)
+    output, part = apply_down(f2t, q_mixed, weighted)
     sums = lax.psum(part, "head")
     q_gate_back, q_up_back, out_back = apply_backward(
         f2t, sums, heads * dh, output, weighted, q_slope, q_silu

time: 72 us -> 72.3 us (level)
    ppermute x18, waiting for transfers between devices: 11.6 us -> 12.7 us  [to_chip(): return lax.ppermute(x, 'tok', chip_perm(chips * CORES, step))]
    pallas_call x21 -> x22, Pallas kernels: 9.49 us -> 9.49 us  [call(): pl.pallas_call(kernel, out_shape=[jax.ShapeDtypeStruct(s, t) for s, t in...]
  transfers between devices with their start and end apart: 41 -> 41, of which waited for: 22 -> 19; matrix products, arithmetic and copies ran while one was open for 2% -> 2% of each run, Pallas kernels for 9% -> 9%
where the time goes in v13:
time: 72.3 us; the launch traced here: 72.2 us
  starting transfers between devices  37.9 us (52%)
  waiting for transfers between devices  21.7 us (30%)
  Pallas kernels  9.49 us (13%)
  local copies, waits for them, and re-layouts  2.12 us (3%)
  between operations  0.9 us (1%)
    ppermute x18, starting transfers between devices, to_chip(): return lax.ppermute(x, 'tok', chip_perm(chips * CORES, step))  26.3 us
    ppermute x18, waiting for transfers between devices, to_chip(): return lax.ppermute(x, 'tok', chip_perm(chips * CORES, step))  12.7 us
    pallas_call x22, Pallas kernels, call(): pl.pallas_call(kernel, out_shape=[jax.ShapeDtypeStruct(s, t) for s, t in...  9.49 us
    ppermute x3, waiting for transfers between devices, exchange(): lax.ppermute(pieces[s], 'tok', chip_perm(count, s))  4.9 us
    ppermute x3, starting transfers between devices, exchange(): lax.ppermute(pieces[s], 'tok', chip_perm(count, s))  4.45 us
    ppermute x3, starting transfers between devices, head_parts(): lax.ppermute(part, 'head', [(h, partner(h, step, heads)) for h in range(h...  3.55 us
    ppermute x3, waiting for transfers between devices, head_parts(): lax.ppermute(part, 'head', [(h, partner(h, step, heads)) for h in range(h...  3.41 us
    unnamed x18, local copies, waits for them, and re-layouts  2.12 us
  transfers between devices with their start and end apart: 41, of which 19 were waited for; matrix products, arithmetic and copies ran while one was open for 2% of the time, Pallas kernels for 9%

profile of v13, /device:TPU:0, one launch (start us, length us, event | category | flops | bytes accessed | tf_op | source)
XLA Modules:
  0.0 72.2 jit_solution(15240256358769872221)
XLA Ops:
  0.6 0.5 collective-permute-start.1
  2.2 1.1 %copy.15 = bf16[1,512,256]{1,2,0:T(8,128)(2,1)S(1)} copy(bf16[1,512,256]{2,1,0:T(8,128)(2,1)} %param.15) | data formatting | bytes 524288 | tf_op args[6]
  3.6 0.7 %copy-done = bf16[256,512]{1,0:T(8,128)(2,1)S(1)} copy-done((bf16[256,512]{1,0:T(8,128)(2,1)S(1)}, bf16[256,512]{1,0:T(8,128)(2,1)}, u32[]{:S(2)}) %copy-start) | copy-done | bytes 262168
  4.4 1.2 %update.1 = (f32[64,512]{1,0:T(8,128)S(1)}, f32[64,512]{1,0:T(8,128)S(1)}, f32[64,512]{1,0:T(8,128)S(1)}, bf16[64,512]{1,0:T(8,128)(2,1)S(1)}, bf16[64,512]{1,0:T(8,128)(2,1)S(1)}, /*index=5*/bf16[64,512]{1,0:T(8,128)(2,1)S(1)}) custom-call(bf16[256,512]{1,0:T(8,128)(2,1)S(1)} %copy-done, bf16[256,512]{1,0:T(8,128)(2,1)S(1)} %collective-permute-done.kx.refs_9_.refs_5_, ...), custom_call_target="tpu_custom_call" | custom-call | flops 805306368 | bytes 1837056 | tf_op jit(solution)/shard_map/update/pallas_call | solution.py:368
  5.6 2.8 %collective-permute-start.9 = (bf16[64,512]{1,0:T(8,128)(2,1)S(1)}, bf16[64,512]{1,0:T(8,128)(2,1)S(1)}, u32[]{:S(2)}, u32[]{:S(2)}) collective-permute-start(bf16[64,512]{1,0:T(8,128)(2,1)S(1)} %get-tuple-element.88), channel_id=1, source_target_pairs={{0,2},{1,3},{2,0},{3,1},{4,6},{5,7},{6,4},{7,5},{8,10},{9,11},{10,... | collective-permute-start | bytes 196616 | tf_op jit(solution)/shard_map/ppermute | solution.py:391
  8.4 1.9 %collective-permute-start.7 = (bf16[64,512]{1,0:T(8,128)(2,1)S(1)}, bf16[64,512]{1,0:T(8,128)(2,1)S(1)}, u32[]{:S(2)}, u32[]{:S(2)}) collective-permute-start(bf16[64,512]{1,0:T(8,128)(2,1)S(1)} %get-tuple-element.84), channel_id=1, source_target_pairs={{0,2},{1,3},{2,0},{3,1},{4,6},{5,7},{6,4},{7,5},{8,10},{9,11},{10,... | collective-permute-start | bytes 196616 | tf_op jit(solution)/shard_map/ppermute | solution.py:391
  10.4 0.6 collective-permute-done.9.got
  11.0 3.0 %collective-permute-start.10 = (bf16[64,512]{1,0:T(8,128)(2,1)S(1)}, bf16[64,512]{1,0:T(8,128)(2,1)S(1)}, u32[]{:S(2)}, u32[]{:S(2)}) collective-permute-start(bf16[64,512]{1,0:T(8,128)(2,1)S(1)} %carry.8.refs_0_), channel_id=1, source_target_pairs={{0,4},{1,5},{2,6},{3,7},{4,0},{5,1},{6,2},{7,3},{8,12},{9,13},{10,... | collective-permute-start | bytes 196616 | tf_op jit(solution)/shard_map/ppermute | solution.py:391
  14.0 1.9 %collective-permute-start.5 = (bf16[64,512]{1,0:T(8,128)(2,1)S(1)}, bf16[64,512]{1,0:T(8,128)(2,1)S(1)}, u32[]{:S(2)}, u32[]{:S(2)}) collective-permute-start(bf16[64,512]{1,0:T(8,128)(2,1)S(1)} %carry.6.refs_0_), channel_id=1, source_target_pairs={{0,4},{1,5},{2,6},{3,7},{4,0},{5,1},{6,2},{7,3},{8,12},{9,13},{10,... | collective-permute-start | bytes 196616 | tf_op jit(solution)/shard_map/ppermute | solution.py:391
  15.9 1.3 %collective-permute-start.8 = (bf16[64,512]{1,0:T(8,128)(2,1)S(1)}, bf16[64,512]{1,0:T(8,128)(2,1)S(1)}, u32[]{:S(2)}, u32[]{:S(2)}) collective-permute-start(bf16[64,512]{1,0:T(8,128)(2,1)S(1)} %carry.7.refs_0_), channel_id=1, source_target_pairs={{0,4},{1,5},{2,6},{3,7},{4,0},{5,1},{6,2},{7,3},{8,12},{9,13},{10,... | collective-permute-start | bytes 196616 | tf_op jit(solution)/shard_map/ppermute | solution.py:391
  17.2 1.1 %saved.1 = (bf16[512,512]{1,0:T(8,128)(2,1)S(1)}, f32[256,512]{1,0:T(8,128)S(1)}, f32[256,512]{1,0:T(8,128)S(1)}, f32[256,512]{1,0:T(8,128)S(1)}, f32[256,512]{1...) custom-call(bf16[256,512]{1,0:T(8,128)(2,1)S(1)} %copy-done, ...), custom_call_target="tpu_custom_call" | custom-call | flops 402653184 | bytes 2363392 | tf_op jit(solution)/shard_map/saved/pallas_call | solution.py:368
  18.4 1.8 %collective-permute-start.16 = (bf16[64,512]{1,0:T(8,128)(2,1)S(1)}, bf16[64,512]{1,0:T(8,128)(2,1)S(1)}, u32[]{:S(2)}, u32[]{:S(2)}) collective-permute-start(bf16[64,512]{1,0:T(8,128)(2,1)S(1)} %get-tuple-element.93.refs_4_), channel_id=1, source_target_pairs={{0,2},{1,3},{2,0},{3,1},{4,6},{5,7},{6,4},{7,5},{8,10},{9,11},{10,... | collective-permute-start | bytes 196616 | tf_op jit(solution)/shard_map/ppermute | solution.py:391
  20.2 3.1 %collective-permute-done.8.refs_1_ = bf16[64,512]{1,0:T(8,128)(2,1)S(1)} collective-permute-done((bf16[64,512]{1,0:T(8,128)(2,1)S(1)}, bf16[64,512]{1,0:T(8,128)(2,1)S(1)}, u32[]{:S(2)}, u32[]{:S(2)}) %collective-permute-start.8) | collective-permute-done | bytes 65568 | tf_op jit(solution)/shard_map/ppermute | solution.py:391
  23.8 1.9 %collective-permute-start.6 = (bf16[64,512]{1,0:T(8,128)(2,1)S(1)}, bf16[64,512]{1,0:T(8,128)(2,1)S(1)}, u32[]{:S(2)}, u32[]{:S(2)}) collective-permute-start(bf16[64,512]{1,0:T(8,128)(2,1)S(1)} %get-tuple-element.90.refs_0_), channel_id=1, source_target_pairs={{0,2},{1,3},{2,0},{3,1},{4,6},{5,7},{6,4},{7,5},{8,10},{9,11},{10,... | collective-permute-start | bytes 196616 | tf_op jit(solution)/shard_map/ppermute | solution.py:391
  25.7 2.0 %collective-permute-done.11.refs_1_ = bf16[64,512]{1,0:T(8,128)(2,1)S(1)} collective-permute-done((bf16[64,512]{1,0:T(8,128)(2,1)S(1)}, bf16[64,512]{1,0:T(8,128)(2,1)S(1)}, u32[]{:S(2)}, u32[]{:S(2)}) %collective-permute-start.11) | collective-permute-done | bytes 65568 | tf_op jit(solution)/shard_map/ppermute | solution.py:391
  27.8 0.5 collective-permute-start.17
  29.5 0.5 apply_first.1
  30.4 2.9 %collective-permute-start.22 = (f32[2,512]{1,0:T(2,128)S(1)}, f32[2,512]{1,0:T(2,128)S(1)}, u32[]{:S(2)}, u32[]{:S(2)}) collective-permute-start(f32[2,512]{1,0:T(2,128)S(1)} %get-tuple-element.96.refs_0_), channel_id=1, source_target_pairs={{0,24},{8,16},{16,8},{24,0},{1,25},{9,17},{17,9},{25,1},{2,26},{10... | collective-permute-start | bytes 12296 | tf_op jit(solution)/shard_map/ppermute | solution.py:409
  33.2 0.5 collective-permute-start.21
  33.9 1.0 %collective-permute-done.22.refs_3_ = f32[2,512]{1,0:T(2,128)S(1)} collective-permute-done((f32[2,512]{1,0:T(2,128)S(1)}, f32[2,512]{1,0:T(2,128)S(1)}, u32[]{:S(2)}, u32[]{:S(2)}) %collective-permute-start.22) | collective-permute-done | bytes 4128 | tf_op jit(solution)/shard_map/ppermute | solution.py:409
  34.9 1.9 %collective-permute-done.21.refs_2_ = f32[2,512]{1,0:T(2,128)S(1)} collective-permute-done((f32[2,512]{1,0:T(2,128)S(1)}, f32[2,512]{1,0:T(2,128)S(1)}, u32[]{:S(2)}, u32[]{:S(2)}) %collective-permute-start.21) | collective-permute-done | bytes 4128 | tf_op jit(solution)/shard_map/ppermute | solution.py:409
  36.8 0.5 collective-permute-done.20.refs_1_
  37.3 0.9 %apply_back.1 = (bf16[256,256]{1,0:T(8,128)(2,1)S(1)}, bf16[256,256]{1,0:T(8,128)(2,1)S(1)}, f32[64,512]{1,0:T(8,128)S(1)}, f32[64,512]{1,0:T(8,128)S(1)}, f32[6...) custom-call(f32[2,512]{1,0:T(2,128)S(1)} %get-tuple-element.96.refs_0, ...), custom_call_target="tpu_custom_call" | custom-call | flops 536870912 | bytes 4210688 | tf_op jit(solution)/shard_map/apply_back/pallas_call | solution.py:368
  38.2 1.2 %collective-permute-start.25 = (bf16[64,512]{1,0:T(8,128)(2,1)S(1)}, bf16[64,512]{1,0:T(8,128)(2,1)S(1)}, u32[]{:S(2)}, u32[]{:S(2)}) collective-permute-start(bf16[64,512]{1,0:T(8,128)(2,1)S(1)} %get-tuple-element.112), channel_id=1, source_target_pairs={{0,2},{1,3},{2,0},{3,1},{4,6},{5,7},{6,4},{7,5},{8,10},{9,11},{10,... | collective-permute-start | bytes 196616 | tf_op jit(solution)/shard_map/ppermute | solution.py:391
  39.5 0.8 %collective-permute-start.23 = (bf16[64,512]{1,0:T(8,128)(2,1)S(1)}, bf16[64,512]{1,0:T(8,128)(2,1)S(1)}, u32[]{:S(2)}, u32[]{:S(2)}) collective-permute-start(bf16[64,512]{1,0:T(8,128)(2,1)S(1)} %get-tuple-element.108), channel_id=1, source_target_pairs={{0,2},{1,3},{2,0},{3,1},{4,6},{5,7},{6,4},{7,5},{8,10},{9,11},{10,... | collective-permute-start | bytes 196616 | tf_op jit(solution)/shard_map/ppermute | solution.py:391
  40.3 1.2 %collective-permute-start.27 = (bf16[64,512]{1,0:T(8,128)(2,1)S(1)}, bf16[64,512]{1,0:T(8,128)(2,1)S(1)}, u32[]{:S(2)}, u32[]{:S(2)}) collective-permute-start(bf16[64,512]{1,0:T(8,128)(2,1)S(1)} %get-tuple-element.116), channel_id=1, source_target_pairs={{0,2},{1,3},{2,0},{3,1},{4,6},{5,7},{6,4},{7,5},{8,10},{9,11},{10,... | collective-permute-start | bytes 196616 | tf_op jit(solution)/shard_map/ppermute | solution.py:391
  41.5 1.1 %collective-permute-done.25.got = bf16[64,512]{1,0:T(8,128)(2,1)S(1)} collective-permute-done((bf16[64,512]{1,0:T(8,128)(2,1)S(1)}, bf16[64,512]{1,0:T(8,128)(2,1)S(1)}, u32[]{:S(2)}, u32[]{:S(2)}) %collective-permute-start.25) | collective-permute-done | bytes 65568 | tf_op jit(solution)/shard_map/ppermute | solution.py:391
  42.6 3.1 %collective-permute-start.26 = (bf16[64,512]{1,0:T(8,128)(2,1)S(1)}, bf16[64,512]{1,0:T(8,128)(2,1)S(1)}, u32[]{:S(2)}, u32[]{:S(2)}) collective-permute-start(bf16[64,512]{1,0:T(8,128)(2,1)S(1)} %carry.10.refs_0_), channel_id=1, source_target_pairs={{0,4},{1,5},{2,6},{3,7},{4,0},{5,1},{6,2},{7,3},{8,12},{9,13},{10,... | collective-permute-start | bytes 196616 | tf_op jit(solution)/shard_map/ppermute | solution.py:391
  45.7 1.0 %collective-permute-start.24 = (bf16[64,512]{1,0:T(8,128)(2,1)S(1)}, bf16[64,512]{1,0:T(8,128)(2,1)S(1)}, u32[]{:S(2)}, u32[]{:S(2)}) collective-permute-start(bf16[64,512]{1,0:T(8,128)(2,1)S(1)} %carry.9.refs_0_), channel_id=1, source_target_pairs={{0,4},{1,5},{2,6},{3,7},{4,0},{5,1},{6,2},{7,3},{8,12},{9,13},{10,... | collective-permute-start | bytes 196616 | tf_op jit(solution)/shard_map/ppermute | solution.py:391
  46.7 2.1 %collective-permute-start.28 = (bf16[64,512]{1,0:T(8,128)(2,1)S(1)}, bf16[64,512]{1,0:T(8,128)(2,1)S(1)}, u32[]{:S(2)}, u32[]{:S(2)}) collective-permute-start(bf16[64,512]{1,0:T(8,128)(2,1)S(1)} %carry.11.refs_0_), channel_id=1, source_target_pairs={{0,4},{1,5},{2,6},{3,7},{4,0},{5,1},{6,2},{7,3},{8,12},{9,13},{10,... | collective-permute-start | bytes 196616 | tf_op jit(solution)/shard_map/ppermute | solution.py:391
  48.8 1.6 %collective-permute-done.26.refs_1_ = bf16[64,512]{1,0:T(8,128)(2,1)S(1)} collective-permute-done((bf16[64,512]{1,0:T(8,128)(2,1)S(1)}, bf16[64,512]{1,0:T(8,128)(2,1)S(1)}, u32[]{:S(2)}, u32[]{:S(2)}) %collective-permute-start.26) | collective-permute-done | bytes 65568 | tf_op jit(solution)/shard_map/ppermute | solution.py:391
  50.6 1.1 %collective-permute-done.24.refs_1_ = bf16[64,512]{1,0:T(8,128)(2,1)S(1)} collective-permute-done((bf16[64,512]{1,0:T(8,128)(2,1)S(1)}, bf16[64,512]{1,0:T(8,128)(2,1)S(1)}, u32[]{:S(2)}, u32[]{:S(2)}) %collective-permute-start.24) | collective-permute-done | bytes 65568 | tf_op jit(solution)/shard_map/ppermute | solution.py:391
  51.8 1.0 %collective-permute-start.29 = (bf16[64,512]{1,0:T(8,128)(2,1)S(1)}, bf16[64,512]{1,0:T(8,128)(2,1)S(1)}, u32[]{:S(2)}, u32[]{:S(2)}) collective-permute-start(bf16[64,512]{1,0:T(8,128)(2,1)S(1)} %get-tuple-element.119.refs_0_), channel_id=1, source_target_pairs={{0,2},{1,3},{2,0},{3,1},{4,6},{5,7},{6,4},{7,5},{8,10},{9,11},{10,... | collective-permute-start | bytes 196616 | tf_op jit(solution)/shard_map/ppermute | solution.py:391
  53.3 0.9 %collective-permute-start.35 = (bf16[64,512]{1,0:T(8,128)(2,1)S(1)}, bf16[64,512]{1,0:T(8,128)(2,1)S(1)}, u32[]{:S(2)}, u32[]{:S(2)}) collective-permute-start(bf16[64,512]{1,0:T(8,128)(2,1)S(1)} %get-tuple-element.127.refs_0_), channel_id=1, source_target_pairs={{0,2},{1,3},{2,0},{3,1},{4,6},{5,7},{6,4},{7,5},{8,10},{9,11},{10,... | collective-permute-start | bytes 196616 | tf_op jit(solution)/shard_map/ppermute | solution.py:391
  54.2 0.6 collective-permute-done.32.refs_5_
  54.8 1.4 %collective-permute-done.29.refs_1_ = bf16[64,512]{1,0:T(8,128)(2,1)S(1)} collective-permute-done((bf16[64,512]{1,0:T(8,128)(2,1)S(1)}, bf16[64,512]{1,0:T(8,128)(2,1)S(1)}, u32[]{:S(2)}, u32[]{:S(2)}) %collective-permute-start.29) | collective-permute-done | bytes 65568 | tf_op jit(solution)/shard_map/ppermute | solution.py:391
  56.2 0.5 collective-permute-start.33
  56.7 0.9 %collective-permute-done.35.refs_1_ = bf16[64,512]{1,0:T(8,128)(2,1)S(1)} collective-permute-done((bf16[64,512]{1,0:T(8,128)(2,1)S(1)}, bf16[64,512]{1,0:T(8,128)(2,1)S(1)}, u32[]{:S(2)}, u32[]{:S(2)}) %collective-permute-start.35) | collective-permute-done | bytes 65568 | tf_op jit(solution)/shard_map/ppermute | solution.py:391
  57.6 0.5 collective-permute-start.37
  58.1 0.8 %second_first.1 = (bf16[256,512]{1,0:T(8,128)(2,1)S(1)}, bf16[256,512]{1,0:T(8,128)(2,1)S(1)}, bf16[256,256]{1,0:T(8,128)(2,1)S(1)}, f32[128,512]{1,0:T(8,128)S(...) custom-call(bf16[64,512]{1,0:T(8,128)(2,1)S(1)} %get-tuple-element.119.refs_0_, ...), custom_call_target="tpu_custom_call" | custom-call | flops 402653184 | bytes 3670016 | tf_op jit(solution)/shard_map/second_first/pallas_call | solution.py:368
  59.0 0.7 %second_last.1 = (bf16[512,256]{1,0:T(8,128)(2,1)S(1)}, bf16[256,256]{1,0:T(8,128)(2,1)S(1)}, bf16[256,256]{1,0:T(8,128)(2,1)S(1)}, f32[96,512]{1,0:T(8,128)S(1)...) custom-call(bf16[64,512]{1,0:T(8,128)(2,1)S(1)} %get-tuple-element.127.refs_0_, ...), custom_call_target="tpu_custom_call" | custom-call | flops 402653184 | bytes 3670016 | tf_op jit(solution)/shard_map/second_last/pallas_call | solution.py:368
  59.7 2.3 %collective-permute-start.38 = (bf16[96,512]{1,0:T(8,128)(2,1)S(1)}, bf16[96,512]{1,0:T(8,128)(2,1)S(1)}, u32[]{:S(2)}, u32[]{:S(2)}) collective-permute-start(bf16[96,512]{1,0:T(8,128)(2,1)S(1)} %get-tuple-element.144), channel_id=1, source_target_pairs={{0,6},{1,7},{2,4},{3,5},{4,2},{5,3},{6,0},{7,1},{8,14},{9,15},{10,... | collective-permute-start | bytes 294920 | tf_op jit(solution)/shard_map/ppermute | solution.py:386
  62.1 2.1 %collective-permute-start.40 = (bf16[96,512]{1,0:T(8,128)(2,1)S(1)}, bf16[96,512]{1,0:T(8,128)(2,1)S(1)}, u32[]{:S(2)}, u32[]{:S(2)}) collective-permute-start(bf16[96,512]{1,0:T(8,128)(2,1)S(1)} %get-tuple-element.146), channel_id=1, source_target_pairs={{0,2},{1,3},{2,0},{3,1},{4,6},{5,7},{6,4},{7,5},{8,10},{9,11},{10,... | collective-permute-start | bytes 294920 | tf_op jit(solution)/shard_map/ppermute | solution.py:386
  64.2 1.0 %query_grad.1 = bf16[256,512]{1,0:T(8,128)(2,1)} custom-call(bf16[256,256]{1,0:T(8,128)(2,1)S(1)} %get-tuple-element.101.gate_back, bf16[256,256]{1,0:T(8,128)(2,1)S(1)} %get-tuple-element.102.up_back, bf16[256,512]{1,0:T(8,128)(2,1)S(1)} %get-tuple-element.103.f1t, bf16[256,512]{1,0:T(8,128)(2,1)S(1)} %get-tuple-element.104.f3t), custom_call_target="tpu_custom_call" | custom-call | flops 134217728 | bytes 786432 | tf_op jit(solution)/shard_map/query_grad/pallas_call | solution.py:368
  65.2 1.4 %token_grads.1 = (bf16[256,512]{1,0:T(8,128)(2,1)}, bf16[256,512]{1,0:T(8,128)(2,1)}) custom-call(f32[1,256]{1,0:T(1,128)S(1)} %bitcast.30, bf16[256,256]{1,0:T(8,128)(2,1)S(1)} %get-tuple-element.105.refs_1_, bf16[256,256]{1,0:T(8,128)(2,1)S(1)} %get-tuple-element.126.refs_2_, bf16[256,256]{1,0:T(8,128)(2,1)S(1)} %get-tuple-element.131.refs_3_, ...), custom_call_target="tpu_custom_call" | custom-call | flops 402653184 | bytes 2360320 | tf_op jit(solution)/shard_map/token_grads/pallas_call | solution.py:368
  66.6 0.7 %collective-permute-done.38.refs_4_ = bf16[96,512]{1,0:T(8,128)(2,1)S(1)} collective-permute-done((bf16[96,512]{1,0:T(8,128)(2,1)S(1)}, bf16[96,512]{1,0:T(8,128)(2,1)S(1)}, u32[]{:S(2)}, u32[]{:S(2)}) %collective-permute-start.38) | collective-permute-done | bytes 98336 | tf_op jit(solution)/shard_map/ppermute | solution.py:386
  67.3 4.2 %collective-permute-done.39.refs_5_ = bf16[96,512]{1,0:T(8,128)(2,1)S(1)} collective-permute-done((bf16[96,512]{1,0:T(8,128)(2,1)S(1)}, bf16[96,512]{1,0:T(8,128)(2,1)S(1)}, u32[]{:S(2)}, u32[]{:S(2)}) %collective-permute-start.39) | collective-permute-done | bytes 98336 | tf_op jit(solution)/shard_map/ppermute | solution.py:386
  71.5 0.7 owner_result.1
  (74 shorter events, 4.9 us)
Async XLA Ops:
  0.6 1.0 %copy-start.5 = (f32[256,1]{0,1:T(1,128)S(1)}, f32[256,1]{0,1:T(1,128)}, u32[]{:S(2)}) copy-start(f32[256,1]{0,1:T(1,128)} %param.13) | copy-start | bytes 3076
  0.6 2.9 %collective-permute-start.1 = (bf16[256,512]{1,0:T(8,128)(2,1)}, bf16[256,512]{1,0:T(8,128)(2,1)S(1)}, u32[]{:S(2)}, u32[]{:S(2)}) collective-permute-start(bf16[256,512]{1,0:T(8,128)(2,1)} %vo.3), channel_id=1, source_target_pairs={{0,1},{1,0},{2,3},{3,2},{4,5},{5,4},{6,7},{7,6},{8,9},{9,8},{10,11... | collective-permute-start | bytes 786440 | tf_op jit(solution)/shard_map/ppermute | solution.py:507
  1.2 2.4 %collective-permute-start = (bf16[256,512]{1,0:T(8,128)(2,1)}, bf16[256,512]{1,0:T(8,128)(2,1)S(1)}, u32[]{:S(2)}, u32[]{:S(2)}) collective-permute-start(bf16[256,512]{1,0:T(8,128)(2,1)} %refs_4_.1), channel_id=1, source_target_pairs={{0,1},{1,0},{2,3},{3,2},{4,5},{5,4},{6,7},{7,6},{8,9},{9,8},{10,11... | collective-permute-start | bytes 786440 | tf_op jit(solution)/shard_map/ppermute | solution.py:507
  1.2 16.0 %collective-permute-start.3 = (bf16[256,512]{1,0:T(8,128)(2,1)}, bf16[256,512]{1,0:T(8,128)(2,1)S(1)}, u32[]{:S(2)}, u32[]{:S(2)}) collective-permute-start(bf16[256,512]{1,0:T(8,128)(2,1)} %go.1), channel_id=1, source_target_pairs={{0,1},{1,0},{2,3},{3,2},{4,5},{5,4},{6,7},{7,6},{8,9},{9,8},{10,11... | collective-permute-start | bytes 786440 | tf_op jit(solution)/shard_map/ppermute | solution.py:507
  1.7 1.7 %copy-start.7 = (bf16[1,512,256]{2,1,0:T(8,128)(2,1)S(1)}, bf16[1,512,256]{2,1,0:T(8,128)(2,1)}, u32[]{:S(2)}) copy-start(bf16[1,512,256]{2,1,0:T(8,128)(2,1)} %param.16) | copy-start | bytes 786436
  1.7 1.8 %collective-permute-start.2 = (f32[1,256]{1,0:T(1,128)S(1)}, f32[1,256]{1,0:T(1,128)S(1)}, u32[]{:S(2)}, u32[]{:S(2)}) collective-permute-start(f32[1,256]{1,0:T(1,128)S(1)} %bitcast.27), channel_id=1, source_target_pairs={{0,1},{1,0},{2,3},{3,2},{4,5},{5,4},{6,7},{7,6},{8,9},{9,8},{10,11... | collective-permute-start | bytes 3080 | tf_op jit(solution)/shard_map/ppermute | solution.py:507
  1.8 26.5 %collective-permute-start.19 = (bf16[256,512]{1,0:T(8,128)(2,1)}, bf16[256,512]{1,0:T(8,128)(2,1)S(1)}, u32[]{:S(2)}, u32[]{:S(2)}) collective-permute-start(bf16[256,512]{1,0:T(8,128)(2,1)} %refs_10_.1), channel_id=1, source_target_pairs={{0,1},{1,0},{2,3},{3,2},{4,5},{5,4},{6,7},{7,6},{8,9},{9,8},{10,11... | collective-permute-start | bytes 786440 | tf_op jit(solution)/shard_map/ppermute | solution.py:507
  2.2 1.4 %copy-start.3 = (bf16[256,512]{1,0:T(8,128)(2,1)S(1)}, bf16[256,512]{1,0:T(8,128)(2,1)}, u32[]{:S(2)}) copy-start(bf16[256,512]{1,0:T(8,128)(2,1)} %vo.3) | copy-start | bytes 786436
  3.4 1.0 %copy-start.1 = (bf16[1,256,512]{2,1,0:T(8,128)(2,1)S(1)}, bf16[1,256,512]{2,1,0:T(8,128)(2,1)}, u32[]{:S(2)}) copy-start(bf16[1,256,512]{2,1,0:T(8,128)(2,1)} %param.17) | copy-start | bytes 786436
  5.6 5.4 %collective-permute-start.9 = (bf16[64,512]{1,0:T(8,128)(2,1)S(1)}, bf16[64,512]{1,0:T(8,128)(2,1)S(1)}, u32[]{:S(2)}, u32[]{:S(2)}) collective-permute-start(bf16[64,512]{1,0:T(8,128)(2,1)S(1)} %get-tuple-element.88), channel_id=1, source_target_pairs={{0,2},{1,3},{2,0},{3,1},{4,6},{5,7},{6,4},{7,5},{8,10},{9,11},{10,... | collective-permute-start | bytes 196616 | tf_op jit(solution)/shard_map/ppermute | solution.py:391
  8.3 5.6 %collective-permute-start.4 = (bf16[64,512]{1,0:T(8,128)(2,1)S(1)}, bf16[64,512]{1,0:T(8,128)(2,1)S(1)}, u32[]{:S(2)}, u32[]{:S(2)}) collective-permute-start(bf16[64,512]{1,0:T(8,128)(2,1)S(1)} %get-tuple-element.80), channel_id=1, source_target_pairs={{0,2},{1,3},{2,0},{3,1},{4,6},{5,7},{6,4},{7,5},{8,10},{9,11},{10,... | collective-permute-start | bytes 196616 | tf_op jit(solution)/shard_map/ppermute | solution.py:391
  8.4 7.5 %collective-permute-start.7 = (bf16[64,512]{1,0:T(8,128)(2,1)S(1)}, bf16[64,512]{1,0:T(8,128)(2,1)S(1)}, u32[]{:S(2)}, u32[]{:S(2)}) collective-permute-start(bf16[64,512]{1,0:T(8,128)(2,1)S(1)} %get-tuple-element.84), channel_id=1, source_target_pairs={{0,2},{1,3},{2,0},{3,1},{4,6},{5,7},{6,4},{7,5},{8,10},{9,11},{10,... | collective-permute-start | bytes 196616 | tf_op jit(solution)/shard_map/ppermute | solution.py:391
  11.0 7.3 %collective-permute-start.10 = (bf16[64,512]{1,0:T(8,128)(2,1)S(1)}, bf16[64,512]{1,0:T(8,128)(2,1)S(1)}, u32[]{:S(2)}, u32[]{:S(2)}) collective-permute-start(bf16[64,512]{1,0:T(8,128)(2,1)S(1)} %carry.8.refs_0_), channel_id=1, source_target_pairs={{0,4},{1,5},{2,6},{3,7},{4,0},{5,1},{6,2},{7,3},{8,12},{9,13},{10,... | collective-permute-start | bytes 196616 | tf_op jit(solution)/shard_map/ppermute | solution.py:391
  14.0 3.2 %copy-start.4 = (bf16[256,512]{1,0:T(8,128)(2,1)S(1)}, bf16[256,512]{1,0:T(8,128)(2,1)}, u32[]{:S(2)}) copy-start(bf16[256,512]{1,0:T(8,128)(2,1)} %go.1) | copy-start | bytes 786436
  14.0 9.7 %collective-permute-start.5 = (bf16[64,512]{1,0:T(8,128)(2,1)S(1)}, bf16[64,512]{1,0:T(8,128)(2,1)S(1)}, u32[]{:S(2)}, u32[]{:S(2)}) collective-permute-start(bf16[64,512]{1,0:T(8,128)(2,1)S(1)} %carry.6.refs_0_), channel_id=1, source_target_pairs={{0,4},{1,5},{2,6},{3,7},{4,0},{5,1},{6,2},{7,3},{8,12},{9,13},{10,... | collective-permute-start | bytes 196616 | tf_op jit(solution)/shard_map/ppermute | solution.py:391
  15.9 1.3 %copy-start.6 = (f32[512]{0:T(512)S(1)}, f32[512]{0:T(512)}, u32[]{:S(2)}) copy-start(f32[512]{0:T(512)} %param.14) | copy-start | bytes 6148
  15.9 7.4 %collective-permute-start.8 = (bf16[64,512]{1,0:T(8,128)(2,1)S(1)}, bf16[64,512]{1,0:T(8,128)(2,1)S(1)}, u32[]{:S(2)}, u32[]{:S(2)}) collective-permute-start(bf16[64,512]{1,0:T(8,128)(2,1)S(1)} %carry.7.refs_0_), channel_id=1, source_target_pairs={{0,4},{1,5},{2,6},{3,7},{4,0},{5,1},{6,2},{7,3},{8,12},{9,13},{10,... | collective-permute-start | bytes 196616 | tf_op jit(solution)/shard_map/ppermute | solution.py:391
  18.4 7.3 %collective-permute-start.16 = (bf16[64,512]{1,0:T(8,128)(2,1)S(1)}, bf16[64,512]{1,0:T(8,128)(2,1)S(1)}, u32[]{:S(2)}, u32[]{:S(2)}) collective-permute-start(bf16[64,512]{1,0:T(8,128)(2,1)S(1)} %get-tuple-element.93.refs_4_), channel_id=1, source_target_pairs={{0,2},{1,3},{2,0},{3,1},{4,6},{5,7},{6,4},{7,5},{8,10},{9,11},{10,... | collective-permute-start | bytes 196616 | tf_op jit(solution)/shard_map/ppermute | solution.py:391
  23.3 6.2 %copy-start.2 = (bf16[256,512]{1,0:T(8,128)(2,1)S(1)}, bf16[256,512]{1,0:T(8,128)(2,1)}, u32[]{:S(2)}) copy-start(bf16[256,512]{1,0:T(8,128)(2,1)} %refs_10_.1) | copy-start | bytes 786436
  23.4 4.3 %collective-permute-start.11 = (bf16[64,512]{1,0:T(8,128)(2,1)S(1)}, bf16[64,512]{1,0:T(8,128)(2,1)S(1)}, u32[]{:S(2)}, u32[]{:S(2)}) collective-permute-start(bf16[64,512]{1,0:T(8,128)(2,1)S(1)} %get-tuple-element.92.refs_0_), channel_id=1, source_target_pairs={{0,2},{1,3},{2,0},{3,1},{4,6},{5,7},{6,4},{7,5},{8,10},{9,11},{10,... | collective-permute-start | bytes 196616 | tf_op jit(solution)/shard_map/ppermute | solution.py:391
  23.8 4.6 %collective-permute-start.6 = (bf16[64,512]{1,0:T(8,128)(2,1)S(1)}, bf16[64,512]{1,0:T(8,128)(2,1)S(1)}, u32[]{:S(2)}, u32[]{:S(2)}) collective-permute-start(bf16[64,512]{1,0:T(8,128)(2,1)S(1)} %get-tuple-element.90.refs_0_), channel_id=1, source_target_pairs={{0,2},{1,3},{2,0},{3,1},{4,6},{5,7},{6,4},{7,5},{8,10},{9,11},{10,... | collective-permute-start | bytes 196616 | tf_op jit(solution)/shard_map/ppermute | solution.py:391
  25.7 3.1 %collective-permute-start.18 = (bf16[64,512]{1,0:T(8,128)(2,1)S(1)}, bf16[64,512]{1,0:T(8,128)(2,1)S(1)}, u32[]{:S(2)}, u32[]{:S(2)}) collective-permute-start(bf16[64,512]{1,0:T(8,128)(2,1)S(1)} %collective-permute-done.16.refs_5_), channel_id=1, source_target_pairs={{0,1},{1,0},{2,3},{3,2},{4,5},{5,4},{6,7},{7,6},{8,9},{9,8},{10,11... | collective-permute-start | bytes 196616 | tf_op jit(solution)/shard_map/ppermute | solution.py:402
  27.8 1.3 %collective-permute-start.14 = (bf16[64,512]{1,0:T(8,128)(2,1)S(1)}, bf16[64,512]{1,0:T(8,128)(2,1)S(1)}, u32[]{:S(2)}, u32[]{:S(2)}) collective-permute-start(bf16[64,512]{1,0:T(8,128)(2,1)S(1)} %get-tuple-element.92.refs_0_), channel_id=1, source_target_pairs={{0,1},{1,0},{2,3},{3,2},{4,5},{5,4},{6,7},{7,6},{8,9},{9,8},{10,11... | collective-permute-start | bytes 196616 | tf_op jit(solution)/shard_map/ppermute | solution.py:402
  27.8 1.4 %collective-permute-start.17 = (bf16[64,512]{1,0:T(8,128)(2,1)S(1)}, bf16[64,512]{1,0:T(8,128)(2,1)S(1)}, u32[]{:S(2)}, u32[]{:S(2)}) collective-permute-start(bf16[64,512]{1,0:T(8,128)(2,1)S(1)} %get-tuple-element.93.refs_4_), channel_id=1, source_target_pairs={{0,1},{1,0},{2,3},{3,2},{4,5},{5,4},{6,7},{7,6},{8,9},{9,8},{10,11... | collective-permute-start | bytes 196616 | tf_op jit(solution)/shard_map/ppermute | solution.py:402
  28.3 1.3 %collective-permute-start.15 = (bf16[64,512]{1,0:T(8,128)(2,1)S(1)}, bf16[64,512]{1,0:T(8,128)(2,1)S(1)}, u32[]{:S(2)}, u32[]{:S(2)}) collective-permute-start(bf16[64,512]{1,0:T(8,128)(2,1)S(1)} %collective-permute-done.11.refs_1_), channel_id=1, source_target_pairs={{0,1},{1,0},{2,3},{3,2},{4,5},{5,4},{6,7},{7,6},{8,9},{9,8},{10,11... | collective-permute-start | bytes 196616 | tf_op jit(solution)/shard_map/ppermute | solution.py:402
  28.5 1.6 %collective-permute-start.12 = (bf16[64,512]{1,0:T(8,128)(2,1)S(1)}, bf16[64,512]{1,0:T(8,128)(2,1)S(1)}, u32[]{:S(2)}, u32[]{:S(2)}) collective-permute-start(bf16[64,512]{1,0:T(8,128)(2,1)S(1)} %get-tuple-element.90.refs_0_), channel_id=1, source_target_pairs={{0,1},{1,0},{2,3},{3,2},{4,5},{5,4},{6,7},{7,6},{8,9},{9,8},{10,11... | collective-permute-start | bytes 196616 | tf_op jit(solution)/shard_map/ppermute | solution.py:402
  28.8 1.3 %collective-permute-start.13 = (bf16[64,512]{1,0:T(8,128)(2,1)S(1)}, bf16[64,512]{1,0:T(8,128)(2,1)S(1)}, u32[]{:S(2)}, u32[]{:S(2)}) collective-permute-start(bf16[64,512]{1,0:T(8,128)(2,1)S(1)} %collective-permute-done.6.refs_1_), channel_id=1, source_target_pairs={{0,1},{1,0},{2,3},{3,2},{4,5},{5,4},{6,7},{7,6},{8,9},{9,8},{10,11... | collective-permute-start | bytes 196616 | tf_op jit(solution)/shard_map/ppermute | solution.py:402
  30.4 4.6 %collective-permute-start.22 = (f32[2,512]{1,0:T(2,128)S(1)}, f32[2,512]{1,0:T(2,128)S(1)}, u32[]{:S(2)}, u32[]{:S(2)}) collective-permute-start(f32[2,512]{1,0:T(2,128)S(1)} %get-tuple-element.96.refs_0_), channel_id=1, source_target_pairs={{0,24},{8,16},{16,8},{24,0},{1,25},{9,17},{17,9},{25,1},{2,26},{10... | collective-permute-start | bytes 12296 | tf_op jit(solution)/shard_map/ppermute | solution.py:409
  33.2 3.6 %collective-permute-start.21 = (f32[2,512]{1,0:T(2,128)S(1)}, f32[2,512]{1,0:T(2,128)S(1)}, u32[]{:S(2)}, u32[]{:S(2)}) collective-permute-start(f32[2,512]{1,0:T(2,128)S(1)} %get-tuple-element.96.refs_0_), channel_id=1, source_target_pairs={{0,16},{8,24},{16,0},{24,8},{1,17},{9,25},{17,1},{25,9},{2,18},{10... | collective-permute-start | bytes 12296 | tf_op jit(solution)/shard_map/ppermute | solution.py:409
  33.7 3.6 %collective-permute-start.20 = (f32[2,512]{1,0:T(2,128)S(1)}, f32[2,512]{1,0:T(2,128)S(1)}, u32[]{:S(2)}, u32[]{:S(2)}) collective-permute-start(f32[2,512]{1,0:T(2,128)S(1)} %get-tuple-element.96.refs_0_), channel_id=1, source_target_pairs={{0,8},{8,0},{16,24},{24,16},{1,9},{9,1},{17,25},{25,17},{2,10},{10... | collective-permute-start | bytes 12296 | tf_op jit(solution)/shard_map/ppermute | solution.py:409
  38.2 4.3 %collective-permute-start.25 = (bf16[64,512]{1,0:T(8,128)(2,1)S(1)}, bf16[64,512]{1,0:T(8,128)(2,1)S(1)}, u32[]{:S(2)}, u32[]{:S(2)}) collective-permute-start(bf16[64,512]{1,0:T(8,128)(2,1)S(1)} %get-tuple-element.112), channel_id=1, source_target_pairs={{0,2},{1,3},{2,0},{3,1},{4,6},{5,7},{6,4},{7,5},{8,10},{9,11},{10,... | collective-permute-start | bytes 196616 | tf_op jit(solution)/shard_map/ppermute | solution.py:391
  39.5 6.2 %collective-permute-start.23 = (bf16[64,512]{1,0:T(8,128)(2,1)S(1)}, bf16[64,512]{1,0:T(8,128)(2,1)S(1)}, u32[]{:S(2)}, u32[]{:S(2)}) collective-permute-start(bf16[64,512]{1,0:T(8,128)(2,1)S(1)} %get-tuple-element.108), channel_id=1, source_target_pairs={{0,2},{1,3},{2,0},{3,1},{4,6},{5,7},{6,4},{7,5},{8,10},{9,11},{10,... | collective-permute-start | bytes 196616 | tf_op jit(solution)/shard_map/ppermute | solution.py:391
  40.3 6.4 %collective-permute-start.27 = (bf16[64,512]{1,0:T(8,128)(2,1)S(1)}, bf16[64,512]{1,0:T(8,128)(2,1)S(1)}, u32[]{:S(2)}, u32[]{:S(2)}) collective-permute-start(bf16[64,512]{1,0:T(8,128)(2,1)S(1)} %get-tuple-element.116), channel_id=1, source_target_pairs={{0,2},{1,3},{2,0},{3,1},{4,6},{5,7},{6,4},{7,5},{8,10},{9,11},{10,... | collective-permute-start | bytes 196616 | tf_op jit(solution)/shard_map/ppermute | solution.py:391
  42.6 7.8 %collective-permute-start.26 = (bf16[64,512]{1,0:T(8,128)(2,1)S(1)}, bf16[64,512]{1,0:T(8,128)(2,1)S(1)}, u32[]{:S(2)}, u32[]{:S(2)}) collective-permute-start(bf16[64,512]{1,0:T(8,128)(2,1)S(1)} %carry.10.refs_0_), channel_id=1, source_target_pairs={{0,4},{1,5},{2,6},{3,7},{4,0},{5,1},{6,2},{7,3},{8,12},{9,13},{10,... | collective-permute-start | bytes 196616 | tf_op jit(solution)/shard_map/ppermute | solution.py:391
  45.7 6.0 %collective-permute-start.24 = (bf16[64,512]{1,0:T(8,128)(2,1)S(1)}, bf16[64,512]{1,0:T(8,128)(2,1)S(1)}, u32[]{:S(2)}, u32[]{:S(2)}) collective-permute-start(bf16[64,512]{1,0:T(8,128)(2,1)S(1)} %carry.9.refs_0_), channel_id=1, source_target_pairs={{0,4},{1,5},{2,6},{3,7},{4,0},{5,1},{6,2},{7,3},{8,12},{9,13},{10,... | collective-permute-start | bytes 196616 | tf_op jit(solution)/shard_map/ppermute | solution.py:391
  46.7 6.4 %collective-permute-start.28 = (bf16[64,512]{1,0:T(8,128)(2,1)S(1)}, bf16[64,512]{1,0:T(8,128)(2,1)S(1)}, u32[]{:S(2)}, u32[]{:S(2)}) collective-permute-start(bf16[64,512]{1,0:T(8,128)(2,1)S(1)} %carry.11.refs_0_), channel_id=1, source_target_pairs={{0,4},{1,5},{2,6},{3,7},{4,0},{5,1},{6,2},{7,3},{8,12},{9,13},{10,... | collective-permute-start | bytes 196616 | tf_op jit(solution)/shard_map/ppermute | solution.py:391
  50.5 4.3 %collective-permute-start.32 = (bf16[64,512]{1,0:T(8,128)(2,1)S(1)}, bf16[64,512]{1,0:T(8,128)(2,1)S(1)}, u32[]{:S(2)}, u32[]{:S(2)}) collective-permute-start(bf16[64,512]{1,0:T(8,128)(2,1)S(1)} %get-tuple-element.120.refs_4_), channel_id=1, source_target_pairs={{0,2},{1,3},{2,0},{3,1},{4,6},{5,7},{6,4},{7,5},{8,10},{9,11},{10,... | collective-permute-start | bytes 196616 | tf_op jit(solution)/shard_map/ppermute | solution.py:391
  51.8 4.3 %collective-permute-start.29 = (bf16[64,512]{1,0:T(8,128)(2,1)S(1)}, bf16[64,512]{1,0:T(8,128)(2,1)S(1)}, u32[]{:S(2)}, u32[]{:S(2)}) collective-permute-start(bf16[64,512]{1,0:T(8,128)(2,1)S(1)} %get-tuple-element.119.refs_0_), channel_id=1, source_target_pairs={{0,2},{1,3},{2,0},{3,1},{4,6},{5,7},{6,4},{7,5},{8,10},{9,11},{10,... | collective-permute-start | bytes 196616 | tf_op jit(solution)/shard_map/ppermute | solution.py:391
  53.3 4.3 %collective-permute-start.35 = (bf16[64,512]{1,0:T(8,128)(2,1)S(1)}, bf16[64,512]{1,0:T(8,128)(2,1)S(1)}, u32[]{:S(2)}, u32[]{:S(2)}) collective-permute-start(bf16[64,512]{1,0:T(8,128)(2,1)S(1)} %get-tuple-element.127.refs_0_), channel_id=1, source_target_pairs={{0,2},{1,3},{2,0},{3,1},{4,6},{5,7},{6,4},{7,5},{8,10},{9,11},{10,... | collective-permute-start | bytes 196616 | tf_op jit(solution)/shard_map/ppermute | solution.py:391
  54.8 2.8 %collective-permute-start.34 = (bf16[64,512]{1,0:T(8,128)(2,1)S(1)}, bf16[64,512]{1,0:T(8,128)(2,1)S(1)}, u32[]{:S(2)}, u32[]{:S(2)}) collective-permute-start(bf16[64,512]{1,0:T(8,128)(2,1)S(1)} %collective-permute-done.32.refs_5_), channel_id=1, source_target_pairs={{0,1},{1,0},{2,3},{3,2},{4,5},{5,4},{6,7},{7,6},{8,9},{9,8},{10,11... | collective-permute-start | bytes 196616 | tf_op jit(solution)/shard_map/ppermute | solution.py:402
  56.2 1.9 %collective-permute-start.30 = (bf16[64,512]{1,0:T(8,128)(2,1)S(1)}, bf16[64,512]{1,0:T(8,128)(2,1)S(1)}, u32[]{:S(2)}, u32[]{:S(2)}) collective-permute-start(bf16[64,512]{1,0:T(8,128)(2,1)S(1)} %get-tuple-element.119.refs_0_), channel_id=1, source_target_pairs={{0,1},{1,0},{2,3},{3,2},{4,5},{5,4},{6,7},{7,6},{8,9},{9,8},{10,11... | collective-permute-start | bytes 196616 | tf_op jit(solution)/shard_map/ppermute | solution.py:402
  56.2 1.9 %collective-permute-start.33 = (bf16[64,512]{1,0:T(8,128)(2,1)S(1)}, bf16[64,512]{1,0:T(8,128)(2,1)S(1)}, u32[]{:S(2)}, u32[]{:S(2)}) collective-permute-start(bf16[64,512]{1,0:T(8,128)(2,1)S(1)} %get-tuple-element.120.refs_4_), channel_id=1, source_target_pairs={{0,1},{1,0},{2,3},{3,2},{4,5},{5,4},{6,7},{7,6},{8,9},{9,8},{10,11... | collective-permute-start | bytes 196616 | tf_op jit(solution)/shard_map/ppermute | solution.py:402
  56.7 1.4 %collective-permute-start.31 = (bf16[64,512]{1,0:T(8,128)(2,1)S(1)}, bf16[64,512]{1,0:T(8,128)(2,1)S(1)}, u32[]{:S(2)}, u32[]{:S(2)}) collective-permute-start(bf16[64,512]{1,0:T(8,128)(2,1)S(1)} %collective-permute-done.29.refs_1_), channel_id=1, source_target_pairs={{0,1},{1,0},{2,3},{3,2},{4,5},{5,4},{6,7},{7,6},{8,9},{9,8},{10,11... | collective-permute-start | bytes 196616 | tf_op jit(solution)/shard_map/ppermute | solution.py:402
  57.6 1.3 %collective-permute-start.36 = (bf16[64,512]{1,0:T(8,128)(2,1)S(1)}, bf16[64,512]{1,0:T(8,128)(2,1)S(1)}, u32[]{:S(2)}, u32[]{:S(2)}) collective-permute-start(bf16[64,512]{1,0:T(8,128)(2,1)S(1)} %get-tuple-element.127.refs_0_), channel_id=1, source_target_pairs={{0,1},{1,0},{2,3},{3,2},{4,5},{5,4},{6,7},{7,6},{8,9},{9,8},{10,11... | collective-permute-start | bytes 196616 | tf_op jit(solution)/shard_map/ppermute | solution.py:402
  57.6 1.4 %collective-permute-start.37 = (bf16[64,512]{1,0:T(8,128)(2,1)S(1)}, bf16[64,512]{1,0:T(8,128)(2,1)S(1)}, u32[]{:S(2)}, u32[]{:S(2)}) collective-permute-start(bf16[64,512]{1,0:T(8,128)(2,1)S(1)} %collective-permute-done.35.refs_1_), channel_id=1, source_target_pairs={{0,1},{1,0},{2,3},{3,2},{4,5},{5,4},{6,7},{7,6},{8,9},{9,8},{10,11... | collective-permute-start | bytes 196616 | tf_op jit(solution)/shard_map/ppermute | solution.py:402
  59.7 7.6 %collective-permute-start.38 = (bf16[96,512]{1,0:T(8,128)(2,1)S(1)}, bf16[96,512]{1,0:T(8,128)(2,1)S(1)}, u32[]{:S(2)}, u32[]{:S(2)}) collective-permute-start(bf16[96,512]{1,0:T(8,128)(2,1)S(1)} %get-tuple-element.144), channel_id=1, source_target_pairs={{0,6},{1,7},{2,4},{3,5},{4,2},{5,3},{6,0},{7,1},{8,14},{9,15},{10,... | collective-permute-start | bytes 294920 | tf_op jit(solution)/shard_map/ppermute | solution.py:386
  62.0 9.4 %collective-permute-start.39 = (bf16[96,512]{1,0:T(8,128)(2,1)S(1)}, bf16[96,512]{1,0:T(8,128)(2,1)S(1)}, u32[]{:S(2)}, u32[]{:S(2)}) collective-permute-start(bf16[96,512]{1,0:T(8,128)(2,1)S(1)} %get-tuple-element.145), channel_id=1, source_target_pairs={{0,4},{1,5},{2,6},{3,7},{4,0},{5,1},{6,2},{7,3},{8,12},{9,13},{10,... | collective-permute-start | bytes 294920 | tf_op jit(solution)/shard_map/ppermute | solution.py:386
  62.1 9.3 %collective-permute-start.40 = (bf16[96,512]{1,0:T(8,128)(2,1)S(1)}, bf16[96,512]{1,0:T(8,128)(2,1)S(1)}, u32[]{:S(2)}, u32[]{:S(2)}) collective-permute-start(bf16[96,512]{1,0:T(8,128)(2,1)S(1)} %get-tuple-element.146), channel_id=1, source_target_pairs={{0,2},{1,3},{2,0},{3,1},{4,6},{5,7},{6,4},{7,5},{8,10},{9,11},{10,... | collective-permute-start | bytes 294920 | tf_op jit(solution)/shard_map/ppermute | solution.py:386
  (1 other events, 1.0 us)

commit v14 on v12

--- a/solution.py
+++ b/solution.py
@@ -87,11 +87,11 @@
     return output, mixed, q_up * slope, silu, jnp.concatenate([square, dot], axis=0)
 
 
-def apply_backward(f2t, sums, full_width, output, weighted, up_slope, silu):
+def apply_backward(f2, sums, full_width, output, weighted, up_slope, silu):
     inverse = lax.rsqrt(sums[0:1] / full_width + EPSILON)
     scale = inverse * inverse * inverse * sums[1:2] / full_width
     out_back = (inverse * weighted - output * scale).astype(BF16)
-    q_back = tn(f2t, out_back)
+    q_back = nn(f2, out_back)
     gate_back = (q_back * up_slope).astype(BF16)
     up_back = (q_back * silu).astype(BF16)
     return gate_back, up_back, out_back
@@ -210,24 +210,29 @@
         outs[3 + k][...] = total[half:].astype(BF16)
 
 
-def update_kernel(chips, folds, ko, kx, vo, vx, ro, rx, w1t, w3t, w2, *rest):
-    outs, (gate, up, push) = rest[:6], rest[6:]
+def push_kernel(vo, vx, ro, rx, push):
+    push[...] = push_of(both(ro, rx, 1), both(vo, vx))
+
+
+def transpose_kernel(x, out):
+    out[...] = x[...].T
+
+
+def update_kernel(chips, folds, ko, kx, push, w1t, w3t, w2, *rest):
+    outs, (gate, up) = rest[:6], rest[6:]
     keys = both(ko, kx)
-    push[...] = push_of(both(ro, rx, 1), both(vo, vx))
     *_, mixed, _, _, gate[...], up[...] = update_forward(w1t[...], w3t[...], w2[...], keys, push[...])
     send_halves(chips, folds, (gate, up, push, keys, mixed), outs)
 
 
 def saved_kernel(
-    chips, folds, ko, kx, vo, vx, ro, rx, w1t, w3t, w2, go, gx, gain,
-    push_ref, up_slope_ref, silu_ref, back_slope_ref, back_curve_ref,
+    chips, folds, ko, kx, push, w1t, w3t, w2, go, gx, gain,
+    up_slope_ref, silu_ref, back_slope_ref, back_curve_ref,
     mixed_ref, gate_back_ref, up_back_ref, weighted_ref, p1_ref, p3_ref, p2_ref,
     gate_ref, up_ref, down_ref,
 ):
-    push = push_of(both(ro, rx, 1), both(vo, vx))
-    push_ref[...] = push
     up_pre, silu, slope, curvature, mixed, down_back, back_slope, gate_back, up_back = (
-        update_forward(w1t[...], w3t[...], w2[...], both(ko, kx), push)
+        update_forward(w1t[...], w3t[...], w2[...], both(ko, kx), push[...])
     )
     up_slope_ref[...] = up_pre * slope
     silu_ref[...] = silu
@@ -299,11 +304,11 @@
     sums = parts[0][...]
     for part in parts[1:]:
         sums = sums + part[...]
-    f2t, output, weighted, mixed, up_slope, silu, qo, qx, gate_back, up_back = refs[:10]
+    f2, output, weighted, mixed, up_slope, silu, qo, qx, gate_back, up_back = refs[:10]
     outs, (gate, up, down) = refs[10:16], refs[16:]
     width = heads * output.shape[0]
     gate[...], up[...], down[...] = apply_backward(
-        f2t[...], sums, width, output[...], weighted[...], up_slope[...], silu[...]
+        f2[...], sums, width, output[...], weighted[...], up_slope[...], silu[...]
     )
     send_halves(chips, folds, (gate, up, down, both(qo, qx), mixed[...]), outs)
     own = gate_back.shape[1]
@@ -503,26 +508,30 @@
     key_other, value_other, rate_other = pair(key_input), pair(value_input), pair(rates)
     w1t, w3t = w1.T, w3.T
     query_other, grad_other = pair(query_input), pair(out_grad)
-    keys_values = (
-        key_input, key_other, value_input, value_other, rates, rate_other, w1t, w3t, w2,
-    )
+    (push,) = call(
+        push_kernel,
+        [((dh, n), BF16)],
+        (value_input, value_other, rates, rate_other),
+        name="push",
+    )
+    keys_values = key_input, key_other, push, w1t, w3t, w2
     sums = call(
         functools.partial(update_kernel, chips, folds),
         half_shares,
         keys_values,
-        operands,
+        operands[:2],
         "update",
         6 * product,
     )
     *saved, weighted, p1, p3, p2 = call(
         functools.partial(saved_kernel, chips, folds),
-        [((dh, n), BF16)] + [hidden] * 4 + [own_hidden] * 3 + [((dh, n), F32)] + [(half, F32)] * 3,
+        [hidden] * 4 + [own_hidden] * 3 + [((dh, n), F32)] + [(half, F32)] * 3,
         (*keys_values, out_grad, grad_other, gain),
         sums_scratch,
         "saved",
         3 * product,
     )
-    push, up_slope, silu, back_slope, back_curve, mixed, gate_back, up_back = saved
+    up_slope, silu, back_slope, back_curve, mixed, gate_back, up_back = saved
     priors = p1, p3, p2
 
     fast, moved = [], []
@@ -543,12 +552,13 @@
         name="apply",
         flops=3 * product,
     )
+    (f2,) = call(transpose_kernel, [((fh, dh), BF16)], (f2t,), name="fast_down", flops=product)
     q_gate_back, q_up_back, *sums = call(
         functools.partial(back_kernel, chips, folds, heads),
         [own_hidden] * 2 + half_shares,
         (
             *head_parts(part, heads),
-            f2t, output, weighted, q_mixed, q_slope, q_silu, query_input, query_other,
+            f2, output, weighted, q_mixed, q_slope, q_silu, query_input, query_other,
         ),
         operands,
         "apply_back",
@@ -638,7 +648,7 @@
     output, q_mixed, q_slope, q_silu, part = apply_forward(f1t, f3t, f2t, queries, weighted)
     sums = lax.psum(part, "head")
     q_gate_back, q_up_back, out_back = apply_backward(
-        f2t, sums, heads * dh, output, weighted, q_slope, q_silu
+        f2t.T, sums, heads * dh, output, weighted, q_slope, q_silu
     )
     grads = nn(q_gate_back, queries), nn(q_up_back, queries), nt(out_back, q_mixed)
     piece, sent = sliced_pieces(*grads, tok, count)

time: 72 us -> 72.2 us (level)
    pallas_call x21 -> x23, Pallas kernels: 9.49 us -> 9.81 us  [call(): pl.pallas_call(kernel, out_shape=[jax.ShapeDtypeStruct(s, t) for s, t in...]
where the time goes in v14:
time: 72.2 us; the launch traced here: 72 us
  starting transfers between devices  38.2 us (53%)
  waiting for transfers between devices  21.1 us (29%)
  Pallas kernels  9.81 us (14%)
  local copies, waits for them, and re-layouts  2.05 us (3%)
  between operations  0.91 us (1%)
    ppermute x18, starting transfers between devices, to_chip(): return lax.ppermute(x, 'tok', chip_perm(chips * CORES, step))  26.9 us
    ppermute x18, waiting for transfers between devices, to_chip(): return lax.ppermute(x, 'tok', chip_perm(chips * CORES, step))  11.8 us
    pallas_call x23, Pallas kernels, call(): pl.pallas_call(kernel, out_shape=[jax.ShapeDtypeStruct(s, t) for s, t in...  9.81 us
    ppermute x3, waiting for transfers between devices, exchange(): lax.ppermute(pieces[s], 'tok', chip_perm(count, s))  4.85 us
    ppermute x3, starting transfers between devices, exchange(): lax.ppermute(pieces[s], 'tok', chip_perm(count, s))  4.47 us
    ppermute x3, starting transfers between devices, head_parts(): lax.ppermute(part, 'head', [(h, partner(h, step, heads)) for h in range(h...  3.55 us
    ppermute x3, waiting for transfers between devices, head_parts(): lax.ppermute(part, 'head', [(h, partner(h, step, heads)) for h in range(h...  3.15 us
    ppermute x12, starting transfers between devices, from_owners(): cross = lambda x: lax.ppermute(x, 'tok', core_perm(chips * CORES))  2.12 us
  transfers between devices with their start and end apart: 41, of which 22 were waited for; matrix products, arithmetic and copies ran while one was open for 2% of the time, Pallas kernels for 9%

profile of v14, /device:TPU:0, one launch (start us, length us, event | category | flops | bytes accessed | tf_op | source)
XLA Modules:
  0.0 72.0 jit_solution(16517720529361426358)
XLA Ops:
  0.6 0.5 collective-permute-start.1
  1.8 1.1 %copy.15 = bf16[1,512,256]{1,2,0:T(8,128)(2,1)S(1)} copy(bf16[1,512,256]{2,1,0:T(8,128)(2,1)} %param.15) | data formatting | bytes 524288 | tf_op args[6]
  3.1 0.7 %copy-done.3 = bf16[256,512]{1,0:T(8,128)(2,1)S(1)} copy-done((bf16[256,512]{1,0:T(8,128)(2,1)S(1)}, bf16[256,512]{1,0:T(8,128)(2,1)}, u32[]{:S(2)}) %copy-start.3) | copy-done | bytes 262168
  4.1 1.2 %update.1 = (f32[64,512]{1,0:T(8,128)S(1)}, f32[64,512]{1,0:T(8,128)S(1)}, f32[64,512]{1,0:T(8,128)S(1)}, bf16[64,512]{1,0:T(8,128)(2,1)S(1)}, bf16[64,512]{1,0:T(8,128)(2,1)S(1)}, /*index=5*/bf16[64,512]{1,0:T(8,128)(2,1)S(1)}) custom-call(bf16[256,512]{1,0:T(8,128)(2,1)S(1)} %copy-done, bf16[256,512]{1,0:T(8,128)(2,1)S(1)} %collective-permute-done.kx.refs_9_.refs_5_, ...), custom_call_target="tpu_custom_call" | custom-call | flops 805306368 | bytes 1835008 | tf_op jit(solution)/shard_map/update/pallas_call | solution.py:368
  5.3 3.1 %collective-permute-start.8 = (bf16[64,512]{1,0:T(8,128)(2,1)S(1)}, bf16[64,512]{1,0:T(8,128)(2,1)S(1)}, u32[]{:S(2)}, u32[]{:S(2)}) collective-permute-start(bf16[64,512]{1,0:T(8,128)(2,1)S(1)} %get-tuple-element.87), channel_id=1, source_target_pairs={{0,2},{1,3},{2,0},{3,1},{4,6},{5,7},{6,4},{7,5},{8,10},{9,11},{10,... | collective-permute-start | bytes 196616 | tf_op jit(solution)/shard_map/ppermute | solution.py:391
  8.5 1.8 %collective-permute-start.6 = (bf16[64,512]{1,0:T(8,128)(2,1)S(1)}, bf16[64,512]{1,0:T(8,128)(2,1)S(1)}, u32[]{:S(2)}, u32[]{:S(2)}) collective-permute-start(bf16[64,512]{1,0:T(8,128)(2,1)S(1)} %get-tuple-element.83), channel_id=1, source_target_pairs={{0,2},{1,3},{2,0},{3,1},{4,6},{5,7},{6,4},{7,5},{8,10},{9,11},{10,... | collective-permute-start | bytes 196616 | tf_op jit(solution)/shard_map/ppermute | solution.py:391
  10.7 3.0 %collective-permute-start.9 = (bf16[64,512]{1,0:T(8,128)(2,1)S(1)}, bf16[64,512]{1,0:T(8,128)(2,1)S(1)}, u32[]{:S(2)}, u32[]{:S(2)}) collective-permute-start(bf16[64,512]{1,0:T(8,128)(2,1)S(1)} %carry.8.refs_0_), channel_id=1, source_target_pairs={{0,4},{1,5},{2,6},{3,7},{4,0},{5,1},{6,2},{7,3},{8,12},{9,13},{10,... | collective-permute-start | bytes 196616 | tf_op jit(solution)/shard_map/ppermute | solution.py:391
  13.7 2.2 %collective-permute-start.5 = (bf16[64,512]{1,0:T(8,128)(2,1)S(1)}, bf16[64,512]{1,0:T(8,128)(2,1)S(1)}, u32[]{:S(2)}, u32[]{:S(2)}) collective-permute-start(bf16[64,512]{1,0:T(8,128)(2,1)S(1)} %carry.6.refs_0_), channel_id=1, source_target_pairs={{0,4},{1,5},{2,6},{3,7},{4,0},{5,1},{6,2},{7,3},{8,12},{9,13},{10,... | collective-permute-start | bytes 196616 | tf_op jit(solution)/shard_map/ppermute | solution.py:391
  15.9 1.4 %collective-permute-start.7 = (bf16[64,512]{1,0:T(8,128)(2,1)S(1)}, bf16[64,512]{1,0:T(8,128)(2,1)S(1)}, u32[]{:S(2)}, u32[]{:S(2)}) collective-permute-start(bf16[64,512]{1,0:T(8,128)(2,1)S(1)} %carry.7.refs_0_), channel_id=1, source_target_pairs={{0,4},{1,5},{2,6},{3,7},{4,0},{5,1},{6,2},{7,3},{8,12},{9,13},{10,... | collective-permute-start | bytes 196616 | tf_op jit(solution)/shard_map/ppermute | solution.py:391
  17.3 1.0 %saved.1 = (f32[256,512]{1,0:T(8,128)S(1)}, f32[256,512]{1,0:T(8,128)S(1)}, f32[256,512]{1,0:T(8,128)S(1)}, f32[256,512]{1,0:T(8,128)S(1)}, bf16[256,256]{1,0:T(...) custom-call(bf16[256,512]{1,0:T(8,128)(2,1)S(1)} %copy-done, ...), custom_call_target="tpu_custom_call" | custom-call | flops 402653184 | bytes 2361344 | tf_op jit(solution)/shard_map/saved/pallas_call | solution.py:368
  18.5 2.7 %collective-permute-start.16 = (bf16[64,512]{1,0:T(8,128)(2,1)S(1)}, bf16[64,512]{1,0:T(8,128)(2,1)S(1)}, u32[]{:S(2)}, u32[]{:S(2)}) collective-permute-start(bf16[64,512]{1,0:T(8,128)(2,1)S(1)} %get-tuple-element.92.refs_8_), channel_id=1, source_target_pairs={{0,2},{1,3},{2,0},{3,1},{4,6},{5,7},{6,4},{7,5},{8,10},{9,11},{10,... | collective-permute-start | bytes 196616 | tf_op jit(solution)/shard_map/ppermute | solution.py:391
  21.5 1.2 %collective-permute-start.10 = (bf16[64,512]{1,0:T(8,128)(2,1)S(1)}, bf16[64,512]{1,0:T(8,128)(2,1)S(1)}, u32[]{:S(2)}, u32[]{:S(2)}) collective-permute-start(bf16[64,512]{1,0:T(8,128)(2,1)S(1)} %get-tuple-element.90.refs_0_), channel_id=1, source_target_pairs={{0,2},{1,3},{2,0},{3,1},{4,6},{5,7},{6,4},{7,5},{8,10},{9,11},{10,... | collective-permute-start | bytes 196616 | tf_op jit(solution)/shard_map/ppermute | solution.py:391
  23.3 0.5 collective-permute-start.13
  23.8 0.7 collective-permute-done.16.refs_9_
  24.5 1.5 %collective-permute-done.10.refs_1_ = bf16[64,512]{1,0:T(8,128)(2,1)S(1)} collective-permute-done((bf16[64,512]{1,0:T(8,128)(2,1)S(1)}, bf16[64,512]{1,0:T(8,128)(2,1)S(1)}, u32[]{:S(2)}, u32[]{:S(2)}) %collective-permute-start.10) | collective-permute-done | bytes 65568 | tf_op jit(solution)/shard_map/ppermute | solution.py:391
  26.0 0.5 collective-permute-start.14
  26.5 1.1 %collective-permute-done.13.refs_5_ = bf16[64,512]{1,0:T(8,128)(2,1)S(1)} collective-permute-done((bf16[64,512]{1,0:T(8,128)(2,1)S(1)}, bf16[64,512]{1,0:T(8,128)(2,1)S(1)}, u32[]{:S(2)}, u32[]{:S(2)}) %collective-permute-start.13) | collective-permute-done | bytes 65568 | tf_op jit(solution)/shard_map/ppermute | solution.py:391
  27.6 0.5 collective-permute-start.17
  28.2 0.7 collective-permute-done.15.refs_7_
  29.4 0.8 %apply.1 = (bf16[256,512]{1,0:T(8,128)(2,1)S(1)}, bf16[256,512]{1,0:T(8,128)(2,1)S(1)}, bf16[512,256]{1,0:T(8,128)(2,1)S(1)}, f32[512,512]{1,0:T(8,128)S(1)}, bf...) custom-call(bf16[64,512]{1,0:T(8,128)(2,1)S(1)} %get-tuple-element.90.refs_0, ...), custom_call_target="tpu_custom_call" | custom-call | flops 402653184 | bytes 2359296 | tf_op jit(solution)/shard_map/apply/pallas_call | solution.py:368
  30.2 2.7 %collective-permute-start.22 = (f32[2,512]{1,0:T(2,128)S(1)}, f32[2,512]{1,0:T(2,128)S(1)}, u32[]{:S(2)}, u32[]{:S(2)}) collective-permute-start(f32[2,512]{1,0:T(2,128)S(1)} %get-tuple-element.94.refs_0_), channel_id=1, source_target_pairs={{0,24},{8,16},{16,8},{24,0},{1,25},{9,17},{17,9},{25,1},{2,26},{10... | collective-permute-start | bytes 12296 | tf_op jit(solution)/shard_map/ppermute | solution.py:409
  33.9 0.9 %collective-permute-done.22.refs_3_ = f32[2,512]{1,0:T(2,128)S(1)} collective-permute-done((f32[2,512]{1,0:T(2,128)S(1)}, f32[2,512]{1,0:T(2,128)S(1)}, u32[]{:S(2)}, u32[]{:S(2)}) %collective-permute-start.22) | collective-permute-done | bytes 4128 | tf_op jit(solution)/shard_map/ppermute | solution.py:409
  34.8 1.8 %collective-permute-done.21.refs_2_ = f32[2,512]{1,0:T(2,128)S(1)} collective-permute-done((f32[2,512]{1,0:T(2,128)S(1)}, f32[2,512]{1,0:T(2,128)S(1)}, u32[]{:S(2)}, u32[]{:S(2)}) %collective-permute-start.21) | collective-permute-done | bytes 4128 | tf_op jit(solution)/shard_map/ppermute | solution.py:409
  37.0 0.9 %apply_back.1 = (bf16[256,256]{1,0:T(8,128)(2,1)S(1)}, bf16[256,256]{1,0:T(8,128)(2,1)S(1)}, f32[64,512]{1,0:T(8,128)S(1)}, f32[64,512]{1,0:T(8,128)S(1)}, f32[6...) custom-call(f32[2,512]{1,0:T(2,128)S(1)} %get-tuple-element.94.refs_0, ...), custom_call_target="tpu_custom_call" | custom-call | flops 536870912 | bytes 4210688 | tf_op jit(solution)/shard_map/apply_back/pallas_call | solution.py:368
  38.0 0.6 collective-permute-start.25
  38.6 1.5 %collective-permute-start.23 = (bf16[64,512]{1,0:T(8,128)(2,1)S(1)}, bf16[64,512]{1,0:T(8,128)(2,1)S(1)}, u32[]{:S(2)}, u32[]{:S(2)}) collective-permute-start(bf16[64,512]{1,0:T(8,128)(2,1)S(1)} %get-tuple-element.107), channel_id=1, source_target_pairs={{0,2},{1,3},{2,0},{3,1},{4,6},{5,7},{6,4},{7,5},{8,10},{9,11},{10,... | collective-permute-start | bytes 196616 | tf_op jit(solution)/shard_map/ppermute | solution.py:391
  40.1 0.5 collective-permute-start.27
  40.6 1.7 %collective-permute-done.25.got = bf16[64,512]{1,0:T(8,128)(2,1)S(1)} collective-permute-done((bf16[64,512]{1,0:T(8,128)(2,1)S(1)}, bf16[64,512]{1,0:T(8,128)(2,1)S(1)}, u32[]{:S(2)}, u32[]{:S(2)}) %collective-permute-start.25) | collective-permute-done | bytes 65568 | tf_op jit(solution)/shard_map/ppermute | solution.py:391
  42.3 3.4 %collective-permute-start.26 = (bf16[64,512]{1,0:T(8,128)(2,1)S(1)}, bf16[64,512]{1,0:T(8,128)(2,1)S(1)}, u32[]{:S(2)}, u32[]{:S(2)}) collective-permute-start(bf16[64,512]{1,0:T(8,128)(2,1)S(1)} %carry.10.refs_0_), channel_id=1, source_target_pairs={{0,4},{1,5},{2,6},{3,7},{4,0},{5,1},{6,2},{7,3},{8,12},{9,13},{10,... | collective-permute-start | bytes 196616 | tf_op jit(solution)/shard_map/ppermute | solution.py:391
  45.8 0.7 collective-permute-start.24
  46.5 2.4 %collective-permute-start.28 = (bf16[64,512]{1,0:T(8,128)(2,1)S(1)}, bf16[64,512]{1,0:T(8,128)(2,1)S(1)}, u32[]{:S(2)}, u32[]{:S(2)}) collective-permute-start(bf16[64,512]{1,0:T(8,128)(2,1)S(1)} %carry.11.refs_0_), channel_id=1, source_target_pairs={{0,4},{1,5},{2,6},{3,7},{4,0},{5,1},{6,2},{7,3},{8,12},{9,13},{10,... | collective-permute-start | bytes 196616 | tf_op jit(solution)/shard_map/ppermute | solution.py:391
  48.8 1.2 %collective-permute-done.26.refs_1_ = bf16[64,512]{1,0:T(8,128)(2,1)S(1)} collective-permute-done((bf16[64,512]{1,0:T(8,128)(2,1)S(1)}, bf16[64,512]{1,0:T(8,128)(2,1)S(1)}, u32[]{:S(2)}, u32[]{:S(2)}) %collective-permute-start.26) | collective-permute-done | bytes 65568 | tf_op jit(solution)/shard_map/ppermute | solution.py:391
  50.2 1.3 %collective-permute-done.24.refs_1_ = bf16[64,512]{1,0:T(8,128)(2,1)S(1)} collective-permute-done((bf16[64,512]{1,0:T(8,128)(2,1)S(1)}, bf16[64,512]{1,0:T(8,128)(2,1)S(1)}, u32[]{:S(2)}, u32[]{:S(2)}) %collective-permute-start.24) | collective-permute-done | bytes 65568 | tf_op jit(solution)/shard_map/ppermute | solution.py:391
  51.6 0.8 %collective-permute-start.29 = (bf16[64,512]{1,0:T(8,128)(2,1)S(1)}, bf16[64,512]{1,0:T(8,128)(2,1)S(1)}, u32[]{:S(2)}, u32[]{:S(2)}) collective-permute-start(bf16[64,512]{1,0:T(8,128)(2,1)S(1)} %get-tuple-element.118.refs_0_), channel_id=1, source_target_pairs={{0,2},{1,3},{2,0},{3,1},{4,6},{5,7},{6,4},{7,5},{8,10},{9,11},{10,... | collective-permute-start | bytes 196616 | tf_op jit(solution)/shard_map/ppermute | solution.py:391
  53.1 0.9 %collective-permute-start.35 = (bf16[64,512]{1,0:T(8,128)(2,1)S(1)}, bf16[64,512]{1,0:T(8,128)(2,1)S(1)}, u32[]{:S(2)}, u32[]{:S(2)}) collective-permute-start(bf16[64,512]{1,0:T(8,128)(2,1)S(1)} %get-tuple-element.125.refs_0_), channel_id=1, source_target_pairs={{0,2},{1,3},{2,0},{3,1},{4,6},{5,7},{6,4},{7,5},{8,10},{9,11},{10,... | collective-permute-start | bytes 196616 | tf_op jit(solution)/shard_map/ppermute | solution.py:391
  54.5 1.5 %collective-permute-done.29.refs_1_ = bf16[64,512]{1,0:T(8,128)(2,1)S(1)} collective-permute-done((bf16[64,512]{1,0:T(8,128)(2,1)S(1)}, bf16[64,512]{1,0:T(8,128)(2,1)S(1)}, u32[]{:S(2)}, u32[]{:S(2)}) %collective-permute-start.29) | collective-permute-done | bytes 65568 | tf_op jit(solution)/shard_map/ppermute | solution.py:391
  56.0 0.5 collective-permute-start.33
  56.5 0.9 %collective-permute-done.35.refs_1_ = bf16[64,512]{1,0:T(8,128)(2,1)S(1)} collective-permute-done((bf16[64,512]{1,0:T(8,128)(2,1)S(1)}, bf16[64,512]{1,0:T(8,128)(2,1)S(1)}, u32[]{:S(2)}, u32[]{:S(2)}) %collective-permute-start.35) | collective-permute-done | bytes 65568 | tf_op jit(solution)/shard_map/ppermute | solution.py:391
  57.4 0.5 collective-permute-start.37
  58.0 0.8 %second_first.1 = (bf16[256,512]{1,0:T(8,128)(2,1)S(1)}, bf16[256,512]{1,0:T(8,128)(2,1)S(1)}, bf16[256,256]{1,0:T(8,128)(2,1)S(1)}, f32[128,512]{1,0:T(8,128)S(...) custom-call(bf16[64,512]{1,0:T(8,128)(2,1)S(1)} %get-tuple-element.118.refs_0_, ...), custom_call_target="tpu_custom_call" | custom-call | flops 402653184 | bytes 3670016 | tf_op jit(solution)/shard_map/second_first/pallas_call | solution.py:368
  58.8 0.7 %second_last.1 = (bf16[512,256]{1,0:T(8,128)(2,1)S(1)}, bf16[256,256]{1,0:T(8,128)(2,1)S(1)}, bf16[256,256]{1,0:T(8,128)(2,1)S(1)}, f32[96,512]{1,0:T(8,128)S(1)...) custom-call(bf16[64,512]{1,0:T(8,128)(2,1)S(1)} %get-tuple-element.125.refs_0_, ...), custom_call_target="tpu_custom_call" | custom-call | flops 402653184 | bytes 3670016 | tf_op jit(solution)/shard_map/second_last/pallas_call | solution.py:368
  59.6 2.3 %collective-permute-start.38 = (bf16[96,512]{1,0:T(8,128)(2,1)S(1)}, bf16[96,512]{1,0:T(8,128)(2,1)S(1)}, u32[]{:S(2)}, u32[]{:S(2)}) collective-permute-start(bf16[96,512]{1,0:T(8,128)(2,1)S(1)} %get-tuple-element.142), channel_id=1, source_target_pairs={{0,6},{1,7},{2,4},{3,5},{4,2},{5,3},{6,0},{7,1},{8,14},{9,15},{10,... | collective-permute-start | bytes 294920 | tf_op jit(solution)/shard_map/ppermute | solution.py:386
  62.0 2.1 %collective-permute-start.40 = (bf16[96,512]{1,0:T(8,128)(2,1)S(1)}, bf16[96,512]{1,0:T(8,128)(2,1)S(1)}, u32[]{:S(2)}, u32[]{:S(2)}) collective-permute-start(bf16[96,512]{1,0:T(8,128)(2,1)S(1)} %get-tuple-element.144), channel_id=1, source_target_pairs={{0,2},{1,3},{2,0},{3,1},{4,6},{5,7},{6,4},{7,5},{8,10},{9,11},{10,... | collective-permute-start | bytes 294920 | tf_op jit(solution)/shard_map/ppermute | solution.py:386
  64.1 1.0 %query_grad.1 = bf16[256,512]{1,0:T(8,128)(2,1)} custom-call(bf16[256,256]{1,0:T(8,128)(2,1)S(1)} %get-tuple-element.100.gate_back, bf16[256,256]{1,0:T(8,128)(2,1)S(1)} %get-tuple-element.101.up_back, bf16[256,512]{1,0:T(8,128)(2,1)S(1)} %get-tuple-element.102.f1t, bf16[256,512]{1,0:T(8,128)(2,1)S(1)} %get-tuple-element.103.f3t), custom_call_target="tpu_custom_call" | custom-call | flops 134217728 | bytes 786432 | tf_op jit(solution)/shard_map/query_grad/pallas_call | solution.py:368
  65.1 1.4 %token_grads.1 = (bf16[256,512]{1,0:T(8,128)(2,1)}, bf16[256,512]{1,0:T(8,128)(2,1)}) custom-call(f32[1,256]{1,0:T(1,128)S(1)} %bitcast.29, bf16[256,256]{1,0:T(8,128)(2,1)S(1)} %get-tuple-element.104.refs_1_, bf16[256,256]{1,0:T(8,128)(2,1)S(1)} %get-tuple-element.124.refs_2_, bf16[256,256]{1,0:T(8,128)(2,1)S(1)} %get-tuple-element.129.refs_3_, ...), custom_call_target="tpu_custom_call" | custom-call | flops 402653184 | bytes 2360320 | tf_op jit(solution)/shard_map/token_grads/pallas_call | solution.py:368
  66.5 0.7 %collective-permute-done.38.refs_4_ = bf16[96,512]{1,0:T(8,128)(2,1)S(1)} collective-permute-done((bf16[96,512]{1,0:T(8,128)(2,1)S(1)}, bf16[96,512]{1,0:T(8,128)(2,1)S(1)}, u32[]{:S(2)}, u32[]{:S(2)}) %collective-permute-start.38) | collective-permute-done | bytes 98336 | tf_op jit(solution)/shard_map/ppermute | solution.py:386
  67.2 4.1 %collective-permute-done.39.refs_5_ = bf16[96,512]{1,0:T(8,128)(2,1)S(1)} collective-permute-done((bf16[96,512]{1,0:T(8,128)(2,1)S(1)}, bf16[96,512]{1,0:T(8,128)(2,1)S(1)}, u32[]{:S(2)}, u32[]{:S(2)}) %collective-permute-start.39) | collective-permute-done | bytes 98336 | tf_op jit(solution)/shard_map/ppermute | solution.py:386
  71.3 0.7 owner_result.1
  (75 shorter events, 6.4 us)
Async XLA Ops:
  0.6 1.0 %copy-start.5 = (f32[256,1]{0,1:T(1,128)S(1)}, f32[256,1]{0,1:T(1,128)}, u32[]{:S(2)}) copy-start(f32[256,1]{0,1:T(1,128)} %param.13) | copy-start | bytes 3076
  0.6 2.4 %collective-permute-start.1 = (bf16[256,512]{1,0:T(8,128)(2,1)}, bf16[256,512]{1,0:T(8,128)(2,1)S(1)}, u32[]{:S(2)}, u32[]{:S(2)}) collective-permute-start(bf16[256,512]{1,0:T(8,128)(2,1)} %vo.1), channel_id=1, source_target_pairs={{0,1},{1,0},{2,3},{3,2},{4,5},{5,4},{6,7},{7,6},{8,9},{9,8},{10,11... | collective-permute-start | bytes 786440 | tf_op jit(solution)/shard_map/ppermute | solution.py:507
  1.2 2.9 %collective-permute-start = (bf16[256,512]{1,0:T(8,128)(2,1)}, bf16[256,512]{1,0:T(8,128)(2,1)S(1)}, u32[]{:S(2)}, u32[]{:S(2)}) collective-permute-start(bf16[256,512]{1,0:T(8,128)(2,1)} %refs_4_.1), channel_id=1, source_target_pairs={{0,1},{1,0},{2,3},{3,2},{4,5},{5,4},{6,7},{7,6},{8,9},{9,8},{10,11... | collective-permute-start | bytes 786440 | tf_op jit(solution)/shard_map/ppermute | solution.py:507
  1.2 16.1 %collective-permute-start.3 = (bf16[256,512]{1,0:T(8,128)(2,1)}, bf16[256,512]{1,0:T(8,128)(2,1)S(1)}, u32[]{:S(2)}, u32[]{:S(2)}) collective-permute-start(bf16[256,512]{1,0:T(8,128)(2,1)} %go.1), channel_id=1, source_target_pairs={{0,1},{1,0},{2,3},{3,2},{4,5},{5,4},{6,7},{7,6},{8,9},{9,8},{10,11... | collective-permute-start | bytes 786440 | tf_op jit(solution)/shard_map/ppermute | solution.py:507
  1.7 1.2 %copy-start.7 = (bf16[1,512,256]{2,1,0:T(8,128)(2,1)S(1)}, bf16[1,512,256]{2,1,0:T(8,128)(2,1)}, u32[]{:S(2)}) copy-start(bf16[1,512,256]{2,1,0:T(8,128)(2,1)} %param.16) | copy-start | bytes 786436
  1.7 1.4 %collective-permute-start.2 = (f32[1,256]{1,0:T(1,128)S(1)}, f32[1,256]{1,0:T(1,128)S(1)}, u32[]{:S(2)}, u32[]{:S(2)}) collective-permute-start(f32[1,256]{1,0:T(1,128)S(1)} %bitcast.27), channel_id=1, source_target_pairs={{0,1},{1,0},{2,3},{3,2},{4,5},{5,4},{6,7},{7,6},{8,9},{9,8},{10,11... | collective-permute-start | bytes 3080 | tf_op jit(solution)/shard_map/ppermute | solution.py:507
  3.0 1.0 %copy-start = (bf16[256,512]{1,0:T(8,128)(2,1)S(1)}, bf16[256,512]{1,0:T(8,128)(2,1)}, u32[]{:S(2)}) copy-start(bf16[256,512]{1,0:T(8,128)(2,1)} %refs_4_.1) | copy-start | bytes 786436
  3.0 1.0 %copy-start.2 = (bf16[1,256,512]{2,1,0:T(8,128)(2,1)S(1)}, bf16[1,256,512]{2,1,0:T(8,128)(2,1)}, u32[]{:S(2)}) copy-start(bf16[1,256,512]{2,1,0:T(8,128)(2,1)} %param.17) | copy-start | bytes 786436
  4.1 4.3 %copy-start.1 = (bf16[256,512]{1,0:T(8,128)(2,1)S(1)}, bf16[256,512]{1,0:T(8,128)(2,1)}, u32[]{:S(2)}) copy-start(bf16[256,512]{1,0:T(8,128)(2,1)} %refs_10_.1) | copy-start | bytes 786436
  5.3 5.4 %collective-permute-start.8 = (bf16[64,512]{1,0:T(8,128)(2,1)S(1)}, bf16[64,512]{1,0:T(8,128)(2,1)S(1)}, u32[]{:S(2)}, u32[]{:S(2)}) collective-permute-start(bf16[64,512]{1,0:T(8,128)(2,1)S(1)} %get-tuple-element.87), channel_id=1, source_target_pairs={{0,2},{1,3},{2,0},{3,1},{4,6},{5,7},{6,4},{7,5},{8,10},{9,11},{10,... | collective-permute-start | bytes 196616 | tf_op jit(solution)/shard_map/ppermute | solution.py:391
  8.3 19.3 %collective-permute-start.19 = (bf16[256,512]{1,0:T(8,128)(2,1)S(1)}, bf16[256,512]{1,0:T(8,128)(2,1)S(1)}, u32[]{:S(2)}, u32[]{:S(2)}) collective-permute-start(bf16[256,512]{1,0:T(8,128)(2,1)S(1)} %copy-done.1), channel_id=1, source_target_pairs={{0,1},{1,0},{2,3},{3,2},{4,5},{5,4},{6,7},{7,6},{8,9},{9,8},{10,11... | collective-permute-start | bytes 786440 | tf_op jit(solution)/shard_map/ppermute | solution.py:507
  8.3 5.4 %collective-permute-start.4 = (bf16[64,512]{1,0:T(8,128)(2,1)S(1)}, bf16[64,512]{1,0:T(8,128)(2,1)S(1)}, u32[]{:S(2)}, u32[]{:S(2)}) collective-permute-start(bf16[64,512]{1,0:T(8,128)(2,1)S(1)} %get-tuple-element.79), channel_id=1, source_target_pairs={{0,2},{1,3},{2,0},{3,1},{4,6},{5,7},{6,4},{7,5},{8,10},{9,11},{10,... | collective-permute-start | bytes 196616 | tf_op jit(solution)/shard_map/ppermute | solution.py:391
  8.5 7.4 %collective-permute-start.6 = (bf16[64,512]{1,0:T(8,128)(2,1)S(1)}, bf16[64,512]{1,0:T(8,128)(2,1)S(1)}, u32[]{:S(2)}, u32[]{:S(2)}) collective-permute-start(bf16[64,512]{1,0:T(8,128)(2,1)S(1)} %get-tuple-element.83), channel_id=1, source_target_pairs={{0,2},{1,3},{2,0},{3,1},{4,6},{5,7},{6,4},{7,5},{8,10},{9,11},{10,... | collective-permute-start | bytes 196616 | tf_op jit(solution)/shard_map/ppermute | solution.py:391
  10.7 7.7 %collective-permute-start.9 = (bf16[64,512]{1,0:T(8,128)(2,1)S(1)}, bf16[64,512]{1,0:T(8,128)(2,1)S(1)}, u32[]{:S(2)}, u32[]{:S(2)}) collective-permute-start(bf16[64,512]{1,0:T(8,128)(2,1)S(1)} %carry.8.refs_0_), channel_id=1, source_target_pairs={{0,4},{1,5},{2,6},{3,7},{4,0},{5,1},{6,2},{7,3},{8,12},{9,13},{10,... | collective-permute-start | bytes 196616 | tf_op jit(solution)/shard_map/ppermute | solution.py:391
  13.7 3.6 %copy-start.4 = (bf16[256,512]{1,0:T(8,128)(2,1)S(1)}, bf16[256,512]{1,0:T(8,128)(2,1)}, u32[]{:S(2)}) copy-start(bf16[256,512]{1,0:T(8,128)(2,1)} %go.1) | copy-start | bytes 786436
  13.7 7.7 %collective-permute-start.5 = (bf16[64,512]{1,0:T(8,128)(2,1)S(1)}, bf16[64,512]{1,0:T(8,128)(2,1)S(1)}, u32[]{:S(2)}, u32[]{:S(2)}) collective-permute-start(bf16[64,512]{1,0:T(8,128)(2,1)S(1)} %carry.6.refs_0_), channel_id=1, source_target_pairs={{0,4},{1,5},{2,6},{3,7},{4,0},{5,1},{6,2},{7,3},{8,12},{9,13},{10,... | collective-permute-start | bytes 196616 | tf_op jit(solution)/shard_map/ppermute | solution.py:391
  15.9 1.4 %copy-start.6 = (f32[512]{0:T(512)S(1)}, f32[512]{0:T(512)}, u32[]{:S(2)}) copy-start(f32[512]{0:T(512)} %param.14) | copy-start | bytes 6148
  15.9 7.2 %collective-permute-start.7 = (bf16[64,512]{1,0:T(8,128)(2,1)S(1)}, bf16[64,512]{1,0:T(8,128)(2,1)S(1)}, u32[]{:S(2)}, u32[]{:S(2)}) collective-permute-start(bf16[64,512]{1,0:T(8,128)(2,1)S(1)} %carry.7.refs_0_), channel_id=1, source_target_pairs={{0,4},{1,5},{2,6},{3,7},{4,0},{5,1},{6,2},{7,3},{8,12},{9,13},{10,... | collective-permute-start | bytes 196616 | tf_op jit(solution)/shard_map/ppermute | solution.py:391
  18.5 6.0 %collective-permute-start.16 = (bf16[64,512]{1,0:T(8,128)(2,1)S(1)}, bf16[64,512]{1,0:T(8,128)(2,1)S(1)}, u32[]{:S(2)}, u32[]{:S(2)}) collective-permute-start(bf16[64,512]{1,0:T(8,128)(2,1)S(1)} %get-tuple-element.92.refs_8_), channel_id=1, source_target_pairs={{0,2},{1,3},{2,0},{3,1},{4,6},{5,7},{6,4},{7,5},{8,10},{9,11},{10,... | collective-permute-start | bytes 196616 | tf_op jit(solution)/shard_map/ppermute | solution.py:391
  21.5 4.5 %collective-permute-start.10 = (bf16[64,512]{1,0:T(8,128)(2,1)S(1)}, bf16[64,512]{1,0:T(8,128)(2,1)S(1)}, u32[]{:S(2)}, u32[]{:S(2)}) collective-permute-start(bf16[64,512]{1,0:T(8,128)(2,1)S(1)} %get-tuple-element.90.refs_0_), channel_id=1, source_target_pairs={{0,2},{1,3},{2,0},{3,1},{4,6},{5,7},{6,4},{7,5},{8,10},{9,11},{10,... | collective-permute-start | bytes 196616 | tf_op jit(solution)/shard_map/ppermute | solution.py:391
  23.3 4.3 %collective-permute-start.13 = (bf16[64,512]{1,0:T(8,128)(2,1)S(1)}, bf16[64,512]{1,0:T(8,128)(2,1)S(1)}, u32[]{:S(2)}, u32[]{:S(2)}) collective-permute-start(bf16[64,512]{1,0:T(8,128)(2,1)S(1)} %get-tuple-element.91.refs_4_), channel_id=1, source_target_pairs={{0,2},{1,3},{2,0},{3,1},{4,6},{5,7},{6,4},{7,5},{8,10},{9,11},{10,... | collective-permute-start | bytes 196616 | tf_op jit(solution)/shard_map/ppermute | solution.py:391
  24.5 3.6 %collective-permute-start.18 = (bf16[64,512]{1,0:T(8,128)(2,1)S(1)}, bf16[64,512]{1,0:T(8,128)(2,1)S(1)}, u32[]{:S(2)}, u32[]{:S(2)}) collective-permute-start(bf16[64,512]{1,0:T(8,128)(2,1)S(1)} %collective-permute-done.16.refs_9_), channel_id=1, source_target_pairs={{0,1},{1,0},{2,3},{3,2},{4,5},{5,4},{6,7},{7,6},{8,9},{9,8},{10,11... | collective-permute-start | bytes 196616 | tf_op jit(solution)/shard_map/ppermute | solution.py:402
  26.0 2.8 %collective-permute-start.11 = (bf16[64,512]{1,0:T(8,128)(2,1)S(1)}, bf16[64,512]{1,0:T(8,128)(2,1)S(1)}, u32[]{:S(2)}, u32[]{:S(2)}) collective-permute-start(bf16[64,512]{1,0:T(8,128)(2,1)S(1)} %get-tuple-element.90.refs_0_), channel_id=1, source_target_pairs={{0,1},{1,0},{2,3},{3,2},{4,5},{5,4},{6,7},{7,6},{8,9},{9,8},{10,11... | collective-permute-start | bytes 196616 | tf_op jit(solution)/shard_map/ppermute | solution.py:402
  26.0 2.8 %collective-permute-start.14 = (bf16[64,512]{1,0:T(8,128)(2,1)S(1)}, bf16[64,512]{1,0:T(8,128)(2,1)S(1)}, u32[]{:S(2)}, u32[]{:S(2)}) collective-permute-start(bf16[64,512]{1,0:T(8,128)(2,1)S(1)} %get-tuple-element.91.refs_4_), channel_id=1, source_target_pairs={{0,1},{1,0},{2,3},{3,2},{4,5},{5,4},{6,7},{7,6},{8,9},{9,8},{10,11... | collective-permute-start | bytes 196616 | tf_op jit(solution)/shard_map/ppermute | solution.py:402
  27.6 1.3 %collective-permute-start.15 = (bf16[64,512]{1,0:T(8,128)(2,1)S(1)}, bf16[64,512]{1,0:T(8,128)(2,1)S(1)}, u32[]{:S(2)}, u32[]{:S(2)}) collective-permute-start(bf16[64,512]{1,0:T(8,128)(2,1)S(1)} %collective-permute-done.13.refs_5_), channel_id=1, source_target_pairs={{0,1},{1,0},{2,3},{3,2},{4,5},{5,4},{6,7},{7,6},{8,9},{9,8},{10,11... | collective-permute-start | bytes 196616 | tf_op jit(solution)/shard_map/ppermute | solution.py:402
  27.6 1.4 %collective-permute-start.17 = (bf16[64,512]{1,0:T(8,128)(2,1)S(1)}, bf16[64,512]{1,0:T(8,128)(2,1)S(1)}, u32[]{:S(2)}, u32[]{:S(2)}) collective-permute-start(bf16[64,512]{1,0:T(8,128)(2,1)S(1)} %get-tuple-element.92.refs_8_), channel_id=1, source_target_pairs={{0,1},{1,0},{2,3},{3,2},{4,5},{5,4},{6,7},{7,6},{8,9},{9,8},{10,11... | collective-permute-start | bytes 196616 | tf_op jit(solution)/shard_map/ppermute | solution.py:402
  28.1 1.3 %collective-permute-start.12 = (bf16[64,512]{1,0:T(8,128)(2,1)S(1)}, bf16[64,512]{1,0:T(8,128)(2,1)S(1)}, u32[]{:S(2)}, u32[]{:S(2)}) collective-permute-start(bf16[64,512]{1,0:T(8,128)(2,1)S(1)} %collective-permute-done.10.refs_1_), channel_id=1, source_target_pairs={{0,1},{1,0},{2,3},{3,2},{4,5},{5,4},{6,7},{7,6},{8,9},{9,8},{10,11... | collective-permute-start | bytes 196616 | tf_op jit(solution)/shard_map/ppermute | solution.py:402
  30.2 4.6 %collective-permute-start.22 = (f32[2,512]{1,0:T(2,128)S(1)}, f32[2,512]{1,0:T(2,128)S(1)}, u32[]{:S(2)}, u32[]{:S(2)}) collective-permute-start(f32[2,512]{1,0:T(2,128)S(1)} %get-tuple-element.94.refs_0_), channel_id=1, source_target_pairs={{0,24},{8,16},{16,8},{24,0},{1,25},{9,17},{17,9},{25,1},{2,26},{10... | collective-permute-start | bytes 12296 | tf_op jit(solution)/shard_map/ppermute | solution.py:409
  32.9 3.6 %collective-permute-start.21 = (f32[2,512]{1,0:T(2,128)S(1)}, f32[2,512]{1,0:T(2,128)S(1)}, u32[]{:S(2)}, u32[]{:S(2)}) collective-permute-start(f32[2,512]{1,0:T(2,128)S(1)} %get-tuple-element.94.refs_0_), channel_id=1, source_target_pairs={{0,16},{8,24},{16,0},{24,8},{1,17},{9,25},{17,1},{25,9},{2,18},{10... | collective-permute-start | bytes 12296 | tf_op jit(solution)/shard_map/ppermute | solution.py:409
  33.4 3.6 %collective-permute-start.20 = (f32[2,512]{1,0:T(2,128)S(1)}, f32[2,512]{1,0:T(2,128)S(1)}, u32[]{:S(2)}, u32[]{:S(2)}) collective-permute-start(f32[2,512]{1,0:T(2,128)S(1)} %get-tuple-element.94.refs_0_), channel_id=1, source_target_pairs={{0,8},{8,0},{16,24},{24,16},{1,9},{9,1},{17,25},{25,17},{2,10},{10... | collective-permute-start | bytes 12296 | tf_op jit(solution)/shard_map/ppermute | solution.py:409
  38.0 4.3 %collective-permute-start.25 = (bf16[64,512]{1,0:T(8,128)(2,1)S(1)}, bf16[64,512]{1,0:T(8,128)(2,1)S(1)}, u32[]{:S(2)}, u32[]{:S(2)}) collective-permute-start(bf16[64,512]{1,0:T(8,128)(2,1)S(1)} %get-tuple-element.111), channel_id=1, source_target_pairs={{0,2},{1,3},{2,0},{3,1},{4,6},{5,7},{6,4},{7,5},{8,10},{9,11},{10,... | collective-permute-start | bytes 196616 | tf_op jit(solution)/shard_map/ppermute | solution.py:391
  38.6 7.2 %collective-permute-start.23 = (bf16[64,512]{1,0:T(8,128)(2,1)S(1)}, bf16[64,512]{1,0:T(8,128)(2,1)S(1)}, u32[]{:S(2)}, u32[]{:S(2)}) collective-permute-start(bf16[64,512]{1,0:T(8,128)(2,1)S(1)} %get-tuple-element.107), channel_id=1, source_target_pairs={{0,2},{1,3},{2,0},{3,1},{4,6},{5,7},{6,4},{7,5},{8,10},{9,11},{10,... | collective-permute-start | bytes 196616 | tf_op jit(solution)/shard_map/ppermute | solution.py:391
  40.1 6.4 %collective-permute-start.27 = (bf16[64,512]{1,0:T(8,128)(2,1)S(1)}, bf16[64,512]{1,0:T(8,128)(2,1)S(1)}, u32[]{:S(2)}, u32[]{:S(2)}) collective-permute-start(bf16[64,512]{1,0:T(8,128)(2,1)S(1)} %get-tuple-element.115), channel_id=1, source_target_pairs={{0,2},{1,3},{2,0},{3,1},{4,6},{5,7},{6,4},{7,5},{8,10},{9,11},{10,... | collective-permute-start | bytes 196616 | tf_op jit(solution)/shard_map/ppermute | solution.py:391
  42.3 7.7 %collective-permute-start.26 = (bf16[64,512]{1,0:T(8,128)(2,1)S(1)}, bf16[64,512]{1,0:T(8,128)(2,1)S(1)}, u32[]{:S(2)}, u32[]{:S(2)}) collective-permute-start(bf16[64,512]{1,0:T(8,128)(2,1)S(1)} %carry.10.refs_0_), channel_id=1, source_target_pairs={{0,4},{1,5},{2,6},{3,7},{4,0},{5,1},{6,2},{7,3},{8,12},{9,13},{10,... | collective-permute-start | bytes 196616 | tf_op jit(solution)/shard_map/ppermute | solution.py:391
  45.8 5.7 %collective-permute-start.24 = (bf16[64,512]{1,0:T(8,128)(2,1)S(1)}, bf16[64,512]{1,0:T(8,128)(2,1)S(1)}, u32[]{:S(2)}, u32[]{:S(2)}) collective-permute-start(bf16[64,512]{1,0:T(8,128)(2,1)S(1)} %carry.9.refs_0_), channel_id=1, source_target_pairs={{0,4},{1,5},{2,6},{3,7},{4,0},{5,1},{6,2},{7,3},{8,12},{9,13},{10,... | collective-permute-start | bytes 196616 | tf_op jit(solution)/shard_map/ppermute | solution.py:391
  46.5 6.4 %collective-permute-start.28 = (bf16[64,512]{1,0:T(8,128)(2,1)S(1)}, bf16[64,512]{1,0:T(8,128)(2,1)S(1)}, u32[]{:S(2)}, u32[]{:S(2)}) collective-permute-start(bf16[64,512]{1,0:T(8,128)(2,1)S(1)} %carry.11.refs_0_), channel_id=1, source_target_pairs={{0,4},{1,5},{2,6},{3,7},{4,0},{5,1},{6,2},{7,3},{8,12},{9,13},{10,... | collective-permute-start | bytes 196616 | tf_op jit(solution)/shard_map/ppermute | solution.py:391
  50.2 4.3 %collective-permute-start.32 = (bf16[64,512]{1,0:T(8,128)(2,1)S(1)}, bf16[64,512]{1,0:T(8,128)(2,1)S(1)}, u32[]{:S(2)}, u32[]{:S(2)}) collective-permute-start(bf16[64,512]{1,0:T(8,128)(2,1)S(1)} %get-tuple-element.119.refs_4_), channel_id=1, source_target_pairs={{0,2},{1,3},{2,0},{3,1},{4,6},{5,7},{6,4},{7,5},{8,10},{9,11},{10,... | collective-permute-start | bytes 196616 | tf_op jit(solution)/shard_map/ppermute | solution.py:391
  51.6 4.3 %collective-permute-start.29 = (bf16[64,512]{1,0:T(8,128)(2,1)S(1)}, bf16[64,512]{1,0:T(8,128)(2,1)S(1)}, u32[]{:S(2)}, u32[]{:S(2)}) collective-permute-start(bf16[64,512]{1,0:T(8,128)(2,1)S(1)} %get-tuple-element.118.refs_0_), channel_id=1, source_target_pairs={{0,2},{1,3},{2,0},{3,1},{4,6},{5,7},{6,4},{7,5},{8,10},{9,11},{10,... | collective-permute-start | bytes 196616 | tf_op jit(solution)/shard_map/ppermute | solution.py:391
  53.1 4.3 %collective-permute-start.35 = (bf16[64,512]{1,0:T(8,128)(2,1)S(1)}, bf16[64,512]{1,0:T(8,128)(2,1)S(1)}, u32[]{:S(2)}, u32[]{:S(2)}) collective-permute-start(bf16[64,512]{1,0:T(8,128)(2,1)S(1)} %get-tuple-element.125.refs_0_), channel_id=1, source_target_pairs={{0,2},{1,3},{2,0},{3,1},{4,6},{5,7},{6,4},{7,5},{8,10},{9,11},{10,... | collective-permute-start | bytes 196616 | tf_op jit(solution)/shard_map/ppermute | solution.py:391
  54.5 3.0 %collective-permute-start.34 = (bf16[64,512]{1,0:T(8,128)(2,1)S(1)}, bf16[64,512]{1,0:T(8,128)(2,1)S(1)}, u32[]{:S(2)}, u32[]{:S(2)}) collective-permute-start(bf16[64,512]{1,0:T(8,128)(2,1)S(1)} %collective-permute-done.32.refs_5_), channel_id=1, source_target_pairs={{0,1},{1,0},{2,3},{3,2},{4,5},{5,4},{6,7},{7,6},{8,9},{9,8},{10,11... | collective-permute-start | bytes 196616 | tf_op jit(solution)/shard_map/ppermute | solution.py:402
  56.0 2.0 %collective-permute-start.30 = (bf16[64,512]{1,0:T(8,128)(2,1)S(1)}, bf16[64,512]{1,0:T(8,128)(2,1)S(1)}, u32[]{:S(2)}, u32[]{:S(2)}) collective-permute-start(bf16[64,512]{1,0:T(8,128)(2,1)S(1)} %get-tuple-element.118.refs_0_), channel_id=1, source_target_pairs={{0,1},{1,0},{2,3},{3,2},{4,5},{5,4},{6,7},{7,6},{8,9},{9,8},{10,11... | collective-permute-start | bytes 196616 | tf_op jit(solution)/shard_map/ppermute | solution.py:402
  56.0 2.0 %collective-permute-start.33 = (bf16[64,512]{1,0:T(8,128)(2,1)S(1)}, bf16[64,512]{1,0:T(8,128)(2,1)S(1)}, u32[]{:S(2)}, u32[]{:S(2)}) collective-permute-start(bf16[64,512]{1,0:T(8,128)(2,1)S(1)} %get-tuple-element.119.refs_4_), channel_id=1, source_target_pairs={{0,1},{1,0},{2,3},{3,2},{4,5},{5,4},{6,7},{7,6},{8,9},{9,8},{10,11... | collective-permute-start | bytes 196616 | tf_op jit(solution)/shard_map/ppermute | solution.py:402
  56.5 1.5 %collective-permute-start.31 = (bf16[64,512]{1,0:T(8,128)(2,1)S(1)}, bf16[64,512]{1,0:T(8,128)(2,1)S(1)}, u32[]{:S(2)}, u32[]{:S(2)}) collective-permute-start(bf16[64,512]{1,0:T(8,128)(2,1)S(1)} %collective-permute-done.29.refs_1_), channel_id=1, source_target_pairs={{0,1},{1,0},{2,3},{3,2},{4,5},{5,4},{6,7},{7,6},{8,9},{9,8},{10,11... | collective-permute-start | bytes 196616 | tf_op jit(solution)/shard_map/ppermute | solution.py:402
  57.4 1.3 %collective-permute-start.36 = (bf16[64,512]{1,0:T(8,128)(2,1)S(1)}, bf16[64,512]{1,0:T(8,128)(2,1)S(1)}, u32[]{:S(2)}, u32[]{:S(2)}) collective-permute-start(bf16[64,512]{1,0:T(8,128)(2,1)S(1)} %get-tuple-element.125.refs_0_), channel_id=1, source_target_pairs={{0,1},{1,0},{2,3},{3,2},{4,5},{5,4},{6,7},{7,6},{8,9},{9,8},{10,11... | collective-permute-start | bytes 196616 | tf_op jit(solution)/shard_map/ppermute | solution.py:402
  57.4 1.4 %collective-permute-start.37 = (bf16[64,512]{1,0:T(8,128)(2,1)S(1)}, bf16[64,512]{1,0:T(8,128)(2,1)S(1)}, u32[]{:S(2)}, u32[]{:S(2)}) collective-permute-start(bf16[64,512]{1,0:T(8,128)(2,1)S(1)} %collective-permute-done.35.refs_1_), channel_id=1, source_target_pairs={{0,1},{1,0},{2,3},{3,2},{4,5},{5,4},{6,7},{7,6},{8,9},{9,8},{10,11... | collective-permute-start | bytes 196616 | tf_op jit(solution)/shard_map/ppermute | solution.py:402
  59.6 7.6 %collective-permute-start.38 = (bf16[96,512]{1,0:T(8,128)(2,1)S(1)}, bf16[96,512]{1,0:T(8,128)(2,1)S(1)}, u32[]{:S(2)}, u32[]{:S(2)}) collective-permute-start(bf16[96,512]{1,0:T(8,128)(2,1)S(1)} %get-tuple-element.142), channel_id=1, source_target_pairs={{0,6},{1,7},{2,4},{3,5},{4,2},{5,3},{6,0},{7,1},{8,14},{9,15},{10,... | collective-permute-start | bytes 294920 | tf_op jit(solution)/shard_map/ppermute | solution.py:386
  61.9 9.4 %collective-permute-start.39 = (bf16[96,512]{1,0:T(8,128)(2,1)S(1)}, bf16[96,512]{1,0:T(8,128)(2,1)S(1)}, u32[]{:S(2)}, u32[]{:S(2)}) collective-permute-start(bf16[96,512]{1,0:T(8,128)(2,1)S(1)} %get-tuple-element.143), channel_id=1, source_target_pairs={{0,4},{1,5},{2,6},{3,7},{4,0},{5,1},{6,2},{7,3},{8,12},{9,13},{10,... | collective-permute-start | bytes 294920 | tf_op jit(solution)/shard_map/ppermute | solution.py:386
  62.0 9.3 %collective-permute-start.40 = (bf16[96,512]{1,0:T(8,128)(2,1)S(1)}, bf16[96,512]{1,0:T(8,128)(2,1)S(1)}, u32[]{:S(2)}, u32[]{:S(2)}) collective-permute-start(bf16[96,512]{1,0:T(8,128)(2,1)S(1)} %get-tuple-element.144), channel_id=1, source_target_pairs={{0,2},{1,3},{2,0},{3,1},{4,6},{5,7},{6,4},{7,5},{8,10},{9,11},{10,... | collective-permute-start | bytes 294920 | tf_op jit(solution)/shard_map/ppermute | solution.py:386
  (1 other events, 1.0 us)

commit v15 on v12

--- a/solution.py
+++ b/solution.py
@@ -26,6 +26,11 @@
     return lax.dot_general(a, b, (((0,), (0,)), ((), ())), preferred_element_type=F32)
 
 
+def stacked(product, first, second, tokens):
+    both_rows = product(jnp.concatenate([first, second], axis=0), tokens)
+    return both_rows[: first.shape[0]], both_rows[first.shape[0] :]
+
+
 def silu_parts(hidden):
     sigmoid_value = jax.nn.sigmoid(hidden)
     silu_value = hidden * sigmoid_value
@@ -67,7 +72,7 @@
 
 
 def update_forward(w1t, w3t, w2, keys, push):
-    gate_pre, up_pre = nt(w1t, keys), nt(w3t, keys)
+    gate_pre, up_pre = stacked(nt, w1t, w3t, keys)
     silu, slope, curvature = silu_parts(gate_pre)
     mixed = (silu * up_pre).astype(BF16)
     down_back = nn(w2, push)
@@ -78,7 +83,7 @@
 
 
 def apply_forward(f1t, f3t, f2t, queries, weighted):
-    q_gate, q_up = nt(f1t, queries), nt(f3t, queries)
+    q_gate, q_up = stacked(nt, f1t, f3t, queries)
     silu, slope, _ = silu_parts(q_gate)
     mixed = (silu * q_up).astype(BF16)
     output = nn(f2t, mixed)
@@ -98,7 +103,7 @@
 
 
 def second_by_gate_and_up(c1t, c3t, keys, up_slope, silu, back_slope, back_curve):
-    gate_bar, up_bar = nt(c1t, keys), nt(c3t, keys)
+    gate_bar, up_bar = stacked(nt, c1t, c3t, keys)
     down_back_bar = (gate_bar * up_slope + up_bar * silu).astype(BF16)
     return down_back_bar, gate_bar * back_slope, up_bar * back_slope + gate_bar * back_curve
 
@@ -202,7 +207,7 @@
     gate_ref, up_ref, down_ref, tokens, hidden = operands
     parity = lax.axis_index("tok") // CORES % 2
     order = [2 * k + p for p in (parity, 1 - parity) for k in range(chips // 2)]
-    sums = [nn(rows_of_core(ref, order, chips), tokens) for ref in (gate_ref, up_ref)]
+    sums = list(stacked(nn, *(rows_of_core(x, order, chips) for x in (gate_ref, up_ref)), tokens))
     sums.append(fold(nt(rows_of_core(down_ref, order, chips), hidden), chips, folds))
     half = outs[0].shape[0]
     for k, total in enumerate(sums):
@@ -338,7 +343,7 @@
         c2t[...], push[...], up_slope[...], silu[...], up_part[...], gate_part[...]
     )
     keys, order = both(ko, kx), pieces_order(chips)
-    sums = [nn(rows_of_core(ref, order, chips), keys) for ref in (gate, up)] + [down[...]]
+    sums = [*stacked(nn, *(rows_of_core(x, order, chips) for x in (gate, up)), keys), down[...]]
     g = sums[0].shape[0] // chips
     for k, out in enumerate(outs):
         parts = [x[k * g : (k + 1) * g] for x in sums]

time: 72 us -> 71.9 us (level)
  no operation moved by 1% of the time
where the time goes in v15:
time: 71.9 us; the launch traced here: 71.8 us
  starting transfers between devices  38.3 us (53%)
  waiting for transfers between devices  21 us (29%)
  Pallas kernels  9.52 us (13%)
  local copies, waits for them, and re-layouts  2.12 us (3%)
  between operations  0.88 us (1%)
    ppermute x18, starting transfers between devices, to_chip(): return lax.ppermute(x, 'tok', chip_perm(chips * CORES, step))  27 us
    ppermute x18, waiting for transfers between devices, to_chip(): return lax.ppermute(x, 'tok', chip_perm(chips * CORES, step))  11.6 us
    pallas_call x21, Pallas kernels, call(): pl.pallas_call(kernel, out_shape=[jax.ShapeDtypeStruct(s, t) for s, t in...  9.52 us
    ppermute x3, waiting for transfers between devices, exchange(): lax.ppermute(pieces[s], 'tok', chip_perm(count, s))  4.87 us
    ppermute x3, starting transfers between devices, exchange(): lax.ppermute(pieces[s], 'tok', chip_perm(count, s))  4.45 us
    ppermute x3, starting transfers between devices, head_parts(): lax.ppermute(part, 'head', [(h, partner(h, step, heads)) for h in range(h...  3.55 us
    ppermute x3, waiting for transfers between devices, head_parts(): lax.ppermute(part, 'head', [(h, partner(h, step, heads)) for h in range(h...  3.25 us
    unnamed x18, local copies, waits for them, and re-layouts  2.12 us
  transfers between devices with their start and end apart: 41, of which 22 were waited for; matrix products, arithmetic and copies ran while one was open for 2% of the time, Pallas kernels for 9%

profile of v15, /device:TPU:0, one launch (start us, length us, event | category | flops | bytes accessed | tf_op | source)
XLA Modules:
  0.0 71.8 jit_solution(13909992679876118643)
XLA Ops:
  0.6 0.5 collective-permute-start.1
  1.8 1.1 %copy.15 = bf16[1,512,256]{1,2,0:T(8,128)(2,1)S(1)} copy(bf16[1,512,256]{2,1,0:T(8,128)(2,1)} %param.15) | data formatting | bytes 524288 | tf_op args[6]
  3.1 0.7 %copy-done = bf16[256,512]{1,0:T(8,128)(2,1)S(1)} copy-done((bf16[256,512]{1,0:T(8,128)(2,1)S(1)}, bf16[256,512]{1,0:T(8,128)(2,1)}, u32[]{:S(2)}) %copy-start) | copy-done | bytes 262168
  4.0 1.1 %update.1 = (f32[64,512]{1,0:T(8,128)S(1)}, f32[64,512]{1,0:T(8,128)S(1)}, f32[64,512]{1,0:T(8,128)S(1)}, bf16[64,512]{1,0:T(8,128)(2,1)S(1)}, bf16[64,512]{1,0:T(8,128)(2,1)S(1)}, /*index=5*/bf16[64,512]{1,0:T(8,128)(2,1)S(1)}) custom-call(bf16[256,512]{1,0:T(8,128)(2,1)S(1)} %copy-done, bf16[256,512]{1,0:T(8,128)(2,1)S(1)} %collective-permute-done.kx.refs_9_.refs_5_, ...), custom_call_target="tpu_custom_call" | custom-call | flops 805306368 | bytes 1837056 | tf_op jit(solution)/shard_map/update/pallas_call | solution.py:368
  5.1 3.1 %collective-permute-start.8 = (bf16[64,512]{1,0:T(8,128)(2,1)S(1)}, bf16[64,512]{1,0:T(8,128)(2,1)S(1)}, u32[]{:S(2)}, u32[]{:S(2)}) collective-permute-start(bf16[64,512]{1,0:T(8,128)(2,1)S(1)} %get-tuple-element.88), channel_id=1, source_target_pairs={{0,2},{1,3},{2,0},{3,1},{4,6},{5,7},{6,4},{7,5},{8,10},{9,11},{10,... | collective-permute-start | bytes 196616 | tf_op jit(solution)/shard_map/ppermute | solution.py:391
  8.3 1.9 %collective-permute-start.6 = (bf16[64,512]{1,0:T(8,128)(2,1)S(1)}, bf16[64,512]{1,0:T(8,128)(2,1)S(1)}, u32[]{:S(2)}, u32[]{:S(2)}) collective-permute-start(bf16[64,512]{1,0:T(8,128)(2,1)S(1)} %get-tuple-element.84), channel_id=1, source_target_pairs={{0,2},{1,3},{2,0},{3,1},{4,6},{5,7},{6,4},{7,5},{8,10},{9,11},{10,... | collective-permute-start | bytes 196616 | tf_op jit(solution)/shard_map/ppermute | solution.py:391
  10.5 3.0 %collective-permute-start.9 = (bf16[64,512]{1,0:T(8,128)(2,1)S(1)}, bf16[64,512]{1,0:T(8,128)(2,1)S(1)}, u32[]{:S(2)}, u32[]{:S(2)}) collective-permute-start(bf16[64,512]{1,0:T(8,128)(2,1)S(1)} %carry.8.refs_0_), channel_id=1, source_target_pairs={{0,4},{1,5},{2,6},{3,7},{4,0},{5,1},{6,2},{7,3},{8,12},{9,13},{10,... | collective-permute-start | bytes 196616 | tf_op jit(solution)/shard_map/ppermute | solution.py:391
  13.5 2.2 %collective-permute-start.5 = (bf16[64,512]{1,0:T(8,128)(2,1)S(1)}, bf16[64,512]{1,0:T(8,128)(2,1)S(1)}, u32[]{:S(2)}, u32[]{:S(2)}) collective-permute-start(bf16[64,512]{1,0:T(8,128)(2,1)S(1)} %carry.6.refs_0_), channel_id=1, source_target_pairs={{0,4},{1,5},{2,6},{3,7},{4,0},{5,1},{6,2},{7,3},{8,12},{9,13},{10,... | collective-permute-start | bytes 196616 | tf_op jit(solution)/shard_map/ppermute | solution.py:391
  15.8 1.4 %collective-permute-start.7 = (bf16[64,512]{1,0:T(8,128)(2,1)S(1)}, bf16[64,512]{1,0:T(8,128)(2,1)S(1)}, u32[]{:S(2)}, u32[]{:S(2)}) collective-permute-start(bf16[64,512]{1,0:T(8,128)(2,1)S(1)} %carry.7.refs_0_), channel_id=1, source_target_pairs={{0,4},{1,5},{2,6},{3,7},{4,0},{5,1},{6,2},{7,3},{8,12},{9,13},{10,... | collective-permute-start | bytes 196616 | tf_op jit(solution)/shard_map/ppermute | solution.py:391
  17.1 1.1 %saved.1 = (bf16[512,512]{1,0:T(8,128)(2,1)S(1)}, f32[256,512]{1,0:T(8,128)S(1)}, f32[256,512]{1,0:T(8,128)S(1)}, f32[256,512]{1,0:T(8,128)S(1)}, f32[256,512]{1...) custom-call(bf16[256,512]{1,0:T(8,128)(2,1)S(1)} %copy-done, ...), custom_call_target="tpu_custom_call" | custom-call | flops 402653184 | bytes 2363392 | tf_op jit(solution)/shard_map/saved/pallas_call | solution.py:368
  18.4 2.7 %collective-permute-start.16 = (bf16[64,512]{1,0:T(8,128)(2,1)S(1)}, bf16[64,512]{1,0:T(8,128)(2,1)S(1)}, u32[]{:S(2)}, u32[]{:S(2)}) collective-permute-start(bf16[64,512]{1,0:T(8,128)(2,1)S(1)} %get-tuple-element.93.refs_8_), channel_id=1, source_target_pairs={{0,2},{1,3},{2,0},{3,1},{4,6},{5,7},{6,4},{7,5},{8,10},{9,11},{10,... | collective-permute-start | bytes 196616 | tf_op jit(solution)/shard_map/ppermute | solution.py:391
  21.3 1.2 %collective-permute-start.10 = (bf16[64,512]{1,0:T(8,128)(2,1)S(1)}, bf16[64,512]{1,0:T(8,128)(2,1)S(1)}, u32[]{:S(2)}, u32[]{:S(2)}) collective-permute-start(bf16[64,512]{1,0:T(8,128)(2,1)S(1)} %get-tuple-element.91.refs_0_), channel_id=1, source_target_pairs={{0,2},{1,3},{2,0},{3,1},{4,6},{5,7},{6,4},{7,5},{8,10},{9,11},{10,... | collective-permute-start | bytes 196616 | tf_op jit(solution)/shard_map/ppermute | solution.py:391
  23.1 0.5 collective-permute-start.13
  23.9 2.0 %collective-permute-done.10.refs_1_ = bf16[64,512]{1,0:T(8,128)(2,1)S(1)} collective-permute-done((bf16[64,512]{1,0:T(8,128)(2,1)S(1)}, bf16[64,512]{1,0:T(8,128)(2,1)S(1)}, u32[]{:S(2)}, u32[]{:S(2)}) %collective-permute-start.10) | collective-permute-done | bytes 65568 | tf_op jit(solution)/shard_map/ppermute | solution.py:391
  25.9 0.5 collective-permute-start.14
  26.4 1.1 %collective-permute-done.13.refs_5_ = bf16[64,512]{1,0:T(8,128)(2,1)S(1)} collective-permute-done((bf16[64,512]{1,0:T(8,128)(2,1)S(1)}, bf16[64,512]{1,0:T(8,128)(2,1)S(1)}, u32[]{:S(2)}, u32[]{:S(2)}) %collective-permute-start.13) | collective-permute-done | bytes 65568 | tf_op jit(solution)/shard_map/ppermute | solution.py:391
  27.4 0.5 collective-permute-start.17
  28.0 0.7 collective-permute-done.15.refs_7_
  29.2 0.9 %apply.1 = (bf16[256,512]{1,0:T(8,128)(2,1)S(1)}, bf16[256,512]{1,0:T(8,128)(2,1)S(1)}, bf16[512,256]{1,0:T(8,128)(2,1)S(1)}, f32[512,512]{1,0:T(8,128)S(1)}, bf...) custom-call(bf16[64,512]{1,0:T(8,128)(2,1)S(1)} %get-tuple-element.91.refs_0, ...), custom_call_target="tpu_custom_call" | custom-call | flops 402653184 | bytes 2359296 | tf_op jit(solution)/shard_map/apply/pallas_call | solution.py:368
  30.1 2.7 %collective-permute-start.22 = (f32[2,512]{1,0:T(2,128)S(1)}, f32[2,512]{1,0:T(2,128)S(1)}, u32[]{:S(2)}, u32[]{:S(2)}) collective-permute-start(f32[2,512]{1,0:T(2,128)S(1)} %get-tuple-element.95.refs_0_), channel_id=1, source_target_pairs={{0,24},{8,16},{16,8},{24,0},{1,25},{9,17},{17,9},{25,1},{2,26},{10... | collective-permute-start | bytes 12296 | tf_op jit(solution)/shard_map/ppermute | solution.py:409
  33.7 1.0 %collective-permute-done.22.refs_3_ = f32[2,512]{1,0:T(2,128)S(1)} collective-permute-done((f32[2,512]{1,0:T(2,128)S(1)}, f32[2,512]{1,0:T(2,128)S(1)}, u32[]{:S(2)}, u32[]{:S(2)}) %collective-permute-start.22) | collective-permute-done | bytes 4128 | tf_op jit(solution)/shard_map/ppermute | solution.py:409
  34.7 1.7 %collective-permute-done.21.refs_2_ = f32[2,512]{1,0:T(2,128)S(1)} collective-permute-done((f32[2,512]{1,0:T(2,128)S(1)}, f32[2,512]{1,0:T(2,128)S(1)}, u32[]{:S(2)}, u32[]{:S(2)}) %collective-permute-start.21) | collective-permute-done | bytes 4128 | tf_op jit(solution)/shard_map/ppermute | solution.py:409
  36.9 0.8 %apply_back.1 = (bf16[256,256]{1,0:T(8,128)(2,1)S(1)}, bf16[256,256]{1,0:T(8,128)(2,1)S(1)}, f32[64,512]{1,0:T(8,128)S(1)}, f32[64,512]{1,0:T(8,128)S(1)}, f32[6...) custom-call(f32[2,512]{1,0:T(2,128)S(1)} %get-tuple-element.95.refs_0, ...), custom_call_target="tpu_custom_call" | custom-call | flops 536870912 | bytes 4210688 | tf_op jit(solution)/shard_map/apply_back/pallas_call | solution.py:368
  37.8 0.6 collective-permute-start.25
  38.4 1.5 %collective-permute-start.23 = (bf16[64,512]{1,0:T(8,128)(2,1)S(1)}, bf16[64,512]{1,0:T(8,128)(2,1)S(1)}, u32[]{:S(2)}, u32[]{:S(2)}) collective-permute-start(bf16[64,512]{1,0:T(8,128)(2,1)S(1)} %get-tuple-element.108), channel_id=1, source_target_pairs={{0,2},{1,3},{2,0},{3,1},{4,6},{5,7},{6,4},{7,5},{8,10},{9,11},{10,... | collective-permute-start | bytes 196616 | tf_op jit(solution)/shard_map/ppermute | solution.py:391
  39.8 0.6 collective-permute-start.27
  40.4 1.7 %collective-permute-done.25.got = bf16[64,512]{1,0:T(8,128)(2,1)S(1)} collective-permute-done((bf16[64,512]{1,0:T(8,128)(2,1)S(1)}, bf16[64,512]{1,0:T(8,128)(2,1)S(1)}, u32[]{:S(2)}, u32[]{:S(2)}) %collective-permute-start.25) | collective-permute-done | bytes 65568 | tf_op jit(solution)/shard_map/ppermute | solution.py:391
  42.1 3.4 %collective-permute-start.26 = (bf16[64,512]{1,0:T(8,128)(2,1)S(1)}, bf16[64,512]{1,0:T(8,128)(2,1)S(1)}, u32[]{:S(2)}, u32[]{:S(2)}) collective-permute-start(bf16[64,512]{1,0:T(8,128)(2,1)S(1)} %carry.10.refs_0_), channel_id=1, source_target_pairs={{0,4},{1,5},{2,6},{3,7},{4,0},{5,1},{6,2},{7,3},{8,12},{9,13},{10,... | collective-permute-start | bytes 196616 | tf_op jit(solution)/shard_map/ppermute | solution.py:391
  45.6 0.7 collective-permute-start.24
  46.3 2.4 %collective-permute-start.28 = (bf16[64,512]{1,0:T(8,128)(2,1)S(1)}, bf16[64,512]{1,0:T(8,128)(2,1)S(1)}, u32[]{:S(2)}, u32[]{:S(2)}) collective-permute-start(bf16[64,512]{1,0:T(8,128)(2,1)S(1)} %carry.11.refs_0_), channel_id=1, source_target_pairs={{0,4},{1,5},{2,6},{3,7},{4,0},{5,1},{6,2},{7,3},{8,12},{9,13},{10,... | collective-permute-start | bytes 196616 | tf_op jit(solution)/shard_map/ppermute | solution.py:391
  48.6 1.2 %collective-permute-done.26.refs_1_ = bf16[64,512]{1,0:T(8,128)(2,1)S(1)} collective-permute-done((bf16[64,512]{1,0:T(8,128)(2,1)S(1)}, bf16[64,512]{1,0:T(8,128)(2,1)S(1)}, u32[]{:S(2)}, u32[]{:S(2)}) %collective-permute-start.26) | collective-permute-done | bytes 65568 | tf_op jit(solution)/shard_map/ppermute | solution.py:391
  50.0 1.3 %collective-permute-done.24.refs_1_ = bf16[64,512]{1,0:T(8,128)(2,1)S(1)} collective-permute-done((bf16[64,512]{1,0:T(8,128)(2,1)S(1)}, bf16[64,512]{1,0:T(8,128)(2,1)S(1)}, u32[]{:S(2)}, u32[]{:S(2)}) %collective-permute-start.24) | collective-permute-done | bytes 65568 | tf_op jit(solution)/shard_map/ppermute | solution.py:391
  51.4 0.8 %collective-permute-start.29 = (bf16[64,512]{1,0:T(8,128)(2,1)S(1)}, bf16[64,512]{1,0:T(8,128)(2,1)S(1)}, u32[]{:S(2)}, u32[]{:S(2)}) collective-permute-start(bf16[64,512]{1,0:T(8,128)(2,1)S(1)} %get-tuple-element.119.refs_0_), channel_id=1, source_target_pairs={{0,2},{1,3},{2,0},{3,1},{4,6},{5,7},{6,4},{7,5},{8,10},{9,11},{10,... | collective-permute-start | bytes 196616 | tf_op jit(solution)/shard_map/ppermute | solution.py:391
  52.9 0.9 %collective-permute-start.35 = (bf16[64,512]{1,0:T(8,128)(2,1)S(1)}, bf16[64,512]{1,0:T(8,128)(2,1)S(1)}, u32[]{:S(2)}, u32[]{:S(2)}) collective-permute-start(bf16[64,512]{1,0:T(8,128)(2,1)S(1)} %get-tuple-element.127.refs_0_), channel_id=1, source_target_pairs={{0,2},{1,3},{2,0},{3,1},{4,6},{5,7},{6,4},{7,5},{8,10},{9,11},{10,... | collective-permute-start | bytes 196616 | tf_op jit(solution)/shard_map/ppermute | solution.py:391
  53.8 0.5 collective-permute-done.32.refs_5_
  54.3 1.5 %collective-permute-done.29.refs_1_ = bf16[64,512]{1,0:T(8,128)(2,1)S(1)} collective-permute-done((bf16[64,512]{1,0:T(8,128)(2,1)S(1)}, bf16[64,512]{1,0:T(8,128)(2,1)S(1)}, u32[]{:S(2)}, u32[]{:S(2)}) %collective-permute-start.29) | collective-permute-done | bytes 65568 | tf_op jit(solution)/shard_map/ppermute | solution.py:391
  55.8 0.5 collective-permute-start.33
  56.3 0.9 %collective-permute-done.35.refs_1_ = bf16[64,512]{1,0:T(8,128)(2,1)S(1)} collective-permute-done((bf16[64,512]{1,0:T(8,128)(2,1)S(1)}, bf16[64,512]{1,0:T(8,128)(2,1)S(1)}, u32[]{:S(2)}, u32[]{:S(2)}) %collective-permute-start.35) | collective-permute-done | bytes 65568 | tf_op jit(solution)/shard_map/ppermute | solution.py:391
  57.2 0.5 collective-permute-start.37
  57.7 0.8 %second_first.1 = (bf16[256,512]{1,0:T(8,128)(2,1)S(1)}, bf16[256,512]{1,0:T(8,128)(2,1)S(1)}, bf16[256,256]{1,0:T(8,128)(2,1)S(1)}, f32[128,512]{1,0:T(8,128)S(...) custom-call(bf16[64,512]{1,0:T(8,128)(2,1)S(1)} %get-tuple-element.119.refs_0_, ...), custom_call_target="tpu_custom_call" | custom-call | flops 402653184 | bytes 3670016 | tf_op jit(solution)/shard_map/second_first/pallas_call | solution.py:368
  58.6 0.7 %second_last.1 = (bf16[512,256]{1,0:T(8,128)(2,1)S(1)}, bf16[256,256]{1,0:T(8,128)(2,1)S(1)}, bf16[256,256]{1,0:T(8,128)(2,1)S(1)}, f32[96,512]{1,0:T(8,128)S(1)...) custom-call(bf16[64,512]{1,0:T(8,128)(2,1)S(1)} %get-tuple-element.127.refs_0_, ...), custom_call_target="tpu_custom_call" | custom-call | flops 402653184 | bytes 3670016 | tf_op jit(solution)/shard_map/second_last/pallas_call | solution.py:368
  59.4 2.3 %collective-permute-start.38 = (bf16[96,512]{1,0:T(8,128)(2,1)S(1)}, bf16[96,512]{1,0:T(8,128)(2,1)S(1)}, u32[]{:S(2)}, u32[]{:S(2)}) collective-permute-start(bf16[96,512]{1,0:T(8,128)(2,1)S(1)} %get-tuple-element.144), channel_id=1, source_target_pairs={{0,6},{1,7},{2,4},{3,5},{4,2},{5,3},{6,0},{7,1},{8,14},{9,15},{10,... | collective-permute-start | bytes 294920 | tf_op jit(solution)/shard_map/ppermute | solution.py:386
  61.7 2.1 %collective-permute-start.40 = (bf16[96,512]{1,0:T(8,128)(2,1)S(1)}, bf16[96,512]{1,0:T(8,128)(2,1)S(1)}, u32[]{:S(2)}, u32[]{:S(2)}) collective-permute-start(bf16[96,512]{1,0:T(8,128)(2,1)S(1)} %get-tuple-element.146), channel_id=1, source_target_pairs={{0,2},{1,3},{2,0},{3,1},{4,6},{5,7},{6,4},{7,5},{8,10},{9,11},{10,... | collective-permute-start | bytes 294920 | tf_op jit(solution)/shard_map/ppermute | solution.py:386
  63.8 1.0 %query_grad.1 = bf16[256,512]{1,0:T(8,128)(2,1)} custom-call(bf16[256,256]{1,0:T(8,128)(2,1)S(1)} %get-tuple-element.101.gate_back, bf16[256,256]{1,0:T(8,128)(2,1)S(1)} %get-tuple-element.102.up_back, bf16[256,512]{1,0:T(8,128)(2,1)S(1)} %get-tuple-element.103.f1t, bf16[256,512]{1,0:T(8,128)(2,1)S(1)} %get-tuple-element.104.f3t), custom_call_target="tpu_custom_call" | custom-call | flops 134217728 | bytes 786432 | tf_op jit(solution)/shard_map/query_grad/pallas_call | solution.py:368
  64.9 1.4 %token_grads.1 = (bf16[256,512]{1,0:T(8,128)(2,1)}, bf16[256,512]{1,0:T(8,128)(2,1)}) custom-call(f32[1,256]{1,0:T(1,128)S(1)} %bitcast.30, bf16[256,256]{1,0:T(8,128)(2,1)S(1)} %get-tuple-element.105.refs_1_, bf16[256,256]{1,0:T(8,128)(2,1)S(1)} %get-tuple-element.126.refs_2_, bf16[256,256]{1,0:T(8,128)(2,1)S(1)} %get-tuple-element.131.refs_3_, ...), custom_call_target="tpu_custom_call" | custom-call | flops 402653184 | bytes 2360320 | tf_op jit(solution)/shard_map/token_grads/pallas_call | solution.py:368
  66.2 0.7 %collective-permute-done.38.refs_4_ = bf16[96,512]{1,0:T(8,128)(2,1)S(1)} collective-permute-done((bf16[96,512]{1,0:T(8,128)(2,1)S(1)}, bf16[96,512]{1,0:T(8,128)(2,1)S(1)}, u32[]{:S(2)}, u32[]{:S(2)}) %collective-permute-start.38) | collective-permute-done | bytes 98336 | tf_op jit(solution)/shard_map/ppermute | solution.py:386
  66.9 4.1 %collective-permute-done.39.refs_5_ = bf16[96,512]{1,0:T(8,128)(2,1)S(1)} collective-permute-done((bf16[96,512]{1,0:T(8,128)(2,1)S(1)}, bf16[96,512]{1,0:T(8,128)(2,1)S(1)}, u32[]{:S(2)}, u32[]{:S(2)}) %collective-permute-start.39) | collective-permute-done | bytes 98336 | tf_op jit(solution)/shard_map/ppermute | solution.py:386
  71.1 0.7 owner_result.1
  (73 shorter events, 5.7 us)
Async XLA Ops:
  0.6 1.0 %copy-start.5 = (f32[256,1]{0,1:T(1,128)S(1)}, f32[256,1]{0,1:T(1,128)}, u32[]{:S(2)}) copy-start(f32[256,1]{0,1:T(1,128)} %param.13) | copy-start | bytes 3076
  0.6 2.5 %collective-permute-start.1 = (bf16[256,512]{1,0:T(8,128)(2,1)}, bf16[256,512]{1,0:T(8,128)(2,1)S(1)}, u32[]{:S(2)}, u32[]{:S(2)}) collective-permute-start(bf16[256,512]{1,0:T(8,128)(2,1)} %vo.3), channel_id=1, source_target_pairs={{0,1},{1,0},{2,3},{3,2},{4,5},{5,4},{6,7},{7,6},{8,9},{9,8},{10,11... | collective-permute-start | bytes 786440 | tf_op jit(solution)/shard_map/ppermute | solution.py:507
  1.2 2.0 %collective-permute-start = (bf16[256,512]{1,0:T(8,128)(2,1)}, bf16[256,512]{1,0:T(8,128)(2,1)S(1)}, u32[]{:S(2)}, u32[]{:S(2)}) collective-permute-start(bf16[256,512]{1,0:T(8,128)(2,1)} %refs_4_.1), channel_id=1, source_target_pairs={{0,1},{1,0},{2,3},{3,2},{4,5},{5,4},{6,7},{7,6},{8,9},{9,8},{10,11... | collective-permute-start | bytes 786440 | tf_op jit(solution)/shard_map/ppermute | solution.py:507
  1.2 15.9 %collective-permute-start.3 = (bf16[256,512]{1,0:T(8,128)(2,1)}, bf16[256,512]{1,0:T(8,128)(2,1)S(1)}, u32[]{:S(2)}, u32[]{:S(2)}) collective-permute-start(bf16[256,512]{1,0:T(8,128)(2,1)} %go.1), channel_id=1, source_target_pairs={{0,1},{1,0},{2,3},{3,2},{4,5},{5,4},{6,7},{7,6},{8,9},{9,8},{10,11... | collective-permute-start | bytes 786440 | tf_op jit(solution)/shard_map/ppermute | solution.py:507
  1.7 1.2 %copy-start.7 = (bf16[1,512,256]{2,1,0:T(8,128)(2,1)S(1)}, bf16[1,512,256]{2,1,0:T(8,128)(2,1)}, u32[]{:S(2)}) copy-start(bf16[1,512,256]{2,1,0:T(8,128)(2,1)} %param.16) | copy-start | bytes 786436
  1.7 1.4 %collective-permute-start.2 = (f32[1,256]{1,0:T(1,128)S(1)}, f32[1,256]{1,0:T(1,128)S(1)}, u32[]{:S(2)}, u32[]{:S(2)}) collective-permute-start(f32[1,256]{1,0:T(1,128)S(1)} %bitcast.27), channel_id=1, source_target_pairs={{0,1},{1,0},{2,3},{3,2},{4,5},{5,4},{6,7},{7,6},{8,9},{9,8},{10,11... | collective-permute-start | bytes 3080 | tf_op jit(solution)/shard_map/ppermute | solution.py:507
  1.8 1.4 %copy-start.3 = (bf16[256,512]{1,0:T(8,128)(2,1)S(1)}, bf16[256,512]{1,0:T(8,128)(2,1)}, u32[]{:S(2)}) copy-start(bf16[256,512]{1,0:T(8,128)(2,1)} %vo.3) | copy-start | bytes 786436
  2.9 1.0 %copy-start.2 = (bf16[1,256,512]{2,1,0:T(8,128)(2,1)S(1)}, bf16[1,256,512]{2,1,0:T(8,128)(2,1)}, u32[]{:S(2)}) copy-start(bf16[1,256,512]{2,1,0:T(8,128)(2,1)} %param.17) | copy-start | bytes 786436
  4.0 4.2 %copy-start.1 = (bf16[256,512]{1,0:T(8,128)(2,1)S(1)}, bf16[256,512]{1,0:T(8,128)(2,1)}, u32[]{:S(2)}) copy-start(bf16[256,512]{1,0:T(8,128)(2,1)} %refs_10_.1) | copy-start | bytes 786436
  5.1 5.4 %collective-permute-start.8 = (bf16[64,512]{1,0:T(8,128)(2,1)S(1)}, bf16[64,512]{1,0:T(8,128)(2,1)S(1)}, u32[]{:S(2)}, u32[]{:S(2)}) collective-permute-start(bf16[64,512]{1,0:T(8,128)(2,1)S(1)} %get-tuple-element.88), channel_id=1, source_target_pairs={{0,2},{1,3},{2,0},{3,1},{4,6},{5,7},{6,4},{7,5},{8,10},{9,11},{10,... | collective-permute-start | bytes 196616 | tf_op jit(solution)/shard_map/ppermute | solution.py:391
  8.2 19.3 %collective-permute-start.19 = (bf16[256,512]{1,0:T(8,128)(2,1)S(1)}, bf16[256,512]{1,0:T(8,128)(2,1)S(1)}, u32[]{:S(2)}, u32[]{:S(2)}) collective-permute-start(bf16[256,512]{1,0:T(8,128)(2,1)S(1)} %copy-done.1), channel_id=1, source_target_pairs={{0,1},{1,0},{2,3},{3,2},{4,5},{5,4},{6,7},{7,6},{8,9},{9,8},{10,11... | collective-permute-start | bytes 786440 | tf_op jit(solution)/shard_map/ppermute | solution.py:507
  8.2 5.4 %collective-permute-start.4 = (bf16[64,512]{1,0:T(8,128)(2,1)S(1)}, bf16[64,512]{1,0:T(8,128)(2,1)S(1)}, u32[]{:S(2)}, u32[]{:S(2)}) collective-permute-start(bf16[64,512]{1,0:T(8,128)(2,1)S(1)} %get-tuple-element.80), channel_id=1, source_target_pairs={{0,2},{1,3},{2,0},{3,1},{4,6},{5,7},{6,4},{7,5},{8,10},{9,11},{10,... | collective-permute-start | bytes 196616 | tf_op jit(solution)/shard_map/ppermute | solution.py:391
  8.3 7.4 %collective-permute-start.6 = (bf16[64,512]{1,0:T(8,128)(2,1)S(1)}, bf16[64,512]{1,0:T(8,128)(2,1)S(1)}, u32[]{:S(2)}, u32[]{:S(2)}) collective-permute-start(bf16[64,512]{1,0:T(8,128)(2,1)S(1)} %get-tuple-element.84), channel_id=1, source_target_pairs={{0,2},{1,3},{2,0},{3,1},{4,6},{5,7},{6,4},{7,5},{8,10},{9,11},{10,... | collective-permute-start | bytes 196616 | tf_op jit(solution)/shard_map/ppermute | solution.py:391
  10.5 7.7 %collective-permute-start.9 = (bf16[64,512]{1,0:T(8,128)(2,1)S(1)}, bf16[64,512]{1,0:T(8,128)(2,1)S(1)}, u32[]{:S(2)}, u32[]{:S(2)}) collective-permute-start(bf16[64,512]{1,0:T(8,128)(2,1)S(1)} %carry.8.refs_0_), channel_id=1, source_target_pairs={{0,4},{1,5},{2,6},{3,7},{4,0},{5,1},{6,2},{7,3},{8,12},{9,13},{10,... | collective-permute-start | bytes 196616 | tf_op jit(solution)/shard_map/ppermute | solution.py:391
  13.5 3.6 %copy-start.4 = (bf16[256,512]{1,0:T(8,128)(2,1)S(1)}, bf16[256,512]{1,0:T(8,128)(2,1)}, u32[]{:S(2)}) copy-start(bf16[256,512]{1,0:T(8,128)(2,1)} %go.1) | copy-start | bytes 786436
  13.5 7.7 %collective-permute-start.5 = (bf16[64,512]{1,0:T(8,128)(2,1)S(1)}, bf16[64,512]{1,0:T(8,128)(2,1)S(1)}, u32[]{:S(2)}, u32[]{:S(2)}) collective-permute-start(bf16[64,512]{1,0:T(8,128)(2,1)S(1)} %carry.6.refs_0_), channel_id=1, source_target_pairs={{0,4},{1,5},{2,6},{3,7},{4,0},{5,1},{6,2},{7,3},{8,12},{9,13},{10,... | collective-permute-start | bytes 196616 | tf_op jit(solution)/shard_map/ppermute | solution.py:391
  15.7 1.4 %copy-start.6 = (f32[512]{0:T(512)S(1)}, f32[512]{0:T(512)}, u32[]{:S(2)}) copy-start(f32[512]{0:T(512)} %param.14) | copy-start | bytes 6148
  15.8 7.2 %collective-permute-start.7 = (bf16[64,512]{1,0:T(8,128)(2,1)S(1)}, bf16[64,512]{1,0:T(8,128)(2,1)S(1)}, u32[]{:S(2)}, u32[]{:S(2)}) collective-permute-start(bf16[64,512]{1,0:T(8,128)(2,1)S(1)} %carry.7.refs_0_), channel_id=1, source_target_pairs={{0,4},{1,5},{2,6},{3,7},{4,0},{5,1},{6,2},{7,3},{8,12},{9,13},{10,... | collective-permute-start | bytes 196616 | tf_op jit(solution)/shard_map/ppermute | solution.py:391
  18.4 5.4 %collective-permute-start.16 = (bf16[64,512]{1,0:T(8,128)(2,1)S(1)}, bf16[64,512]{1,0:T(8,128)(2,1)S(1)}, u32[]{:S(2)}, u32[]{:S(2)}) collective-permute-start(bf16[64,512]{1,0:T(8,128)(2,1)S(1)} %get-tuple-element.93.refs_8_), channel_id=1, source_target_pairs={{0,2},{1,3},{2,0},{3,1},{4,6},{5,7},{6,4},{7,5},{8,10},{9,11},{10,... | collective-permute-start | bytes 196616 | tf_op jit(solution)/shard_map/ppermute | solution.py:391
  21.3 4.5 %collective-permute-start.10 = (bf16[64,512]{1,0:T(8,128)(2,1)S(1)}, bf16[64,512]{1,0:T(8,128)(2,1)S(1)}, u32[]{:S(2)}, u32[]{:S(2)}) collective-permute-start(bf16[64,512]{1,0:T(8,128)(2,1)S(1)} %get-tuple-element.91.refs_0_), channel_id=1, source_target_pairs={{0,2},{1,3},{2,0},{3,1},{4,6},{5,7},{6,4},{7,5},{8,10},{9,11},{10,... | collective-permute-start | bytes 196616 | tf_op jit(solution)/shard_map/ppermute | solution.py:391
  23.1 4.3 %collective-permute-start.13 = (bf16[64,512]{1,0:T(8,128)(2,1)S(1)}, bf16[64,512]{1,0:T(8,128)(2,1)S(1)}, u32[]{:S(2)}, u32[]{:S(2)}) collective-permute-start(bf16[64,512]{1,0:T(8,128)(2,1)S(1)} %get-tuple-element.92.refs_4_), channel_id=1, source_target_pairs={{0,2},{1,3},{2,0},{3,1},{4,6},{5,7},{6,4},{7,5},{8,10},{9,11},{10,... | collective-permute-start | bytes 196616 | tf_op jit(solution)/shard_map/ppermute | solution.py:391
  23.9 4.1 %collective-permute-start.18 = (bf16[64,512]{1,0:T(8,128)(2,1)S(1)}, bf16[64,512]{1,0:T(8,128)(2,1)S(1)}, u32[]{:S(2)}, u32[]{:S(2)}) collective-permute-start(bf16[64,512]{1,0:T(8,128)(2,1)S(1)} %collective-permute-done.16.refs_9_), channel_id=1, source_target_pairs={{0,1},{1,0},{2,3},{3,2},{4,5},{5,4},{6,7},{7,6},{8,9},{9,8},{10,11... | collective-permute-start | bytes 196616 | tf_op jit(solution)/shard_map/ppermute | solution.py:402
  25.9 2.8 %collective-permute-start.11 = (bf16[64,512]{1,0:T(8,128)(2,1)S(1)}, bf16[64,512]{1,0:T(8,128)(2,1)S(1)}, u32[]{:S(2)}, u32[]{:S(2)}) collective-permute-start(bf16[64,512]{1,0:T(8,128)(2,1)S(1)} %get-tuple-element.91.refs_0_), channel_id=1, source_target_pairs={{0,1},{1,0},{2,3},{3,2},{4,5},{5,4},{6,7},{7,6},{8,9},{9,8},{10,11... | collective-permute-start | bytes 196616 | tf_op jit(solution)/shard_map/ppermute | solution.py:402
  25.9 2.8 %collective-permute-start.14 = (bf16[64,512]{1,0:T(8,128)(2,1)S(1)}, bf16[64,512]{1,0:T(8,128)(2,1)S(1)}, u32[]{:S(2)}, u32[]{:S(2)}) collective-permute-start(bf16[64,512]{1,0:T(8,128)(2,1)S(1)} %get-tuple-element.92.refs_4_), channel_id=1, source_target_pairs={{0,1},{1,0},{2,3},{3,2},{4,5},{5,4},{6,7},{7,6},{8,9},{9,8},{10,11... | collective-permute-start | bytes 196616 | tf_op jit(solution)/shard_map/ppermute | solution.py:402
  27.4 1.3 %collective-permute-start.15 = (bf16[64,512]{1,0:T(8,128)(2,1)S(1)}, bf16[64,512]{1,0:T(8,128)(2,1)S(1)}, u32[]{:S(2)}, u32[]{:S(2)}) collective-permute-start(bf16[64,512]{1,0:T(8,128)(2,1)S(1)} %collective-permute-done.13.refs_5_), channel_id=1, source_target_pairs={{0,1},{1,0},{2,3},{3,2},{4,5},{5,4},{6,7},{7,6},{8,9},{9,8},{10,11... | collective-permute-start | bytes 196616 | tf_op jit(solution)/shard_map/ppermute | solution.py:402
  27.4 1.4 %collective-permute-start.17 = (bf16[64,512]{1,0:T(8,128)(2,1)S(1)}, bf16[64,512]{1,0:T(8,128)(2,1)S(1)}, u32[]{:S(2)}, u32[]{:S(2)}) collective-permute-start(bf16[64,512]{1,0:T(8,128)(2,1)S(1)} %get-tuple-element.93.refs_8_), channel_id=1, source_target_pairs={{0,1},{1,0},{2,3},{3,2},{4,5},{5,4},{6,7},{7,6},{8,9},{9,8},{10,11... | collective-permute-start | bytes 196616 | tf_op jit(solution)/shard_map/ppermute | solution.py:402
  28.0 1.3 %collective-permute-start.12 = (bf16[64,512]{1,0:T(8,128)(2,1)S(1)}, bf16[64,512]{1,0:T(8,128)(2,1)S(1)}, u32[]{:S(2)}, u32[]{:S(2)}) collective-permute-start(bf16[64,512]{1,0:T(8,128)(2,1)S(1)} %collective-permute-done.10.refs_1_), channel_id=1, source_target_pairs={{0,1},{1,0},{2,3},{3,2},{4,5},{5,4},{6,7},{7,6},{8,9},{9,8},{10,11... | collective-permute-start | bytes 196616 | tf_op jit(solution)/shard_map/ppermute | solution.py:402
  30.1 4.6 %collective-permute-start.22 = (f32[2,512]{1,0:T(2,128)S(1)}, f32[2,512]{1,0:T(2,128)S(1)}, u32[]{:S(2)}, u32[]{:S(2)}) collective-permute-start(f32[2,512]{1,0:T(2,128)S(1)} %get-tuple-element.95.refs_0_), channel_id=1, source_target_pairs={{0,24},{8,16},{16,8},{24,0},{1,25},{9,17},{17,9},{25,1},{2,26},{10... | collective-permute-start | bytes 12296 | tf_op jit(solution)/shard_map/ppermute | solution.py:409
  32.8 3.6 %collective-permute-start.21 = (f32[2,512]{1,0:T(2,128)S(1)}, f32[2,512]{1,0:T(2,128)S(1)}, u32[]{:S(2)}, u32[]{:S(2)}) collective-permute-start(f32[2,512]{1,0:T(2,128)S(1)} %get-tuple-element.95.refs_0_), channel_id=1, source_target_pairs={{0,16},{8,24},{16,0},{24,8},{1,17},{9,25},{17,1},{25,9},{2,18},{10... | collective-permute-start | bytes 12296 | tf_op jit(solution)/shard_map/ppermute | solution.py:409
  33.3 3.6 %collective-permute-start.20 = (f32[2,512]{1,0:T(2,128)S(1)}, f32[2,512]{1,0:T(2,128)S(1)}, u32[]{:S(2)}, u32[]{:S(2)}) collective-permute-start(f32[2,512]{1,0:T(2,128)S(1)} %get-tuple-element.95.refs_0_), channel_id=1, source_target_pairs={{0,8},{8,0},{16,24},{24,16},{1,9},{9,1},{17,25},{25,17},{2,10},{10... | collective-permute-start | bytes 12296 | tf_op jit(solution)/shard_map/ppermute | solution.py:409
  37.8 4.3 %collective-permute-start.25 = (bf16[64,512]{1,0:T(8,128)(2,1)S(1)}, bf16[64,512]{1,0:T(8,128)(2,1)S(1)}, u32[]{:S(2)}, u32[]{:S(2)}) collective-permute-start(bf16[64,512]{1,0:T(8,128)(2,1)S(1)} %get-tuple-element.112), channel_id=1, source_target_pairs={{0,2},{1,3},{2,0},{3,1},{4,6},{5,7},{6,4},{7,5},{8,10},{9,11},{10,... | collective-permute-start | bytes 196616 | tf_op jit(solution)/shard_map/ppermute | solution.py:391
  38.4 7.2 %collective-permute-start.23 = (bf16[64,512]{1,0:T(8,128)(2,1)S(1)}, bf16[64,512]{1,0:T(8,128)(2,1)S(1)}, u32[]{:S(2)}, u32[]{:S(2)}) collective-permute-start(bf16[64,512]{1,0:T(8,128)(2,1)S(1)} %get-tuple-element.108), channel_id=1, source_target_pairs={{0,2},{1,3},{2,0},{3,1},{4,6},{5,7},{6,4},{7,5},{8,10},{9,11},{10,... | collective-permute-start | bytes 196616 | tf_op jit(solution)/shard_map/ppermute | solution.py:391
  39.8 6.4 %collective-permute-start.27 = (bf16[64,512]{1,0:T(8,128)(2,1)S(1)}, bf16[64,512]{1,0:T(8,128)(2,1)S(1)}, u32[]{:S(2)}, u32[]{:S(2)}) collective-permute-start(bf16[64,512]{1,0:T(8,128)(2,1)S(1)} %get-tuple-element.116), channel_id=1, source_target_pairs={{0,2},{1,3},{2,0},{3,1},{4,6},{5,7},{6,4},{7,5},{8,10},{9,11},{10,... | collective-permute-start | bytes 196616 | tf_op jit(solution)/shard_map/ppermute | solution.py:391
  42.1 7.7 %collective-permute-start.26 = (bf16[64,512]{1,0:T(8,128)(2,1)S(1)}, bf16[64,512]{1,0:T(8,128)(2,1)S(1)}, u32[]{:S(2)}, u32[]{:S(2)}) collective-permute-start(bf16[64,512]{1,0:T(8,128)(2,1)S(1)} %carry.10.refs_0_), channel_id=1, source_target_pairs={{0,4},{1,5},{2,6},{3,7},{4,0},{5,1},{6,2},{7,3},{8,12},{9,13},{10,... | collective-permute-start | bytes 196616 | tf_op jit(solution)/shard_map/ppermute | solution.py:391
  45.6 5.7 %collective-permute-start.24 = (bf16[64,512]{1,0:T(8,128)(2,1)S(1)}, bf16[64,512]{1,0:T(8,128)(2,1)S(1)}, u32[]{:S(2)}, u32[]{:S(2)}) collective-permute-start(bf16[64,512]{1,0:T(8,128)(2,1)S(1)} %carry.9.refs_0_), channel_id=1, source_target_pairs={{0,4},{1,5},{2,6},{3,7},{4,0},{5,1},{6,2},{7,3},{8,12},{9,13},{10,... | collective-permute-start | bytes 196616 | tf_op jit(solution)/shard_map/ppermute | solution.py:391
  46.3 6.4 %collective-permute-start.28 = (bf16[64,512]{1,0:T(8,128)(2,1)S(1)}, bf16[64,512]{1,0:T(8,128)(2,1)S(1)}, u32[]{:S(2)}, u32[]{:S(2)}) collective-permute-start(bf16[64,512]{1,0:T(8,128)(2,1)S(1)} %carry.11.refs_0_), channel_id=1, source_target_pairs={{0,4},{1,5},{2,6},{3,7},{4,0},{5,1},{6,2},{7,3},{8,12},{9,13},{10,... | collective-permute-start | bytes 196616 | tf_op jit(solution)/shard_map/ppermute | solution.py:391
  50.0 4.3 %collective-permute-start.32 = (bf16[64,512]{1,0:T(8,128)(2,1)S(1)}, bf16[64,512]{1,0:T(8,128)(2,1)S(1)}, u32[]{:S(2)}, u32[]{:S(2)}) collective-permute-start(bf16[64,512]{1,0:T(8,128)(2,1)S(1)} %get-tuple-element.120.refs_4_), channel_id=1, source_target_pairs={{0,2},{1,3},{2,0},{3,1},{4,6},{5,7},{6,4},{7,5},{8,10},{9,11},{10,... | collective-permute-start | bytes 196616 | tf_op jit(solution)/shard_map/ppermute | solution.py:391
  51.4 4.3 %collective-permute-start.29 = (bf16[64,512]{1,0:T(8,128)(2,1)S(1)}, bf16[64,512]{1,0:T(8,128)(2,1)S(1)}, u32[]{:S(2)}, u32[]{:S(2)}) collective-permute-start(bf16[64,512]{1,0:T(8,128)(2,1)S(1)} %get-tuple-element.119.refs_0_), channel_id=1, source_target_pairs={{0,2},{1,3},{2,0},{3,1},{4,6},{5,7},{6,4},{7,5},{8,10},{9,11},{10,... | collective-permute-start | bytes 196616 | tf_op jit(solution)/shard_map/ppermute | solution.py:391
  52.9 4.3 %collective-permute-start.35 = (bf16[64,512]{1,0:T(8,128)(2,1)S(1)}, bf16[64,512]{1,0:T(8,128)(2,1)S(1)}, u32[]{:S(2)}, u32[]{:S(2)}) collective-permute-start(bf16[64,512]{1,0:T(8,128)(2,1)S(1)} %get-tuple-element.127.refs_0_), channel_id=1, source_target_pairs={{0,2},{1,3},{2,0},{3,1},{4,6},{5,7},{6,4},{7,5},{8,10},{9,11},{10,... | collective-permute-start | bytes 196616 | tf_op jit(solution)/shard_map/ppermute | solution.py:391
  54.3 2.9 %collective-permute-start.34 = (bf16[64,512]{1,0:T(8,128)(2,1)S(1)}, bf16[64,512]{1,0:T(8,128)(2,1)S(1)}, u32[]{:S(2)}, u32[]{:S(2)}) collective-permute-start(bf16[64,512]{1,0:T(8,128)(2,1)S(1)} %collective-permute-done.32.refs_5_), channel_id=1, source_target_pairs={{0,1},{1,0},{2,3},{3,2},{4,5},{5,4},{6,7},{7,6},{8,9},{9,8},{10,11... | collective-permute-start | bytes 196616 | tf_op jit(solution)/shard_map/ppermute | solution.py:402
  55.8 2.0 %collective-permute-start.30 = (bf16[64,512]{1,0:T(8,128)(2,1)S(1)}, bf16[64,512]{1,0:T(8,128)(2,1)S(1)}, u32[]{:S(2)}, u32[]{:S(2)}) collective-permute-start(bf16[64,512]{1,0:T(8,128)(2,1)S(1)} %get-tuple-element.119.refs_0_), channel_id=1, source_target_pairs={{0,1},{1,0},{2,3},{3,2},{4,5},{5,4},{6,7},{7,6},{8,9},{9,8},{10,11... | collective-permute-start | bytes 196616 | tf_op jit(solution)/shard_map/ppermute | solution.py:402
  55.8 2.0 %collective-permute-start.33 = (bf16[64,512]{1,0:T(8,128)(2,1)S(1)}, bf16[64,512]{1,0:T(8,128)(2,1)S(1)}, u32[]{:S(2)}, u32[]{:S(2)}) collective-permute-start(bf16[64,512]{1,0:T(8,128)(2,1)S(1)} %get-tuple-element.120.refs_4_), channel_id=1, source_target_pairs={{0,1},{1,0},{2,3},{3,2},{4,5},{5,4},{6,7},{7,6},{8,9},{9,8},{10,11... | collective-permute-start | bytes 196616 | tf_op jit(solution)/shard_map/ppermute | solution.py:402
  56.3 1.5 %collective-permute-start.31 = (bf16[64,512]{1,0:T(8,128)(2,1)S(1)}, bf16[64,512]{1,0:T(8,128)(2,1)S(1)}, u32[]{:S(2)}, u32[]{:S(2)}) collective-permute-start(bf16[64,512]{1,0:T(8,128)(2,1)S(1)} %collective-permute-done.29.refs_1_), channel_id=1, source_target_pairs={{0,1},{1,0},{2,3},{3,2},{4,5},{5,4},{6,7},{7,6},{8,9},{9,8},{10,11... | collective-permute-start | bytes 196616 | tf_op jit(solution)/shard_map/ppermute | solution.py:402
  57.2 1.3 %collective-permute-start.36 = (bf16[64,512]{1,0:T(8,128)(2,1)S(1)}, bf16[64,512]{1,0:T(8,128)(2,1)S(1)}, u32[]{:S(2)}, u32[]{:S(2)}) collective-permute-start(bf16[64,512]{1,0:T(8,128)(2,1)S(1)} %get-tuple-element.127.refs_0_), channel_id=1, source_target_pairs={{0,1},{1,0},{2,3},{3,2},{4,5},{5,4},{6,7},{7,6},{8,9},{9,8},{10,11... | collective-permute-start | bytes 196616 | tf_op jit(solution)/shard_map/ppermute | solution.py:402
  57.2 1.4 %collective-permute-start.37 = (bf16[64,512]{1,0:T(8,128)(2,1)S(1)}, bf16[64,512]{1,0:T(8,128)(2,1)S(1)}, u32[]{:S(2)}, u32[]{:S(2)}) collective-permute-start(bf16[64,512]{1,0:T(8,128)(2,1)S(1)} %collective-permute-done.35.refs_1_), channel_id=1, source_target_pairs={{0,1},{1,0},{2,3},{3,2},{4,5},{5,4},{6,7},{7,6},{8,9},{9,8},{10,11... | collective-permute-start | bytes 196616 | tf_op jit(solution)/shard_map/ppermute | solution.py:402
  59.4 7.6 %collective-permute-start.38 = (bf16[96,512]{1,0:T(8,128)(2,1)S(1)}, bf16[96,512]{1,0:T(8,128)(2,1)S(1)}, u32[]{:S(2)}, u32[]{:S(2)}) collective-permute-start(bf16[96,512]{1,0:T(8,128)(2,1)S(1)} %get-tuple-element.144), channel_id=1, source_target_pairs={{0,6},{1,7},{2,4},{3,5},{4,2},{5,3},{6,0},{7,1},{8,14},{9,15},{10,... | collective-permute-start | bytes 294920 | tf_op jit(solution)/shard_map/ppermute | solution.py:386
  61.7 9.4 %collective-permute-start.39 = (bf16[96,512]{1,0:T(8,128)(2,1)S(1)}, bf16[96,512]{1,0:T(8,128)(2,1)S(1)}, u32[]{:S(2)}, u32[]{:S(2)}) collective-permute-start(bf16[96,512]{1,0:T(8,128)(2,1)S(1)} %get-tuple-element.145), channel_id=1, source_target_pairs={{0,4},{1,5},{2,6},{3,7},{4,0},{5,1},{6,2},{7,3},{8,12},{9,13},{10,... | collective-permute-start | bytes 294920 | tf_op jit(solution)/shard_map/ppermute | solution.py:386
  61.7 9.3 %collective-permute-start.40 = (bf16[96,512]{1,0:T(8,128)(2,1)S(1)}, bf16[96,512]{1,0:T(8,128)(2,1)S(1)}, u32[]{:S(2)}, u32[]{:S(2)}) collective-permute-start(bf16[96,512]{1,0:T(8,128)(2,1)S(1)} %get-tuple-element.146), channel_id=1, source_target_pairs={{0,2},{1,3},{2,0},{3,1},{4,6},{5,7},{6,4},{7,5},{8,10},{9,11},{10,... | collective-permute-start | bytes 294920 | tf_op jit(solution)/shard_map/ppermute | solution.py:386
  (1 other events, 1.0 us)

commit v16 on v15

--- a/solution.py
+++ b/solution.py
@@ -83,7 +83,7 @@
 
 
 def apply_forward(f1t, f3t, f2t, queries, weighted):
-    q_gate, q_up = stacked(nt, f1t, f3t, queries)
+    q_gate, q_up = nt(f1t, queries), nt(f3t, queries)
     silu, slope, _ = silu_parts(q_gate)
     mixed = (silu * q_up).astype(BF16)
     output = nn(f2t, mixed)
@@ -507,7 +507,7 @@
     pair = lambda x: lax.ppermute(x, "tok", core_perm(count))
     key_other, value_other, rate_other = pair(key_input), pair(value_input), pair(rates)
     w1t, w3t = w1.T, w3.T
-    query_other, grad_other = pair(query_input), pair(out_grad)
+    grad_other = pair(out_grad)
     keys_values = (
         key_input, key_other, value_input, value_other, rates, rate_other, w1t, w3t, w2,
     )
@@ -541,6 +541,8 @@
         )
         moved.append(rows_moved)
         fast.append(rows)
+    query_later, weighted = lax.optimization_barrier((query_input, weighted))
+    query_other = pair(query_later)
     f1t, f3t, f2t, output, q_mixed, q_slope, q_silu, part = call(
         functools.partial(apply_kernel, chips, folds),
         matrices + [((dh, n), F32), ((fh, n), BF16), hidden, hidden, ((2, n), F32)],

time: 71.9 us -> 71.5 us (level)
  starting transfers between devices: 38.3 us -> 33.2 us
  waiting for transfers between devices: 21 us -> 25.7 us
    ppermute x18, waiting for transfers between devices: 11.6 us -> 16.9 us  [to_chip(): return lax.ppermute(x, 'tok', chip_perm(chips * CORES, step))]
    ppermute x18, starting transfers between devices: 27 us -> 22 us  [to_chip(): return lax.ppermute(x, 'tok', chip_perm(chips * CORES, step))]
  transfers between devices with their start and end apart: 41 -> 41, of which waited for: 22 -> 24; matrix products, arithmetic and copies ran while one was open for 2% -> 2% of each run, Pallas kernels for 9% -> 9%
where the time goes in v16:
time: 71.5 us; the launch traced here: 71.4 us
  starting transfers between devices  33.2 us (46%)
  waiting for transfers between devices  25.7 us (36%)
  Pallas kernels  9.46 us (13%)
  local copies, waits for them, and re-layouts  2.13 us (3%)
  between operations  0.9 us (1%)
    ppermute x18, starting transfers between devices, to_chip(): return lax.ppermute(x, 'tok', chip_perm(chips * CORES, step))  22 us
    ppermute x18, waiting for transfers between devices, to_chip(): return lax.ppermute(x, 'tok', chip_perm(chips * CORES, step))  16.9 us
    pallas_call x21, Pallas kernels, call(): pl.pallas_call(kernel, out_shape=[jax.ShapeDtypeStruct(s, t) for s, t in...  9.46 us
    ppermute x3, waiting for transfers between devices, exchange(): lax.ppermute(pieces[s], 'tok', chip_perm(count, s))  4.75 us
    ppermute x3, starting transfers between devices, exchange(): lax.ppermute(pieces[s], 'tok', chip_perm(count, s))  4.45 us
    ppermute x3, starting transfers between devices, head_parts(): lax.ppermute(part, 'head', [(h, partner(h, step, heads)) for h in range(h...  3.57 us
    ppermute x3, waiting for transfers between devices, head_parts(): lax.ppermute(part, 'head', [(h, partner(h, step, heads)) for h in range(h...  3.06 us
    unnamed x18, local copies, waits for them, and re-layouts  2.13 us
  transfers between devices with their start and end apart: 41, of which 24 were waited for; matrix products, arithmetic and copies ran while one was open for 2% of the time, Pallas kernels for 9%

profile of v16, /device:TPU:0, one launch (start us, length us, event | category | flops | bytes accessed | tf_op | source)
XLA Modules:
  0.0 71.4 jit_solution(13714611053760920249)
XLA Ops:
  0.6 0.5 collective-permute-start.1
  1.8 1.1 %copy.15 = bf16[1,512,256]{1,2,0:T(8,128)(2,1)S(1)} copy(bf16[1,512,256]{2,1,0:T(8,128)(2,1)} %param.15) | data formatting | bytes 524288 | tf_op args[6]
  3.1 0.7 %copy-done = bf16[256,512]{1,0:T(8,128)(2,1)S(1)} copy-done((bf16[256,512]{1,0:T(8,128)(2,1)S(1)}, bf16[256,512]{1,0:T(8,128)(2,1)}, u32[]{:S(2)}) %copy-start) | copy-done | bytes 262168
  4.0 1.1 %update.1 = (f32[64,512]{1,0:T(8,128)S(1)}, f32[64,512]{1,0:T(8,128)S(1)}, f32[64,512]{1,0:T(8,128)S(1)}, bf16[64,512]{1,0:T(8,128)(2,1)S(1)}, bf16[64,512]{1,0:T(8,128)(2,1)S(1)}, /*index=5*/bf16[64,512]{1,0:T(8,128)(2,1)S(1)}) custom-call(bf16[256,512]{1,0:T(8,128)(2,1)S(1)} %copy-done, bf16[256,512]{1,0:T(8,128)(2,1)S(1)} %collective-permute-done.kx.refs_9_.refs_5_, ...), custom_call_target="tpu_custom_call" | custom-call | flops 805306368 | bytes 1837056 | tf_op jit(solution)/shard_map/update/pallas_call | solution.py:368
  5.1 3.1 %collective-permute-start.6 = (bf16[64,512]{1,0:T(8,128)(2,1)S(1)}, bf16[64,512]{1,0:T(8,128)(2,1)S(1)}, u32[]{:S(2)}, u32[]{:S(2)}) collective-permute-start(bf16[64,512]{1,0:T(8,128)(2,1)S(1)} %get-tuple-element.86), channel_id=1, source_target_pairs={{0,2},{1,3},{2,0},{3,1},{4,6},{5,7},{6,4},{7,5},{8,10},{9,11},{10,... | collective-permute-start | bytes 196616 | tf_op jit(solution)/shard_map/ppermute | solution.py:391
  8.2 1.9 %collective-permute-start.4 = (bf16[64,512]{1,0:T(8,128)(2,1)S(1)}, bf16[64,512]{1,0:T(8,128)(2,1)S(1)}, u32[]{:S(2)}, u32[]{:S(2)}) collective-permute-start(bf16[64,512]{1,0:T(8,128)(2,1)S(1)} %get-tuple-element.82), channel_id=1, source_target_pairs={{0,2},{1,3},{2,0},{3,1},{4,6},{5,7},{6,4},{7,5},{8,10},{9,11},{10,... | collective-permute-start | bytes 196616 | tf_op jit(solution)/shard_map/ppermute | solution.py:391
  10.6 3.2 %collective-permute-start.7 = (bf16[64,512]{1,0:T(8,128)(2,1)S(1)}, bf16[64,512]{1,0:T(8,128)(2,1)S(1)}, u32[]{:S(2)}, u32[]{:S(2)}) collective-permute-start(bf16[64,512]{1,0:T(8,128)(2,1)S(1)} %carry.7.refs_0_), channel_id=1, source_target_pairs={{0,4},{1,5},{2,6},{3,7},{4,0},{5,1},{6,2},{7,3},{8,12},{9,13},{10,... | collective-permute-start | bytes 196616 | tf_op jit(solution)/shard_map/ppermute | solution.py:391
  13.9 1.9 %collective-permute-start.9 = (bf16[64,512]{1,0:T(8,128)(2,1)S(1)}, bf16[64,512]{1,0:T(8,128)(2,1)S(1)}, u32[]{:S(2)}, u32[]{:S(2)}) collective-permute-start(bf16[64,512]{1,0:T(8,128)(2,1)S(1)} %carry.8.refs_0_), channel_id=1, source_target_pairs={{0,4},{1,5},{2,6},{3,7},{4,0},{5,1},{6,2},{7,3},{8,12},{9,13},{10,... | collective-permute-start | bytes 196616 | tf_op jit(solution)/shard_map/ppermute | solution.py:391
  15.8 1.1 %saved.1 = (bf16[512,512]{1,0:T(8,128)(2,1)S(1)}, f32[256,512]{1,0:T(8,128)S(1)}, f32[256,512]{1,0:T(8,128)S(1)}, f32[256,512]{1,0:T(8,128)S(1)}, f32[256,512]{1...) custom-call(bf16[256,512]{1,0:T(8,128)(2,1)S(1)} %copy-done, ...), custom_call_target="tpu_custom_call" | custom-call | flops 402653184 | bytes 2363392 | tf_op jit(solution)/shard_map/saved/pallas_call | solution.py:368
  17.1 1.1 %collective-permute-start.5 = (bf16[64,512]{1,0:T(8,128)(2,1)S(1)}, bf16[64,512]{1,0:T(8,128)(2,1)S(1)}, u32[]{:S(2)}, u32[]{:S(2)}) collective-permute-start(bf16[64,512]{1,0:T(8,128)(2,1)S(1)} %carry.6.refs_0_), channel_id=1, source_target_pairs={{0,4},{1,5},{2,6},{3,7},{4,0},{5,1},{6,2},{7,3},{8,12},{9,13},{10,... | collective-permute-start | bytes 196616 | tf_op jit(solution)/shard_map/ppermute | solution.py:391
  18.2 1.1 %collective-permute-done.9.refs_1_ = bf16[64,512]{1,0:T(8,128)(2,1)S(1)} collective-permute-done((bf16[64,512]{1,0:T(8,128)(2,1)S(1)}, bf16[64,512]{1,0:T(8,128)(2,1)S(1)}, u32[]{:S(2)}, u32[]{:S(2)}) %collective-permute-start.9) | collective-permute-done | bytes 65568 | tf_op jit(solution)/shard_map/ppermute | solution.py:391
  19.5 1.8 %collective-permute-start.16 = (bf16[64,512]{1,0:T(8,128)(2,1)S(1)}, bf16[64,512]{1,0:T(8,128)(2,1)S(1)}, u32[]{:S(2)}, u32[]{:S(2)}) collective-permute-start(bf16[64,512]{1,0:T(8,128)(2,1)S(1)} %get-tuple-element.95.refs_8_), channel_id=1, source_target_pairs={{0,2},{1,3},{2,0},{3,1},{4,6},{5,7},{6,4},{7,5},{8,10},{9,11},{10,... | collective-permute-start | bytes 196616 | tf_op jit(solution)/shard_map/ppermute | solution.py:391
  21.7 2.3 %collective-permute-done.5.refs_1_ = bf16[64,512]{1,0:T(8,128)(2,1)S(1)} collective-permute-done((bf16[64,512]{1,0:T(8,128)(2,1)S(1)}, bf16[64,512]{1,0:T(8,128)(2,1)S(1)}, u32[]{:S(2)}, u32[]{:S(2)}) %collective-permute-start.5) | collective-permute-done | bytes 65568 | tf_op jit(solution)/shard_map/ppermute | solution.py:391
  24.4 0.7 collective-permute-done.16.refs_9_
  25.0 0.7 collective-permute-done.13.refs_5_
  25.7 2.7 %collective-permute-done.10.refs_1_ = bf16[64,512]{1,0:T(8,128)(2,1)S(1)} collective-permute-done((bf16[64,512]{1,0:T(8,128)(2,1)S(1)}, bf16[64,512]{1,0:T(8,128)(2,1)S(1)}, u32[]{:S(2)}, u32[]{:S(2)}) %collective-permute-start.10) | collective-permute-done | bytes 65568 | tf_op jit(solution)/shard_map/ppermute | solution.py:391
  28.5 0.5 collective-permute-start.14
  29.0 0.5 collective-permute-start.12
  30.4 0.8 %apply.1 = (bf16[256,512]{1,0:T(8,128)(2,1)S(1)}, bf16[256,512]{1,0:T(8,128)(2,1)S(1)}, bf16[512,256]{1,0:T(8,128)(2,1)S(1)}, f32[512,512]{1,0:T(8,128)S(1)}, bf...) custom-call(bf16[64,512]{1,0:T(8,128)(2,1)S(1)} %get-tuple-element.93.refs_0, ...), custom_call_target="tpu_custom_call" | custom-call | flops 402653184 | bytes 2359296 | tf_op jit(solution)/shard_map/apply/pallas_call | solution.py:368
  31.2 2.5 %collective-permute-start.22 = (f32[2,512]{1,0:T(2,128)S(1)}, f32[2,512]{1,0:T(2,128)S(1)}, u32[]{:S(2)}, u32[]{:S(2)}) collective-permute-start(f32[2,512]{1,0:T(2,128)S(1)} %get-tuple-element.99.refs_0_), channel_id=1, source_target_pairs={{0,24},{8,16},{16,8},{24,0},{1,25},{9,17},{17,9},{25,1},{2,26},{10... | collective-permute-start | bytes 12296 | tf_op jit(solution)/shard_map/ppermute | solution.py:409
  33.8 0.5 collective-permute-start.21
  34.3 0.5 collective-permute-start.20
  34.8 1.0 %collective-permute-done.22.refs_3_ = f32[2,512]{1,0:T(2,128)S(1)} collective-permute-done((f32[2,512]{1,0:T(2,128)S(1)}, f32[2,512]{1,0:T(2,128)S(1)}, u32[]{:S(2)}, u32[]{:S(2)}) %collective-permute-start.22) | collective-permute-done | bytes 4128 | tf_op jit(solution)/shard_map/ppermute | solution.py:409
  35.8 1.5 %collective-permute-done.21.refs_2_ = f32[2,512]{1,0:T(2,128)S(1)} collective-permute-done((f32[2,512]{1,0:T(2,128)S(1)}, f32[2,512]{1,0:T(2,128)S(1)}, u32[]{:S(2)}, u32[]{:S(2)}) %collective-permute-start.21) | collective-permute-done | bytes 4128 | tf_op jit(solution)/shard_map/ppermute | solution.py:409
  37.9 0.8 %apply_back.1 = (bf16[256,256]{1,0:T(8,128)(2,1)S(1)}, bf16[256,256]{1,0:T(8,128)(2,1)S(1)}, f32[64,512]{1,0:T(8,128)S(1)}, f32[64,512]{1,0:T(8,128)S(1)}, f32[6...) custom-call(f32[2,512]{1,0:T(2,128)S(1)} %get-tuple-element.99.refs_0, ...), custom_call_target="tpu_custom_call" | custom-call | flops 536870912 | bytes 4210688 | tf_op jit(solution)/shard_map/apply_back/pallas_call | solution.py:368
  38.9 1.9 %collective-permute-start.23 = (bf16[64,512]{1,0:T(8,128)(2,1)S(1)}, bf16[64,512]{1,0:T(8,128)(2,1)S(1)}, u32[]{:S(2)}, u32[]{:S(2)}) collective-permute-start(bf16[64,512]{1,0:T(8,128)(2,1)S(1)} %get-tuple-element.112), channel_id=1, source_target_pairs={{0,2},{1,3},{2,0},{3,1},{4,6},{5,7},{6,4},{7,5},{8,10},{9,11},{10,... | collective-permute-start | bytes 196616 | tf_op jit(solution)/shard_map/ppermute | solution.py:391
  40.9 2.1 %collective-permute-done.25.got = bf16[64,512]{1,0:T(8,128)(2,1)S(1)} collective-permute-done((bf16[64,512]{1,0:T(8,128)(2,1)S(1)}, bf16[64,512]{1,0:T(8,128)(2,1)S(1)}, u32[]{:S(2)}, u32[]{:S(2)}) %collective-permute-start.25) | collective-permute-done | bytes 65568 | tf_op jit(solution)/shard_map/ppermute | solution.py:391
  43.1 1.4 %collective-permute-start.26 = (bf16[64,512]{1,0:T(8,128)(2,1)S(1)}, bf16[64,512]{1,0:T(8,128)(2,1)S(1)}, u32[]{:S(2)}, u32[]{:S(2)}) collective-permute-start(bf16[64,512]{1,0:T(8,128)(2,1)S(1)} %carry.10.refs_0_), channel_id=1, source_target_pairs={{0,4},{1,5},{2,6},{3,7},{4,0},{5,1},{6,2},{7,3},{8,12},{9,13},{10,... | collective-permute-start | bytes 196616 | tf_op jit(solution)/shard_map/ppermute | solution.py:391
  44.5 1.6 %collective-permute-start.24 = (bf16[64,512]{1,0:T(8,128)(2,1)S(1)}, bf16[64,512]{1,0:T(8,128)(2,1)S(1)}, u32[]{:S(2)}, u32[]{:S(2)}) collective-permute-start(bf16[64,512]{1,0:T(8,128)(2,1)S(1)} %carry.9.refs_0_), channel_id=1, source_target_pairs={{0,4},{1,5},{2,6},{3,7},{4,0},{5,1},{6,2},{7,3},{8,12},{9,13},{10,... | collective-permute-start | bytes 196616 | tf_op jit(solution)/shard_map/ppermute | solution.py:391
  46.5 1.1 %collective-permute-start.28 = (bf16[64,512]{1,0:T(8,128)(2,1)S(1)}, bf16[64,512]{1,0:T(8,128)(2,1)S(1)}, u32[]{:S(2)}, u32[]{:S(2)}) collective-permute-start(bf16[64,512]{1,0:T(8,128)(2,1)S(1)} %carry.11.refs_0_), channel_id=1, source_target_pairs={{0,4},{1,5},{2,6},{3,7},{4,0},{5,1},{6,2},{7,3},{8,12},{9,13},{10,... | collective-permute-start | bytes 196616 | tf_op jit(solution)/shard_map/ppermute | solution.py:391
  47.6 1.9 %collective-permute-done.26.refs_1_ = bf16[64,512]{1,0:T(8,128)(2,1)S(1)} collective-permute-done((bf16[64,512]{1,0:T(8,128)(2,1)S(1)}, bf16[64,512]{1,0:T(8,128)(2,1)S(1)}, u32[]{:S(2)}, u32[]{:S(2)}) %collective-permute-start.26) | collective-permute-done | bytes 65568 | tf_op jit(solution)/shard_map/ppermute | solution.py:391
  49.7 1.1 %collective-permute-done.24.refs_1_ = bf16[64,512]{1,0:T(8,128)(2,1)S(1)} collective-permute-done((bf16[64,512]{1,0:T(8,128)(2,1)S(1)}, bf16[64,512]{1,0:T(8,128)(2,1)S(1)}, u32[]{:S(2)}, u32[]{:S(2)}) %collective-permute-start.24) | collective-permute-done | bytes 65568 | tf_op jit(solution)/shard_map/ppermute | solution.py:391
  51.0 1.0 %collective-permute-start.29 = (bf16[64,512]{1,0:T(8,128)(2,1)S(1)}, bf16[64,512]{1,0:T(8,128)(2,1)S(1)}, u32[]{:S(2)}, u32[]{:S(2)}) collective-permute-start(bf16[64,512]{1,0:T(8,128)(2,1)S(1)} %get-tuple-element.123.refs_0_), channel_id=1, source_target_pairs={{0,2},{1,3},{2,0},{3,1},{4,6},{5,7},{6,4},{7,5},{8,10},{9,11},{10,... | collective-permute-start | bytes 196616 | tf_op jit(solution)/shard_map/ppermute | solution.py:391
  52.6 0.8 %collective-permute-start.35 = (bf16[64,512]{1,0:T(8,128)(2,1)S(1)}, bf16[64,512]{1,0:T(8,128)(2,1)S(1)}, u32[]{:S(2)}, u32[]{:S(2)}) collective-permute-start(bf16[64,512]{1,0:T(8,128)(2,1)S(1)} %get-tuple-element.131.refs_0_), channel_id=1, source_target_pairs={{0,2},{1,3},{2,0},{3,1},{4,6},{5,7},{6,4},{7,5},{8,10},{9,11},{10,... | collective-permute-start | bytes 196616 | tf_op jit(solution)/shard_map/ppermute | solution.py:391
  53.4 0.6 collective-permute-done.32.refs_5_
  54.0 1.4 %collective-permute-done.29.refs_1_ = bf16[64,512]{1,0:T(8,128)(2,1)S(1)} collective-permute-done((bf16[64,512]{1,0:T(8,128)(2,1)S(1)}, bf16[64,512]{1,0:T(8,128)(2,1)S(1)}, u32[]{:S(2)}, u32[]{:S(2)}) %collective-permute-start.29) | collective-permute-done | bytes 65568 | tf_op jit(solution)/shard_map/ppermute | solution.py:391
  55.4 0.5 collective-permute-start.33
  55.9 1.0 %collective-permute-done.35.refs_1_ = bf16[64,512]{1,0:T(8,128)(2,1)S(1)} collective-permute-done((bf16[64,512]{1,0:T(8,128)(2,1)S(1)}, bf16[64,512]{1,0:T(8,128)(2,1)S(1)}, u32[]{:S(2)}, u32[]{:S(2)}) %collective-permute-start.35) | collective-permute-done | bytes 65568 | tf_op jit(solution)/shard_map/ppermute | solution.py:391
  56.9 0.5 collective-permute-start.37
  57.4 0.8 %second_first.1 = (bf16[256,512]{1,0:T(8,128)(2,1)S(1)}, bf16[256,512]{1,0:T(8,128)(2,1)S(1)}, bf16[256,256]{1,0:T(8,128)(2,1)S(1)}, f32[128,512]{1,0:T(8,128)S(...) custom-call(bf16[64,512]{1,0:T(8,128)(2,1)S(1)} %get-tuple-element.123.refs_0_, ...), custom_call_target="tpu_custom_call" | custom-call | flops 402653184 | bytes 3670016 | tf_op jit(solution)/shard_map/second_first/pallas_call | solution.py:368
  58.3 0.7 %second_last.1 = (bf16[512,256]{1,0:T(8,128)(2,1)S(1)}, bf16[256,256]{1,0:T(8,128)(2,1)S(1)}, bf16[256,256]{1,0:T(8,128)(2,1)S(1)}, f32[96,512]{1,0:T(8,128)S(1)...) custom-call(bf16[64,512]{1,0:T(8,128)(2,1)S(1)} %get-tuple-element.131.refs_0_, ...), custom_call_target="tpu_custom_call" | custom-call | flops 402653184 | bytes 3670016 | tf_op jit(solution)/shard_map/second_last/pallas_call | solution.py:368
  59.1 2.0 %collective-permute-start.38 = (bf16[96,512]{1,0:T(8,128)(2,1)S(1)}, bf16[96,512]{1,0:T(8,128)(2,1)S(1)}, u32[]{:S(2)}, u32[]{:S(2)}) collective-permute-start(bf16[96,512]{1,0:T(8,128)(2,1)S(1)} %get-tuple-element.148), channel_id=1, source_target_pairs={{0,6},{1,7},{2,4},{3,5},{4,2},{5,3},{6,0},{7,1},{8,14},{9,15},{10,... | collective-permute-start | bytes 294920 | tf_op jit(solution)/shard_map/ppermute | solution.py:386
  61.3 2.2 %collective-permute-start.40 = (bf16[96,512]{1,0:T(8,128)(2,1)S(1)}, bf16[96,512]{1,0:T(8,128)(2,1)S(1)}, u32[]{:S(2)}, u32[]{:S(2)}) collective-permute-start(bf16[96,512]{1,0:T(8,128)(2,1)S(1)} %get-tuple-element.150), channel_id=1, source_target_pairs={{0,2},{1,3},{2,0},{3,1},{4,6},{5,7},{6,4},{7,5},{8,10},{9,11},{10,... | collective-permute-start | bytes 294920 | tf_op jit(solution)/shard_map/ppermute | solution.py:386
  63.5 1.0 %query_grad.1 = bf16[256,512]{1,0:T(8,128)(2,1)} custom-call(bf16[256,256]{1,0:T(8,128)(2,1)S(1)} %get-tuple-element.105.gate_back, bf16[256,256]{1,0:T(8,128)(2,1)S(1)} %get-tuple-element.106.up_back, bf16[256,512]{1,0:T(8,128)(2,1)S(1)} %get-tuple-element.107.f1t, bf16[256,512]{1,0:T(8,128)(2,1)S(1)} %get-tuple-element.108.f3t), custom_call_target="tpu_custom_call" | custom-call | flops 134217728 | bytes 786432 | tf_op jit(solution)/shard_map/query_grad/pallas_call | solution.py:368
  64.6 1.4 %token_grads.1 = (bf16[256,512]{1,0:T(8,128)(2,1)}, bf16[256,512]{1,0:T(8,128)(2,1)}) custom-call(f32[1,256]{1,0:T(1,128)S(1)} %bitcast.30, bf16[256,256]{1,0:T(8,128)(2,1)S(1)} %get-tuple-element.109.refs_1_, bf16[256,256]{1,0:T(8,128)(2,1)S(1)} %get-tuple-element.130.refs_2_, bf16[256,256]{1,0:T(8,128)(2,1)S(1)} %get-tuple-element.135.refs_3_, ...), custom_call_target="tpu_custom_call" | custom-call | flops 402653184 | bytes 2360320 | tf_op jit(solution)/shard_map/token_grads/pallas_call | solution.py:368
  65.9 0.7 %collective-permute-done.38.refs_4_ = bf16[96,512]{1,0:T(8,128)(2,1)S(1)} collective-permute-done((bf16[96,512]{1,0:T(8,128)(2,1)S(1)}, bf16[96,512]{1,0:T(8,128)(2,1)S(1)}, u32[]{:S(2)}, u32[]{:S(2)}) %collective-permute-start.38) | collective-permute-done | bytes 98336 | tf_op jit(solution)/shard_map/ppermute | solution.py:386
  66.6 4.0 %collective-permute-done.39.refs_5_ = bf16[96,512]{1,0:T(8,128)(2,1)S(1)} collective-permute-done((bf16[96,512]{1,0:T(8,128)(2,1)S(1)}, bf16[96,512]{1,0:T(8,128)(2,1)S(1)}, u32[]{:S(2)}, u32[]{:S(2)}) %collective-permute-start.39) | collective-permute-done | bytes 98336 | tf_op jit(solution)/shard_map/ppermute | solution.py:386
  70.7 0.7 owner_result.1
  (73 shorter events, 5.9 us)
Async XLA Ops:
  0.6 1.0 %copy-start.5 = (f32[256,1]{0,1:T(1,128)S(1)}, f32[256,1]{0,1:T(1,128)}, u32[]{:S(2)}) copy-start(f32[256,1]{0,1:T(1,128)} %param.13) | copy-start | bytes 3076
  0.6 2.5 %collective-permute-start.1 = (bf16[256,512]{1,0:T(8,128)(2,1)}, bf16[256,512]{1,0:T(8,128)(2,1)S(1)}, u32[]{:S(2)}, u32[]{:S(2)}) collective-permute-start(bf16[256,512]{1,0:T(8,128)(2,1)} %vo.3), channel_id=1, source_target_pairs={{0,1},{1,0},{2,3},{3,2},{4,5},{5,4},{6,7},{7,6},{8,9},{9,8},{10,11... | collective-permute-start | bytes 786440 | tf_op jit(solution)/shard_map/ppermute | solution.py:507
  1.2 2.0 %collective-permute-start = (bf16[256,512]{1,0:T(8,128)(2,1)}, bf16[256,512]{1,0:T(8,128)(2,1)S(1)}, u32[]{:S(2)}, u32[]{:S(2)}) collective-permute-start(bf16[256,512]{1,0:T(8,128)(2,1)} %refs_4_.1), channel_id=1, source_target_pairs={{0,1},{1,0},{2,3},{3,2},{4,5},{5,4},{6,7},{7,6},{8,9},{9,8},{10,11... | collective-permute-start | bytes 786440 | tf_op jit(solution)/shard_map/ppermute | solution.py:507
  1.2 14.6 %collective-permute-start.3 = (bf16[256,512]{1,0:T(8,128)(2,1)}, bf16[256,512]{1,0:T(8,128)(2,1)S(1)}, u32[]{:S(2)}, u32[]{:S(2)}) collective-permute-start(bf16[256,512]{1,0:T(8,128)(2,1)} %go.1), channel_id=1, source_target_pairs={{0,1},{1,0},{2,3},{3,2},{4,5},{5,4},{6,7},{7,6},{8,9},{9,8},{10,11... | collective-permute-start | bytes 786440 | tf_op jit(solution)/shard_map/ppermute | solution.py:507
  1.7 1.2 %copy-start.7 = (bf16[1,512,256]{2,1,0:T(8,128)(2,1)S(1)}, bf16[1,512,256]{2,1,0:T(8,128)(2,1)}, u32[]{:S(2)}) copy-start(bf16[1,512,256]{2,1,0:T(8,128)(2,1)} %param.16) | copy-start | bytes 786436
  1.7 1.4 %collective-permute-start.2 = (f32[1,256]{1,0:T(1,128)S(1)}, f32[1,256]{1,0:T(1,128)S(1)}, u32[]{:S(2)}, u32[]{:S(2)}) collective-permute-start(f32[1,256]{1,0:T(1,128)S(1)} %bitcast.27), channel_id=1, source_target_pairs={{0,1},{1,0},{2,3},{3,2},{4,5},{5,4},{6,7},{7,6},{8,9},{9,8},{10,11... | collective-permute-start | bytes 3080 | tf_op jit(solution)/shard_map/ppermute | solution.py:507
  1.8 1.4 %copy-start.3 = (bf16[256,512]{1,0:T(8,128)(2,1)S(1)}, bf16[256,512]{1,0:T(8,128)(2,1)}, u32[]{:S(2)}) copy-start(bf16[256,512]{1,0:T(8,128)(2,1)} %vo.3) | copy-start | bytes 786436
  2.9 1.0 %copy-start.2 = (bf16[1,256,512]{2,1,0:T(8,128)(2,1)S(1)}, bf16[1,256,512]{2,1,0:T(8,128)(2,1)}, u32[]{:S(2)}) copy-start(bf16[1,256,512]{2,1,0:T(8,128)(2,1)} %param.17) | copy-start | bytes 786436
  5.1 5.5 %collective-permute-start.6 = (bf16[64,512]{1,0:T(8,128)(2,1)S(1)}, bf16[64,512]{1,0:T(8,128)(2,1)S(1)}, u32[]{:S(2)}, u32[]{:S(2)}) collective-permute-start(bf16[64,512]{1,0:T(8,128)(2,1)S(1)} %get-tuple-element.86), channel_id=1, source_target_pairs={{0,2},{1,3},{2,0},{3,1},{4,6},{5,7},{6,4},{7,5},{8,10},{9,11},{10,... | collective-permute-start | bytes 196616 | tf_op jit(solution)/shard_map/ppermute | solution.py:391
  8.2 5.7 %collective-permute-start.8 = (bf16[64,512]{1,0:T(8,128)(2,1)S(1)}, bf16[64,512]{1,0:T(8,128)(2,1)S(1)}, u32[]{:S(2)}, u32[]{:S(2)}) collective-permute-start(bf16[64,512]{1,0:T(8,128)(2,1)S(1)} %get-tuple-element.90), channel_id=1, source_target_pairs={{0,2},{1,3},{2,0},{3,1},{4,6},{5,7},{6,4},{7,5},{8,10},{9,11},{10,... | collective-permute-start | bytes 196616 | tf_op jit(solution)/shard_map/ppermute | solution.py:391
  8.2 8.8 %collective-permute-start.4 = (bf16[64,512]{1,0:T(8,128)(2,1)S(1)}, bf16[64,512]{1,0:T(8,128)(2,1)S(1)}, u32[]{:S(2)}, u32[]{:S(2)}) collective-permute-start(bf16[64,512]{1,0:T(8,128)(2,1)S(1)} %get-tuple-element.82), channel_id=1, source_target_pairs={{0,2},{1,3},{2,0},{3,1},{4,6},{5,7},{6,4},{7,5},{8,10},{9,11},{10,... | collective-permute-start | bytes 196616 | tf_op jit(solution)/shard_map/ppermute | solution.py:391
  10.6 5.2 %copy-start.4 = (bf16[256,512]{1,0:T(8,128)(2,1)S(1)}, bf16[256,512]{1,0:T(8,128)(2,1)}, u32[]{:S(2)}) copy-start(bf16[256,512]{1,0:T(8,128)(2,1)} %go.1) | copy-start | bytes 786436
  10.6 10.6 %collective-permute-start.7 = (bf16[64,512]{1,0:T(8,128)(2,1)S(1)}, bf16[64,512]{1,0:T(8,128)(2,1)S(1)}, u32[]{:S(2)}, u32[]{:S(2)}) collective-permute-start(bf16[64,512]{1,0:T(8,128)(2,1)S(1)} %carry.7.refs_0_), channel_id=1, source_target_pairs={{0,4},{1,5},{2,6},{3,7},{4,0},{5,1},{6,2},{7,3},{8,12},{9,13},{10,... | collective-permute-start | bytes 196616 | tf_op jit(solution)/shard_map/ppermute | solution.py:391
  13.9 2.0 %copy-start.6 = (f32[512]{0:T(512)S(1)}, f32[512]{0:T(512)}, u32[]{:S(2)}) copy-start(f32[512]{0:T(512)} %param.14) | copy-start | bytes 6148
  13.9 5.4 %collective-permute-start.9 = (bf16[64,512]{1,0:T(8,128)(2,1)S(1)}, bf16[64,512]{1,0:T(8,128)(2,1)S(1)}, u32[]{:S(2)}, u32[]{:S(2)}) collective-permute-start(bf16[64,512]{1,0:T(8,128)(2,1)S(1)} %carry.8.refs_0_), channel_id=1, source_target_pairs={{0,4},{1,5},{2,6},{3,7},{4,0},{5,1},{6,2},{7,3},{8,12},{9,13},{10,... | collective-permute-start | bytes 196616 | tf_op jit(solution)/shard_map/ppermute | solution.py:391
  15.8 1.1 %copy-start.1 = (bf16[256,512]{1,0:T(8,128)(2,1)S(1)}, bf16[256,512]{1,0:T(8,128)(2,1)}, u32[]{:S(2)}) copy-start(bf16[256,512]{1,0:T(8,128)(2,1)} %refs_10_.1) | copy-start | bytes 786436
  17.0 13.5 %collective-permute-start.19 = (bf16[256,512]{1,0:T(8,128)(2,1)S(1)}, bf16[256,512]{1,0:T(8,128)(2,1)S(1)}, u32[]{:S(2)}, u32[]{:S(2)}) collective-permute-start(bf16[256,512]{1,0:T(8,128)(2,1)S(1)} %copy-done.1), channel_id=1, source_target_pairs={{0,1},{1,0},{2,3},{3,2},{4,5},{5,4},{6,7},{7,6},{8,9},{9,8},{10,11... | collective-permute-start | bytes 786440 | tf_op jit(solution)/shard_map/ppermute | solution.py:507
  17.1 7.0 %collective-permute-start.5 = (bf16[64,512]{1,0:T(8,128)(2,1)S(1)}, bf16[64,512]{1,0:T(8,128)(2,1)S(1)}, u32[]{:S(2)}, u32[]{:S(2)}) collective-permute-start(bf16[64,512]{1,0:T(8,128)(2,1)S(1)} %carry.6.refs_0_), channel_id=1, source_target_pairs={{0,4},{1,5},{2,6},{3,7},{4,0},{5,1},{6,2},{7,3},{8,12},{9,13},{10,... | collective-permute-start | bytes 196616 | tf_op jit(solution)/shard_map/ppermute | solution.py:391
  19.5 5.6 %collective-permute-start.16 = (bf16[64,512]{1,0:T(8,128)(2,1)S(1)}, bf16[64,512]{1,0:T(8,128)(2,1)S(1)}, u32[]{:S(2)}, u32[]{:S(2)}) collective-permute-start(bf16[64,512]{1,0:T(8,128)(2,1)S(1)} %get-tuple-element.95.refs_8_), channel_id=1, source_target_pairs={{0,2},{1,3},{2,0},{3,1},{4,6},{5,7},{6,4},{7,5},{8,10},{9,11},{10,... | collective-permute-start | bytes 196616 | tf_op jit(solution)/shard_map/ppermute | solution.py:391
  21.4 4.4 %collective-permute-start.13 = (bf16[64,512]{1,0:T(8,128)(2,1)S(1)}, bf16[64,512]{1,0:T(8,128)(2,1)S(1)}, u32[]{:S(2)}, u32[]{:S(2)}) collective-permute-start(bf16[64,512]{1,0:T(8,128)(2,1)S(1)} %get-tuple-element.94.refs_4_), channel_id=1, source_target_pairs={{0,2},{1,3},{2,0},{3,1},{4,6},{5,7},{6,4},{7,5},{8,10},{9,11},{10,... | collective-permute-start | bytes 196616 | tf_op jit(solution)/shard_map/ppermute | solution.py:391
  24.2 4.3 %collective-permute-start.10 = (bf16[64,512]{1,0:T(8,128)(2,1)S(1)}, bf16[64,512]{1,0:T(8,128)(2,1)S(1)}, u32[]{:S(2)}, u32[]{:S(2)}) collective-permute-start(bf16[64,512]{1,0:T(8,128)(2,1)S(1)} %get-tuple-element.93.refs_0_), channel_id=1, source_target_pairs={{0,2},{1,3},{2,0},{3,1},{4,6},{5,7},{6,4},{7,5},{8,10},{9,11},{10,... | collective-permute-start | bytes 196616 | tf_op jit(solution)/shard_map/ppermute | solution.py:391
  25.0 4.0 %collective-permute-start.18 = (bf16[64,512]{1,0:T(8,128)(2,1)S(1)}, bf16[64,512]{1,0:T(8,128)(2,1)S(1)}, u32[]{:S(2)}, u32[]{:S(2)}) collective-permute-start(bf16[64,512]{1,0:T(8,128)(2,1)S(1)} %collective-permute-done.16.refs_9_), channel_id=1, source_target_pairs={{0,1},{1,0},{2,3},{3,2},{4,5},{5,4},{6,7},{7,6},{8,9},{9,8},{10,11... | collective-permute-start | bytes 196616 | tf_op jit(solution)/shard_map/ppermute | solution.py:402
  25.7 3.3 %collective-permute-start.15 = (bf16[64,512]{1,0:T(8,128)(2,1)S(1)}, bf16[64,512]{1,0:T(8,128)(2,1)S(1)}, u32[]{:S(2)}, u32[]{:S(2)}) collective-permute-start(bf16[64,512]{1,0:T(8,128)(2,1)S(1)} %collective-permute-done.13.refs_5_), channel_id=1, source_target_pairs={{0,1},{1,0},{2,3},{3,2},{4,5},{5,4},{6,7},{7,6},{8,9},{9,8},{10,11... | collective-permute-start | bytes 196616 | tf_op jit(solution)/shard_map/ppermute | solution.py:402
  28.5 1.3 %collective-permute-start.11 = (bf16[64,512]{1,0:T(8,128)(2,1)S(1)}, bf16[64,512]{1,0:T(8,128)(2,1)S(1)}, u32[]{:S(2)}, u32[]{:S(2)}) collective-permute-start(bf16[64,512]{1,0:T(8,128)(2,1)S(1)} %get-tuple-element.93.refs_0_), channel_id=1, source_target_pairs={{0,1},{1,0},{2,3},{3,2},{4,5},{5,4},{6,7},{7,6},{8,9},{9,8},{10,11... | collective-permute-start | bytes 196616 | tf_op jit(solution)/shard_map/ppermute | solution.py:402
  28.5 1.4 %collective-permute-start.14 = (bf16[64,512]{1,0:T(8,128)(2,1)S(1)}, bf16[64,512]{1,0:T(8,128)(2,1)S(1)}, u32[]{:S(2)}, u32[]{:S(2)}) collective-permute-start(bf16[64,512]{1,0:T(8,128)(2,1)S(1)} %get-tuple-element.94.refs_4_), channel_id=1, source_target_pairs={{0,1},{1,0},{2,3},{3,2},{4,5},{5,4},{6,7},{7,6},{8,9},{9,8},{10,11... | collective-permute-start | bytes 196616 | tf_op jit(solution)/shard_map/ppermute | solution.py:402
  29.0 1.3 %collective-permute-start.17 = (bf16[64,512]{1,0:T(8,128)(2,1)S(1)}, bf16[64,512]{1,0:T(8,128)(2,1)S(1)}, u32[]{:S(2)}, u32[]{:S(2)}) collective-permute-start(bf16[64,512]{1,0:T(8,128)(2,1)S(1)} %get-tuple-element.95.refs_8_), channel_id=1, source_target_pairs={{0,1},{1,0},{2,3},{3,2},{4,5},{5,4},{6,7},{7,6},{8,9},{9,8},{10,11... | collective-permute-start | bytes 196616 | tf_op jit(solution)/shard_map/ppermute | solution.py:402
  29.0 1.4 %collective-permute-start.12 = (bf16[64,512]{1,0:T(8,128)(2,1)S(1)}, bf16[64,512]{1,0:T(8,128)(2,1)S(1)}, u32[]{:S(2)}, u32[]{:S(2)}) collective-permute-start(bf16[64,512]{1,0:T(8,128)(2,1)S(1)} %collective-permute-done.10.refs_1_), channel_id=1, source_target_pairs={{0,1},{1,0},{2,3},{3,2},{4,5},{5,4},{6,7},{7,6},{8,9},{9,8},{10,11... | collective-permute-start | bytes 196616 | tf_op jit(solution)/shard_map/ppermute | solution.py:402
  31.2 4.6 %collective-permute-start.22 = (f32[2,512]{1,0:T(2,128)S(1)}, f32[2,512]{1,0:T(2,128)S(1)}, u32[]{:S(2)}, u32[]{:S(2)}) collective-permute-start(f32[2,512]{1,0:T(2,128)S(1)} %get-tuple-element.99.refs_0_), channel_id=1, source_target_pairs={{0,24},{8,16},{16,8},{24,0},{1,25},{9,17},{17,9},{25,1},{2,26},{10... | collective-permute-start | bytes 12296 | tf_op jit(solution)/shard_map/ppermute | solution.py:409
  33.8 3.6 %collective-permute-start.21 = (f32[2,512]{1,0:T(2,128)S(1)}, f32[2,512]{1,0:T(2,128)S(1)}, u32[]{:S(2)}, u32[]{:S(2)}) collective-permute-start(f32[2,512]{1,0:T(2,128)S(1)} %get-tuple-element.99.refs_0_), channel_id=1, source_target_pairs={{0,16},{8,24},{16,0},{24,8},{1,17},{9,25},{17,1},{25,9},{2,18},{10... | collective-permute-start | bytes 12296 | tf_op jit(solution)/shard_map/ppermute | solution.py:409
  34.3 3.6 %collective-permute-start.20 = (f32[2,512]{1,0:T(2,128)S(1)}, f32[2,512]{1,0:T(2,128)S(1)}, u32[]{:S(2)}, u32[]{:S(2)}) collective-permute-start(f32[2,512]{1,0:T(2,128)S(1)} %get-tuple-element.99.refs_0_), channel_id=1, source_target_pairs={{0,8},{8,0},{16,24},{24,16},{1,9},{9,1},{17,25},{25,17},{2,10},{10... | collective-permute-start | bytes 12296 | tf_op jit(solution)/shard_map/ppermute | solution.py:409
  38.7 4.3 %collective-permute-start.25 = (bf16[64,512]{1,0:T(8,128)(2,1)S(1)}, bf16[64,512]{1,0:T(8,128)(2,1)S(1)}, u32[]{:S(2)}, u32[]{:S(2)}) collective-permute-start(bf16[64,512]{1,0:T(8,128)(2,1)S(1)} %get-tuple-element.116), channel_id=1, source_target_pairs={{0,2},{1,3},{2,0},{3,1},{4,6},{5,7},{6,4},{7,5},{8,10},{9,11},{10,... | collective-permute-start | bytes 196616 | tf_op jit(solution)/shard_map/ppermute | solution.py:391
  38.9 5.6 %collective-permute-start.23 = (bf16[64,512]{1,0:T(8,128)(2,1)S(1)}, bf16[64,512]{1,0:T(8,128)(2,1)S(1)}, u32[]{:S(2)}, u32[]{:S(2)}) collective-permute-start(bf16[64,512]{1,0:T(8,128)(2,1)S(1)} %get-tuple-element.112), channel_id=1, source_target_pairs={{0,2},{1,3},{2,0},{3,1},{4,6},{5,7},{6,4},{7,5},{8,10},{9,11},{10,... | collective-permute-start | bytes 196616 | tf_op jit(solution)/shard_map/ppermute | solution.py:391
  40.8 5.6 %collective-permute-start.27 = (bf16[64,512]{1,0:T(8,128)(2,1)S(1)}, bf16[64,512]{1,0:T(8,128)(2,1)S(1)}, u32[]{:S(2)}, u32[]{:S(2)}) collective-permute-start(bf16[64,512]{1,0:T(8,128)(2,1)S(1)} %get-tuple-element.120), channel_id=1, source_target_pairs={{0,2},{1,3},{2,0},{3,1},{4,6},{5,7},{6,4},{7,5},{8,10},{9,11},{10,... | collective-permute-start | bytes 196616 | tf_op jit(solution)/shard_map/ppermute | solution.py:391
  43.1 6.4 %collective-permute-start.26 = (bf16[64,512]{1,0:T(8,128)(2,1)S(1)}, bf16[64,512]{1,0:T(8,128)(2,1)S(1)}, u32[]{:S(2)}, u32[]{:S(2)}) collective-permute-start(bf16[64,512]{1,0:T(8,128)(2,1)S(1)} %carry.10.refs_0_), channel_id=1, source_target_pairs={{0,4},{1,5},{2,6},{3,7},{4,0},{5,1},{6,2},{7,3},{8,12},{9,13},{10,... | collective-permute-start | bytes 196616 | tf_op jit(solution)/shard_map/ppermute | solution.py:391
  44.5 6.4 %collective-permute-start.24 = (bf16[64,512]{1,0:T(8,128)(2,1)S(1)}, bf16[64,512]{1,0:T(8,128)(2,1)S(1)}, u32[]{:S(2)}, u32[]{:S(2)}) collective-permute-start(bf16[64,512]{1,0:T(8,128)(2,1)S(1)} %carry.9.refs_0_), channel_id=1, source_target_pairs={{0,4},{1,5},{2,6},{3,7},{4,0},{5,1},{6,2},{7,3},{8,12},{9,13},{10,... | collective-permute-start | bytes 196616 | tf_op jit(solution)/shard_map/ppermute | solution.py:391
  46.5 5.9 %collective-permute-start.28 = (bf16[64,512]{1,0:T(8,128)(2,1)S(1)}, bf16[64,512]{1,0:T(8,128)(2,1)S(1)}, u32[]{:S(2)}, u32[]{:S(2)}) collective-permute-start(bf16[64,512]{1,0:T(8,128)(2,1)S(1)} %carry.11.refs_0_), channel_id=1, source_target_pairs={{0,4},{1,5},{2,6},{3,7},{4,0},{5,1},{6,2},{7,3},{8,12},{9,13},{10,... | collective-permute-start | bytes 196616 | tf_op jit(solution)/shard_map/ppermute | solution.py:391
  49.7 4.3 %collective-permute-start.32 = (bf16[64,512]{1,0:T(8,128)(2,1)S(1)}, bf16[64,512]{1,0:T(8,128)(2,1)S(1)}, u32[]{:S(2)}, u32[]{:S(2)}) collective-permute-start(bf16[64,512]{1,0:T(8,128)(2,1)S(1)} %get-tuple-element.124.refs_4_), channel_id=1, source_target_pairs={{0,2},{1,3},{2,0},{3,1},{4,6},{5,7},{6,4},{7,5},{8,10},{9,11},{10,... | collective-permute-start | bytes 196616 | tf_op jit(solution)/shard_map/ppermute | solution.py:391
  51.0 4.3 %collective-permute-start.29 = (bf16[64,512]{1,0:T(8,128)(2,1)S(1)}, bf16[64,512]{1,0:T(8,128)(2,1)S(1)}, u32[]{:S(2)}, u32[]{:S(2)}) collective-permute-start(bf16[64,512]{1,0:T(8,128)(2,1)S(1)} %get-tuple-element.123.refs_0_), channel_id=1, source_target_pairs={{0,2},{1,3},{2,0},{3,1},{4,6},{5,7},{6,4},{7,5},{8,10},{9,11},{10,... | collective-permute-start | bytes 196616 | tf_op jit(solution)/shard_map/ppermute | solution.py:391
  52.6 4.3 %collective-permute-start.35 = (bf16[64,512]{1,0:T(8,128)(2,1)S(1)}, bf16[64,512]{1,0:T(8,128)(2,1)S(1)}, u32[]{:S(2)}, u32[]{:S(2)}) collective-permute-start(bf16[64,512]{1,0:T(8,128)(2,1)S(1)} %get-tuple-element.131.refs_0_), channel_id=1, source_target_pairs={{0,2},{1,3},{2,0},{3,1},{4,6},{5,7},{6,4},{7,5},{8,10},{9,11},{10,... | collective-permute-start | bytes 196616 | tf_op jit(solution)/shard_map/ppermute | solution.py:391
  54.0 2.9 %collective-permute-start.34 = (bf16[64,512]{1,0:T(8,128)(2,1)S(1)}, bf16[64,512]{1,0:T(8,128)(2,1)S(1)}, u32[]{:S(2)}, u32[]{:S(2)}) collective-permute-start(bf16[64,512]{1,0:T(8,128)(2,1)S(1)} %collective-permute-done.32.refs_5_), channel_id=1, source_target_pairs={{0,1},{1,0},{2,3},{3,2},{4,5},{5,4},{6,7},{7,6},{8,9},{9,8},{10,11... | collective-permute-start | bytes 196616 | tf_op jit(solution)/shard_map/ppermute | solution.py:402
  55.4 2.1 %collective-permute-start.30 = (bf16[64,512]{1,0:T(8,128)(2,1)S(1)}, bf16[64,512]{1,0:T(8,128)(2,1)S(1)}, u32[]{:S(2)}, u32[]{:S(2)}) collective-permute-start(bf16[64,512]{1,0:T(8,128)(2,1)S(1)} %get-tuple-element.123.refs_0_), channel_id=1, source_target_pairs={{0,1},{1,0},{2,3},{3,2},{4,5},{5,4},{6,7},{7,6},{8,9},{9,8},{10,11... | collective-permute-start | bytes 196616 | tf_op jit(solution)/shard_map/ppermute | solution.py:402
  55.4 2.1 %collective-permute-start.33 = (bf16[64,512]{1,0:T(8,128)(2,1)S(1)}, bf16[64,512]{1,0:T(8,128)(2,1)S(1)}, u32[]{:S(2)}, u32[]{:S(2)}) collective-permute-start(bf16[64,512]{1,0:T(8,128)(2,1)S(1)} %get-tuple-element.124.refs_4_), channel_id=1, source_target_pairs={{0,1},{1,0},{2,3},{3,2},{4,5},{5,4},{6,7},{7,6},{8,9},{9,8},{10,11... | collective-permute-start | bytes 196616 | tf_op jit(solution)/shard_map/ppermute | solution.py:402
  55.9 1.6 %collective-permute-start.31 = (bf16[64,512]{1,0:T(8,128)(2,1)S(1)}, bf16[64,512]{1,0:T(8,128)(2,1)S(1)}, u32[]{:S(2)}, u32[]{:S(2)}) collective-permute-start(bf16[64,512]{1,0:T(8,128)(2,1)S(1)} %collective-permute-done.29.refs_1_), channel_id=1, source_target_pairs={{0,1},{1,0},{2,3},{3,2},{4,5},{5,4},{6,7},{7,6},{8,9},{9,8},{10,11... | collective-permute-start | bytes 196616 | tf_op jit(solution)/shard_map/ppermute | solution.py:402
  56.9 1.3 %collective-permute-start.36 = (bf16[64,512]{1,0:T(8,128)(2,1)S(1)}, bf16[64,512]{1,0:T(8,128)(2,1)S(1)}, u32[]{:S(2)}, u32[]{:S(2)}) collective-permute-start(bf16[64,512]{1,0:T(8,128)(2,1)S(1)} %get-tuple-element.131.refs_0_), channel_id=1, source_target_pairs={{0,1},{1,0},{2,3},{3,2},{4,5},{5,4},{6,7},{7,6},{8,9},{9,8},{10,11... | collective-permute-start | bytes 196616 | tf_op jit(solution)/shard_map/ppermute | solution.py:402
  56.9 1.4 %collective-permute-start.37 = (bf16[64,512]{1,0:T(8,128)(2,1)S(1)}, bf16[64,512]{1,0:T(8,128)(2,1)S(1)}, u32[]{:S(2)}, u32[]{:S(2)}) collective-permute-start(bf16[64,512]{1,0:T(8,128)(2,1)S(1)} %collective-permute-done.35.refs_1_), channel_id=1, source_target_pairs={{0,1},{1,0},{2,3},{3,2},{4,5},{5,4},{6,7},{7,6},{8,9},{9,8},{10,11... | collective-permute-start | bytes 196616 | tf_op jit(solution)/shard_map/ppermute | solution.py:402
  59.1 7.6 %collective-permute-start.38 = (bf16[96,512]{1,0:T(8,128)(2,1)S(1)}, bf16[96,512]{1,0:T(8,128)(2,1)S(1)}, u32[]{:S(2)}, u32[]{:S(2)}) collective-permute-start(bf16[96,512]{1,0:T(8,128)(2,1)S(1)} %get-tuple-element.148), channel_id=1, source_target_pairs={{0,6},{1,7},{2,4},{3,5},{4,2},{5,3},{6,0},{7,1},{8,14},{9,15},{10,... | collective-permute-start | bytes 294920 | tf_op jit(solution)/shard_map/ppermute | solution.py:386
  61.1 9.6 %collective-permute-start.39 = (bf16[96,512]{1,0:T(8,128)(2,1)S(1)}, bf16[96,512]{1,0:T(8,128)(2,1)S(1)}, u32[]{:S(2)}, u32[]{:S(2)}) collective-permute-start(bf16[96,512]{1,0:T(8,128)(2,1)S(1)} %get-tuple-element.149), channel_id=1, source_target_pairs={{0,4},{1,5},{2,6},{3,7},{4,0},{5,1},{6,2},{7,3},{8,12},{9,13},{10,... | collective-permute-start | bytes 294920 | tf_op jit(solution)/shard_map/ppermute | solution.py:386
  61.3 9.3 %collective-permute-start.40 = (bf16[96,512]{1,0:T(8,128)(2,1)S(1)}, bf16[96,512]{1,0:T(8,128)(2,1)S(1)}, u32[]{:S(2)}, u32[]{:S(2)}) collective-permute-start(bf16[96,512]{1,0:T(8,128)(2,1)S(1)} %get-tuple-element.150), channel_id=1, source_target_pairs={{0,2},{1,3},{2,0},{3,1},{4,6},{5,7},{6,4},{7,5},{8,10},{9,11},{10,... | collective-permute-start | bytes 294920 | tf_op jit(solution)/shard_map/ppermute | solution.py:386
  (1 other events, 1.0 us)

commit v17 on v16

--- a/solution.py
+++ b/solution.py
@@ -223,11 +223,23 @@
     send_halves(chips, folds, (gate, up, push, keys, mixed), outs)
 
 
+def prior_kernel(
+    chips, folds, w1t, w3t, w2, go, gx, gain, weighted_ref, p1_ref, p3_ref, p2_ref, gate_ref, up_ref, down_ref
+):
+    weighted_ref[...] = (both(go, gx).astype(F32) * gain[...]).T
+    gate_ref[...] = w1t[...].astype(F32)
+    up_ref[...] = w3t[...].astype(F32)
+    down_ref[...] = w2[...].astype(F32).T
+    parity = lax.axis_index("tok") // CORES % 2
+    cut_half(p1_ref, gate_ref, parity, chips, 1)
+    cut_half(p3_ref, up_ref, parity, chips, 1)
+    cut_half(p2_ref, down_ref, parity, chips, folds)
+
+
 def saved_kernel(
-    chips, folds, ko, kx, vo, vx, ro, rx, w1t, w3t, w2, go, gx, gain,
+    ko, kx, vo, vx, ro, rx, w1t, w3t, w2,
     push_ref, up_slope_ref, silu_ref, back_slope_ref, back_curve_ref,
-    mixed_ref, gate_back_ref, up_back_ref, weighted_ref, p1_ref, p3_ref, p2_ref,
-    gate_ref, up_ref, down_ref,
+    mixed_ref, gate_back_ref, up_back_ref,
 ):
     push = push_of(both(ro, rx, 1), both(vo, vx))
     push_ref[...] = push
@@ -242,14 +254,6 @@
     mixed_ref[...] = mixed[:, :own]
     gate_back_ref[...] = gate_back[:, :own]
     up_back_ref[...] = up_back[:, :own]
-    weighted_ref[...] = (both(go, gx).astype(F32) * gain[...]).T
-    gate_ref[...] = w1t[...].astype(F32)
-    up_ref[...] = w3t[...].astype(F32)
-    down_ref[...] = w2[...].astype(F32).T
-    parity = lax.axis_index("tok") // CORES % 2
-    cut_half(p1_ref, gate_ref, parity, chips, 1)
-    cut_half(p3_ref, up_ref, parity, chips, 1)
-    cut_half(p2_ref, down_ref, parity, chips, folds)
 
 
 def carry_kernel(own, got, out):
@@ -300,7 +304,7 @@
 
 
 def back_kernel(chips, folds, heads, *refs):
-    parts, refs = refs[:heads], refs[heads:]
+    parts, refs = refs[:heads], refs[heads + 1 :]
     sums = parts[0][...]
     for part in parts[1:]:
         sums = sums + part[...]
@@ -519,16 +523,20 @@
         "update",
         6 * product,
     )
-    *saved, weighted, p1, p3, p2 = call(
-        functools.partial(saved_kernel, chips, folds),
-        [((dh, n), BF16)] + [hidden] * 4 + [own_hidden] * 3 + [((dh, n), F32)] + [(half, F32)] * 3,
-        (*keys_values, out_grad, grad_other, gain),
+    weighted, *priors = call(
+        functools.partial(prior_kernel, chips, folds),
+        [((dh, n), F32)] + [(half, F32)] * 3,
+        (w1t, w3t, w2, out_grad, grad_other, gain),
         sums_scratch,
-        "saved",
-        3 * product,
-    )
-    push, up_slope, silu, back_slope, back_curve, mixed, gate_back, up_back = saved
-    priors = p1, p3, p2
+        "priors",
+    )
+    push, up_slope, silu, back_slope, back_curve, mixed, gate_back, up_back = call(
+        saved_kernel,
+        [((dh, n), BF16)] + [hidden] * 4 + [own_hidden] * 3,
+        keys_values,
+        name="saved",
+        flops=3 * product,
+    )
 
     fast, moved = [], []
     for k in range(3):
@@ -554,7 +562,7 @@
         functools.partial(back_kernel, chips, folds, heads),
         [own_hidden] * 2 + half_shares,
         (
-            *head_parts(part, heads),
+            *head_parts(part, heads), up_back,
             f2t, output, weighted, q_mixed, q_slope, q_silu, query_input, query_other,
         ),
         operands,

time: 71.5 us -> 71.3 us (level)
  waiting for transfers between devices: 25.7 us -> 24.6 us
    ppermute x3, waiting for transfers between devices: 3.06 us -> 2.15 us  [head_parts(): lax.ppermute(part, 'head', [(h, partner(h, step, heads)) for h in range(h...]
    pallas_call x21 -> x22, Pallas kernels: 9.46 us -> 9.74 us  [call(): pl.pallas_call(kernel, out_shape=[jax.ShapeDtypeStruct(s, t) for s, t in...]
  transfers between devices with their start and end apart: 41 -> 41, of which waited for: 24 -> 23; matrix products, arithmetic and copies ran while one was open for 2% -> 2% of each run, Pallas kernels for 9% -> 9%
where the time goes in v17:
time: 71.3 us; the launch traced here: 71.1 us
  starting transfers between devices  33.4 us (47%)
  waiting for transfers between devices  24.6 us (35%)
  Pallas kernels  9.74 us (14%)
  local copies, waits for them, and re-layouts  2.59 us (4%)
  between operations  0.89 us (1%)
    ppermute x18, starting transfers between devices, to_chip(): return lax.ppermute(x, 'tok', chip_perm(chips * CORES, step))  22.2 us
    ppermute x18, waiting for transfers between devices, to_chip(): return lax.ppermute(x, 'tok', chip_perm(chips * CORES, step))  16.7 us
    pallas_call x22, Pallas kernels, call(): pl.pallas_call(kernel, out_shape=[jax.ShapeDtypeStruct(s, t) for s, t in...  9.74 us
    ppermute x3, waiting for transfers between devices, exchange(): lax.ppermute(pieces[s], 'tok', chip_perm(count, s))  4.76 us
    ppermute x3, starting transfers between devices, exchange(): lax.ppermute(pieces[s], 'tok', chip_perm(count, s))  4.45 us
    ppermute x3, starting transfers between devices, head_parts(): lax.ppermute(part, 'head', [(h, partner(h, step, heads)) for h in range(h...  3.57 us
    unnamed x18, local copies, waits for them, and re-layouts  2.59 us
    ppermute x3, waiting for transfers between devices, head_parts(): lax.ppermute(part, 'head', [(h, partner(h, step, heads)) for h in range(h...  2.15 us
  transfers between devices with their start and end apart: 41, of which 23 were waited for; matrix products, arithmetic and copies ran while one was open for 2% of the time, Pallas kernels for 9%

profile of v17, /device:TPU:0, one launch (start us, length us, event | category | flops | bytes accessed | tf_op | source)
XLA Modules:
  0.0 71.1 jit_solution(16387653628101975727)
XLA Ops:
  0.6 0.5 collective-permute-start.2
  1.8 1.1 %copy.15 = bf16[1,512,256]{1,2,0:T(8,128)(2,1)S(1)} copy(bf16[1,512,256]{2,1,0:T(8,128)(2,1)} %param.15) | data formatting | bytes 524288 | tf_op args[6]
  3.1 0.7 %copy-done = bf16[256,512]{1,0:T(8,128)(2,1)S(1)} copy-done((bf16[256,512]{1,0:T(8,128)(2,1)S(1)}, bf16[256,512]{1,0:T(8,128)(2,1)}, u32[]{:S(2)}) %copy-start) | copy-done | bytes 262168
  4.0 1.1 %update.1 = (f32[64,512]{1,0:T(8,128)S(1)}, f32[64,512]{1,0:T(8,128)S(1)}, f32[64,512]{1,0:T(8,128)S(1)}, bf16[64,512]{1,0:T(8,128)(2,1)S(1)}, bf16[64,512]{1,0:T(8,128)(2,1)S(1)}, /*index=5*/bf16[64,512]{1,0:T(8,128)(2,1)S(1)}) custom-call(bf16[256,512]{1,0:T(8,128)(2,1)S(1)} %copy-done, bf16[256,512]{1,0:T(8,128)(2,1)S(1)} %collective-permute-done.1.kx.refs_9_.refs_5_, ...), custom_call_target="tpu_custom_call" | custom-call | flops 805306368 | bytes 1837056 | tf_op jit(solution)/shard_map/update/pallas_call | solution.py:372
  5.1 3.1 %collective-permute-start.8 = (bf16[64,512]{1,0:T(8,128)(2,1)S(1)}, bf16[64,512]{1,0:T(8,128)(2,1)S(1)}, u32[]{:S(2)}, u32[]{:S(2)}) collective-permute-start(bf16[64,512]{1,0:T(8,128)(2,1)S(1)} %get-tuple-element.90), channel_id=1, source_target_pairs={{0,2},{1,3},{2,0},{3,1},{4,6},{5,7},{6,4},{7,5},{8,10},{9,11},{10,... | collective-permute-start | bytes 196616 | tf_op jit(solution)/shard_map/ppermute | solution.py:395
  8.2 1.9 %collective-permute-start.4 = (bf16[64,512]{1,0:T(8,128)(2,1)S(1)}, bf16[64,512]{1,0:T(8,128)(2,1)S(1)}, u32[]{:S(2)}, u32[]{:S(2)}) collective-permute-start(bf16[64,512]{1,0:T(8,128)(2,1)S(1)} %get-tuple-element.82), channel_id=1, source_target_pairs={{0,2},{1,3},{2,0},{3,1},{4,6},{5,7},{6,4},{7,5},{8,10},{9,11},{10,... | collective-permute-start | bytes 196616 | tf_op jit(solution)/shard_map/ppermute | solution.py:395
  10.6 3.2 %collective-permute-start.9 = (bf16[64,512]{1,0:T(8,128)(2,1)S(1)}, bf16[64,512]{1,0:T(8,128)(2,1)S(1)}, u32[]{:S(2)}, u32[]{:S(2)}) collective-permute-start(bf16[64,512]{1,0:T(8,128)(2,1)S(1)} %carry.8.refs_0_), channel_id=1, source_target_pairs={{0,4},{1,5},{2,6},{3,7},{4,0},{5,1},{6,2},{7,3},{8,12},{9,13},{10,... | collective-permute-start | bytes 196616 | tf_op jit(solution)/shard_map/ppermute | solution.py:395
  13.9 1.9 %collective-permute-start.7 = (bf16[64,512]{1,0:T(8,128)(2,1)S(1)}, bf16[64,512]{1,0:T(8,128)(2,1)S(1)}, u32[]{:S(2)}, u32[]{:S(2)}) collective-permute-start(bf16[64,512]{1,0:T(8,128)(2,1)S(1)} %carry.7.refs_0_), channel_id=1, source_target_pairs={{0,4},{1,5},{2,6},{3,7},{4,0},{5,1},{6,2},{7,3},{8,12},{9,13},{10,... | collective-permute-start | bytes 196616 | tf_op jit(solution)/shard_map/ppermute | solution.py:395
  16.8 1.1 %collective-permute-start.5 = (bf16[64,512]{1,0:T(8,128)(2,1)S(1)}, bf16[64,512]{1,0:T(8,128)(2,1)S(1)}, u32[]{:S(2)}, u32[]{:S(2)}) collective-permute-start(bf16[64,512]{1,0:T(8,128)(2,1)S(1)} %carry.6.refs_0_), channel_id=1, source_target_pairs={{0,4},{1,5},{2,6},{3,7},{4,0},{5,1},{6,2},{7,3},{8,12},{9,13},{10,... | collective-permute-start | bytes 196616 | tf_op jit(solution)/shard_map/ppermute | solution.py:395
  17.9 0.5 collective-permute-done.9.refs_1_
  18.6 1.5 %collective-permute-start.16 = (bf16[64,512]{1,0:T(8,128)(2,1)S(1)}, bf16[64,512]{1,0:T(8,128)(2,1)S(1)}, u32[]{:S(2)}, u32[]{:S(2)}) collective-permute-start(bf16[64,512]{1,0:T(8,128)(2,1)S(1)} %get-tuple-element.95.refs_8_), channel_id=1, source_target_pairs={{0,2},{1,3},{2,0},{3,1},{4,6},{5,7},{6,4},{7,5},{8,10},{9,11},{10,... | collective-permute-start | bytes 196616 | tf_op jit(solution)/shard_map/ppermute | solution.py:395
  20.2 1.0 %collective-permute-start.13 = (bf16[64,512]{1,0:T(8,128)(2,1)S(1)}, bf16[64,512]{1,0:T(8,128)(2,1)S(1)}, u32[]{:S(2)}, u32[]{:S(2)}) collective-permute-start(bf16[64,512]{1,0:T(8,128)(2,1)S(1)} %get-tuple-element.94.refs_4_), channel_id=1, source_target_pairs={{0,2},{1,3},{2,0},{3,1},{4,6},{5,7},{6,4},{7,5},{8,10},{9,11},{10,... | collective-permute-start | bytes 196616 | tf_op jit(solution)/shard_map/ppermute | solution.py:395
  21.2 2.6 %collective-permute-done.5.refs_1_ = bf16[64,512]{1,0:T(8,128)(2,1)S(1)} collective-permute-done((bf16[64,512]{1,0:T(8,128)(2,1)S(1)}, bf16[64,512]{1,0:T(8,128)(2,1)S(1)}, u32[]{:S(2)}, u32[]{:S(2)}) %collective-permute-start.5) | collective-permute-done | bytes 65568 | tf_op jit(solution)/shard_map/ppermute | solution.py:395
  24.1 1.0 %collective-permute-done.13.refs_5_ = bf16[64,512]{1,0:T(8,128)(2,1)S(1)} collective-permute-done((bf16[64,512]{1,0:T(8,128)(2,1)S(1)}, bf16[64,512]{1,0:T(8,128)(2,1)S(1)}, u32[]{:S(2)}, u32[]{:S(2)}) %collective-permute-start.13) | collective-permute-done | bytes 65568 | tf_op jit(solution)/shard_map/ppermute | solution.py:395
  25.1 3.2 %collective-permute-done.10.refs_1_ = bf16[64,512]{1,0:T(8,128)(2,1)S(1)} collective-permute-done((bf16[64,512]{1,0:T(8,128)(2,1)S(1)}, bf16[64,512]{1,0:T(8,128)(2,1)S(1)}, u32[]{:S(2)}, u32[]{:S(2)}) %collective-permute-start.10) | collective-permute-done | bytes 65568 | tf_op jit(solution)/shard_map/ppermute | solution.py:395
  28.3 0.5 collective-permute-start.14
  28.8 0.5 collective-permute-start.12
  30.2 0.8 %apply.1 = (bf16[256,512]{1,0:T(8,128)(2,1)S(1)}, bf16[256,512]{1,0:T(8,128)(2,1)S(1)}, bf16[512,256]{1,0:T(8,128)(2,1)S(1)}, f32[512,512]{1,0:T(8,128)S(1)}, bf...) custom-call(bf16[64,512]{1,0:T(8,128)(2,1)S(1)} %get-tuple-element.93.refs_0, ...), custom_call_target="tpu_custom_call" | custom-call | flops 402653184 | bytes 2359296 | tf_op jit(solution)/shard_map/apply/pallas_call | solution.py:372
  31.0 2.5 %collective-permute-start.22 = (f32[2,512]{1,0:T(2,128)S(1)}, f32[2,512]{1,0:T(2,128)S(1)}, u32[]{:S(2)}, u32[]{:S(2)}) collective-permute-start(f32[2,512]{1,0:T(2,128)S(1)} %get-tuple-element.99.refs_0_), channel_id=1, source_target_pairs={{0,24},{8,16},{16,8},{24,0},{1,25},{9,17},{17,9},{25,1},{2,26},{10... | collective-permute-start | bytes 12296 | tf_op jit(solution)/shard_map/ppermute | solution.py:413
  33.5 0.5 collective-permute-start.21
  34.0 0.5 collective-permute-start.20
  34.6 0.9 %saved.1 = (bf16[512,512]{1,0:T(8,128)(2,1)S(1)}, f32[256,512]{1,0:T(8,128)S(1)}, f32[256,512]{1,0:T(8,128)S(1)}, f32[256,512]{1,0:T(8,128)S(1)}, f32[256,512]{1...) custom-call(bf16[256,512]{1,0:T(8,128)(2,1)S(1)} %copy-done, ...), custom_call_target="tpu_custom_call" | custom-call | flops 402653184 | bytes 1837056 | tf_op jit(solution)/shard_map/saved/pallas_call | solution.py:372
  35.6 1.5 %collective-permute-done.21.refs_2_ = f32[2,512]{1,0:T(2,128)S(1)} collective-permute-done((f32[2,512]{1,0:T(2,128)S(1)}, f32[2,512]{1,0:T(2,128)S(1)}, u32[]{:S(2)}, u32[]{:S(2)}) %collective-permute-start.21) | collective-permute-done | bytes 4128 | tf_op jit(solution)/shard_map/ppermute | solution.py:413
  37.1 0.5 collective-permute-done.20.refs_1_
  37.6 0.8 %apply_back.1 = (bf16[256,256]{1,0:T(8,128)(2,1)S(1)}, bf16[256,256]{1,0:T(8,128)(2,1)S(1)}, f32[64,512]{1,0:T(8,128)S(1)}, f32[64,512]{1,0:T(8,128)S(1)}, f32[6...) custom-call(f32[2,512]{1,0:T(2,128)S(1)} %get-tuple-element.99.refs_0, ...), custom_call_target="tpu_custom_call" | custom-call | flops 536870912 | bytes 4341760 | tf_op jit(solution)/shard_map/apply_back/pallas_call | solution.py:372
  38.6 1.9 %collective-permute-start.23 = (bf16[64,512]{1,0:T(8,128)(2,1)S(1)}, bf16[64,512]{1,0:T(8,128)(2,1)S(1)}, u32[]{:S(2)}, u32[]{:S(2)}) collective-permute-start(bf16[64,512]{1,0:T(8,128)(2,1)S(1)} %get-tuple-element.113), channel_id=1, source_target_pairs={{0,2},{1,3},{2,0},{3,1},{4,6},{5,7},{6,4},{7,5},{8,10},{9,11},{10,... | collective-permute-start | bytes 196616 | tf_op jit(solution)/shard_map/ppermute | solution.py:395
  40.7 2.1 %collective-permute-done.25.got = bf16[64,512]{1,0:T(8,128)(2,1)S(1)} collective-permute-done((bf16[64,512]{1,0:T(8,128)(2,1)S(1)}, bf16[64,512]{1,0:T(8,128)(2,1)S(1)}, u32[]{:S(2)}, u32[]{:S(2)}) %collective-permute-start.25) | collective-permute-done | bytes 65568 | tf_op jit(solution)/shard_map/ppermute | solution.py:395
  42.8 1.3 %collective-permute-start.26 = (bf16[64,512]{1,0:T(8,128)(2,1)S(1)}, bf16[64,512]{1,0:T(8,128)(2,1)S(1)}, u32[]{:S(2)}, u32[]{:S(2)}) collective-permute-start(bf16[64,512]{1,0:T(8,128)(2,1)S(1)} %carry.10.refs_0_), channel_id=1, source_target_pairs={{0,4},{1,5},{2,6},{3,7},{4,0},{5,1},{6,2},{7,3},{8,12},{9,13},{10,... | collective-permute-start | bytes 196616 | tf_op jit(solution)/shard_map/ppermute | solution.py:395
  44.1 1.8 %collective-permute-start.24 = (bf16[64,512]{1,0:T(8,128)(2,1)S(1)}, bf16[64,512]{1,0:T(8,128)(2,1)S(1)}, u32[]{:S(2)}, u32[]{:S(2)}) collective-permute-start(bf16[64,512]{1,0:T(8,128)(2,1)S(1)} %carry.9.refs_0_), channel_id=1, source_target_pairs={{0,4},{1,5},{2,6},{3,7},{4,0},{5,1},{6,2},{7,3},{8,12},{9,13},{10,... | collective-permute-start | bytes 196616 | tf_op jit(solution)/shard_map/ppermute | solution.py:395
  46.2 1.0 %collective-permute-start.28 = (bf16[64,512]{1,0:T(8,128)(2,1)S(1)}, bf16[64,512]{1,0:T(8,128)(2,1)S(1)}, u32[]{:S(2)}, u32[]{:S(2)}) collective-permute-start(bf16[64,512]{1,0:T(8,128)(2,1)S(1)} %carry.11.refs_0_), channel_id=1, source_target_pairs={{0,4},{1,5},{2,6},{3,7},{4,0},{5,1},{6,2},{7,3},{8,12},{9,13},{10,... | collective-permute-start | bytes 196616 | tf_op jit(solution)/shard_map/ppermute | solution.py:395
  47.2 2.1 %collective-permute-done.26.refs_1_ = bf16[64,512]{1,0:T(8,128)(2,1)S(1)} collective-permute-done((bf16[64,512]{1,0:T(8,128)(2,1)S(1)}, bf16[64,512]{1,0:T(8,128)(2,1)S(1)}, u32[]{:S(2)}, u32[]{:S(2)}) %collective-permute-start.26) | collective-permute-done | bytes 65568 | tf_op jit(solution)/shard_map/ppermute | solution.py:395
  49.5 1.1 %collective-permute-done.24.refs_1_ = bf16[64,512]{1,0:T(8,128)(2,1)S(1)} collective-permute-done((bf16[64,512]{1,0:T(8,128)(2,1)S(1)}, bf16[64,512]{1,0:T(8,128)(2,1)S(1)}, u32[]{:S(2)}, u32[]{:S(2)}) %collective-permute-start.24) | collective-permute-done | bytes 65568 | tf_op jit(solution)/shard_map/ppermute | solution.py:395
  50.8 1.0 %collective-permute-start.29 = (bf16[64,512]{1,0:T(8,128)(2,1)S(1)}, bf16[64,512]{1,0:T(8,128)(2,1)S(1)}, u32[]{:S(2)}, u32[]{:S(2)}) collective-permute-start(bf16[64,512]{1,0:T(8,128)(2,1)S(1)} %get-tuple-element.124.refs_0_), channel_id=1, source_target_pairs={{0,2},{1,3},{2,0},{3,1},{4,6},{5,7},{6,4},{7,5},{8,10},{9,11},{10,... | collective-permute-start | bytes 196616 | tf_op jit(solution)/shard_map/ppermute | solution.py:395
  52.3 0.8 %collective-permute-start.35 = (bf16[64,512]{1,0:T(8,128)(2,1)S(1)}, bf16[64,512]{1,0:T(8,128)(2,1)S(1)}, u32[]{:S(2)}, u32[]{:S(2)}) collective-permute-start(bf16[64,512]{1,0:T(8,128)(2,1)S(1)} %get-tuple-element.132.refs_0_), channel_id=1, source_target_pairs={{0,2},{1,3},{2,0},{3,1},{4,6},{5,7},{6,4},{7,5},{8,10},{9,11},{10,... | collective-permute-start | bytes 196616 | tf_op jit(solution)/shard_map/ppermute | solution.py:395
  53.1 0.6 collective-permute-done.32.refs_5_
  53.7 1.4 %collective-permute-done.29.refs_1_ = bf16[64,512]{1,0:T(8,128)(2,1)S(1)} collective-permute-done((bf16[64,512]{1,0:T(8,128)(2,1)S(1)}, bf16[64,512]{1,0:T(8,128)(2,1)S(1)}, u32[]{:S(2)}, u32[]{:S(2)}) %collective-permute-start.29) | collective-permute-done | bytes 65568 | tf_op jit(solution)/shard_map/ppermute | solution.py:395
  55.1 0.5 collective-permute-start.33
  55.6 1.0 %collective-permute-done.35.refs_1_ = bf16[64,512]{1,0:T(8,128)(2,1)S(1)} collective-permute-done((bf16[64,512]{1,0:T(8,128)(2,1)S(1)}, bf16[64,512]{1,0:T(8,128)(2,1)S(1)}, u32[]{:S(2)}, u32[]{:S(2)}) %collective-permute-start.35) | collective-permute-done | bytes 65568 | tf_op jit(solution)/shard_map/ppermute | solution.py:395
  56.7 0.5 collective-permute-start.37
  57.2 0.8 %second_first.1 = (bf16[256,512]{1,0:T(8,128)(2,1)S(1)}, bf16[256,512]{1,0:T(8,128)(2,1)S(1)}, bf16[256,256]{1,0:T(8,128)(2,1)S(1)}, f32[128,512]{1,0:T(8,128)S(...) custom-call(bf16[64,512]{1,0:T(8,128)(2,1)S(1)} %get-tuple-element.124.refs_0_, ...), custom_call_target="tpu_custom_call" | custom-call | flops 402653184 | bytes 3670016 | tf_op jit(solution)/shard_map/second_first/pallas_call | solution.py:372
  58.1 0.7 %second_last.1 = (bf16[512,256]{1,0:T(8,128)(2,1)S(1)}, bf16[256,256]{1,0:T(8,128)(2,1)S(1)}, bf16[256,256]{1,0:T(8,128)(2,1)S(1)}, f32[96,512]{1,0:T(8,128)S(1)...) custom-call(bf16[64,512]{1,0:T(8,128)(2,1)S(1)} %get-tuple-element.132.refs_0_, ...), custom_call_target="tpu_custom_call" | custom-call | flops 402653184 | bytes 3670016 | tf_op jit(solution)/shard_map/second_last/pallas_call | solution.py:372
  58.8 2.0 %collective-permute-start.38 = (bf16[96,512]{1,0:T(8,128)(2,1)S(1)}, bf16[96,512]{1,0:T(8,128)(2,1)S(1)}, u32[]{:S(2)}, u32[]{:S(2)}) collective-permute-start(bf16[96,512]{1,0:T(8,128)(2,1)S(1)} %get-tuple-element.148), channel_id=1, source_target_pairs={{0,6},{1,7},{2,4},{3,5},{4,2},{5,3},{6,0},{7,1},{8,14},{9,15},{10,... | collective-permute-start | bytes 294920 | tf_op jit(solution)/shard_map/ppermute | solution.py:390
  61.1 2.2 %collective-permute-start.40 = (bf16[96,512]{1,0:T(8,128)(2,1)S(1)}, bf16[96,512]{1,0:T(8,128)(2,1)S(1)}, u32[]{:S(2)}, u32[]{:S(2)}) collective-permute-start(bf16[96,512]{1,0:T(8,128)(2,1)S(1)} %get-tuple-element.150), channel_id=1, source_target_pairs={{0,2},{1,3},{2,0},{3,1},{4,6},{5,7},{6,4},{7,5},{8,10},{9,11},{10,... | collective-permute-start | bytes 294920 | tf_op jit(solution)/shard_map/ppermute | solution.py:390
  63.3 1.0 %query_grad.1 = bf16[256,512]{1,0:T(8,128)(2,1)} custom-call(bf16[256,256]{1,0:T(8,128)(2,1)S(1)} %get-tuple-element.106.gate_back, bf16[256,256]{1,0:T(8,128)(2,1)S(1)} %get-tuple-element.107.up_back, bf16[256,512]{1,0:T(8,128)(2,1)S(1)} %get-tuple-element.108.f1t, bf16[256,512]{1,0:T(8,128)(2,1)S(1)} %get-tuple-element.109.f3t), custom_call_target="tpu_custom_call" | custom-call | flops 134217728 | bytes 786432 | tf_op jit(solution)/shard_map/query_grad/pallas_call | solution.py:372
  64.3 1.4 %token_grads.1 = (bf16[256,512]{1,0:T(8,128)(2,1)}, bf16[256,512]{1,0:T(8,128)(2,1)}) custom-call(f32[1,256]{1,0:T(1,128)S(1)} %bitcast.33, bf16[256,256]{1,0:T(8,128)(2,1)S(1)} %get-tuple-element.110.refs_1_, bf16[256,256]{1,0:T(8,128)(2,1)S(1)} %get-tuple-element.131.refs_2_, bf16[256,256]{1,0:T(8,128)(2,1)S(1)} %get-tuple-element.136.refs_3_, ...), custom_call_target="tpu_custom_call" | custom-call | flops 402653184 | bytes 2360320 | tf_op jit(solution)/shard_map/token_grads/pallas_call | solution.py:372
  65.7 0.7 %collective-permute-done.38.refs_4_ = bf16[96,512]{1,0:T(8,128)(2,1)S(1)} collective-permute-done((bf16[96,512]{1,0:T(8,128)(2,1)S(1)}, bf16[96,512]{1,0:T(8,128)(2,1)S(1)}, u32[]{:S(2)}, u32[]{:S(2)}) %collective-permute-start.38) | collective-permute-done | bytes 98336 | tf_op jit(solution)/shard_map/ppermute | solution.py:390
  66.4 4.0 %collective-permute-done.39.refs_5_ = bf16[96,512]{1,0:T(8,128)(2,1)S(1)} collective-permute-done((bf16[96,512]{1,0:T(8,128)(2,1)S(1)}, bf16[96,512]{1,0:T(8,128)(2,1)S(1)}, u32[]{:S(2)}, u32[]{:S(2)}) %collective-permute-start.39) | collective-permute-done | bytes 98336 | tf_op jit(solution)/shard_map/ppermute | solution.py:390
  70.4 0.7 owner_result.1
  (74 shorter events, 6.0 us)
Async XLA Ops:
  0.6 1.0 %copy-start.5 = (f32[256,1]{0,1:T(1,128)S(1)}, f32[256,1]{0,1:T(1,128)}, u32[]{:S(2)}) copy-start(f32[256,1]{0,1:T(1,128)} %param.13) | copy-start | bytes 3076
  0.6 2.5 %collective-permute-start.2 = (bf16[256,512]{1,0:T(8,128)(2,1)}, bf16[256,512]{1,0:T(8,128)(2,1)S(1)}, u32[]{:S(2)}, u32[]{:S(2)}) collective-permute-start(bf16[256,512]{1,0:T(8,128)(2,1)} %vo.3), channel_id=1, source_target_pairs={{0,1},{1,0},{2,3},{3,2},{4,5},{5,4},{6,7},{7,6},{8,9},{9,8},{10,11... | collective-permute-start | bytes 786440 | tf_op jit(solution)/shard_map/ppermute | solution.py:511
  1.2 2.0 %collective-permute-start.1 = (bf16[256,512]{1,0:T(8,128)(2,1)}, bf16[256,512]{1,0:T(8,128)(2,1)S(1)}, u32[]{:S(2)}, u32[]{:S(2)}) collective-permute-start(bf16[256,512]{1,0:T(8,128)(2,1)} %refs_4_.1), channel_id=1, source_target_pairs={{0,1},{1,0},{2,3},{3,2},{4,5},{5,4},{6,7},{7,6},{8,9},{9,8},{10,11... | collective-permute-start | bytes 786440 | tf_op jit(solution)/shard_map/ppermute | solution.py:511
  1.2 14.6 %collective-permute-start = (bf16[256,512]{1,0:T(8,128)(2,1)}, bf16[256,512]{1,0:T(8,128)(2,1)S(1)}, u32[]{:S(2)}, u32[]{:S(2)}) collective-permute-start(bf16[256,512]{1,0:T(8,128)(2,1)} %go.1), channel_id=1, source_target_pairs={{0,1},{1,0},{2,3},{3,2},{4,5},{5,4},{6,7},{7,6},{8,9},{9,8},{10,11... | collective-permute-start | bytes 786440 | tf_op jit(solution)/shard_map/ppermute | solution.py:511
  1.7 1.2 %copy-start.7 = (bf16[1,512,256]{2,1,0:T(8,128)(2,1)S(1)}, bf16[1,512,256]{2,1,0:T(8,128)(2,1)}, u32[]{:S(2)}) copy-start(bf16[1,512,256]{2,1,0:T(8,128)(2,1)} %param.16) | copy-start | bytes 786436
  1.7 1.4 %collective-permute-start.3 = (f32[1,256]{1,0:T(1,128)S(1)}, f32[1,256]{1,0:T(1,128)S(1)}, u32[]{:S(2)}, u32[]{:S(2)}) collective-permute-start(f32[1,256]{1,0:T(1,128)S(1)} %bitcast.30), channel_id=1, source_target_pairs={{0,1},{1,0},{2,3},{3,2},{4,5},{5,4},{6,7},{7,6},{8,9},{9,8},{10,11... | collective-permute-start | bytes 3080 | tf_op jit(solution)/shard_map/ppermute | solution.py:511
  1.8 1.4 %copy-start.4 = (bf16[256,512]{1,0:T(8,128)(2,1)S(1)}, bf16[256,512]{1,0:T(8,128)(2,1)}, u32[]{:S(2)}) copy-start(bf16[256,512]{1,0:T(8,128)(2,1)} %vo.3) | copy-start | bytes 786436
  2.9 1.0 %copy-start = (bf16[256,512]{1,0:T(8,128)(2,1)S(1)}, bf16[256,512]{1,0:T(8,128)(2,1)}, u32[]{:S(2)}) copy-start(bf16[256,512]{1,0:T(8,128)(2,1)} %refs_4_.1) | copy-start | bytes 786436
  2.9 1.0 %copy-start.1 = (bf16[1,256,512]{2,1,0:T(8,128)(2,1)S(1)}, bf16[1,256,512]{2,1,0:T(8,128)(2,1)}, u32[]{:S(2)}) copy-start(bf16[1,256,512]{2,1,0:T(8,128)(2,1)} %param.17) | copy-start | bytes 786436
  5.1 5.5 %collective-permute-start.8 = (bf16[64,512]{1,0:T(8,128)(2,1)S(1)}, bf16[64,512]{1,0:T(8,128)(2,1)S(1)}, u32[]{:S(2)}, u32[]{:S(2)}) collective-permute-start(bf16[64,512]{1,0:T(8,128)(2,1)S(1)} %get-tuple-element.90), channel_id=1, source_target_pairs={{0,2},{1,3},{2,0},{3,1},{4,6},{5,7},{6,4},{7,5},{8,10},{9,11},{10,... | collective-permute-start | bytes 196616 | tf_op jit(solution)/shard_map/ppermute | solution.py:395
  8.2 5.7 %collective-permute-start.6 = (bf16[64,512]{1,0:T(8,128)(2,1)S(1)}, bf16[64,512]{1,0:T(8,128)(2,1)S(1)}, u32[]{:S(2)}, u32[]{:S(2)}) collective-permute-start(bf16[64,512]{1,0:T(8,128)(2,1)S(1)} %get-tuple-element.86), channel_id=1, source_target_pairs={{0,2},{1,3},{2,0},{3,1},{4,6},{5,7},{6,4},{7,5},{8,10},{9,11},{10,... | collective-permute-start | bytes 196616 | tf_op jit(solution)/shard_map/ppermute | solution.py:395
  8.2 8.6 %collective-permute-start.4 = (bf16[64,512]{1,0:T(8,128)(2,1)S(1)}, bf16[64,512]{1,0:T(8,128)(2,1)S(1)}, u32[]{:S(2)}, u32[]{:S(2)}) collective-permute-start(bf16[64,512]{1,0:T(8,128)(2,1)S(1)} %get-tuple-element.82), channel_id=1, source_target_pairs={{0,2},{1,3},{2,0},{3,1},{4,6},{5,7},{6,4},{7,5},{8,10},{9,11},{10,... | collective-permute-start | bytes 196616 | tf_op jit(solution)/shard_map/ppermute | solution.py:395
  10.6 5.2 %copy-start.3 = (bf16[256,512]{1,0:T(8,128)(2,1)S(1)}, bf16[256,512]{1,0:T(8,128)(2,1)}, u32[]{:S(2)}) copy-start(bf16[256,512]{1,0:T(8,128)(2,1)} %go.1) | copy-start | bytes 786436
  10.6 7.8 %collective-permute-start.9 = (bf16[64,512]{1,0:T(8,128)(2,1)S(1)}, bf16[64,512]{1,0:T(8,128)(2,1)S(1)}, u32[]{:S(2)}, u32[]{:S(2)}) collective-permute-start(bf16[64,512]{1,0:T(8,128)(2,1)S(1)} %carry.8.refs_0_), channel_id=1, source_target_pairs={{0,4},{1,5},{2,6},{3,7},{4,0},{5,1},{6,2},{7,3},{8,12},{9,13},{10,... | collective-permute-start | bytes 196616 | tf_op jit(solution)/shard_map/ppermute | solution.py:395
  13.9 2.0 %copy-start.6 = (f32[512]{0:T(512)S(1)}, f32[512]{0:T(512)}, u32[]{:S(2)}) copy-start(f32[512]{0:T(512)} %param.14) | copy-start | bytes 6148
  13.9 6.2 %collective-permute-start.7 = (bf16[64,512]{1,0:T(8,128)(2,1)S(1)}, bf16[64,512]{1,0:T(8,128)(2,1)S(1)}, u32[]{:S(2)}, u32[]{:S(2)}) collective-permute-start(bf16[64,512]{1,0:T(8,128)(2,1)S(1)} %carry.7.refs_0_), channel_id=1, source_target_pairs={{0,4},{1,5},{2,6},{3,7},{4,0},{5,1},{6,2},{7,3},{8,12},{9,13},{10,... | collective-permute-start | bytes 196616 | tf_op jit(solution)/shard_map/ppermute | solution.py:395
  16.8 13.4 %collective-permute-start.19 = (bf16[256,512]{1,0:T(8,128)(2,1)S(1)}, bf16[256,512]{1,0:T(8,128)(2,1)S(1)}, u32[]{:S(2)}, u32[]{:S(2)}) collective-permute-start(bf16[256,512]{1,0:T(8,128)(2,1)S(1)} %copy-done.2), channel_id=1, source_target_pairs={{0,1},{1,0},{2,3},{3,2},{4,5},{5,4},{6,7},{7,6},{8,9},{9,8},{10,11... | collective-permute-start | bytes 786440 | tf_op jit(solution)/shard_map/ppermute | solution.py:511
  16.8 7.0 %collective-permute-start.5 = (bf16[64,512]{1,0:T(8,128)(2,1)S(1)}, bf16[64,512]{1,0:T(8,128)(2,1)S(1)}, u32[]{:S(2)}, u32[]{:S(2)}) collective-permute-start(bf16[64,512]{1,0:T(8,128)(2,1)S(1)} %carry.6.refs_0_), channel_id=1, source_target_pairs={{0,4},{1,5},{2,6},{3,7},{4,0},{5,1},{6,2},{7,3},{8,12},{9,13},{10,... | collective-permute-start | bytes 196616 | tf_op jit(solution)/shard_map/ppermute | solution.py:395
  18.6 5.6 %collective-permute-start.16 = (bf16[64,512]{1,0:T(8,128)(2,1)S(1)}, bf16[64,512]{1,0:T(8,128)(2,1)S(1)}, u32[]{:S(2)}, u32[]{:S(2)}) collective-permute-start(bf16[64,512]{1,0:T(8,128)(2,1)S(1)} %get-tuple-element.95.refs_8_), channel_id=1, source_target_pairs={{0,2},{1,3},{2,0},{3,1},{4,6},{5,7},{6,4},{7,5},{8,10},{9,11},{10,... | collective-permute-start | bytes 196616 | tf_op jit(solution)/shard_map/ppermute | solution.py:395
  20.2 4.9 %collective-permute-start.13 = (bf16[64,512]{1,0:T(8,128)(2,1)S(1)}, bf16[64,512]{1,0:T(8,128)(2,1)S(1)}, u32[]{:S(2)}, u32[]{:S(2)}) collective-permute-start(bf16[64,512]{1,0:T(8,128)(2,1)S(1)} %get-tuple-element.94.refs_4_), channel_id=1, source_target_pairs={{0,2},{1,3},{2,0},{3,1},{4,6},{5,7},{6,4},{7,5},{8,10},{9,11},{10,... | collective-permute-start | bytes 196616 | tf_op jit(solution)/shard_map/ppermute | solution.py:395
  23.9 4.3 %collective-permute-start.10 = (bf16[64,512]{1,0:T(8,128)(2,1)S(1)}, bf16[64,512]{1,0:T(8,128)(2,1)S(1)}, u32[]{:S(2)}, u32[]{:S(2)}) collective-permute-start(bf16[64,512]{1,0:T(8,128)(2,1)S(1)} %get-tuple-element.93.refs_0_), channel_id=1, source_target_pairs={{0,2},{1,3},{2,0},{3,1},{4,6},{5,7},{6,4},{7,5},{8,10},{9,11},{10,... | collective-permute-start | bytes 196616 | tf_op jit(solution)/shard_map/ppermute | solution.py:395
  24.1 4.6 %collective-permute-start.18 = (bf16[64,512]{1,0:T(8,128)(2,1)S(1)}, bf16[64,512]{1,0:T(8,128)(2,1)S(1)}, u32[]{:S(2)}, u32[]{:S(2)}) collective-permute-start(bf16[64,512]{1,0:T(8,128)(2,1)S(1)} %collective-permute-done.16.refs_9_), channel_id=1, source_target_pairs={{0,1},{1,0},{2,3},{3,2},{4,5},{5,4},{6,7},{7,6},{8,9},{9,8},{10,11... | collective-permute-start | bytes 196616 | tf_op jit(solution)/shard_map/ppermute | solution.py:406
  25.1 3.7 %collective-permute-start.15 = (bf16[64,512]{1,0:T(8,128)(2,1)S(1)}, bf16[64,512]{1,0:T(8,128)(2,1)S(1)}, u32[]{:S(2)}, u32[]{:S(2)}) collective-permute-start(bf16[64,512]{1,0:T(8,128)(2,1)S(1)} %collective-permute-done.13.refs_5_), channel_id=1, source_target_pairs={{0,1},{1,0},{2,3},{3,2},{4,5},{5,4},{6,7},{7,6},{8,9},{9,8},{10,11... | collective-permute-start | bytes 196616 | tf_op jit(solution)/shard_map/ppermute | solution.py:406
  28.3 1.3 %collective-permute-start.11 = (bf16[64,512]{1,0:T(8,128)(2,1)S(1)}, bf16[64,512]{1,0:T(8,128)(2,1)S(1)}, u32[]{:S(2)}, u32[]{:S(2)}) collective-permute-start(bf16[64,512]{1,0:T(8,128)(2,1)S(1)} %get-tuple-element.93.refs_0_), channel_id=1, source_target_pairs={{0,1},{1,0},{2,3},{3,2},{4,5},{5,4},{6,7},{7,6},{8,9},{9,8},{10,11... | collective-permute-start | bytes 196616 | tf_op jit(solution)/shard_map/ppermute | solution.py:406
  28.3 1.4 %collective-permute-start.14 = (bf16[64,512]{1,0:T(8,128)(2,1)S(1)}, bf16[64,512]{1,0:T(8,128)(2,1)S(1)}, u32[]{:S(2)}, u32[]{:S(2)}) collective-permute-start(bf16[64,512]{1,0:T(8,128)(2,1)S(1)} %get-tuple-element.94.refs_4_), channel_id=1, source_target_pairs={{0,1},{1,0},{2,3},{3,2},{4,5},{5,4},{6,7},{7,6},{8,9},{9,8},{10,11... | collective-permute-start | bytes 196616 | tf_op jit(solution)/shard_map/ppermute | solution.py:406
  28.8 1.3 %collective-permute-start.17 = (bf16[64,512]{1,0:T(8,128)(2,1)S(1)}, bf16[64,512]{1,0:T(8,128)(2,1)S(1)}, u32[]{:S(2)}, u32[]{:S(2)}) collective-permute-start(bf16[64,512]{1,0:T(8,128)(2,1)S(1)} %get-tuple-element.95.refs_8_), channel_id=1, source_target_pairs={{0,1},{1,0},{2,3},{3,2},{4,5},{5,4},{6,7},{7,6},{8,9},{9,8},{10,11... | collective-permute-start | bytes 196616 | tf_op jit(solution)/shard_map/ppermute | solution.py:406
  28.8 1.4 %collective-permute-start.12 = (bf16[64,512]{1,0:T(8,128)(2,1)S(1)}, bf16[64,512]{1,0:T(8,128)(2,1)S(1)}, u32[]{:S(2)}, u32[]{:S(2)}) collective-permute-start(bf16[64,512]{1,0:T(8,128)(2,1)S(1)} %collective-permute-done.10.refs_1_), channel_id=1, source_target_pairs={{0,1},{1,0},{2,3},{3,2},{4,5},{5,4},{6,7},{7,6},{8,9},{9,8},{10,11... | collective-permute-start | bytes 196616 | tf_op jit(solution)/shard_map/ppermute | solution.py:406
  31.0 4.6 %collective-permute-start.22 = (f32[2,512]{1,0:T(2,128)S(1)}, f32[2,512]{1,0:T(2,128)S(1)}, u32[]{:S(2)}, u32[]{:S(2)}) collective-permute-start(f32[2,512]{1,0:T(2,128)S(1)} %get-tuple-element.99.refs_0_), channel_id=1, source_target_pairs={{0,24},{8,16},{16,8},{24,0},{1,25},{9,17},{17,9},{25,1},{2,26},{10... | collective-permute-start | bytes 12296 | tf_op jit(solution)/shard_map/ppermute | solution.py:413
  33.5 3.6 %collective-permute-start.21 = (f32[2,512]{1,0:T(2,128)S(1)}, f32[2,512]{1,0:T(2,128)S(1)}, u32[]{:S(2)}, u32[]{:S(2)}) collective-permute-start(f32[2,512]{1,0:T(2,128)S(1)} %get-tuple-element.99.refs_0_), channel_id=1, source_target_pairs={{0,16},{8,24},{16,0},{24,8},{1,17},{9,25},{17,1},{25,9},{2,18},{10... | collective-permute-start | bytes 12296 | tf_op jit(solution)/shard_map/ppermute | solution.py:413
  34.0 3.6 %collective-permute-start.20 = (f32[2,512]{1,0:T(2,128)S(1)}, f32[2,512]{1,0:T(2,128)S(1)}, u32[]{:S(2)}, u32[]{:S(2)}) collective-permute-start(f32[2,512]{1,0:T(2,128)S(1)} %get-tuple-element.99.refs_0_), channel_id=1, source_target_pairs={{0,8},{8,0},{16,24},{24,16},{1,9},{9,1},{17,25},{25,17},{2,10},{10... | collective-permute-start | bytes 12296 | tf_op jit(solution)/shard_map/ppermute | solution.py:413
  38.5 4.3 %collective-permute-start.25 = (bf16[64,512]{1,0:T(8,128)(2,1)S(1)}, bf16[64,512]{1,0:T(8,128)(2,1)S(1)}, u32[]{:S(2)}, u32[]{:S(2)}) collective-permute-start(bf16[64,512]{1,0:T(8,128)(2,1)S(1)} %get-tuple-element.117), channel_id=1, source_target_pairs={{0,2},{1,3},{2,0},{3,1},{4,6},{5,7},{6,4},{7,5},{8,10},{9,11},{10,... | collective-permute-start | bytes 196616 | tf_op jit(solution)/shard_map/ppermute | solution.py:395
  38.6 5.4 %collective-permute-start.23 = (bf16[64,512]{1,0:T(8,128)(2,1)S(1)}, bf16[64,512]{1,0:T(8,128)(2,1)S(1)}, u32[]{:S(2)}, u32[]{:S(2)}) collective-permute-start(bf16[64,512]{1,0:T(8,128)(2,1)S(1)} %get-tuple-element.113), channel_id=1, source_target_pairs={{0,2},{1,3},{2,0},{3,1},{4,6},{5,7},{6,4},{7,5},{8,10},{9,11},{10,... | collective-permute-start | bytes 196616 | tf_op jit(solution)/shard_map/ppermute | solution.py:395
  40.6 5.6 %collective-permute-start.27 = (bf16[64,512]{1,0:T(8,128)(2,1)S(1)}, bf16[64,512]{1,0:T(8,128)(2,1)S(1)}, u32[]{:S(2)}, u32[]{:S(2)}) collective-permute-start(bf16[64,512]{1,0:T(8,128)(2,1)S(1)} %get-tuple-element.121), channel_id=1, source_target_pairs={{0,2},{1,3},{2,0},{3,1},{4,6},{5,7},{6,4},{7,5},{8,10},{9,11},{10,... | collective-permute-start | bytes 196616 | tf_op jit(solution)/shard_map/ppermute | solution.py:395
  42.8 6.5 %collective-permute-start.26 = (bf16[64,512]{1,0:T(8,128)(2,1)S(1)}, bf16[64,512]{1,0:T(8,128)(2,1)S(1)}, u32[]{:S(2)}, u32[]{:S(2)}) collective-permute-start(bf16[64,512]{1,0:T(8,128)(2,1)S(1)} %carry.10.refs_0_), channel_id=1, source_target_pairs={{0,4},{1,5},{2,6},{3,7},{4,0},{5,1},{6,2},{7,3},{8,12},{9,13},{10,... | collective-permute-start | bytes 196616 | tf_op jit(solution)/shard_map/ppermute | solution.py:395
  44.1 6.5 %collective-permute-start.24 = (bf16[64,512]{1,0:T(8,128)(2,1)S(1)}, bf16[64,512]{1,0:T(8,128)(2,1)S(1)}, u32[]{:S(2)}, u32[]{:S(2)}) collective-permute-start(bf16[64,512]{1,0:T(8,128)(2,1)S(1)} %carry.9.refs_0_), channel_id=1, source_target_pairs={{0,4},{1,5},{2,6},{3,7},{4,0},{5,1},{6,2},{7,3},{8,12},{9,13},{10,... | collective-permute-start | bytes 196616 | tf_op jit(solution)/shard_map/ppermute | solution.py:395
  46.2 5.9 %collective-permute-start.28 = (bf16[64,512]{1,0:T(8,128)(2,1)S(1)}, bf16[64,512]{1,0:T(8,128)(2,1)S(1)}, u32[]{:S(2)}, u32[]{:S(2)}) collective-permute-start(bf16[64,512]{1,0:T(8,128)(2,1)S(1)} %carry.11.refs_0_), channel_id=1, source_target_pairs={{0,4},{1,5},{2,6},{3,7},{4,0},{5,1},{6,2},{7,3},{8,12},{9,13},{10,... | collective-permute-start | bytes 196616 | tf_op jit(solution)/shard_map/ppermute | solution.py:395
  49.4 4.3 %collective-permute-start.32 = (bf16[64,512]{1,0:T(8,128)(2,1)S(1)}, bf16[64,512]{1,0:T(8,128)(2,1)S(1)}, u32[]{:S(2)}, u32[]{:S(2)}) collective-permute-start(bf16[64,512]{1,0:T(8,128)(2,1)S(1)} %get-tuple-element.125.refs_4_), channel_id=1, source_target_pairs={{0,2},{1,3},{2,0},{3,1},{4,6},{5,7},{6,4},{7,5},{8,10},{9,11},{10,... | collective-permute-start | bytes 196616 | tf_op jit(solution)/shard_map/ppermute | solution.py:395
  50.8 4.3 %collective-permute-start.29 = (bf16[64,512]{1,0:T(8,128)(2,1)S(1)}, bf16[64,512]{1,0:T(8,128)(2,1)S(1)}, u32[]{:S(2)}, u32[]{:S(2)}) collective-permute-start(bf16[64,512]{1,0:T(8,128)(2,1)S(1)} %get-tuple-element.124.refs_0_), channel_id=1, source_target_pairs={{0,2},{1,3},{2,0},{3,1},{4,6},{5,7},{6,4},{7,5},{8,10},{9,11},{10,... | collective-permute-start | bytes 196616 | tf_op jit(solution)/shard_map/ppermute | solution.py:395
  52.3 4.3 %collective-permute-start.35 = (bf16[64,512]{1,0:T(8,128)(2,1)S(1)}, bf16[64,512]{1,0:T(8,128)(2,1)S(1)}, u32[]{:S(2)}, u32[]{:S(2)}) collective-permute-start(bf16[64,512]{1,0:T(8,128)(2,1)S(1)} %get-tuple-element.132.refs_0_), channel_id=1, source_target_pairs={{0,2},{1,3},{2,0},{3,1},{4,6},{5,7},{6,4},{7,5},{8,10},{9,11},{10,... | collective-permute-start | bytes 196616 | tf_op jit(solution)/shard_map/ppermute | solution.py:395
  53.7 2.9 %collective-permute-start.34 = (bf16[64,512]{1,0:T(8,128)(2,1)S(1)}, bf16[64,512]{1,0:T(8,128)(2,1)S(1)}, u32[]{:S(2)}, u32[]{:S(2)}) collective-permute-start(bf16[64,512]{1,0:T(8,128)(2,1)S(1)} %collective-permute-done.32.refs_5_), channel_id=1, source_target_pairs={{0,1},{1,0},{2,3},{3,2},{4,5},{5,4},{6,7},{7,6},{8,9},{9,8},{10,11... | collective-permute-start | bytes 196616 | tf_op jit(solution)/shard_map/ppermute | solution.py:406
  55.1 2.1 %collective-permute-start.30 = (bf16[64,512]{1,0:T(8,128)(2,1)S(1)}, bf16[64,512]{1,0:T(8,128)(2,1)S(1)}, u32[]{:S(2)}, u32[]{:S(2)}) collective-permute-start(bf16[64,512]{1,0:T(8,128)(2,1)S(1)} %get-tuple-element.124.refs_0_), channel_id=1, source_target_pairs={{0,1},{1,0},{2,3},{3,2},{4,5},{5,4},{6,7},{7,6},{8,9},{9,8},{10,11... | collective-permute-start | bytes 196616 | tf_op jit(solution)/shard_map/ppermute | solution.py:406
  55.1 2.1 %collective-permute-start.33 = (bf16[64,512]{1,0:T(8,128)(2,1)S(1)}, bf16[64,512]{1,0:T(8,128)(2,1)S(1)}, u32[]{:S(2)}, u32[]{:S(2)}) collective-permute-start(bf16[64,512]{1,0:T(8,128)(2,1)S(1)} %get-tuple-element.125.refs_4_), channel_id=1, source_target_pairs={{0,1},{1,0},{2,3},{3,2},{4,5},{5,4},{6,7},{7,6},{8,9},{9,8},{10,11... | collective-permute-start | bytes 196616 | tf_op jit(solution)/shard_map/ppermute | solution.py:406
  55.6 1.6 %collective-permute-start.31 = (bf16[64,512]{1,0:T(8,128)(2,1)S(1)}, bf16[64,512]{1,0:T(8,128)(2,1)S(1)}, u32[]{:S(2)}, u32[]{:S(2)}) collective-permute-start(bf16[64,512]{1,0:T(8,128)(2,1)S(1)} %collective-permute-done.29.refs_1_), channel_id=1, source_target_pairs={{0,1},{1,0},{2,3},{3,2},{4,5},{5,4},{6,7},{7,6},{8,9},{9,8},{10,11... | collective-permute-start | bytes 196616 | tf_op jit(solution)/shard_map/ppermute | solution.py:406
  56.6 1.4 %collective-permute-start.36 = (bf16[64,512]{1,0:T(8,128)(2,1)S(1)}, bf16[64,512]{1,0:T(8,128)(2,1)S(1)}, u32[]{:S(2)}, u32[]{:S(2)}) collective-permute-start(bf16[64,512]{1,0:T(8,128)(2,1)S(1)} %get-tuple-element.132.refs_0_), channel_id=1, source_target_pairs={{0,1},{1,0},{2,3},{3,2},{4,5},{5,4},{6,7},{7,6},{8,9},{9,8},{10,11... | collective-permute-start | bytes 196616 | tf_op jit(solution)/shard_map/ppermute | solution.py:406
  56.7 1.4 %collective-permute-start.37 = (bf16[64,512]{1,0:T(8,128)(2,1)S(1)}, bf16[64,512]{1,0:T(8,128)(2,1)S(1)}, u32[]{:S(2)}, u32[]{:S(2)}) collective-permute-start(bf16[64,512]{1,0:T(8,128)(2,1)S(1)} %collective-permute-done.35.refs_1_), channel_id=1, source_target_pairs={{0,1},{1,0},{2,3},{3,2},{4,5},{5,4},{6,7},{7,6},{8,9},{9,8},{10,11... | collective-permute-start | bytes 196616 | tf_op jit(solution)/shard_map/ppermute | solution.py:406
  58.8 7.6 %collective-permute-start.38 = (bf16[96,512]{1,0:T(8,128)(2,1)S(1)}, bf16[96,512]{1,0:T(8,128)(2,1)S(1)}, u32[]{:S(2)}, u32[]{:S(2)}) collective-permute-start(bf16[96,512]{1,0:T(8,128)(2,1)S(1)} %get-tuple-element.148), channel_id=1, source_target_pairs={{0,6},{1,7},{2,4},{3,5},{4,2},{5,3},{6,0},{7,1},{8,14},{9,15},{10,... | collective-permute-start | bytes 294920 | tf_op jit(solution)/shard_map/ppermute | solution.py:390
  60.8 9.6 %collective-permute-start.39 = (bf16[96,512]{1,0:T(8,128)(2,1)S(1)}, bf16[96,512]{1,0:T(8,128)(2,1)S(1)}, u32[]{:S(2)}, u32[]{:S(2)}) collective-permute-start(bf16[96,512]{1,0:T(8,128)(2,1)S(1)} %get-tuple-element.149), channel_id=1, source_target_pairs={{0,4},{1,5},{2,6},{3,7},{4,0},{5,1},{6,2},{7,3},{8,12},{9,13},{10,... | collective-permute-start | bytes 294920 | tf_op jit(solution)/shard_map/ppermute | solution.py:390
  61.1 9.3 %collective-permute-start.40 = (bf16[96,512]{1,0:T(8,128)(2,1)S(1)}, bf16[96,512]{1,0:T(8,128)(2,1)S(1)}, u32[]{:S(2)}, u32[]{:S(2)}) collective-permute-start(bf16[96,512]{1,0:T(8,128)(2,1)S(1)} %get-tuple-element.150), channel_id=1, source_target_pairs={{0,2},{1,3},{2,0},{3,1},{4,6},{5,7},{6,4},{7,5},{8,10},{9,11},{10,... | collective-permute-start | bytes 294920 | tf_op jit(solution)/shard_map/ppermute | solution.py:390
  (1 other events, 1.0 us)

commit v18 on v17

--- a/solution.py
+++ b/solution.py
@@ -511,7 +511,7 @@
     pair = lambda x: lax.ppermute(x, "tok", core_perm(count))
     key_other, value_other, rate_other = pair(key_input), pair(value_input), pair(rates)
     w1t, w3t = w1.T, w3.T
-    grad_other = pair(out_grad)
+    query_other, grad_other = pair(query_input), pair(out_grad)
     keys_values = (
         key_input, key_other, value_input, value_other, rates, rate_other, w1t, w3t, w2,
     )
@@ -549,8 +549,6 @@
         )
         moved.append(rows_moved)
         fast.append(rows)
-    query_later, weighted = lax.optimization_barrier((query_input, weighted))
-    query_other = pair(query_later)
     f1t, f3t, f2t, output, q_mixed, q_slope, q_silu, part = call(
         functools.partial(apply_kernel, chips, folds),
         matrices + [((dh, n), F32), ((fh, n), BF16), hidden, hidden, ((2, n), F32)],

time: 71.3 us -> 72 us (level)
  starting transfers between devices: 33.4 us -> 38.5 us
  waiting for transfers between devices: 24.6 us -> 20.5 us
    ppermute x18, starting transfers between devices: 22.2 us -> 27.3 us  [to_chip(): return lax.ppermute(x, 'tok', chip_perm(chips * CORES, step))]
    ppermute x18, waiting for transfers between devices: 16.7 us -> 11.9 us  [to_chip(): return lax.ppermute(x, 'tok', chip_perm(chips * CORES, step))]
  transfers between devices with their start and end apart: 41 -> 41, of which waited for: 23 -> 22; matrix products, arithmetic and copies ran while one was open for 2% -> 2% of each run, Pallas kernels for 9% -> 9%
where the time goes in v18:
time: 72 us; the launch traced here: 71.8 us
  starting transfers between devices  38.5 us (53%)
  waiting for transfers between devices  20.5 us (28%)
  Pallas kernels  9.74 us (14%)
  local copies, waits for them, and re-layouts  2.12 us (3%)
  between operations  0.89 us (1%)
    ppermute x18, starting transfers between devices, to_chip(): return lax.ppermute(x, 'tok', chip_perm(chips * CORES, step))  27.3 us
    ppermute x18, waiting for transfers between devices, to_chip(): return lax.ppermute(x, 'tok', chip_perm(chips * CORES, step))  11.9 us
    pallas_call x22, Pallas kernels, call(): pl.pallas_call(kernel, out_shape=[jax.ShapeDtypeStruct(s, t) for s, t in...  9.74 us
    ppermute x3, waiting for transfers between devices, exchange(): lax.ppermute(pieces[s], 'tok', chip_perm(count, s))  4.86 us
    ppermute x3, starting transfers between devices, exchange(): lax.ppermute(pieces[s], 'tok', chip_perm(count, s))  4.45 us
    ppermute x3, starting transfers between devices, head_parts(): lax.ppermute(part, 'head', [(h, partner(h, step, heads)) for h in range(h...  3.55 us
    ppermute x3, waiting for transfers between devices, head_parts(): lax.ppermute(part, 'head', [(h, partner(h, step, heads)) for h in range(h...  2.49 us
    unnamed x18, local copies, waits for them, and re-layouts  2.12 us
  transfers between devices with their start and end apart: 41, of which 22 were waited for; matrix products, arithmetic and copies ran while one was open for 2% of the time, Pallas kernels for 9%

profile of v18, /device:TPU:0, one launch (start us, length us, event | category | flops | bytes accessed | tf_op | source)
XLA Modules:
  0.0 71.8 jit_solution(10375966984565685004)
XLA Ops:
  0.6 0.5 collective-permute-start.2
  1.8 1.1 %copy.15 = bf16[1,512,256]{1,2,0:T(8,128)(2,1)S(1)} copy(bf16[1,512,256]{2,1,0:T(8,128)(2,1)} %param.15) | data formatting | bytes 524288 | tf_op args[6]
  3.1 0.7 %copy-done = bf16[256,512]{1,0:T(8,128)(2,1)S(1)} copy-done((bf16[256,512]{1,0:T(8,128)(2,1)S(1)}, bf16[256,512]{1,0:T(8,128)(2,1)}, u32[]{:S(2)}) %copy-start) | copy-done | bytes 262168
  4.0 1.1 %update.1 = (f32[64,512]{1,0:T(8,128)S(1)}, f32[64,512]{1,0:T(8,128)S(1)}, f32[64,512]{1,0:T(8,128)S(1)}, bf16[64,512]{1,0:T(8,128)(2,1)S(1)}, bf16[64,512]{1,0:T(8,128)(2,1)S(1)}, /*index=5*/bf16[64,512]{1,0:T(8,128)(2,1)S(1)}) custom-call(bf16[256,512]{1,0:T(8,128)(2,1)S(1)} %copy-done, bf16[256,512]{1,0:T(8,128)(2,1)S(1)} %collective-permute-done.1.kx.refs_9_.refs_5_, ...), custom_call_target="tpu_custom_call" | custom-call | flops 805306368 | bytes 1837056 | tf_op jit(solution)/shard_map/update/pallas_call | solution.py:372
  5.1 3.1 %collective-permute-start.8 = (bf16[64,512]{1,0:T(8,128)(2,1)S(1)}, bf16[64,512]{1,0:T(8,128)(2,1)S(1)}, u32[]{:S(2)}, u32[]{:S(2)}) collective-permute-start(bf16[64,512]{1,0:T(8,128)(2,1)S(1)} %get-tuple-element.88), channel_id=1, source_target_pairs={{0,2},{1,3},{2,0},{3,1},{4,6},{5,7},{6,4},{7,5},{8,10},{9,11},{10,... | collective-permute-start | bytes 196616 | tf_op jit(solution)/shard_map/ppermute | solution.py:395
  8.3 1.9 %collective-permute-start.6 = (bf16[64,512]{1,0:T(8,128)(2,1)S(1)}, bf16[64,512]{1,0:T(8,128)(2,1)S(1)}, u32[]{:S(2)}, u32[]{:S(2)}) collective-permute-start(bf16[64,512]{1,0:T(8,128)(2,1)S(1)} %get-tuple-element.84), channel_id=1, source_target_pairs={{0,2},{1,3},{2,0},{3,1},{4,6},{5,7},{6,4},{7,5},{8,10},{9,11},{10,... | collective-permute-start | bytes 196616 | tf_op jit(solution)/shard_map/ppermute | solution.py:395
  10.5 3.0 %collective-permute-start.9 = (bf16[64,512]{1,0:T(8,128)(2,1)S(1)}, bf16[64,512]{1,0:T(8,128)(2,1)S(1)}, u32[]{:S(2)}, u32[]{:S(2)}) collective-permute-start(bf16[64,512]{1,0:T(8,128)(2,1)S(1)} %carry.8.refs_0_), channel_id=1, source_target_pairs={{0,4},{1,5},{2,6},{3,7},{4,0},{5,1},{6,2},{7,3},{8,12},{9,13},{10,... | collective-permute-start | bytes 196616 | tf_op jit(solution)/shard_map/ppermute | solution.py:395
  13.6 2.2 %collective-permute-start.5 = (bf16[64,512]{1,0:T(8,128)(2,1)S(1)}, bf16[64,512]{1,0:T(8,128)(2,1)S(1)}, u32[]{:S(2)}, u32[]{:S(2)}) collective-permute-start(bf16[64,512]{1,0:T(8,128)(2,1)S(1)} %carry.6.refs_0_), channel_id=1, source_target_pairs={{0,4},{1,5},{2,6},{3,7},{4,0},{5,1},{6,2},{7,3},{8,12},{9,13},{10,... | collective-permute-start | bytes 196616 | tf_op jit(solution)/shard_map/ppermute | solution.py:395
  15.8 1.4 %collective-permute-start.7 = (bf16[64,512]{1,0:T(8,128)(2,1)S(1)}, bf16[64,512]{1,0:T(8,128)(2,1)S(1)}, u32[]{:S(2)}, u32[]{:S(2)}) collective-permute-start(bf16[64,512]{1,0:T(8,128)(2,1)S(1)} %carry.7.refs_0_), channel_id=1, source_target_pairs={{0,4},{1,5},{2,6},{3,7},{4,0},{5,1},{6,2},{7,3},{8,12},{9,13},{10,... | collective-permute-start | bytes 196616 | tf_op jit(solution)/shard_map/ppermute | solution.py:395
  17.8 3.0 %collective-permute-start.16 = (bf16[64,512]{1,0:T(8,128)(2,1)S(1)}, bf16[64,512]{1,0:T(8,128)(2,1)S(1)}, u32[]{:S(2)}, u32[]{:S(2)}) collective-permute-start(bf16[64,512]{1,0:T(8,128)(2,1)S(1)} %get-tuple-element.93.refs_8_), channel_id=1, source_target_pairs={{0,2},{1,3},{2,0},{3,1},{4,6},{5,7},{6,4},{7,5},{8,10},{9,11},{10,... | collective-permute-start | bytes 196616 | tf_op jit(solution)/shard_map/ppermute | solution.py:395
  21.2 1.3 %collective-permute-start.10 = (bf16[64,512]{1,0:T(8,128)(2,1)S(1)}, bf16[64,512]{1,0:T(8,128)(2,1)S(1)}, u32[]{:S(2)}, u32[]{:S(2)}) collective-permute-start(bf16[64,512]{1,0:T(8,128)(2,1)S(1)} %get-tuple-element.91.refs_0_), channel_id=1, source_target_pairs={{0,2},{1,3},{2,0},{3,1},{4,6},{5,7},{6,4},{7,5},{8,10},{9,11},{10,... | collective-permute-start | bytes 196616 | tf_op jit(solution)/shard_map/ppermute | solution.py:395
  23.5 0.5 collective-permute-done.16.refs_9_
  24.1 1.6 %collective-permute-done.10.refs_1_ = bf16[64,512]{1,0:T(8,128)(2,1)S(1)} collective-permute-done((bf16[64,512]{1,0:T(8,128)(2,1)S(1)}, bf16[64,512]{1,0:T(8,128)(2,1)S(1)}, u32[]{:S(2)}, u32[]{:S(2)}) %collective-permute-start.10) | collective-permute-done | bytes 65568 | tf_op jit(solution)/shard_map/ppermute | solution.py:395
  25.6 0.5 collective-permute-start.14
  26.1 1.3 %collective-permute-done.13.refs_5_ = bf16[64,512]{1,0:T(8,128)(2,1)S(1)} collective-permute-done((bf16[64,512]{1,0:T(8,128)(2,1)S(1)}, bf16[64,512]{1,0:T(8,128)(2,1)S(1)}, u32[]{:S(2)}, u32[]{:S(2)}) %collective-permute-start.13) | collective-permute-done | bytes 65568 | tf_op jit(solution)/shard_map/ppermute | solution.py:395
  27.5 0.5 collective-permute-start.17
  28.1 0.7 collective-permute-done.15.refs_7_
  29.2 0.8 %apply.1 = (bf16[256,512]{1,0:T(8,128)(2,1)S(1)}, bf16[256,512]{1,0:T(8,128)(2,1)S(1)}, bf16[512,256]{1,0:T(8,128)(2,1)S(1)}, f32[512,512]{1,0:T(8,128)S(1)}, bf...) custom-call(bf16[64,512]{1,0:T(8,128)(2,1)S(1)} %get-tuple-element.91.refs_0, ...), custom_call_target="tpu_custom_call" | custom-call | flops 402653184 | bytes 2359296 | tf_op jit(solution)/shard_map/apply/pallas_call | solution.py:372
  30.0 2.9 %collective-permute-start.22 = (f32[2,512]{1,0:T(2,128)S(1)}, f32[2,512]{1,0:T(2,128)S(1)}, u32[]{:S(2)}, u32[]{:S(2)}) collective-permute-start(f32[2,512]{1,0:T(2,128)S(1)} %get-tuple-element.95.refs_0_), channel_id=1, source_target_pairs={{0,24},{8,16},{16,8},{24,0},{1,25},{9,17},{17,9},{25,1},{2,26},{10... | collective-permute-start | bytes 12296 | tf_op jit(solution)/shard_map/ppermute | solution.py:413
  32.9 0.5 collective-permute-start.21
  33.6 0.9 %saved.1 = (bf16[512,512]{1,0:T(8,128)(2,1)S(1)}, f32[256,512]{1,0:T(8,128)S(1)}, f32[256,512]{1,0:T(8,128)S(1)}, f32[256,512]{1,0:T(8,128)S(1)}, f32[256,512]{1...) custom-call(bf16[256,512]{1,0:T(8,128)(2,1)S(1)} %copy-done, ...), custom_call_target="tpu_custom_call" | custom-call | flops 402653184 | bytes 1837056 | tf_op jit(solution)/shard_map/saved/pallas_call | solution.py:372
  34.6 1.9 %collective-permute-done.21.refs_2_ = f32[2,512]{1,0:T(2,128)S(1)} collective-permute-done((f32[2,512]{1,0:T(2,128)S(1)}, f32[2,512]{1,0:T(2,128)S(1)}, u32[]{:S(2)}, u32[]{:S(2)}) %collective-permute-start.21) | collective-permute-done | bytes 4128 | tf_op jit(solution)/shard_map/ppermute | solution.py:413
  37.0 0.8 %apply_back.1 = (bf16[256,256]{1,0:T(8,128)(2,1)S(1)}, bf16[256,256]{1,0:T(8,128)(2,1)S(1)}, f32[64,512]{1,0:T(8,128)S(1)}, f32[64,512]{1,0:T(8,128)S(1)}, f32[6...) custom-call(f32[2,512]{1,0:T(2,128)S(1)} %get-tuple-element.95.refs_0, ...), custom_call_target="tpu_custom_call" | custom-call | flops 536870912 | bytes 4341760 | tf_op jit(solution)/shard_map/apply_back/pallas_call | solution.py:372
  37.8 0.9 %collective-permute-start.25 = (bf16[64,512]{1,0:T(8,128)(2,1)S(1)}, bf16[64,512]{1,0:T(8,128)(2,1)S(1)}, u32[]{:S(2)}, u32[]{:S(2)}) collective-permute-start(bf16[64,512]{1,0:T(8,128)(2,1)S(1)} %get-tuple-element.113), channel_id=1, source_target_pairs={{0,2},{1,3},{2,0},{3,1},{4,6},{5,7},{6,4},{7,5},{8,10},{9,11},{10,... | collective-permute-start | bytes 196616 | tf_op jit(solution)/shard_map/ppermute | solution.py:395
  38.7 1.2 %collective-permute-start.23 = (bf16[64,512]{1,0:T(8,128)(2,1)S(1)}, bf16[64,512]{1,0:T(8,128)(2,1)S(1)}, u32[]{:S(2)}, u32[]{:S(2)}) collective-permute-start(bf16[64,512]{1,0:T(8,128)(2,1)S(1)} %get-tuple-element.109), channel_id=1, source_target_pairs={{0,2},{1,3},{2,0},{3,1},{4,6},{5,7},{6,4},{7,5},{8,10},{9,11},{10,... | collective-permute-start | bytes 196616 | tf_op jit(solution)/shard_map/ppermute | solution.py:395
  39.9 0.8 %collective-permute-start.27 = (bf16[64,512]{1,0:T(8,128)(2,1)S(1)}, bf16[64,512]{1,0:T(8,128)(2,1)S(1)}, u32[]{:S(2)}, u32[]{:S(2)}) collective-permute-start(bf16[64,512]{1,0:T(8,128)(2,1)S(1)} %get-tuple-element.117), channel_id=1, source_target_pairs={{0,2},{1,3},{2,0},{3,1},{4,6},{5,7},{6,4},{7,5},{8,10},{9,11},{10,... | collective-permute-start | bytes 196616 | tf_op jit(solution)/shard_map/ppermute | solution.py:395
  40.7 1.4 %collective-permute-done.25.got = bf16[64,512]{1,0:T(8,128)(2,1)S(1)} collective-permute-done((bf16[64,512]{1,0:T(8,128)(2,1)S(1)}, bf16[64,512]{1,0:T(8,128)(2,1)S(1)}, u32[]{:S(2)}, u32[]{:S(2)}) %collective-permute-start.25) | collective-permute-done | bytes 65568 | tf_op jit(solution)/shard_map/ppermute | solution.py:395
  42.2 3.3 %collective-permute-start.26 = (bf16[64,512]{1,0:T(8,128)(2,1)S(1)}, bf16[64,512]{1,0:T(8,128)(2,1)S(1)}, u32[]{:S(2)}, u32[]{:S(2)}) collective-permute-start(bf16[64,512]{1,0:T(8,128)(2,1)S(1)} %carry.10.refs_0_), channel_id=1, source_target_pairs={{0,4},{1,5},{2,6},{3,7},{4,0},{5,1},{6,2},{7,3},{8,12},{9,13},{10,... | collective-permute-start | bytes 196616 | tf_op jit(solution)/shard_map/ppermute | solution.py:395
  45.5 0.7 collective-permute-start.24
  46.2 2.4 %collective-permute-start.28 = (bf16[64,512]{1,0:T(8,128)(2,1)S(1)}, bf16[64,512]{1,0:T(8,128)(2,1)S(1)}, u32[]{:S(2)}, u32[]{:S(2)}) collective-permute-start(bf16[64,512]{1,0:T(8,128)(2,1)S(1)} %carry.11.refs_0_), channel_id=1, source_target_pairs={{0,4},{1,5},{2,6},{3,7},{4,0},{5,1},{6,2},{7,3},{8,12},{9,13},{10,... | collective-permute-start | bytes 196616 | tf_op jit(solution)/shard_map/ppermute | solution.py:395
  48.5 1.2 %collective-permute-done.26.refs_1_ = bf16[64,512]{1,0:T(8,128)(2,1)S(1)} collective-permute-done((bf16[64,512]{1,0:T(8,128)(2,1)S(1)}, bf16[64,512]{1,0:T(8,128)(2,1)S(1)}, u32[]{:S(2)}, u32[]{:S(2)}) %collective-permute-start.26) | collective-permute-done | bytes 65568 | tf_op jit(solution)/shard_map/ppermute | solution.py:395
  49.9 1.4 %collective-permute-done.24.refs_1_ = bf16[64,512]{1,0:T(8,128)(2,1)S(1)} collective-permute-done((bf16[64,512]{1,0:T(8,128)(2,1)S(1)}, bf16[64,512]{1,0:T(8,128)(2,1)S(1)}, u32[]{:S(2)}, u32[]{:S(2)}) %collective-permute-start.24) | collective-permute-done | bytes 65568 | tf_op jit(solution)/shard_map/ppermute | solution.py:395
  51.5 0.7 collective-permute-start.29
  52.2 0.6 collective-permute-done.28.refs_1_
  52.9 0.9 %collective-permute-start.35 = (bf16[64,512]{1,0:T(8,128)(2,1)S(1)}, bf16[64,512]{1,0:T(8,128)(2,1)S(1)}, u32[]{:S(2)}, u32[]{:S(2)}) collective-permute-start(bf16[64,512]{1,0:T(8,128)(2,1)S(1)} %get-tuple-element.128.refs_0_), channel_id=1, source_target_pairs={{0,2},{1,3},{2,0},{3,1},{4,6},{5,7},{6,4},{7,5},{8,10},{9,11},{10,... | collective-permute-start | bytes 196616 | tf_op jit(solution)/shard_map/ppermute | solution.py:395
  54.2 1.6 %collective-permute-done.29.refs_1_ = bf16[64,512]{1,0:T(8,128)(2,1)S(1)} collective-permute-done((bf16[64,512]{1,0:T(8,128)(2,1)S(1)}, bf16[64,512]{1,0:T(8,128)(2,1)S(1)}, u32[]{:S(2)}, u32[]{:S(2)}) %collective-permute-start.29) | collective-permute-done | bytes 65568 | tf_op jit(solution)/shard_map/ppermute | solution.py:395
  55.8 0.5 collective-permute-start.33
  56.3 0.9 %collective-permute-done.35.refs_1_ = bf16[64,512]{1,0:T(8,128)(2,1)S(1)} collective-permute-done((bf16[64,512]{1,0:T(8,128)(2,1)S(1)}, bf16[64,512]{1,0:T(8,128)(2,1)S(1)}, u32[]{:S(2)}, u32[]{:S(2)}) %collective-permute-start.35) | collective-permute-done | bytes 65568 | tf_op jit(solution)/shard_map/ppermute | solution.py:395
  57.2 0.5 collective-permute-start.37
  57.8 0.8 %second_first.1 = (bf16[256,512]{1,0:T(8,128)(2,1)S(1)}, bf16[256,512]{1,0:T(8,128)(2,1)S(1)}, bf16[256,256]{1,0:T(8,128)(2,1)S(1)}, f32[128,512]{1,0:T(8,128)S(...) custom-call(bf16[64,512]{1,0:T(8,128)(2,1)S(1)} %get-tuple-element.120.refs_0_, ...), custom_call_target="tpu_custom_call" | custom-call | flops 402653184 | bytes 3670016 | tf_op jit(solution)/shard_map/second_first/pallas_call | solution.py:372
  58.6 0.7 %second_last.1 = (bf16[512,256]{1,0:T(8,128)(2,1)S(1)}, bf16[256,256]{1,0:T(8,128)(2,1)S(1)}, bf16[256,256]{1,0:T(8,128)(2,1)S(1)}, f32[96,512]{1,0:T(8,128)S(1)...) custom-call(bf16[64,512]{1,0:T(8,128)(2,1)S(1)} %get-tuple-element.128.refs_0_, ...), custom_call_target="tpu_custom_call" | custom-call | flops 402653184 | bytes 3670016 | tf_op jit(solution)/shard_map/second_last/pallas_call | solution.py:372
  59.4 2.0 %collective-permute-start.38 = (bf16[96,512]{1,0:T(8,128)(2,1)S(1)}, bf16[96,512]{1,0:T(8,128)(2,1)S(1)}, u32[]{:S(2)}, u32[]{:S(2)}) collective-permute-start(bf16[96,512]{1,0:T(8,128)(2,1)S(1)} %get-tuple-element.144), channel_id=1, source_target_pairs={{0,6},{1,7},{2,4},{3,5},{4,2},{5,3},{6,0},{7,1},{8,14},{9,15},{10,... | collective-permute-start | bytes 294920 | tf_op jit(solution)/shard_map/ppermute | solution.py:390
  61.8 2.1 %collective-permute-start.40 = (bf16[96,512]{1,0:T(8,128)(2,1)S(1)}, bf16[96,512]{1,0:T(8,128)(2,1)S(1)}, u32[]{:S(2)}, u32[]{:S(2)}) collective-permute-start(bf16[96,512]{1,0:T(8,128)(2,1)S(1)} %get-tuple-element.146), channel_id=1, source_target_pairs={{0,2},{1,3},{2,0},{3,1},{4,6},{5,7},{6,4},{7,5},{8,10},{9,11},{10,... | collective-permute-start | bytes 294920 | tf_op jit(solution)/shard_map/ppermute | solution.py:390
  63.8 1.0 %query_grad.1 = bf16[256,512]{1,0:T(8,128)(2,1)} custom-call(bf16[256,256]{1,0:T(8,128)(2,1)S(1)} %get-tuple-element.102.gate_back, bf16[256,256]{1,0:T(8,128)(2,1)S(1)} %get-tuple-element.103.up_back, bf16[256,512]{1,0:T(8,128)(2,1)S(1)} %get-tuple-element.104.f1t, bf16[256,512]{1,0:T(8,128)(2,1)S(1)} %get-tuple-element.105.f3t), custom_call_target="tpu_custom_call" | custom-call | flops 134217728 | bytes 786432 | tf_op jit(solution)/shard_map/query_grad/pallas_call | solution.py:372
  64.9 1.4 %token_grads.1 = (bf16[256,512]{1,0:T(8,128)(2,1)}, bf16[256,512]{1,0:T(8,128)(2,1)}) custom-call(f32[1,256]{1,0:T(1,128)S(1)} %bitcast.33, bf16[256,256]{1,0:T(8,128)(2,1)S(1)} %get-tuple-element.106.refs_1_, bf16[256,256]{1,0:T(8,128)(2,1)S(1)} %get-tuple-element.127.refs_2_, bf16[256,256]{1,0:T(8,128)(2,1)S(1)} %get-tuple-element.132.refs_3_, ...), custom_call_target="tpu_custom_call" | custom-call | flops 402653184 | bytes 2360320 | tf_op jit(solution)/shard_map/token_grads/pallas_call | solution.py:372
  66.2 0.7 %collective-permute-done.38.refs_4_ = bf16[96,512]{1,0:T(8,128)(2,1)S(1)} collective-permute-done((bf16[96,512]{1,0:T(8,128)(2,1)S(1)}, bf16[96,512]{1,0:T(8,128)(2,1)S(1)}, u32[]{:S(2)}, u32[]{:S(2)}) %collective-permute-start.38) | collective-permute-done | bytes 98336 | tf_op jit(solution)/shard_map/ppermute | solution.py:390
  67.0 4.1 %collective-permute-done.39.refs_5_ = bf16[96,512]{1,0:T(8,128)(2,1)S(1)} collective-permute-done((bf16[96,512]{1,0:T(8,128)(2,1)S(1)}, bf16[96,512]{1,0:T(8,128)(2,1)S(1)}, u32[]{:S(2)}, u32[]{:S(2)}) %collective-permute-start.39) | collective-permute-done | bytes 98336 | tf_op jit(solution)/shard_map/ppermute | solution.py:390
  71.1 0.7 owner_result.1
  (74 shorter events, 6.2 us)
Async XLA Ops:
  0.6 1.0 %copy-start.5 = (f32[256,1]{0,1:T(1,128)S(1)}, f32[256,1]{0,1:T(1,128)}, u32[]{:S(2)}) copy-start(f32[256,1]{0,1:T(1,128)} %param.13) | copy-start | bytes 3076
  0.6 2.5 %collective-permute-start.2 = (bf16[256,512]{1,0:T(8,128)(2,1)}, bf16[256,512]{1,0:T(8,128)(2,1)S(1)}, u32[]{:S(2)}, u32[]{:S(2)}) collective-permute-start(bf16[256,512]{1,0:T(8,128)(2,1)} %vo.3), channel_id=1, source_target_pairs={{0,1},{1,0},{2,3},{3,2},{4,5},{5,4},{6,7},{7,6},{8,9},{9,8},{10,11... | collective-permute-start | bytes 786440 | tf_op jit(solution)/shard_map/ppermute | solution.py:511
  1.2 2.0 %collective-permute-start.1 = (bf16[256,512]{1,0:T(8,128)(2,1)}, bf16[256,512]{1,0:T(8,128)(2,1)S(1)}, u32[]{:S(2)}, u32[]{:S(2)}) collective-permute-start(bf16[256,512]{1,0:T(8,128)(2,1)} %refs_4_.1), channel_id=1, source_target_pairs={{0,1},{1,0},{2,3},{3,2},{4,5},{5,4},{6,7},{7,6},{8,9},{9,8},{10,11... | collective-permute-start | bytes 786440 | tf_op jit(solution)/shard_map/ppermute | solution.py:511
  1.2 15.9 %collective-permute-start = (bf16[256,512]{1,0:T(8,128)(2,1)}, bf16[256,512]{1,0:T(8,128)(2,1)S(1)}, u32[]{:S(2)}, u32[]{:S(2)}) collective-permute-start(bf16[256,512]{1,0:T(8,128)(2,1)} %go.1), channel_id=1, source_target_pairs={{0,1},{1,0},{2,3},{3,2},{4,5},{5,4},{6,7},{7,6},{8,9},{9,8},{10,11... | collective-permute-start | bytes 786440 | tf_op jit(solution)/shard_map/ppermute | solution.py:511
  1.7 1.2 %copy-start.7 = (bf16[1,512,256]{2,1,0:T(8,128)(2,1)S(1)}, bf16[1,512,256]{2,1,0:T(8,128)(2,1)}, u32[]{:S(2)}) copy-start(bf16[1,512,256]{2,1,0:T(8,128)(2,1)} %param.16) | copy-start | bytes 786436
  1.7 1.4 %collective-permute-start.3 = (f32[1,256]{1,0:T(1,128)S(1)}, f32[1,256]{1,0:T(1,128)S(1)}, u32[]{:S(2)}, u32[]{:S(2)}) collective-permute-start(f32[1,256]{1,0:T(1,128)S(1)} %bitcast.30), channel_id=1, source_target_pairs={{0,1},{1,0},{2,3},{3,2},{4,5},{5,4},{6,7},{7,6},{8,9},{9,8},{10,11... | collective-permute-start | bytes 3080 | tf_op jit(solution)/shard_map/ppermute | solution.py:511
  1.8 1.4 %copy-start.4 = (bf16[256,512]{1,0:T(8,128)(2,1)S(1)}, bf16[256,512]{1,0:T(8,128)(2,1)}, u32[]{:S(2)}) copy-start(bf16[256,512]{1,0:T(8,128)(2,1)} %vo.3) | copy-start | bytes 786436
  2.9 1.0 %copy-start.1 = (bf16[1,256,512]{2,1,0:T(8,128)(2,1)S(1)}, bf16[1,256,512]{2,1,0:T(8,128)(2,1)}, u32[]{:S(2)}) copy-start(bf16[1,256,512]{2,1,0:T(8,128)(2,1)} %param.17) | copy-start | bytes 786436
  4.0 4.2 %copy-start.2 = (bf16[256,512]{1,0:T(8,128)(2,1)S(1)}, bf16[256,512]{1,0:T(8,128)(2,1)}, u32[]{:S(2)}) copy-start(bf16[256,512]{1,0:T(8,128)(2,1)} %refs_11_.1) | copy-start | bytes 786436
  5.1 5.4 %collective-permute-start.8 = (bf16[64,512]{1,0:T(8,128)(2,1)S(1)}, bf16[64,512]{1,0:T(8,128)(2,1)S(1)}, u32[]{:S(2)}, u32[]{:S(2)}) collective-permute-start(bf16[64,512]{1,0:T(8,128)(2,1)S(1)} %get-tuple-element.88), channel_id=1, source_target_pairs={{0,2},{1,3},{2,0},{3,1},{4,6},{5,7},{6,4},{7,5},{8,10},{9,11},{10,... | collective-permute-start | bytes 196616 | tf_op jit(solution)/shard_map/ppermute | solution.py:395
  8.2 19.3 %collective-permute-start.19 = (bf16[256,512]{1,0:T(8,128)(2,1)S(1)}, bf16[256,512]{1,0:T(8,128)(2,1)S(1)}, u32[]{:S(2)}, u32[]{:S(2)}) collective-permute-start(bf16[256,512]{1,0:T(8,128)(2,1)S(1)} %copy-done.2), channel_id=1, source_target_pairs={{0,1},{1,0},{2,3},{3,2},{4,5},{5,4},{6,7},{7,6},{8,9},{9,8},{10,11... | collective-permute-start | bytes 786440 | tf_op jit(solution)/shard_map/ppermute | solution.py:511
  8.2 5.4 %collective-permute-start.4 = (bf16[64,512]{1,0:T(8,128)(2,1)S(1)}, bf16[64,512]{1,0:T(8,128)(2,1)S(1)}, u32[]{:S(2)}, u32[]{:S(2)}) collective-permute-start(bf16[64,512]{1,0:T(8,128)(2,1)S(1)} %get-tuple-element.80), channel_id=1, source_target_pairs={{0,2},{1,3},{2,0},{3,1},{4,6},{5,7},{6,4},{7,5},{8,10},{9,11},{10,... | collective-permute-start | bytes 196616 | tf_op jit(solution)/shard_map/ppermute | solution.py:395
  8.3 7.4 %collective-permute-start.6 = (bf16[64,512]{1,0:T(8,128)(2,1)S(1)}, bf16[64,512]{1,0:T(8,128)(2,1)S(1)}, u32[]{:S(2)}, u32[]{:S(2)}) collective-permute-start(bf16[64,512]{1,0:T(8,128)(2,1)S(1)} %get-tuple-element.84), channel_id=1, source_target_pairs={{0,2},{1,3},{2,0},{3,1},{4,6},{5,7},{6,4},{7,5},{8,10},{9,11},{10,... | collective-permute-start | bytes 196616 | tf_op jit(solution)/shard_map/ppermute | solution.py:395
  10.5 7.1 %collective-permute-start.9 = (bf16[64,512]{1,0:T(8,128)(2,1)S(1)}, bf16[64,512]{1,0:T(8,128)(2,1)S(1)}, u32[]{:S(2)}, u32[]{:S(2)}) collective-permute-start(bf16[64,512]{1,0:T(8,128)(2,1)S(1)} %carry.8.refs_0_), channel_id=1, source_target_pairs={{0,4},{1,5},{2,6},{3,7},{4,0},{5,1},{6,2},{7,3},{8,12},{9,13},{10,... | collective-permute-start | bytes 196616 | tf_op jit(solution)/shard_map/ppermute | solution.py:395
  13.5 3.6 %copy-start.3 = (bf16[256,512]{1,0:T(8,128)(2,1)S(1)}, bf16[256,512]{1,0:T(8,128)(2,1)}, u32[]{:S(2)}) copy-start(bf16[256,512]{1,0:T(8,128)(2,1)} %go.1) | copy-start | bytes 786436
  13.6 7.6 %collective-permute-start.5 = (bf16[64,512]{1,0:T(8,128)(2,1)S(1)}, bf16[64,512]{1,0:T(8,128)(2,1)S(1)}, u32[]{:S(2)}, u32[]{:S(2)}) collective-permute-start(bf16[64,512]{1,0:T(8,128)(2,1)S(1)} %carry.6.refs_0_), channel_id=1, source_target_pairs={{0,4},{1,5},{2,6},{3,7},{4,0},{5,1},{6,2},{7,3},{8,12},{9,13},{10,... | collective-permute-start | bytes 196616 | tf_op jit(solution)/shard_map/ppermute | solution.py:395
  15.7 1.4 %copy-start.6 = (f32[512]{0:T(512)S(1)}, f32[512]{0:T(512)}, u32[]{:S(2)}) copy-start(f32[512]{0:T(512)} %param.14) | copy-start | bytes 6148
  15.8 7.2 %collective-permute-start.7 = (bf16[64,512]{1,0:T(8,128)(2,1)S(1)}, bf16[64,512]{1,0:T(8,128)(2,1)S(1)}, u32[]{:S(2)}, u32[]{:S(2)}) collective-permute-start(bf16[64,512]{1,0:T(8,128)(2,1)S(1)} %carry.7.refs_0_), channel_id=1, source_target_pairs={{0,4},{1,5},{2,6},{3,7},{4,0},{5,1},{6,2},{7,3},{8,12},{9,13},{10,... | collective-permute-start | bytes 196616 | tf_op jit(solution)/shard_map/ppermute | solution.py:395
  17.8 6.3 %collective-permute-start.16 = (bf16[64,512]{1,0:T(8,128)(2,1)S(1)}, bf16[64,512]{1,0:T(8,128)(2,1)S(1)}, u32[]{:S(2)}, u32[]{:S(2)}) collective-permute-start(bf16[64,512]{1,0:T(8,128)(2,1)S(1)} %get-tuple-element.93.refs_8_), channel_id=1, source_target_pairs={{0,2},{1,3},{2,0},{3,1},{4,6},{5,7},{6,4},{7,5},{8,10},{9,11},{10,... | collective-permute-start | bytes 196616 | tf_op jit(solution)/shard_map/ppermute | solution.py:395
  21.2 4.4 %collective-permute-start.10 = (bf16[64,512]{1,0:T(8,128)(2,1)S(1)}, bf16[64,512]{1,0:T(8,128)(2,1)S(1)}, u32[]{:S(2)}, u32[]{:S(2)}) collective-permute-start(bf16[64,512]{1,0:T(8,128)(2,1)S(1)} %get-tuple-element.91.refs_0_), channel_id=1, source_target_pairs={{0,2},{1,3},{2,0},{3,1},{4,6},{5,7},{6,4},{7,5},{8,10},{9,11},{10,... | collective-permute-start | bytes 196616 | tf_op jit(solution)/shard_map/ppermute | solution.py:395
  23.1 4.3 %collective-permute-start.13 = (bf16[64,512]{1,0:T(8,128)(2,1)S(1)}, bf16[64,512]{1,0:T(8,128)(2,1)S(1)}, u32[]{:S(2)}, u32[]{:S(2)}) collective-permute-start(bf16[64,512]{1,0:T(8,128)(2,1)S(1)} %get-tuple-element.92.refs_4_), channel_id=1, source_target_pairs={{0,2},{1,3},{2,0},{3,1},{4,6},{5,7},{6,4},{7,5},{8,10},{9,11},{10,... | collective-permute-start | bytes 196616 | tf_op jit(solution)/shard_map/ppermute | solution.py:395
  24.1 3.9 %collective-permute-start.18 = (bf16[64,512]{1,0:T(8,128)(2,1)S(1)}, bf16[64,512]{1,0:T(8,128)(2,1)S(1)}, u32[]{:S(2)}, u32[]{:S(2)}) collective-permute-start(bf16[64,512]{1,0:T(8,128)(2,1)S(1)} %collective-permute-done.16.refs_9_), channel_id=1, source_target_pairs={{0,1},{1,0},{2,3},{3,2},{4,5},{5,4},{6,7},{7,6},{8,9},{9,8},{10,11... | collective-permute-start | bytes 196616 | tf_op jit(solution)/shard_map/ppermute | solution.py:406
  25.6 3.1 %collective-permute-start.11 = (bf16[64,512]{1,0:T(8,128)(2,1)S(1)}, bf16[64,512]{1,0:T(8,128)(2,1)S(1)}, u32[]{:S(2)}, u32[]{:S(2)}) collective-permute-start(bf16[64,512]{1,0:T(8,128)(2,1)S(1)} %get-tuple-element.91.refs_0_), channel_id=1, source_target_pairs={{0,1},{1,0},{2,3},{3,2},{4,5},{5,4},{6,7},{7,6},{8,9},{9,8},{10,11... | collective-permute-start | bytes 196616 | tf_op jit(solution)/shard_map/ppermute | solution.py:406
  25.6 3.1 %collective-permute-start.14 = (bf16[64,512]{1,0:T(8,128)(2,1)S(1)}, bf16[64,512]{1,0:T(8,128)(2,1)S(1)}, u32[]{:S(2)}, u32[]{:S(2)}) collective-permute-start(bf16[64,512]{1,0:T(8,128)(2,1)S(1)} %get-tuple-element.92.refs_4_), channel_id=1, source_target_pairs={{0,1},{1,0},{2,3},{3,2},{4,5},{5,4},{6,7},{7,6},{8,9},{9,8},{10,11... | collective-permute-start | bytes 196616 | tf_op jit(solution)/shard_map/ppermute | solution.py:406
  27.5 1.3 %collective-permute-start.15 = (bf16[64,512]{1,0:T(8,128)(2,1)S(1)}, bf16[64,512]{1,0:T(8,128)(2,1)S(1)}, u32[]{:S(2)}, u32[]{:S(2)}) collective-permute-start(bf16[64,512]{1,0:T(8,128)(2,1)S(1)} %collective-permute-done.13.refs_5_), channel_id=1, source_target_pairs={{0,1},{1,0},{2,3},{3,2},{4,5},{5,4},{6,7},{7,6},{8,9},{9,8},{10,11... | collective-permute-start | bytes 196616 | tf_op jit(solution)/shard_map/ppermute | solution.py:406
  27.5 1.4 %collective-permute-start.17 = (bf16[64,512]{1,0:T(8,128)(2,1)S(1)}, bf16[64,512]{1,0:T(8,128)(2,1)S(1)}, u32[]{:S(2)}, u32[]{:S(2)}) collective-permute-start(bf16[64,512]{1,0:T(8,128)(2,1)S(1)} %get-tuple-element.93.refs_8_), channel_id=1, source_target_pairs={{0,1},{1,0},{2,3},{3,2},{4,5},{5,4},{6,7},{7,6},{8,9},{9,8},{10,11... | collective-permute-start | bytes 196616 | tf_op jit(solution)/shard_map/ppermute | solution.py:406
  28.0 1.3 %collective-permute-start.12 = (bf16[64,512]{1,0:T(8,128)(2,1)S(1)}, bf16[64,512]{1,0:T(8,128)(2,1)S(1)}, u32[]{:S(2)}, u32[]{:S(2)}) collective-permute-start(bf16[64,512]{1,0:T(8,128)(2,1)S(1)} %collective-permute-done.10.refs_1_), channel_id=1, source_target_pairs={{0,1},{1,0},{2,3},{3,2},{4,5},{5,4},{6,7},{7,6},{8,9},{9,8},{10,11... | collective-permute-start | bytes 196616 | tf_op jit(solution)/shard_map/ppermute | solution.py:406
  30.0 4.6 %collective-permute-start.22 = (f32[2,512]{1,0:T(2,128)S(1)}, f32[2,512]{1,0:T(2,128)S(1)}, u32[]{:S(2)}, u32[]{:S(2)}) collective-permute-start(f32[2,512]{1,0:T(2,128)S(1)} %get-tuple-element.95.refs_0_), channel_id=1, source_target_pairs={{0,24},{8,16},{16,8},{24,0},{1,25},{9,17},{17,9},{25,1},{2,26},{10... | collective-permute-start | bytes 12296 | tf_op jit(solution)/shard_map/ppermute | solution.py:413
  32.9 3.6 %collective-permute-start.21 = (f32[2,512]{1,0:T(2,128)S(1)}, f32[2,512]{1,0:T(2,128)S(1)}, u32[]{:S(2)}, u32[]{:S(2)}) collective-permute-start(f32[2,512]{1,0:T(2,128)S(1)} %get-tuple-element.95.refs_0_), channel_id=1, source_target_pairs={{0,16},{8,24},{16,0},{24,8},{1,17},{9,25},{17,1},{25,9},{2,18},{10... | collective-permute-start | bytes 12296 | tf_op jit(solution)/shard_map/ppermute | solution.py:413
  33.4 3.6 %collective-permute-start.20 = (f32[2,512]{1,0:T(2,128)S(1)}, f32[2,512]{1,0:T(2,128)S(1)}, u32[]{:S(2)}, u32[]{:S(2)}) collective-permute-start(f32[2,512]{1,0:T(2,128)S(1)} %get-tuple-element.95.refs_0_), channel_id=1, source_target_pairs={{0,8},{8,0},{16,24},{24,16},{1,9},{9,1},{17,25},{25,17},{2,10},{10... | collective-permute-start | bytes 12296 | tf_op jit(solution)/shard_map/ppermute | solution.py:413
  37.8 4.3 %collective-permute-start.25 = (bf16[64,512]{1,0:T(8,128)(2,1)S(1)}, bf16[64,512]{1,0:T(8,128)(2,1)S(1)}, u32[]{:S(2)}, u32[]{:S(2)}) collective-permute-start(bf16[64,512]{1,0:T(8,128)(2,1)S(1)} %get-tuple-element.113), channel_id=1, source_target_pairs={{0,2},{1,3},{2,0},{3,1},{4,6},{5,7},{6,4},{7,5},{8,10},{9,11},{10,... | collective-permute-start | bytes 196616 | tf_op jit(solution)/shard_map/ppermute | solution.py:395
  38.7 6.7 %collective-permute-start.23 = (bf16[64,512]{1,0:T(8,128)(2,1)S(1)}, bf16[64,512]{1,0:T(8,128)(2,1)S(1)}, u32[]{:S(2)}, u32[]{:S(2)}) collective-permute-start(bf16[64,512]{1,0:T(8,128)(2,1)S(1)} %get-tuple-element.109), channel_id=1, source_target_pairs={{0,2},{1,3},{2,0},{3,1},{4,6},{5,7},{6,4},{7,5},{8,10},{9,11},{10,... | collective-permute-start | bytes 196616 | tf_op jit(solution)/shard_map/ppermute | solution.py:395
  39.9 6.2 %collective-permute-start.27 = (bf16[64,512]{1,0:T(8,128)(2,1)S(1)}, bf16[64,512]{1,0:T(8,128)(2,1)S(1)}, u32[]{:S(2)}, u32[]{:S(2)}) collective-permute-start(bf16[64,512]{1,0:T(8,128)(2,1)S(1)} %get-tuple-element.117), channel_id=1, source_target_pairs={{0,2},{1,3},{2,0},{3,1},{4,6},{5,7},{6,4},{7,5},{8,10},{9,11},{10,... | collective-permute-start | bytes 196616 | tf_op jit(solution)/shard_map/ppermute | solution.py:395
  42.2 7.5 %collective-permute-start.26 = (bf16[64,512]{1,0:T(8,128)(2,1)S(1)}, bf16[64,512]{1,0:T(8,128)(2,1)S(1)}, u32[]{:S(2)}, u32[]{:S(2)}) collective-permute-start(bf16[64,512]{1,0:T(8,128)(2,1)S(1)} %carry.10.refs_0_), channel_id=1, source_target_pairs={{0,4},{1,5},{2,6},{3,7},{4,0},{5,1},{6,2},{7,3},{8,12},{9,13},{10,... | collective-permute-start | bytes 196616 | tf_op jit(solution)/shard_map/ppermute | solution.py:395
  45.5 5.8 %collective-permute-start.24 = (bf16[64,512]{1,0:T(8,128)(2,1)S(1)}, bf16[64,512]{1,0:T(8,128)(2,1)S(1)}, u32[]{:S(2)}, u32[]{:S(2)}) collective-permute-start(bf16[64,512]{1,0:T(8,128)(2,1)S(1)} %carry.9.refs_0_), channel_id=1, source_target_pairs={{0,4},{1,5},{2,6},{3,7},{4,0},{5,1},{6,2},{7,3},{8,12},{9,13},{10,... | collective-permute-start | bytes 196616 | tf_op jit(solution)/shard_map/ppermute | solution.py:395
  46.2 6.5 %collective-permute-start.28 = (bf16[64,512]{1,0:T(8,128)(2,1)S(1)}, bf16[64,512]{1,0:T(8,128)(2,1)S(1)}, u32[]{:S(2)}, u32[]{:S(2)}) collective-permute-start(bf16[64,512]{1,0:T(8,128)(2,1)S(1)} %carry.11.refs_0_), channel_id=1, source_target_pairs={{0,4},{1,5},{2,6},{3,7},{4,0},{5,1},{6,2},{7,3},{8,12},{9,13},{10,... | collective-permute-start | bytes 196616 | tf_op jit(solution)/shard_map/ppermute | solution.py:395
  49.9 4.3 %collective-permute-start.32 = (bf16[64,512]{1,0:T(8,128)(2,1)S(1)}, bf16[64,512]{1,0:T(8,128)(2,1)S(1)}, u32[]{:S(2)}, u32[]{:S(2)}) collective-permute-start(bf16[64,512]{1,0:T(8,128)(2,1)S(1)} %get-tuple-element.121.refs_4_), channel_id=1, source_target_pairs={{0,2},{1,3},{2,0},{3,1},{4,6},{5,7},{6,4},{7,5},{8,10},{9,11},{10,... | collective-permute-start | bytes 196616 | tf_op jit(solution)/shard_map/ppermute | solution.py:395
  51.5 4.3 %collective-permute-start.29 = (bf16[64,512]{1,0:T(8,128)(2,1)S(1)}, bf16[64,512]{1,0:T(8,128)(2,1)S(1)}, u32[]{:S(2)}, u32[]{:S(2)}) collective-permute-start(bf16[64,512]{1,0:T(8,128)(2,1)S(1)} %get-tuple-element.120.refs_0_), channel_id=1, source_target_pairs={{0,2},{1,3},{2,0},{3,1},{4,6},{5,7},{6,4},{7,5},{8,10},{9,11},{10,... | collective-permute-start | bytes 196616 | tf_op jit(solution)/shard_map/ppermute | solution.py:395
  52.9 4.3 %collective-permute-start.35 = (bf16[64,512]{1,0:T(8,128)(2,1)S(1)}, bf16[64,512]{1,0:T(8,128)(2,1)S(1)}, u32[]{:S(2)}, u32[]{:S(2)}) collective-permute-start(bf16[64,512]{1,0:T(8,128)(2,1)S(1)} %get-tuple-element.128.refs_0_), channel_id=1, source_target_pairs={{0,2},{1,3},{2,0},{3,1},{4,6},{5,7},{6,4},{7,5},{8,10},{9,11},{10,... | collective-permute-start | bytes 196616 | tf_op jit(solution)/shard_map/ppermute | solution.py:395
  54.2 3.1 %collective-permute-start.34 = (bf16[64,512]{1,0:T(8,128)(2,1)S(1)}, bf16[64,512]{1,0:T(8,128)(2,1)S(1)}, u32[]{:S(2)}, u32[]{:S(2)}) collective-permute-start(bf16[64,512]{1,0:T(8,128)(2,1)S(1)} %collective-permute-done.32.refs_5_), channel_id=1, source_target_pairs={{0,1},{1,0},{2,3},{3,2},{4,5},{5,4},{6,7},{7,6},{8,9},{9,8},{10,11... | collective-permute-start | bytes 196616 | tf_op jit(solution)/shard_map/ppermute | solution.py:406
  55.8 2.0 %collective-permute-start.30 = (bf16[64,512]{1,0:T(8,128)(2,1)S(1)}, bf16[64,512]{1,0:T(8,128)(2,1)S(1)}, u32[]{:S(2)}, u32[]{:S(2)}) collective-permute-start(bf16[64,512]{1,0:T(8,128)(2,1)S(1)} %get-tuple-element.120.refs_0_), channel_id=1, source_target_pairs={{0,1},{1,0},{2,3},{3,2},{4,5},{5,4},{6,7},{7,6},{8,9},{9,8},{10,11... | collective-permute-start | bytes 196616 | tf_op jit(solution)/shard_map/ppermute | solution.py:406
  55.8 2.0 %collective-permute-start.33 = (bf16[64,512]{1,0:T(8,128)(2,1)S(1)}, bf16[64,512]{1,0:T(8,128)(2,1)S(1)}, u32[]{:S(2)}, u32[]{:S(2)}) collective-permute-start(bf16[64,512]{1,0:T(8,128)(2,1)S(1)} %get-tuple-element.121.refs_4_), channel_id=1, source_target_pairs={{0,1},{1,0},{2,3},{3,2},{4,5},{5,4},{6,7},{7,6},{8,9},{9,8},{10,11... | collective-permute-start | bytes 196616 | tf_op jit(solution)/shard_map/ppermute | solution.py:406
  56.3 1.5 %collective-permute-start.31 = (bf16[64,512]{1,0:T(8,128)(2,1)S(1)}, bf16[64,512]{1,0:T(8,128)(2,1)S(1)}, u32[]{:S(2)}, u32[]{:S(2)}) collective-permute-start(bf16[64,512]{1,0:T(8,128)(2,1)S(1)} %collective-permute-done.29.refs_1_), channel_id=1, source_target_pairs={{0,1},{1,0},{2,3},{3,2},{4,5},{5,4},{6,7},{7,6},{8,9},{9,8},{10,11... | collective-permute-start | bytes 196616 | tf_op jit(solution)/shard_map/ppermute | solution.py:406
  57.2 1.4 %collective-permute-start.36 = (bf16[64,512]{1,0:T(8,128)(2,1)S(1)}, bf16[64,512]{1,0:T(8,128)(2,1)S(1)}, u32[]{:S(2)}, u32[]{:S(2)}) collective-permute-start(bf16[64,512]{1,0:T(8,128)(2,1)S(1)} %get-tuple-element.128.refs_0_), channel_id=1, source_target_pairs={{0,1},{1,0},{2,3},{3,2},{4,5},{5,4},{6,7},{7,6},{8,9},{9,8},{10,11... | collective-permute-start | bytes 196616 | tf_op jit(solution)/shard_map/ppermute | solution.py:406
  57.2 1.4 %collective-permute-start.37 = (bf16[64,512]{1,0:T(8,128)(2,1)S(1)}, bf16[64,512]{1,0:T(8,128)(2,1)S(1)}, u32[]{:S(2)}, u32[]{:S(2)}) collective-permute-start(bf16[64,512]{1,0:T(8,128)(2,1)S(1)} %collective-permute-done.35.refs_1_), channel_id=1, source_target_pairs={{0,1},{1,0},{2,3},{3,2},{4,5},{5,4},{6,7},{7,6},{8,9},{9,8},{10,11... | collective-permute-start | bytes 196616 | tf_op jit(solution)/shard_map/ppermute | solution.py:406
  59.4 7.6 %collective-permute-start.38 = (bf16[96,512]{1,0:T(8,128)(2,1)S(1)}, bf16[96,512]{1,0:T(8,128)(2,1)S(1)}, u32[]{:S(2)}, u32[]{:S(2)}) collective-permute-start(bf16[96,512]{1,0:T(8,128)(2,1)S(1)} %get-tuple-element.144), channel_id=1, source_target_pairs={{0,6},{1,7},{2,4},{3,5},{4,2},{5,3},{6,0},{7,1},{8,14},{9,15},{10,... | collective-permute-start | bytes 294920 | tf_op jit(solution)/shard_map/ppermute | solution.py:390
  61.4 9.7 %collective-permute-start.39 = (bf16[96,512]{1,0:T(8,128)(2,1)S(1)}, bf16[96,512]{1,0:T(8,128)(2,1)S(1)}, u32[]{:S(2)}, u32[]{:S(2)}) collective-permute-start(bf16[96,512]{1,0:T(8,128)(2,1)S(1)} %get-tuple-element.145), channel_id=1, source_target_pairs={{0,4},{1,5},{2,6},{3,7},{4,0},{5,1},{6,2},{7,3},{8,12},{9,13},{10,... | collective-permute-start | bytes 294920 | tf_op jit(solution)/shard_map/ppermute | solution.py:390
  61.8 9.3 %collective-permute-start.40 = (bf16[96,512]{1,0:T(8,128)(2,1)S(1)}, bf16[96,512]{1,0:T(8,128)(2,1)S(1)}, u32[]{:S(2)}, u32[]{:S(2)}) collective-permute-start(bf16[96,512]{1,0:T(8,128)(2,1)S(1)} %get-tuple-element.146), channel_id=1, source_target_pairs={{0,2},{1,3},{2,0},{3,1},{4,6},{5,7},{6,4},{7,5},{8,10},{9,11},{10,... | collective-permute-start | bytes 294920 | tf_op jit(solution)/shard_map/ppermute | solution.py:390
  (1 other events, 1.0 us)

commit v19 on v17

--- a/solution.py
+++ b/solution.py
@@ -400,9 +400,9 @@
     return [mine, *(to_chip(mine, step, chips) for step in range(2, chips, 2))]
 
 
-def from_owners(halves, chips):
+def from_owners(halves, chips, first):
     others = [to_chip(half, 1, chips) for half in halves]
-    *later, others[0] = lax.optimization_barrier((*halves, others[0]))
+    *later, others[first] = lax.optimization_barrier((*halves, others[first]))
     cross = lambda x: lax.ppermute(x, "tok", core_perm(chips * CORES))
     parts = zip(halves, others, map(cross, later), map(cross, others))
     return [x for part in parts for x in part]
@@ -554,7 +554,7 @@
     f1t, f3t, f2t, output, q_mixed, q_slope, q_silu, part = call(
         functools.partial(apply_kernel, chips, folds),
         matrices + [((dh, n), F32), ((fh, n), BF16), hidden, hidden, ((2, n), F32)],
-        (*from_owners(fast, chips), query_input, query_other, weighted),
+        (*from_owners(fast, chips, 2), query_input, query_other, weighted),
         name="apply",
         flops=3 * product,
     )
@@ -588,7 +588,7 @@
         )
         owned.append(rows_owned)
         cotangent.append(rows)
-    arrived = from_owners(cotangent, chips)
+    arrived = from_owners(cotangent, chips, 0)
     c1t, c3t, dbb, down_sums, up_part, gate_part = call(
         functools.partial(second_first_kernel, chips, folds),
         matrices[:2] + [own_hidden, ((g * chips, dh), F32), hidden, hidden],

time: 71.3 us -> 72.3 us (1.014)
  starting transfers between devices: 33.4 us -> 35.6 us
  waiting for transfers between devices: 24.6 us -> 23.2 us
    ppermute x18, starting transfers between devices: 22.2 us -> 24.4 us  [to_chip(): return lax.ppermute(x, 'tok', chip_perm(chips * CORES, step))]
    ppermute x18, waiting for transfers between devices: 16.7 us -> 15 us  [to_chip(): return lax.ppermute(x, 'tok', chip_perm(chips * CORES, step))]
where the time goes in v19:
time: 72.3 us; the launch traced here: 72.1 us
  starting transfers between devices  35.6 us (49%)
  waiting for transfers between devices  23.2 us (32%)
  Pallas kernels  9.73 us (13%)
  local copies, waits for them, and re-layouts  2.6 us (4%)
  between operations  0.89 us (1%)
    ppermute x18, starting transfers between devices, to_chip(): return lax.ppermute(x, 'tok', chip_perm(chips * CORES, step))  24.4 us
    ppermute x18, waiting for transfers between devices, to_chip(): return lax.ppermute(x, 'tok', chip_perm(chips * CORES, step))  15 us
    pallas_call x22, Pallas kernels, call(): pl.pallas_call(kernel, out_shape=[jax.ShapeDtypeStruct(s, t) for s, t in...  9.73 us
    ppermute x3, waiting for transfers between devices, exchange(): lax.ppermute(pieces[s], 'tok', chip_perm(count, s))  4.76 us
    ppermute x3, starting transfers between devices, exchange(): lax.ppermute(pieces[s], 'tok', chip_perm(count, s))  4.45 us
    ppermute x3, starting transfers between devices, head_parts(): lax.ppermute(part, 'head', [(h, partner(h, step, heads)) for h in range(h...  3.55 us
    unnamed x18, local copies, waits for them, and re-layouts  2.6 us
    ppermute x3, waiting for transfers between devices, head_parts(): lax.ppermute(part, 'head', [(h, partner(h, step, heads)) for h in range(h...  2.19 us
  transfers between devices with their start and end apart: 41, of which 23 were waited for; matrix products, arithmetic and copies ran while one was open for 2% of the time, Pallas kernels for 9%

profile of v19, /device:TPU:0, one launch (start us, length us, event | category | flops | bytes accessed | tf_op | source)
XLA Modules:
  0.0 72.1 jit_solution(8387603331942795342)
XLA Ops:
  0.6 0.5 collective-permute-start.2
  1.8 1.1 %copy.15 = bf16[1,512,256]{1,2,0:T(8,128)(2,1)S(1)} copy(bf16[1,512,256]{2,1,0:T(8,128)(2,1)} %param.15) | data formatting | bytes 524288 | tf_op args[6]
  3.1 0.7 %copy-done = bf16[256,512]{1,0:T(8,128)(2,1)S(1)} copy-done((bf16[256,512]{1,0:T(8,128)(2,1)S(1)}, bf16[256,512]{1,0:T(8,128)(2,1)}, u32[]{:S(2)}) %copy-start) | copy-done | bytes 262168
  4.0 1.1 %update.1 = (f32[64,512]{1,0:T(8,128)S(1)}, f32[64,512]{1,0:T(8,128)S(1)}, f32[64,512]{1,0:T(8,128)S(1)}, bf16[64,512]{1,0:T(8,128)(2,1)S(1)}, bf16[64,512]{1,0:T(8,128)(2,1)S(1)}, /*index=5*/bf16[64,512]{1,0:T(8,128)(2,1)S(1)}) custom-call(bf16[256,512]{1,0:T(8,128)(2,1)S(1)} %copy-done, bf16[256,512]{1,0:T(8,128)(2,1)S(1)} %collective-permute-done.1.kx.refs_9_.refs_5_, ...), custom_call_target="tpu_custom_call" | custom-call | flops 805306368 | bytes 1837056 | tf_op jit(solution)/shard_map/update/pallas_call | solution.py:372
  5.1 3.1 %collective-permute-start.9 = (bf16[64,512]{1,0:T(8,128)(2,1)S(1)}, bf16[64,512]{1,0:T(8,128)(2,1)S(1)}, u32[]{:S(2)}, u32[]{:S(2)}) collective-permute-start(bf16[64,512]{1,0:T(8,128)(2,1)S(1)} %get-tuple-element.90), channel_id=1, source_target_pairs={{0,2},{1,3},{2,0},{3,1},{4,6},{5,7},{6,4},{7,5},{8,10},{9,11},{10,... | collective-permute-start | bytes 196616 | tf_op jit(solution)/shard_map/ppermute | solution.py:395
  8.2 1.9 %collective-permute-start.4 = (bf16[64,512]{1,0:T(8,128)(2,1)S(1)}, bf16[64,512]{1,0:T(8,128)(2,1)S(1)}, u32[]{:S(2)}, u32[]{:S(2)}) collective-permute-start(bf16[64,512]{1,0:T(8,128)(2,1)S(1)} %get-tuple-element.82), channel_id=1, source_target_pairs={{0,2},{1,3},{2,0},{3,1},{4,6},{5,7},{6,4},{7,5},{8,10},{9,11},{10,... | collective-permute-start | bytes 196616 | tf_op jit(solution)/shard_map/ppermute | solution.py:395
  10.7 3.2 %collective-permute-start.10 = (bf16[64,512]{1,0:T(8,128)(2,1)S(1)}, bf16[64,512]{1,0:T(8,128)(2,1)S(1)}, u32[]{:S(2)}, u32[]{:S(2)}) collective-permute-start(bf16[64,512]{1,0:T(8,128)(2,1)S(1)} %carry.8.refs_0_), channel_id=1, source_target_pairs={{0,4},{1,5},{2,6},{3,7},{4,0},{5,1},{6,2},{7,3},{8,12},{9,13},{10,... | collective-permute-start | bytes 196616 | tf_op jit(solution)/shard_map/ppermute | solution.py:395
  14.9 1.0 %collective-permute-start.8 = (bf16[64,512]{1,0:T(8,128)(2,1)S(1)}, bf16[64,512]{1,0:T(8,128)(2,1)S(1)}, u32[]{:S(2)}, u32[]{:S(2)}) collective-permute-start(bf16[64,512]{1,0:T(8,128)(2,1)S(1)} %carry.7.refs_0_), channel_id=1, source_target_pairs={{0,4},{1,5},{2,6},{3,7},{4,0},{5,1},{6,2},{7,3},{8,12},{9,13},{10,... | collective-permute-start | bytes 196616 | tf_op jit(solution)/shard_map/ppermute | solution.py:395
  15.9 2.1 %collective-permute-start.5 = (bf16[64,512]{1,0:T(8,128)(2,1)S(1)}, bf16[64,512]{1,0:T(8,128)(2,1)S(1)}, u32[]{:S(2)}, u32[]{:S(2)}) collective-permute-start(bf16[64,512]{1,0:T(8,128)(2,1)S(1)} %carry.6.refs_0_), channel_id=1, source_target_pairs={{0,4},{1,5},{2,6},{3,7},{4,0},{5,1},{6,2},{7,3},{8,12},{9,13},{10,... | collective-permute-start | bytes 196616 | tf_op jit(solution)/shard_map/ppermute | solution.py:395
  18.1 2.0 %collective-permute-start.11 = (bf16[64,512]{1,0:T(8,128)(2,1)S(1)}, bf16[64,512]{1,0:T(8,128)(2,1)S(1)}, u32[]{:S(2)}, u32[]{:S(2)}) collective-permute-start(bf16[64,512]{1,0:T(8,128)(2,1)S(1)} %get-tuple-element.95.refs_8_), channel_id=1, source_target_pairs={{0,2},{1,3},{2,0},{3,1},{4,6},{5,7},{6,4},{7,5},{8,10},{9,11},{10,... | collective-permute-start | bytes 196616 | tf_op jit(solution)/shard_map/ppermute | solution.py:395
  20.1 3.6 %collective-permute-done.8.refs_1_ = bf16[64,512]{1,0:T(8,128)(2,1)S(1)} collective-permute-done((bf16[64,512]{1,0:T(8,128)(2,1)S(1)}, bf16[64,512]{1,0:T(8,128)(2,1)S(1)}, u32[]{:S(2)}, u32[]{:S(2)}) %collective-permute-start.8) | collective-permute-done | bytes 65568 | tf_op jit(solution)/shard_map/ppermute | solution.py:395
  23.9 0.8 %collective-permute-done.5.refs_1_ = bf16[64,512]{1,0:T(8,128)(2,1)S(1)} collective-permute-done((bf16[64,512]{1,0:T(8,128)(2,1)S(1)}, bf16[64,512]{1,0:T(8,128)(2,1)S(1)}, u32[]{:S(2)}, u32[]{:S(2)}) %collective-permute-start.5) | collective-permute-done | bytes 65568 | tf_op jit(solution)/shard_map/ppermute | solution.py:395
  24.8 1.3 %collective-permute-start.6 = (bf16[64,512]{1,0:T(8,128)(2,1)S(1)}, bf16[64,512]{1,0:T(8,128)(2,1)S(1)}, u32[]{:S(2)}, u32[]{:S(2)}) collective-permute-start(bf16[64,512]{1,0:T(8,128)(2,1)S(1)} %get-tuple-element.92.refs_0_), channel_id=1, source_target_pairs={{0,2},{1,3},{2,0},{3,1},{4,6},{5,7},{6,4},{7,5},{8,10},{9,11},{10,... | collective-permute-start | bytes 196616 | tf_op jit(solution)/shard_map/ppermute | solution.py:395
  26.6 1.9 %collective-permute-done.14.refs_5_ = bf16[64,512]{1,0:T(8,128)(2,1)S(1)} collective-permute-done((bf16[64,512]{1,0:T(8,128)(2,1)S(1)}, bf16[64,512]{1,0:T(8,128)(2,1)S(1)}, u32[]{:S(2)}, u32[]{:S(2)}) %collective-permute-start.14) | collective-permute-done | bytes 65568 | tf_op jit(solution)/shard_map/ppermute | solution.py:395
  28.5 0.7 collective-permute-done.6.refs_1_
  29.8 0.7 collective-permute-done.18.refs_11_
  31.0 0.8 %apply.1 = (bf16[256,512]{1,0:T(8,128)(2,1)S(1)}, bf16[256,512]{1,0:T(8,128)(2,1)S(1)}, bf16[512,256]{1,0:T(8,128)(2,1)S(1)}, f32[512,512]{1,0:T(8,128)S(1)}, bf...) custom-call(bf16[64,512]{1,0:T(8,128)(2,1)S(1)} %get-tuple-element.92.refs_0, ...), custom_call_target="tpu_custom_call" | custom-call | flops 402653184 | bytes 2359296 | tf_op jit(solution)/shard_map/apply/pallas_call | solution.py:372
  31.8 2.5 %collective-permute-start.22 = (f32[2,512]{1,0:T(2,128)S(1)}, f32[2,512]{1,0:T(2,128)S(1)}, u32[]{:S(2)}, u32[]{:S(2)}) collective-permute-start(f32[2,512]{1,0:T(2,128)S(1)} %get-tuple-element.99.refs_0_), channel_id=1, source_target_pairs={{0,24},{8,16},{16,8},{24,0},{1,25},{9,17},{17,9},{25,1},{2,26},{10... | collective-permute-start | bytes 12296 | tf_op jit(solution)/shard_map/ppermute | solution.py:413
  34.3 0.5 collective-permute-start.21
  35.3 0.9 %saved.1 = (bf16[512,512]{1,0:T(8,128)(2,1)S(1)}, f32[256,512]{1,0:T(8,128)S(1)}, f32[256,512]{1,0:T(8,128)S(1)}, f32[256,512]{1,0:T(8,128)S(1)}, f32[256,512]{1...) custom-call(bf16[256,512]{1,0:T(8,128)(2,1)S(1)} %copy-done, ...), custom_call_target="tpu_custom_call" | custom-call | flops 402653184 | bytes 1837056 | tf_op jit(solution)/shard_map/saved/pallas_call | solution.py:372
  36.3 1.6 %collective-permute-done.21.refs_2_ = f32[2,512]{1,0:T(2,128)S(1)} collective-permute-done((f32[2,512]{1,0:T(2,128)S(1)}, f32[2,512]{1,0:T(2,128)S(1)}, u32[]{:S(2)}, u32[]{:S(2)}) %collective-permute-start.21) | collective-permute-done | bytes 4128 | tf_op jit(solution)/shard_map/ppermute | solution.py:413
  37.9 0.5 collective-permute-done.20.refs_1_
  38.4 0.8 %apply_back.1 = (bf16[256,256]{1,0:T(8,128)(2,1)S(1)}, bf16[256,256]{1,0:T(8,128)(2,1)S(1)}, f32[64,512]{1,0:T(8,128)S(1)}, f32[64,512]{1,0:T(8,128)S(1)}, f32[6...) custom-call(f32[2,512]{1,0:T(2,128)S(1)} %get-tuple-element.99.refs_0, ...), custom_call_target="tpu_custom_call" | custom-call | flops 536870912 | bytes 4341760 | tf_op jit(solution)/shard_map/apply_back/pallas_call | solution.py:372
  39.3 1.2 %collective-permute-start.25 = (bf16[64,512]{1,0:T(8,128)(2,1)S(1)}, bf16[64,512]{1,0:T(8,128)(2,1)S(1)}, u32[]{:S(2)}, u32[]{:S(2)}) collective-permute-start(bf16[64,512]{1,0:T(8,128)(2,1)S(1)} %get-tuple-element.117), channel_id=1, source_target_pairs={{0,2},{1,3},{2,0},{3,1},{4,6},{5,7},{6,4},{7,5},{8,10},{9,11},{10,... | collective-permute-start | bytes 196616 | tf_op jit(solution)/shard_map/ppermute | solution.py:395
  40.5 0.9 %collective-permute-start.23 = (bf16[64,512]{1,0:T(8,128)(2,1)S(1)}, bf16[64,512]{1,0:T(8,128)(2,1)S(1)}, u32[]{:S(2)}, u32[]{:S(2)}) collective-permute-start(bf16[64,512]{1,0:T(8,128)(2,1)S(1)} %get-tuple-element.113), channel_id=1, source_target_pairs={{0,2},{1,3},{2,0},{3,1},{4,6},{5,7},{6,4},{7,5},{8,10},{9,11},{10,... | collective-permute-start | bytes 196616 | tf_op jit(solution)/shard_map/ppermute | solution.py:395
  41.3 1.1 %collective-permute-start.27 = (bf16[64,512]{1,0:T(8,128)(2,1)S(1)}, bf16[64,512]{1,0:T(8,128)(2,1)S(1)}, u32[]{:S(2)}, u32[]{:S(2)}) collective-permute-start(bf16[64,512]{1,0:T(8,128)(2,1)S(1)} %get-tuple-element.121), channel_id=1, source_target_pairs={{0,2},{1,3},{2,0},{3,1},{4,6},{5,7},{6,4},{7,5},{8,10},{9,11},{10,... | collective-permute-start | bytes 196616 | tf_op jit(solution)/shard_map/ppermute | solution.py:395
  42.5 1.1 %collective-permute-done.25.got = bf16[64,512]{1,0:T(8,128)(2,1)S(1)} collective-permute-done((bf16[64,512]{1,0:T(8,128)(2,1)S(1)}, bf16[64,512]{1,0:T(8,128)(2,1)S(1)}, u32[]{:S(2)}, u32[]{:S(2)}) %collective-permute-start.25) | collective-permute-done | bytes 65568 | tf_op jit(solution)/shard_map/ppermute | solution.py:395
  43.6 1.1 %collective-permute-start.26 = (bf16[64,512]{1,0:T(8,128)(2,1)S(1)}, bf16[64,512]{1,0:T(8,128)(2,1)S(1)}, u32[]{:S(2)}, u32[]{:S(2)}) collective-permute-start(bf16[64,512]{1,0:T(8,128)(2,1)S(1)} %carry.10.refs_0_), channel_id=1, source_target_pairs={{0,4},{1,5},{2,6},{3,7},{4,0},{5,1},{6,2},{7,3},{8,12},{9,13},{10,... | collective-permute-start | bytes 196616 | tf_op jit(solution)/shard_map/ppermute | solution.py:395
  44.7 0.8 %collective-permute-done.23.got = bf16[64,512]{1,0:T(8,128)(2,1)S(1)} collective-permute-done((bf16[64,512]{1,0:T(8,128)(2,1)S(1)}, bf16[64,512]{1,0:T(8,128)(2,1)S(1)}, u32[]{:S(2)}, u32[]{:S(2)}) %collective-permute-start.23) | collective-permute-done | bytes 65568 | tf_op jit(solution)/shard_map/ppermute | solution.py:395
  45.5 1.2 %collective-permute-start.24 = (bf16[64,512]{1,0:T(8,128)(2,1)S(1)}, bf16[64,512]{1,0:T(8,128)(2,1)S(1)}, u32[]{:S(2)}, u32[]{:S(2)}) collective-permute-start(bf16[64,512]{1,0:T(8,128)(2,1)S(1)} %carry.9.refs_0_), channel_id=1, source_target_pairs={{0,4},{1,5},{2,6},{3,7},{4,0},{5,1},{6,2},{7,3},{8,12},{9,13},{10,... | collective-permute-start | bytes 196616 | tf_op jit(solution)/shard_map/ppermute | solution.py:395
  46.9 1.7 %collective-permute-start.28 = (bf16[64,512]{1,0:T(8,128)(2,1)S(1)}, bf16[64,512]{1,0:T(8,128)(2,1)S(1)}, u32[]{:S(2)}, u32[]{:S(2)}) collective-permute-start(bf16[64,512]{1,0:T(8,128)(2,1)S(1)} %carry.11.refs_0_), channel_id=1, source_target_pairs={{0,4},{1,5},{2,6},{3,7},{4,0},{5,1},{6,2},{7,3},{8,12},{9,13},{10,... | collective-permute-start | bytes 196616 | tf_op jit(solution)/shard_map/ppermute | solution.py:395
  48.6 1.4 %collective-permute-done.26.refs_1_ = bf16[64,512]{1,0:T(8,128)(2,1)S(1)} collective-permute-done((bf16[64,512]{1,0:T(8,128)(2,1)S(1)}, bf16[64,512]{1,0:T(8,128)(2,1)S(1)}, u32[]{:S(2)}, u32[]{:S(2)}) %collective-permute-start.26) | collective-permute-done | bytes 65568 | tf_op jit(solution)/shard_map/ppermute | solution.py:395
  50.1 1.0 %collective-permute-start.32 = (bf16[64,512]{1,0:T(8,128)(2,1)S(1)}, bf16[64,512]{1,0:T(8,128)(2,1)S(1)}, u32[]{:S(2)}, u32[]{:S(2)}) collective-permute-start(bf16[64,512]{1,0:T(8,128)(2,1)S(1)} %get-tuple-element.125.refs_4_), channel_id=1, source_target_pairs={{0,2},{1,3},{2,0},{3,1},{4,6},{5,7},{6,4},{7,5},{8,10},{9,11},{10,... | collective-permute-start | bytes 196616 | tf_op jit(solution)/shard_map/ppermute | solution.py:395
  51.7 0.7 collective-permute-start.29
  52.4 0.7 collective-permute-done.28.refs_1_
  53.3 0.8 %collective-permute-start.35 = (bf16[64,512]{1,0:T(8,128)(2,1)S(1)}, bf16[64,512]{1,0:T(8,128)(2,1)S(1)}, u32[]{:S(2)}, u32[]{:S(2)}) collective-permute-start(bf16[64,512]{1,0:T(8,128)(2,1)S(1)} %get-tuple-element.132.refs_0_), channel_id=1, source_target_pairs={{0,2},{1,3},{2,0},{3,1},{4,6},{5,7},{6,4},{7,5},{8,10},{9,11},{10,... | collective-permute-start | bytes 196616 | tf_op jit(solution)/shard_map/ppermute | solution.py:395
  54.4 1.6 %collective-permute-done.29.refs_1_ = bf16[64,512]{1,0:T(8,128)(2,1)S(1)} collective-permute-done((bf16[64,512]{1,0:T(8,128)(2,1)S(1)}, bf16[64,512]{1,0:T(8,128)(2,1)S(1)}, u32[]{:S(2)}, u32[]{:S(2)}) %collective-permute-start.29) | collective-permute-done | bytes 65568 | tf_op jit(solution)/shard_map/ppermute | solution.py:395
  56.6 1.0 %collective-permute-done.35.refs_1_ = bf16[64,512]{1,0:T(8,128)(2,1)S(1)} collective-permute-done((bf16[64,512]{1,0:T(8,128)(2,1)S(1)}, bf16[64,512]{1,0:T(8,128)(2,1)S(1)}, u32[]{:S(2)}, u32[]{:S(2)}) %collective-permute-start.35) | collective-permute-done | bytes 65568 | tf_op jit(solution)/shard_map/ppermute | solution.py:395
  58.1 0.8 %second_first.1 = (bf16[256,512]{1,0:T(8,128)(2,1)S(1)}, bf16[256,512]{1,0:T(8,128)(2,1)S(1)}, bf16[256,256]{1,0:T(8,128)(2,1)S(1)}, f32[128,512]{1,0:T(8,128)S(...) custom-call(bf16[64,512]{1,0:T(8,128)(2,1)S(1)} %get-tuple-element.124.refs_0_, ...), custom_call_target="tpu_custom_call" | custom-call | flops 402653184 | bytes 3670016 | tf_op jit(solution)/shard_map/second_first/pallas_call | solution.py:372
  59.0 0.7 %second_last.1 = (bf16[512,256]{1,0:T(8,128)(2,1)S(1)}, bf16[256,256]{1,0:T(8,128)(2,1)S(1)}, bf16[256,256]{1,0:T(8,128)(2,1)S(1)}, f32[96,512]{1,0:T(8,128)S(1)...) custom-call(bf16[64,512]{1,0:T(8,128)(2,1)S(1)} %get-tuple-element.132.refs_0_, ...), custom_call_target="tpu_custom_call" | custom-call | flops 402653184 | bytes 3670016 | tf_op jit(solution)/shard_map/second_last/pallas_call | solution.py:372
  59.8 1.7 %collective-permute-start.38 = (bf16[96,512]{1,0:T(8,128)(2,1)S(1)}, bf16[96,512]{1,0:T(8,128)(2,1)S(1)}, u32[]{:S(2)}, u32[]{:S(2)}) collective-permute-start(bf16[96,512]{1,0:T(8,128)(2,1)S(1)} %get-tuple-element.148), channel_id=1, source_target_pairs={{0,6},{1,7},{2,4},{3,5},{4,2},{5,3},{6,0},{7,1},{8,14},{9,15},{10,... | collective-permute-start | bytes 294920 | tf_op jit(solution)/shard_map/ppermute | solution.py:390
  61.5 0.6 collective-permute-start.39
  62.1 2.2 %collective-permute-start.40 = (bf16[96,512]{1,0:T(8,128)(2,1)S(1)}, bf16[96,512]{1,0:T(8,128)(2,1)S(1)}, u32[]{:S(2)}, u32[]{:S(2)}) collective-permute-start(bf16[96,512]{1,0:T(8,128)(2,1)S(1)} %get-tuple-element.150), channel_id=1, source_target_pairs={{0,2},{1,3},{2,0},{3,1},{4,6},{5,7},{6,4},{7,5},{8,10},{9,11},{10,... | collective-permute-start | bytes 294920 | tf_op jit(solution)/shard_map/ppermute | solution.py:390
  64.2 1.0 %query_grad.1 = bf16[256,512]{1,0:T(8,128)(2,1)} custom-call(bf16[256,256]{1,0:T(8,128)(2,1)S(1)} %get-tuple-element.106.gate_back, bf16[256,256]{1,0:T(8,128)(2,1)S(1)} %get-tuple-element.107.up_back, bf16[256,512]{1,0:T(8,128)(2,1)S(1)} %get-tuple-element.108.f1t, bf16[256,512]{1,0:T(8,128)(2,1)S(1)} %get-tuple-element.109.f3t), custom_call_target="tpu_custom_call" | custom-call | flops 134217728 | bytes 786432 | tf_op jit(solution)/shard_map/query_grad/pallas_call | solution.py:372
  65.3 1.4 %token_grads.1 = (bf16[256,512]{1,0:T(8,128)(2,1)}, bf16[256,512]{1,0:T(8,128)(2,1)}) custom-call(f32[1,256]{1,0:T(1,128)S(1)} %bitcast.33, bf16[256,256]{1,0:T(8,128)(2,1)S(1)} %get-tuple-element.110.refs_1_, bf16[256,256]{1,0:T(8,128)(2,1)S(1)} %get-tuple-element.131.refs_2_, bf16[256,256]{1,0:T(8,128)(2,1)S(1)} %get-tuple-element.136.refs_3_, ...), custom_call_target="tpu_custom_call" | custom-call | flops 402653184 | bytes 2360320 | tf_op jit(solution)/shard_map/token_grads/pallas_call | solution.py:372
  66.6 0.7 %collective-permute-done.38.refs_4_ = bf16[96,512]{1,0:T(8,128)(2,1)S(1)} collective-permute-done((bf16[96,512]{1,0:T(8,128)(2,1)S(1)}, bf16[96,512]{1,0:T(8,128)(2,1)S(1)}, u32[]{:S(2)}, u32[]{:S(2)}) %collective-permute-start.38) | collective-permute-done | bytes 98336 | tf_op jit(solution)/shard_map/ppermute | solution.py:390
  67.4 4.0 %collective-permute-done.39.refs_5_ = bf16[96,512]{1,0:T(8,128)(2,1)S(1)} collective-permute-done((bf16[96,512]{1,0:T(8,128)(2,1)S(1)}, bf16[96,512]{1,0:T(8,128)(2,1)S(1)}, u32[]{:S(2)}, u32[]{:S(2)}) %collective-permute-start.39) | collective-permute-done | bytes 98336 | tf_op jit(solution)/shard_map/ppermute | solution.py:390
  71.4 0.7 owner_result.1
  (74 shorter events, 7.7 us)
Async XLA Ops:
  0.6 1.0 %copy-start.5 = (f32[256,1]{0,1:T(1,128)S(1)}, f32[256,1]{0,1:T(1,128)}, u32[]{:S(2)}) copy-start(f32[256,1]{0,1:T(1,128)} %param.13) | copy-start | bytes 3076
  0.6 2.5 %collective-permute-start.2 = (bf16[256,512]{1,0:T(8,128)(2,1)}, bf16[256,512]{1,0:T(8,128)(2,1)S(1)}, u32[]{:S(2)}, u32[]{:S(2)}) collective-permute-start(bf16[256,512]{1,0:T(8,128)(2,1)} %vo.3), channel_id=1, source_target_pairs={{0,1},{1,0},{2,3},{3,2},{4,5},{5,4},{6,7},{7,6},{8,9},{9,8},{10,11... | collective-permute-start | bytes 786440 | tf_op jit(solution)/shard_map/ppermute | solution.py:511
  1.2 2.0 %collective-permute-start.1 = (bf16[256,512]{1,0:T(8,128)(2,1)}, bf16[256,512]{1,0:T(8,128)(2,1)S(1)}, u32[]{:S(2)}, u32[]{:S(2)}) collective-permute-start(bf16[256,512]{1,0:T(8,128)(2,1)} %refs_4_.1), channel_id=1, source_target_pairs={{0,1},{1,0},{2,3},{3,2},{4,5},{5,4},{6,7},{7,6},{8,9},{9,8},{10,11... | collective-permute-start | bytes 786440 | tf_op jit(solution)/shard_map/ppermute | solution.py:511
  1.2 12.6 %collective-permute-start = (bf16[256,512]{1,0:T(8,128)(2,1)}, bf16[256,512]{1,0:T(8,128)(2,1)S(1)}, u32[]{:S(2)}, u32[]{:S(2)}) collective-permute-start(bf16[256,512]{1,0:T(8,128)(2,1)} %go.1), channel_id=1, source_target_pairs={{0,1},{1,0},{2,3},{3,2},{4,5},{5,4},{6,7},{7,6},{8,9},{9,8},{10,11... | collective-permute-start | bytes 786440 | tf_op jit(solution)/shard_map/ppermute | solution.py:511
  1.7 1.2 %copy-start.7 = (bf16[1,512,256]{2,1,0:T(8,128)(2,1)S(1)}, bf16[1,512,256]{2,1,0:T(8,128)(2,1)}, u32[]{:S(2)}) copy-start(bf16[1,512,256]{2,1,0:T(8,128)(2,1)} %param.16) | copy-start | bytes 786436
  1.7 1.4 %collective-permute-start.3 = (f32[1,256]{1,0:T(1,128)S(1)}, f32[1,256]{1,0:T(1,128)S(1)}, u32[]{:S(2)}, u32[]{:S(2)}) collective-permute-start(f32[1,256]{1,0:T(1,128)S(1)} %bitcast.30), channel_id=1, source_target_pairs={{0,1},{1,0},{2,3},{3,2},{4,5},{5,4},{6,7},{7,6},{8,9},{9,8},{10,11... | collective-permute-start | bytes 3080 | tf_op jit(solution)/shard_map/ppermute | solution.py:511
  1.8 1.4 %copy-start.4 = (bf16[256,512]{1,0:T(8,128)(2,1)S(1)}, bf16[256,512]{1,0:T(8,128)(2,1)}, u32[]{:S(2)}) copy-start(bf16[256,512]{1,0:T(8,128)(2,1)} %vo.3) | copy-start | bytes 786436
  2.9 1.0 %copy-start = (bf16[256,512]{1,0:T(8,128)(2,1)S(1)}, bf16[256,512]{1,0:T(8,128)(2,1)}, u32[]{:S(2)}) copy-start(bf16[256,512]{1,0:T(8,128)(2,1)} %refs_4_.1) | copy-start | bytes 786436
  2.9 1.0 %copy-start.1 = (bf16[1,256,512]{2,1,0:T(8,128)(2,1)S(1)}, bf16[1,256,512]{2,1,0:T(8,128)(2,1)}, u32[]{:S(2)}) copy-start(bf16[1,256,512]{2,1,0:T(8,128)(2,1)} %param.17) | copy-start | bytes 786436
  5.1 8.8 %copy-start.3 = (bf16[256,512]{1,0:T(8,128)(2,1)S(1)}, bf16[256,512]{1,0:T(8,128)(2,1)}, u32[]{:S(2)}) copy-start(bf16[256,512]{1,0:T(8,128)(2,1)} %go.1) | copy-start | bytes 786436
  5.1 5.5 %collective-permute-start.9 = (bf16[64,512]{1,0:T(8,128)(2,1)S(1)}, bf16[64,512]{1,0:T(8,128)(2,1)S(1)}, u32[]{:S(2)}, u32[]{:S(2)}) collective-permute-start(bf16[64,512]{1,0:T(8,128)(2,1)S(1)} %get-tuple-element.90), channel_id=1, source_target_pairs={{0,2},{1,3},{2,0},{3,1},{4,6},{5,7},{6,4},{7,5},{8,10},{9,11},{10,... | collective-permute-start | bytes 196616 | tf_op jit(solution)/shard_map/ppermute | solution.py:395
  8.2 6.7 %collective-permute-start.7 = (bf16[64,512]{1,0:T(8,128)(2,1)S(1)}, bf16[64,512]{1,0:T(8,128)(2,1)S(1)}, u32[]{:S(2)}, u32[]{:S(2)}) collective-permute-start(bf16[64,512]{1,0:T(8,128)(2,1)S(1)} %get-tuple-element.86), channel_id=1, source_target_pairs={{0,2},{1,3},{2,0},{3,1},{4,6},{5,7},{6,4},{7,5},{8,10},{9,11},{10,... | collective-permute-start | bytes 196616 | tf_op jit(solution)/shard_map/ppermute | solution.py:395
  8.2 7.6 %collective-permute-start.4 = (bf16[64,512]{1,0:T(8,128)(2,1)S(1)}, bf16[64,512]{1,0:T(8,128)(2,1)S(1)}, u32[]{:S(2)}, u32[]{:S(2)}) collective-permute-start(bf16[64,512]{1,0:T(8,128)(2,1)S(1)} %get-tuple-element.82), channel_id=1, source_target_pairs={{0,2},{1,3},{2,0},{3,1},{4,6},{5,7},{6,4},{7,5},{8,10},{9,11},{10,... | collective-permute-start | bytes 196616 | tf_op jit(solution)/shard_map/ppermute | solution.py:395
  10.6 3.3 %copy-start.6 = (f32[512]{0:T(512)S(1)}, f32[512]{0:T(512)}, u32[]{:S(2)}) copy-start(f32[512]{0:T(512)} %param.14) | copy-start | bytes 6148
  10.7 7.3 %collective-permute-start.10 = (bf16[64,512]{1,0:T(8,128)(2,1)S(1)}, bf16[64,512]{1,0:T(8,128)(2,1)S(1)}, u32[]{:S(2)}, u32[]{:S(2)}) collective-permute-start(bf16[64,512]{1,0:T(8,128)(2,1)S(1)} %carry.8.refs_0_), channel_id=1, source_target_pairs={{0,4},{1,5},{2,6},{3,7},{4,0},{5,1},{6,2},{7,3},{8,12},{9,13},{10,... | collective-permute-start | bytes 196616 | tf_op jit(solution)/shard_map/ppermute | solution.py:395
  14.8 16.1 %collective-permute-start.19 = (bf16[256,512]{1,0:T(8,128)(2,1)S(1)}, bf16[256,512]{1,0:T(8,128)(2,1)S(1)}, u32[]{:S(2)}, u32[]{:S(2)}) collective-permute-start(bf16[256,512]{1,0:T(8,128)(2,1)S(1)} %copy-done.2), channel_id=1, source_target_pairs={{0,1},{1,0},{2,3},{3,2},{4,5},{5,4},{6,7},{7,6},{8,9},{9,8},{10,11... | collective-permute-start | bytes 786440 | tf_op jit(solution)/shard_map/ppermute | solution.py:511
  14.9 8.8 %collective-permute-start.8 = (bf16[64,512]{1,0:T(8,128)(2,1)S(1)}, bf16[64,512]{1,0:T(8,128)(2,1)S(1)}, u32[]{:S(2)}, u32[]{:S(2)}) collective-permute-start(bf16[64,512]{1,0:T(8,128)(2,1)S(1)} %carry.7.refs_0_), channel_id=1, source_target_pairs={{0,4},{1,5},{2,6},{3,7},{4,0},{5,1},{6,2},{7,3},{8,12},{9,13},{10,... | collective-permute-start | bytes 196616 | tf_op jit(solution)/shard_map/ppermute | solution.py:395
  15.9 8.8 %collective-permute-start.5 = (bf16[64,512]{1,0:T(8,128)(2,1)S(1)}, bf16[64,512]{1,0:T(8,128)(2,1)S(1)}, u32[]{:S(2)}, u32[]{:S(2)}) collective-permute-start(bf16[64,512]{1,0:T(8,128)(2,1)S(1)} %carry.6.refs_0_), channel_id=1, source_target_pairs={{0,4},{1,5},{2,6},{3,7},{4,0},{5,1},{6,2},{7,3},{8,12},{9,13},{10,... | collective-permute-start | bytes 196616 | tf_op jit(solution)/shard_map/ppermute | solution.py:395
  18.1 8.0 %collective-permute-start.11 = (bf16[64,512]{1,0:T(8,128)(2,1)S(1)}, bf16[64,512]{1,0:T(8,128)(2,1)S(1)}, u32[]{:S(2)}, u32[]{:S(2)}) collective-permute-start(bf16[64,512]{1,0:T(8,128)(2,1)S(1)} %get-tuple-element.95.refs_8_), channel_id=1, source_target_pairs={{0,2},{1,3},{2,0},{3,1},{4,6},{5,7},{6,4},{7,5},{8,10},{9,11},{10,... | collective-permute-start | bytes 196616 | tf_op jit(solution)/shard_map/ppermute | solution.py:395
  23.8 4.7 %collective-permute-start.14 = (bf16[64,512]{1,0:T(8,128)(2,1)S(1)}, bf16[64,512]{1,0:T(8,128)(2,1)S(1)}, u32[]{:S(2)}, u32[]{:S(2)}) collective-permute-start(bf16[64,512]{1,0:T(8,128)(2,1)S(1)} %get-tuple-element.93.refs_4_), channel_id=1, source_target_pairs={{0,2},{1,3},{2,0},{3,1},{4,6},{5,7},{6,4},{7,5},{8,10},{9,11},{10,... | collective-permute-start | bytes 196616 | tf_op jit(solution)/shard_map/ppermute | solution.py:395
  24.8 4.4 %collective-permute-start.6 = (bf16[64,512]{1,0:T(8,128)(2,1)S(1)}, bf16[64,512]{1,0:T(8,128)(2,1)S(1)}, u32[]{:S(2)}, u32[]{:S(2)}) collective-permute-start(bf16[64,512]{1,0:T(8,128)(2,1)S(1)} %get-tuple-element.92.refs_0_), channel_id=1, source_target_pairs={{0,2},{1,3},{2,0},{3,1},{4,6},{5,7},{6,4},{7,5},{8,10},{9,11},{10,... | collective-permute-start | bytes 196616 | tf_op jit(solution)/shard_map/ppermute | solution.py:395
  26.1 3.1 %collective-permute-start.12 = (bf16[64,512]{1,0:T(8,128)(2,1)S(1)}, bf16[64,512]{1,0:T(8,128)(2,1)S(1)}, u32[]{:S(2)}, u32[]{:S(2)}) collective-permute-start(bf16[64,512]{1,0:T(8,128)(2,1)S(1)} %get-tuple-element.92.refs_0_), channel_id=1, source_target_pairs={{0,1},{1,0},{2,3},{3,2},{4,5},{5,4},{6,7},{7,6},{8,9},{9,8},{10,11... | collective-permute-start | bytes 196616 | tf_op jit(solution)/shard_map/ppermute | solution.py:406
  26.1 3.6 %collective-permute-start.15 = (bf16[64,512]{1,0:T(8,128)(2,1)S(1)}, bf16[64,512]{1,0:T(8,128)(2,1)S(1)}, u32[]{:S(2)}, u32[]{:S(2)}) collective-permute-start(bf16[64,512]{1,0:T(8,128)(2,1)S(1)} %get-tuple-element.93.refs_4_), channel_id=1, source_target_pairs={{0,1},{1,0},{2,3},{3,2},{4,5},{5,4},{6,7},{7,6},{8,9},{9,8},{10,11... | collective-permute-start | bytes 196616 | tf_op jit(solution)/shard_map/ppermute | solution.py:406
  28.5 1.3 %collective-permute-start.17 = (bf16[64,512]{1,0:T(8,128)(2,1)S(1)}, bf16[64,512]{1,0:T(8,128)(2,1)S(1)}, u32[]{:S(2)}, u32[]{:S(2)}) collective-permute-start(bf16[64,512]{1,0:T(8,128)(2,1)S(1)} %get-tuple-element.95.refs_8_), channel_id=1, source_target_pairs={{0,1},{1,0},{2,3},{3,2},{4,5},{5,4},{6,7},{7,6},{8,9},{9,8},{10,11... | collective-permute-start | bytes 196616 | tf_op jit(solution)/shard_map/ppermute | solution.py:406
  29.2 1.3 %collective-permute-start.18 = (bf16[64,512]{1,0:T(8,128)(2,1)S(1)}, bf16[64,512]{1,0:T(8,128)(2,1)S(1)}, u32[]{:S(2)}, u32[]{:S(2)}) collective-permute-start(bf16[64,512]{1,0:T(8,128)(2,1)S(1)} %collective-permute-done.11.refs_9_), channel_id=1, source_target_pairs={{0,1},{1,0},{2,3},{3,2},{4,5},{5,4},{6,7},{7,6},{8,9},{9,8},{10,11... | collective-permute-start | bytes 196616 | tf_op jit(solution)/shard_map/ppermute | solution.py:406
  29.2 1.4 %collective-permute-start.16 = (bf16[64,512]{1,0:T(8,128)(2,1)S(1)}, bf16[64,512]{1,0:T(8,128)(2,1)S(1)}, u32[]{:S(2)}, u32[]{:S(2)}) collective-permute-start(bf16[64,512]{1,0:T(8,128)(2,1)S(1)} %collective-permute-done.14.refs_5_), channel_id=1, source_target_pairs={{0,1},{1,0},{2,3},{3,2},{4,5},{5,4},{6,7},{7,6},{8,9},{9,8},{10,11... | collective-permute-start | bytes 196616 | tf_op jit(solution)/shard_map/ppermute | solution.py:406
  29.7 1.3 %collective-permute-start.13 = (bf16[64,512]{1,0:T(8,128)(2,1)S(1)}, bf16[64,512]{1,0:T(8,128)(2,1)S(1)}, u32[]{:S(2)}, u32[]{:S(2)}) collective-permute-start(bf16[64,512]{1,0:T(8,128)(2,1)S(1)} %collective-permute-done.6.refs_1_), channel_id=1, source_target_pairs={{0,1},{1,0},{2,3},{3,2},{4,5},{5,4},{6,7},{7,6},{8,9},{9,8},{10,11... | collective-permute-start | bytes 196616 | tf_op jit(solution)/shard_map/ppermute | solution.py:406
  31.8 4.6 %collective-permute-start.22 = (f32[2,512]{1,0:T(2,128)S(1)}, f32[2,512]{1,0:T(2,128)S(1)}, u32[]{:S(2)}, u32[]{:S(2)}) collective-permute-start(f32[2,512]{1,0:T(2,128)S(1)} %get-tuple-element.99.refs_0_), channel_id=1, source_target_pairs={{0,24},{8,16},{16,8},{24,0},{1,25},{9,17},{17,9},{25,1},{2,26},{10... | collective-permute-start | bytes 12296 | tf_op jit(solution)/shard_map/ppermute | solution.py:413
  34.3 3.6 %collective-permute-start.21 = (f32[2,512]{1,0:T(2,128)S(1)}, f32[2,512]{1,0:T(2,128)S(1)}, u32[]{:S(2)}, u32[]{:S(2)}) collective-permute-start(f32[2,512]{1,0:T(2,128)S(1)} %get-tuple-element.99.refs_0_), channel_id=1, source_target_pairs={{0,16},{8,24},{16,0},{24,8},{1,17},{9,25},{17,1},{25,9},{2,18},{10... | collective-permute-start | bytes 12296 | tf_op jit(solution)/shard_map/ppermute | solution.py:413
  34.8 3.6 %collective-permute-start.20 = (f32[2,512]{1,0:T(2,128)S(1)}, f32[2,512]{1,0:T(2,128)S(1)}, u32[]{:S(2)}, u32[]{:S(2)}) collective-permute-start(f32[2,512]{1,0:T(2,128)S(1)} %get-tuple-element.99.refs_0_), channel_id=1, source_target_pairs={{0,8},{8,0},{16,24},{24,16},{1,9},{9,1},{17,25},{25,17},{2,10},{10... | collective-permute-start | bytes 12296 | tf_op jit(solution)/shard_map/ppermute | solution.py:413
  39.3 4.3 %collective-permute-start.25 = (bf16[64,512]{1,0:T(8,128)(2,1)S(1)}, bf16[64,512]{1,0:T(8,128)(2,1)S(1)}, u32[]{:S(2)}, u32[]{:S(2)}) collective-permute-start(bf16[64,512]{1,0:T(8,128)(2,1)S(1)} %get-tuple-element.117), channel_id=1, source_target_pairs={{0,2},{1,3},{2,0},{3,1},{4,6},{5,7},{6,4},{7,5},{8,10},{9,11},{10,... | collective-permute-start | bytes 196616 | tf_op jit(solution)/shard_map/ppermute | solution.py:395
  40.5 5.0 %collective-permute-start.23 = (bf16[64,512]{1,0:T(8,128)(2,1)S(1)}, bf16[64,512]{1,0:T(8,128)(2,1)S(1)}, u32[]{:S(2)}, u32[]{:S(2)}) collective-permute-start(bf16[64,512]{1,0:T(8,128)(2,1)S(1)} %get-tuple-element.113), channel_id=1, source_target_pairs={{0,2},{1,3},{2,0},{3,1},{4,6},{5,7},{6,4},{7,5},{8,10},{9,11},{10,... | collective-permute-start | bytes 196616 | tf_op jit(solution)/shard_map/ppermute | solution.py:395
  41.3 5.5 %collective-permute-start.27 = (bf16[64,512]{1,0:T(8,128)(2,1)S(1)}, bf16[64,512]{1,0:T(8,128)(2,1)S(1)}, u32[]{:S(2)}, u32[]{:S(2)}) collective-permute-start(bf16[64,512]{1,0:T(8,128)(2,1)S(1)} %get-tuple-element.121), channel_id=1, source_target_pairs={{0,2},{1,3},{2,0},{3,1},{4,6},{5,7},{6,4},{7,5},{8,10},{9,11},{10,... | collective-permute-start | bytes 196616 | tf_op jit(solution)/shard_map/ppermute | solution.py:395
  43.6 6.4 %collective-permute-start.26 = (bf16[64,512]{1,0:T(8,128)(2,1)S(1)}, bf16[64,512]{1,0:T(8,128)(2,1)S(1)}, u32[]{:S(2)}, u32[]{:S(2)}) collective-permute-start(bf16[64,512]{1,0:T(8,128)(2,1)S(1)} %carry.10.refs_0_), channel_id=1, source_target_pairs={{0,4},{1,5},{2,6},{3,7},{4,0},{5,1},{6,2},{7,3},{8,12},{9,13},{10,... | collective-permute-start | bytes 196616 | tf_op jit(solution)/shard_map/ppermute | solution.py:395
  45.5 6.1 %collective-permute-start.24 = (bf16[64,512]{1,0:T(8,128)(2,1)S(1)}, bf16[64,512]{1,0:T(8,128)(2,1)S(1)}, u32[]{:S(2)}, u32[]{:S(2)}) collective-permute-start(bf16[64,512]{1,0:T(8,128)(2,1)S(1)} %carry.9.refs_0_), channel_id=1, source_target_pairs={{0,4},{1,5},{2,6},{3,7},{4,0},{5,1},{6,2},{7,3},{8,12},{9,13},{10,... | collective-permute-start | bytes 196616 | tf_op jit(solution)/shard_map/ppermute | solution.py:395
  46.9 6.3 %collective-permute-start.28 = (bf16[64,512]{1,0:T(8,128)(2,1)S(1)}, bf16[64,512]{1,0:T(8,128)(2,1)S(1)}, u32[]{:S(2)}, u32[]{:S(2)}) collective-permute-start(bf16[64,512]{1,0:T(8,128)(2,1)S(1)} %carry.11.refs_0_), channel_id=1, source_target_pairs={{0,4},{1,5},{2,6},{3,7},{4,0},{5,1},{6,2},{7,3},{8,12},{9,13},{10,... | collective-permute-start | bytes 196616 | tf_op jit(solution)/shard_map/ppermute | solution.py:395
  50.1 4.3 %collective-permute-start.32 = (bf16[64,512]{1,0:T(8,128)(2,1)S(1)}, bf16[64,512]{1,0:T(8,128)(2,1)S(1)}, u32[]{:S(2)}, u32[]{:S(2)}) collective-permute-start(bf16[64,512]{1,0:T(8,128)(2,1)S(1)} %get-tuple-element.125.refs_4_), channel_id=1, source_target_pairs={{0,2},{1,3},{2,0},{3,1},{4,6},{5,7},{6,4},{7,5},{8,10},{9,11},{10,... | collective-permute-start | bytes 196616 | tf_op jit(solution)/shard_map/ppermute | solution.py:395
  51.7 4.3 %collective-permute-start.29 = (bf16[64,512]{1,0:T(8,128)(2,1)S(1)}, bf16[64,512]{1,0:T(8,128)(2,1)S(1)}, u32[]{:S(2)}, u32[]{:S(2)}) collective-permute-start(bf16[64,512]{1,0:T(8,128)(2,1)S(1)} %get-tuple-element.124.refs_0_), channel_id=1, source_target_pairs={{0,2},{1,3},{2,0},{3,1},{4,6},{5,7},{6,4},{7,5},{8,10},{9,11},{10,... | collective-permute-start | bytes 196616 | tf_op jit(solution)/shard_map/ppermute | solution.py:395
  53.3 4.3 %collective-permute-start.35 = (bf16[64,512]{1,0:T(8,128)(2,1)S(1)}, bf16[64,512]{1,0:T(8,128)(2,1)S(1)}, u32[]{:S(2)}, u32[]{:S(2)}) collective-permute-start(bf16[64,512]{1,0:T(8,128)(2,1)S(1)} %get-tuple-element.132.refs_0_), channel_id=1, source_target_pairs={{0,2},{1,3},{2,0},{3,1},{4,6},{5,7},{6,4},{7,5},{8,10},{9,11},{10,... | collective-permute-start | bytes 196616 | tf_op jit(solution)/shard_map/ppermute | solution.py:395
  54.4 3.2 %collective-permute-start.34 = (bf16[64,512]{1,0:T(8,128)(2,1)S(1)}, bf16[64,512]{1,0:T(8,128)(2,1)S(1)}, u32[]{:S(2)}, u32[]{:S(2)}) collective-permute-start(bf16[64,512]{1,0:T(8,128)(2,1)S(1)} %collective-permute-done.32.refs_5_), channel_id=1, source_target_pairs={{0,1},{1,0},{2,3},{3,2},{4,5},{5,4},{6,7},{7,6},{8,9},{9,8},{10,11... | collective-permute-start | bytes 196616 | tf_op jit(solution)/shard_map/ppermute | solution.py:406
  56.1 2.1 %collective-permute-start.30 = (bf16[64,512]{1,0:T(8,128)(2,1)S(1)}, bf16[64,512]{1,0:T(8,128)(2,1)S(1)}, u32[]{:S(2)}, u32[]{:S(2)}) collective-permute-start(bf16[64,512]{1,0:T(8,128)(2,1)S(1)} %get-tuple-element.124.refs_0_), channel_id=1, source_target_pairs={{0,1},{1,0},{2,3},{3,2},{4,5},{5,4},{6,7},{7,6},{8,9},{9,8},{10,11... | collective-permute-start | bytes 196616 | tf_op jit(solution)/shard_map/ppermute | solution.py:406
  56.1 2.1 %collective-permute-start.33 = (bf16[64,512]{1,0:T(8,128)(2,1)S(1)}, bf16[64,512]{1,0:T(8,128)(2,1)S(1)}, u32[]{:S(2)}, u32[]{:S(2)}) collective-permute-start(bf16[64,512]{1,0:T(8,128)(2,1)S(1)} %get-tuple-element.125.refs_4_), channel_id=1, source_target_pairs={{0,1},{1,0},{2,3},{3,2},{4,5},{5,4},{6,7},{7,6},{8,9},{9,8},{10,11... | collective-permute-start | bytes 196616 | tf_op jit(solution)/shard_map/ppermute | solution.py:406
  56.6 1.6 %collective-permute-start.31 = (bf16[64,512]{1,0:T(8,128)(2,1)S(1)}, bf16[64,512]{1,0:T(8,128)(2,1)S(1)}, u32[]{:S(2)}, u32[]{:S(2)}) collective-permute-start(bf16[64,512]{1,0:T(8,128)(2,1)S(1)} %collective-permute-done.29.refs_1_), channel_id=1, source_target_pairs={{0,1},{1,0},{2,3},{3,2},{4,5},{5,4},{6,7},{7,6},{8,9},{9,8},{10,11... | collective-permute-start | bytes 196616 | tf_op jit(solution)/shard_map/ppermute | solution.py:406
  57.6 1.3 %collective-permute-start.36 = (bf16[64,512]{1,0:T(8,128)(2,1)S(1)}, bf16[64,512]{1,0:T(8,128)(2,1)S(1)}, u32[]{:S(2)}, u32[]{:S(2)}) collective-permute-start(bf16[64,512]{1,0:T(8,128)(2,1)S(1)} %get-tuple-element.132.refs_0_), channel_id=1, source_target_pairs={{0,1},{1,0},{2,3},{3,2},{4,5},{5,4},{6,7},{7,6},{8,9},{9,8},{10,11... | collective-permute-start | bytes 196616 | tf_op jit(solution)/shard_map/ppermute | solution.py:406
  57.6 1.4 %collective-permute-start.37 = (bf16[64,512]{1,0:T(8,128)(2,1)S(1)}, bf16[64,512]{1,0:T(8,128)(2,1)S(1)}, u32[]{:S(2)}, u32[]{:S(2)}) collective-permute-start(bf16[64,512]{1,0:T(8,128)(2,1)S(1)} %collective-permute-done.35.refs_1_), channel_id=1, source_target_pairs={{0,1},{1,0},{2,3},{3,2},{4,5},{5,4},{6,7},{7,6},{8,9},{9,8},{10,11... | collective-permute-start | bytes 196616 | tf_op jit(solution)/shard_map/ppermute | solution.py:406
  59.8 7.6 %collective-permute-start.38 = (bf16[96,512]{1,0:T(8,128)(2,1)S(1)}, bf16[96,512]{1,0:T(8,128)(2,1)S(1)}, u32[]{:S(2)}, u32[]{:S(2)}) collective-permute-start(bf16[96,512]{1,0:T(8,128)(2,1)S(1)} %get-tuple-element.148), channel_id=1, source_target_pairs={{0,6},{1,7},{2,4},{3,5},{4,2},{5,3},{6,0},{7,1},{8,14},{9,15},{10,... | collective-permute-start | bytes 294920 | tf_op jit(solution)/shard_map/ppermute | solution.py:390
  61.5 9.9 %collective-permute-start.39 = (bf16[96,512]{1,0:T(8,128)(2,1)S(1)}, bf16[96,512]{1,0:T(8,128)(2,1)S(1)}, u32[]{:S(2)}, u32[]{:S(2)}) collective-permute-start(bf16[96,512]{1,0:T(8,128)(2,1)S(1)} %get-tuple-element.149), channel_id=1, source_target_pairs={{0,4},{1,5},{2,6},{3,7},{4,0},{5,1},{6,2},{7,3},{8,12},{9,13},{10,... | collective-permute-start | bytes 294920 | tf_op jit(solution)/shard_map/ppermute | solution.py:390
  62.1 9.3 %collective-permute-start.40 = (bf16[96,512]{1,0:T(8,128)(2,1)S(1)}, bf16[96,512]{1,0:T(8,128)(2,1)S(1)}, u32[]{:S(2)}, u32[]{:S(2)}) collective-permute-start(bf16[96,512]{1,0:T(8,128)(2,1)S(1)} %get-tuple-element.150), channel_id=1, source_target_pairs={{0,2},{1,3},{2,0},{3,1},{4,6},{5,7},{6,4},{7,5},{8,10},{9,11},{10,... | collective-permute-start | bytes 294920 | tf_op jit(solution)/shard_map/ppermute | solution.py:390
  (1 other events, 1.0 us)
